TPU v7x, 32 devices: a whole 2x2x4 slice. The times are simulated.
32 devices in a mesh: groups: 2 (over y), gx: 8 (over z, x), gy: 2 (over core).
Axes of the slice: x: 2, y: 2, z: 4, core: 2. Of those that a mesh axis runs over, the one named last changes fastest.
Arguments:
- activations: bfloat16 [16, 16384], P(('groups', 'gy'), 'gx'), parts along dimension 0, may hold values from -60 to 60
- w_query: bfloat16 [16384, 8192], P('gx', 'gy'), may hold values from -0.046875 to 0.046875
- key_weight: bfloat16 [16384, 512], P('gx', 'gy'), may hold values from -0.046875 to 0.046875
- value_weight: bfloat16 [16384, 512], P('gx', 'gy'), may hold values from -0.046875 to 0.046875
- w_out: bfloat16 [8192, 16384], P('gy', 'gx'), may hold values from -0.5 to 0.5
- k_cache: bfloat16 [16, 4, 2048, 128], P(('groups', 'gx'), 'gy'), parts along dimension 0, may hold values from -800 to 800
- value_cache: bfloat16 [16, 4, 2048, 128], P(('groups', 'gx'), 'gy'), parts along dimension 0, may hold values from -6 to 6
- lengths: int32 [16], P(('groups', 'gx')), parts along dimension 0, may hold values from 1 to 2048, as said below
Outputs:
- attn_out: bfloat16 [16, 16384], P(('groups', 'gy'), 'gx'), parts along dimension 0
There are 2 independent parts, one for each index of `groups`. A program takes and returns all parts, laid end to end along the dimension named above; an argument that names none is the same for every part. Nothing has to cross between parts.
Inputs may be any that keep to these rules, and one draw needn't show every extreme that they name: `lengths`: one row of every part has exactly 2048 cached tokens.
All inputs are finite; a program needn't handle non-finite values.
Results may differ from a plain program's by a relative error of at most 0.011.
Values may be sent and summed in bfloat16 or wider, within the bound.
No kernel may reach another device: no remote copies, remote signals or barrier semaphores. Data moves between devices by JAX's collectives and lax.ppermute only.
A program may use at most 128 MiB of HBM per device.

v0:
```python
import math

import jax
import jax.numpy as jnp
from jax import lax
from jax.sharding import PartitionSpec as P

MODEL_WIDTH = 16384
HEAD_SIZE = 128


def apply_rotary(vectors, token_positions):
    half = vectors.shape[-1] // 2
    frequency = jnp.power(
        jnp.float32(500000.0), -2.0 * jnp.arange(half, dtype=jnp.float32) / vectors.shape[-1]
    )
    angle = token_positions[:, None, None] * frequency
    cosine = jnp.cos(angle)
    sine = jnp.sin(angle)
    first_halfpart = vectors[..., :half]
    second_halfpart = vectors[..., half:]
    return jnp.concatenate(
        [
            first_halfpart * cosine - second_halfpart * sine,
            second_halfpart * cosine + first_halfpart * sine,
        ],
        axis=-1,
    )


def softmax_weights(scores, own):
    top = jnp.maximum(jnp.max(scores, axis=-1), own)
    exponent = jnp.exp(scores - top[..., None])
    own_exp = jnp.exp(own - top)
    total = jnp.sum(exponent, axis=-1) + own_exp
    return (
        (exponent / total[..., None]).astype(jnp.bfloat16),
        (own_exp / total).astype(jnp.bfloat16),
    )


def body(activations, w_query, key_weight, value_weight, w_out, k_cache, value_cache, lengths):
    rows_all = lax.all_gather(activations, "gy", axis=0, tiled=True)
    widened = rows_all.astype(jnp.float32)
    squares = lax.psum(jnp.sum(widened * widened, axis=1), "gx")
    scale_rows = lax.rsqrt(squares / MODEL_WIDTH + 1e-05)
    rows_dev = k_cache.shape[0]
    kv_local = k_cache.shape[1]
    cache_len = k_cache.shape[2]
    query_width = w_query.shape[1]
    key_width = key_weight.shape[1]
    first_row = lax.axis_index("gx") * rows_dev
    summed = lax.psum(
        jnp.concatenate(
            [
                jnp.dot(rows_all, w_query, preferred_element_type=jnp.float32),
                jnp.dot(rows_all, key_weight, preferred_element_type=jnp.float32),
                jnp.dot(rows_all, value_weight, preferred_element_type=jnp.float32),
            ],
            axis=1,
        ),
        "gx",
    )
    owned = lax.dynamic_slice_in_dim(summed, first_row, rows_dev, 0)
    owned = owned * lax.dynamic_slice_in_dim(scale_rows, first_row, rows_dev, 0)[:, None]
    token_positions = lengths.astype(jnp.float32)
    query_rows = apply_rotary(
        owned[:, :query_width].reshape(rows_dev, -1, HEAD_SIZE), token_positions
    ).astype(jnp.bfloat16)
    fresh_keys = apply_rotary(
        owned[:, query_width : query_width + key_width].reshape(rows_dev, kv_local, HEAD_SIZE),
        token_positions,
    ).astype(jnp.bfloat16)
    fresh_values = (
        owned[:, query_width + key_width :]
        .reshape(rows_dev, kv_local, HEAD_SIZE)
        .astype(jnp.bfloat16)
    )
    grouped_queries = query_rows.reshape(rows_dev, kv_local, -1, HEAD_SIZE)
    factor = 1.0 / math.sqrt(HEAD_SIZE)
    own = (
        jnp.einsum("rhgd,rhd->rhg", grouped_queries, fresh_keys, preferred_element_type=jnp.float32)
        * factor
    )
    slots = jnp.arange(cache_len)[None, None, None, :] < lengths[:, None, None, None]
    scores = (
        jnp.einsum("rhgd,rhtd->rhgt", grouped_queries, k_cache, preferred_element_type=jnp.float32)
        * factor
    )
    scores = jnp.where(slots, scores, -jnp.inf)
    weights, own_weight = softmax_weights(scores, own)
    heads = jnp.einsum("rhgt,rhtd->rhgd", weights, value_cache, preferred_element_type=jnp.float32)
    heads = (
        heads
        + own_weight.astype(jnp.float32)[..., None]
        * fresh_values.astype(jnp.float32)[:, :, None, :]
    )
    heads = heads.astype(jnp.bfloat16).reshape(rows_dev, query_width)
    partial_out = jnp.dot(
        lax.all_gather(heads, "gx", axis=0, tiled=True), w_out, preferred_element_type=jnp.float32
    )
    return lax.psum_scatter(partial_out, "gy", scatter_dimension=0, tiled=True).astype(jnp.bfloat16)


def solution(mesh):
    placed = (
        P(("groups", "gy"), "gx"),
        P("gx", "gy"),
        P("gx", "gy"),
        P("gx", "gy"),
        P("gy", "gx"),
        P(("groups", "gx"), "gy", None, None),
        P(("groups", "gx"), "gy", None, None),
        P(("groups", "gx")),
    )
    return jax.shard_map(
        body, mesh=mesh, in_specs=placed, out_specs=P(("groups", "gy"), "gx"), check_vma=False
    )
```

profile of v0, /device:TPU:0, one launch (start us, length us, event | category | flops | bytes accessed | tf_op | source)
XLA Modules:
  0.0 145.9 jit_solution(5569077212349255282)
XLA Ops:
  6.5 2.3 %all-gather = bf16[2,4,2048]{2,1,0:T(4,128)(2,1)S(1)} all-gather(bf16[1,4,2048]{2,1,0:T(4,128)(2,1)} %bitcast.42), channel_id=1, replica_groups=mesh['groups'=2,'gx'=8,'gy'=2] {'gy'}, dimensions={0}, use_global_device_ids=true | all-gather | bytes 49152 | tf_op jit(solution)/shard_map/all_gather | solution.py:43
  8.9 1.5 %fusion.24 = f32[8,256]{1,0:T(8,128)S(1)} fusion(bf16[8,2048]{1,0:T(8,128)(2,1)S(1)} %reshape.154, bf16[2048,256]{1,0:T(8,128)(2,1)} %param.11), kind=kOutput, calls=%fused_computation.45 | convolution fusion | flops 8388608 | bytes 1089536 | tf_op jit(solution)/shard_map/dot_general | solution.py:58
  10.3 1.5 %fusion.23 = f32[8,256]{1,0:T(8,128)S(1)} fusion(bf16[8,2048]{1,0:T(8,128)(2,1)S(1)} %reshape.154, bf16[2048,256]{1,0:T(8,128)(2,1)} %param.10), kind=kOutput, calls=%fused_computation.44 | convolution fusion | flops 8388608 | bytes 1089536 | tf_op jit(solution)/shard_map/dot_general | solution.py:57
  11.8 8.0 %fusion.22 = f32[8,4096]{1,0:T(8,128)S(1)} fusion(bf16[8,2048]{1,0:T(8,128)(2,1)S(1)} %reshape.154, bf16[2048,4096]{1,0:T(8,128)(2,1)} %param.9), kind=kOutput, calls=%fused_computation.43 | convolution fusion | flops 134217728 | bytes 16941056 | tf_op jit(solution)/shard_map/dot_general | solution.py:56
  19.8 0.7 pad_maximum_fusion
  20.5 0.0 all-reduce.3.cloned.1.call-update
  20.5 0.1 multiply_reduce_fusion
  21.3 23.0 %psum.15 = f32[8]{0:T(128)S(1)} all-reduce(f32[8]{0:T(128)S(1)} %multiply_reduce_fusion), channel_id=1, replica_groups=mesh['groups'=2,'gx'=8,'gy'=2] {'gx'}, use_global_device_ids=true, to_apply=%region_2.0 | all-reduce | flops 8 | bytes 64 | tf_op jit(solution)/shard_map/psum | solution.py:45
  44.3 0.1 fusion.16
  44.4 0.6 dynamic-slice
  45.6 0.6 dynamic_slice.7
  46.2 46.9 %all-reduce.3.cloned.1.call-done = f32[8,4608]{1,0:T(8,128)} async-done(((f32[8,4608]{1,0:T(8,128)}), f32[8,4608]{1,0:T(8,128)}) %all-reduce.3.cloned.1.call-update) | async-done | bytes 147472 | tf_op jit(solution)/shard_map/psum | solution.py:53
  93.1 1.6 %dynamic-slice_multiply_fusion = f32[1,4608]{1,0:T(1,128)S(1)} fusion(f32[8,4608]{1,0:T(8,128)} %all-reduce.3.cloned.1.call-done, s32[]{:T(128)S(6)} %select_n.9, f32[]{:T(128)} %bitcast.2), kind=kLoop, calls=%fused_computation.17 | loop fusion | flops 4608 | bytes 36872 | tf_op jit(solution)/shard_map/mul | solution.py:65
  94.7 0.1 fusion.14
  94.8 0.1 subtract_convert_fusion
  94.9 0.1 maximum_bitcast_fusion
  94.9 0.2 fusion.10
  95.1 0.5 fusion.21
  95.6 0.2 fusion.4
  95.9 0.3 fusion.1
  96.2 30.6 %all-gather.1 = bf16[8,1,4096]{2,1,0:T(2,128)(2,1)S(1)} all-gather(bf16[1,1,4096]{2,1,0:T(2,128)(2,1)S(1)} %reshape.155), channel_id=1, replica_groups=mesh['groups'=2,'gx'=8,'gy'=2] {'gx'}, dimensions={0}, use_global_device_ids=true | all-gather | bytes 73728 | tf_op jit(solution)/shard_map/all_gather | solution.py:100
  126.8 8.1 %fusion.7 = f32[8,2048]{1,0:T(8,128)S(1)} fusion(bf16[4096,2048]{1,0:T(8,128)(2,1)} %param.12, bf16[8,1,4096]{2,1,0:T(2,128)(2,1)S(1)} %all-gather.1), kind=kOutput, calls=%fused_computation.12 | convolution fusion | flops 134217728 | bytes 16908288 | tf_op jit(solution)/shard_map/dot_general | solution.py:99
  134.8 3.6 %all-reduce = bf16[8,2048]{1,0:T(8,128)(2,1)S(1)} all-reduce(f32[8,2048]{1,0:T(8,128)S(1)} %fusion.7), channel_id=2, replica_groups=mesh['groups'=2,'gx'=8,'gy'=2] {'gy'}, use_global_device_ids=true, to_apply=%region_5.6.clone | all-reduce | flops 16384 | bytes 98304
  138.4 0.6 dynamic-slice_convert_fusion
  (16 shorter events, 0.1 us)
Async XLA Ops:
  6.5 88.6 %copy-start = (bf16[1,2,2048,128]{3,2,1,0:T(8,128)(2,1)S(1)}, bf16[1,2,2048,128]{3,2,1,0:T(8,128)(2,1)}, u32[]{:S(2)}) copy-start(bf16[1,2,2048,128]{3,2,1,0:T(8,128)(2,1)} %param.13) | copy-start | bytes 3145732
  6.5 37.9 %copy-start.2 = (u32[32]{0:T(128)S(1)}, u32[32]{0:T(128)}, u32[]{:S(2)}) copy-start(u32[32]{0:T(128)} %constant.35) | copy-start | bytes 388
  6.5 89.3 %copy-start.1 = (bf16[1,2,2048,128]{3,2,1,0:T(8,128)(2,1)S(1)}, bf16[1,2,2048,128]{3,2,1,0:T(8,128)(2,1)}, u32[]{:S(2)}) copy-start(bf16[1,2,2048,128]{3,2,1,0:T(8,128)(2,1)} %param.14) | copy-start | bytes 3145732
  6.5 86.5 %all-reduce.3.cloned.1.call-start = ((), (), s32[]{:S(2)}) async-start(), calls=%async_computation | async-start | bytes 294912 | tf_op jit(solution)/shard_map/psum | solution.py:53
Sparse Core Ops, SparseCore 0:
  20.7 72.3 all-reduce.2
where the time goes:
time: 146 us
  blocking collectives  59.4 us (41%)
  waiting for transfers between devices  46.9 us (32%)
  matrix products  20.1 us (14%)
  between operations  14.8 us (10%)
  other arithmetic  2.9 us (2%)
  local copies, waits for them, and re-layouts  1.84 us (1%)
    psum x1, waiting for transfers between devices, body(): lax.psum(jnp.concatenate([jnp.dot(rows_all, w_query, preferred_element_ty...  46.9 us
    all_gather x1, blocking collectives, body(): lax.all_gather(heads, 'gx', axis=0, tiled=True)  30.6 us
    psum x1, blocking collectives, body(): squares = lax.psum(jnp.sum(widened * widened, axis=1), 'gx')  23 us
    dot_general x1, matrix products, body(): jnp.dot(lax.all_gather(heads, 'gx', axis=0, tiled=True), w_out, preferred...  8.05 us
    dot_general x1, matrix products, body(): jnp.dot(rows_all, w_query, preferred_element_type=jnp.float32)  8.05 us
    unnamed x1, blocking collectives  3.61 us
  transfers between devices with their start and end apart: 1, of which 1 were waited for; matrix products, arithmetic and copies ran while one was open for 1% of the time, Pallas kernels for 0%

commit v1 on v0

--- a/solution.py
+++ b/solution.py
@@ -39,30 +39,53 @@
     )
 
 
-def body(activations, w_query, key_weight, value_weight, w_out, k_cache, value_cache, lengths):
-    rows_all = lax.all_gather(activations, "gy", axis=0, tiled=True)
+def swap_pair(block):
+    return lax.ppermute(block, "gy", [(0, 1), (1, 0)])
+
+
+def to_owner(pieces, devices):
+    total = pieces[0]
+    moved = [
+        lax.ppermute(pieces[k], "gx", [(i, (i + k) % devices) for i in range(devices)])
+        for k in range(1, devices)
+    ]
+    for piece in moved:
+        total = total + piece
+    return total
+
+
+def body(devices, activations, w_query, key_weight, value_weight, w_out, k_cache, value_cache, lengths):
+    gx = lax.axis_index("gx")
+    gy = lax.axis_index("gy")
+    other = swap_pair(activations)
+    rows_all = jnp.where(
+        gy == 0,
+        jnp.concatenate([activations, other], axis=0),
+        jnp.concatenate([other, activations], axis=0),
+    )
     widened = rows_all.astype(jnp.float32)
-    squares = lax.psum(jnp.sum(widened * widened, axis=1), "gx")
-    scale_rows = lax.rsqrt(squares / MODEL_WIDTH + 1e-05)
+    squares = jnp.sum(widened * widened, axis=1, keepdims=True)
     rows_dev = k_cache.shape[0]
     kv_local = k_cache.shape[1]
     cache_len = k_cache.shape[2]
     query_width = w_query.shape[1]
     key_width = key_weight.shape[1]
-    first_row = lax.axis_index("gx") * rows_dev
-    summed = lax.psum(
-        jnp.concatenate(
-            [
-                jnp.dot(rows_all, w_query, preferred_element_type=jnp.float32),
-                jnp.dot(rows_all, key_weight, preferred_element_type=jnp.float32),
-                jnp.dot(rows_all, value_weight, preferred_element_type=jnp.float32),
-            ],
-            axis=1,
-        ),
-        "gx",
+    partial = jnp.concatenate(
+        [
+            jnp.dot(rows_all, w_query, preferred_element_type=jnp.float32),
+            jnp.dot(rows_all, key_weight, preferred_element_type=jnp.float32),
+            jnp.dot(rows_all, value_weight, preferred_element_type=jnp.float32),
+            jnp.broadcast_to(squares, (squares.shape[0], HEAD_SIZE)),
+        ],
+        axis=1,
     )
-    owned = lax.dynamic_slice_in_dim(summed, first_row, rows_dev, 0)
-    owned = owned * lax.dynamic_slice_in_dim(scale_rows, first_row, rows_dev, 0)[:, None]
+    pieces = [
+        lax.dynamic_slice_in_dim(partial, lax.rem(gx + k, devices) * rows_dev, rows_dev, 0)
+        for k in range(devices)
+    ]
+    owned = to_owner(pieces, devices)
+    scale_rows = lax.rsqrt(owned[:, -1] / MODEL_WIDTH + 1e-05)
+    owned = owned[:, :-HEAD_SIZE] * scale_rows[:, None]
     token_positions = lengths.astype(jnp.float32)
     query_rows = apply_rotary(
         owned[:, :query_width].reshape(rows_dev, -1, HEAD_SIZE), token_positions
@@ -96,10 +119,17 @@
         * fresh_values.astype(jnp.float32)[:, :, None, :]
     )
     heads = heads.astype(jnp.bfloat16).reshape(rows_dev, query_width)
-    partial_out = jnp.dot(
-        lax.all_gather(heads, "gx", axis=0, tiled=True), w_out, preferred_element_type=jnp.float32
-    )
-    return lax.psum_scatter(partial_out, "gy", scatter_dimension=0, tiled=True).astype(jnp.bfloat16)
+    arrived = [heads] + [
+        lax.ppermute(heads, "gx", [(i, (i - k) % devices) for i in range(devices)])
+        for k in range(1, devices)
+    ]
+    turned = jnp.concatenate(arrived, axis=0)
+    partial_out = jnp.dot(turned, w_out, preferred_element_type=jnp.float32)
+    partial_out = jnp.roll(partial_out, gx * rows_dev, axis=0)
+    half = partial_out.shape[0] // 2
+    mine = lax.dynamic_slice_in_dim(partial_out, gy * half, half, 0)
+    theirs = lax.dynamic_slice_in_dim(partial_out, (1 - gy) * half, half, 0)
+    return (mine + swap_pair(theirs)).astype(jnp.bfloat16)
 
 
 def solution(mesh):
@@ -113,6 +143,10 @@
         P(("groups", "gx"), "gy", None, None),
         P(("groups", "gx")),
     )
+
+    def run(*args):
+        return body(mesh.shape["gx"], *args)
+
     return jax.shard_map(
-        body, mesh=mesh, in_specs=placed, out_specs=P(("groups", "gy"), "gx"), check_vma=False
+        run, mesh=mesh, in_specs=placed, out_specs=P(("groups", "gy"), "gx"), check_vma=False
     )

time: 146 us -> 56.7 us (0.39)
  blocking collectives: 59.4 us -> 0 us
  waiting for transfers between devices: 46.9 us -> 6.74 us
  starting transfers between devices: 0.01 us -> 25.8 us
  between operations: 14.8 us -> 1.72 us
    psum x1 -> x0, waiting for transfers between devices: 46.9 us -> none  [body(): lax.psum(jnp.concatenate([jnp.dot(rows_all, w_query, preferred_element_ty...]
    all_gather x2 -> x0, blocking collectives: 32.8 us -> none  [the longest x1 30.6 us: body(): lax.all_gather(heads, 'gx', axis=0, tiled=True)]
    ppermute x0 -> x16, starting transfers between devices: none -> 25.8 us  [the longest x7 13.7 us: to_owner(): lax.ppermute(pieces[k], 'gx', [(i, (i + k) % devices) for i in range(devi...]
    psum x1 -> x0, blocking collectives: 23 us -> none  [body(): squares = lax.psum(jnp.sum(widened * widened, axis=1), 'gx')]
    ppermute x0 -> x16, waiting for transfers between devices: none -> 6.74 us  [the longest x7 3.13 us: body(): lax.ppermute(heads, 'gx', [(i, (i - k) % devices) for i in range(devices)])]
    unnamed x1 -> x0, blocking collectives: 3.61 us -> none
    mul x1, other arithmetic: 1.58 us -> 0.02 us  [body(): owned = owned[:, :-HEAD_SIZE] * scale_rows[:, None]]
  transfers between devices with their start and end apart: 1 -> 16, of which waited for: 1 -> 7; matrix products, arithmetic and copies ran while one was open for 1% -> 0% of each run, Pallas kernels for 0% -> 0%
where the time goes in v1:
time: 56.7 us; the launch traced here: 56.4 us
  starting transfers between devices  25.8 us (46%)
  matrix products  18.9 us (33%)
  waiting for transfers between devices  6.74 us (12%)
  other arithmetic  2.22 us (4%)
  between operations  1.72 us (3%)
  local copies, waits for them, and re-layouts  0.98 us (2%)
    ppermute x7, starting transfers between devices, to_owner(): lax.ppermute(pieces[k], 'gx', [(i, (i + k) % devices) for i in range(devi...  13.7 us
    ppermute x7, starting transfers between devices, body(): lax.ppermute(heads, 'gx', [(i, (i - k) % devices) for i in range(devices)])  11.6 us
    dot_general x1, matrix products, body(): jnp.dot(rows_all, w_query, preferred_element_type=jnp.float32)  8.07 us
    dot_general x1, matrix products, body(): partial_out = jnp.dot(turned, w_out, preferred_element_type=jnp.float32)  8.04 us
    ppermute x7, waiting for transfers between devices, body(): lax.ppermute(heads, 'gx', [(i, (i - k) % devices) for i in range(devices)])  3.13 us
    ppermute x7, waiting for transfers between devices, to_owner(): lax.ppermute(pieces[k], 'gx', [(i, (i + k) % devices) for i in range(devi...  2.25 us
    dot_general x1, matrix products, body(): jnp.einsum('rhgt,rhtd->rhgd', weights, value_cache, preferred_element_typ...  1.55 us
    ppermute x2, waiting for transfers between devices, swap_pair(): return lax.ppermute(block, 'gy', [(0, 1), (1, 0)])  1.36 us
  transfers between devices with their start and end apart: 16, of which 7 were waited for; matrix products, arithmetic and copies ran while one was open for 0% of the time, Pallas kernels for 0%

profile of v1, /device:TPU:0, one launch (start us, length us, event | category | flops | bytes accessed | tf_op | source)
XLA Modules:
  0.0 56.4 jit_solution(13720336200372512177)
XLA Ops:
  1.6 0.9 %multiply_reduce_fusion = f32[8]{0:T(128)S(1)} fusion(bf16[4,2048]{1,0:T(4,128)(2,1)} %param.8, bf16[4,2048]{1,0:T(4,128)(2,1)S(1)} %collective-permute-done, pred[]{:T(512)S(6)} %eq.6), kind=kLoop, calls=%fused_computation.16 | loop fusion | flops 196600 | bytes 32801 | tf_op jit(solution)/shard_map/reduce_sum | solution.py:67
  2.5 8.1 %fusion.24 = f32[8,4096]{1,0:T(8,128)S(1)} fusion(bf16[2048,4096]{1,0:T(8,128)(2,1)} %param.9, bf16[4,2048]{1,0:T(4,128)(2,1)S(1)} %collective-permute-done, bf16[4,2048]{1,0:T(4,128)(2,1)} %param.8, pred[]{:T(512)S(6)} %eq.6), kind=kOutput, calls=%fused_computation.56 | convolution fusion | flops 134365184 | bytes 16941056 | tf_op jit(solution)/shard_map/dot_general | solution.py:75
  11.3 2.9 %collective-permute-start.1 = (f32[1,4736]{1,0:T(1,128)S(1)}, f32[1,4736]{1,0:T(1,128)S(1)}, u32[]{:S(2)}, u32[]{:S(2)}) collective-permute-start(f32[1,4736]{1,0:T(1,128)S(1)} %get-tuple-element.5), channel_id=1, source_target_pairs={{0,2},{2,4},{4,6},{6,8},{8,10},{10,12},{12,14},{14,0},{1,3},{3,5},... | collective-permute-start | bytes 56840 | tf_op jit(solution)/shard_map/ppermute | solution.py:49
  14.2 1.6 %collective-permute-start.2 = (f32[1,4736]{1,0:T(1,128)S(1)}, f32[1,4736]{1,0:T(1,128)S(1)}, u32[]{:S(2)}, u32[]{:S(2)}) collective-permute-start(f32[1,4736]{1,0:T(1,128)S(1)} %get-tuple-element.11), channel_id=1, source_target_pairs={{0,4},{2,6},{4,8},{6,10},{8,12},{10,14},{12,0},{14,2},{1,5},{3,7},... | collective-permute-start | bytes 56840 | tf_op jit(solution)/shard_map/ppermute | solution.py:49
  15.8 2.6 %collective-permute-start.3 = (f32[1,4736]{1,0:T(1,128)S(1)}, f32[1,4736]{1,0:T(1,128)S(1)}, u32[]{:S(2)}, u32[]{:S(2)}) collective-permute-start(f32[1,4736]{1,0:T(1,128)S(1)} %get-tuple-element.10), channel_id=1, source_target_pairs={{0,6},{2,8},{4,10},{6,12},{8,14},{10,0},{12,2},{14,4},{1,7},{3,9},... | collective-permute-start | bytes 56840 | tf_op jit(solution)/shard_map/ppermute | solution.py:49
  18.4 1.2 %collective-permute-start.4 = (f32[1,4736]{1,0:T(1,128)S(1)}, f32[1,4736]{1,0:T(1,128)S(1)}, u32[]{:S(2)}, u32[]{:S(2)}) collective-permute-start(f32[1,4736]{1,0:T(1,128)S(1)} %get-tuple-element.9), channel_id=1, source_target_pairs={{0,8},{2,10},{4,12},{6,14},{8,0},{10,2},{12,4},{14,6},{1,9},{3,11}... | collective-permute-start | bytes 56840 | tf_op jit(solution)/shard_map/ppermute | solution.py:49
  19.6 2.6 %collective-permute-start.5 = (f32[1,4736]{1,0:T(1,128)S(1)}, f32[1,4736]{1,0:T(1,128)S(1)}, u32[]{:S(2)}, u32[]{:S(2)}) collective-permute-start(f32[1,4736]{1,0:T(1,128)S(1)} %get-tuple-element.8), channel_id=1, source_target_pairs={{0,10},{2,12},{4,14},{6,0},{8,2},{10,4},{12,6},{14,8},{1,11},{3,13... | collective-permute-start | bytes 56840 | tf_op jit(solution)/shard_map/ppermute | solution.py:49
  22.2 1.3 %collective-permute-start.6 = (f32[1,4736]{1,0:T(1,128)S(1)}, f32[1,4736]{1,0:T(1,128)S(1)}, u32[]{:S(2)}, u32[]{:S(2)}) collective-permute-start(f32[1,4736]{1,0:T(1,128)S(1)} %get-tuple-element.7), channel_id=1, source_target_pairs={{0,12},{2,14},{4,0},{6,2},{8,4},{10,6},{12,8},{14,10},{1,13},{3,15... | collective-permute-start | bytes 56840 | tf_op jit(solution)/shard_map/ppermute | solution.py:49
  23.6 1.4 %collective-permute-start.7 = (f32[1,4736]{1,0:T(1,128)S(1)}, f32[1,4736]{1,0:T(1,128)S(1)}, u32[]{:S(2)}, u32[]{:S(2)}) collective-permute-start(f32[1,4736]{1,0:T(1,128)S(1)} %get-tuple-element.6), channel_id=1, source_target_pairs={{0,14},{2,0},{4,2},{6,4},{8,6},{10,8},{12,10},{14,12},{1,15},{3,1}... | collective-permute-start | bytes 56840 | tf_op jit(solution)/shard_map/ppermute | solution.py:49
  25.1 0.9 %collective-permute-done.6 = f32[1,4736]{1,0:T(1,128)S(1)} collective-permute-done((f32[1,4736]{1,0:T(1,128)S(1)}, f32[1,4736]{1,0:T(1,128)S(1)}, u32[]{:S(2)}, u32[]{:S(2)}) %collective-permute-start.6) | collective-permute-done | bytes 18976 | tf_op jit(solution)/shard_map/ppermute | solution.py:49
  26.0 1.4 %collective-permute-done.7 = f32[1,4736]{1,0:T(1,128)S(1)} collective-permute-done((f32[1,4736]{1,0:T(1,128)S(1)}, f32[1,4736]{1,0:T(1,128)S(1)}, u32[]{:S(2)}, u32[]{:S(2)}) %collective-permute-start.7) | collective-permute-done | bytes 18976 | tf_op jit(solution)/shard_map/ppermute | solution.py:49
  29.9 1.5 %fusion.1 = bf16[2,16,128]{2,1,0:T(8,128)(2,1)S(1)} fusion(bf16[1,2,2048,128]{3,2,1,0:T(8,128)(2,1)} %param.14, f32[2,16,2048]{2,1,0:T(8,128)S(1)} %get-tuple-element.19, f32[2,16]{1,0:T(2,128)S(1)} %get-tuple-element.15, f32[2,16]{1,0:T(2,128)S(1)} %multiply_maximum_fusion, f32[2,128]{1,0:T(2,128)S(1)} %bitcast.38, f32[2,16]{1,0:T(2,128)S(1)} %get-tuple-element.14), kind=kOutput, calls=%fused_computation.3 | convolution fusion | flops 16986112 | bytes 1320320 | tf_op jit(solution)/shard_map/rhgt,rhtd->rhgd/dot_general | solution.py:115
  31.5 1.4 %collective-permute-start.10 = (bf16[1,4096]{1,0:T(2,128)(2,1)S(1)}, bf16[1,4096]{1,0:T(2,128)(2,1)S(1)}, u32[]{:S(2)}, u32[]{:S(2)}) collective-permute-start(bf16[1,4096]{1,0:T(2,128)(2,1)S(1)} %reshape.158), channel_id=1, source_target_pairs={{0,10},{2,12},{4,14},{6,0},{8,2},{10,4},{12,6},{14,8},{1,11},{3,13... | collective-permute-start | bytes 24584 | tf_op jit(solution)/shard_map/ppermute | solution.py:123
  32.8 2.6 %collective-permute-start.11 = (bf16[1,4096]{1,0:T(2,128)(2,1)S(1)}, bf16[1,4096]{1,0:T(2,128)(2,1)S(1)}, u32[]{:S(2)}, u32[]{:S(2)}) collective-permute-start(bf16[1,4096]{1,0:T(2,128)(2,1)S(1)} %reshape.158), channel_id=1, source_target_pairs={{0,8},{2,10},{4,12},{6,14},{8,0},{10,2},{12,4},{14,6},{1,9},{3,11}... | collective-permute-start | bytes 24584 | tf_op jit(solution)/shard_map/ppermute | solution.py:123
  35.4 0.9 %collective-permute-start.12 = (bf16[1,4096]{1,0:T(2,128)(2,1)S(1)}, bf16[1,4096]{1,0:T(2,128)(2,1)S(1)}, u32[]{:S(2)}, u32[]{:S(2)}) collective-permute-start(bf16[1,4096]{1,0:T(2,128)(2,1)S(1)} %reshape.158), channel_id=1, source_target_pairs={{0,6},{2,8},{4,10},{6,12},{8,14},{10,0},{12,2},{14,4},{1,7},{3,9},... | collective-permute-start | bytes 24584 | tf_op jit(solution)/shard_map/ppermute | solution.py:123
  36.3 1.4 %collective-permute-start.13 = (bf16[1,4096]{1,0:T(2,128)(2,1)S(1)}, bf16[1,4096]{1,0:T(2,128)(2,1)S(1)}, u32[]{:S(2)}, u32[]{:S(2)}) collective-permute-start(bf16[1,4096]{1,0:T(2,128)(2,1)S(1)} %reshape.158), channel_id=1, source_target_pairs={{0,4},{2,6},{4,8},{6,10},{8,12},{10,14},{12,0},{14,2},{1,5},{3,7},... | collective-permute-start | bytes 24584 | tf_op jit(solution)/shard_map/ppermute | solution.py:123
  37.7 2.9 %collective-permute-start.14 = (bf16[1,4096]{1,0:T(2,128)(2,1)S(1)}, bf16[1,4096]{1,0:T(2,128)(2,1)S(1)}, u32[]{:S(2)}, u32[]{:S(2)}) collective-permute-start(bf16[1,4096]{1,0:T(2,128)(2,1)S(1)} %reshape.158), channel_id=1, source_target_pairs={{0,2},{2,4},{4,6},{6,8},{8,10},{10,12},{12,14},{14,0},{1,3},{3,5},... | collective-permute-start | bytes 24584 | tf_op jit(solution)/shard_map/ppermute | solution.py:123
  40.6 1.8 %collective-permute-start.8 = (bf16[1,4096]{1,0:T(2,128)(2,1)S(1)}, bf16[1,4096]{1,0:T(2,128)(2,1)S(1)}, u32[]{:S(2)}, u32[]{:S(2)}) collective-permute-start(bf16[1,4096]{1,0:T(2,128)(2,1)S(1)} %reshape.158), channel_id=1, source_target_pairs={{0,14},{2,0},{4,2},{6,4},{8,6},{10,8},{12,10},{14,12},{1,15},{3,1}... | collective-permute-start | bytes 24584 | tf_op jit(solution)/shard_map/ppermute | solution.py:123
  42.4 0.6 %collective-permute-start.9 = (bf16[1,4096]{1,0:T(2,128)(2,1)S(1)}, bf16[1,4096]{1,0:T(2,128)(2,1)S(1)}, u32[]{:S(2)}, u32[]{:S(2)}) collective-permute-start(bf16[1,4096]{1,0:T(2,128)(2,1)S(1)} %reshape.158), channel_id=1, source_target_pairs={{0,12},{2,14},{4,0},{6,2},{8,4},{10,6},{12,8},{14,10},{1,13},{3,15... | collective-permute-start | bytes 24584 | tf_op jit(solution)/shard_map/ppermute | solution.py:123
  43.1 1.1 %collective-permute-done.14 = bf16[1,4096]{1,0:T(2,128)(2,1)S(1)} collective-permute-done((bf16[1,4096]{1,0:T(2,128)(2,1)S(1)}, bf16[1,4096]{1,0:T(2,128)(2,1)S(1)}, u32[]{:S(2)}, u32[]{:S(2)}) %collective-permute-start.14) | collective-permute-done | bytes 8224 | tf_op jit(solution)/shard_map/ppermute | solution.py:123
  44.4 1.8 %collective-permute-done.9 = bf16[1,4096]{1,0:T(2,128)(2,1)S(1)} collective-permute-done((bf16[1,4096]{1,0:T(2,128)(2,1)S(1)}, bf16[1,4096]{1,0:T(2,128)(2,1)S(1)}, u32[]{:S(2)}, u32[]{:S(2)}) %collective-permute-start.9) | collective-permute-done | bytes 8224 | tf_op jit(solution)/shard_map/ppermute | solution.py:123
  46.4 8.0 %fusion.26 = f32[8,2048]{1,0:T(8,128)S(1)} fusion(bf16[8,4096]{1,0:T(8,128)(2,1)S(1)} %concatenate.49, bf16[4096,2048]{1,0:T(8,128)(2,1)} %param.12), kind=kOutput, calls=%fused_computation.58 | convolution fusion | flops 134217728 | bytes 16908288 | tf_op jit(solution)/shard_map/dot_general | solution.py:127
  54.5 1.2 %collective-permute-done.15 = f32[4,2048]{1,0:T(4,128)S(1)} collective-permute-done((f32[4,2048]{1,0:T(4,128)S(1)}, f32[4,2048]{1,0:T(4,128)S(1)}, u32[]{:S(2)}, u32[]{:S(2)}) %collective-permute-start.15) | collective-permute-done | bytes 32800 | tf_op jit(solution)/shard_map/ppermute | solution.py:43
  55.7 0.6 %fusion.10 = bf16[4,2048]{1,0:T(4,128)(2,1)} fusion(f32[4,2048]{1,0:T(4,128)S(1)} %collective-permute-done.15, s32[]{:T(128)S(6)} %dynamic_slice.46, f32[8,2048]{1,0:T(8,128)S(1)} %fusion.26), kind=kLoop, calls=%fused_computation.20 | loop fusion | flops 24576 | bytes 114692 | tf_op jit(solution)/shard_map/convert_element_type | solution.py:132
  (45 shorter events, 3.8 us)
Async XLA Ops:
  0.0 29.2 %copy-start = (bf16[1,2,2048,128]{3,2,1,0:T(8,128)(2,1)S(1)}, bf16[1,2,2048,128]{3,2,1,0:T(8,128)(2,1)}, u32[]{:S(2)}) copy-start(bf16[1,2,2048,128]{3,2,1,0:T(8,128)(2,1)} %param.13) | copy-start | bytes 3145732
  0.0 10.6 %copy-start.3 = (bf16[4,2048]{1,0:T(4,128)(2,1)S(1)}, bf16[4,2048]{1,0:T(4,128)(2,1)}, u32[]{:S(2)}) copy-start(bf16[4,2048]{1,0:T(4,128)(2,1)} %param.8) | copy-start | bytes 49156
  0.0 10.6 %copy-start.1 = (bf16[2048,256]{1,0:T(8,128)(2,1)S(1)}, bf16[2048,256]{1,0:T(8,128)(2,1)}, u32[]{:S(2)}) copy-start(bf16[2048,256]{1,0:T(8,128)(2,1)} %param.11) | copy-start | bytes 3145732
  0.0 10.9 %copy-start.2 = (bf16[2048,256]{1,0:T(8,128)(2,1)S(1)}, bf16[2048,256]{1,0:T(8,128)(2,1)}, u32[]{:S(2)}) copy-start(bf16[2048,256]{1,0:T(8,128)(2,1)} %param.10) | copy-start | bytes 3145732
  0.0 1.6 %collective-permute-start = (bf16[4,2048]{1,0:T(4,128)(2,1)}, bf16[4,2048]{1,0:T(4,128)(2,1)S(1)}, u32[]{:S(2)}, u32[]{:S(2)}) collective-permute-start(bf16[4,2048]{1,0:T(4,128)(2,1)} %param.8), channel_id=1, source_target_pairs={{0,1},{1,0},{2,3},{3,2},{4,5},{5,4},{6,7},{7,6},{8,9},{9,8},{10,11... | collective-permute-start | bytes 49160 | tf_op jit(solution)/shard_map/ppermute | solution.py:43
  11.3 10.9 %collective-permute-start.1 = (f32[1,4736]{1,0:T(1,128)S(1)}, f32[1,4736]{1,0:T(1,128)S(1)}, u32[]{:S(2)}, u32[]{:S(2)}) collective-permute-start(f32[1,4736]{1,0:T(1,128)S(1)} %get-tuple-element.5), channel_id=1, source_target_pairs={{0,2},{2,4},{4,6},{6,8},{8,10},{10,12},{12,14},{14,0},{1,3},{3,5},... | collective-permute-start | bytes 56840 | tf_op jit(solution)/shard_map/ppermute | solution.py:49
  14.2 9.4 %collective-permute-start.2 = (f32[1,4736]{1,0:T(1,128)S(1)}, f32[1,4736]{1,0:T(1,128)S(1)}, u32[]{:S(2)}, u32[]{:S(2)}) collective-permute-start(f32[1,4736]{1,0:T(1,128)S(1)} %get-tuple-element.11), channel_id=1, source_target_pairs={{0,4},{2,6},{4,8},{6,10},{8,12},{10,14},{12,0},{14,2},{1,5},{3,7},... | collective-permute-start | bytes 56840 | tf_op jit(solution)/shard_map/ppermute | solution.py:49
  15.8 9.3 %collective-permute-start.3 = (f32[1,4736]{1,0:T(1,128)S(1)}, f32[1,4736]{1,0:T(1,128)S(1)}, u32[]{:S(2)}, u32[]{:S(2)}) collective-permute-start(f32[1,4736]{1,0:T(1,128)S(1)} %get-tuple-element.10), channel_id=1, source_target_pairs={{0,6},{2,8},{4,10},{6,12},{8,14},{10,0},{12,2},{14,4},{1,7},{3,9},... | collective-permute-start | bytes 56840 | tf_op jit(solution)/shard_map/ppermute | solution.py:49
  18.4 6.7 %collective-permute-start.4 = (f32[1,4736]{1,0:T(1,128)S(1)}, f32[1,4736]{1,0:T(1,128)S(1)}, u32[]{:S(2)}, u32[]{:S(2)}) collective-permute-start(f32[1,4736]{1,0:T(1,128)S(1)} %get-tuple-element.9), channel_id=1, source_target_pairs={{0,8},{2,10},{4,12},{6,14},{8,0},{10,2},{12,4},{14,6},{1,9},{3,11}... | collective-permute-start | bytes 56840 | tf_op jit(solution)/shard_map/ppermute | solution.py:49
  19.6 5.5 %collective-permute-start.5 = (f32[1,4736]{1,0:T(1,128)S(1)}, f32[1,4736]{1,0:T(1,128)S(1)}, u32[]{:S(2)}, u32[]{:S(2)}) collective-permute-start(f32[1,4736]{1,0:T(1,128)S(1)} %get-tuple-element.8), channel_id=1, source_target_pairs={{0,10},{2,12},{4,14},{6,0},{8,2},{10,4},{12,6},{14,8},{1,11},{3,13... | collective-permute-start | bytes 56840 | tf_op jit(solution)/shard_map/ppermute | solution.py:49
  22.2 3.8 %collective-permute-start.6 = (f32[1,4736]{1,0:T(1,128)S(1)}, f32[1,4736]{1,0:T(1,128)S(1)}, u32[]{:S(2)}, u32[]{:S(2)}) collective-permute-start(f32[1,4736]{1,0:T(1,128)S(1)} %get-tuple-element.7), channel_id=1, source_target_pairs={{0,12},{2,14},{4,0},{6,2},{8,4},{10,6},{12,8},{14,10},{1,13},{3,15... | collective-permute-start | bytes 56840 | tf_op jit(solution)/shard_map/ppermute | solution.py:49
  23.6 3.8 %collective-permute-start.7 = (f32[1,4736]{1,0:T(1,128)S(1)}, f32[1,4736]{1,0:T(1,128)S(1)}, u32[]{:S(2)}, u32[]{:S(2)}) collective-permute-start(f32[1,4736]{1,0:T(1,128)S(1)} %get-tuple-element.6), channel_id=1, source_target_pairs={{0,14},{2,0},{4,2},{6,4},{8,6},{10,8},{12,10},{14,12},{1,15},{3,1}... | collective-permute-start | bytes 56840 | tf_op jit(solution)/shard_map/ppermute | solution.py:49
  31.5 9.1 %collective-permute-start.10 = (bf16[1,4096]{1,0:T(2,128)(2,1)S(1)}, bf16[1,4096]{1,0:T(2,128)(2,1)S(1)}, u32[]{:S(2)}, u32[]{:S(2)}) collective-permute-start(bf16[1,4096]{1,0:T(2,128)(2,1)S(1)} %reshape.158), channel_id=1, source_target_pairs={{0,10},{2,12},{4,14},{6,0},{8,2},{10,4},{12,6},{14,8},{1,11},{3,13... | collective-permute-start | bytes 24584 | tf_op jit(solution)/shard_map/ppermute | solution.py:123
  32.8 9.6 %collective-permute-start.11 = (bf16[1,4096]{1,0:T(2,128)(2,1)S(1)}, bf16[1,4096]{1,0:T(2,128)(2,1)S(1)}, u32[]{:S(2)}, u32[]{:S(2)}) collective-permute-start(bf16[1,4096]{1,0:T(2,128)(2,1)S(1)} %reshape.158), channel_id=1, source_target_pairs={{0,8},{2,10},{4,12},{6,14},{8,0},{10,2},{12,4},{14,6},{1,9},{3,11}... | collective-permute-start | bytes 24584 | tf_op jit(solution)/shard_map/ppermute | solution.py:123
  35.4 7.6 %collective-permute-start.12 = (bf16[1,4096]{1,0:T(2,128)(2,1)S(1)}, bf16[1,4096]{1,0:T(2,128)(2,1)S(1)}, u32[]{:S(2)}, u32[]{:S(2)}) collective-permute-start(bf16[1,4096]{1,0:T(2,128)(2,1)S(1)} %reshape.158), channel_id=1, source_target_pairs={{0,6},{2,8},{4,10},{6,12},{8,14},{10,0},{12,2},{14,4},{1,7},{3,9},... | collective-permute-start | bytes 24584 | tf_op jit(solution)/shard_map/ppermute | solution.py:123
  36.3 6.8 %collective-permute-start.13 = (bf16[1,4096]{1,0:T(2,128)(2,1)S(1)}, bf16[1,4096]{1,0:T(2,128)(2,1)S(1)}, u32[]{:S(2)}, u32[]{:S(2)}) collective-permute-start(bf16[1,4096]{1,0:T(2,128)(2,1)S(1)} %reshape.158), channel_id=1, source_target_pairs={{0,4},{2,6},{4,8},{6,10},{8,12},{10,14},{12,0},{14,2},{1,5},{3,7},... | collective-permute-start | bytes 24584 | tf_op jit(solution)/shard_map/ppermute | solution.py:123
  37.7 6.4 %collective-permute-start.14 = (bf16[1,4096]{1,0:T(2,128)(2,1)S(1)}, bf16[1,4096]{1,0:T(2,128)(2,1)S(1)}, u32[]{:S(2)}, u32[]{:S(2)}) collective-permute-start(bf16[1,4096]{1,0:T(2,128)(2,1)S(1)} %reshape.158), channel_id=1, source_target_pairs={{0,2},{2,4},{4,6},{6,8},{8,10},{10,12},{12,14},{14,0},{1,3},{3,5},... | collective-permute-start | bytes 24584 | tf_op jit(solution)/shard_map/ppermute | solution.py:123
  40.6 3.7 %collective-permute-start.8 = (bf16[1,4096]{1,0:T(2,128)(2,1)S(1)}, bf16[1,4096]{1,0:T(2,128)(2,1)S(1)}, u32[]{:S(2)}, u32[]{:S(2)}) collective-permute-start(bf16[1,4096]{1,0:T(2,128)(2,1)S(1)} %reshape.158), channel_id=1, source_target_pairs={{0,14},{2,0},{4,2},{6,4},{8,6},{10,8},{12,10},{14,12},{1,15},{3,1}... | collective-permute-start | bytes 24584 | tf_op jit(solution)/shard_map/ppermute | solution.py:123
  42.4 3.7 %collective-permute-start.9 = (bf16[1,4096]{1,0:T(2,128)(2,1)S(1)}, bf16[1,4096]{1,0:T(2,128)(2,1)S(1)}, u32[]{:S(2)}, u32[]{:S(2)}) collective-permute-start(bf16[1,4096]{1,0:T(2,128)(2,1)S(1)} %reshape.158), channel_id=1, source_target_pairs={{0,12},{2,14},{4,0},{6,2},{8,4},{10,6},{12,8},{14,10},{1,13},{3,15... | collective-permute-start | bytes 24584 | tf_op jit(solution)/shard_map/ppermute | solution.py:123
  54.5 1.3 %collective-permute-start.15 = (f32[4,2048]{1,0:T(4,128)S(1)}, f32[4,2048]{1,0:T(4,128)S(1)}, u32[]{:S(2)}, u32[]{:S(2)}) collective-permute-start(f32[4,2048]{1,0:T(4,128)S(1)} %fusion.7), channel_id=1, source_target_pairs={{0,1},{1,0},{2,3},{3,2},{4,5},{5,4},{6,7},{7,6},{8,9},{9,8},{10,11... | collective-permute-start | bytes 98312 | tf_op jit(solution)/shard_map/ppermute | solution.py:43

commit v2 on v1

--- a/solution.py
+++ b/solution.py
@@ -43,19 +43,7 @@
     return lax.ppermute(block, "gy", [(0, 1), (1, 0)])
 
 
-def to_owner(pieces, devices):
-    total = pieces[0]
-    moved = [
-        lax.ppermute(pieces[k], "gx", [(i, (i + k) % devices) for i in range(devices)])
-        for k in range(1, devices)
-    ]
-    for piece in moved:
-        total = total + piece
-    return total
-
-
 def body(devices, activations, w_query, key_weight, value_weight, w_out, k_cache, value_cache, lengths):
-    gx = lax.axis_index("gx")
     gy = lax.axis_index("gy")
     other = swap_pair(activations)
     rows_all = jnp.where(
@@ -79,11 +67,8 @@
         ],
         axis=1,
     )
-    pieces = [
-        lax.dynamic_slice_in_dim(partial, lax.rem(gx + k, devices) * rows_dev, rows_dev, 0)
-        for k in range(devices)
-    ]
-    owned = to_owner(pieces, devices)
+    blocks = partial.reshape(devices, rows_dev, partial.shape[1])
+    owned = jnp.sum(lax.all_to_all(blocks, "gx", 0, 0, tiled=True), axis=0)
     scale_rows = lax.rsqrt(owned[:, -1] / MODEL_WIDTH + 1e-05)
     owned = owned[:, :-HEAD_SIZE] * scale_rows[:, None]
     token_positions = lengths.astype(jnp.float32)
@@ -119,13 +104,9 @@
         * fresh_values.astype(jnp.float32)[:, :, None, :]
     )
     heads = heads.astype(jnp.bfloat16).reshape(rows_dev, query_width)
-    arrived = [heads] + [
-        lax.ppermute(heads, "gx", [(i, (i - k) % devices) for i in range(devices)])
-        for k in range(1, devices)
-    ]
-    turned = jnp.concatenate(arrived, axis=0)
-    partial_out = jnp.dot(turned, w_out, preferred_element_type=jnp.float32)
-    partial_out = jnp.roll(partial_out, gx * rows_dev, axis=0)
+    copies = jnp.broadcast_to(heads, (devices, rows_dev, query_width))
+    everyone = lax.all_to_all(copies, "gx", 0, 0, tiled=True).reshape(-1, query_width)
+    partial_out = jnp.dot(everyone, w_out, preferred_element_type=jnp.float32)
     half = partial_out.shape[0] // 2
     mine = lax.dynamic_slice_in_dim(partial_out, gy * half, half, 0)
     theirs = lax.dynamic_slice_in_dim(partial_out, (1 - gy) * half, half, 0)

time: 56.7 us -> 53.9 us (0.951)
  starting transfers between devices: 25.8 us -> 11.1 us
  waiting for transfers between devices: 6.74 us -> 16 us
  local copies, waits for them, and re-layouts: 0.98 us -> 2.82 us
  other arithmetic: 2.22 us -> 3.24 us
    ppermute x14 -> x0, starting transfers between devices: 25.2 us -> none  [the longest x7 13.7 us: to_owner(): lax.ppermute(pieces[k], 'gx', [(i, (i + k) % devices) for i in range(devi...]
    all_to_all x0 -> x2, waiting for transfers between devices: none -> 13.7 us  [the longest x1 6.89 us: body(): owned = jnp.sum(lax.all_to_all(blocks, 'gx', 0, 0, tiled=True), axis=0)]
    all_to_all x0 -> x2, starting transfers between devices: none -> 10.5 us  [the longest x1 7.15 us: body(): owned = jnp.sum(lax.all_to_all(blocks, 'gx', 0, 0, tiled=True), axis=0)]
    ppermute x14 -> x0, waiting for transfers between devices: 5.38 us -> none  [the longest x7 3.13 us: body(): lax.ppermute(heads, 'gx', [(i, (i - k) % devices) for i in range(devices)])]
    broadcast_in_dim x0 -> x1, other arithmetic: none -> 1.01 us  [body(): copies = jnp.broadcast_to(heads, (devices, rows_dev, query_width))]
    ppermute x2, waiting for transfers between devices: 1.36 us -> 2.24 us  [swap_pair(): return lax.ppermute(block, 'gy', [(0, 1), (1, 0)])]
    reshape x1, local copies, waits for them, and re-layouts: 0.01 us -> 0.82 us  [body(): blocks = partial.reshape(devices, rows_dev, partial.shape[1])]
    unnamed x8 -> x10, local copies, waits for them, and re-layouts: 0.02 us -> 0.73 us
  transfers between devices with their start and end apart: 16 -> 4, of which waited for: 7 -> 4; matrix products, arithmetic and copies ran while one was open for 0% -> 0% of each run, Pallas kernels for 0% -> 0%
where the time goes in v2:
time: 53.9 us; the launch traced here: 53.5 us
  matrix products  18.9 us (35%)
  waiting for transfers between devices  16 us (30%)
  starting transfers between devices  11.1 us (21%)
  other arithmetic  3.24 us (6%)
  local copies, waits for them, and re-layouts  2.82 us (5%)
  between operations  1.48 us (3%)
    dot_general x1, matrix products, body(): jnp.dot(rows_all, w_query, preferred_element_type=jnp.float32)  8.07 us
    dot_general x1, matrix products, body(): partial_out = jnp.dot(everyone, w_out, preferred_element_type=jnp.float32)  8.04 us
    all_to_all x1, starting transfers between devices, body(): owned = jnp.sum(lax.all_to_all(blocks, 'gx', 0, 0, tiled=True), axis=0)  7.15 us
    all_to_all x1, waiting for transfers between devices, body(): owned = jnp.sum(lax.all_to_all(blocks, 'gx', 0, 0, tiled=True), axis=0)  6.89 us
    all_to_all x1, waiting for transfers between devices, body(): lax.all_to_all(copies, 'gx', 0, 0, tiled=True).reshape(-1, query_width)  6.84 us
    all_to_all x1, starting transfers between devices, body(): lax.all_to_all(copies, 'gx', 0, 0, tiled=True).reshape(-1, query_width)  3.35 us
    ppermute x2, waiting for transfers between devices, swap_pair(): return lax.ppermute(block, 'gy', [(0, 1), (1, 0)])  2.24 us
    dot_general x1, matrix products, body(): jnp.einsum('rhgt,rhtd->rhgd', weights, value_cache, preferred_element_typ...  1.55 us
  transfers between devices with their start and end apart: 4, of which 4 were waited for; matrix products, arithmetic and copies ran while one was open for 0% of the time, Pallas kernels for 0%

profile of v2, /device:TPU:0, one launch (start us, length us, event | category | flops | bytes accessed | tf_op | source)
XLA Modules:
  0.0 53.5 jit_solution(8617030891661774043)
XLA Ops:
  0.0 0.5 collective-permute-start
  0.5 1.0 %collective-permute-done = bf16[4,2048]{1,0:T(4,128)(2,1)S(1)} collective-permute-done((bf16[4,2048]{1,0:T(4,128)(2,1)}, bf16[4,2048]{1,0:T(4,128)(2,1)S(1)}, u32[]{:S(2)}, u32[]{:S(2)}) %collective-permute-start) | collective-permute-done | bytes 16416 | tf_op jit(solution)/shard_map/ppermute | solution.py:43
  1.6 0.9 %multiply_reduce_fusion = f32[8]{0:T(128)S(1)} fusion(bf16[4,2048]{1,0:T(4,128)(2,1)} %param.8, bf16[4,2048]{1,0:T(4,128)(2,1)S(1)} %collective-permute-done, pred[]{:T(512)S(6)} %eq.3), kind=kLoop, calls=%fused_computation.15 | loop fusion | flops 196600 | bytes 32801 | tf_op jit(solution)/shard_map/reduce_sum | solution.py:55
  2.5 8.1 %fusion.23 = f32[8,4096]{1,0:T(8,128)S(1)} fusion(bf16[2048,4096]{1,0:T(8,128)(2,1)} %param.9, bf16[4,2048]{1,0:T(4,128)(2,1)S(1)} %collective-permute-done, bf16[4,2048]{1,0:T(4,128)(2,1)} %param.8, pred[]{:T(512)S(6)} %eq.3), kind=kOutput, calls=%fused_computation.45 | convolution fusion | flops 134365184 | bytes 16941056 | tf_op jit(solution)/shard_map/dot_general | solution.py:63
  10.6 0.3 fusion.21
  10.9 0.3 fusion.22
  11.2 0.8 %copy.9 = f32[8,1,4736]{2,1,0:T(1,128)} copy(f32[8,1,4736]{2,0,1:T(8,128)S(1)} %maximum_bitcast_fusion) | data formatting | bytes 303104 | tf_op jit(solution)/shard_map/reshape | solution.py:70
  12.0 7.1 %all-to-all-start = ((f32[8,1,4736]{2,1,0:T(1,128)}), f32[8,1,4736]{2,1,0:T(1,128)S(1)}, u32[]{:S(2)}, u32[]{:S(2)}) async-start(f32[8,1,4736]{2,1,0:T(1,128)} %copy.9), calls=%async_computation | async-start | bytes 303104 | tf_op jit(solution)/shard_map/all_to_all | solution.py:71
  19.9 6.9 %all-to-all-done = f32[8,1,4736]{2,1,0:T(1,128)S(1)} async-done(((f32[8,1,4736]{2,1,0:T(1,128)}), f32[8,1,4736]{2,1,0:T(1,128)S(1)}, u32[]{:S(2)}, u32[]{:S(2)}) %all-to-all-start) | async-done | bytes 151584 | tf_op jit(solution)/shard_map/all_to_all | solution.py:71
  26.8 0.1 reduce_sum.30
  26.9 0.6 %slice.38 = f32[1,1]{1,0:T(1,128)} slice(f32[1,4736]{1,0:T(1,128)S(1)} %reduce_sum.31), slice={[0:1], [4735:4736]} | slice | bytes 8 | tf_op jit(solution)/shard_map/slice | solution.py:72
  28.5 0.2 fusion.10
  28.7 0.5 fusion.24
  29.2 0.2 fusion.4
  29.4 1.6 %fusion.1 = bf16[2,16,128]{2,1,0:T(8,128)(2,1)S(1)} fusion(bf16[1,2,2048,128]{3,2,1,0:T(8,128)(2,1)} %param.14, f32[2,16,2048]{2,1,0:T(8,128)S(1)} %get-tuple-element.12, f32[2,16]{1,0:T(2,128)S(1)} %get-tuple-element.8, f32[2,16]{1,0:T(2,128)S(1)} %multiply_maximum_fusion, f32[2,128]{1,0:T(2,128)S(1)} %bitcast.44, f32[2,16]{1,0:T(2,128)S(1)} %get-tuple-element.7), kind=kOutput, calls=%fused_computation.3 | convolution fusion | flops 16986112 | bytes 1320320 | tf_op jit(solution)/shard_map/rhgt,rhtd->rhgd/dot_general | solution.py:100
  31.0 0.1 broadcast_in_dim.19
  31.1 0.5 broadcast.68
  31.6 1.0 %reduce.5 = bf16[8,4096]{1,0:T(8,128)(2,1)S(1)} reduce(bf16[8,1,4096]{2,1,0:T(2,128)(2,1)S(1)} %broadcast_in_dim.19, bf16[]{:T(256)} %broadcast.68), dimensions={1}, to_apply=%broadcast_in_dim.19.reduce_sub_computation | reduce | bytes 131074 | tf_op jit(solution)/shard_map/broadcast_in_dim | solution.py:107
  32.6 0.6 %reshape.173 = bf16[8,2,2048]{2,1,0:T(2,128)(2,1)} reshape(bf16[8,4096]{1,0:T(8,128)(2,1)S(1)} %reduce.5) | data formatting | bytes 131072
  33.3 3.3 %all-to-all-start.1 = ((bf16[8,2,2048]{2,1,0:T(2,128)(2,1)}), bf16[8,2,2048]{2,1,0:T(2,128)(2,1)S(1)}, u32[]{:S(2)}, u32[]{:S(2)}) async-start(bf16[8,2,2048]{2,1,0:T(2,128)(2,1)} %reshape.173), calls=%async_computation.1 | async-start | bytes 131072 | tf_op jit(solution)/shard_map/all_to_all | solution.py:108
  36.6 6.8 %all-to-all-done.1 = bf16[8,2,2048]{2,1,0:T(2,128)(2,1)S(1)} async-done(((bf16[8,2,2048]{2,1,0:T(2,128)(2,1)}), bf16[8,2,2048]{2,1,0:T(2,128)(2,1)S(1)}, u32[]{:S(2)}, u32[]{:S(2)}) %all-to-all-start.1) | async-done | bytes 65568 | tf_op jit(solution)/shard_map/all_to_all | solution.py:108
  43.5 8.0 %fusion.7 = f32[8,2048]{1,0:T(8,128)S(1)} fusion(bf16[4096,2048]{1,0:T(8,128)(2,1)} %param.12, bf16[8,1,4096]{2,1,0:T(2,128)(2,1)S(1)} %reshape.174), kind=kOutput, calls=%fused_computation.12 | convolution fusion | flops 134217728 | bytes 16908288 | tf_op jit(solution)/shard_map/dot_general | solution.py:109
  51.7 1.2 %collective-permute-done.1 = f32[4,2048]{1,0:T(4,128)S(1)} collective-permute-done((f32[4,2048]{1,0:T(4,128)S(1)}, f32[4,2048]{1,0:T(4,128)S(1)}, u32[]{:S(2)}, u32[]{:S(2)}) %collective-permute-start.1) | collective-permute-done | bytes 32800 | tf_op jit(solution)/shard_map/ppermute | solution.py:43
  52.9 0.6 %add_convert_fusion = bf16[4,2048]{1,0:T(4,128)(2,1)} fusion(f32[4,2048]{1,0:T(4,128)S(1)} %collective-permute-done.1, f32[8,2048]{1,0:T(8,128)S(1)} %fusion.7, s32[]{:T(128)S(6)} %select_n.22), kind=kLoop, calls=%fused_computation.17 | loop fusion | flops 16384 | bytes 81924 | tf_op jit(solution)/shard_map/convert_element_type | solution.py:113
  (25 shorter events, 0.6 us)
Async XLA Ops:
  0.0 28.7 %copy-start = (bf16[1,2,2048,128]{3,2,1,0:T(8,128)(2,1)S(1)}, bf16[1,2,2048,128]{3,2,1,0:T(8,128)(2,1)}, u32[]{:S(2)}) copy-start(bf16[1,2,2048,128]{3,2,1,0:T(8,128)(2,1)} %param.13) | copy-start | bytes 3145732
  0.0 10.6 %copy-start.3 = (bf16[4,2048]{1,0:T(4,128)(2,1)S(1)}, bf16[4,2048]{1,0:T(4,128)(2,1)}, u32[]{:S(2)}) copy-start(bf16[4,2048]{1,0:T(4,128)(2,1)} %param.8) | copy-start | bytes 49156
  0.0 10.6 %copy-start.1 = (bf16[2048,256]{1,0:T(8,128)(2,1)S(1)}, bf16[2048,256]{1,0:T(8,128)(2,1)}, u32[]{:S(2)}) copy-start(bf16[2048,256]{1,0:T(8,128)(2,1)} %param.11) | copy-start | bytes 3145732
  0.0 10.9 %copy-start.2 = (bf16[2048,256]{1,0:T(8,128)(2,1)S(1)}, bf16[2048,256]{1,0:T(8,128)(2,1)}, u32[]{:S(2)}) copy-start(bf16[2048,256]{1,0:T(8,128)(2,1)} %param.10) | copy-start | bytes 3145732
  0.0 1.6 %collective-permute-start = (bf16[4,2048]{1,0:T(4,128)(2,1)}, bf16[4,2048]{1,0:T(4,128)(2,1)S(1)}, u32[]{:S(2)}, u32[]{:S(2)}) collective-permute-start(bf16[4,2048]{1,0:T(4,128)(2,1)} %param.8), channel_id=1, source_target_pairs={{0,1},{1,0},{2,3},{3,2},{4,5},{5,4},{6,7},{7,6},{8,9},{9,8},{10,11... | collective-permute-start | bytes 49160 | tf_op jit(solution)/shard_map/ppermute | solution.py:43
  12.0 14.8 %all-to-all-start = ((f32[8,1,4736]{2,1,0:T(1,128)}), f32[8,1,4736]{2,1,0:T(1,128)S(1)}, u32[]{:S(2)}, u32[]{:S(2)}) async-start(f32[8,1,4736]{2,1,0:T(1,128)} %copy.9), calls=%async_computation | async-start | bytes 303104 | tf_op jit(solution)/shard_map/all_to_all | solution.py:71
  33.3 10.2 %all-to-all-start.1 = ((bf16[8,2,2048]{2,1,0:T(2,128)(2,1)}), bf16[8,2,2048]{2,1,0:T(2,128)(2,1)S(1)}, u32[]{:S(2)}, u32[]{:S(2)}) async-start(bf16[8,2,2048]{2,1,0:T(2,128)(2,1)} %reshape.173), calls=%async_computation.1 | async-start | bytes 131072 | tf_op jit(solution)/shard_map/all_to_all | solution.py:108
  51.6 1.3 %collective-permute-start.1 = (f32[4,2048]{1,0:T(4,128)S(1)}, f32[4,2048]{1,0:T(4,128)S(1)}, u32[]{:S(2)}, u32[]{:S(2)}) collective-permute-start(f32[4,2048]{1,0:T(4,128)S(1)} %constant_dynamic-slice_fusion), channel_id=1, source_target_pairs={{0,1},{1,0},{2,3},{3,2},{4,5},{5,4},{6,7},{7,6},{8,9},{9,8},{10,11... | collective-permute-start | bytes 98312 | tf_op jit(solution)/shard_map/ppermute | solution.py:43

commit v3 on v0

v3 whole, which is shorter than its diff:
```python
import functools
import math

import jax
import jax.numpy as jnp
from jax import lax
from jax.experimental import pallas as pl
from jax.experimental.pallas import tpu as pltpu
from jax.sharding import PartitionSpec as P

MODEL_WIDTH = 16384
LANES = 128
HEAD_SIZE = 128
CHUNK = 256
STAGE_VMEM = 8 * 2**20
PROJECT_VMEM = 50 * 2**20
OUTPUT_VMEM = 50 * 2**20


def bit_reverse(value, bits):
    turned = 0
    for bit in range(bits):
        turned = turned | (((value >> bit) & 1) << (bits - 1 - bit))
    return turned


def stage_kernel(*refs):
    count = len(refs) // 2
    sems = refs[-1]
    copies = [
        pltpu.make_async_copy(refs[i], refs[count + i], sems.at[i]) for i in range(count)
    ]
    for copy in copies:
        copy.start()
    for copy in copies:
        copy.wait()


def stage(*arrays):
    return pl.pallas_call(
        stage_kernel,
        out_shape=tuple(jax.ShapeDtypeStruct(a.shape, a.dtype) for a in arrays),
        in_specs=[pl.BlockSpec(memory_space=pltpu.HBM)] * len(arrays),
        out_specs=tuple(pl.BlockSpec(memory_space=pltpu.VMEM) for _ in arrays),
        scratch_shapes=[pltpu.SemaphoreType.DMA((len(arrays),))],
        compiler_params=pltpu.CompilerParams(vmem_limit_bytes=STAGE_VMEM),
        cost_estimate=pl.CostEstimate(
            flops=0, bytes_accessed=sum(2 * a.size for a in arrays), transcendentals=0
        ),
        name="stage",
    )(*arrays)


def project_kernel(
    bits, rows_ref, other_ref, wq_hbm, wk, wv, send_ref, keep_ref, wq, rows, out, sems
):
    depth = wq.shape[0]
    chunk = min(CHUNK, depth)
    steps = depth // chunk
    copies = []
    for step in range(steps):
        part = pl.ds(step * chunk, chunk)
        copies.append(pltpu.make_async_copy(wq_hbm.at[part], wq.at[part], sems.at[step]))
        copies[-1].start()

    slots = rows.shape[0]
    half = slots // 2
    turn = bit_reverse(lax.axis_index("gx"), bits)
    gy = lax.axis_index("gy")
    for ref, side in ((rows_ref, gy), (other_ref, 1 - gy)):
        block = ref[...].astype(jnp.float32)
        for t in range(half):
            slot = bit_reverse(t, bits) ^ turn ^ side
            rows[pl.ds(slot, 1), :] = block[t : t + 1, :]
    wide = rows[...]
    squares = jnp.sum(wide * wide, axis=1, keepdims=True)
    narrow = wide.astype(jnp.bfloat16)

    fresh = [jnp.dot(narrow, w[...], preferred_element_type=jnp.float32) for w in (wk, wv)]
    sums = None
    for step, copy in enumerate(copies):
        part = slice(step * chunk, (step + 1) * chunk)
        copy.wait()
        term = jnp.dot(narrow[:, part], wq[part, :], preferred_element_type=jnp.float32)
        sums = term if sums is None else sums + term

    total = out.shape[1]
    blocks = []
    for part in (sums, *fresh):
        blocks += [part[:, i : i + LANES] for i in range(0, part.shape[1], LANES)]
    blocks.append(jnp.broadcast_to(squares, (slots, LANES)))
    blocks += [jnp.zeros((slots, LANES), jnp.float32)] * (total - len(blocks))
    flat = out.reshape(slots * total, LANES)
    for i, block in enumerate(blocks):
        flat[pl.ds(i, slots, stride=total), :] = block
    keep_ref[...] = out[:half]
    send_ref[...] = out[half:]


def project(rows, other, w_query, key_weight, value_weight, slots):
    bits = slots.bit_length() - 1
    depth, query_width = w_query.shape
    kv_width = key_weight.shape[1]
    used = (query_width + 2 * kv_width) // LANES + 1
    total = -(-used // 8) * 8
    piece = jax.ShapeDtypeStruct((slots // 2, total, LANES), jnp.float32)
    whole = pl.BlockSpec(memory_space=pltpu.VMEM)
    stay = pl.BlockSpec(memory_space=pltpu.HBM)
    steps = depth // min(CHUNK, depth)
    return pl.pallas_call(
        functools.partial(project_kernel, bits),
        out_shape=(piece, piece),
        in_specs=[whole, whole, stay, whole, whole],
        out_specs=(whole, whole),
        scratch_shapes=[
            pltpu.VMEM(w_query.shape, jnp.bfloat16),
            pltpu.VMEM((slots, depth), jnp.float32),
            pltpu.VMEM((slots, total, LANES), jnp.float32),
            pltpu.SemaphoreType.DMA((steps,)),
        ],
        compiler_params=pltpu.CompilerParams(vmem_limit_bytes=PROJECT_VMEM),
        cost_estimate=pl.CostEstimate(
            flops=2 * slots * depth * (query_width + 2 * kv_width),
            bytes_accessed=2 * depth * (query_width + 2 * kv_width),
            transcendentals=0,
        ),
        name="project",
    )(rows, other, w_query, key_weight, value_weight)


def attend_kernel(
    query_heads, kv_heads, length_ref, mine_ref, arrived_ref, cosine_ref, sine_ref, k_ref, v_ref, heads_ref
):
    total = mine_ref[0] + arrived_ref[0]
    at = query_heads + 2 * kv_heads
    scale = lax.rsqrt(total[at : at + 1, :] / MODEL_WIDTH + 1e-05)
    turned = total[: query_heads + kv_heads] * scale
    half = HEAD_SIZE // 2
    swapped = jnp.concatenate([turned[:, half:], turned[:, :half]], axis=1)
    turned = (turned * cosine_ref[...] + swapped * sine_ref[...]).astype(jnp.bfloat16)
    fresh_values = (total[query_heads + kv_heads : at] * scale).astype(jnp.bfloat16)
    group = query_heads // kv_heads
    factor = 1.0 / math.sqrt(HEAD_SIZE)
    length = length_ref[0]
    for head in range(kv_heads):
        queries = turned[head * group : (head + 1) * group]
        fresh_key = turned[query_heads + head : query_heads + head + 1].astype(jnp.float32)
        own = jnp.sum(queries.astype(jnp.float32) * fresh_key, axis=1, keepdims=True) * factor
        scores = (
            lax.dot_general(
                queries,
                k_ref[0, head],
                (((1,), (1,)), ((), ())),
                preferred_element_type=jnp.float32,
            )
            * factor
        )
        slot = lax.broadcasted_iota(jnp.int32, scores.shape, 1)
        scores = jnp.where(slot < length, scores, -jnp.inf)
        top = jnp.maximum(jnp.max(scores, axis=1, keepdims=True), own)
        exponent = jnp.exp(scores - top)
        own_exp = jnp.exp(own - top)
        share = 1.0 / (jnp.sum(exponent, axis=1, keepdims=True) + own_exp)
        weights = (exponent * share).astype(jnp.bfloat16)
        own_weight = (own_exp * share).astype(jnp.bfloat16)
        mixed = jnp.dot(weights, v_ref[0, head], preferred_element_type=jnp.float32)
        mixed = mixed + own_weight.astype(jnp.float32) * fresh_values[head : head + 1].astype(
            jnp.float32
        )
        heads_ref[0, pl.ds(head * group, group), :] = mixed.astype(jnp.bfloat16)


def attend(mine, arrived, cosine, sine, k_cache, value_cache, lengths, query_heads):
    kv_heads, cache_len = k_cache.shape[1:3]
    whole = pl.BlockSpec(memory_space=pltpu.VMEM)
    return pl.pallas_call(
        functools.partial(attend_kernel, query_heads, kv_heads),
        out_shape=jax.ShapeDtypeStruct((1, query_heads, HEAD_SIZE), jnp.bfloat16),
        in_specs=[pl.BlockSpec(memory_space=pltpu.SMEM)] + [whole] * 6,
        out_specs=whole,
        compiler_params=pltpu.CompilerParams(vmem_limit_bytes=12 * 2**20),
        cost_estimate=pl.CostEstimate(
            flops=4 * query_heads * cache_len * HEAD_SIZE,
            bytes_accessed=64 * kv_heads * cache_len * HEAD_SIZE,
            transcendentals=query_heads * cache_len,
        ),
        name="attend",
    )(lengths, mine, arrived, cosine, sine, k_cache, value_cache)


def output_kernel(bits, pieces, *refs):
    parts = refs[:pieces]
    w_hbm, mine_ref, theirs_ref, w_ref, flat, left, sums, sems = refs[pieces:]
    depth = w_ref.shape[0]
    chunk = min(2 * CHUNK, depth)
    copies = []
    for step in range(depth // chunk):
        part = pl.ds(step * chunk, chunk)
        copies.append(pltpu.make_async_copy(w_hbm.at[part], w_ref.at[part], sems.at[step]))
        copies[-1].start()
    slots = left.shape[0]
    heads = flat.shape[0] // slots
    at = 0
    for ref in parts:
        for i in range(ref.shape[0]):
            flat[at : at + heads, :] = ref[i].astype(jnp.float32)
            at += heads
    for head in range(heads):
        left[:, head * HEAD_SIZE : (head + 1) * HEAD_SIZE] = flat[
            pl.ds(head, slots, stride=heads), :
        ].astype(jnp.bfloat16)
    total = None
    for step, copy in enumerate(copies):
        part = slice(step * chunk, (step + 1) * chunk)
        copy.wait()
        term = jnp.dot(left[:, part], w_ref[part, :], preferred_element_type=jnp.float32)
        total = term if total is None else total + term
    sums[...] = total
    half = slots // 2
    turn = bit_reverse(lax.axis_index("gx"), bits)
    gy = lax.axis_index("gy")
    for ref, side in ((mine_ref, gy), (theirs_ref, 1 - gy)):
        for t in range(half):
            slot = bit_reverse(t, bits) ^ turn ^ side
            ref[t : t + 1, :] = sums[pl.ds(slot, 1), :]


def output(parts, w_out, slots):
    bits = slots.bit_length() - 1
    depth, width = w_out.shape
    heads = depth // HEAD_SIZE
    whole = pl.BlockSpec(memory_space=pltpu.VMEM)
    piece = jax.ShapeDtypeStruct((slots // 2, width), jnp.float32)
    return pl.pallas_call(
        functools.partial(output_kernel, bits, len(parts)),
        out_shape=(piece, piece),
        in_specs=[whole] * len(parts) + [pl.BlockSpec(memory_space=pltpu.HBM)],
        out_specs=(whole, whole),
        scratch_shapes=[
            pltpu.VMEM(w_out.shape, jnp.bfloat16),
            pltpu.VMEM((slots * heads, HEAD_SIZE), jnp.float32),
            pltpu.VMEM((slots, depth), jnp.bfloat16),
            pltpu.VMEM((slots, width), jnp.float32),
            pltpu.SemaphoreType.DMA((depth // min(2 * CHUNK, depth),)),
        ],
        compiler_params=pltpu.CompilerParams(vmem_limit_bytes=OUTPUT_VMEM),
        cost_estimate=pl.CostEstimate(
            flops=2 * slots * depth * width, bytes_accessed=2 * depth * width, transcendentals=0
        ),
        name="output",
    )(*parts, w_out)


def swap(block, axis, devices, mask):
    return lax.ppermute(block, axis, [(i, i ^ mask) for i in range(devices)])


def body(devices, activations, w_query, key_weight, value_weight, w_out, k_cache, value_cache, lengths):
    slots = devices
    query_heads = w_query.shape[1] // HEAD_SIZE
    half = HEAD_SIZE // 2
    frequency = jnp.power(
        jnp.float32(500000.0), -2.0 * jnp.arange(half, dtype=jnp.float32) / HEAD_SIZE
    )
    angle = lengths.astype(jnp.float32)[:, None] * frequency
    cosine = jnp.cos(angle)
    sine = jnp.sin(angle)
    cosine = jnp.concatenate([cosine, cosine], axis=1)
    sine = jnp.concatenate([-sine, sine], axis=1)

    other = swap(activations, "gy", 2, 1)
    key_weight, value_weight, k_cache, value_cache = stage(
        key_weight, value_weight, k_cache, value_cache
    )
    send, keep = project(activations, other, w_query, key_weight, value_weight, slots)
    mask = 1
    while send.shape[0] > 1:
        arrived = swap(send, "gx", devices, mask)
        rest = keep.shape[0] // 2
        send = keep[rest:] + arrived[rest:]
        keep = keep[:rest] + arrived[:rest]
        mask *= 2
    arrived = swap(send, "gx", devices, mask)
    heads = attend(keep, arrived, cosine, sine, k_cache, value_cache, lengths, query_heads)
    parts = [heads]
    while mask:
        held = parts[0] if len(parts) == 1 else jnp.concatenate(parts, axis=0)
        parts.append(swap(held, "gx", devices, mask))
        mask //= 2
    mine, theirs = output(parts, w_out, slots)
    return (mine + swap(theirs, "gy", 2, 1)).astype(jnp.bfloat16)


def solution(mesh):
    placed = (
        P(("groups", "gy"), "gx"),
        P("gx", "gy"),
        P("gx", "gy"),
        P("gx", "gy"),
        P("gy", "gx"),
        P(("groups", "gx"), "gy", None, None),
        P(("groups", "gx"), "gy", None, None),
        P(("groups", "gx")),
    )
    return jax.shard_map(
        functools.partial(body, mesh.shape["gx"]),
        mesh=mesh,
        in_specs=placed,
        out_specs=P(("groups", "gy"), "gx"),
        check_vma=False,
    )
```

time: 146 us -> 49.9 us (0.34)
  blocking collectives: 59.4 us -> 0 us
  waiting for transfers between devices: 46.9 us -> 13.8 us
  matrix products: 20.1 us -> 0 us
  starting transfers between devices: 0.01 us -> 14.4 us
  Pallas kernels: 0 us -> 14.2 us
  between operations: 14.8 us -> 0.73 us
  local copies, waits for them, and re-layouts: 1.84 us -> 5.61 us
  other arithmetic: 2.9 us -> 0.89 us
    psum x1 -> x0, waiting for transfers between devices: 46.9 us -> none  [body(): lax.psum(jnp.concatenate([jnp.dot(rows_all, w_query, preferred_element_ty...]
    all_gather x2 -> x0, blocking collectives: 32.8 us -> none  [the longest x1 30.6 us: body(): lax.all_gather(heads, 'gx', axis=0, tiled=True)]
    psum x1 -> x0, blocking collectives: 23 us -> none  [body(): squares = lax.psum(jnp.sum(widened * widened, axis=1), 'gx')]
    dot_general x7 -> x0, matrix products: 20.1 us -> none  [the longest x1 8.05 us: body(): jnp.dot(lax.all_gather(heads, 'gx', axis=0, tiled=True), w_out, preferred...]
    ppermute x0 -> x8, starting transfers between devices: none -> 14.4 us  [swap(): return lax.ppermute(block, axis, [(i, i ^ mask) for i in range(devices)])]
    pallas_call x0 -> x4, Pallas kernels: none -> 14.2 us  [the longest x1 6.37 us: project(): pl.pallas_call(functools.partial(project_kernel, bits), out_shape=(piece,...]
    ppermute x0 -> x8, waiting for transfers between devices: none -> 13.8 us  [swap(): return lax.ppermute(block, axis, [(i, i ^ mask) for i in range(devices)])]
    unnamed x9 -> x10, local copies, waits for them, and re-layouts: 0.62 us -> 5.61 us
  transfers between devices with their start and end apart: 1 -> 8, of which waited for: 1 -> 7; matrix products, arithmetic and copies ran while one was open for 1% -> 1% of each run, Pallas kernels for 0% -> 1%
where the time goes in v3:
time: 49.9 us; the launch traced here: 49.6 us
  starting transfers between devices  14.4 us (29%)
  Pallas kernels  14.2 us (28%)
  waiting for transfers between devices  13.8 us (28%)
  local copies, waits for them, and re-layouts  5.61 us (11%)
  other arithmetic  0.89 us (2%)
  between operations  0.73 us (1%)
    ppermute x8, starting transfers between devices, swap(): return lax.ppermute(block, axis, [(i, i ^ mask) for i in range(devices)])  14.4 us
    ppermute x8, waiting for transfers between devices, swap(): return lax.ppermute(block, axis, [(i, i ^ mask) for i in range(devices)])  13.8 us
    pallas_call x1, Pallas kernels, project(): pl.pallas_call(functools.partial(project_kernel, bits), out_shape=(piece,...  6.37 us
    pallas_call x1, Pallas kernels, output(): pl.pallas_call(functools.partial(output_kernel, bits, len(parts)), out_sh...  6.33 us
    unnamed x10, local copies, waits for them, and re-layouts  5.61 us
    pallas_call x1, Pallas kernels, attend(): pl.pallas_call(functools.partial(attend_kernel, query_heads, kv_heads), o...  1.16 us
  transfers between devices with their start and end apart: 8, of which 7 were waited for; matrix products, arithmetic and copies ran while one was open for 1% of the time, Pallas kernels for 1%

profile of v3, /device:TPU:0, one launch (start us, length us, event | category | flops | bytes accessed | tf_op | source)
XLA Modules:
  0.0 49.6 jit_solution(829499859736170661)
XLA Ops:
  0.0 0.5 collective-permute-start
  1.2 1.2 %copy-done = bf16[2048,256]{1,0:T(8,128)(2,1)S(1)} copy-done((bf16[2048,256]{1,0:T(8,128)(2,1)S(1)}, bf16[2048,256]{1,0:T(8,128)(2,1)}, u32[]{:S(2)}) %copy-start) | copy-done | bytes 1048600
  2.4 1.2 %copy-done.1 = bf16[2048,256]{1,0:T(8,128)(2,1)S(1)} copy-done((bf16[2048,256]{1,0:T(8,128)(2,1)S(1)}, bf16[2048,256]{1,0:T(8,128)(2,1)}, u32[]{:S(2)}) %copy-start.1) | copy-done | bytes 1048600
  3.6 1.2 %copy-done.2 = bf16[1,2,2048,128]{3,2,1,0:T(8,128)(2,1)S(1)} copy-done((bf16[1,2,2048,128]{3,2,1,0:T(8,128)(2,1)S(1)}, bf16[1,2,2048,128]{3,2,1,0:T(8,128)(2,1)}, u32[]{:S(2)}) %copy-start.2) | copy-done | bytes 1048600
  4.8 1.2 %copy-done.3 = bf16[1,2,2048,128]{3,2,1,0:T(8,128)(2,1)S(1)} copy-done((bf16[1,2,2048,128]{3,2,1,0:T(8,128)(2,1)S(1)}, bf16[1,2,2048,128]{3,2,1,0:T(8,128)(2,1)}, u32[]{:S(2)}) %copy-start.3) | copy-done | bytes 1048600
  6.1 0.3 stage.1
  6.4 0.7 %copy-done.4 = bf16[4,2048]{1,0:T(4,128)(2,1)S(1)} copy-done((bf16[4,2048]{1,0:T(4,128)(2,1)S(1)}, bf16[4,2048]{1,0:T(4,128)(2,1)}, u32[]{:S(2)}) %copy-start.4) | copy-done | bytes 16408
  7.1 6.4 %project.1 = (f32[4,40,128]{2,1,0:T(8,128)S(1)}, f32[4,40,128]{2,1,0:T(8,128)S(1)}) custom-call(bf16[4,2048]{1,0:T(4,128)(2,1)S(1)} %copy-done.4, bf16[4,2048]{1,0:T(4,128)(2,1)S(1)} %collective-permute-done.other_ref, bf16[2048,4096]{1,0:T(8,128)(2,1)} %wq_hbm.1, bf16[2048,256]{1,0:T(8,128)(2,1)S(1)} %get-tuple-element.13.wk, ...), custom_call_target="tpu_custom_call" | custom-call | flops 150994944 | bytes 18874368 | tf_op jit(solution)/shard_map/project/pallas_call | solution.py:110
  13.5 2.6 %collective-permute-start.1 = (f32[4,40,128]{2,1,0:T(8,128)S(1)}, f32[4,40,128]{2,1,0:T(8,128)S(1)}, u32[]{:S(2)}, u32[]{:S(2)}) collective-permute-start(f32[4,40,128]{2,1,0:T(8,128)S(1)} %get-tuple-element.16), channel_id=1, source_target_pairs={{0,2},{2,0},{4,6},{6,4},{8,10},{10,8},{12,14},{14,12},{1,3},{3,1},... | collective-permute-start | bytes 245768 | tf_op jit(solution)/shard_map/ppermute | solution.py:255
  16.1 3.1 %collective-permute-done.1 = f32[4,40,128]{2,1,0:T(8,128)S(1)} collective-permute-done((f32[4,40,128]{2,1,0:T(8,128)S(1)}, f32[4,40,128]{2,1,0:T(8,128)S(1)}, u32[]{:S(2)}, u32[]{:S(2)}) %collective-permute-start.1) | collective-permute-done | bytes 81952 | tf_op jit(solution)/shard_map/ppermute | solution.py:255
  19.2 1.9 %collective-permute-start.2 = (f32[2,40,128]{2,1,0:T(8,128)S(1)}, f32[2,40,128]{2,1,0:T(8,128)S(1)}, u32[]{:S(2)}, u32[]{:S(2)}) collective-permute-start(f32[2,40,128]{2,1,0:T(8,128)S(1)} %get-tuple-element.22), channel_id=1, source_target_pairs={{0,4},{2,6},{4,0},{6,2},{8,12},{10,14},{12,8},{14,10},{1,5},{3,7},... | collective-permute-start | bytes 122888 | tf_op jit(solution)/shard_map/ppermute | solution.py:255
  21.2 2.1 %collective-permute-done.2 = f32[2,40,128]{2,1,0:T(8,128)S(1)} collective-permute-done((f32[2,40,128]{2,1,0:T(8,128)S(1)}, f32[2,40,128]{2,1,0:T(8,128)S(1)}, u32[]{:S(2)}, u32[]{:S(2)}) %collective-permute-start.2) | collective-permute-done | bytes 40992 | tf_op jit(solution)/shard_map/ppermute | solution.py:255
  23.3 2.8 %collective-permute-start.3 = (f32[1,40,128]{2,1,0:T(8,128)S(1)}, f32[1,40,128]{2,1,0:T(8,128)S(1)}, u32[]{:S(2)}, u32[]{:S(2)}) collective-permute-start(f32[1,40,128]{2,1,0:T(8,128)S(1)} %get-tuple-element.23), channel_id=1, source_target_pairs={{0,8},{2,10},{4,12},{6,14},{8,0},{10,2},{12,4},{14,6},{1,9},{3,11}... | collective-permute-start | bytes 61448 | tf_op jit(solution)/shard_map/ppermute | solution.py:255
  26.2 1.8 %collective-permute-done.3.arrived_ref = f32[1,40,128]{2,1,0:T(8,128)S(1)} collective-permute-done((f32[1,40,128]{2,1,0:T(8,128)S(1)}, f32[1,40,128]{2,1,0:T(8,128)S(1)}, u32[]{:S(2)}, u32[]{:S(2)}) %collective-permute-start.3) | collective-permute-done | bytes 20512 | tf_op jit(solution)/shard_map/ppermute | solution.py:255
  27.9 1.2 %attend.1.refs_0_ = bf16[1,32,128]{2,1,0:T(8,128)(2,1)S(1)} custom-call(s32[1]{0:T(128)S(6)} %copy.9.length_ref, f32[1,40,128]{2,1,0:T(8,128)S(1)} %get-tuple-element.24.mine_ref, f32[1,40,128]{2,1,0:T(8,128)S(1)} %collective-permute-done.3.arrived_ref, f32[1,128]{1,0:T(1,128)S(1)} %pad_maximum_fusion.2.cosine_ref, f32[1,128]{1,0:T(1,128)S(1)} %pad_maximum_fusion.3.sine_ref, ...), custom_call_target="tpu_custom_call" | custom-call | flops 33554432 | bytes 33554432 | tf_op jit(solution)/shard_map/attend/pallas_call | solution.py:176
  29.1 2.9 %collective-permute-start.4 = (bf16[1,32,128]{2,1,0:T(8,128)(2,1)S(1)}, bf16[1,32,128]{2,1,0:T(8,128)(2,1)S(1)}, u32[]{:S(2)}, u32[]{:S(2)}) collective-permute-start(bf16[1,32,128]{2,1,0:T(8,128)(2,1)S(1)} %attend.1.refs_0_), channel_id=1, source_target_pairs={{0,8},{2,10},{4,12},{6,14},{8,0},{10,2},{12,4},{14,6},{1,9},{3,11}... | collective-permute-start | bytes 24584 | tf_op jit(solution)/shard_map/ppermute | solution.py:255
  32.0 1.7 %collective-permute-done.4.refs_1_ = bf16[1,32,128]{2,1,0:T(8,128)(2,1)S(1)} collective-permute-done((bf16[1,32,128]{2,1,0:T(8,128)(2,1)S(1)}, bf16[1,32,128]{2,1,0:T(8,128)(2,1)S(1)}, u32[]{:S(2)}, u32[]{:S(2)}) %collective-permute-start.4) | collective-permute-done | bytes 8224 | tf_op jit(solution)/shard_map/ppermute | solution.py:255
  33.7 1.9 %collective-permute-start.5 = (bf16[2,32,128]{2,1,0:T(8,128)(2,1)S(1)}, bf16[2,32,128]{2,1,0:T(8,128)(2,1)S(1)}, u32[]{:S(2)}, u32[]{:S(2)}) collective-permute-start(bf16[2,32,128]{2,1,0:T(8,128)(2,1)S(1)} %pad_maximum_fusion.1), channel_id=1, source_target_pairs={{0,4},{2,6},{4,0},{6,2},{8,12},{10,14},{12,8},{14,10},{1,5},{3,7},... | collective-permute-start | bytes 49160 | tf_op jit(solution)/shard_map/ppermute | solution.py:255
  35.6 1.8 %collective-permute-done.5.refs_2_ = bf16[2,32,128]{2,1,0:T(8,128)(2,1)S(1)} collective-permute-done((bf16[2,32,128]{2,1,0:T(8,128)(2,1)S(1)}, bf16[2,32,128]{2,1,0:T(8,128)(2,1)S(1)}, u32[]{:S(2)}, u32[]{:S(2)}) %collective-permute-start.5) | collective-permute-done | bytes 16416 | tf_op jit(solution)/shard_map/ppermute | solution.py:255
  37.5 1.7 %collective-permute-start.6 = (bf16[4,32,128]{2,1,0:T(8,128)(2,1)S(1)}, bf16[4,32,128]{2,1,0:T(8,128)(2,1)S(1)}, u32[]{:S(2)}, u32[]{:S(2)}) collective-permute-start(bf16[4,32,128]{2,1,0:T(8,128)(2,1)S(1)} %pad_maximum_fusion), channel_id=1, source_target_pairs={{0,2},{2,0},{4,6},{6,4},{8,10},{10,8},{12,14},{14,12},{1,3},{3,1},... | collective-permute-start | bytes 98312 | tf_op jit(solution)/shard_map/ppermute | solution.py:255
  39.2 2.2 %collective-permute-done.6.refs_3_ = bf16[4,32,128]{2,1,0:T(8,128)(2,1)S(1)} collective-permute-done((bf16[4,32,128]{2,1,0:T(8,128)(2,1)S(1)}, bf16[4,32,128]{2,1,0:T(8,128)(2,1)S(1)}, u32[]{:S(2)}, u32[]{:S(2)}) %collective-permute-start.6) | collective-permute-done | bytes 32800 | tf_op jit(solution)/shard_map/ppermute | solution.py:255
  41.4 6.3 %output.1 = (f32[4,2048]{1,0:T(4,128)S(1)}, f32[4,2048]{1,0:T(4,128)S(1)}) custom-call(bf16[1,32,128]{2,1,0:T(8,128)(2,1)S(1)} %attend.1.refs_0_, bf16[1,32,128]{2,1,0:T(8,128)(2,1)S(1)} %collective-permute-done.4.refs_1_, bf16[2,32,128]{2,1,0:T(8,128)(2,1)S(1)} %collective-permute-done.5.refs_2_, bf16[4,32,128]{2,1,0:T(8,128)(2,1)S(1)} %collective-permute-done.6.refs_3_, ...), custom_call_target="tpu_custom_call" | custom-call | flops 134217728 | bytes 16777216 | tf_op jit(solution)/shard_map/output/pallas_call | solution.py:234
  47.8 1.2 %collective-permute-done.7 = f32[4,2048]{1,0:T(4,128)S(1)} collective-permute-done((f32[4,2048]{1,0:T(4,128)S(1)}, f32[4,2048]{1,0:T(4,128)S(1)}, u32[]{:S(2)}, u32[]{:S(2)}) %collective-permute-start.7) | collective-permute-done | bytes 32800 | tf_op jit(solution)/shard_map/ppermute | solution.py:255
  49.0 0.6 %add_convert_fusion = bf16[4,2048]{1,0:T(4,128)(2,1)} fusion(f32[4,2048]{1,0:T(4,128)S(1)} %get-tuple-element.19, f32[4,2048]{1,0:T(4,128)S(1)} %collective-permute-done.7), kind=kLoop, calls=%fused_computation.3 | loop fusion | flops 16384 | bytes 81920 | tf_op jit(solution)/shard_map/convert_element_type | solution.py:291
  (15 shorter events, 0.4 us)
Async XLA Ops:
  0.0 6.4 %collective-permute-start = (bf16[4,2048]{1,0:T(4,128)(2,1)}, bf16[4,2048]{1,0:T(4,128)(2,1)S(1)}, u32[]{:S(2)}, u32[]{:S(2)}) collective-permute-start(bf16[4,2048]{1,0:T(4,128)(2,1)} %rows_ref.1), channel_id=1, source_target_pairs={{0,1},{1,0},{2,3},{3,2},{4,5},{5,4},{6,7},{7,6},{8,9},{9,8},{10,11... | collective-permute-start | bytes 49160 | tf_op jit(solution)/shard_map/ppermute | solution.py:255
  1.2 1.2 %copy-start = (bf16[2048,256]{1,0:T(8,128)(2,1)S(1)}, bf16[2048,256]{1,0:T(8,128)(2,1)}, u32[]{:S(2)}) copy-start(bf16[2048,256]{1,0:T(8,128)(2,1)} %refs_0_.1) | copy-start | bytes 3145732
  2.4 1.2 %copy-start.1 = (bf16[2048,256]{1,0:T(8,128)(2,1)S(1)}, bf16[2048,256]{1,0:T(8,128)(2,1)}, u32[]{:S(2)}) copy-start(bf16[2048,256]{1,0:T(8,128)(2,1)} %refs_1_.1) | copy-start | bytes 3145732
  3.6 1.2 %copy-start.2 = (bf16[1,2,2048,128]{3,2,1,0:T(8,128)(2,1)S(1)}, bf16[1,2,2048,128]{3,2,1,0:T(8,128)(2,1)}, u32[]{:S(2)}) copy-start(bf16[1,2,2048,128]{3,2,1,0:T(8,128)(2,1)} %refs_2_.1) | copy-start | bytes 3145732
  4.8 1.2 %copy-start.3 = (bf16[1,2,2048,128]{3,2,1,0:T(8,128)(2,1)S(1)}, bf16[1,2,2048,128]{3,2,1,0:T(8,128)(2,1)}, u32[]{:S(2)}) copy-start(bf16[1,2,2048,128]{3,2,1,0:T(8,128)(2,1)} %refs_3_.1) | copy-start | bytes 3145732
  6.4 0.7 %copy-start.4 = (bf16[4,2048]{1,0:T(4,128)(2,1)S(1)}, bf16[4,2048]{1,0:T(4,128)(2,1)}, u32[]{:S(2)}) copy-start(bf16[4,2048]{1,0:T(4,128)(2,1)} %rows_ref.1) | copy-start | bytes 49156
  13.5 5.7 %collective-permute-start.1 = (f32[4,40,128]{2,1,0:T(8,128)S(1)}, f32[4,40,128]{2,1,0:T(8,128)S(1)}, u32[]{:S(2)}, u32[]{:S(2)}) collective-permute-start(f32[4,40,128]{2,1,0:T(8,128)S(1)} %get-tuple-element.16), channel_id=1, source_target_pairs={{0,2},{2,0},{4,6},{6,4},{8,10},{10,8},{12,14},{14,12},{1,3},{3,1},... | collective-permute-start | bytes 245768 | tf_op jit(solution)/shard_map/ppermute | solution.py:255
  19.2 4.1 %collective-permute-start.2 = (f32[2,40,128]{2,1,0:T(8,128)S(1)}, f32[2,40,128]{2,1,0:T(8,128)S(1)}, u32[]{:S(2)}, u32[]{:S(2)}) collective-permute-start(f32[2,40,128]{2,1,0:T(8,128)S(1)} %get-tuple-element.22), channel_id=1, source_target_pairs={{0,4},{2,6},{4,0},{6,2},{8,12},{10,14},{12,8},{14,10},{1,5},{3,7},... | collective-permute-start | bytes 122888 | tf_op jit(solution)/shard_map/ppermute | solution.py:255
  23.3 4.7 %collective-permute-start.3 = (f32[1,40,128]{2,1,0:T(8,128)S(1)}, f32[1,40,128]{2,1,0:T(8,128)S(1)}, u32[]{:S(2)}, u32[]{:S(2)}) collective-permute-start(f32[1,40,128]{2,1,0:T(8,128)S(1)} %get-tuple-element.23), channel_id=1, source_target_pairs={{0,8},{2,10},{4,12},{6,14},{8,0},{10,2},{12,4},{14,6},{1,9},{3,11}... | collective-permute-start | bytes 61448 | tf_op jit(solution)/shard_map/ppermute | solution.py:255
  29.1 4.6 %collective-permute-start.4 = (bf16[1,32,128]{2,1,0:T(8,128)(2,1)S(1)}, bf16[1,32,128]{2,1,0:T(8,128)(2,1)S(1)}, u32[]{:S(2)}, u32[]{:S(2)}) collective-permute-start(bf16[1,32,128]{2,1,0:T(8,128)(2,1)S(1)} %attend.1.refs_0_), channel_id=1, source_target_pairs={{0,8},{2,10},{4,12},{6,14},{8,0},{10,2},{12,4},{14,6},{1,9},{3,11}... | collective-permute-start | bytes 24584 | tf_op jit(solution)/shard_map/ppermute | solution.py:255
  33.7 3.7 %collective-permute-start.5 = (bf16[2,32,128]{2,1,0:T(8,128)(2,1)S(1)}, bf16[2,32,128]{2,1,0:T(8,128)(2,1)S(1)}, u32[]{:S(2)}, u32[]{:S(2)}) collective-permute-start(bf16[2,32,128]{2,1,0:T(8,128)(2,1)S(1)} %pad_maximum_fusion.1), channel_id=1, source_target_pairs={{0,4},{2,6},{4,0},{6,2},{8,12},{10,14},{12,8},{14,10},{1,5},{3,7},... | collective-permute-start | bytes 49160 | tf_op jit(solution)/shard_map/ppermute | solution.py:255
  37.5 3.9 %collective-permute-start.6 = (bf16[4,32,128]{2,1,0:T(8,128)(2,1)S(1)}, bf16[4,32,128]{2,1,0:T(8,128)(2,1)S(1)}, u32[]{:S(2)}, u32[]{:S(2)}) collective-permute-start(bf16[4,32,128]{2,1,0:T(8,128)(2,1)S(1)} %pad_maximum_fusion), channel_id=1, source_target_pairs={{0,2},{2,0},{4,6},{6,4},{8,10},{10,8},{12,14},{14,12},{1,3},{3,1},... | collective-permute-start | bytes 98312 | tf_op jit(solution)/shard_map/ppermute | solution.py:255
  47.7 1.3 %collective-permute-start.7 = (f32[4,2048]{1,0:T(4,128)S(1)}, f32[4,2048]{1,0:T(4,128)S(1)}, u32[]{:S(2)}, u32[]{:S(2)}) collective-permute-start(f32[4,2048]{1,0:T(4,128)S(1)} %get-tuple-element.20), channel_id=1, source_target_pairs={{0,1},{1,0},{2,3},{3,2},{4,5},{5,4},{6,7},{7,6},{8,9},{9,8},{10,11... | collective-permute-start | bytes 98312 | tf_op jit(solution)/shard_map/ppermute | solution.py:255

commit v4 on v3

v4 whole, which is shorter than its diff:
```python
import functools
import math

import jax
import jax.numpy as jnp
from jax import lax
from jax.experimental import pallas as pl
from jax.experimental.pallas import tpu as pltpu
from jax.sharding import PartitionSpec as P

MODEL_WIDTH = 16384
LANES = 128
HEAD_SIZE = 128
CHUNK = 256
MIB = 2**20


def bit_reverse(value, bits):
    turned = 0
    for bit in range(bits):
        turned = turned | (((value >> bit) & 1) << (bits - 1 - bit))
    return turned


def in_hbm(array):
    return pltpu.with_memory_space_constraint(array, pltpu.HBM)


def stage_kernel(parts, *refs):
    count = len(parts)
    sems = refs[-1]
    copies = [
        pltpu.make_async_copy(refs[i].at[pl.ds(*part)], refs[count + i], sems.at[i])
        for i, part in enumerate(parts)
    ]
    for copy in copies:
        copy.start()
    for copy in copies:
        copy.wait()


def stage(arrays, parts):
    shapes = tuple(
        jax.ShapeDtypeStruct((part[1], *a.shape[1:]), a.dtype) for a, part in zip(arrays, parts)
    )
    return pl.pallas_call(
        functools.partial(stage_kernel, parts),
        out_shape=shapes,
        in_specs=[pl.BlockSpec(memory_space=pltpu.HBM)] * len(arrays),
        out_specs=tuple(pl.BlockSpec(memory_space=pltpu.VMEM) for _ in arrays),
        scratch_shapes=[pltpu.SemaphoreType.DMA((len(arrays),))],
        compiler_params=pltpu.CompilerParams(vmem_limit_bytes=16 * MIB),
        cost_estimate=pl.CostEstimate(
            flops=0, bytes_accessed=sum(2 * math.prod(x.shape) for x in shapes), transcendentals=0
        ),
        name="stage",
    )(*[in_hbm(a) for a in arrays])


def spread(depth, skip, chunk):
    return [(at, min(chunk, depth - at)) for at in range(skip, depth, chunk)]


def project_kernel(
    bits, rows_ref, other_ref, wq_hbm, first, wk, wv, send_ref, keep_ref, wq, rows, sems
):
    skip = first.shape[0]
    ranges = spread(wq_hbm.shape[0], skip, CHUNK)
    copies = []
    for i, (start, size) in enumerate(ranges):
        copies.append(
            pltpu.make_async_copy(
                wq_hbm.at[pl.ds(start, size)], wq.at[pl.ds(start - skip, size)], sems.at[i]
            )
        )
        copies[-1].start()

    slots = rows.shape[0]
    half = slots // 2
    turn = bit_reverse(lax.axis_index("gx"), bits)
    gy = lax.axis_index("gy")
    for ref, side in ((rows_ref, gy), (other_ref, 1 - gy)):
        block = ref[...].astype(jnp.float32)
        for t in range(half):
            slot = bit_reverse(t, bits) ^ turn ^ side
            rows[pl.ds(slot, 1), :] = block[t : t + 1, :]
    wide = rows[...]
    squares = jnp.sum(wide * wide, axis=1, keepdims=True)
    narrow = wide.astype(jnp.bfloat16)

    fresh = [jnp.dot(narrow, w[...], preferred_element_type=jnp.float32) for w in (wk, wv)]
    sums = jnp.dot(narrow[:, :skip], first[...], preferred_element_type=jnp.float32)
    for (start, size), copy in zip(ranges, copies):
        copy.wait()
        sums = sums + jnp.dot(
            narrow[:, start : start + size],
            wq[start - skip : start - skip + size, :],
            preferred_element_type=jnp.float32,
        )

    total = keep_ref.shape[1]
    blocks = []
    for part in (sums, *fresh):
        blocks += [part[:, i : i + LANES] for i in range(0, part.shape[1], LANES)]
    blocks.append(jnp.broadcast_to(squares, (slots, LANES)))
    blocks += [jnp.zeros((slots, LANES), jnp.float32)] * (total - len(blocks))
    for ref, rows_at in ((keep_ref, 0), (send_ref, half)):
        flat = ref.reshape(half * total, LANES)
        for i, block in enumerate(blocks):
            flat[pl.ds(i, half, stride=total), :] = block[rows_at : rows_at + half]


def project(rows, other, w_query, first, key_weight, value_weight, slots):
    bits = slots.bit_length() - 1
    depth, query_width = w_query.shape
    kv_width = key_weight.shape[1]
    used = (query_width + 2 * kv_width) // LANES + 1
    total = -(-used // 8) * 8
    skip = first.shape[0]
    piece = jax.ShapeDtypeStruct((slots // 2, total, LANES), jnp.float32)
    whole = pl.BlockSpec(memory_space=pltpu.VMEM)
    return pl.pallas_call(
        functools.partial(project_kernel, bits),
        out_shape=(piece, piece),
        in_specs=[whole, whole, pl.BlockSpec(memory_space=pltpu.HBM), whole, whole, whole],
        out_specs=(whole, whole),
        scratch_shapes=[
            pltpu.VMEM((max(depth - skip, 16), query_width), jnp.bfloat16),
            pltpu.VMEM((slots, depth), jnp.float32),
            pltpu.SemaphoreType.DMA((max(1, len(spread(depth, skip, CHUNK))),)),
        ],
        compiler_params=pltpu.CompilerParams(vmem_limit_bytes=32 * MIB),
        cost_estimate=pl.CostEstimate(
            flops=2 * slots * depth * (query_width + 2 * kv_width),
            bytes_accessed=2 * depth * (query_width + 2 * kv_width),
            transcendentals=0,
        ),
        name="project",
    )(rows, other, in_hbm(w_query), first, key_weight, value_weight)


def attend_kernel(
    query_heads, kv_heads, pieces, length_ref, cosine_ref, sine_ref, k_ref, v_ref, *refs
):
    heads_ref = refs[pieces]
    total = refs[0][0]
    for ref in refs[1:pieces]:
        total = total + ref[0]
    at = query_heads + 2 * kv_heads
    scale = lax.rsqrt(total[at : at + 1, :] / MODEL_WIDTH + 1e-05)
    turned = total[: query_heads + kv_heads] * scale
    half = HEAD_SIZE // 2
    swapped = jnp.concatenate([turned[:, half:], turned[:, :half]], axis=1)
    turned = (turned * cosine_ref[...] + swapped * sine_ref[...]).astype(jnp.bfloat16)
    fresh_values = (total[query_heads + kv_heads : at] * scale).astype(jnp.bfloat16)
    group = query_heads // kv_heads
    factor = 1.0 / math.sqrt(HEAD_SIZE)
    length = length_ref[0]
    for head in range(kv_heads):
        queries = turned[head * group : (head + 1) * group]
        fresh_key = turned[query_heads + head : query_heads + head + 1].astype(jnp.float32)
        own = jnp.sum(queries.astype(jnp.float32) * fresh_key, axis=1, keepdims=True) * factor
        scores = (
            lax.dot_general(
                queries,
                k_ref[0, head],
                (((1,), (1,)), ((), ())),
                preferred_element_type=jnp.float32,
            )
            * factor
        )
        slot = lax.broadcasted_iota(jnp.int32, scores.shape, 1)
        scores = jnp.where(slot < length, scores, -jnp.inf)
        top = jnp.maximum(jnp.max(scores, axis=1, keepdims=True), own)
        exponent = jnp.exp(scores - top)
        own_exp = jnp.exp(own - top)
        share = 1.0 / (jnp.sum(exponent, axis=1, keepdims=True) + own_exp)
        weights = (exponent * share).astype(jnp.bfloat16)
        own_weight = (own_exp * share).astype(jnp.bfloat16)
        mixed = jnp.dot(weights, v_ref[0, head], preferred_element_type=jnp.float32)
        mixed = mixed + own_weight.astype(jnp.float32) * fresh_values[head : head + 1].astype(
            jnp.float32
        )
        heads_ref[0, pl.ds(head * group, group), :] = mixed.astype(jnp.bfloat16)


def attend(parts, cosine, sine, k_cache, value_cache, lengths, query_heads):
    kv_heads, cache_len = k_cache.shape[1:3]
    whole = pl.BlockSpec(memory_space=pltpu.VMEM)
    return pl.pallas_call(
        functools.partial(attend_kernel, query_heads, kv_heads, len(parts)),
        out_shape=jax.ShapeDtypeStruct((1, query_heads, HEAD_SIZE), jnp.bfloat16),
        in_specs=[pl.BlockSpec(memory_space=pltpu.SMEM)] + [whole] * (4 + len(parts)),
        out_specs=whole,
        compiler_params=pltpu.CompilerParams(vmem_limit_bytes=12 * MIB),
        cost_estimate=pl.CostEstimate(
            flops=4 * query_heads * cache_len * HEAD_SIZE,
            bytes_accessed=4 * kv_heads * cache_len * HEAD_SIZE,
            transcendentals=query_heads * cache_len,
        ),
        name="attend",
    )(lengths, cosine, sine, k_cache, value_cache, *parts)


def output_kernel(bits, pieces, staged, *refs):
    parts = refs[:pieces]
    ready = refs[pieces : pieces + staged]
    w_hbm, mine_ref, theirs_ref, rest, flat, left, sums, sems = refs[pieces + staged :]
    skip = sum(ref.shape[0] for ref in ready)
    ranges = spread(w_hbm.shape[0], skip, 2 * CHUNK)
    copies = []
    for i, (start, size) in enumerate(ranges):
        copies.append(
            pltpu.make_async_copy(
                w_hbm.at[pl.ds(start, size)], rest.at[pl.ds(start - skip, size)], sems.at[i]
            )
        )
        copies[-1].start()
    slots = left.shape[0]
    heads = flat.shape[0] // slots
    at = 0
    for ref in parts:
        for i in range(ref.shape[0]):
            flat[at : at + heads, :] = ref[i].astype(jnp.float32)
            at += heads
    for head in range(heads):
        left[:, head * HEAD_SIZE : (head + 1) * HEAD_SIZE] = flat[
            pl.ds(head, slots, stride=heads), :
        ].astype(jnp.bfloat16)
    total = None
    at = 0
    for ref in ready:
        size = ref.shape[0]
        term = jnp.dot(left[:, at : at + size], ref[...], preferred_element_type=jnp.float32)
        total = term if total is None else total + term
        at += size
    for (start, size), copy in zip(ranges, copies):
        copy.wait()
        term = jnp.dot(
            left[:, start : start + size],
            rest[start - skip : start - skip + size, :],
            preferred_element_type=jnp.float32,
        )
        total = term if total is None else total + term
    sums[...] = total
    half = slots // 2
    turn = bit_reverse(lax.axis_index("gx"), bits)
    gy = lax.axis_index("gy")
    for ref, side in ((mine_ref, gy), (theirs_ref, 1 - gy)):
        for t in range(half):
            slot = bit_reverse(t, bits) ^ turn ^ side
            ref[t : t + 1, :] = sums[pl.ds(slot, 1), :]


def output(parts, ready, w_out, slots):
    bits = slots.bit_length() - 1
    depth, width = w_out.shape
    heads = depth // HEAD_SIZE
    skip = sum(x.shape[0] for x in ready)
    whole = pl.BlockSpec(memory_space=pltpu.VMEM)
    piece = jax.ShapeDtypeStruct((slots // 2, width), jnp.float32)
    return pl.pallas_call(
        functools.partial(output_kernel, bits, len(parts), len(ready)),
        out_shape=(piece, piece),
        in_specs=[whole] * (len(parts) + len(ready)) + [pl.BlockSpec(memory_space=pltpu.HBM)],
        out_specs=(whole, whole),
        scratch_shapes=[
            pltpu.VMEM((max(depth - skip, 16), width), jnp.bfloat16),
            pltpu.VMEM((slots * heads, HEAD_SIZE), jnp.float32),
            pltpu.VMEM((slots, depth), jnp.bfloat16),
            pltpu.VMEM((slots, width), jnp.float32),
            pltpu.SemaphoreType.DMA((max(1, len(spread(depth, skip, 2 * CHUNK))),)),
        ],
        compiler_params=pltpu.CompilerParams(vmem_limit_bytes=24 * MIB),
        cost_estimate=pl.CostEstimate(
            flops=2 * slots * depth * width, bytes_accessed=2 * depth * width, transcendentals=0
        ),
        name="output",
    )(*parts, *ready, in_hbm(w_out))


def swap(block, axis, devices, mask):
    return lax.ppermute(block, axis, [(i, i ^ mask) for i in range(devices)])


def body(devices, activations, w_query, key_weight, value_weight, w_out, k_cache, value_cache, lengths):
    slots = devices
    query_heads = w_query.shape[1] // HEAD_SIZE
    half = HEAD_SIZE // 2
    frequency = jnp.power(
        jnp.float32(500000.0), -2.0 * jnp.arange(half, dtype=jnp.float32) / HEAD_SIZE
    )
    angle = lengths.astype(jnp.float32)[:, None] * frequency
    cosine = jnp.cos(angle)
    sine = jnp.sin(angle)
    cosine = jnp.concatenate([cosine, cosine], axis=1)
    sine = jnp.concatenate([-sine, sine], axis=1)

    bits = slots.bit_length() - 1
    direct = min(slots, 4)

    other = swap(activations, "gy", 2, 1)
    depth = w_query.shape[0]
    first, key_weight, value_weight = stage(
        (w_query, key_weight, value_weight), ((0, min(CHUNK, depth)), (0, depth), (0, depth))
    )
    send, keep = project(activations, other, w_query, first, key_weight, value_weight, slots)

    w_out, keep = lax.optimization_barrier((w_out, keep))
    rows_out = w_out.shape[0]
    third = rows_out * 3 // 8
    k_cache, value_cache, ready_one = stage(
        (k_cache, value_cache, w_out),
        ((0, k_cache.shape[0]), (0, value_cache.shape[0]), (0, third)),
    )
    mask = 1
    while True:
        arrived = swap(send, "gx", devices, mask)
        total = keep + arrived
        mask *= 2
        if total.shape[0] <= direct:
            break
        rest = total.shape[0] // 2
        keep, send = total[:rest], total[rest:]
    w_out, total = lax.optimization_barrier((w_out, total))
    (ready_two,) = stage((w_out,), ((third, third),))
    parts = [total[:1]] + [
        swap(total[j : j + 1], "gx", devices, bit_reverse(j, bits)) for j in range(1, direct)
    ]
    heads = attend(parts, cosine, sine, k_cache, value_cache, lengths, query_heads)

    parts = [heads] + [
        swap(heads, "gx", devices, bit_reverse(j, bits)) for j in range(1, direct)
    ]
    mask //= 2
    while mask:
        parts.append(swap(jnp.concatenate(parts, axis=0), "gx", devices, mask))
        mask //= 2
    mine, theirs = output(parts, (ready_one, ready_two), w_out, slots)
    return (mine + swap(theirs, "gy", 2, 1)).astype(jnp.bfloat16)


def solution(mesh):
    placed = (
        P(("groups", "gy"), "gx"),
        P("gx", "gy"),
        P("gx", "gy"),
        P("gx", "gy"),
        P("gy", "gx"),
        P(("groups", "gx"), "gy", None, None),
        P(("groups", "gx"), "gy", None, None),
        P(("groups", "gx")),
    )
    return jax.shard_map(
        functools.partial(body, mesh.shape["gx"]),
        mesh=mesh,
        in_specs=placed,
        out_specs=P(("groups", "gy"), "gx"),
        check_vma=False,
    )
```

time: 49.9 us -> 44 us (0.88)
  local copies, waits for them, and re-layouts: 5.61 us -> 0.01 us
  Pallas kernels: 14.2 us -> 18.8 us
  waiting for transfers between devices: 13.8 us -> 9.7 us
  starting transfers between devices: 14.4 us -> 13.5 us
    unnamed x10 -> x2, local copies, waits for them, and re-layouts: 5.61 us -> 0.01 us
    pallas_call x3 -> x5, Pallas kernels: 7.81 us -> 13 us  [the longest x3 8.46 us: stage(): pl.pallas_call(functools.partial(stage_kernel, parts), out_shape=shapes,...]
    ppermute x8 -> x10, waiting for transfers between devices: 13.8 us -> 9.7 us  [swap(): return lax.ppermute(block, axis, [(i, i ^ mask) for i in range(devices)])]
    ppermute x8 -> x10, starting transfers between devices: 14.4 us -> 13.5 us  [swap(): return lax.ppermute(block, axis, [(i, i ^ mask) for i in range(devices)])]
    pallas_call x1, Pallas kernels: 6.37 us -> 5.8 us  [project(): pl.pallas_call(functools.partial(project_kernel, bits), out_shape=(piece,...]
  transfers between devices with their start and end apart: 8 -> 10, of which waited for: 7 -> 5; matrix products, arithmetic and copies ran while one was open for 1% -> 1% of each run, Pallas kernels for 1% -> 19%
where the time goes in v4:
time: 44 us; the launch traced here: 43.8 us
  Pallas kernels  18.8 us (43%)
  starting transfers between devices  13.5 us (31%)
  waiting for transfers between devices  9.7 us (22%)
  other arithmetic  0.89 us (2%)
  between operations  0.78 us (2%)
    ppermute x10, starting transfers between devices, swap(): return lax.ppermute(block, axis, [(i, i ^ mask) for i in range(devices)])  13.5 us
    ppermute x10, waiting for transfers between devices, swap(): return lax.ppermute(block, axis, [(i, i ^ mask) for i in range(devices)])  9.7 us
    pallas_call x3, Pallas kernels, stage(): pl.pallas_call(functools.partial(stage_kernel, parts), out_shape=shapes,...  8.46 us
    pallas_call x1, Pallas kernels, project(): pl.pallas_call(functools.partial(project_kernel, bits), out_shape=(piece,...  5.8 us
    pallas_call x1, Pallas kernels, output(): pl.pallas_call(functools.partial(output_kernel, bits, len(parts), len(rea...  3.42 us
    pallas_call x1, Pallas kernels, attend(): pl.pallas_call(functools.partial(attend_kernel, query_heads, kv_heads, le...  1.16 us
  transfers between devices with their start and end apart: 10, of which 5 were waited for; matrix products, arithmetic and copies ran while one was open for 1% of the time, Pallas kernels for 19%

profile of v4, /device:TPU:0, one launch (start us, length us, event | category | flops | bytes accessed | tf_op | source)
XLA Modules:
  0.0 43.8 jit_solution(6020010101986744370)
XLA Ops:
  0.0 0.5 %collective-permute-start = (bf16[4,2048]{1,0:T(4,128)(2,1)}, bf16[4,2048]{1,0:T(4,128)(2,1)S(1)}, u32[]{:S(2)}, u32[]{:S(2)}) collective-permute-start(bf16[4,2048]{1,0:T(4,128)(2,1)} %rows_ref.1), channel_id=1, source_target_pairs={{0,1},{1,0},{2,3},{3,2},{4,5},{5,4},{6,7},{7,6},{8,9},{9,8},{10,11... | collective-permute-start | bytes 49160 | tf_op jit(solution)/shard_map/ppermute | solution.py:283
  1.2 0.1 fusion.2
  1.2 2.2 %stage.3 = (bf16[256,4096]{1,0:T(8,128)(2,1)S(1)}, bf16[2048,256]{1,0:T(8,128)(2,1)S(1)}, bf16[2048,256]{1,0:T(8,128)(2,1)S(1)}) custom-call(bf16[2048,4096]{1,0:T(8,128)(2,1)} %wq_hbm.1, bf16[2048,256]{1,0:T(8,128)(2,1)} %refs_1_.2, bf16[2048,256]{1,0:T(8,128)(2,1)} %refs_2_.1), custom_call_target="tpu_custom_call" | custom-call | bytes 4194304 | tf_op jit(solution)/shard_map/stage/pallas_call | solution.py:46
  3.5 5.8 %project.1 = (f32[4,40,128]{2,1,0:T(8,128)S(1)}, f32[4,40,128]{2,1,0:T(8,128)S(1)}) custom-call(bf16[4,2048]{1,0:T(4,128)(2,1)S(1)} %copy-done, bf16[4,2048]{1,0:T(4,128)(2,1)S(1)} %collective-permute-done.other_ref, bf16[2048,4096]{1,0:T(8,128)(2,1)} %wq_hbm.1, bf16[256,4096]{1,0:T(8,128)(2,1)S(1)} %get-tuple-element.19.first, ...), custom_call_target="tpu_custom_call" | custom-call | flops 150994944 | bytes 18874368 | tf_op jit(solution)/shard_map/project/pallas_call | solution.py:122
  9.3 2.6 %collective-permute-start.1 = (f32[4,40,128]{2,1,0:T(8,128)S(1)}, f32[4,40,128]{2,1,0:T(8,128)S(1)}, u32[]{:S(2)}, u32[]{:S(2)}) collective-permute-start(f32[4,40,128]{2,1,0:T(8,128)S(1)} %get-tuple-element.27), channel_id=1, source_target_pairs={{0,2},{2,0},{4,6},{6,4},{8,10},{10,8},{12,14},{14,12},{1,3},{3,1},... | collective-permute-start | bytes 245768 | tf_op jit(solution)/shard_map/ppermute | solution.py:283
  11.8 0.1 pad_maximum_fusion.1.cosine_ref
  11.9 3.0 %collective-permute-done.1 = f32[4,40,128]{2,1,0:T(8,128)S(1)} collective-permute-done((f32[4,40,128]{2,1,0:T(8,128)S(1)}, f32[4,40,128]{2,1,0:T(8,128)S(1)}, u32[]{:S(2)}, u32[]{:S(2)}) %collective-permute-start.1) | collective-permute-done | bytes 81952 | tf_op jit(solution)/shard_map/ppermute | solution.py:283
  15.0 2.9 %collective-permute-start.2 = (f32[1,40,128]{2,1,0:T(8,128)S(1)}, f32[1,40,128]{2,1,0:T(8,128)S(1)}, u32[]{:S(2)}, u32[]{:S(2)}) collective-permute-start(f32[1,40,128]{2,1,0:T(8,128)S(1)} %get-tuple-element.35), channel_id=1, source_target_pairs={{0,8},{2,10},{4,12},{6,14},{8,0},{10,2},{12,4},{14,6},{1,9},{3,11}... | collective-permute-start | bytes 61448 | tf_op jit(solution)/shard_map/ppermute | solution.py:283
  17.9 1.6 %collective-permute-start.3 = (f32[1,40,128]{2,1,0:T(8,128)S(1)}, f32[1,40,128]{2,1,0:T(8,128)S(1)}, u32[]{:S(2)}, u32[]{:S(2)}) collective-permute-start(f32[1,40,128]{2,1,0:T(8,128)S(1)} %get-tuple-element.34), channel_id=1, source_target_pairs={{0,4},{2,6},{4,0},{6,2},{8,12},{10,14},{12,8},{14,10},{1,5},{3,7},... | collective-permute-start | bytes 61448 | tf_op jit(solution)/shard_map/ppermute | solution.py:283
  19.5 0.1 pad_maximum_fusion.2.sine_ref
  19.5 3.5 %stage.4 = (bf16[1,2,2048,128]{3,2,1,0:T(8,128)(2,1)S(1)}, bf16[1,2,2048,128]{3,2,1,0:T(8,128)(2,1)S(1)}, bf16[1536,2048]{1,0:T(8,128)(2,1)S(1)}) custom-call(bf16[1,2,2048,128]{3,2,1,0:T(8,128)(2,1)} %refs_0_.3, bf16[1,2,2048,128]{3,2,1,0:T(8,128)(2,1)} %refs_1_.3, bf16[4096,2048]{1,0:T(8,128)(2,1)} %refs_7_), custom_call_target="tpu_custom_call" | custom-call | bytes 8388608 | tf_op jit(solution)/shard_map/stage/pallas_call | solution.py:46
  23.0 2.0 %collective-permute-done.4.refs_3_ = f32[1,40,128]{2,1,0:T(8,128)S(1)} collective-permute-done((f32[1,40,128]{2,1,0:T(8,128)S(1)}, f32[1,40,128]{2,1,0:T(8,128)S(1)}, u32[]{:S(2)}, u32[]{:S(2)}) %collective-permute-start.4) | collective-permute-done | bytes 20512 | tf_op jit(solution)/shard_map/ppermute | solution.py:283
  25.0 1.2 %attend.1.refs_0_ = bf16[1,32,128]{2,1,0:T(8,128)(2,1)S(1)} custom-call(s32[1]{0:T(128)S(6)} %copy.9.length_ref, f32[1,128]{1,0:T(1,128)S(1)} %pad_maximum_fusion.1.cosine_ref, f32[1,128]{1,0:T(1,128)S(1)} %pad_maximum_fusion.2.sine_ref, bf16[1,2,2048,128]{3,2,1,0:T(8,128)(2,1)S(1)} %get-tuple-element.24.k_ref, ...), custom_call_target="tpu_custom_call" | custom-call | flops 33554432 | bytes 2097152 | tf_op jit(solution)/shard_map/attend/pallas_call | solution.py:190
  26.2 0.1 collective-permute-start.5
  26.3 2.4 %collective-permute-start.6 = (bf16[1,32,128]{2,1,0:T(8,128)(2,1)S(1)}, bf16[1,32,128]{2,1,0:T(8,128)(2,1)S(1)}, u32[]{:S(2)}, u32[]{:S(2)}) collective-permute-start(bf16[1,32,128]{2,1,0:T(8,128)(2,1)S(1)} %attend.1.refs_0_), channel_id=1, source_target_pairs={{0,4},{2,6},{4,0},{6,2},{8,12},{10,14},{12,8},{14,10},{1,5},{3,7},... | collective-permute-start | bytes 24584 | tf_op jit(solution)/shard_map/ppermute | solution.py:283
  28.7 2.0 %collective-permute-start.7 = (bf16[1,32,128]{2,1,0:T(8,128)(2,1)S(1)}, bf16[1,32,128]{2,1,0:T(8,128)(2,1)S(1)}, u32[]{:S(2)}, u32[]{:S(2)}) collective-permute-start(bf16[1,32,128]{2,1,0:T(8,128)(2,1)S(1)} %attend.1.refs_0_), channel_id=1, source_target_pairs={{0,12},{2,14},{4,8},{6,10},{8,4},{10,6},{12,0},{14,2},{1,13},{3,15... | collective-permute-start | bytes 24584 | tf_op jit(solution)/shard_map/ppermute | solution.py:283
  30.7 0.2 collective-permute-done.5.refs_1_
  30.8 3.3 %collective-permute-done.7.refs_3_ = bf16[1,32,128]{2,1,0:T(8,128)(2,1)S(1)} collective-permute-done((bf16[1,32,128]{2,1,0:T(8,128)(2,1)S(1)}, bf16[1,32,128]{2,1,0:T(8,128)(2,1)S(1)}, u32[]{:S(2)}, u32[]{:S(2)}) %collective-permute-start.7) | collective-permute-done | bytes 8224 | tf_op jit(solution)/shard_map/ppermute | solution.py:283
  34.1 1.6 %collective-permute-start.8 = (bf16[4,32,128]{2,1,0:T(8,128)(2,1)S(1)}, bf16[4,32,128]{2,1,0:T(8,128)(2,1)S(1)}, u32[]{:S(2)}, u32[]{:S(2)}) collective-permute-start(bf16[4,32,128]{2,1,0:T(8,128)(2,1)S(1)} %pad_maximum_fusion), channel_id=1, source_target_pairs={{0,2},{2,0},{4,6},{6,4},{8,10},{10,8},{12,14},{14,12},{1,3},{3,1},... | collective-permute-start | bytes 98312 | tf_op jit(solution)/shard_map/ppermute | solution.py:283
  35.7 2.8 %stage.5.refs_6_ = bf16[1536,2048]{1,0:T(8,128)(2,1)S(1)} custom-call(bf16[4096,2048]{1,0:T(8,128)(2,1)} %refs_7_), custom_call_target="tpu_custom_call" | custom-call | bytes 6291456 | tf_op jit(solution)/shard_map/stage/pallas_call | solution.py:46
  38.5 3.4 %output.1 = (f32[4,2048]{1,0:T(4,128)S(1)}, f32[4,2048]{1,0:T(4,128)S(1)}) custom-call(bf16[1,32,128]{2,1,0:T(8,128)(2,1)S(1)} %attend.1.refs_0_, bf16[1,32,128]{2,1,0:T(8,128)(2,1)S(1)} %collective-permute-done.5.refs_1_, bf16[1,32,128]{2,1,0:T(8,128)(2,1)S(1)} %collective-permute-done.6.refs_2_, bf16[1,32,128]{2,1,0:T(8,128)(2,1)S(1)} %collective-permute-done.7.refs_3_, ...), custom_call_target="tpu_custom_call" | custom-call | flops 134217728 | bytes 16777216 | tf_op jit(solution)/shard_map/output/pallas_call | solution.py:262
  41.9 0.1 collective-permute-start.9
  42.0 1.2 %collective-permute-done.9 = f32[4,2048]{1,0:T(4,128)S(1)} collective-permute-done((f32[4,2048]{1,0:T(4,128)S(1)}, f32[4,2048]{1,0:T(4,128)S(1)}, u32[]{:S(2)}, u32[]{:S(2)}) %collective-permute-start.9) | collective-permute-done | bytes 32800 | tf_op jit(solution)/shard_map/ppermute | solution.py:283
  43.2 0.6 %add_convert_fusion = bf16[4,2048]{1,0:T(4,128)(2,1)} fusion(f32[4,2048]{1,0:T(4,128)S(1)} %get-tuple-element.31, f32[4,2048]{1,0:T(4,128)S(1)} %collective-permute-done.9), kind=kLoop, calls=%fused_computation.1 | loop fusion | flops 16384 | bytes 81920 | tf_op jit(solution)/shard_map/convert_element_type | solution.py:340
  (12 shorter events, 0.1 us)
Async XLA Ops:
  0.0 3.4 %collective-permute-start = (bf16[4,2048]{1,0:T(4,128)(2,1)}, bf16[4,2048]{1,0:T(4,128)(2,1)S(1)}, u32[]{:S(2)}, u32[]{:S(2)}) collective-permute-start(bf16[4,2048]{1,0:T(4,128)(2,1)} %rows_ref.1), channel_id=1, source_target_pairs={{0,1},{1,0},{2,3},{3,2},{4,5},{5,4},{6,7},{7,6},{8,9},{9,8},{10,11... | collective-permute-start | bytes 49160 | tf_op jit(solution)/shard_map/ppermute | solution.py:283
  1.2 2.2 %copy-start = (bf16[4,2048]{1,0:T(4,128)(2,1)S(1)}, bf16[4,2048]{1,0:T(4,128)(2,1)}, u32[]{:S(2)}) copy-start(bf16[4,2048]{1,0:T(4,128)(2,1)} %rows_ref.1) | copy-start | bytes 49156
  9.3 5.7 %collective-permute-start.1 = (f32[4,40,128]{2,1,0:T(8,128)S(1)}, f32[4,40,128]{2,1,0:T(8,128)S(1)}, u32[]{:S(2)}, u32[]{:S(2)}) collective-permute-start(f32[4,40,128]{2,1,0:T(8,128)S(1)} %get-tuple-element.27), channel_id=1, source_target_pairs={{0,2},{2,0},{4,6},{6,4},{8,10},{10,8},{12,14},{14,12},{1,3},{3,1},... | collective-permute-start | bytes 245768 | tf_op jit(solution)/shard_map/ppermute | solution.py:283
  15.0 8.0 %collective-permute-start.2 = (f32[1,40,128]{2,1,0:T(8,128)S(1)}, f32[1,40,128]{2,1,0:T(8,128)S(1)}, u32[]{:S(2)}, u32[]{:S(2)}) collective-permute-start(f32[1,40,128]{2,1,0:T(8,128)S(1)} %get-tuple-element.35), channel_id=1, source_target_pairs={{0,8},{2,10},{4,12},{6,14},{8,0},{10,2},{12,4},{14,6},{1,9},{3,11}... | collective-permute-start | bytes 61448 | tf_op jit(solution)/shard_map/ppermute | solution.py:283
  17.9 5.1 %collective-permute-start.3 = (f32[1,40,128]{2,1,0:T(8,128)S(1)}, f32[1,40,128]{2,1,0:T(8,128)S(1)}, u32[]{:S(2)}, u32[]{:S(2)}) collective-permute-start(f32[1,40,128]{2,1,0:T(8,128)S(1)} %get-tuple-element.34), channel_id=1, source_target_pairs={{0,4},{2,6},{4,0},{6,2},{8,12},{10,14},{12,8},{14,10},{1,5},{3,7},... | collective-permute-start | bytes 61448 | tf_op jit(solution)/shard_map/ppermute | solution.py:283
  19.5 5.6 %collective-permute-start.4 = (f32[1,40,128]{2,1,0:T(8,128)S(1)}, f32[1,40,128]{2,1,0:T(8,128)S(1)}, u32[]{:S(2)}, u32[]{:S(2)}) collective-permute-start(f32[1,40,128]{2,1,0:T(8,128)S(1)} %get-tuple-element.33), channel_id=1, source_target_pairs={{0,12},{2,14},{4,8},{6,10},{8,4},{10,6},{12,0},{14,2},{1,13},{3,15... | collective-permute-start | bytes 61448 | tf_op jit(solution)/shard_map/ppermute | solution.py:283
  26.2 4.6 %collective-permute-start.5 = (bf16[1,32,128]{2,1,0:T(8,128)(2,1)S(1)}, bf16[1,32,128]{2,1,0:T(8,128)(2,1)S(1)}, u32[]{:S(2)}, u32[]{:S(2)}) collective-permute-start(bf16[1,32,128]{2,1,0:T(8,128)(2,1)S(1)} %attend.1.refs_0_), channel_id=1, source_target_pairs={{0,8},{2,10},{4,12},{6,14},{8,0},{10,2},{12,4},{14,6},{1,9},{3,11}... | collective-permute-start | bytes 24584 | tf_op jit(solution)/shard_map/ppermute | solution.py:283
  26.3 4.5 %collective-permute-start.6 = (bf16[1,32,128]{2,1,0:T(8,128)(2,1)S(1)}, bf16[1,32,128]{2,1,0:T(8,128)(2,1)S(1)}, u32[]{:S(2)}, u32[]{:S(2)}) collective-permute-start(bf16[1,32,128]{2,1,0:T(8,128)(2,1)S(1)} %attend.1.refs_0_), channel_id=1, source_target_pairs={{0,4},{2,6},{4,0},{6,2},{8,12},{10,14},{12,8},{14,10},{1,5},{3,7},... | collective-permute-start | bytes 24584 | tf_op jit(solution)/shard_map/ppermute | solution.py:283
  28.7 5.4 %collective-permute-start.7 = (bf16[1,32,128]{2,1,0:T(8,128)(2,1)S(1)}, bf16[1,32,128]{2,1,0:T(8,128)(2,1)S(1)}, u32[]{:S(2)}, u32[]{:S(2)}) collective-permute-start(bf16[1,32,128]{2,1,0:T(8,128)(2,1)S(1)} %attend.1.refs_0_), channel_id=1, source_target_pairs={{0,12},{2,14},{4,8},{6,10},{8,4},{10,6},{12,0},{14,2},{1,13},{3,15... | collective-permute-start | bytes 24584 | tf_op jit(solution)/shard_map/ppermute | solution.py:283
  34.1 4.4 %collective-permute-start.8 = (bf16[4,32,128]{2,1,0:T(8,128)(2,1)S(1)}, bf16[4,32,128]{2,1,0:T(8,128)(2,1)S(1)}, u32[]{:S(2)}, u32[]{:S(2)}) collective-permute-start(bf16[4,32,128]{2,1,0:T(8,128)(2,1)S(1)} %pad_maximum_fusion), channel_id=1, source_target_pairs={{0,2},{2,0},{4,6},{6,4},{8,10},{10,8},{12,14},{14,12},{1,3},{3,1},... | collective-permute-start | bytes 98312 | tf_op jit(solution)/shard_map/ppermute | solution.py:283
  41.9 1.3 %collective-permute-start.9 = (f32[4,2048]{1,0:T(4,128)S(1)}, f32[4,2048]{1,0:T(4,128)S(1)}, u32[]{:S(2)}, u32[]{:S(2)}) collective-permute-start(f32[4,2048]{1,0:T(4,128)S(1)} %get-tuple-element.32), channel_id=1, source_target_pairs={{0,1},{1,0},{2,3},{3,2},{4,5},{5,4},{6,7},{7,6},{8,9},{9,8},{10,11... | collective-permute-start | bytes 98312 | tf_op jit(solution)/shard_map/ppermute | solution.py:283

commit v5 on v4

--- a/solution.py
+++ b/solution.py
@@ -12,6 +12,7 @@
 LANES = 128
 HEAD_SIZE = 128
 CHUNK = 256
+FAN = 4
 MIB = 2**20
 
 
@@ -62,8 +63,9 @@
 
 
 def project_kernel(
-    bits, rows_ref, other_ref, wq_hbm, first, wk, wv, send_ref, keep_ref, wq, rows, sems
+    bits, length_ref, rows_ref, other_ref, frequency_ref, wq_hbm, first, wk, wv, *refs
 ):
+    pieces, (turn_ref, wq, rows, sems) = refs[:FAN], refs[FAN:]
     skip = first.shape[0]
     ranges = spread(wq_hbm.shape[0], skip, CHUNK)
     copies = []
@@ -88,6 +90,14 @@
     squares = jnp.sum(wide * wide, axis=1, keepdims=True)
     narrow = wide.astype(jnp.bfloat16)
 
+    position = length_ref[0].astype(jnp.float32)
+    angle = position * frequency_ref[...]
+    lane = lax.broadcasted_iota(jnp.int32, angle.shape, 1)
+    sine = jnp.sin(angle)
+    turn_ref[0:1, :] = jnp.cos(angle)
+    turn_ref[1:2, :] = jnp.where(lane < HEAD_SIZE // 2, -sine, sine)
+    turn_ref[2:3, :] = jnp.full(angle.shape, position)
+
     fresh = [jnp.dot(narrow, w[...], preferred_element_type=jnp.float32) for w in (wk, wv)]
     sums = jnp.dot(narrow[:, :skip], first[...], preferred_element_type=jnp.float32)
     for (start, size), copy in zip(ranges, copies):
@@ -98,32 +108,34 @@
             preferred_element_type=jnp.float32,
         )
 
-    total = keep_ref.shape[1]
+    total = pieces[0].shape[1]
     blocks = []
     for part in (sums, *fresh):
         blocks += [part[:, i : i + LANES] for i in range(0, part.shape[1], LANES)]
     blocks.append(jnp.broadcast_to(squares, (slots, LANES)))
     blocks += [jnp.zeros((slots, LANES), jnp.float32)] * (total - len(blocks))
-    for ref, rows_at in ((keep_ref, 0), (send_ref, half)):
-        flat = ref.reshape(half * total, LANES)
+    size = slots // FAN
+    for at, ref in enumerate(pieces):
+        flat = ref.reshape(size * total, LANES)
         for i, block in enumerate(blocks):
-            flat[pl.ds(i, half, stride=total), :] = block[rows_at : rows_at + half]
-
-
-def project(rows, other, w_query, first, key_weight, value_weight, slots):
+            flat[pl.ds(i, size, stride=total), :] = block[at * size : (at + 1) * size]
+
+
+def project(lengths, rows, other, frequency, w_query, first, key_weight, value_weight, slots):
     bits = slots.bit_length() - 1
     depth, query_width = w_query.shape
     kv_width = key_weight.shape[1]
     used = (query_width + 2 * kv_width) // LANES + 1
     total = -(-used // 8) * 8
     skip = first.shape[0]
-    piece = jax.ShapeDtypeStruct((slots // 2, total, LANES), jnp.float32)
+    piece = jax.ShapeDtypeStruct((slots // FAN, total, LANES), jnp.float32)
+    hbm = pl.BlockSpec(memory_space=pltpu.HBM)
     whole = pl.BlockSpec(memory_space=pltpu.VMEM)
     return pl.pallas_call(
         functools.partial(project_kernel, bits),
-        out_shape=(piece, piece),
-        in_specs=[whole, whole, pl.BlockSpec(memory_space=pltpu.HBM), whole, whole, whole],
-        out_specs=(whole, whole),
+        out_shape=(piece,) * FAN + (jax.ShapeDtypeStruct((8, HEAD_SIZE), jnp.float32),),
+        in_specs=[pl.BlockSpec(memory_space=pltpu.SMEM), whole, whole, whole, hbm, whole, whole, whole],
+        out_specs=(whole,) * (FAN + 1),
         scratch_shapes=[
             pltpu.VMEM((max(depth - skip, 16), query_width), jnp.bfloat16),
             pltpu.VMEM((slots, depth), jnp.float32),
@@ -136,11 +148,11 @@
             transcendentals=0,
         ),
         name="project",
-    )(rows, other, in_hbm(w_query), first, key_weight, value_weight)
+    )(lengths, rows, other, frequency, in_hbm(w_query), first, key_weight, value_weight)
 
 
 def attend_kernel(
-    query_heads, kv_heads, pieces, length_ref, cosine_ref, sine_ref, k_ref, v_ref, *refs
+    query_heads, kv_heads, pieces, turn_ref, k_ref, v_ref, *refs
 ):
     heads_ref = refs[pieces]
     total = refs[0][0]
@@ -151,11 +163,11 @@
     turned = total[: query_heads + kv_heads] * scale
     half = HEAD_SIZE // 2
     swapped = jnp.concatenate([turned[:, half:], turned[:, :half]], axis=1)
-    turned = (turned * cosine_ref[...] + swapped * sine_ref[...]).astype(jnp.bfloat16)
+    turned = (turned * turn_ref[0:1, :] + swapped * turn_ref[1:2, :]).astype(jnp.bfloat16)
     fresh_values = (total[query_heads + kv_heads : at] * scale).astype(jnp.bfloat16)
     group = query_heads // kv_heads
     factor = 1.0 / math.sqrt(HEAD_SIZE)
-    length = length_ref[0]
+    length = turn_ref[2:3, 0:1].astype(jnp.int32)
     for head in range(kv_heads):
         queries = turned[head * group : (head + 1) * group]
         fresh_key = turned[query_heads + head : query_heads + head + 1].astype(jnp.float32)
@@ -184,13 +196,13 @@
         heads_ref[0, pl.ds(head * group, group), :] = mixed.astype(jnp.bfloat16)
 
 
-def attend(parts, cosine, sine, k_cache, value_cache, lengths, query_heads):
+def attend(parts, turn, k_cache, value_cache, query_heads):
     kv_heads, cache_len = k_cache.shape[1:3]
     whole = pl.BlockSpec(memory_space=pltpu.VMEM)
     return pl.pallas_call(
         functools.partial(attend_kernel, query_heads, kv_heads, len(parts)),
         out_shape=jax.ShapeDtypeStruct((1, query_heads, HEAD_SIZE), jnp.bfloat16),
-        in_specs=[pl.BlockSpec(memory_space=pltpu.SMEM)] + [whole] * (4 + len(parts)),
+        in_specs=[whole] * (3 + len(parts)),
         out_specs=whole,
         compiler_params=pltpu.CompilerParams(vmem_limit_bytes=12 * MIB),
         cost_estimate=pl.CostEstimate(
@@ -199,7 +211,7 @@
             transcendentals=query_heads * cache_len,
         ),
         name="attend",
-    )(lengths, cosine, sine, k_cache, value_cache, *parts)
+    )(turn, k_cache, value_cache, *parts)
 
 
 def output_kernel(bits, pieces, staged, *refs):
@@ -283,60 +295,62 @@
     return lax.ppermute(block, axis, [(i, i ^ mask) for i in range(devices)])
 
 
+def fan(pieces, devices):
+    masks = [bit_reverse(q, 2) for q in range(FAN)]
+    arrived = [None] * FAN
+    for q in sorted(range(1, FAN), key=lambda q: (masks[q] + 1) % FAN):
+        arrived[q] = swap(pieces[q], "gx", devices, masks[q])
+    return arrived[1:]
+
+
 def body(devices, activations, w_query, key_weight, value_weight, w_out, k_cache, value_cache, lengths):
     slots = devices
     query_heads = w_query.shape[1] // HEAD_SIZE
-    half = HEAD_SIZE // 2
-    frequency = jnp.power(
-        jnp.float32(500000.0), -2.0 * jnp.arange(half, dtype=jnp.float32) / HEAD_SIZE
-    )
-    angle = lengths.astype(jnp.float32)[:, None] * frequency
-    cosine = jnp.cos(angle)
-    sine = jnp.sin(angle)
-    cosine = jnp.concatenate([cosine, cosine], axis=1)
-    sine = jnp.concatenate([-sine, sine], axis=1)
-
-    bits = slots.bit_length() - 1
-    direct = min(slots, 4)
-
     other = swap(activations, "gy", 2, 1)
     depth = w_query.shape[0]
     first, key_weight, value_weight = stage(
         (w_query, key_weight, value_weight), ((0, min(CHUNK, depth)), (0, depth), (0, depth))
     )
-    send, keep = project(activations, other, w_query, first, key_weight, value_weight, slots)
-
-    w_out, keep = lax.optimization_barrier((w_out, keep))
+    half = HEAD_SIZE // 2
+    frequency = jnp.power(
+        jnp.float32(500000.0), -2.0 * jnp.arange(half, dtype=jnp.float32) / HEAD_SIZE
+    )
+    frequency = jnp.concatenate([frequency, frequency])[None, :]
+    *pieces, turn = project(
+        lengths, activations, other, frequency, w_query, first, key_weight, value_weight, slots
+    )
+
     rows_out = w_out.shape[0]
-    third = rows_out * 3 // 8
+    few, most = rows_out // 8, rows_out * 3 // 8
+    arrived = fan(pieces, devices)
     k_cache, value_cache, ready_one = stage(
         (k_cache, value_cache, w_out),
-        ((0, k_cache.shape[0]), (0, value_cache.shape[0]), (0, third)),
-    )
-    mask = 1
-    while True:
-        arrived = swap(send, "gx", devices, mask)
-        total = keep + arrived
+        ((0, k_cache.shape[0]), (0, value_cache.shape[0]), (0, few)),
+    )
+    total = pieces[0] + (arrived[2] + (arrived[1] + arrived[0]))
+    mask = FAN
+    while total.shape[0] > 2:
+        rest = total.shape[0] // 2
+        total = total[:rest] + swap(total[rest:], "gx", devices, mask)
         mask *= 2
-        if total.shape[0] <= direct:
-            break
-        rest = total.shape[0] // 2
-        keep, send = total[:rest], total[rest:]
-    w_out, total = lax.optimization_barrier((w_out, total))
-    (ready_two,) = stage((w_out,), ((third, third),))
-    parts = [total[:1]] + [
-        swap(total[j : j + 1], "gx", devices, bit_reverse(j, bits)) for j in range(1, direct)
-    ]
-    heads = attend(parts, cosine, sine, k_cache, value_cache, lengths, query_heads)
-
-    parts = [heads] + [
-        swap(heads, "gx", devices, bit_reverse(j, bits)) for j in range(1, direct)
-    ]
-    mask //= 2
-    while mask:
+    total, w_out, k_cache, value_cache, ready_one = lax.optimization_barrier(
+        (total, w_out, k_cache, value_cache, ready_one)
+    )
+    (ready_two,) = stage((w_out,), ((few, most),))
+    parts = [total[:1], swap(total[1:], "gx", devices, mask)]
+    parts[1], ready_two = lax.optimization_barrier((parts[1], ready_two))
+    heads = attend(parts, turn, k_cache, value_cache, query_heads)
+
+    heads, w_out = lax.optimization_barrier((heads, w_out))
+    (ready_three,) = stage((w_out,), ((few + most, most),))
+    parts = [heads, swap(heads, "gx", devices, mask)]
+    parts[1], ready_three = lax.optimization_barrier((parts[1], ready_three))
+    while mask > FAN:
+        mask //= 2
         parts.append(swap(jnp.concatenate(parts, axis=0), "gx", devices, mask))
-        mask //= 2
-    mine, theirs = output(parts, (ready_one, ready_two), w_out, slots)
+    held = jnp.concatenate(parts, axis=0)
+    parts += fan([held] * FAN, devices)
+    mine, theirs = output(parts, (ready_one, ready_two, ready_three), w_out, slots)
     return (mine + swap(theirs, "gy", 2, 1)).astype(jnp.bfloat16)
 
 

time: 44 us -> 39.8 us (0.905)
  waiting for transfers between devices: 9.7 us -> 4.98 us
  Pallas kernels: 18.8 us -> 20.2 us
  starting transfers between devices: 13.5 us -> 12.9 us
    ppermute x10, waiting for transfers between devices: 9.7 us -> 4.98 us  [swap(): return lax.ppermute(block, axis, [(i, i ^ mask) for i in range(devices)])]
    pallas_call x3 -> x4, Pallas kernels: 8.46 us -> 10 us  [stage(): pl.pallas_call(functools.partial(stage_kernel, parts), out_shape=shapes,...]
    ppermute x10, starting transfers between devices: 13.5 us -> 12.9 us  [swap(): return lax.ppermute(block, axis, [(i, i ^ mask) for i in range(devices)])]
  transfers between devices with their start and end apart: 10 -> 10, of which waited for: 5 -> 6; matrix products, arithmetic and copies ran while one was open for 1% -> 0% of each run, Pallas kernels for 19% -> 25%
where the time goes in v5:
time: 39.8 us; the launch traced here: 39.5 us
  Pallas kernels  20.2 us (51%)
  starting transfers between devices  12.9 us (32%)
  waiting for transfers between devices  4.98 us (13%)
  between operations  0.78 us (2%)
  other arithmetic  0.72 us (2%)
    ppermute x10, starting transfers between devices, swap(): return lax.ppermute(block, axis, [(i, i ^ mask) for i in range(devices)])  12.9 us
    pallas_call x4, Pallas kernels, stage(): pl.pallas_call(functools.partial(stage_kernel, parts), out_shape=shapes,...  10 us
    pallas_call x1, Pallas kernels, project(): pl.pallas_call(functools.partial(project_kernel, bits), out_shape=(piece,...  5.77 us
    ppermute x10, waiting for transfers between devices, swap(): return lax.ppermute(block, axis, [(i, i ^ mask) for i in range(devices)])  4.98 us
    pallas_call x1, Pallas kernels, output(): pl.pallas_call(functools.partial(output_kernel, bits, len(parts), len(rea...  3.19 us
    pallas_call x1, Pallas kernels, attend(): pl.pallas_call(functools.partial(attend_kernel, query_heads, kv_heads, le...  1.16 us
  transfers between devices with their start and end apart: 10, of which 6 were waited for; matrix products, arithmetic and copies ran while one was open for 0% of the time, Pallas kernels for 25%

profile of v5, /device:TPU:0, one launch (start us, length us, event | category | flops | bytes accessed | tf_op | source)
XLA Modules:
  0.0 39.5 jit_solution(5120781503235468444)
XLA Ops:
  0.0 0.5 %collective-permute-start = (bf16[4,2048]{1,0:T(4,128)(2,1)}, bf16[4,2048]{1,0:T(4,128)(2,1)S(1)}, u32[]{:S(2)}, u32[]{:S(2)}) collective-permute-start(bf16[4,2048]{1,0:T(4,128)(2,1)} %rows_ref.1), channel_id=1, source_target_pairs={{0,1},{1,0},{2,3},{3,2},{4,5},{5,4},{6,7},{7,6},{8,9},{9,8},{10,11... | collective-permute-start | bytes 49160 | tf_op jit(solution)/shard_map/ppermute | solution.py:295
  0.5 0.1 maximum_bitcast_fusion.frequency_ref
  1.2 2.2 %stage.4 = (bf16[256,4096]{1,0:T(8,128)(2,1)S(1)}, bf16[2048,256]{1,0:T(8,128)(2,1)S(1)}, bf16[2048,256]{1,0:T(8,128)(2,1)S(1)}) custom-call(bf16[2048,4096]{1,0:T(8,128)(2,1)} %wq_hbm.1, bf16[2048,256]{1,0:T(8,128)(2,1)} %refs_1_.2, bf16[2048,256]{1,0:T(8,128)(2,1)} %refs_2_.2), custom_call_target="tpu_custom_call" | custom-call | bytes 4194304 | tf_op jit(solution)/shard_map/stage/pallas_call | solution.py:47
  3.4 5.8 %project.1 = (f32[2,40,128]{2,1,0:T(8,128)S(1)}, f32[2,40,128]{2,1,0:T(8,128)S(1)}, f32[2,40,128]{2,1,0:T(8,128)S(1)}, f32[2,40,128]{2,1,0:T(8,128)S(1)}, f32[8,128]{1,0:T(8,128)S(1)}) custom-call(s32[1]{0:T(128)S(6)} %copy.10.length_ref, bf16[4,2048]{1,0:T(4,128)(2,1)S(1)} %copy-done, bf16[4,2048]{1,0:T(4,128)(2,1)S(1)} %collective-permute-done.other_ref, ...), custom_call_target="tpu_custom_call" | custom-call | flops 150994944 | bytes 18874368 | tf_op jit(solution)/shard_map/project/pallas_call | solution.py:134
  9.2 3.6 %collective-permute-start.1 = (f32[2,40,128]{2,1,0:T(8,128)S(1)}, f32[2,40,128]{2,1,0:T(8,128)S(1)}, u32[]{:S(2)}, u32[]{:S(2)}) collective-permute-start(f32[2,40,128]{2,1,0:T(8,128)S(1)} %get-tuple-element.34), channel_id=1, source_target_pairs={{0,6},{2,4},{4,2},{6,0},{8,14},{10,12},{12,10},{14,8},{1,7},{3,5},... | collective-permute-start | bytes 122888 | tf_op jit(solution)/shard_map/ppermute | solution.py:295
  12.8 0.5 %collective-permute-start.2 = (f32[2,40,128]{2,1,0:T(8,128)S(1)}, f32[2,40,128]{2,1,0:T(8,128)S(1)}, u32[]{:S(2)}, u32[]{:S(2)}) collective-permute-start(f32[2,40,128]{2,1,0:T(8,128)S(1)} %get-tuple-element.35), channel_id=1, source_target_pairs={{0,2},{2,0},{4,6},{6,4},{8,10},{10,8},{12,14},{14,12},{1,3},{3,1},... | collective-permute-start | bytes 122888 | tf_op jit(solution)/shard_map/ppermute | solution.py:295
  13.3 0.1 collective-permute-start.3
  13.4 2.3 %stage.5 = (bf16[1,2,2048,128]{3,2,1,0:T(8,128)(2,1)S(1)}, bf16[1,2,2048,128]{3,2,1,0:T(8,128)(2,1)S(1)}, bf16[512,2048]{1,0:T(8,128)(2,1)S(1)}) custom-call(bf16[1,2,2048,128]{3,2,1,0:T(8,128)(2,1)} %refs_0_.3, bf16[1,2,2048,128]{3,2,1,0:T(8,128)(2,1)} %refs_1_.3, bf16[4096,2048]{1,0:T(8,128)(2,1)} %refs_8_), custom_call_target="tpu_custom_call" | custom-call | bytes 4194304 | tf_op jit(solution)/shard_map/stage/pallas_call | solution.py:47
  15.7 1.1 %collective-permute-done.2 = f32[2,40,128]{2,1,0:T(8,128)S(1)} collective-permute-done((f32[2,40,128]{2,1,0:T(8,128)S(1)}, f32[2,40,128]{2,1,0:T(8,128)S(1)}, u32[]{:S(2)}, u32[]{:S(2)}) %collective-permute-start.2) | collective-permute-done | bytes 40992 | tf_op jit(solution)/shard_map/ppermute | solution.py:295
  16.8 0.5 %collective-permute-done.3 = f32[2,40,128]{2,1,0:T(8,128)S(1)} collective-permute-done((f32[2,40,128]{2,1,0:T(8,128)S(1)}, f32[2,40,128]{2,1,0:T(8,128)S(1)}, u32[]{:S(2)}, u32[]{:S(2)}) %collective-permute-start.3) | collective-permute-done | bytes 40992 | tf_op jit(solution)/shard_map/ppermute | solution.py:295
  17.3 2.7 %collective-permute-start.4 = (f32[1,40,128]{2,1,0:T(8,128)S(1)}, f32[1,40,128]{2,1,0:T(8,128)S(1)}, u32[]{:S(2)}, u32[]{:S(2)}) collective-permute-start(f32[1,40,128]{2,1,0:T(8,128)S(1)} %get-tuple-element.53), channel_id=1, source_target_pairs={{0,8},{2,10},{4,12},{6,14},{8,0},{10,2},{12,4},{14,6},{1,9},{3,11}... | collective-permute-start | bytes 61448 | tf_op jit(solution)/shard_map/ppermute | solution.py:295
  20.0 2.8 %stage.6.refs_6_ = bf16[1536,2048]{1,0:T(8,128)(2,1)S(1)} custom-call(bf16[4096,2048]{1,0:T(8,128)(2,1)} %refs_8_), custom_call_target="tpu_custom_call" | custom-call | bytes 6291456 | tf_op jit(solution)/shard_map/stage/pallas_call | solution.py:47
  22.8 1.2 %attend.1.refs_0_ = bf16[1,32,128]{2,1,0:T(8,128)(2,1)S(1)} custom-call(f32[8,128]{1,0:T(8,128)S(1)} %get-tuple-element.32.turn_ref, bf16[1,2,2048,128]{3,2,1,0:T(8,128)(2,1)S(1)} %get-tuple-element.40.k_ref, bf16[1,2,2048,128]{3,2,1,0:T(8,128)(2,1)S(1)} %get-tuple-element.41.v_ref, f32[1,40,128]{2,1,0:T(8,128)S(1)} %get-tuple-element.54.refs_0_, ...), custom_call_target="tpu_custom_call" | custom-call | flops 33554432 | bytes 2097152 | tf_op jit(solution)/shard_map/attend/pallas_call | solution.py:202
  24.0 1.9 %collective-permute-start.5 = (bf16[1,32,128]{2,1,0:T(8,128)(2,1)S(1)}, bf16[1,32,128]{2,1,0:T(8,128)(2,1)S(1)}, u32[]{:S(2)}, u32[]{:S(2)}) collective-permute-start(bf16[1,32,128]{2,1,0:T(8,128)(2,1)S(1)} %attend.1.refs_0_), channel_id=1, source_target_pairs={{0,8},{2,10},{4,12},{6,14},{8,0},{10,2},{12,4},{14,6},{1,9},{3,11}... | collective-permute-start | bytes 24584 | tf_op jit(solution)/shard_map/ppermute | solution.py:295
  25.9 2.8 %stage.7.refs_7_ = bf16[1536,2048]{1,0:T(8,128)(2,1)S(1)} custom-call(bf16[4096,2048]{1,0:T(8,128)(2,1)} %refs_8_), custom_call_target="tpu_custom_call" | custom-call | bytes 6291456 | tf_op jit(solution)/shard_map/stage/pallas_call | solution.py:47
  28.7 1.4 %collective-permute-start.8 = (bf16[2,32,128]{2,1,0:T(8,128)(2,1)S(1)}, bf16[2,32,128]{2,1,0:T(8,128)(2,1)S(1)}, u32[]{:S(2)}, u32[]{:S(2)}) collective-permute-start(bf16[2,32,128]{2,1,0:T(8,128)(2,1)S(1)} %constant_dynamic-update-slice_fusion), channel_id=1, source_target_pairs={{0,6},{2,4},{4,2},{6,0},{8,14},{10,12},{12,10},{14,8},{1,7},{3,5},... | collective-permute-start | bytes 49160 | tf_op jit(solution)/shard_map/ppermute | solution.py:295
  30.2 0.5 %collective-permute-start.7 = (bf16[2,32,128]{2,1,0:T(8,128)(2,1)S(1)}, bf16[2,32,128]{2,1,0:T(8,128)(2,1)S(1)}, u32[]{:S(2)}, u32[]{:S(2)}) collective-permute-start(bf16[2,32,128]{2,1,0:T(8,128)(2,1)S(1)} %constant_dynamic-update-slice_fusion), channel_id=1, source_target_pairs={{0,2},{2,0},{4,6},{6,4},{8,10},{10,8},{12,14},{14,12},{1,3},{3,1},... | collective-permute-start | bytes 49160 | tf_op jit(solution)/shard_map/ppermute | solution.py:295
  30.7 1.6 %collective-permute-start.6 = (bf16[2,32,128]{2,1,0:T(8,128)(2,1)S(1)}, bf16[2,32,128]{2,1,0:T(8,128)(2,1)S(1)}, u32[]{:S(2)}, u32[]{:S(2)}) collective-permute-start(bf16[2,32,128]{2,1,0:T(8,128)(2,1)S(1)} %constant_dynamic-update-slice_fusion), channel_id=1, source_target_pairs={{0,4},{2,6},{4,0},{6,2},{8,12},{10,14},{12,8},{14,10},{1,5},{3,7},... | collective-permute-start | bytes 49160 | tf_op jit(solution)/shard_map/ppermute | solution.py:295
  32.3 1.1 %collective-permute-done.8.refs_4_ = bf16[2,32,128]{2,1,0:T(8,128)(2,1)S(1)} collective-permute-done((bf16[2,32,128]{2,1,0:T(8,128)(2,1)S(1)}, bf16[2,32,128]{2,1,0:T(8,128)(2,1)S(1)}, u32[]{:S(2)}, u32[]{:S(2)}) %collective-permute-start.8) | collective-permute-done | bytes 16416 | tf_op jit(solution)/shard_map/ppermute | solution.py:295
  33.4 0.5 %collective-permute-done.7.refs_3_ = bf16[2,32,128]{2,1,0:T(8,128)(2,1)S(1)} collective-permute-done((bf16[2,32,128]{2,1,0:T(8,128)(2,1)S(1)}, bf16[2,32,128]{2,1,0:T(8,128)(2,1)S(1)}, u32[]{:S(2)}, u32[]{:S(2)}) %collective-permute-start.7) | collective-permute-done | bytes 16416 | tf_op jit(solution)/shard_map/ppermute | solution.py:295
  33.9 0.5 %collective-permute-done.6.refs_2_ = bf16[2,32,128]{2,1,0:T(8,128)(2,1)S(1)} collective-permute-done((bf16[2,32,128]{2,1,0:T(8,128)(2,1)S(1)}, bf16[2,32,128]{2,1,0:T(8,128)(2,1)S(1)}, u32[]{:S(2)}, u32[]{:S(2)}) %collective-permute-start.6) | collective-permute-done | bytes 16416 | tf_op jit(solution)/shard_map/ppermute | solution.py:295
  34.4 3.2 %output.1 = (f32[4,2048]{1,0:T(4,128)S(1)}, f32[4,2048]{1,0:T(4,128)S(1)}) custom-call(bf16[1,32,128]{2,1,0:T(8,128)(2,1)S(1)} %attend.1.refs_0_, bf16[1,32,128]{2,1,0:T(8,128)(2,1)S(1)} %collective-permute-done.5.refs_1_, bf16[2,32,128]{2,1,0:T(8,128)(2,1)S(1)} %collective-permute-done.6.refs_2_, bf16[2,32,128]{2,1,0:T(8,128)(2,1)S(1)} %collective-permute-done.7.refs_3_, ...), custom_call_target="tpu_custom_call" | custom-call | flops 134217728 | bytes 16777216 | tf_op jit(solution)/shard_map/output/pallas_call | solution.py:274
  37.7 1.2 %collective-permute-done.9 = f32[4,2048]{1,0:T(4,128)S(1)} collective-permute-done((f32[4,2048]{1,0:T(4,128)S(1)}, f32[4,2048]{1,0:T(4,128)S(1)}, u32[]{:S(2)}, u32[]{:S(2)}) %collective-permute-start.9) | collective-permute-done | bytes 32800 | tf_op jit(solution)/shard_map/ppermute | solution.py:295
  38.9 0.6 %add_convert_fusion = bf16[4,2048]{1,0:T(4,128)(2,1)} fusion(f32[4,2048]{1,0:T(4,128)S(1)} %get-tuple-element.51, f32[4,2048]{1,0:T(4,128)S(1)} %collective-permute-done.9), kind=kLoop, calls=%fused_computation.1 | loop fusion | flops 16384 | bytes 81920 | tf_op jit(solution)/shard_map/convert_element_type | solution.py:354
  (12 shorter events, 0.1 us)
Async XLA Ops:
  0.0 3.4 %collective-permute-start = (bf16[4,2048]{1,0:T(4,128)(2,1)}, bf16[4,2048]{1,0:T(4,128)(2,1)S(1)}, u32[]{:S(2)}, u32[]{:S(2)}) collective-permute-start(bf16[4,2048]{1,0:T(4,128)(2,1)} %rows_ref.1), channel_id=1, source_target_pairs={{0,1},{1,0},{2,3},{3,2},{4,5},{5,4},{6,7},{7,6},{8,9},{9,8},{10,11... | collective-permute-start | bytes 49160 | tf_op jit(solution)/shard_map/ppermute | solution.py:295
  1.2 2.2 %copy-start = (bf16[4,2048]{1,0:T(4,128)(2,1)S(1)}, bf16[4,2048]{1,0:T(4,128)(2,1)}, u32[]{:S(2)}) copy-start(bf16[4,2048]{1,0:T(4,128)(2,1)} %rows_ref.1) | copy-start | bytes 49156
  9.2 6.5 %collective-permute-start.1 = (f32[2,40,128]{2,1,0:T(8,128)S(1)}, f32[2,40,128]{2,1,0:T(8,128)S(1)}, u32[]{:S(2)}, u32[]{:S(2)}) collective-permute-start(f32[2,40,128]{2,1,0:T(8,128)S(1)} %get-tuple-element.34), channel_id=1, source_target_pairs={{0,6},{2,4},{4,2},{6,0},{8,14},{10,12},{12,10},{14,8},{1,7},{3,5},... | collective-permute-start | bytes 122888 | tf_op jit(solution)/shard_map/ppermute | solution.py:295
  12.8 4.0 %collective-permute-start.2 = (f32[2,40,128]{2,1,0:T(8,128)S(1)}, f32[2,40,128]{2,1,0:T(8,128)S(1)}, u32[]{:S(2)}, u32[]{:S(2)}) collective-permute-start(f32[2,40,128]{2,1,0:T(8,128)S(1)} %get-tuple-element.35), channel_id=1, source_target_pairs={{0,2},{2,0},{4,6},{6,4},{8,10},{10,8},{12,14},{14,12},{1,3},{3,1},... | collective-permute-start | bytes 122888 | tf_op jit(solution)/shard_map/ppermute | solution.py:295
  13.3 4.0 %collective-permute-start.3 = (f32[2,40,128]{2,1,0:T(8,128)S(1)}, f32[2,40,128]{2,1,0:T(8,128)S(1)}, u32[]{:S(2)}, u32[]{:S(2)}) collective-permute-start(f32[2,40,128]{2,1,0:T(8,128)S(1)} %get-tuple-element.36), channel_id=1, source_target_pairs={{0,4},{2,6},{4,0},{6,2},{8,12},{10,14},{12,8},{14,10},{1,5},{3,7},... | collective-permute-start | bytes 122888 | tf_op jit(solution)/shard_map/ppermute | solution.py:295
  17.3 5.5 %collective-permute-start.4 = (f32[1,40,128]{2,1,0:T(8,128)S(1)}, f32[1,40,128]{2,1,0:T(8,128)S(1)}, u32[]{:S(2)}, u32[]{:S(2)}) collective-permute-start(f32[1,40,128]{2,1,0:T(8,128)S(1)} %get-tuple-element.53), channel_id=1, source_target_pairs={{0,8},{2,10},{4,12},{6,14},{8,0},{10,2},{12,4},{14,6},{1,9},{3,11}... | collective-permute-start | bytes 61448 | tf_op jit(solution)/shard_map/ppermute | solution.py:295
  24.0 4.7 %collective-permute-start.5 = (bf16[1,32,128]{2,1,0:T(8,128)(2,1)S(1)}, bf16[1,32,128]{2,1,0:T(8,128)(2,1)S(1)}, u32[]{:S(2)}, u32[]{:S(2)}) collective-permute-start(bf16[1,32,128]{2,1,0:T(8,128)(2,1)S(1)} %attend.1.refs_0_), channel_id=1, source_target_pairs={{0,8},{2,10},{4,12},{6,14},{8,0},{10,2},{12,4},{14,6},{1,9},{3,11}... | collective-permute-start | bytes 24584 | tf_op jit(solution)/shard_map/ppermute | solution.py:295
  28.7 4.7 %collective-permute-start.8 = (bf16[2,32,128]{2,1,0:T(8,128)(2,1)S(1)}, bf16[2,32,128]{2,1,0:T(8,128)(2,1)S(1)}, u32[]{:S(2)}, u32[]{:S(2)}) collective-permute-start(bf16[2,32,128]{2,1,0:T(8,128)(2,1)S(1)} %constant_dynamic-update-slice_fusion), channel_id=1, source_target_pairs={{0,6},{2,4},{4,2},{6,0},{8,14},{10,12},{12,10},{14,8},{1,7},{3,5},... | collective-permute-start | bytes 49160 | tf_op jit(solution)/shard_map/ppermute | solution.py:295
  30.2 3.7 %collective-permute-start.7 = (bf16[2,32,128]{2,1,0:T(8,128)(2,1)S(1)}, bf16[2,32,128]{2,1,0:T(8,128)(2,1)S(1)}, u32[]{:S(2)}, u32[]{:S(2)}) collective-permute-start(bf16[2,32,128]{2,1,0:T(8,128)(2,1)S(1)} %constant_dynamic-update-slice_fusion), channel_id=1, source_target_pairs={{0,2},{2,0},{4,6},{6,4},{8,10},{10,8},{12,14},{14,12},{1,3},{3,1},... | collective-permute-start | bytes 49160 | tf_op jit(solution)/shard_map/ppermute | solution.py:295
  30.7 3.7 %collective-permute-start.6 = (bf16[2,32,128]{2,1,0:T(8,128)(2,1)S(1)}, bf16[2,32,128]{2,1,0:T(8,128)(2,1)S(1)}, u32[]{:S(2)}, u32[]{:S(2)}) collective-permute-start(bf16[2,32,128]{2,1,0:T(8,128)(2,1)S(1)} %constant_dynamic-update-slice_fusion), channel_id=1, source_target_pairs={{0,4},{2,6},{4,0},{6,2},{8,12},{10,14},{12,8},{14,10},{1,5},{3,7},... | collective-permute-start | bytes 49160 | tf_op jit(solution)/shard_map/ppermute | solution.py:295
  37.6 1.3 %collective-permute-start.9 = (f32[4,2048]{1,0:T(4,128)S(1)}, f32[4,2048]{1,0:T(4,128)S(1)}, u32[]{:S(2)}, u32[]{:S(2)}) collective-permute-start(f32[4,2048]{1,0:T(4,128)S(1)} %get-tuple-element.52), channel_id=1, source_target_pairs={{0,1},{1,0},{2,3},{3,2},{4,5},{5,4},{6,7},{7,6},{8,9},{9,8},{10,11... | collective-permute-start | bytes 98312 | tf_op jit(solution)/shard_map/ppermute | solution.py:295

commit v6 on v5

--- a/solution.py
+++ b/solution.py
@@ -12,6 +12,7 @@
 LANES = 128
 HEAD_SIZE = 128
 CHUNK = 256
+PIECES = 4
 FAN = 4
 MIB = 2**20
 
@@ -27,55 +28,108 @@
     return pltpu.with_memory_space_constraint(array, pltpu.HBM)
 
 
+def cut(start, size):
+    if size % (16 * PIECES):
+        return [(start, size)]
+    return [(start + i * (size // PIECES), size // PIECES) for i in range(PIECES)]
+
+
+def copies_in(src, dst, sems, start, size, offset):
+    return [
+        pltpu.make_async_copy(
+            src.at[pl.ds(at, rows)], dst.at[pl.ds(at - start + offset, rows)], sems.at[i]
+        )
+        for i, (at, rows) in enumerate(cut(start, size))
+    ]
+
+
 def stage_kernel(parts, *refs):
     count = len(parts)
     sems = refs[-1]
-    copies = [
-        pltpu.make_async_copy(refs[i].at[pl.ds(*part)], refs[count + i], sems.at[i])
-        for i, part in enumerate(parts)
-    ]
+    copies = []
+    for i, (start, size) in enumerate(parts):
+        copies += copies_in(refs[i], refs[count + i], sems.at[i], start, size, 0)
     for copy in copies:
         copy.start()
+    return copies
+
+
+def plain_stage_kernel(parts, *refs):
+    for copy in stage_kernel(parts, *refs):
+        copy.wait()
+
+
+def turning_stage_kernel(parts, length_ref, frequency_ref, turn_ref, *refs):
+    copies = stage_kernel(parts, *refs)
+    position = length_ref[0].astype(jnp.float32)
+    angle = position * frequency_ref[...]
+    lane = lax.broadcasted_iota(jnp.int32, angle.shape, 1)
+    sine = jnp.sin(angle)
+    turn_ref[0:1, :] = jnp.cos(angle)
+    turn_ref[1:2, :] = jnp.where(lane < HEAD_SIZE // 2, -sine, sine)
+    turn_ref[2:3, :] = jnp.full(angle.shape, position)
     for copy in copies:
         copy.wait()
 
 
-def stage(arrays, parts):
+def stage(arrays, parts, lengths=None, frequency=None):
     shapes = tuple(
         jax.ShapeDtypeStruct((part[1], *a.shape[1:]), a.dtype) for a, part in zip(arrays, parts)
     )
+    vmem = pl.BlockSpec(memory_space=pltpu.VMEM)
+    in_specs = [pl.BlockSpec(memory_space=pltpu.HBM)] * len(arrays)
+    out_specs = [vmem] * len(arrays)
+    kernel = functools.partial(plain_stage_kernel, parts)
+    pinned = [in_hbm(a) for a in arrays]
+    out_shape = shapes
+    if lengths is not None:
+        count = len(arrays)
+
+        def kernel(length_ref, frequency_ref, *refs):
+            turn_ref = refs[count]
+            turning_stage_kernel(
+                parts, length_ref, frequency_ref, turn_ref, *refs[:count], *refs[count + 1 :]
+            )
+
+        in_specs = [pl.BlockSpec(memory_space=pltpu.SMEM), vmem] + in_specs
+        out_specs = [vmem] + out_specs
+        out_shape = (jax.ShapeDtypeStruct((8, HEAD_SIZE), jnp.float32), *shapes)
+        pinned = [lengths, frequency] + pinned
     return pl.pallas_call(
-        functools.partial(stage_kernel, parts),
-        out_shape=shapes,
-        in_specs=[pl.BlockSpec(memory_space=pltpu.HBM)] * len(arrays),
-        out_specs=tuple(pl.BlockSpec(memory_space=pltpu.VMEM) for _ in arrays),
-        scratch_shapes=[pltpu.SemaphoreType.DMA((len(arrays),))],
+        kernel,
+        out_shape=out_shape,
+        in_specs=in_specs,
+        out_specs=tuple(out_specs),
+        scratch_shapes=[pltpu.SemaphoreType.DMA((len(arrays), PIECES))],
         compiler_params=pltpu.CompilerParams(vmem_limit_bytes=16 * MIB),
         cost_estimate=pl.CostEstimate(
             flops=0, bytes_accessed=sum(2 * math.prod(x.shape) for x in shapes), transcendentals=0
         ),
         name="stage",
-    )(*[in_hbm(a) for a in arrays])
+    )(*pinned)
 
 
 def spread(depth, skip, chunk):
-    return [(at, min(chunk, depth - at)) for at in range(skip, depth, chunk)]
+    ranges = [(at, min(chunk, depth - at)) for at in range(skip, depth, chunk)]
+    if ranges and ranges[-1][1] >= 2 * LANES:
+        start, size = ranges.pop()
+        ranges += [(start, size - LANES), (start + size - LANES, LANES)]
+    return ranges
 
 
 def project_kernel(
-    bits, length_ref, rows_ref, other_ref, frequency_ref, wq_hbm, first, wk, wv, *refs
+    bits, rows_ref, other_ref, wq_hbm, first, wk, wv, *refs
 ):
-    pieces, (turn_ref, wq, rows, sems) = refs[:FAN], refs[FAN:]
+    pieces, (wq, rows, sems) = refs[:FAN], refs[FAN:]
     skip = first.shape[0]
     ranges = spread(wq_hbm.shape[0], skip, CHUNK)
-    copies = []
-    for i, (start, size) in enumerate(ranges):
-        copies.append(
-            pltpu.make_async_copy(
-                wq_hbm.at[pl.ds(start, size)], wq.at[pl.ds(start - skip, size)], sems.at[i]
-            )
-        )
-        copies[-1].start()
+    copies = [
+        copies_in(wq_hbm, wq, sems.at[i], start, size, start - skip)
+        for i, (start, size) in enumerate(ranges)
+    ]
+    for group in copies:
+        for copy in group:
+            copy.start()
 
     slots = rows.shape[0]
     half = slots // 2
@@ -90,18 +144,11 @@
     squares = jnp.sum(wide * wide, axis=1, keepdims=True)
     narrow = wide.astype(jnp.bfloat16)
 
-    position = length_ref[0].astype(jnp.float32)
-    angle = position * frequency_ref[...]
-    lane = lax.broadcasted_iota(jnp.int32, angle.shape, 1)
-    sine = jnp.sin(angle)
-    turn_ref[0:1, :] = jnp.cos(angle)
-    turn_ref[1:2, :] = jnp.where(lane < HEAD_SIZE // 2, -sine, sine)
-    turn_ref[2:3, :] = jnp.full(angle.shape, position)
-
     fresh = [jnp.dot(narrow, w[...], preferred_element_type=jnp.float32) for w in (wk, wv)]
     sums = jnp.dot(narrow[:, :skip], first[...], preferred_element_type=jnp.float32)
-    for (start, size), copy in zip(ranges, copies):
-        copy.wait()
+    for (start, size), group in zip(ranges, copies):
+        for copy in group:
+            copy.wait()
         sums = sums + jnp.dot(
             narrow[:, start : start + size],
             wq[start - skip : start - skip + size, :],
@@ -121,7 +168,7 @@
             flat[pl.ds(i, size, stride=total), :] = block[at * size : (at + 1) * size]
 
 
-def project(lengths, rows, other, frequency, w_query, first, key_weight, value_weight, slots):
+def project(rows, other, w_query, first, key_weight, value_weight, slots):
     bits = slots.bit_length() - 1
     depth, query_width = w_query.shape
     kv_width = key_weight.shape[1]
@@ -133,13 +180,13 @@
     whole = pl.BlockSpec(memory_space=pltpu.VMEM)
     return pl.pallas_call(
         functools.partial(project_kernel, bits),
-        out_shape=(piece,) * FAN + (jax.ShapeDtypeStruct((8, HEAD_SIZE), jnp.float32),),
-        in_specs=[pl.BlockSpec(memory_space=pltpu.SMEM), whole, whole, whole, hbm, whole, whole, whole],
-        out_specs=(whole,) * (FAN + 1),
+        out_shape=(piece,) * FAN,
+        in_specs=[whole, whole, hbm, whole, whole, whole],
+        out_specs=(whole,) * FAN,
         scratch_shapes=[
             pltpu.VMEM((max(depth - skip, 16), query_width), jnp.bfloat16),
             pltpu.VMEM((slots, depth), jnp.float32),
-            pltpu.SemaphoreType.DMA((max(1, len(spread(depth, skip, CHUNK))),)),
+            pltpu.SemaphoreType.DMA((max(1, len(spread(depth, skip, CHUNK))), PIECES)),
         ],
         compiler_params=pltpu.CompilerParams(vmem_limit_bytes=32 * MIB),
         cost_estimate=pl.CostEstimate(
@@ -148,7 +195,7 @@
             transcendentals=0,
         ),
         name="project",
-    )(lengths, rows, other, frequency, in_hbm(w_query), first, key_weight, value_weight)
+    )(rows, other, in_hbm(w_query), first, key_weight, value_weight)
 
 
 def attend_kernel(
@@ -220,14 +267,13 @@
     w_hbm, mine_ref, theirs_ref, rest, flat, left, sums, sems = refs[pieces + staged :]
     skip = sum(ref.shape[0] for ref in ready)
     ranges = spread(w_hbm.shape[0], skip, 2 * CHUNK)
-    copies = []
-    for i, (start, size) in enumerate(ranges):
-        copies.append(
-            pltpu.make_async_copy(
-                w_hbm.at[pl.ds(start, size)], rest.at[pl.ds(start - skip, size)], sems.at[i]
-            )
-        )
-        copies[-1].start()
+    copies = [
+        copies_in(w_hbm, rest, sems.at[i], start, size, start - skip)
+        for i, (start, size) in enumerate(ranges)
+    ]
+    for group in copies:
+        for copy in group:
+            copy.start()
     slots = left.shape[0]
     heads = flat.shape[0] // slots
     at = 0
@@ -246,8 +292,9 @@
         term = jnp.dot(left[:, at : at + size], ref[...], preferred_element_type=jnp.float32)
         total = term if total is None else total + term
         at += size
-    for (start, size), copy in zip(ranges, copies):
-        copy.wait()
+    for (start, size), group in zip(ranges, copies):
+        for copy in group:
+            copy.wait()
         term = jnp.dot(
             left[:, start : start + size],
             rest[start - skip : start - skip + size, :],
@@ -281,7 +328,7 @@
             pltpu.VMEM((slots * heads, HEAD_SIZE), jnp.float32),
             pltpu.VMEM((slots, depth), jnp.bfloat16),
             pltpu.VMEM((slots, width), jnp.float32),
-            pltpu.SemaphoreType.DMA((max(1, len(spread(depth, skip, 2 * CHUNK))),)),
+            pltpu.SemaphoreType.DMA((max(1, len(spread(depth, skip, 2 * CHUNK))), PIECES)),
         ],
         compiler_params=pltpu.CompilerParams(vmem_limit_bytes=24 * MIB),
         cost_estimate=pl.CostEstimate(
@@ -311,21 +358,22 @@
     first, key_weight, value_weight = stage(
         (w_query, key_weight, value_weight), ((0, min(CHUNK, depth)), (0, depth), (0, depth))
     )
+    pieces = project(activations, other, w_query, first, key_weight, value_weight, slots)
+
+    rows_out = w_out.shape[0]
+    *pieces, w_out = lax.optimization_barrier((*pieces, w_out))
+    few, most = rows_out // 8, rows_out // 4
+    arrived = fan(pieces, devices)
     half = HEAD_SIZE // 2
     frequency = jnp.power(
         jnp.float32(500000.0), -2.0 * jnp.arange(half, dtype=jnp.float32) / HEAD_SIZE
     )
     frequency = jnp.concatenate([frequency, frequency])[None, :]
-    *pieces, turn = project(
-        lengths, activations, other, frequency, w_query, first, key_weight, value_weight, slots
-    )
-
-    rows_out = w_out.shape[0]
-    few, most = rows_out // 8, rows_out * 3 // 8
-    arrived = fan(pieces, devices)
-    k_cache, value_cache, ready_one = stage(
+    turn, k_cache, value_cache, ready_one = stage(
         (k_cache, value_cache, w_out),
         ((0, k_cache.shape[0]), (0, value_cache.shape[0]), (0, few)),
+        lengths,
+        frequency,
     )
     total = pieces[0] + (arrived[2] + (arrived[1] + arrived[0]))
     mask = FAN

time: 39.8 us -> 39.7 us (level)
  starting transfers between devices: 12.9 us -> 13.5 us
  Pallas kernels: 20.2 us -> 19.7 us
    pallas_call x4, Pallas kernels: 10 us -> 8.91 us  [stage(): pl.pallas_call(kernel, out_shape=out_shape, in_specs=in_specs, out_specs=...]
    pallas_call x1, Pallas kernels: 3.19 us -> 3.88 us  [output(): pl.pallas_call(functools.partial(output_kernel, bits, len(parts), len(rea...]
    ppermute x10, starting transfers between devices: 12.9 us -> 13.5 us  [swap(): return lax.ppermute(block, axis, [(i, i ^ mask) for i in range(devices)])]
  transfers between devices with their start and end apart: 10 -> 10, of which waited for: 6 -> 6; matrix products, arithmetic and copies ran while one was open for 0% -> 0% of each run, Pallas kernels for 25% -> 23%
where the time goes in v6:
time: 39.7 us; the launch traced here: 39.5 us
  Pallas kernels  19.7 us (50%)
  starting transfers between devices  13.5 us (34%)
  waiting for transfers between devices  4.86 us (12%)
  between operations  0.77 us (2%)
  other arithmetic  0.71 us (2%)
    ppermute x10, starting transfers between devices, swap(): return lax.ppermute(block, axis, [(i, i ^ mask) for i in range(devices)])  13.5 us
    pallas_call x4, Pallas kernels, stage(): pl.pallas_call(kernel, out_shape=out_shape, in_specs=in_specs, out_specs=...  8.91 us
    pallas_call x1, Pallas kernels, project(): pl.pallas_call(functools.partial(project_kernel, bits), out_shape=(piece,...  5.74 us
    ppermute x10, waiting for transfers between devices, swap(): return lax.ppermute(block, axis, [(i, i ^ mask) for i in range(devices)])  4.86 us
    pallas_call x1, Pallas kernels, output(): pl.pallas_call(functools.partial(output_kernel, bits, len(parts), len(rea...  3.88 us
    pallas_call x1, Pallas kernels, attend(): pl.pallas_call(functools.partial(attend_kernel, query_heads, kv_heads, le...  1.16 us
  transfers between devices with their start and end apart: 10, of which 6 were waited for; matrix products, arithmetic and copies ran while one was open for 0% of the time, Pallas kernels for 23%

profile of v6, /device:TPU:0, one launch (start us, length us, event | category | flops | bytes accessed | tf_op | source)
XLA Modules:
  0.0 39.5 jit_solution(10972874659491019327)
XLA Ops:
  0.0 0.5 %collective-permute-start = (bf16[4,2048]{1,0:T(4,128)(2,1)}, bf16[4,2048]{1,0:T(4,128)(2,1)S(1)}, u32[]{:S(2)}, u32[]{:S(2)}) collective-permute-start(bf16[4,2048]{1,0:T(4,128)(2,1)} %rows_ref.1), channel_id=1, source_target_pairs={{0,1},{1,0},{2,3},{3,2},{4,5},{5,4},{6,7},{7,6},{8,9},{9,8},{10,11... | collective-permute-start | bytes 49160 | tf_op jit(solution)/shard_map/ppermute | solution.py:342
  0.5 2.2 %stage.4 = (bf16[256,4096]{1,0:T(8,128)(2,1)S(1)}, bf16[2048,256]{1,0:T(8,128)(2,1)S(1)}, bf16[2048,256]{1,0:T(8,128)(2,1)S(1)}) custom-call(bf16[2048,4096]{1,0:T(8,128)(2,1)} %wq_hbm.1, bf16[2048,256]{1,0:T(8,128)(2,1)} %refs_1_.2, bf16[2048,256]{1,0:T(8,128)(2,1)} %refs_2_.1), custom_call_target="tpu_custom_call" | custom-call | bytes 4194304 | tf_op jit(solution)/shard_map/stage/pallas_call | solution.py:98
  2.7 5.7 %project.1 = (f32[2,40,128]{2,1,0:T(8,128)S(1)}, f32[2,40,128]{2,1,0:T(8,128)S(1)}, f32[2,40,128]{2,1,0:T(8,128)S(1)}, f32[2,40,128]{2,1,0:T(8,128)S(1)}) custom-call(bf16[4,2048]{1,0:T(4,128)(2,1)S(1)} %copy-done, bf16[4,2048]{1,0:T(4,128)(2,1)S(1)} %collective-permute-done.other_ref, bf16[2048,4096]{1,0:T(8,128)(2,1)} %wq_hbm.1, ...), custom_call_target="tpu_custom_call" | custom-call | flops 150994944 | bytes 18874368 | tf_op jit(solution)/shard_map/project/pallas_call | solution.py:181
  8.5 3.6 %collective-permute-start.1 = (f32[2,40,128]{2,1,0:T(8,128)S(1)}, f32[2,40,128]{2,1,0:T(8,128)S(1)}, u32[]{:S(2)}, u32[]{:S(2)}) collective-permute-start(f32[2,40,128]{2,1,0:T(8,128)S(1)} %get-tuple-element.44), channel_id=1, source_target_pairs={{0,6},{2,4},{4,2},{6,0},{8,14},{10,12},{12,10},{14,8},{1,7},{3,5},... | collective-permute-start | bytes 122888 | tf_op jit(solution)/shard_map/ppermute | solution.py:342
  12.1 0.5 %collective-permute-start.2 = (f32[2,40,128]{2,1,0:T(8,128)S(1)}, f32[2,40,128]{2,1,0:T(8,128)S(1)}, u32[]{:S(2)}, u32[]{:S(2)}) collective-permute-start(f32[2,40,128]{2,1,0:T(8,128)S(1)} %get-tuple-element.45), channel_id=1, source_target_pairs={{0,2},{2,0},{4,6},{6,4},{8,10},{10,8},{12,14},{14,12},{1,3},{3,1},... | collective-permute-start | bytes 122888 | tf_op jit(solution)/shard_map/ppermute | solution.py:342
  12.6 0.1 collective-permute-start.3
  12.7 0.1 maximum_bitcast_fusion.frequency_ref
  13.4 2.3 %stage.5 = (f32[8,128]{1,0:T(8,128)S(1)}, bf16[1,2,2048,128]{3,2,1,0:T(8,128)(2,1)S(1)}, bf16[1,2,2048,128]{3,2,1,0:T(8,128)(2,1)S(1)}, bf16[512,2048]{1,0:T(8,128)(2,1)S(1)}) custom-call(s32[1]{0:T(128)S(6)} %copy.10.length_ref, f32[1,128]{1,0:T(1,128)S(1)} %maximum_bitcast_fusion.frequency_ref, bf16[1,2,2048,128]{3,2,1,0:T(8,128)(2,1)} %refs_0_.3, ...), custom_call_target="tpu_custom_call" | custom-call | bytes 4194304 | tf_op jit(solution)/shard_map/stage/pallas_call | solution.py:98
  15.7 0.4 collective-permute-done.2
  16.1 0.5 %collective-permute-done.3 = f32[2,40,128]{2,1,0:T(8,128)S(1)} collective-permute-done((f32[2,40,128]{2,1,0:T(8,128)S(1)}, f32[2,40,128]{2,1,0:T(8,128)S(1)}, u32[]{:S(2)}, u32[]{:S(2)}) %collective-permute-start.3) | collective-permute-done | bytes 40992 | tf_op jit(solution)/shard_map/ppermute | solution.py:342
  16.6 2.7 %collective-permute-start.4 = (f32[1,40,128]{2,1,0:T(8,128)S(1)}, f32[1,40,128]{2,1,0:T(8,128)S(1)}, u32[]{:S(2)}, u32[]{:S(2)}) collective-permute-start(f32[1,40,128]{2,1,0:T(8,128)S(1)} %get-tuple-element.63), channel_id=1, source_target_pairs={{0,8},{2,10},{4,12},{6,14},{8,0},{10,2},{12,4},{14,6},{1,9},{3,11}... | collective-permute-start | bytes 61448 | tf_op jit(solution)/shard_map/ppermute | solution.py:342
  19.3 2.2 %stage.6.refs_6_ = bf16[1024,2048]{1,0:T(8,128)(2,1)S(1)} custom-call(bf16[4096,2048]{1,0:T(8,128)(2,1)} %refs_8_), custom_call_target="tpu_custom_call" | custom-call | bytes 4194304 | tf_op jit(solution)/shard_map/stage/pallas_call | solution.py:98
  21.5 1.2 %attend.1.refs_0_ = bf16[1,32,128]{2,1,0:T(8,128)(2,1)S(1)} custom-call(f32[8,128]{1,0:T(8,128)S(1)} %get-tuple-element.42.turn_ref, bf16[1,2,2048,128]{3,2,1,0:T(8,128)(2,1)S(1)} %get-tuple-element.50.k_ref, bf16[1,2,2048,128]{3,2,1,0:T(8,128)(2,1)S(1)} %get-tuple-element.51.v_ref, f32[1,40,128]{2,1,0:T(8,128)S(1)} %get-tuple-element.64.refs_0_, ...), custom_call_target="tpu_custom_call" | custom-call | flops 33554432 | bytes 2097152 | tf_op jit(solution)/shard_map/attend/pallas_call | solution.py:249
  22.7 2.5 %collective-permute-start.5 = (bf16[1,32,128]{2,1,0:T(8,128)(2,1)S(1)}, bf16[1,32,128]{2,1,0:T(8,128)(2,1)S(1)}, u32[]{:S(2)}, u32[]{:S(2)}) collective-permute-start(bf16[1,32,128]{2,1,0:T(8,128)(2,1)S(1)} %attend.1.refs_0_), channel_id=1, source_target_pairs={{0,8},{2,10},{4,12},{6,14},{8,0},{10,2},{12,4},{14,6},{1,9},{3,11}... | collective-permute-start | bytes 24584 | tf_op jit(solution)/shard_map/ppermute | solution.py:342
  25.2 2.2 %stage.7.refs_7_ = bf16[1024,2048]{1,0:T(8,128)(2,1)S(1)} custom-call(bf16[4096,2048]{1,0:T(8,128)(2,1)} %refs_8_), custom_call_target="tpu_custom_call" | custom-call | bytes 4194304 | tf_op jit(solution)/shard_map/stage/pallas_call | solution.py:98
  27.4 2.0 %collective-permute-start.8 = (bf16[2,32,128]{2,1,0:T(8,128)(2,1)S(1)}, bf16[2,32,128]{2,1,0:T(8,128)(2,1)S(1)}, u32[]{:S(2)}, u32[]{:S(2)}) collective-permute-start(bf16[2,32,128]{2,1,0:T(8,128)(2,1)S(1)} %constant_dynamic-update-slice_fusion), channel_id=1, source_target_pairs={{0,6},{2,4},{4,2},{6,0},{8,14},{10,12},{12,10},{14,8},{1,7},{3,5},... | collective-permute-start | bytes 49160 | tf_op jit(solution)/shard_map/ppermute | solution.py:342
  29.5 0.5 %collective-permute-start.7 = (bf16[2,32,128]{2,1,0:T(8,128)(2,1)S(1)}, bf16[2,32,128]{2,1,0:T(8,128)(2,1)S(1)}, u32[]{:S(2)}, u32[]{:S(2)}) collective-permute-start(bf16[2,32,128]{2,1,0:T(8,128)(2,1)S(1)} %constant_dynamic-update-slice_fusion), channel_id=1, source_target_pairs={{0,2},{2,0},{4,6},{6,4},{8,10},{10,8},{12,14},{14,12},{1,3},{3,1},... | collective-permute-start | bytes 49160 | tf_op jit(solution)/shard_map/ppermute | solution.py:342
  30.0 1.0 %collective-permute-start.6 = (bf16[2,32,128]{2,1,0:T(8,128)(2,1)S(1)}, bf16[2,32,128]{2,1,0:T(8,128)(2,1)S(1)}, u32[]{:S(2)}, u32[]{:S(2)}) collective-permute-start(bf16[2,32,128]{2,1,0:T(8,128)(2,1)S(1)} %constant_dynamic-update-slice_fusion), channel_id=1, source_target_pairs={{0,4},{2,6},{4,0},{6,2},{8,12},{10,14},{12,8},{14,10},{1,5},{3,7},... | collective-permute-start | bytes 49160 | tf_op jit(solution)/shard_map/ppermute | solution.py:342
  31.0 1.1 %collective-permute-done.8.refs_4_ = bf16[2,32,128]{2,1,0:T(8,128)(2,1)S(1)} collective-permute-done((bf16[2,32,128]{2,1,0:T(8,128)(2,1)S(1)}, bf16[2,32,128]{2,1,0:T(8,128)(2,1)S(1)}, u32[]{:S(2)}, u32[]{:S(2)}) %collective-permute-start.8) | collective-permute-done | bytes 16416 | tf_op jit(solution)/shard_map/ppermute | solution.py:342
  32.1 1.1 %collective-permute-done.7.refs_3_ = bf16[2,32,128]{2,1,0:T(8,128)(2,1)S(1)} collective-permute-done((bf16[2,32,128]{2,1,0:T(8,128)(2,1)S(1)}, bf16[2,32,128]{2,1,0:T(8,128)(2,1)S(1)}, u32[]{:S(2)}, u32[]{:S(2)}) %collective-permute-start.7) | collective-permute-done | bytes 16416 | tf_op jit(solution)/shard_map/ppermute | solution.py:342
  33.2 0.5 %collective-permute-done.6.refs_2_ = bf16[2,32,128]{2,1,0:T(8,128)(2,1)S(1)} collective-permute-done((bf16[2,32,128]{2,1,0:T(8,128)(2,1)S(1)}, bf16[2,32,128]{2,1,0:T(8,128)(2,1)S(1)}, u32[]{:S(2)}, u32[]{:S(2)}) %collective-permute-start.6) | collective-permute-done | bytes 16416 | tf_op jit(solution)/shard_map/ppermute | solution.py:342
  33.7 3.9 %output.1 = (f32[4,2048]{1,0:T(4,128)S(1)}, f32[4,2048]{1,0:T(4,128)S(1)}) custom-call(bf16[1,32,128]{2,1,0:T(8,128)(2,1)S(1)} %attend.1.refs_0_, bf16[1,32,128]{2,1,0:T(8,128)(2,1)S(1)} %collective-permute-done.5.refs_1_, bf16[2,32,128]{2,1,0:T(8,128)(2,1)S(1)} %collective-permute-done.6.refs_2_, bf16[2,32,128]{2,1,0:T(8,128)(2,1)S(1)} %collective-permute-done.7.refs_3_, ...), custom_call_target="tpu_custom_call" | custom-call | flops 134217728 | bytes 16777216 | tf_op jit(solution)/shard_map/output/pallas_call | solution.py:321
  37.7 1.2 %collective-permute-done.9 = f32[4,2048]{1,0:T(4,128)S(1)} collective-permute-done((f32[4,2048]{1,0:T(4,128)S(1)}, f32[4,2048]{1,0:T(4,128)S(1)}, u32[]{:S(2)}, u32[]{:S(2)}) %collective-permute-start.9) | collective-permute-done | bytes 32800 | tf_op jit(solution)/shard_map/ppermute | solution.py:342
  38.9 0.6 %add_convert_fusion = bf16[4,2048]{1,0:T(4,128)(2,1)} fusion(f32[4,2048]{1,0:T(4,128)S(1)} %get-tuple-element.61, f32[4,2048]{1,0:T(4,128)S(1)} %collective-permute-done.9), kind=kLoop, calls=%fused_computation.1 | loop fusion | flops 16384 | bytes 81920 | tf_op jit(solution)/shard_map/convert_element_type | solution.py:402
  (12 shorter events, 0.1 us)
Async XLA Ops:
  0.0 2.7 %collective-permute-start = (bf16[4,2048]{1,0:T(4,128)(2,1)}, bf16[4,2048]{1,0:T(4,128)(2,1)S(1)}, u32[]{:S(2)}, u32[]{:S(2)}) collective-permute-start(bf16[4,2048]{1,0:T(4,128)(2,1)} %rows_ref.1), channel_id=1, source_target_pairs={{0,1},{1,0},{2,3},{3,2},{4,5},{5,4},{6,7},{7,6},{8,9},{9,8},{10,11... | collective-permute-start | bytes 49160 | tf_op jit(solution)/shard_map/ppermute | solution.py:342
  0.5 2.3 %copy-start = (bf16[4,2048]{1,0:T(4,128)(2,1)S(1)}, bf16[4,2048]{1,0:T(4,128)(2,1)}, u32[]{:S(2)}) copy-start(bf16[4,2048]{1,0:T(4,128)(2,1)} %rows_ref.1) | copy-start | bytes 49156
  8.5 7.2 %collective-permute-start.1 = (f32[2,40,128]{2,1,0:T(8,128)S(1)}, f32[2,40,128]{2,1,0:T(8,128)S(1)}, u32[]{:S(2)}, u32[]{:S(2)}) collective-permute-start(f32[2,40,128]{2,1,0:T(8,128)S(1)} %get-tuple-element.44), channel_id=1, source_target_pairs={{0,6},{2,4},{4,2},{6,0},{8,14},{10,12},{12,10},{14,8},{1,7},{3,5},... | collective-permute-start | bytes 122888 | tf_op jit(solution)/shard_map/ppermute | solution.py:342
  12.1 4.0 %collective-permute-start.2 = (f32[2,40,128]{2,1,0:T(8,128)S(1)}, f32[2,40,128]{2,1,0:T(8,128)S(1)}, u32[]{:S(2)}, u32[]{:S(2)}) collective-permute-start(f32[2,40,128]{2,1,0:T(8,128)S(1)} %get-tuple-element.45), channel_id=1, source_target_pairs={{0,2},{2,0},{4,6},{6,4},{8,10},{10,8},{12,14},{14,12},{1,3},{3,1},... | collective-permute-start | bytes 122888 | tf_op jit(solution)/shard_map/ppermute | solution.py:342
  12.6 4.0 %collective-permute-start.3 = (f32[2,40,128]{2,1,0:T(8,128)S(1)}, f32[2,40,128]{2,1,0:T(8,128)S(1)}, u32[]{:S(2)}, u32[]{:S(2)}) collective-permute-start(f32[2,40,128]{2,1,0:T(8,128)S(1)} %get-tuple-element.46), channel_id=1, source_target_pairs={{0,4},{2,6},{4,0},{6,2},{8,12},{10,14},{12,8},{14,10},{1,5},{3,7},... | collective-permute-start | bytes 122888 | tf_op jit(solution)/shard_map/ppermute | solution.py:342
  16.6 4.9 %collective-permute-start.4 = (f32[1,40,128]{2,1,0:T(8,128)S(1)}, f32[1,40,128]{2,1,0:T(8,128)S(1)}, u32[]{:S(2)}, u32[]{:S(2)}) collective-permute-start(f32[1,40,128]{2,1,0:T(8,128)S(1)} %get-tuple-element.63), channel_id=1, source_target_pairs={{0,8},{2,10},{4,12},{6,14},{8,0},{10,2},{12,4},{14,6},{1,9},{3,11}... | collective-permute-start | bytes 61448 | tf_op jit(solution)/shard_map/ppermute | solution.py:342
  22.7 4.7 %collective-permute-start.5 = (bf16[1,32,128]{2,1,0:T(8,128)(2,1)S(1)}, bf16[1,32,128]{2,1,0:T(8,128)(2,1)S(1)}, u32[]{:S(2)}, u32[]{:S(2)}) collective-permute-start(bf16[1,32,128]{2,1,0:T(8,128)(2,1)S(1)} %attend.1.refs_0_), channel_id=1, source_target_pairs={{0,8},{2,10},{4,12},{6,14},{8,0},{10,2},{12,4},{14,6},{1,9},{3,11}... | collective-permute-start | bytes 24584 | tf_op jit(solution)/shard_map/ppermute | solution.py:342
  27.4 4.7 %collective-permute-start.8 = (bf16[2,32,128]{2,1,0:T(8,128)(2,1)S(1)}, bf16[2,32,128]{2,1,0:T(8,128)(2,1)S(1)}, u32[]{:S(2)}, u32[]{:S(2)}) collective-permute-start(bf16[2,32,128]{2,1,0:T(8,128)(2,1)S(1)} %constant_dynamic-update-slice_fusion), channel_id=1, source_target_pairs={{0,6},{2,4},{4,2},{6,0},{8,14},{10,12},{12,10},{14,8},{1,7},{3,5},... | collective-permute-start | bytes 49160 | tf_op jit(solution)/shard_map/ppermute | solution.py:342
  29.5 3.7 %collective-permute-start.7 = (bf16[2,32,128]{2,1,0:T(8,128)(2,1)S(1)}, bf16[2,32,128]{2,1,0:T(8,128)(2,1)S(1)}, u32[]{:S(2)}, u32[]{:S(2)}) collective-permute-start(bf16[2,32,128]{2,1,0:T(8,128)(2,1)S(1)} %constant_dynamic-update-slice_fusion), channel_id=1, source_target_pairs={{0,2},{2,0},{4,6},{6,4},{8,10},{10,8},{12,14},{14,12},{1,3},{3,1},... | collective-permute-start | bytes 49160 | tf_op jit(solution)/shard_map/ppermute | solution.py:342
  30.0 3.7 %collective-permute-start.6 = (bf16[2,32,128]{2,1,0:T(8,128)(2,1)S(1)}, bf16[2,32,128]{2,1,0:T(8,128)(2,1)S(1)}, u32[]{:S(2)}, u32[]{:S(2)}) collective-permute-start(bf16[2,32,128]{2,1,0:T(8,128)(2,1)S(1)} %constant_dynamic-update-slice_fusion), channel_id=1, source_target_pairs={{0,4},{2,6},{4,0},{6,2},{8,12},{10,14},{12,8},{14,10},{1,5},{3,7},... | collective-permute-start | bytes 49160 | tf_op jit(solution)/shard_map/ppermute | solution.py:342
  37.6 1.3 %collective-permute-start.9 = (f32[4,2048]{1,0:T(4,128)S(1)}, f32[4,2048]{1,0:T(4,128)S(1)}, u32[]{:S(2)}, u32[]{:S(2)}) collective-permute-start(f32[4,2048]{1,0:T(4,128)S(1)} %get-tuple-element.62), channel_id=1, source_target_pairs={{0,1},{1,0},{2,3},{3,2},{4,5},{5,4},{6,7},{7,6},{8,9},{9,8},{10,11... | collective-permute-start | bytes 98312 | tf_op jit(solution)/shard_map/ppermute | solution.py:342

commit v7 on v6

--- a/solution.py
+++ b/solution.py
@@ -12,6 +12,7 @@
 LANES = 128
 HEAD_SIZE = 128
 CHUNK = 256
+FIRST = 256
 PIECES = 4
 FAN = 4
 MIB = 2**20
@@ -355,9 +356,7 @@
     query_heads = w_query.shape[1] // HEAD_SIZE
     other = swap(activations, "gy", 2, 1)
     depth = w_query.shape[0]
-    first, key_weight, value_weight = stage(
-        (w_query, key_weight, value_weight), ((0, min(CHUNK, depth)), (0, depth), (0, depth))
-    )
+    (first,) = stage((w_query,), ((0, min(FIRST, depth)),))
     pieces = project(activations, other, w_query, first, key_weight, value_weight, slots)
 
     rows_out = w_out.shape[0]
@@ -369,21 +368,14 @@
         jnp.float32(500000.0), -2.0 * jnp.arange(half, dtype=jnp.float32) / HEAD_SIZE
     )
     frequency = jnp.concatenate([frequency, frequency])[None, :]
-    turn, k_cache, value_cache, ready_one = stage(
-        (k_cache, value_cache, w_out),
-        ((0, k_cache.shape[0]), (0, value_cache.shape[0]), (0, few)),
-        lengths,
-        frequency,
-    )
+    turn, ready_one = stage((w_out,), ((0, few),), lengths, frequency)
     total = pieces[0] + (arrived[2] + (arrived[1] + arrived[0]))
     mask = FAN
     while total.shape[0] > 2:
         rest = total.shape[0] // 2
         total = total[:rest] + swap(total[rest:], "gx", devices, mask)
         mask *= 2
-    total, w_out, k_cache, value_cache, ready_one = lax.optimization_barrier(
-        (total, w_out, k_cache, value_cache, ready_one)
-    )
+    total, w_out, ready_one = lax.optimization_barrier((total, w_out, ready_one))
     (ready_two,) = stage((w_out,), ((few, most),))
     parts = [total[:1], swap(total[1:], "gx", devices, mask)]
     parts[1], ready_two = lax.optimization_barrier((parts[1], ready_two))
@@ -397,8 +389,12 @@
         mask //= 2
         parts.append(swap(jnp.concatenate(parts, axis=0), "gx", devices, mask))
     held = jnp.concatenate(parts, axis=0)
+    held, w_out = lax.optimization_barrier((held, w_out))
+    (ready_four,) = stage((w_out,), ((few + 2 * most, most),))
     parts += fan([held] * FAN, devices)
-    mine, theirs = output(parts, (ready_one, ready_two, ready_three), w_out, slots)
+    parts[-1], ready_four = lax.optimization_barrier((parts[-1], ready_four))
+    ready = (ready_one, ready_two, ready_three, ready_four)
+    mine, theirs = output(parts, ready, w_out, slots)
     return (mine + swap(theirs, "gy", 2, 1)).astype(jnp.bfloat16)
 
 

time: 39.7 us -> 38.2 us (0.962)
  waiting for transfers between devices: 4.86 us -> 2.81 us
  local copies, waits for them, and re-layouts: 0.02 us -> 0.46 us
    ppermute x10, waiting for transfers between devices: 4.86 us -> 2.81 us  [swap(): return lax.ppermute(block, axis, [(i, i ^ mask) for i in range(devices)])]
    pallas_call x4 -> x5, Pallas kernels: 8.91 us -> 9.86 us  [stage(): pl.pallas_call(kernel, out_shape=out_shape, in_specs=in_specs, out_specs=...]
    pallas_call x1, Pallas kernels: 3.88 us -> 2.96 us  [output(): pl.pallas_call(functools.partial(output_kernel, bits, len(parts), len(rea...]
    unnamed x3 -> x10, local copies, waits for them, and re-layouts: 0.01 us -> 0.46 us
  transfers between devices with their start and end apart: 10 -> 10, of which waited for: 6 -> 3; matrix products, arithmetic and copies ran while one was open for 0% -> 0% of each run, Pallas kernels for 23% -> 26%
where the time goes in v7:
time: 38.2 us; the launch traced here: 38 us
  Pallas kernels  19.7 us (52%)
  starting transfers between devices  13.4 us (35%)
  waiting for transfers between devices  2.81 us (7%)
  between operations  0.84 us (2%)
  other arithmetic  0.72 us (2%)
  local copies, waits for them, and re-layouts  0.46 us (1%)
    ppermute x10, starting transfers between devices, swap(): return lax.ppermute(block, axis, [(i, i ^ mask) for i in range(devices)])  13.4 us
    pallas_call x5, Pallas kernels, stage(): pl.pallas_call(kernel, out_shape=out_shape, in_specs=in_specs, out_specs=...  9.86 us
    pallas_call x1, Pallas kernels, project(): pl.pallas_call(functools.partial(project_kernel, bits), out_shape=(piece,...  5.73 us
    pallas_call x1, Pallas kernels, output(): pl.pallas_call(functools.partial(output_kernel, bits, len(parts), len(rea...  2.96 us
    ppermute x10, waiting for transfers between devices, swap(): return lax.ppermute(block, axis, [(i, i ^ mask) for i in range(devices)])  2.81 us
    pallas_call x1, Pallas kernels, attend(): pl.pallas_call(functools.partial(attend_kernel, query_heads, kv_heads, le...  1.16 us
  transfers between devices with their start and end apart: 10, of which 3 were waited for; matrix products, arithmetic and copies ran while one was open for 0% of the time, Pallas kernels for 26%

profile of v7, /device:TPU:0, one launch (start us, length us, event | category | flops | bytes accessed | tf_op | source)
XLA Modules:
  0.0 38.0 jit_solution(13594364136738072701)
XLA Ops:
  0.0 0.5 %collective-permute-start = (bf16[4,2048]{1,0:T(4,128)(2,1)}, bf16[4,2048]{1,0:T(4,128)(2,1)S(1)}, u32[]{:S(2)}, u32[]{:S(2)}) collective-permute-start(bf16[4,2048]{1,0:T(4,128)(2,1)} %rows_ref.1), channel_id=1, source_target_pairs={{0,1},{1,0},{2,3},{3,2},{4,5},{5,4},{6,7},{7,6},{8,9},{9,8},{10,11... | collective-permute-start | bytes 49160 | tf_op jit(solution)/shard_map/ppermute | solution.py:343
  0.5 1.7 %stage.5.first = bf16[256,4096]{1,0:T(8,128)(2,1)S(1)} custom-call(bf16[2048,4096]{1,0:T(8,128)(2,1)} %wq_hbm.1), custom_call_target="tpu_custom_call" | custom-call | bytes 2097152 | tf_op jit(solution)/shard_map/stage/pallas_call | solution.py:99
  2.2 0.1 copy-done
  2.3 0.3 copy-done.1
  2.6 5.7 %project.1 = (f32[2,40,128]{2,1,0:T(8,128)S(1)}, f32[2,40,128]{2,1,0:T(8,128)S(1)}, f32[2,40,128]{2,1,0:T(8,128)S(1)}, f32[2,40,128]{2,1,0:T(8,128)S(1)}) custom-call(bf16[4,2048]{1,0:T(4,128)(2,1)S(1)} %copy-done.4, bf16[4,2048]{1,0:T(4,128)(2,1)S(1)} %collective-permute-done.other_ref, bf16[2048,4096]{1,0:T(8,128)(2,1)} %wq_hbm.1, ...), custom_call_target="tpu_custom_call" | custom-call | flops 150994944 | bytes 18874368 | tf_op jit(solution)/shard_map/project/pallas_call | solution.py:182
  8.4 3.6 %collective-permute-start.1 = (f32[2,40,128]{2,1,0:T(8,128)S(1)}, f32[2,40,128]{2,1,0:T(8,128)S(1)}, u32[]{:S(2)}, u32[]{:S(2)}) collective-permute-start(f32[2,40,128]{2,1,0:T(8,128)S(1)} %get-tuple-element.38), channel_id=1, source_target_pairs={{0,6},{2,4},{4,2},{6,0},{8,14},{10,12},{12,10},{14,8},{1,7},{3,5},... | collective-permute-start | bytes 122888 | tf_op jit(solution)/shard_map/ppermute | solution.py:343
  12.0 0.5 %collective-permute-start.2 = (f32[2,40,128]{2,1,0:T(8,128)S(1)}, f32[2,40,128]{2,1,0:T(8,128)S(1)}, u32[]{:S(2)}, u32[]{:S(2)}) collective-permute-start(f32[2,40,128]{2,1,0:T(8,128)S(1)} %get-tuple-element.39), channel_id=1, source_target_pairs={{0,2},{2,0},{4,6},{6,4},{8,10},{10,8},{12,14},{14,12},{1,3},{3,1},... | collective-permute-start | bytes 122888 | tf_op jit(solution)/shard_map/ppermute | solution.py:343
  12.5 0.1 collective-permute-start.3
  12.6 0.1 maximum_bitcast_fusion.frequency_ref
  13.3 1.6 %stage.6 = (f32[8,128]{1,0:T(8,128)S(1)}, bf16[512,2048]{1,0:T(8,128)(2,1)S(1)}) custom-call(s32[1]{0:T(128)S(6)} %copy.9.length_ref, f32[1,128]{1,0:T(1,128)S(1)} %maximum_bitcast_fusion.frequency_ref, bf16[4096,2048]{1,0:T(8,128)(2,1)} %refs_9_), custom_call_target="tpu_custom_call" | custom-call | bytes 2097152 | tf_op jit(solution)/shard_map/stage/pallas_call | solution.py:99
  14.9 1.1 %collective-permute-done.2 = f32[2,40,128]{2,1,0:T(8,128)S(1)} collective-permute-done((f32[2,40,128]{2,1,0:T(8,128)S(1)}, f32[2,40,128]{2,1,0:T(8,128)S(1)}, u32[]{:S(2)}, u32[]{:S(2)}) %collective-permute-start.2) | collective-permute-done | bytes 40992 | tf_op jit(solution)/shard_map/ppermute | solution.py:343
  16.0 0.5 %collective-permute-done.3 = f32[2,40,128]{2,1,0:T(8,128)S(1)} collective-permute-done((f32[2,40,128]{2,1,0:T(8,128)S(1)}, f32[2,40,128]{2,1,0:T(8,128)S(1)}, u32[]{:S(2)}, u32[]{:S(2)}) %collective-permute-start.3) | collective-permute-done | bytes 40992 | tf_op jit(solution)/shard_map/ppermute | solution.py:343
  16.5 2.7 %collective-permute-start.4 = (f32[1,40,128]{2,1,0:T(8,128)S(1)}, f32[1,40,128]{2,1,0:T(8,128)S(1)}, u32[]{:S(2)}, u32[]{:S(2)}) collective-permute-start(f32[1,40,128]{2,1,0:T(8,128)S(1)} %get-tuple-element.57), channel_id=1, source_target_pairs={{0,8},{2,10},{4,12},{6,14},{8,0},{10,2},{12,4},{14,6},{1,9},{3,11}... | collective-permute-start | bytes 61448 | tf_op jit(solution)/shard_map/ppermute | solution.py:343
  19.2 2.2 %stage.7.refs_6_ = bf16[1024,2048]{1,0:T(8,128)(2,1)S(1)} custom-call(bf16[4096,2048]{1,0:T(8,128)(2,1)} %refs_9_), custom_call_target="tpu_custom_call" | custom-call | bytes 4194304 | tf_op jit(solution)/shard_map/stage/pallas_call | solution.py:99
  21.4 1.2 %attend.1.refs_0_ = bf16[1,32,128]{2,1,0:T(8,128)(2,1)S(1)} custom-call(f32[8,128]{1,0:T(8,128)S(1)} %get-tuple-element.36.turn_ref, bf16[1,2,2048,128]{3,2,1,0:T(8,128)(2,1)S(1)} %copy-done.2, bf16[1,2,2048,128]{3,2,1,0:T(8,128)(2,1)S(1)} %copy-done.3, f32[1,40,128]{2,1,0:T(8,128)S(1)} %get-tuple-element.58.refs_0_, ...), custom_call_target="tpu_custom_call" | custom-call | flops 33554432 | bytes 2097152 | tf_op jit(solution)/shard_map/attend/pallas_call | solution.py:250
  22.6 2.5 %collective-permute-start.5 = (bf16[1,32,128]{2,1,0:T(8,128)(2,1)S(1)}, bf16[1,32,128]{2,1,0:T(8,128)(2,1)S(1)}, u32[]{:S(2)}, u32[]{:S(2)}) collective-permute-start(bf16[1,32,128]{2,1,0:T(8,128)(2,1)S(1)} %attend.1.refs_0_), channel_id=1, source_target_pairs={{0,8},{2,10},{4,12},{6,14},{8,0},{10,2},{12,4},{14,6},{1,9},{3,11}... | collective-permute-start | bytes 24584 | tf_op jit(solution)/shard_map/ppermute | solution.py:343
  25.1 2.2 %stage.8.refs_7_ = bf16[1024,2048]{1,0:T(8,128)(2,1)S(1)} custom-call(bf16[4096,2048]{1,0:T(8,128)(2,1)} %refs_9_), custom_call_target="tpu_custom_call" | custom-call | bytes 4194304 | tf_op jit(solution)/shard_map/stage/pallas_call | solution.py:99
  27.3 1.4 %collective-permute-start.8 = (bf16[2,32,128]{2,1,0:T(8,128)(2,1)S(1)}, bf16[2,32,128]{2,1,0:T(8,128)(2,1)S(1)}, u32[]{:S(2)}, u32[]{:S(2)}) collective-permute-start(bf16[2,32,128]{2,1,0:T(8,128)(2,1)S(1)} %pad_maximum_fusion), channel_id=1, source_target_pairs={{0,6},{2,4},{4,2},{6,0},{8,14},{10,12},{12,10},{14,8},{1,7},{3,5},... | collective-permute-start | bytes 49160 | tf_op jit(solution)/shard_map/ppermute | solution.py:343
  28.8 0.5 %collective-permute-start.7 = (bf16[2,32,128]{2,1,0:T(8,128)(2,1)S(1)}, bf16[2,32,128]{2,1,0:T(8,128)(2,1)S(1)}, u32[]{:S(2)}, u32[]{:S(2)}) collective-permute-start(bf16[2,32,128]{2,1,0:T(8,128)(2,1)S(1)} %pad_maximum_fusion), channel_id=1, source_target_pairs={{0,2},{2,0},{4,6},{6,4},{8,10},{10,8},{12,14},{14,12},{1,3},{3,1},... | collective-permute-start | bytes 49160 | tf_op jit(solution)/shard_map/ppermute | solution.py:343
  29.3 1.6 %collective-permute-start.6 = (bf16[2,32,128]{2,1,0:T(8,128)(2,1)S(1)}, bf16[2,32,128]{2,1,0:T(8,128)(2,1)S(1)}, u32[]{:S(2)}, u32[]{:S(2)}) collective-permute-start(bf16[2,32,128]{2,1,0:T(8,128)(2,1)S(1)} %pad_maximum_fusion), channel_id=1, source_target_pairs={{0,4},{2,6},{4,0},{6,2},{8,12},{10,14},{12,8},{14,10},{1,5},{3,7},... | collective-permute-start | bytes 49160 | tf_op jit(solution)/shard_map/ppermute | solution.py:343
  30.9 2.2 %stage.9.refs_8_ = bf16[1024,2048]{1,0:T(8,128)(2,1)S(1)} custom-call(bf16[4096,2048]{1,0:T(8,128)(2,1)} %refs_9_), custom_call_target="tpu_custom_call" | custom-call | bytes 4194304 | tf_op jit(solution)/shard_map/stage/pallas_call | solution.py:99
  33.1 3.0 %output.1 = (f32[4,2048]{1,0:T(4,128)S(1)}, f32[4,2048]{1,0:T(4,128)S(1)}) custom-call(bf16[1,32,128]{2,1,0:T(8,128)(2,1)S(1)} %attend.1.refs_0_, bf16[1,32,128]{2,1,0:T(8,128)(2,1)S(1)} %collective-permute-done.5.refs_1_, bf16[2,32,128]{2,1,0:T(8,128)(2,1)S(1)} %collective-permute-done.6.refs_2_, bf16[2,32,128]{2,1,0:T(8,128)(2,1)S(1)} %collective-permute-done.7.refs_3_, ...), custom_call_target="tpu_custom_call" | custom-call | flops 134217728 | bytes 16777216 | tf_op jit(solution)/shard_map/output/pallas_call | solution.py:322
  36.2 1.2 %collective-permute-done.9 = f32[4,2048]{1,0:T(4,128)S(1)} collective-permute-done((f32[4,2048]{1,0:T(4,128)S(1)}, f32[4,2048]{1,0:T(4,128)S(1)}, u32[]{:S(2)}, u32[]{:S(2)}) %collective-permute-start.9) | collective-permute-done | bytes 32800 | tf_op jit(solution)/shard_map/ppermute | solution.py:343
  37.4 0.6 %add_convert_fusion = bf16[4,2048]{1,0:T(4,128)(2,1)} fusion(f32[4,2048]{1,0:T(4,128)S(1)} %get-tuple-element.55, f32[4,2048]{1,0:T(4,128)S(1)} %collective-permute-done.9), kind=kLoop, calls=%fused_computation.1 | loop fusion | flops 16384 | bytes 81920 | tf_op jit(solution)/shard_map/convert_element_type | solution.py:398
  (20 shorter events, 0.1 us)
Async XLA Ops:
  0.0 2.2 %collective-permute-start = (bf16[4,2048]{1,0:T(4,128)(2,1)}, bf16[4,2048]{1,0:T(4,128)(2,1)S(1)}, u32[]{:S(2)}, u32[]{:S(2)}) collective-permute-start(bf16[4,2048]{1,0:T(4,128)(2,1)} %rows_ref.1), channel_id=1, source_target_pairs={{0,1},{1,0},{2,3},{3,2},{4,5},{5,4},{6,7},{7,6},{8,9},{9,8},{10,11... | collective-permute-start | bytes 49160 | tf_op jit(solution)/shard_map/ppermute | solution.py:343
  0.5 1.9 %copy-start = (bf16[2048,256]{1,0:T(8,128)(2,1)S(1)}, bf16[2048,256]{1,0:T(8,128)(2,1)}, u32[]{:S(2)}) copy-start(bf16[2048,256]{1,0:T(8,128)(2,1)} %wk.1) | copy-start | bytes 3145732
  0.5 2.2 %copy-start.1 = (bf16[2048,256]{1,0:T(8,128)(2,1)S(1)}, bf16[2048,256]{1,0:T(8,128)(2,1)}, u32[]{:S(2)}) copy-start(bf16[2048,256]{1,0:T(8,128)(2,1)} %wv.1) | copy-start | bytes 3145732
  0.5 2.2 %copy-start.4 = (bf16[4,2048]{1,0:T(4,128)(2,1)S(1)}, bf16[4,2048]{1,0:T(4,128)(2,1)}, u32[]{:S(2)}) copy-start(bf16[4,2048]{1,0:T(4,128)(2,1)} %rows_ref.1) | copy-start | bytes 49156
  8.4 6.5 %collective-permute-start.1 = (f32[2,40,128]{2,1,0:T(8,128)S(1)}, f32[2,40,128]{2,1,0:T(8,128)S(1)}, u32[]{:S(2)}, u32[]{:S(2)}) collective-permute-start(f32[2,40,128]{2,1,0:T(8,128)S(1)} %get-tuple-element.38), channel_id=1, source_target_pairs={{0,6},{2,4},{4,2},{6,0},{8,14},{10,12},{12,10},{14,8},{1,7},{3,5},... | collective-permute-start | bytes 122888 | tf_op jit(solution)/shard_map/ppermute | solution.py:343
  12.0 4.0 %collective-permute-start.2 = (f32[2,40,128]{2,1,0:T(8,128)S(1)}, f32[2,40,128]{2,1,0:T(8,128)S(1)}, u32[]{:S(2)}, u32[]{:S(2)}) collective-permute-start(f32[2,40,128]{2,1,0:T(8,128)S(1)} %get-tuple-element.39), channel_id=1, source_target_pairs={{0,2},{2,0},{4,6},{6,4},{8,10},{10,8},{12,14},{14,12},{1,3},{3,1},... | collective-permute-start | bytes 122888 | tf_op jit(solution)/shard_map/ppermute | solution.py:343
  12.5 4.0 %collective-permute-start.3 = (f32[2,40,128]{2,1,0:T(8,128)S(1)}, f32[2,40,128]{2,1,0:T(8,128)S(1)}, u32[]{:S(2)}, u32[]{:S(2)}) collective-permute-start(f32[2,40,128]{2,1,0:T(8,128)S(1)} %get-tuple-element.40), channel_id=1, source_target_pairs={{0,4},{2,6},{4,0},{6,2},{8,12},{10,14},{12,8},{14,10},{1,5},{3,7},... | collective-permute-start | bytes 122888 | tf_op jit(solution)/shard_map/ppermute | solution.py:343
  16.5 4.9 %copy-start.2 = (bf16[1,2,2048,128]{3,2,1,0:T(8,128)(2,1)S(1)}, bf16[1,2,2048,128]{3,2,1,0:T(8,128)(2,1)}, u32[]{:S(2)}) copy-start(bf16[1,2,2048,128]{3,2,1,0:T(8,128)(2,1)} %k_ref.1) | copy-start | bytes 3145732
  16.5 4.9 %copy-start.3 = (bf16[1,2,2048,128]{3,2,1,0:T(8,128)(2,1)S(1)}, bf16[1,2,2048,128]{3,2,1,0:T(8,128)(2,1)}, u32[]{:S(2)}) copy-start(bf16[1,2,2048,128]{3,2,1,0:T(8,128)(2,1)} %v_ref.1) | copy-start | bytes 3145732
  16.5 4.9 %collective-permute-start.4 = (f32[1,40,128]{2,1,0:T(8,128)S(1)}, f32[1,40,128]{2,1,0:T(8,128)S(1)}, u32[]{:S(2)}, u32[]{:S(2)}) collective-permute-start(f32[1,40,128]{2,1,0:T(8,128)S(1)} %get-tuple-element.57), channel_id=1, source_target_pairs={{0,8},{2,10},{4,12},{6,14},{8,0},{10,2},{12,4},{14,6},{1,9},{3,11}... | collective-permute-start | bytes 61448 | tf_op jit(solution)/shard_map/ppermute | solution.py:343
  22.6 4.7 %collective-permute-start.5 = (bf16[1,32,128]{2,1,0:T(8,128)(2,1)S(1)}, bf16[1,32,128]{2,1,0:T(8,128)(2,1)S(1)}, u32[]{:S(2)}, u32[]{:S(2)}) collective-permute-start(bf16[1,32,128]{2,1,0:T(8,128)(2,1)S(1)} %attend.1.refs_0_), channel_id=1, source_target_pairs={{0,8},{2,10},{4,12},{6,14},{8,0},{10,2},{12,4},{14,6},{1,9},{3,11}... | collective-permute-start | bytes 24584 | tf_op jit(solution)/shard_map/ppermute | solution.py:343
  27.3 5.8 %collective-permute-start.8 = (bf16[2,32,128]{2,1,0:T(8,128)(2,1)S(1)}, bf16[2,32,128]{2,1,0:T(8,128)(2,1)S(1)}, u32[]{:S(2)}, u32[]{:S(2)}) collective-permute-start(bf16[2,32,128]{2,1,0:T(8,128)(2,1)S(1)} %pad_maximum_fusion), channel_id=1, source_target_pairs={{0,6},{2,4},{4,2},{6,0},{8,14},{10,12},{12,10},{14,8},{1,7},{3,5},... | collective-permute-start | bytes 49160 | tf_op jit(solution)/shard_map/ppermute | solution.py:343
  28.8 4.3 %collective-permute-start.7 = (bf16[2,32,128]{2,1,0:T(8,128)(2,1)S(1)}, bf16[2,32,128]{2,1,0:T(8,128)(2,1)S(1)}, u32[]{:S(2)}, u32[]{:S(2)}) collective-permute-start(bf16[2,32,128]{2,1,0:T(8,128)(2,1)S(1)} %pad_maximum_fusion), channel_id=1, source_target_pairs={{0,2},{2,0},{4,6},{6,4},{8,10},{10,8},{12,14},{14,12},{1,3},{3,1},... | collective-permute-start | bytes 49160 | tf_op jit(solution)/shard_map/ppermute | solution.py:343
  29.3 3.8 %collective-permute-start.6 = (bf16[2,32,128]{2,1,0:T(8,128)(2,1)S(1)}, bf16[2,32,128]{2,1,0:T(8,128)(2,1)S(1)}, u32[]{:S(2)}, u32[]{:S(2)}) collective-permute-start(bf16[2,32,128]{2,1,0:T(8,128)(2,1)S(1)} %pad_maximum_fusion), channel_id=1, source_target_pairs={{0,4},{2,6},{4,0},{6,2},{8,12},{10,14},{12,8},{14,10},{1,5},{3,7},... | collective-permute-start | bytes 49160 | tf_op jit(solution)/shard_map/ppermute | solution.py:343
  36.1 1.3 %collective-permute-start.9 = (f32[4,2048]{1,0:T(4,128)S(1)}, f32[4,2048]{1,0:T(4,128)S(1)}, u32[]{:S(2)}, u32[]{:S(2)}) collective-permute-start(f32[4,2048]{1,0:T(4,128)S(1)} %get-tuple-element.56), channel_id=1, source_target_pairs={{0,1},{1,0},{2,3},{3,2},{4,5},{5,4},{6,7},{7,6},{8,9},{9,8},{10,11... | collective-permute-start | bytes 98312 | tf_op jit(solution)/shard_map/ppermute | solution.py:343

commit v8 on v7

--- a/solution.py
+++ b/solution.py
@@ -44,24 +44,31 @@
     ]
 
 
-def stage_kernel(parts, *refs):
-    count = len(parts)
-    sems = refs[-1]
-    copies = []
-    for i, (start, size) in enumerate(parts):
-        copies += copies_in(refs[i], refs[count + i], sems.at[i], start, size, 0)
+def stage_kernel(rows, src, dst, sems):
+    copies = copies_in(src, dst, sems, 0, rows, 0)
     for copy in copies:
         copy.start()
-    return copies
-
-
-def plain_stage_kernel(parts, *refs):
-    for copy in stage_kernel(parts, *refs):
+    for copy in copies:
         copy.wait()
 
 
-def turning_stage_kernel(parts, length_ref, frequency_ref, turn_ref, *refs):
-    copies = stage_kernel(parts, *refs)
+def stage_rows(array, rows):
+    vmem = pl.BlockSpec(memory_space=pltpu.VMEM)
+    return pl.pallas_call(
+        functools.partial(stage_kernel, rows),
+        out_shape=jax.ShapeDtypeStruct((rows, array.shape[1]), array.dtype),
+        in_specs=[pl.BlockSpec(memory_space=pltpu.HBM)],
+        out_specs=vmem,
+        scratch_shapes=[pltpu.SemaphoreType.DMA((PIECES,))],
+        compiler_params=pltpu.CompilerParams(vmem_limit_bytes=16 * MIB),
+        cost_estimate=pl.CostEstimate(
+            flops=0, bytes_accessed=2 * rows * array.shape[1], transcendentals=0
+        ),
+        name="stage",
+    )(in_hbm(array))
+
+
+def turning_kernel(length_ref, frequency_ref, beside_ref, turn_ref):
     position = length_ref[0].astype(jnp.float32)
     angle = position * frequency_ref[...]
     lane = lax.broadcasted_iota(jnp.int32, angle.shape, 1)
@@ -69,45 +76,22 @@
     turn_ref[0:1, :] = jnp.cos(angle)
     turn_ref[1:2, :] = jnp.where(lane < HEAD_SIZE // 2, -sine, sine)
     turn_ref[2:3, :] = jnp.full(angle.shape, position)
-    for copy in copies:
-        copy.wait()
-
-
-def stage(arrays, parts, lengths=None, frequency=None):
-    shapes = tuple(
-        jax.ShapeDtypeStruct((part[1], *a.shape[1:]), a.dtype) for a, part in zip(arrays, parts)
-    )
+
+
+def turning(lengths, frequency, beside):
     vmem = pl.BlockSpec(memory_space=pltpu.VMEM)
-    in_specs = [pl.BlockSpec(memory_space=pltpu.HBM)] * len(arrays)
-    out_specs = [vmem] * len(arrays)
-    kernel = functools.partial(plain_stage_kernel, parts)
-    pinned = [in_hbm(a) for a in arrays]
-    out_shape = shapes
-    if lengths is not None:
-        count = len(arrays)
-
-        def kernel(length_ref, frequency_ref, *refs):
-            turn_ref = refs[count]
-            turning_stage_kernel(
-                parts, length_ref, frequency_ref, turn_ref, *refs[:count], *refs[count + 1 :]
-            )
-
-        in_specs = [pl.BlockSpec(memory_space=pltpu.SMEM), vmem] + in_specs
-        out_specs = [vmem] + out_specs
-        out_shape = (jax.ShapeDtypeStruct((8, HEAD_SIZE), jnp.float32), *shapes)
-        pinned = [lengths, frequency] + pinned
-    return pl.pallas_call(
-        kernel,
-        out_shape=out_shape,
-        in_specs=in_specs,
-        out_specs=tuple(out_specs),
-        scratch_shapes=[pltpu.SemaphoreType.DMA((len(arrays), PIECES))],
-        compiler_params=pltpu.CompilerParams(vmem_limit_bytes=16 * MIB),
-        cost_estimate=pl.CostEstimate(
-            flops=0, bytes_accessed=sum(2 * math.prod(x.shape) for x in shapes), transcendentals=0
-        ),
-        name="stage",
-    )(*pinned)
+    return pl.pallas_call(
+        turning_kernel,
+        out_shape=jax.ShapeDtypeStruct((8, HEAD_SIZE), jnp.float32),
+        in_specs=[
+            pl.BlockSpec(memory_space=pltpu.SMEM),
+            vmem,
+            pl.BlockSpec(memory_space=pltpu.HBM),
+        ],
+        out_specs=vmem,
+        cost_estimate=pl.CostEstimate(flops=0, bytes_accessed=2 * beside.size, transcendentals=256),
+        name="turning",
+    )(lengths, frequency, in_hbm(beside))
 
 
 def spread(depth, skip, chunk):
@@ -189,7 +173,7 @@
             pltpu.VMEM((slots, depth), jnp.float32),
             pltpu.SemaphoreType.DMA((max(1, len(spread(depth, skip, CHUNK))), PIECES)),
         ],
-        compiler_params=pltpu.CompilerParams(vmem_limit_bytes=32 * MIB),
+        compiler_params=pltpu.CompilerParams(vmem_limit_bytes=46 * MIB),
         cost_estimate=pl.CostEstimate(
             flops=2 * slots * depth * (query_width + 2 * kv_width),
             bytes_accessed=2 * depth * (query_width + 2 * kv_width),
@@ -200,7 +184,7 @@
 
 
 def attend_kernel(
-    query_heads, kv_heads, pieces, turn_ref, k_ref, v_ref, *refs
+    query_heads, kv_heads, pieces, beside_ref, turn_ref, k_ref, v_ref, *refs
 ):
     heads_ref = refs[pieces]
     total = refs[0][0]
@@ -244,13 +228,13 @@
         heads_ref[0, pl.ds(head * group, group), :] = mixed.astype(jnp.bfloat16)
 
 
-def attend(parts, turn, k_cache, value_cache, query_heads):
+def attend(parts, turn, k_cache, value_cache, query_heads, beside):
     kv_heads, cache_len = k_cache.shape[1:3]
     whole = pl.BlockSpec(memory_space=pltpu.VMEM)
     return pl.pallas_call(
         functools.partial(attend_kernel, query_heads, kv_heads, len(parts)),
         out_shape=jax.ShapeDtypeStruct((1, query_heads, HEAD_SIZE), jnp.bfloat16),
-        in_specs=[whole] * (3 + len(parts)),
+        in_specs=[pl.BlockSpec(memory_space=pltpu.HBM)] + [whole] * (3 + len(parts)),
         out_specs=whole,
         compiler_params=pltpu.CompilerParams(vmem_limit_bytes=12 * MIB),
         cost_estimate=pl.CostEstimate(
@@ -259,22 +243,12 @@
             transcendentals=query_heads * cache_len,
         ),
         name="attend",
-    )(turn, k_cache, value_cache, *parts)
-
-
-def output_kernel(bits, pieces, staged, *refs):
+    )(in_hbm(beside), turn, k_cache, value_cache, *parts)
+
+
+def output_kernel(bits, pieces, *refs):
     parts = refs[:pieces]
-    ready = refs[pieces : pieces + staged]
-    w_hbm, mine_ref, theirs_ref, rest, flat, left, sums, sems = refs[pieces + staged :]
-    skip = sum(ref.shape[0] for ref in ready)
-    ranges = spread(w_hbm.shape[0], skip, 2 * CHUNK)
-    copies = [
-        copies_in(w_hbm, rest, sems.at[i], start, size, start - skip)
-        for i, (start, size) in enumerate(ranges)
-    ]
-    for group in copies:
-        for copy in group:
-            copy.start()
+    w_ref, mine_ref, theirs_ref, flat, left, sums = refs[pieces:]
     slots = left.shape[0]
     heads = flat.shape[0] // slots
     at = 0
@@ -287,20 +261,11 @@
             pl.ds(head, slots, stride=heads), :
         ].astype(jnp.bfloat16)
     total = None
-    at = 0
-    for ref in ready:
-        size = ref.shape[0]
-        term = jnp.dot(left[:, at : at + size], ref[...], preferred_element_type=jnp.float32)
-        total = term if total is None else total + term
-        at += size
-    for (start, size), group in zip(ranges, copies):
-        for copy in group:
-            copy.wait()
-        term = jnp.dot(
-            left[:, start : start + size],
-            rest[start - skip : start - skip + size, :],
-            preferred_element_type=jnp.float32,
-        )
+    depth = w_ref.shape[0]
+    chunk = min(2 * CHUNK, depth)
+    for at in range(0, depth, chunk):
+        part = slice(at, at + chunk)
+        term = jnp.dot(left[:, part], w_ref[part, :], preferred_element_type=jnp.float32)
         total = term if total is None else total + term
     sums[...] = total
     half = slots // 2
@@ -312,31 +277,28 @@
             ref[t : t + 1, :] = sums[pl.ds(slot, 1), :]
 
 
-def output(parts, ready, w_out, slots):
+def output(parts, w_out, slots):
     bits = slots.bit_length() - 1
     depth, width = w_out.shape
     heads = depth // HEAD_SIZE
-    skip = sum(x.shape[0] for x in ready)
     whole = pl.BlockSpec(memory_space=pltpu.VMEM)
     piece = jax.ShapeDtypeStruct((slots // 2, width), jnp.float32)
     return pl.pallas_call(
-        functools.partial(output_kernel, bits, len(parts), len(ready)),
+        functools.partial(output_kernel, bits, len(parts)),
         out_shape=(piece, piece),
-        in_specs=[whole] * (len(parts) + len(ready)) + [pl.BlockSpec(memory_space=pltpu.HBM)],
+        in_specs=[whole] * (len(parts) + 1),
         out_specs=(whole, whole),
         scratch_shapes=[
-            pltpu.VMEM((max(depth - skip, 16), width), jnp.bfloat16),
             pltpu.VMEM((slots * heads, HEAD_SIZE), jnp.float32),
             pltpu.VMEM((slots, depth), jnp.bfloat16),
             pltpu.VMEM((slots, width), jnp.float32),
-            pltpu.SemaphoreType.DMA((max(1, len(spread(depth, skip, 2 * CHUNK))), PIECES)),
         ],
         compiler_params=pltpu.CompilerParams(vmem_limit_bytes=24 * MIB),
         cost_estimate=pl.CostEstimate(
             flops=2 * slots * depth * width, bytes_accessed=2 * depth * width, transcendentals=0
         ),
         name="output",
-    )(*parts, *ready, in_hbm(w_out))
+    )(*parts, w_out)
 
 
 def swap(block, axis, devices, mask):
@@ -356,45 +318,32 @@
     query_heads = w_query.shape[1] // HEAD_SIZE
     other = swap(activations, "gy", 2, 1)
     depth = w_query.shape[0]
-    (first,) = stage((w_query,), ((0, min(FIRST, depth)),))
+    first = stage_rows(w_query, min(FIRST, depth))
     pieces = project(activations, other, w_query, first, key_weight, value_weight, slots)
 
-    rows_out = w_out.shape[0]
-    *pieces, w_out = lax.optimization_barrier((*pieces, w_out))
-    few, most = rows_out // 8, rows_out // 4
     arrived = fan(pieces, devices)
     half = HEAD_SIZE // 2
     frequency = jnp.power(
         jnp.float32(500000.0), -2.0 * jnp.arange(half, dtype=jnp.float32) / HEAD_SIZE
     )
     frequency = jnp.concatenate([frequency, frequency])[None, :]
-    turn, ready_one = stage((w_out,), ((0, few),), lengths, frequency)
+    turn = turning(lengths, frequency, w_out)
     total = pieces[0] + (arrived[2] + (arrived[1] + arrived[0]))
     mask = FAN
     while total.shape[0] > 2:
         rest = total.shape[0] // 2
         total = total[:rest] + swap(total[rest:], "gx", devices, mask)
         mask *= 2
-    total, w_out, ready_one = lax.optimization_barrier((total, w_out, ready_one))
-    (ready_two,) = stage((w_out,), ((few, most),))
     parts = [total[:1], swap(total[1:], "gx", devices, mask)]
-    parts[1], ready_two = lax.optimization_barrier((parts[1], ready_two))
-    heads = attend(parts, turn, k_cache, value_cache, query_heads)
-
-    heads, w_out = lax.optimization_barrier((heads, w_out))
-    (ready_three,) = stage((w_out,), ((few + most, most),))
+    heads = attend(parts, turn, k_cache, value_cache, query_heads, w_out)
+
     parts = [heads, swap(heads, "gx", devices, mask)]
-    parts[1], ready_three = lax.optimization_barrier((parts[1], ready_three))
     while mask > FAN:
         mask //= 2
         parts.append(swap(jnp.concatenate(parts, axis=0), "gx", devices, mask))
     held = jnp.concatenate(parts, axis=0)
-    held, w_out = lax.optimization_barrier((held, w_out))
-    (ready_four,) = stage((w_out,), ((few + 2 * most, most),))
     parts += fan([held] * FAN, devices)
-    parts[-1], ready_four = lax.optimization_barrier((parts[-1], ready_four))
-    ready = (ready_one, ready_two, ready_three, ready_four)
-    mine, theirs = output(parts, ready, w_out, slots)
+    mine, theirs = output(parts, w_out, slots)
     return (mine + swap(theirs, "gy", 2, 1)).astype(jnp.bfloat16)
 
 

time: 38.2 us -> 45.2 us (1.18)
  waiting for transfers between devices: 2.81 us -> 10.5 us
  Pallas kernels: 19.7 us -> 12.3 us
  local copies, waits for them, and re-layouts: 0.46 us -> 6.48 us
  other arithmetic: 0.72 us -> 1.3 us
    ppermute x10, waiting for transfers between devices: 2.81 us -> 10.5 us  [swap(): return lax.ppermute(block, axis, [(i, i ^ mask) for i in range(devices)])]
    pallas_call x6 -> x3, Pallas kernels: 12.8 us -> 5.29 us  [the longest x1 2.31 us: output(): pl.pallas_call(functools.partial(output_kernel, bits, len(parts)), out_sh...]
    unnamed x10 -> x14, local copies, waits for them, and re-layouts: 0.46 us -> 6.48 us
    broadcast_in_dim x1, other arithmetic: 0.07 us -> 0.66 us  [body(): frequency = jnp.concatenate([frequency, frequency])[None, :]]
  transfers between devices with their start and end apart: 10 -> 10, of which waited for: 3 -> 8; matrix products, arithmetic and copies ran while one was open for 0% -> 1% of each run, Pallas kernels for 26% -> 7%
where the time goes in v8:
time: 45.2 us; the launch traced here: 45 us
  starting transfers between devices  13.7 us (30%)
  Pallas kernels  12.3 us (27%)
  waiting for transfers between devices  10.5 us (23%)
  local copies, waits for them, and re-layouts  6.48 us (14%)
  other arithmetic  1.3 us (3%)
  between operations  0.77 us (2%)
    ppermute x10, starting transfers between devices, swap(): return lax.ppermute(block, axis, [(i, i ^ mask) for i in range(devices)])  13.7 us
    ppermute x10, waiting for transfers between devices, swap(): return lax.ppermute(block, axis, [(i, i ^ mask) for i in range(devices)])  10.5 us
    unnamed x14, local copies, waits for them, and re-layouts  6.48 us
    pallas_call x1, Pallas kernels, project(): pl.pallas_call(functools.partial(project_kernel, bits), out_shape=(piece,...  5.86 us
    pallas_call x1, Pallas kernels, output(): pl.pallas_call(functools.partial(output_kernel, bits, len(parts)), out_sh...  2.31 us
    pallas_call x1, Pallas kernels, stage_rows(): pl.pallas_call(functools.partial(stage_kernel, rows), out_shape=jax.Shape...  1.67 us
    pallas_call x1, Pallas kernels, turning(): pl.pallas_call(turning_kernel, out_shape=jax.ShapeDtypeStruct((8, HEAD_SI...  1.31 us
    pallas_call x1, Pallas kernels, attend(): pl.pallas_call(functools.partial(attend_kernel, query_heads, kv_heads, le...  1.16 us
  transfers between devices with their start and end apart: 10, of which 8 were waited for; matrix products, arithmetic and copies ran while one was open for 1% of the time, Pallas kernels for 7%

profile of v8, /device:TPU:0, one launch (start us, length us, event | category | flops | bytes accessed | tf_op | source)
XLA Modules:
  0.0 45.0 jit_solution(3580382651335857967)
XLA Ops:
  0.0 0.5 %collective-permute-start = (bf16[4,2048]{1,0:T(4,128)(2,1)}, bf16[4,2048]{1,0:T(4,128)(2,1)S(1)}, u32[]{:S(2)}, u32[]{:S(2)}) collective-permute-start(bf16[4,2048]{1,0:T(4,128)(2,1)} %rows_ref.1), channel_id=1, source_target_pairs={{0,1},{1,0},{2,3},{3,2},{4,5},{5,4},{6,7},{7,6},{8,9},{9,8},{10,11... | collective-permute-start | bytes 49160 | tf_op jit(solution)/shard_map/ppermute | solution.py:305
  0.5 1.7 %stage.1.first = bf16[256,4096]{1,0:T(8,128)(2,1)S(1)} custom-call(bf16[2048,4096]{1,0:T(8,128)(2,1)} %wq_hbm.1), custom_call_target="tpu_custom_call" | custom-call | bytes 2097152 | tf_op jit(solution)/shard_map/stage/pallas_call | solution.py:57
  2.3 5.9 %project.1 = (f32[2,40,128]{2,1,0:T(8,128)S(1)}, f32[2,40,128]{2,1,0:T(8,128)S(1)}, f32[2,40,128]{2,1,0:T(8,128)S(1)}, f32[2,40,128]{2,1,0:T(8,128)S(1)}) custom-call(bf16[4,2048]{1,0:T(4,128)(2,1)S(1)} %copy-done.5, bf16[4,2048]{1,0:T(4,128)(2,1)S(1)} %collective-permute-done.other_ref, bf16[2048,4096]{1,0:T(8,128)(2,1)} %wq_hbm.1, ...), custom_call_target="tpu_custom_call" | custom-call | flops 150994944 | bytes 18874368 | tf_op jit(solution)/shard_map/project/pallas_call | solution.py:166
  8.1 4.0 %collective-permute-start.1 = (f32[2,40,128]{2,1,0:T(8,128)S(1)}, f32[2,40,128]{2,1,0:T(8,128)S(1)}, u32[]{:S(2)}, u32[]{:S(2)}) collective-permute-start(f32[2,40,128]{2,1,0:T(8,128)S(1)} %get-tuple-element.12), channel_id=1, source_target_pairs={{0,6},{2,4},{4,2},{6,0},{8,14},{10,12},{12,10},{14,8},{1,7},{3,5},... | collective-permute-start | bytes 122888 | tf_op jit(solution)/shard_map/ppermute | solution.py:305
  12.1 0.5 %collective-permute-start.2 = (f32[2,40,128]{2,1,0:T(8,128)S(1)}, f32[2,40,128]{2,1,0:T(8,128)S(1)}, u32[]{:S(2)}, u32[]{:S(2)}) collective-permute-start(f32[2,40,128]{2,1,0:T(8,128)S(1)} %get-tuple-element.13), channel_id=1, source_target_pairs={{0,2},{2,0},{4,6},{6,4},{8,10},{10,8},{12,14},{14,12},{1,3},{3,1},... | collective-permute-start | bytes 122888 | tf_op jit(solution)/shard_map/ppermute | solution.py:305
  12.8 1.3 %collective-permute-done.1 = f32[2,40,128]{2,1,0:T(8,128)S(1)} collective-permute-done((f32[2,40,128]{2,1,0:T(8,128)S(1)}, f32[2,40,128]{2,1,0:T(8,128)S(1)}, u32[]{:S(2)}, u32[]{:S(2)}) %collective-permute-start.1) | collective-permute-done | bytes 40992 | tf_op jit(solution)/shard_map/ppermute | solution.py:305
  14.1 2.0 %collective-permute-done.2 = f32[2,40,128]{2,1,0:T(8,128)S(1)} collective-permute-done((f32[2,40,128]{2,1,0:T(8,128)S(1)}, f32[2,40,128]{2,1,0:T(8,128)S(1)}, u32[]{:S(2)}, u32[]{:S(2)}) %collective-permute-start.2) | collective-permute-done | bytes 40992 | tf_op jit(solution)/shard_map/ppermute | solution.py:305
  16.1 0.5 %collective-permute-done.3 = f32[2,40,128]{2,1,0:T(8,128)S(1)} collective-permute-done((f32[2,40,128]{2,1,0:T(8,128)S(1)}, f32[2,40,128]{2,1,0:T(8,128)S(1)}, u32[]{:S(2)}, u32[]{:S(2)}) %collective-permute-start.3) | collective-permute-done | bytes 40992 | tf_op jit(solution)/shard_map/ppermute | solution.py:305
  16.7 2.9 %collective-permute-start.4 = (f32[1,40,128]{2,1,0:T(8,128)S(1)}, f32[1,40,128]{2,1,0:T(8,128)S(1)}, u32[]{:S(2)}, u32[]{:S(2)}) collective-permute-start(f32[1,40,128]{2,1,0:T(8,128)S(1)} %get-tuple-element.17), channel_id=1, source_target_pairs={{0,8},{2,10},{4,12},{6,14},{8,0},{10,2},{12,4},{14,6},{1,9},{3,11}... | collective-permute-start | bytes 61448 | tf_op jit(solution)/shard_map/ppermute | solution.py:305
  19.6 0.7 %maximum_bitcast_fusion.frequency_ref = f32[1,128]{1,0:T(1,128)} fusion(f32[64]{0:T(128)S(1)} %multiply_power_fusion), kind=kLoop, calls=%fused_computation.3 | loop fusion | flops 128 | bytes 768 | tf_op jit(solution)/shard_map/broadcast_in_dim | solution.py:329
  20.9 1.3 %turning.1.turn_ref = f32[8,128]{1,0:T(8,128)} custom-call(s32[1]{0:T(128)S(6)} %copy.9.length_ref, f32[1,128]{1,0:T(1,128)} %maximum_bitcast_fusion.frequency_ref, bf16[4096,2048]{1,0:T(8,128)(2,1)} %refs_5_.1), custom_call_target="tpu_custom_call" | custom-call | bytes 16777216 | tf_op jit(solution)/shard_map/turning/pallas_call | solution.py:83
  22.2 0.7 %copy-done.6 = f32[8,128]{1,0:T(8,128)S(1)} copy-done((f32[8,128]{1,0:T(8,128)S(1)}, f32[8,128]{1,0:T(8,128)}, u32[]{:S(2)}) %copy-start.6) | copy-done | bytes 4120
  22.9 1.2 %attend.1.refs_0_ = bf16[1,32,128]{2,1,0:T(8,128)(2,1)S(1)} custom-call(bf16[4096,2048]{1,0:T(8,128)(2,1)} %refs_5_.1, f32[8,128]{1,0:T(8,128)S(1)} %copy-done.6, bf16[1,2,2048,128]{3,2,1,0:T(8,128)(2,1)S(1)} %copy-done.3, bf16[1,2,2048,128]{3,2,1,0:T(8,128)(2,1)S(1)} %copy-done.4, f32[1,40,128]{2,1,0:T(8,128)S(1)} %get-tuple-element.18.refs_0_, ...), custom_call_target="tpu_custom_call" | custom-call | flops 33554432 | bytes 2097152 | tf_op jit(solution)/shard_map/attend/pallas_call | solution.py:234
  24.1 2.1 %collective-permute-start.5 = (bf16[1,32,128]{2,1,0:T(8,128)(2,1)S(1)}, bf16[1,32,128]{2,1,0:T(8,128)(2,1)S(1)}, u32[]{:S(2)}, u32[]{:S(2)}) collective-permute-start(bf16[1,32,128]{2,1,0:T(8,128)(2,1)S(1)} %attend.1.refs_0_), channel_id=1, source_target_pairs={{0,8},{2,10},{4,12},{6,14},{8,0},{10,2},{12,4},{14,6},{1,9},{3,11}... | collective-permute-start | bytes 24584 | tf_op jit(solution)/shard_map/ppermute | solution.py:305
  26.2 2.5 %collective-permute-done.5.refs_1_ = bf16[1,32,128]{2,1,0:T(8,128)(2,1)S(1)} collective-permute-done((bf16[1,32,128]{2,1,0:T(8,128)(2,1)S(1)}, bf16[1,32,128]{2,1,0:T(8,128)(2,1)S(1)}, u32[]{:S(2)}, u32[]{:S(2)}) %collective-permute-start.5) | collective-permute-done | bytes 8224 | tf_op jit(solution)/shard_map/ppermute | solution.py:305
  28.7 0.2 collective-permute-start.6
  28.9 1.5 %collective-permute-start.7 = (bf16[2,32,128]{2,1,0:T(8,128)(2,1)S(1)}, bf16[2,32,128]{2,1,0:T(8,128)(2,1)S(1)}, u32[]{:S(2)}, u32[]{:S(2)}) collective-permute-start(bf16[2,32,128]{2,1,0:T(8,128)(2,1)S(1)} %pad_maximum_fusion), channel_id=1, source_target_pairs={{0,2},{2,0},{4,6},{6,4},{8,10},{10,8},{12,14},{14,12},{1,3},{3,1},... | collective-permute-start | bytes 49160 | tf_op jit(solution)/shard_map/ppermute | solution.py:305
  30.4 1.8 %collective-permute-start.8 = (bf16[2,32,128]{2,1,0:T(8,128)(2,1)S(1)}, bf16[2,32,128]{2,1,0:T(8,128)(2,1)S(1)}, u32[]{:S(2)}, u32[]{:S(2)}) collective-permute-start(bf16[2,32,128]{2,1,0:T(8,128)(2,1)S(1)} %pad_maximum_fusion), channel_id=1, source_target_pairs={{0,6},{2,4},{4,2},{6,0},{8,14},{10,12},{12,10},{14,8},{1,7},{3,5},... | collective-permute-start | bytes 49160 | tf_op jit(solution)/shard_map/ppermute | solution.py:305
  32.2 0.2 collective-permute-done.6.refs_2_
  32.6 2.4 %collective-permute-done.8.refs_4_ = bf16[2,32,128]{2,1,0:T(8,128)(2,1)S(1)} collective-permute-done((bf16[2,32,128]{2,1,0:T(8,128)(2,1)S(1)}, bf16[2,32,128]{2,1,0:T(8,128)(2,1)S(1)}, u32[]{:S(2)}, u32[]{:S(2)}) %collective-permute-start.8) | collective-permute-done | bytes 16416 | tf_op jit(solution)/shard_map/ppermute | solution.py:305
  35.0 5.8 %copy-done = bf16[4096,2048]{1,0:T(8,128)(2,1)S(1)} copy-done((bf16[4096,2048]{1,0:T(8,128)(2,1)S(1)}, bf16[4096,2048]{1,0:T(8,128)(2,1)}, u32[]{:S(2)}) %copy-start) | copy-done | bytes 16777240
  40.8 2.3 %output.1 = (f32[4,2048]{1,0:T(4,128)S(1)}, f32[4,2048]{1,0:T(4,128)S(1)}) custom-call(bf16[1,32,128]{2,1,0:T(8,128)(2,1)S(1)} %attend.1.refs_0_, bf16[1,32,128]{2,1,0:T(8,128)(2,1)S(1)} %collective-permute-done.5.refs_1_, bf16[2,32,128]{2,1,0:T(8,128)(2,1)S(1)} %collective-permute-done.6.refs_2_, bf16[2,32,128]{2,1,0:T(8,128)(2,1)S(1)} %collective-permute-done.7.refs_3_, ...), custom_call_target="tpu_custom_call" | custom-call | flops 134217728 | bytes 16777216 | tf_op jit(solution)/shard_map/output/pallas_call | solution.py:286
  43.2 1.2 %collective-permute-done.9 = f32[4,2048]{1,0:T(4,128)S(1)} collective-permute-done((f32[4,2048]{1,0:T(4,128)S(1)}, f32[4,2048]{1,0:T(4,128)S(1)}, u32[]{:S(2)}, u32[]{:S(2)}) %collective-permute-start.9) | collective-permute-done | bytes 32800 | tf_op jit(solution)/shard_map/ppermute | solution.py:305
  44.4 0.6 %add_convert_fusion = bf16[4,2048]{1,0:T(4,128)(2,1)} fusion(f32[4,2048]{1,0:T(4,128)S(1)} %get-tuple-element.15, f32[4,2048]{1,0:T(4,128)S(1)} %collective-permute-done.9), kind=kLoop, calls=%fused_computation.1 | loop fusion | flops 16384 | bytes 81920 | tf_op jit(solution)/shard_map/convert_element_type | solution.py:347
  (21 shorter events, 0.5 us)
Async XLA Ops:
  0.0 2.2 %copy-start.5 = (bf16[4,2048]{1,0:T(4,128)(2,1)S(1)}, bf16[4,2048]{1,0:T(4,128)(2,1)}, u32[]{:S(2)}) copy-start(bf16[4,2048]{1,0:T(4,128)(2,1)} %rows_ref.1) | copy-start | bytes 49156
  0.0 2.2 %copy-start.1 = (bf16[2048,256]{1,0:T(8,128)(2,1)S(1)}, bf16[2048,256]{1,0:T(8,128)(2,1)}, u32[]{:S(2)}) copy-start(bf16[2048,256]{1,0:T(8,128)(2,1)} %wk.1) | copy-start | bytes 3145732
  0.0 2.3 %copy-start.2 = (bf16[2048,256]{1,0:T(8,128)(2,1)S(1)}, bf16[2048,256]{1,0:T(8,128)(2,1)}, u32[]{:S(2)}) copy-start(bf16[2048,256]{1,0:T(8,128)(2,1)} %wv.1) | copy-start | bytes 3145732
  0.0 2.2 %collective-permute-start = (bf16[4,2048]{1,0:T(4,128)(2,1)}, bf16[4,2048]{1,0:T(4,128)(2,1)S(1)}, u32[]{:S(2)}, u32[]{:S(2)}) collective-permute-start(bf16[4,2048]{1,0:T(4,128)(2,1)} %rows_ref.1), channel_id=1, source_target_pairs={{0,1},{1,0},{2,3},{3,2},{4,5},{5,4},{6,7},{7,6},{8,9},{9,8},{10,11... | collective-permute-start | bytes 49160 | tf_op jit(solution)/shard_map/ppermute | solution.py:305
  2.2 20.0 %copy-start.3 = (bf16[1,2,2048,128]{3,2,1,0:T(8,128)(2,1)S(1)}, bf16[1,2,2048,128]{3,2,1,0:T(8,128)(2,1)}, u32[]{:S(2)}) copy-start(bf16[1,2,2048,128]{3,2,1,0:T(8,128)(2,1)} %k_ref.1) | copy-start | bytes 3145732
  2.2 20.0 %copy-start.4 = (bf16[1,2,2048,128]{3,2,1,0:T(8,128)(2,1)S(1)}, bf16[1,2,2048,128]{3,2,1,0:T(8,128)(2,1)}, u32[]{:S(2)}) copy-start(bf16[1,2,2048,128]{3,2,1,0:T(8,128)(2,1)} %v_ref.1) | copy-start | bytes 3145732
  8.1 6.0 %collective-permute-start.1 = (f32[2,40,128]{2,1,0:T(8,128)S(1)}, f32[2,40,128]{2,1,0:T(8,128)S(1)}, u32[]{:S(2)}, u32[]{:S(2)}) collective-permute-start(f32[2,40,128]{2,1,0:T(8,128)S(1)} %get-tuple-element.12), channel_id=1, source_target_pairs={{0,6},{2,4},{4,2},{6,0},{8,14},{10,12},{12,10},{14,8},{1,7},{3,5},... | collective-permute-start | bytes 122888 | tf_op jit(solution)/shard_map/ppermute | solution.py:305
  12.1 4.0 %collective-permute-start.2 = (f32[2,40,128]{2,1,0:T(8,128)S(1)}, f32[2,40,128]{2,1,0:T(8,128)S(1)}, u32[]{:S(2)}, u32[]{:S(2)}) collective-permute-start(f32[2,40,128]{2,1,0:T(8,128)S(1)} %get-tuple-element.13), channel_id=1, source_target_pairs={{0,2},{2,0},{4,6},{6,4},{8,10},{10,8},{12,14},{14,12},{1,3},{3,1},... | collective-permute-start | bytes 122888 | tf_op jit(solution)/shard_map/ppermute | solution.py:305
  12.7 4.0 %collective-permute-start.3 = (f32[2,40,128]{2,1,0:T(8,128)S(1)}, f32[2,40,128]{2,1,0:T(8,128)S(1)}, u32[]{:S(2)}, u32[]{:S(2)}) collective-permute-start(f32[2,40,128]{2,1,0:T(8,128)S(1)} %get-tuple-element.14), channel_id=1, source_target_pairs={{0,4},{2,6},{4,0},{6,2},{8,12},{10,14},{12,8},{14,10},{1,5},{3,7},... | collective-permute-start | bytes 122888 | tf_op jit(solution)/shard_map/ppermute | solution.py:305
  16.7 5.5 %collective-permute-start.4 = (f32[1,40,128]{2,1,0:T(8,128)S(1)}, f32[1,40,128]{2,1,0:T(8,128)S(1)}, u32[]{:S(2)}, u32[]{:S(2)}) collective-permute-start(f32[1,40,128]{2,1,0:T(8,128)S(1)} %get-tuple-element.17), channel_id=1, source_target_pairs={{0,8},{2,10},{4,12},{6,14},{8,0},{10,2},{12,4},{14,6},{1,9},{3,11}... | collective-permute-start | bytes 61448 | tf_op jit(solution)/shard_map/ppermute | solution.py:305
  22.2 0.7 %copy-start.6 = (f32[8,128]{1,0:T(8,128)S(1)}, f32[8,128]{1,0:T(8,128)}, u32[]{:S(2)}) copy-start(f32[8,128]{1,0:T(8,128)} %turning.1.turn_ref) | copy-start | bytes 12292
  24.1 4.6 %collective-permute-start.5 = (bf16[1,32,128]{2,1,0:T(8,128)(2,1)S(1)}, bf16[1,32,128]{2,1,0:T(8,128)(2,1)S(1)}, u32[]{:S(2)}, u32[]{:S(2)}) collective-permute-start(bf16[1,32,128]{2,1,0:T(8,128)(2,1)S(1)} %attend.1.refs_0_), channel_id=1, source_target_pairs={{0,8},{2,10},{4,12},{6,14},{8,0},{10,2},{12,4},{14,6},{1,9},{3,11}... | collective-permute-start | bytes 24584 | tf_op jit(solution)/shard_map/ppermute | solution.py:305
  28.7 3.7 %collective-permute-start.6 = (bf16[2,32,128]{2,1,0:T(8,128)(2,1)S(1)}, bf16[2,32,128]{2,1,0:T(8,128)(2,1)S(1)}, u32[]{:S(2)}, u32[]{:S(2)}) collective-permute-start(bf16[2,32,128]{2,1,0:T(8,128)(2,1)S(1)} %pad_maximum_fusion), channel_id=1, source_target_pairs={{0,4},{2,6},{4,0},{6,2},{8,12},{10,14},{12,8},{14,10},{1,5},{3,7},... | collective-permute-start | bytes 49160 | tf_op jit(solution)/shard_map/ppermute | solution.py:305
  28.9 3.7 %collective-permute-start.7 = (bf16[2,32,128]{2,1,0:T(8,128)(2,1)S(1)}, bf16[2,32,128]{2,1,0:T(8,128)(2,1)S(1)}, u32[]{:S(2)}, u32[]{:S(2)}) collective-permute-start(bf16[2,32,128]{2,1,0:T(8,128)(2,1)S(1)} %pad_maximum_fusion), channel_id=1, source_target_pairs={{0,2},{2,0},{4,6},{6,4},{8,10},{10,8},{12,14},{14,12},{1,3},{3,1},... | collective-permute-start | bytes 49160 | tf_op jit(solution)/shard_map/ppermute | solution.py:305
  30.4 4.6 %collective-permute-start.8 = (bf16[2,32,128]{2,1,0:T(8,128)(2,1)S(1)}, bf16[2,32,128]{2,1,0:T(8,128)(2,1)S(1)}, u32[]{:S(2)}, u32[]{:S(2)}) collective-permute-start(bf16[2,32,128]{2,1,0:T(8,128)(2,1)S(1)} %pad_maximum_fusion), channel_id=1, source_target_pairs={{0,6},{2,4},{4,2},{6,0},{8,14},{10,12},{12,10},{14,8},{1,7},{3,5},... | collective-permute-start | bytes 49160 | tf_op jit(solution)/shard_map/ppermute | solution.py:305
  35.0 5.8 %copy-start = (bf16[4096,2048]{1,0:T(8,128)(2,1)S(1)}, bf16[4096,2048]{1,0:T(8,128)(2,1)}, u32[]{:S(2)}) copy-start(bf16[4096,2048]{1,0:T(8,128)(2,1)} %refs_5_.1) | copy-start | bytes 50331652
  43.1 1.3 %collective-permute-start.9 = (f32[4,2048]{1,0:T(4,128)S(1)}, f32[4,2048]{1,0:T(4,128)S(1)}, u32[]{:S(2)}, u32[]{:S(2)}) collective-permute-start(f32[4,2048]{1,0:T(4,128)S(1)} %get-tuple-element.16), channel_id=1, source_target_pairs={{0,1},{1,0},{2,3},{3,2},{4,5},{5,4},{6,7},{7,6},{8,9},{9,8},{10,11... | collective-permute-start | bytes 98312 | tf_op jit(solution)/shard_map/ppermute | solution.py:305

commit v9 on v7

--- a/solution.py
+++ b/solution.py
@@ -111,11 +111,19 @@
 
 
 def spread(depth, skip, chunk):
-    ranges = [(at, min(chunk, depth - at)) for at in range(skip, depth, chunk)]
-    if ranges and ranges[-1][1] >= 2 * LANES:
-        start, size = ranges.pop()
-        ranges += [(start, size - LANES), (start + size - LANES, LANES)]
-    return ranges
+    return [(at, min(chunk, depth - at)) for at in range(skip, depth, chunk)]
+
+
+def tapered(ranges):
+    *most, (start, size) = ranges
+    if size < 2 * LANES:
+        return ranges
+    return most + [(start, size - LANES), (start + size - LANES, LANES)]
+
+
+def feed(depth, skip):
+    ranges = spread(depth, skip, CHUNK)
+    return tapered(ranges) if ranges else ranges
 
 
 def project_kernel(
@@ -123,7 +131,7 @@
 ):
     pieces, (wq, rows, sems) = refs[:FAN], refs[FAN:]
     skip = first.shape[0]
-    ranges = spread(wq_hbm.shape[0], skip, CHUNK)
+    ranges = feed(wq_hbm.shape[0], skip)
     copies = [
         copies_in(wq_hbm, wq, sems.at[i], start, size, start - skip)
         for i, (start, size) in enumerate(ranges)
@@ -187,7 +195,7 @@
         scratch_shapes=[
             pltpu.VMEM((max(depth - skip, 16), query_width), jnp.bfloat16),
             pltpu.VMEM((slots, depth), jnp.float32),
-            pltpu.SemaphoreType.DMA((max(1, len(spread(depth, skip, CHUNK))), PIECES)),
+            pltpu.SemaphoreType.DMA((max(1, len(feed(depth, skip))), PIECES)),
         ],
         compiler_params=pltpu.CompilerParams(vmem_limit_bytes=32 * MIB),
         cost_estimate=pl.CostEstimate(
@@ -200,9 +208,12 @@
 
 
 def attend_kernel(
-    query_heads, kv_heads, pieces, turn_ref, k_ref, v_ref, *refs
+    query_heads, kv_heads, pieces, part, w_hbm, turn_ref, k_ref, v_ref, *refs
 ):
-    heads_ref = refs[pieces]
+    heads_ref, w_ref, sems = refs[pieces:]
+    copies = copies_in(w_hbm, w_ref, sems, *part, 0)
+    for copy in copies:
+        copy.start()
     total = refs[0][0]
     for ref in refs[1:pieces]:
         total = total + ref[0]
@@ -216,24 +227,26 @@
     group = query_heads // kv_heads
     factor = 1.0 / math.sqrt(HEAD_SIZE)
     length = turn_ref[2:3, 0:1].astype(jnp.int32)
+    scores = []
+    own = []
     for head in range(kv_heads):
         queries = turned[head * group : (head + 1) * group]
-        fresh_key = turned[query_heads + head : query_heads + head + 1].astype(jnp.float32)
-        own = jnp.sum(queries.astype(jnp.float32) * fresh_key, axis=1, keepdims=True) * factor
-        scores = (
+        scores.append(
             lax.dot_general(
                 queries,
                 k_ref[0, head],
                 (((1,), (1,)), ((), ())),
                 preferred_element_type=jnp.float32,
             )
-            * factor
         )
-        slot = lax.broadcasted_iota(jnp.int32, scores.shape, 1)
-        scores = jnp.where(slot < length, scores, -jnp.inf)
-        top = jnp.maximum(jnp.max(scores, axis=1, keepdims=True), own)
-        exponent = jnp.exp(scores - top)
-        own_exp = jnp.exp(own - top)
+        fresh_key = turned[query_heads + head : query_heads + head + 1].astype(jnp.float32)
+        own.append(jnp.sum(queries.astype(jnp.float32) * fresh_key, axis=1, keepdims=True) * factor)
+    slot = lax.broadcasted_iota(jnp.int32, scores[0].shape, 1)
+    for head in range(kv_heads):
+        live = jnp.where(slot < length, scores[head] * factor, -jnp.inf)
+        top = jnp.maximum(jnp.max(live, axis=1, keepdims=True), own[head])
+        exponent = jnp.exp(live - top)
+        own_exp = jnp.exp(own[head] - top)
         share = 1.0 / (jnp.sum(exponent, axis=1, keepdims=True) + own_exp)
         weights = (exponent * share).astype(jnp.bfloat16)
         own_weight = (own_exp * share).astype(jnp.bfloat16)
@@ -242,16 +255,22 @@
             jnp.float32
         )
         heads_ref[0, pl.ds(head * group, group), :] = mixed.astype(jnp.bfloat16)
-
-
-def attend(parts, turn, k_cache, value_cache, query_heads):
+    for copy in copies:
+        copy.wait()
+
+
+def attend(parts, turn, k_cache, value_cache, query_heads, w_out, part):
     kv_heads, cache_len = k_cache.shape[1:3]
     whole = pl.BlockSpec(memory_space=pltpu.VMEM)
     return pl.pallas_call(
-        functools.partial(attend_kernel, query_heads, kv_heads, len(parts)),
-        out_shape=jax.ShapeDtypeStruct((1, query_heads, HEAD_SIZE), jnp.bfloat16),
-        in_specs=[whole] * (3 + len(parts)),
-        out_specs=whole,
+        functools.partial(attend_kernel, query_heads, kv_heads, len(parts), part),
+        out_shape=(
+            jax.ShapeDtypeStruct((1, query_heads, HEAD_SIZE), jnp.bfloat16),
+            jax.ShapeDtypeStruct((part[1], w_out.shape[1]), w_out.dtype),
+        ),
+        in_specs=[pl.BlockSpec(memory_space=pltpu.HBM)] + [whole] * (3 + len(parts)),
+        out_specs=(whole, whole),
+        scratch_shapes=[pltpu.SemaphoreType.DMA((PIECES,))],
         compiler_params=pltpu.CompilerParams(vmem_limit_bytes=12 * MIB),
         cost_estimate=pl.CostEstimate(
             flops=4 * query_heads * cache_len * HEAD_SIZE,
@@ -259,22 +278,13 @@
             transcendentals=query_heads * cache_len,
         ),
         name="attend",
-    )(turn, k_cache, value_cache, *parts)
-
-
-def output_kernel(bits, pieces, staged, *refs):
+    )(in_hbm(w_out), turn, k_cache, value_cache, *parts)
+
+
+def output_kernel(bits, pieces, *refs):
     parts = refs[:pieces]
-    ready = refs[pieces : pieces + staged]
-    w_hbm, mine_ref, theirs_ref, rest, flat, left, sums, sems = refs[pieces + staged :]
-    skip = sum(ref.shape[0] for ref in ready)
-    ranges = spread(w_hbm.shape[0], skip, 2 * CHUNK)
-    copies = [
-        copies_in(w_hbm, rest, sems.at[i], start, size, start - skip)
-        for i, (start, size) in enumerate(ranges)
-    ]
-    for group in copies:
-        for copy in group:
-            copy.start()
+    ready = refs[pieces:-5]
+    mine_ref, theirs_ref, flat, left, sums = refs[-5:]
     slots = left.shape[0]
     heads = flat.shape[0] // slots
     at = 0
@@ -290,18 +300,14 @@
     at = 0
     for ref in ready:
         size = ref.shape[0]
-        term = jnp.dot(left[:, at : at + size], ref[...], preferred_element_type=jnp.float32)
-        total = term if total is None else total + term
+        for start, rows in spread(size, 0, 2 * CHUNK):
+            term = jnp.dot(
+                left[:, at + start : at + start + rows],
+                ref[start : start + rows, :],
+                preferred_element_type=jnp.float32,
+            )
+            total = term if total is None else total + term
         at += size
-    for (start, size), group in zip(ranges, copies):
-        for copy in group:
-            copy.wait()
-        term = jnp.dot(
-            left[:, start : start + size],
-            rest[start - skip : start - skip + size, :],
-            preferred_element_type=jnp.float32,
-        )
-        total = term if total is None else total + term
     sums[...] = total
     half = slots // 2
     turn = bit_reverse(lax.axis_index("gx"), bits)
@@ -312,31 +318,28 @@
             ref[t : t + 1, :] = sums[pl.ds(slot, 1), :]
 
 
-def output(parts, ready, w_out, slots):
+def output(parts, ready, slots):
     bits = slots.bit_length() - 1
-    depth, width = w_out.shape
+    depth, width = sum(x.shape[0] for x in ready), ready[0].shape[1]
     heads = depth // HEAD_SIZE
-    skip = sum(x.shape[0] for x in ready)
     whole = pl.BlockSpec(memory_space=pltpu.VMEM)
     piece = jax.ShapeDtypeStruct((slots // 2, width), jnp.float32)
     return pl.pallas_call(
-        functools.partial(output_kernel, bits, len(parts), len(ready)),
+        functools.partial(output_kernel, bits, len(parts)),
         out_shape=(piece, piece),
-        in_specs=[whole] * (len(parts) + len(ready)) + [pl.BlockSpec(memory_space=pltpu.HBM)],
+        in_specs=[whole] * (len(parts) + len(ready)),
         out_specs=(whole, whole),
         scratch_shapes=[
-            pltpu.VMEM((max(depth - skip, 16), width), jnp.bfloat16),
             pltpu.VMEM((slots * heads, HEAD_SIZE), jnp.float32),
             pltpu.VMEM((slots, depth), jnp.bfloat16),
             pltpu.VMEM((slots, width), jnp.float32),
-            pltpu.SemaphoreType.DMA((max(1, len(spread(depth, skip, 2 * CHUNK))), PIECES)),
         ],
         compiler_params=pltpu.CompilerParams(vmem_limit_bytes=24 * MIB),
         cost_estimate=pl.CostEstimate(
             flops=2 * slots * depth * width, bytes_accessed=2 * depth * width, transcendentals=0
         ),
         name="output",
-    )(*parts, *ready, in_hbm(w_out))
+    )(*parts, *ready)
 
 
 def swap(block, axis, devices, mask):
@@ -379,10 +382,12 @@
     (ready_two,) = stage((w_out,), ((few, most),))
     parts = [total[:1], swap(total[1:], "gx", devices, mask)]
     parts[1], ready_two = lax.optimization_barrier((parts[1], ready_two))
-    heads = attend(parts, turn, k_cache, value_cache, query_heads)
+    heads, ready_more = attend(
+        parts, turn, k_cache, value_cache, query_heads, w_out, (few + most, few)
+    )
 
     heads, w_out = lax.optimization_barrier((heads, w_out))
-    (ready_three,) = stage((w_out,), ((few + most, most),))
+    (ready_three,) = stage((w_out,), ((2 * few + most, most),))
     parts = [heads, swap(heads, "gx", devices, mask)]
     parts[1], ready_three = lax.optimization_barrier((parts[1], ready_three))
     while mask > FAN:
@@ -390,11 +395,11 @@
         parts.append(swap(jnp.concatenate(parts, axis=0), "gx", devices, mask))
     held = jnp.concatenate(parts, axis=0)
     held, w_out = lax.optimization_barrier((held, w_out))
-    (ready_four,) = stage((w_out,), ((few + 2 * most, most),))
+    (ready_four,) = stage((w_out,), ((2 * few + 2 * most, most),))
     parts += fan([held] * FAN, devices)
     parts[-1], ready_four = lax.optimization_barrier((parts[-1], ready_four))
-    ready = (ready_one, ready_two, ready_three, ready_four)
-    mine, theirs = output(parts, ready, w_out, slots)
+    ready = (ready_one, ready_two, ready_more, ready_three, ready_four)
+    mine, theirs = output(parts, ready, slots)
     return (mine + swap(theirs, "gy", 2, 1)).astype(jnp.bfloat16)
 
 

time: 38.2 us -> 38 us (level)
    pallas_call x1, Pallas kernels: 2.96 us -> 2.33 us  [output(): pl.pallas_call(functools.partial(output_kernel, bits, len(parts)), out_sh...]
    pallas_call x1, Pallas kernels: 1.16 us -> 1.56 us  [attend(): pl.pallas_call(functools.partial(attend_kernel, query_heads, kv_heads, le...]
where the time goes in v9:
time: 38 us; the launch traced here: 37.8 us
  Pallas kernels  19.5 us (51%)
  starting transfers between devices  13.4 us (35%)
  waiting for transfers between devices  2.81 us (7%)
  between operations  0.85 us (2%)
  other arithmetic  0.72 us (2%)
  local copies, waits for them, and re-layouts  0.46 us (1%)
    ppermute x10, starting transfers between devices, swap(): return lax.ppermute(block, axis, [(i, i ^ mask) for i in range(devices)])  13.4 us
    pallas_call x5, Pallas kernels, stage(): pl.pallas_call(kernel, out_shape=out_shape, in_specs=in_specs, out_specs=...  9.86 us
    pallas_call x1, Pallas kernels, project(): pl.pallas_call(functools.partial(project_kernel, bits), out_shape=(piece,...  5.73 us
    ppermute x10, waiting for transfers between devices, swap(): return lax.ppermute(block, axis, [(i, i ^ mask) for i in range(devices)])  2.81 us
    pallas_call x1, Pallas kernels, output(): pl.pallas_call(functools.partial(output_kernel, bits, len(parts)), out_sh...  2.33 us
    pallas_call x1, Pallas kernels, attend(): pl.pallas_call(functools.partial(attend_kernel, query_heads, kv_heads, le...  1.56 us
  transfers between devices with their start and end apart: 10, of which 3 were waited for; matrix products, arithmetic and copies ran while one was open for 0% of the time, Pallas kernels for 26%

profile of v9, /device:TPU:0, one launch (start us, length us, event | category | flops | bytes accessed | tf_op | source)
XLA Modules:
  0.0 37.8 jit_solution(2639754552814374257)
XLA Ops:
  0.0 0.5 %collective-permute-start = (bf16[4,2048]{1,0:T(4,128)(2,1)}, bf16[4,2048]{1,0:T(4,128)(2,1)S(1)}, u32[]{:S(2)}, u32[]{:S(2)}) collective-permute-start(bf16[4,2048]{1,0:T(4,128)(2,1)} %rows_ref.1), channel_id=1, source_target_pairs={{0,1},{1,0},{2,3},{3,2},{4,5},{5,4},{6,7},{7,6},{8,9},{9,8},{10,11... | collective-permute-start | bytes 49160 | tf_op jit(solution)/shard_map/ppermute | solution.py:346
  0.5 1.7 %stage.5.first = bf16[256,4096]{1,0:T(8,128)(2,1)S(1)} custom-call(bf16[2048,4096]{1,0:T(8,128)(2,1)} %wq_hbm.1), custom_call_target="tpu_custom_call" | custom-call | bytes 2097152 | tf_op jit(solution)/shard_map/stage/pallas_call | solution.py:99
  2.2 0.1 copy-done
  2.3 0.3 copy-done.1
  2.6 5.7 %project.1 = (f32[2,40,128]{2,1,0:T(8,128)S(1)}, f32[2,40,128]{2,1,0:T(8,128)S(1)}, f32[2,40,128]{2,1,0:T(8,128)S(1)}, f32[2,40,128]{2,1,0:T(8,128)S(1)}) custom-call(bf16[4,2048]{1,0:T(4,128)(2,1)S(1)} %copy-done.4, bf16[4,2048]{1,0:T(4,128)(2,1)S(1)} %collective-permute-done.other_ref, bf16[2048,4096]{1,0:T(8,128)(2,1)} %wq_hbm.1, ...), custom_call_target="tpu_custom_call" | custom-call | flops 150994944 | bytes 18874368 | tf_op jit(solution)/shard_map/project/pallas_call | solution.py:190
  8.4 3.6 %collective-permute-start.1 = (f32[2,40,128]{2,1,0:T(8,128)S(1)}, f32[2,40,128]{2,1,0:T(8,128)S(1)}, u32[]{:S(2)}, u32[]{:S(2)}) collective-permute-start(f32[2,40,128]{2,1,0:T(8,128)S(1)} %get-tuple-element.38), channel_id=1, source_target_pairs={{0,6},{2,4},{4,2},{6,0},{8,14},{10,12},{12,10},{14,8},{1,7},{3,5},... | collective-permute-start | bytes 122888 | tf_op jit(solution)/shard_map/ppermute | solution.py:346
  12.0 0.5 %collective-permute-start.2 = (f32[2,40,128]{2,1,0:T(8,128)S(1)}, f32[2,40,128]{2,1,0:T(8,128)S(1)}, u32[]{:S(2)}, u32[]{:S(2)}) collective-permute-start(f32[2,40,128]{2,1,0:T(8,128)S(1)} %get-tuple-element.39), channel_id=1, source_target_pairs={{0,2},{2,0},{4,6},{6,4},{8,10},{10,8},{12,14},{14,12},{1,3},{3,1},... | collective-permute-start | bytes 122888 | tf_op jit(solution)/shard_map/ppermute | solution.py:346
  12.5 0.1 collective-permute-start.3
  12.6 0.1 maximum_bitcast_fusion.frequency_ref
  13.3 1.6 %stage.6 = (f32[8,128]{1,0:T(8,128)S(1)}, bf16[512,2048]{1,0:T(8,128)(2,1)S(1)}) custom-call(s32[1]{0:T(128)S(6)} %copy.9.length_ref, f32[1,128]{1,0:T(1,128)S(1)} %maximum_bitcast_fusion.frequency_ref, bf16[4096,2048]{1,0:T(8,128)(2,1)} %refs_0_.5), custom_call_target="tpu_custom_call" | custom-call | bytes 2097152 | tf_op jit(solution)/shard_map/stage/pallas_call | solution.py:99
  14.9 1.1 %collective-permute-done.2 = f32[2,40,128]{2,1,0:T(8,128)S(1)} collective-permute-done((f32[2,40,128]{2,1,0:T(8,128)S(1)}, f32[2,40,128]{2,1,0:T(8,128)S(1)}, u32[]{:S(2)}, u32[]{:S(2)}) %collective-permute-start.2) | collective-permute-done | bytes 40992 | tf_op jit(solution)/shard_map/ppermute | solution.py:346
  16.0 0.5 %collective-permute-done.3 = f32[2,40,128]{2,1,0:T(8,128)S(1)} collective-permute-done((f32[2,40,128]{2,1,0:T(8,128)S(1)}, f32[2,40,128]{2,1,0:T(8,128)S(1)}, u32[]{:S(2)}, u32[]{:S(2)}) %collective-permute-start.3) | collective-permute-done | bytes 40992 | tf_op jit(solution)/shard_map/ppermute | solution.py:346
  16.5 2.7 %collective-permute-start.4 = (f32[1,40,128]{2,1,0:T(8,128)S(1)}, f32[1,40,128]{2,1,0:T(8,128)S(1)}, u32[]{:S(2)}, u32[]{:S(2)}) collective-permute-start(f32[1,40,128]{2,1,0:T(8,128)S(1)} %get-tuple-element.61), channel_id=1, source_target_pairs={{0,8},{2,10},{4,12},{6,14},{8,0},{10,2},{12,4},{14,6},{1,9},{3,11}... | collective-permute-start | bytes 61448 | tf_op jit(solution)/shard_map/ppermute | solution.py:346
  19.2 2.2 %stage.7.refs_6_ = bf16[1024,2048]{1,0:T(8,128)(2,1)S(1)} custom-call(bf16[4096,2048]{1,0:T(8,128)(2,1)} %refs_0_.5), custom_call_target="tpu_custom_call" | custom-call | bytes 4194304 | tf_op jit(solution)/shard_map/stage/pallas_call | solution.py:99
  21.4 1.6 %attend.1 = (bf16[1,32,128]{2,1,0:T(8,128)(2,1)S(1)}, bf16[512,2048]{1,0:T(8,128)(2,1)S(1)}) custom-call(bf16[4096,2048]{1,0:T(8,128)(2,1)} %refs_0_.5, f32[8,128]{1,0:T(8,128)S(1)} %get-tuple-element.44.turn_ref, bf16[1,2,2048,128]{3,2,1,0:T(8,128)(2,1)S(1)} %copy-done.2, bf16[1,2,2048,128]{3,2,1,0:T(8,128)(2,1)S(1)} %copy-done.3, ...), custom_call_target="tpu_custom_call" | custom-call | flops 33554432 | bytes 2097152 | tf_op jit(solution)/shard_map/attend/pallas_call | solution.py:265
  23.0 2.5 %collective-permute-start.5 = (bf16[1,32,128]{2,1,0:T(8,128)(2,1)S(1)}, bf16[1,32,128]{2,1,0:T(8,128)(2,1)S(1)}, u32[]{:S(2)}, u32[]{:S(2)}) collective-permute-start(bf16[1,32,128]{2,1,0:T(8,128)(2,1)S(1)} %get-tuple-element.48.refs_0_), channel_id=1, source_target_pairs={{0,8},{2,10},{4,12},{6,14},{8,0},{10,2},{12,4},{14,6},{1,9},{3,11}... | collective-permute-start | bytes 24584 | tf_op jit(solution)/shard_map/ppermute | solution.py:346
  25.5 2.2 %stage.8.refs_8_ = bf16[1024,2048]{1,0:T(8,128)(2,1)S(1)} custom-call(bf16[4096,2048]{1,0:T(8,128)(2,1)} %refs_0_.5), custom_call_target="tpu_custom_call" | custom-call | bytes 4194304 | tf_op jit(solution)/shard_map/stage/pallas_call | solution.py:99
  27.8 1.4 %collective-permute-start.8 = (bf16[2,32,128]{2,1,0:T(8,128)(2,1)S(1)}, bf16[2,32,128]{2,1,0:T(8,128)(2,1)S(1)}, u32[]{:S(2)}, u32[]{:S(2)}) collective-permute-start(bf16[2,32,128]{2,1,0:T(8,128)(2,1)S(1)} %pad_maximum_fusion), channel_id=1, source_target_pairs={{0,6},{2,4},{4,2},{6,0},{8,14},{10,12},{12,10},{14,8},{1,7},{3,5},... | collective-permute-start | bytes 49160 | tf_op jit(solution)/shard_map/ppermute | solution.py:346
  29.2 0.5 %collective-permute-start.7 = (bf16[2,32,128]{2,1,0:T(8,128)(2,1)S(1)}, bf16[2,32,128]{2,1,0:T(8,128)(2,1)S(1)}, u32[]{:S(2)}, u32[]{:S(2)}) collective-permute-start(bf16[2,32,128]{2,1,0:T(8,128)(2,1)S(1)} %pad_maximum_fusion), channel_id=1, source_target_pairs={{0,2},{2,0},{4,6},{6,4},{8,10},{10,8},{12,14},{14,12},{1,3},{3,1},... | collective-permute-start | bytes 49160 | tf_op jit(solution)/shard_map/ppermute | solution.py:346
  29.7 1.6 %collective-permute-start.6 = (bf16[2,32,128]{2,1,0:T(8,128)(2,1)S(1)}, bf16[2,32,128]{2,1,0:T(8,128)(2,1)S(1)}, u32[]{:S(2)}, u32[]{:S(2)}) collective-permute-start(bf16[2,32,128]{2,1,0:T(8,128)(2,1)S(1)} %pad_maximum_fusion), channel_id=1, source_target_pairs={{0,4},{2,6},{4,0},{6,2},{8,12},{10,14},{12,8},{14,10},{1,5},{3,7},... | collective-permute-start | bytes 49160 | tf_op jit(solution)/shard_map/ppermute | solution.py:346
  31.3 2.2 %stage.9.refs_9_ = bf16[1024,2048]{1,0:T(8,128)(2,1)S(1)} custom-call(bf16[4096,2048]{1,0:T(8,128)(2,1)} %refs_0_.5), custom_call_target="tpu_custom_call" | custom-call | bytes 4194304 | tf_op jit(solution)/shard_map/stage/pallas_call | solution.py:99
  33.6 2.3 %output.1 = (f32[4,2048]{1,0:T(4,128)S(1)}, f32[4,2048]{1,0:T(4,128)S(1)}) custom-call(bf16[1,32,128]{2,1,0:T(8,128)(2,1)S(1)} %get-tuple-element.48.refs_0_, bf16[1,32,128]{2,1,0:T(8,128)(2,1)S(1)} %collective-permute-done.5.refs_1_, bf16[2,32,128]{2,1,0:T(8,128)(2,1)S(1)} %collective-permute-done.6.refs_2_, ...), custom_call_target="tpu_custom_call" | custom-call | flops 134217728 | bytes 16777216 | tf_op jit(solution)/shard_map/output/pallas_call | solution.py:327
  36.0 1.2 %collective-permute-done.9 = f32[4,2048]{1,0:T(4,128)S(1)} collective-permute-done((f32[4,2048]{1,0:T(4,128)S(1)}, f32[4,2048]{1,0:T(4,128)S(1)}, u32[]{:S(2)}, u32[]{:S(2)}) %collective-permute-start.9) | collective-permute-done | bytes 32800 | tf_op jit(solution)/shard_map/ppermute | solution.py:346
  37.2 0.6 %add_convert_fusion = bf16[4,2048]{1,0:T(4,128)(2,1)} fusion(f32[4,2048]{1,0:T(4,128)S(1)} %get-tuple-element.59, f32[4,2048]{1,0:T(4,128)S(1)} %collective-permute-done.9), kind=kLoop, calls=%fused_computation.1 | loop fusion | flops 16384 | bytes 81920 | tf_op jit(solution)/shard_map/convert_element_type | solution.py:403
  (20 shorter events, 0.1 us)
Async XLA Ops:
  0.0 2.2 %collective-permute-start = (bf16[4,2048]{1,0:T(4,128)(2,1)}, bf16[4,2048]{1,0:T(4,128)(2,1)S(1)}, u32[]{:S(2)}, u32[]{:S(2)}) collective-permute-start(bf16[4,2048]{1,0:T(4,128)(2,1)} %rows_ref.1), channel_id=1, source_target_pairs={{0,1},{1,0},{2,3},{3,2},{4,5},{5,4},{6,7},{7,6},{8,9},{9,8},{10,11... | collective-permute-start | bytes 49160 | tf_op jit(solution)/shard_map/ppermute | solution.py:346
  0.5 1.9 %copy-start = (bf16[2048,256]{1,0:T(8,128)(2,1)S(1)}, bf16[2048,256]{1,0:T(8,128)(2,1)}, u32[]{:S(2)}) copy-start(bf16[2048,256]{1,0:T(8,128)(2,1)} %wk.1) | copy-start | bytes 3145732
  0.5 2.2 %copy-start.1 = (bf16[2048,256]{1,0:T(8,128)(2,1)S(1)}, bf16[2048,256]{1,0:T(8,128)(2,1)}, u32[]{:S(2)}) copy-start(bf16[2048,256]{1,0:T(8,128)(2,1)} %wv.1) | copy-start | bytes 3145732
  0.5 2.2 %copy-start.4 = (bf16[4,2048]{1,0:T(4,128)(2,1)S(1)}, bf16[4,2048]{1,0:T(4,128)(2,1)}, u32[]{:S(2)}) copy-start(bf16[4,2048]{1,0:T(4,128)(2,1)} %rows_ref.1) | copy-start | bytes 49156
  8.4 6.5 %collective-permute-start.1 = (f32[2,40,128]{2,1,0:T(8,128)S(1)}, f32[2,40,128]{2,1,0:T(8,128)S(1)}, u32[]{:S(2)}, u32[]{:S(2)}) collective-permute-start(f32[2,40,128]{2,1,0:T(8,128)S(1)} %get-tuple-element.38), channel_id=1, source_target_pairs={{0,6},{2,4},{4,2},{6,0},{8,14},{10,12},{12,10},{14,8},{1,7},{3,5},... | collective-permute-start | bytes 122888 | tf_op jit(solution)/shard_map/ppermute | solution.py:346
  12.0 4.0 %collective-permute-start.2 = (f32[2,40,128]{2,1,0:T(8,128)S(1)}, f32[2,40,128]{2,1,0:T(8,128)S(1)}, u32[]{:S(2)}, u32[]{:S(2)}) collective-permute-start(f32[2,40,128]{2,1,0:T(8,128)S(1)} %get-tuple-element.39), channel_id=1, source_target_pairs={{0,2},{2,0},{4,6},{6,4},{8,10},{10,8},{12,14},{14,12},{1,3},{3,1},... | collective-permute-start | bytes 122888 | tf_op jit(solution)/shard_map/ppermute | solution.py:346
  12.5 4.0 %collective-permute-start.3 = (f32[2,40,128]{2,1,0:T(8,128)S(1)}, f32[2,40,128]{2,1,0:T(8,128)S(1)}, u32[]{:S(2)}, u32[]{:S(2)}) collective-permute-start(f32[2,40,128]{2,1,0:T(8,128)S(1)} %get-tuple-element.40), channel_id=1, source_target_pairs={{0,4},{2,6},{4,0},{6,2},{8,12},{10,14},{12,8},{14,10},{1,5},{3,7},... | collective-permute-start | bytes 122888 | tf_op jit(solution)/shard_map/ppermute | solution.py:346
  16.5 4.9 %copy-start.2 = (bf16[1,2,2048,128]{3,2,1,0:T(8,128)(2,1)S(1)}, bf16[1,2,2048,128]{3,2,1,0:T(8,128)(2,1)}, u32[]{:S(2)}) copy-start(bf16[1,2,2048,128]{3,2,1,0:T(8,128)(2,1)} %k_ref.1) | copy-start | bytes 3145732
  16.5 4.9 %copy-start.3 = (bf16[1,2,2048,128]{3,2,1,0:T(8,128)(2,1)S(1)}, bf16[1,2,2048,128]{3,2,1,0:T(8,128)(2,1)}, u32[]{:S(2)}) copy-start(bf16[1,2,2048,128]{3,2,1,0:T(8,128)(2,1)} %v_ref.1) | copy-start | bytes 3145732
  16.5 4.9 %collective-permute-start.4 = (f32[1,40,128]{2,1,0:T(8,128)S(1)}, f32[1,40,128]{2,1,0:T(8,128)S(1)}, u32[]{:S(2)}, u32[]{:S(2)}) collective-permute-start(f32[1,40,128]{2,1,0:T(8,128)S(1)} %get-tuple-element.61), channel_id=1, source_target_pairs={{0,8},{2,10},{4,12},{6,14},{8,0},{10,2},{12,4},{14,6},{1,9},{3,11}... | collective-permute-start | bytes 61448 | tf_op jit(solution)/shard_map/ppermute | solution.py:346
  23.0 4.7 %collective-permute-start.5 = (bf16[1,32,128]{2,1,0:T(8,128)(2,1)S(1)}, bf16[1,32,128]{2,1,0:T(8,128)(2,1)S(1)}, u32[]{:S(2)}, u32[]{:S(2)}) collective-permute-start(bf16[1,32,128]{2,1,0:T(8,128)(2,1)S(1)} %get-tuple-element.48.refs_0_), channel_id=1, source_target_pairs={{0,8},{2,10},{4,12},{6,14},{8,0},{10,2},{12,4},{14,6},{1,9},{3,11}... | collective-permute-start | bytes 24584 | tf_op jit(solution)/shard_map/ppermute | solution.py:346
  27.8 5.8 %collective-permute-start.8 = (bf16[2,32,128]{2,1,0:T(8,128)(2,1)S(1)}, bf16[2,32,128]{2,1,0:T(8,128)(2,1)S(1)}, u32[]{:S(2)}, u32[]{:S(2)}) collective-permute-start(bf16[2,32,128]{2,1,0:T(8,128)(2,1)S(1)} %pad_maximum_fusion), channel_id=1, source_target_pairs={{0,6},{2,4},{4,2},{6,0},{8,14},{10,12},{12,10},{14,8},{1,7},{3,5},... | collective-permute-start | bytes 49160 | tf_op jit(solution)/shard_map/ppermute | solution.py:346
  29.2 4.3 %collective-permute-start.7 = (bf16[2,32,128]{2,1,0:T(8,128)(2,1)S(1)}, bf16[2,32,128]{2,1,0:T(8,128)(2,1)S(1)}, u32[]{:S(2)}, u32[]{:S(2)}) collective-permute-start(bf16[2,32,128]{2,1,0:T(8,128)(2,1)S(1)} %pad_maximum_fusion), channel_id=1, source_target_pairs={{0,2},{2,0},{4,6},{6,4},{8,10},{10,8},{12,14},{14,12},{1,3},{3,1},... | collective-permute-start | bytes 49160 | tf_op jit(solution)/shard_map/ppermute | solution.py:346
  29.7 3.8 %collective-permute-start.6 = (bf16[2,32,128]{2,1,0:T(8,128)(2,1)S(1)}, bf16[2,32,128]{2,1,0:T(8,128)(2,1)S(1)}, u32[]{:S(2)}, u32[]{:S(2)}) collective-permute-start(bf16[2,32,128]{2,1,0:T(8,128)(2,1)S(1)} %pad_maximum_fusion), channel_id=1, source_target_pairs={{0,4},{2,6},{4,0},{6,2},{8,12},{10,14},{12,8},{14,10},{1,5},{3,7},... | collective-permute-start | bytes 49160 | tf_op jit(solution)/shard_map/ppermute | solution.py:346
  35.9 1.3 %collective-permute-start.9 = (f32[4,2048]{1,0:T(4,128)S(1)}, f32[4,2048]{1,0:T(4,128)S(1)}, u32[]{:S(2)}, u32[]{:S(2)}) collective-permute-start(f32[4,2048]{1,0:T(4,128)S(1)} %get-tuple-element.60), channel_id=1, source_target_pairs={{0,1},{1,0},{2,3},{3,2},{4,5},{5,4},{6,7},{7,6},{8,9},{9,8},{10,11... | collective-permute-start | bytes 98312 | tf_op jit(solution)/shard_map/ppermute | solution.py:346

commit v10 on v7

--- a/solution.py
+++ b/solution.py
@@ -111,11 +111,19 @@
 
 
 def spread(depth, skip, chunk):
-    ranges = [(at, min(chunk, depth - at)) for at in range(skip, depth, chunk)]
-    if ranges and ranges[-1][1] >= 2 * LANES:
-        start, size = ranges.pop()
-        ranges += [(start, size - LANES), (start + size - LANES, LANES)]
-    return ranges
+    return [(at, min(chunk, depth - at)) for at in range(skip, depth, chunk)]
+
+
+def tapered(ranges):
+    *most, (start, size) = ranges
+    if size < 2 * LANES:
+        return ranges
+    return most + [(start, size - LANES), (start + size - LANES, LANES)]
+
+
+def feed(depth, skip):
+    ranges = spread(depth, skip, CHUNK)
+    return tapered(ranges) if ranges else ranges
 
 
 def project_kernel(
@@ -123,7 +131,7 @@
 ):
     pieces, (wq, rows, sems) = refs[:FAN], refs[FAN:]
     skip = first.shape[0]
-    ranges = spread(wq_hbm.shape[0], skip, CHUNK)
+    ranges = feed(wq_hbm.shape[0], skip)
     copies = [
         copies_in(wq_hbm, wq, sems.at[i], start, size, start - skip)
         for i, (start, size) in enumerate(ranges)
@@ -187,7 +195,7 @@
         scratch_shapes=[
             pltpu.VMEM((max(depth - skip, 16), query_width), jnp.bfloat16),
             pltpu.VMEM((slots, depth), jnp.float32),
-            pltpu.SemaphoreType.DMA((max(1, len(spread(depth, skip, CHUNK))), PIECES)),
+            pltpu.SemaphoreType.DMA((max(1, len(feed(depth, skip))), PIECES)),
         ],
         compiler_params=pltpu.CompilerParams(vmem_limit_bytes=32 * MIB),
         cost_estimate=pl.CostEstimate(
@@ -199,9 +207,7 @@
     )(rows, other, in_hbm(w_query), first, key_weight, value_weight)
 
 
-def attend_kernel(
-    query_heads, kv_heads, pieces, turn_ref, k_ref, v_ref, *refs
-):
+def attend_kernel(query_heads, kv_heads, pieces, turn_ref, k_ref, v_ref, *refs):
     heads_ref = refs[pieces]
     total = refs[0][0]
     for ref in refs[1:pieces]:
@@ -216,19 +222,38 @@
     group = query_heads // kv_heads
     factor = 1.0 / math.sqrt(HEAD_SIZE)
     length = turn_ref[2:3, 0:1].astype(jnp.int32)
-    for head in range(kv_heads):
-        queries = turned[head * group : (head + 1) * group]
-        fresh_key = turned[query_heads + head : query_heads + head + 1].astype(jnp.float32)
-        own = jnp.sum(queries.astype(jnp.float32) * fresh_key, axis=1, keepdims=True) * factor
+    side = 2 if kv_heads % 2 == 0 else 1
+    for first in range(0, kv_heads, side):
+        members = range(first, first + side)
+        queries = [turned[head * group : (head + 1) * group] for head in members]
+        empty = jnp.zeros((group, HEAD_SIZE), jnp.bfloat16)
+        spread_out = jnp.concatenate(
+            [
+                jnp.concatenate([q if i == j else empty for j in range(side)], axis=1)
+                for i, q in enumerate(queries)
+            ],
+            axis=0,
+        )
+        keys = jnp.concatenate([k_ref[0, head] for head in members], axis=1)
+        values = jnp.concatenate([v_ref[0, head] for head in members], axis=1)
         scores = (
             lax.dot_general(
-                queries,
-                k_ref[0, head],
-                (((1,), (1,)), ((), ())),
-                preferred_element_type=jnp.float32,
+                spread_out, keys, (((1,), (1,)), ((), ())), preferred_element_type=jnp.float32
             )
             * factor
         )
+        own = jnp.concatenate(
+            [
+                jnp.sum(
+                    q.astype(jnp.float32)
+                    * turned[query_heads + head : query_heads + head + 1].astype(jnp.float32),
+                    axis=1,
+                    keepdims=True,
+                )
+                for q, head in zip(queries, members)
+            ],
+            axis=0,
+        ) * factor
         slot = lax.broadcasted_iota(jnp.int32, scores.shape, 1)
         scores = jnp.where(slot < length, scores, -jnp.inf)
         top = jnp.maximum(jnp.max(scores, axis=1, keepdims=True), own)
@@ -236,12 +261,14 @@
         own_exp = jnp.exp(own - top)
         share = 1.0 / (jnp.sum(exponent, axis=1, keepdims=True) + own_exp)
         weights = (exponent * share).astype(jnp.bfloat16)
-        own_weight = (own_exp * share).astype(jnp.bfloat16)
-        mixed = jnp.dot(weights, v_ref[0, head], preferred_element_type=jnp.float32)
-        mixed = mixed + own_weight.astype(jnp.float32) * fresh_values[head : head + 1].astype(
-            jnp.float32
-        )
-        heads_ref[0, pl.ds(head * group, group), :] = mixed.astype(jnp.bfloat16)
+        own_weight = (own_exp * share).astype(jnp.bfloat16).astype(jnp.float32)
+        mixed = jnp.dot(weights, values, preferred_element_type=jnp.float32)
+        for i, head in enumerate(members):
+            block = mixed[i * group : (i + 1) * group, i * HEAD_SIZE : (i + 1) * HEAD_SIZE]
+            block = block + own_weight[i * group : (i + 1) * group] * fresh_values[
+                head : head + 1
+            ].astype(jnp.float32)
+            heads_ref[0, pl.ds(head * group, group), :] = block.astype(jnp.bfloat16)
 
 
 def attend(parts, turn, k_cache, value_cache, query_heads):
@@ -262,19 +289,14 @@
     )(turn, k_cache, value_cache, *parts)
 
 
-def output_kernel(bits, pieces, staged, *refs):
+def output_kernel(bits, pieces, *refs):
     parts = refs[:pieces]
-    ready = refs[pieces : pieces + staged]
-    w_hbm, mine_ref, theirs_ref, rest, flat, left, sums, sems = refs[pieces + staged :]
-    skip = sum(ref.shape[0] for ref in ready)
-    ranges = spread(w_hbm.shape[0], skip, 2 * CHUNK)
-    copies = [
-        copies_in(w_hbm, rest, sems.at[i], start, size, start - skip)
-        for i, (start, size) in enumerate(ranges)
-    ]
-    for group in copies:
-        for copy in group:
-            copy.start()
+    ready = refs[pieces:-8]
+    w_hbm, mine_ref, theirs_ref, rest, flat, left, sums, sems = refs[-8:]
+    skip = w_hbm.shape[0] - rest.shape[0]
+    copies = copies_in(w_hbm, rest, sems, skip, rest.shape[0], 0)
+    for copy in copies:
+        copy.start()
     slots = left.shape[0]
     heads = flat.shape[0] // slots
     at = 0
@@ -288,20 +310,19 @@
         ].astype(jnp.bfloat16)
     total = None
     at = 0
-    for ref in ready:
+    for ref in (*ready, rest):
+        if ref is rest:
+            for copy in copies:
+                copy.wait()
         size = ref.shape[0]
-        term = jnp.dot(left[:, at : at + size], ref[...], preferred_element_type=jnp.float32)
-        total = term if total is None else total + term
+        for start, rows in spread(size, 0, 2 * CHUNK):
+            term = jnp.dot(
+                left[:, at + start : at + start + rows],
+                ref[start : start + rows, :],
+                preferred_element_type=jnp.float32,
+            )
+            total = term if total is None else total + term
         at += size
-    for (start, size), group in zip(ranges, copies):
-        for copy in group:
-            copy.wait()
-        term = jnp.dot(
-            left[:, start : start + size],
-            rest[start - skip : start - skip + size, :],
-            preferred_element_type=jnp.float32,
-        )
-        total = term if total is None else total + term
     sums[...] = total
     half = slots // 2
     turn = bit_reverse(lax.axis_index("gx"), bits)
@@ -316,20 +337,20 @@
     bits = slots.bit_length() - 1
     depth, width = w_out.shape
     heads = depth // HEAD_SIZE
-    skip = sum(x.shape[0] for x in ready)
+    rest = depth - sum(x.shape[0] for x in ready)
     whole = pl.BlockSpec(memory_space=pltpu.VMEM)
     piece = jax.ShapeDtypeStruct((slots // 2, width), jnp.float32)
     return pl.pallas_call(
-        functools.partial(output_kernel, bits, len(parts), len(ready)),
+        functools.partial(output_kernel, bits, len(parts)),
         out_shape=(piece, piece),
         in_specs=[whole] * (len(parts) + len(ready)) + [pl.BlockSpec(memory_space=pltpu.HBM)],
         out_specs=(whole, whole),
         scratch_shapes=[
-            pltpu.VMEM((max(depth - skip, 16), width), jnp.bfloat16),
+            pltpu.VMEM((rest, width), jnp.bfloat16),
             pltpu.VMEM((slots * heads, HEAD_SIZE), jnp.float32),
             pltpu.VMEM((slots, depth), jnp.bfloat16),
             pltpu.VMEM((slots, width), jnp.float32),
-            pltpu.SemaphoreType.DMA((max(1, len(spread(depth, skip, 2 * CHUNK))), PIECES)),
+            pltpu.SemaphoreType.DMA((PIECES,)),
         ],
         compiler_params=pltpu.CompilerParams(vmem_limit_bytes=24 * MIB),
         cost_estimate=pl.CostEstimate(

time: 38.2 us -> 38.6 us (1.010)
  Pallas kernels: 19.7 us -> 20.1 us
    pallas_call x1, Pallas kernels: 2.96 us -> 3.55 us  [output(): pl.pallas_call(functools.partial(output_kernel, bits, len(parts)), out_sh...]
where the time goes in v10:
time: 38.6 us; the launch traced here: 38.4 us
  Pallas kernels  20.1 us (52%)
  starting transfers between devices  13.4 us (35%)
  waiting for transfers between devices  2.81 us (7%)
  between operations  0.84 us (2%)
  other arithmetic  0.72 us (2%)
  local copies, waits for them, and re-layouts  0.46 us (1%)
    ppermute x10, starting transfers between devices, swap(): return lax.ppermute(block, axis, [(i, i ^ mask) for i in range(devices)])  13.4 us
    pallas_call x5, Pallas kernels, stage(): pl.pallas_call(kernel, out_shape=out_shape, in_specs=in_specs, out_specs=...  9.86 us
    pallas_call x1, Pallas kernels, project(): pl.pallas_call(functools.partial(project_kernel, bits), out_shape=(piece,...  5.73 us
    pallas_call x1, Pallas kernels, output(): pl.pallas_call(functools.partial(output_kernel, bits, len(parts)), out_sh...  3.55 us
    ppermute x10, waiting for transfers between devices, swap(): return lax.ppermute(block, axis, [(i, i ^ mask) for i in range(devices)])  2.81 us
    pallas_call x1, Pallas kernels, attend(): pl.pallas_call(functools.partial(attend_kernel, query_heads, kv_heads, le...  0.97 us
  transfers between devices with their start and end apart: 10, of which 3 were waited for; matrix products, arithmetic and copies ran while one was open for 0% of the time, Pallas kernels for 26%

profile of v10, /device:TPU:0, one launch (start us, length us, event | category | flops | bytes accessed | tf_op | source)
XLA Modules:
  0.0 38.4 jit_solution(13056750072176389933)
XLA Ops:
  0.0 0.5 %collective-permute-start = (bf16[4,2048]{1,0:T(4,128)(2,1)}, bf16[4,2048]{1,0:T(4,128)(2,1)S(1)}, u32[]{:S(2)}, u32[]{:S(2)}) collective-permute-start(bf16[4,2048]{1,0:T(4,128)(2,1)} %rows_ref.1), channel_id=1, source_target_pairs={{0,1},{1,0},{2,3},{3,2},{4,5},{5,4},{6,7},{7,6},{8,9},{9,8},{10,11... | collective-permute-start | bytes 49160 | tf_op jit(solution)/shard_map/ppermute | solution.py:364
  0.5 1.7 %stage.5.first = bf16[256,4096]{1,0:T(8,128)(2,1)S(1)} custom-call(bf16[2048,4096]{1,0:T(8,128)(2,1)} %wq_hbm.1), custom_call_target="tpu_custom_call" | custom-call | bytes 2097152 | tf_op jit(solution)/shard_map/stage/pallas_call | solution.py:99
  2.2 0.1 copy-done
  2.3 0.3 copy-done.1
  2.6 5.7 %project.1 = (f32[2,40,128]{2,1,0:T(8,128)S(1)}, f32[2,40,128]{2,1,0:T(8,128)S(1)}, f32[2,40,128]{2,1,0:T(8,128)S(1)}, f32[2,40,128]{2,1,0:T(8,128)S(1)}) custom-call(bf16[4,2048]{1,0:T(4,128)(2,1)S(1)} %copy-done.4, bf16[4,2048]{1,0:T(4,128)(2,1)S(1)} %collective-permute-done.other_ref, bf16[2048,4096]{1,0:T(8,128)(2,1)} %wq_hbm.1, ...), custom_call_target="tpu_custom_call" | custom-call | flops 150994944 | bytes 18874368 | tf_op jit(solution)/shard_map/project/pallas_call | solution.py:190
  8.4 3.6 %collective-permute-start.1 = (f32[2,40,128]{2,1,0:T(8,128)S(1)}, f32[2,40,128]{2,1,0:T(8,128)S(1)}, u32[]{:S(2)}, u32[]{:S(2)}) collective-permute-start(f32[2,40,128]{2,1,0:T(8,128)S(1)} %get-tuple-element.38), channel_id=1, source_target_pairs={{0,6},{2,4},{4,2},{6,0},{8,14},{10,12},{12,10},{14,8},{1,7},{3,5},... | collective-permute-start | bytes 122888 | tf_op jit(solution)/shard_map/ppermute | solution.py:364
  12.0 0.5 %collective-permute-start.2 = (f32[2,40,128]{2,1,0:T(8,128)S(1)}, f32[2,40,128]{2,1,0:T(8,128)S(1)}, u32[]{:S(2)}, u32[]{:S(2)}) collective-permute-start(f32[2,40,128]{2,1,0:T(8,128)S(1)} %get-tuple-element.39), channel_id=1, source_target_pairs={{0,2},{2,0},{4,6},{6,4},{8,10},{10,8},{12,14},{14,12},{1,3},{3,1},... | collective-permute-start | bytes 122888 | tf_op jit(solution)/shard_map/ppermute | solution.py:364
  12.5 0.1 collective-permute-start.3
  12.6 0.1 maximum_bitcast_fusion.frequency_ref
  13.3 1.6 %stage.6 = (f32[8,128]{1,0:T(8,128)S(1)}, bf16[512,2048]{1,0:T(8,128)(2,1)S(1)}) custom-call(s32[1]{0:T(128)S(6)} %copy.9.length_ref, f32[1,128]{1,0:T(1,128)S(1)} %maximum_bitcast_fusion.frequency_ref, bf16[4096,2048]{1,0:T(8,128)(2,1)} %refs_9_), custom_call_target="tpu_custom_call" | custom-call | bytes 2097152 | tf_op jit(solution)/shard_map/stage/pallas_call | solution.py:99
  14.9 1.1 %collective-permute-done.2 = f32[2,40,128]{2,1,0:T(8,128)S(1)} collective-permute-done((f32[2,40,128]{2,1,0:T(8,128)S(1)}, f32[2,40,128]{2,1,0:T(8,128)S(1)}, u32[]{:S(2)}, u32[]{:S(2)}) %collective-permute-start.2) | collective-permute-done | bytes 40992 | tf_op jit(solution)/shard_map/ppermute | solution.py:364
  16.0 0.5 %collective-permute-done.3 = f32[2,40,128]{2,1,0:T(8,128)S(1)} collective-permute-done((f32[2,40,128]{2,1,0:T(8,128)S(1)}, f32[2,40,128]{2,1,0:T(8,128)S(1)}, u32[]{:S(2)}, u32[]{:S(2)}) %collective-permute-start.3) | collective-permute-done | bytes 40992 | tf_op jit(solution)/shard_map/ppermute | solution.py:364
  16.5 2.7 %collective-permute-start.4 = (f32[1,40,128]{2,1,0:T(8,128)S(1)}, f32[1,40,128]{2,1,0:T(8,128)S(1)}, u32[]{:S(2)}, u32[]{:S(2)}) collective-permute-start(f32[1,40,128]{2,1,0:T(8,128)S(1)} %get-tuple-element.57), channel_id=1, source_target_pairs={{0,8},{2,10},{4,12},{6,14},{8,0},{10,2},{12,4},{14,6},{1,9},{3,11}... | collective-permute-start | bytes 61448 | tf_op jit(solution)/shard_map/ppermute | solution.py:364
  19.2 2.2 %stage.7.refs_6_ = bf16[1024,2048]{1,0:T(8,128)(2,1)S(1)} custom-call(bf16[4096,2048]{1,0:T(8,128)(2,1)} %refs_9_), custom_call_target="tpu_custom_call" | custom-call | bytes 4194304 | tf_op jit(solution)/shard_map/stage/pallas_call | solution.py:99
  21.4 1.0 %attend.1.refs_0_ = bf16[1,32,128]{2,1,0:T(8,128)(2,1)S(1)} custom-call(f32[8,128]{1,0:T(8,128)S(1)} %get-tuple-element.36.turn_ref, bf16[1,2,2048,128]{3,2,1,0:T(8,128)(2,1)S(1)} %copy-done.2, bf16[1,2,2048,128]{3,2,1,0:T(8,128)(2,1)S(1)} %copy-done.3, f32[1,40,128]{2,1,0:T(8,128)S(1)} %get-tuple-element.58.refs_0_, ...), custom_call_target="tpu_custom_call" | custom-call | flops 33554432 | bytes 2097152 | tf_op jit(solution)/shard_map/attend/pallas_call | solution.py:277
  22.4 2.5 %collective-permute-start.5 = (bf16[1,32,128]{2,1,0:T(8,128)(2,1)S(1)}, bf16[1,32,128]{2,1,0:T(8,128)(2,1)S(1)}, u32[]{:S(2)}, u32[]{:S(2)}) collective-permute-start(bf16[1,32,128]{2,1,0:T(8,128)(2,1)S(1)} %attend.1.refs_0_), channel_id=1, source_target_pairs={{0,8},{2,10},{4,12},{6,14},{8,0},{10,2},{12,4},{14,6},{1,9},{3,11}... | collective-permute-start | bytes 24584 | tf_op jit(solution)/shard_map/ppermute | solution.py:364
  24.9 2.2 %stage.8.refs_7_ = bf16[1024,2048]{1,0:T(8,128)(2,1)S(1)} custom-call(bf16[4096,2048]{1,0:T(8,128)(2,1)} %refs_9_), custom_call_target="tpu_custom_call" | custom-call | bytes 4194304 | tf_op jit(solution)/shard_map/stage/pallas_call | solution.py:99
  27.1 1.4 %collective-permute-start.8 = (bf16[2,32,128]{2,1,0:T(8,128)(2,1)S(1)}, bf16[2,32,128]{2,1,0:T(8,128)(2,1)S(1)}, u32[]{:S(2)}, u32[]{:S(2)}) collective-permute-start(bf16[2,32,128]{2,1,0:T(8,128)(2,1)S(1)} %pad_maximum_fusion), channel_id=1, source_target_pairs={{0,6},{2,4},{4,2},{6,0},{8,14},{10,12},{12,10},{14,8},{1,7},{3,5},... | collective-permute-start | bytes 49160 | tf_op jit(solution)/shard_map/ppermute | solution.py:364
  28.6 0.5 %collective-permute-start.7 = (bf16[2,32,128]{2,1,0:T(8,128)(2,1)S(1)}, bf16[2,32,128]{2,1,0:T(8,128)(2,1)S(1)}, u32[]{:S(2)}, u32[]{:S(2)}) collective-permute-start(bf16[2,32,128]{2,1,0:T(8,128)(2,1)S(1)} %pad_maximum_fusion), channel_id=1, source_target_pairs={{0,2},{2,0},{4,6},{6,4},{8,10},{10,8},{12,14},{14,12},{1,3},{3,1},... | collective-permute-start | bytes 49160 | tf_op jit(solution)/shard_map/ppermute | solution.py:364
  29.1 1.6 %collective-permute-start.6 = (bf16[2,32,128]{2,1,0:T(8,128)(2,1)S(1)}, bf16[2,32,128]{2,1,0:T(8,128)(2,1)S(1)}, u32[]{:S(2)}, u32[]{:S(2)}) collective-permute-start(bf16[2,32,128]{2,1,0:T(8,128)(2,1)S(1)} %pad_maximum_fusion), channel_id=1, source_target_pairs={{0,4},{2,6},{4,0},{6,2},{8,12},{10,14},{12,8},{14,10},{1,5},{3,7},... | collective-permute-start | bytes 49160 | tf_op jit(solution)/shard_map/ppermute | solution.py:364
  30.7 2.2 %stage.9.refs_8_ = bf16[1024,2048]{1,0:T(8,128)(2,1)S(1)} custom-call(bf16[4096,2048]{1,0:T(8,128)(2,1)} %refs_9_), custom_call_target="tpu_custom_call" | custom-call | bytes 4194304 | tf_op jit(solution)/shard_map/stage/pallas_call | solution.py:99
  32.9 3.6 %output.1 = (f32[4,2048]{1,0:T(4,128)S(1)}, f32[4,2048]{1,0:T(4,128)S(1)}) custom-call(bf16[1,32,128]{2,1,0:T(8,128)(2,1)S(1)} %attend.1.refs_0_, bf16[1,32,128]{2,1,0:T(8,128)(2,1)S(1)} %collective-permute-done.5.refs_1_, bf16[2,32,128]{2,1,0:T(8,128)(2,1)S(1)} %collective-permute-done.6.refs_2_, bf16[2,32,128]{2,1,0:T(8,128)(2,1)S(1)} %collective-permute-done.7.refs_3_, ...), custom_call_target="tpu_custom_call" | custom-call | flops 134217728 | bytes 16777216 | tf_op jit(solution)/shard_map/output/pallas_call | solution.py:343
  36.6 1.2 %collective-permute-done.9 = f32[4,2048]{1,0:T(4,128)S(1)} collective-permute-done((f32[4,2048]{1,0:T(4,128)S(1)}, f32[4,2048]{1,0:T(4,128)S(1)}, u32[]{:S(2)}, u32[]{:S(2)}) %collective-permute-start.9) | collective-permute-done | bytes 32800 | tf_op jit(solution)/shard_map/ppermute | solution.py:364
  37.8 0.6 %add_convert_fusion = bf16[4,2048]{1,0:T(4,128)(2,1)} fusion(f32[4,2048]{1,0:T(4,128)S(1)} %get-tuple-element.55, f32[4,2048]{1,0:T(4,128)S(1)} %collective-permute-done.9), kind=kLoop, calls=%fused_computation.1 | loop fusion | flops 16384 | bytes 81920 | tf_op jit(solution)/shard_map/convert_element_type | solution.py:419
  (20 shorter events, 0.1 us)
Async XLA Ops:
  0.0 2.2 %collective-permute-start = (bf16[4,2048]{1,0:T(4,128)(2,1)}, bf16[4,2048]{1,0:T(4,128)(2,1)S(1)}, u32[]{:S(2)}, u32[]{:S(2)}) collective-permute-start(bf16[4,2048]{1,0:T(4,128)(2,1)} %rows_ref.1), channel_id=1, source_target_pairs={{0,1},{1,0},{2,3},{3,2},{4,5},{5,4},{6,7},{7,6},{8,9},{9,8},{10,11... | collective-permute-start | bytes 49160 | tf_op jit(solution)/shard_map/ppermute | solution.py:364
  0.5 1.9 %copy-start = (bf16[2048,256]{1,0:T(8,128)(2,1)S(1)}, bf16[2048,256]{1,0:T(8,128)(2,1)}, u32[]{:S(2)}) copy-start(bf16[2048,256]{1,0:T(8,128)(2,1)} %wk.1) | copy-start | bytes 3145732
  0.5 2.2 %copy-start.1 = (bf16[2048,256]{1,0:T(8,128)(2,1)S(1)}, bf16[2048,256]{1,0:T(8,128)(2,1)}, u32[]{:S(2)}) copy-start(bf16[2048,256]{1,0:T(8,128)(2,1)} %wv.1) | copy-start | bytes 3145732
  0.5 2.2 %copy-start.4 = (bf16[4,2048]{1,0:T(4,128)(2,1)S(1)}, bf16[4,2048]{1,0:T(4,128)(2,1)}, u32[]{:S(2)}) copy-start(bf16[4,2048]{1,0:T(4,128)(2,1)} %rows_ref.1) | copy-start | bytes 49156
  8.4 6.5 %collective-permute-start.1 = (f32[2,40,128]{2,1,0:T(8,128)S(1)}, f32[2,40,128]{2,1,0:T(8,128)S(1)}, u32[]{:S(2)}, u32[]{:S(2)}) collective-permute-start(f32[2,40,128]{2,1,0:T(8,128)S(1)} %get-tuple-element.38), channel_id=1, source_target_pairs={{0,6},{2,4},{4,2},{6,0},{8,14},{10,12},{12,10},{14,8},{1,7},{3,5},... | collective-permute-start | bytes 122888 | tf_op jit(solution)/shard_map/ppermute | solution.py:364
  12.0 4.0 %collective-permute-start.2 = (f32[2,40,128]{2,1,0:T(8,128)S(1)}, f32[2,40,128]{2,1,0:T(8,128)S(1)}, u32[]{:S(2)}, u32[]{:S(2)}) collective-permute-start(f32[2,40,128]{2,1,0:T(8,128)S(1)} %get-tuple-element.39), channel_id=1, source_target_pairs={{0,2},{2,0},{4,6},{6,4},{8,10},{10,8},{12,14},{14,12},{1,3},{3,1},... | collective-permute-start | bytes 122888 | tf_op jit(solution)/shard_map/ppermute | solution.py:364
  12.5 4.0 %collective-permute-start.3 = (f32[2,40,128]{2,1,0:T(8,128)S(1)}, f32[2,40,128]{2,1,0:T(8,128)S(1)}, u32[]{:S(2)}, u32[]{:S(2)}) collective-permute-start(f32[2,40,128]{2,1,0:T(8,128)S(1)} %get-tuple-element.40), channel_id=1, source_target_pairs={{0,4},{2,6},{4,0},{6,2},{8,12},{10,14},{12,8},{14,10},{1,5},{3,7},... | collective-permute-start | bytes 122888 | tf_op jit(solution)/shard_map/ppermute | solution.py:364
  16.5 4.9 %copy-start.2 = (bf16[1,2,2048,128]{3,2,1,0:T(8,128)(2,1)S(1)}, bf16[1,2,2048,128]{3,2,1,0:T(8,128)(2,1)}, u32[]{:S(2)}) copy-start(bf16[1,2,2048,128]{3,2,1,0:T(8,128)(2,1)} %k_ref.1) | copy-start | bytes 3145732
  16.5 4.9 %copy-start.3 = (bf16[1,2,2048,128]{3,2,1,0:T(8,128)(2,1)S(1)}, bf16[1,2,2048,128]{3,2,1,0:T(8,128)(2,1)}, u32[]{:S(2)}) copy-start(bf16[1,2,2048,128]{3,2,1,0:T(8,128)(2,1)} %v_ref.1) | copy-start | bytes 3145732
  16.5 4.9 %collective-permute-start.4 = (f32[1,40,128]{2,1,0:T(8,128)S(1)}, f32[1,40,128]{2,1,0:T(8,128)S(1)}, u32[]{:S(2)}, u32[]{:S(2)}) collective-permute-start(f32[1,40,128]{2,1,0:T(8,128)S(1)} %get-tuple-element.57), channel_id=1, source_target_pairs={{0,8},{2,10},{4,12},{6,14},{8,0},{10,2},{12,4},{14,6},{1,9},{3,11}... | collective-permute-start | bytes 61448 | tf_op jit(solution)/shard_map/ppermute | solution.py:364
  22.4 4.7 %collective-permute-start.5 = (bf16[1,32,128]{2,1,0:T(8,128)(2,1)S(1)}, bf16[1,32,128]{2,1,0:T(8,128)(2,1)S(1)}, u32[]{:S(2)}, u32[]{:S(2)}) collective-permute-start(bf16[1,32,128]{2,1,0:T(8,128)(2,1)S(1)} %attend.1.refs_0_), channel_id=1, source_target_pairs={{0,8},{2,10},{4,12},{6,14},{8,0},{10,2},{12,4},{14,6},{1,9},{3,11}... | collective-permute-start | bytes 24584 | tf_op jit(solution)/shard_map/ppermute | solution.py:364
  27.1 5.8 %collective-permute-start.8 = (bf16[2,32,128]{2,1,0:T(8,128)(2,1)S(1)}, bf16[2,32,128]{2,1,0:T(8,128)(2,1)S(1)}, u32[]{:S(2)}, u32[]{:S(2)}) collective-permute-start(bf16[2,32,128]{2,1,0:T(8,128)(2,1)S(1)} %pad_maximum_fusion), channel_id=1, source_target_pairs={{0,6},{2,4},{4,2},{6,0},{8,14},{10,12},{12,10},{14,8},{1,7},{3,5},... | collective-permute-start | bytes 49160 | tf_op jit(solution)/shard_map/ppermute | solution.py:364
  28.6 4.3 %collective-permute-start.7 = (bf16[2,32,128]{2,1,0:T(8,128)(2,1)S(1)}, bf16[2,32,128]{2,1,0:T(8,128)(2,1)S(1)}, u32[]{:S(2)}, u32[]{:S(2)}) collective-permute-start(bf16[2,32,128]{2,1,0:T(8,128)(2,1)S(1)} %pad_maximum_fusion), channel_id=1, source_target_pairs={{0,2},{2,0},{4,6},{6,4},{8,10},{10,8},{12,14},{14,12},{1,3},{3,1},... | collective-permute-start | bytes 49160 | tf_op jit(solution)/shard_map/ppermute | solution.py:364
  29.1 3.8 %collective-permute-start.6 = (bf16[2,32,128]{2,1,0:T(8,128)(2,1)S(1)}, bf16[2,32,128]{2,1,0:T(8,128)(2,1)S(1)}, u32[]{:S(2)}, u32[]{:S(2)}) collective-permute-start(bf16[2,32,128]{2,1,0:T(8,128)(2,1)S(1)} %pad_maximum_fusion), channel_id=1, source_target_pairs={{0,4},{2,6},{4,0},{6,2},{8,12},{10,14},{12,8},{14,10},{1,5},{3,7},... | collective-permute-start | bytes 49160 | tf_op jit(solution)/shard_map/ppermute | solution.py:364
  36.5 1.3 %collective-permute-start.9 = (f32[4,2048]{1,0:T(4,128)S(1)}, f32[4,2048]{1,0:T(4,128)S(1)}, u32[]{:S(2)}, u32[]{:S(2)}) collective-permute-start(f32[4,2048]{1,0:T(4,128)S(1)} %get-tuple-element.56), channel_id=1, source_target_pairs={{0,1},{1,0},{2,3},{3,2},{4,5},{5,4},{6,7},{7,6},{8,9},{9,8},{10,11... | collective-permute-start | bytes 98312 | tf_op jit(solution)/shard_map/ppermute | solution.py:364

commit v11 on v10

--- a/solution.py
+++ b/solution.py
@@ -127,16 +127,17 @@
 
 
 def project_kernel(
-    bits, rows_ref, other_ref, wq_hbm, first, wk, wv, *refs
+    bits, rows_ref, other_ref, wq_hbm, w_out_hbm, first, wk, wv, *refs
 ):
-    pieces, (wq, rows, sems) = refs[:FAN], refs[FAN:]
+    pieces, (early, wq, rows, early_sems, sems) = refs[:FAN], refs[FAN:]
     skip = first.shape[0]
     ranges = feed(wq_hbm.shape[0], skip)
     copies = [
         copies_in(wq_hbm, wq, sems.at[i], start, size, start - skip)
         for i, (start, size) in enumerate(ranges)
     ]
-    for group in copies:
+    early_copies = copies_in(w_out_hbm, early, early_sems, 0, early.shape[0], 0)
+    for group in (*copies, early_copies):
         for copy in group:
             copy.start()
 
@@ -175,9 +176,11 @@
         flat = ref.reshape(size * total, LANES)
         for i, block in enumerate(blocks):
             flat[pl.ds(i, size, stride=total), :] = block[at * size : (at + 1) * size]
-
-
-def project(rows, other, w_query, first, key_weight, value_weight, slots):
+    for copy in early_copies:
+        copy.wait()
+
+
+def project(rows, other, w_query, first, key_weight, value_weight, w_out, early, slots):
     bits = slots.bit_length() - 1
     depth, query_width = w_query.shape
     kv_width = key_weight.shape[1]
@@ -189,12 +192,14 @@
     whole = pl.BlockSpec(memory_space=pltpu.VMEM)
     return pl.pallas_call(
         functools.partial(project_kernel, bits),
-        out_shape=(piece,) * FAN,
-        in_specs=[whole, whole, hbm, whole, whole, whole],
-        out_specs=(whole,) * FAN,
+        out_shape=(piece,) * FAN
+        + (jax.ShapeDtypeStruct((early, w_out.shape[1]), w_out.dtype),),
+        in_specs=[whole, whole, hbm, hbm, whole, whole, whole],
+        out_specs=(whole,) * (FAN + 1),
         scratch_shapes=[
             pltpu.VMEM((max(depth - skip, 16), query_width), jnp.bfloat16),
             pltpu.VMEM((slots, depth), jnp.float32),
+            pltpu.SemaphoreType.DMA((PIECES,)),
             pltpu.SemaphoreType.DMA((max(1, len(feed(depth, skip))), PIECES)),
         ],
         compiler_params=pltpu.CompilerParams(vmem_limit_bytes=32 * MIB),
@@ -204,11 +209,14 @@
             transcendentals=0,
         ),
         name="project",
-    )(rows, other, in_hbm(w_query), first, key_weight, value_weight)
-
-
-def attend_kernel(query_heads, kv_heads, pieces, turn_ref, k_ref, v_ref, *refs):
-    heads_ref = refs[pieces]
+    )(rows, other, in_hbm(w_query), in_hbm(w_out), first, key_weight, value_weight)
+
+
+def attend_kernel(query_heads, kv_heads, pieces, part, w_hbm, turn_ref, k_ref, v_ref, *refs):
+    heads_ref, w_ref, sems = refs[pieces:]
+    copies = copies_in(w_hbm, w_ref, sems, *part, 0)
+    for copy in copies:
+        copy.start()
     total = refs[0][0]
     for ref in refs[1:pieces]:
         total = total + ref[0]
@@ -269,16 +277,22 @@
                 head : head + 1
             ].astype(jnp.float32)
             heads_ref[0, pl.ds(head * group, group), :] = block.astype(jnp.bfloat16)
-
-
-def attend(parts, turn, k_cache, value_cache, query_heads):
+    for copy in copies:
+        copy.wait()
+
+
+def attend(parts, turn, k_cache, value_cache, query_heads, w_out, part):
     kv_heads, cache_len = k_cache.shape[1:3]
     whole = pl.BlockSpec(memory_space=pltpu.VMEM)
     return pl.pallas_call(
-        functools.partial(attend_kernel, query_heads, kv_heads, len(parts)),
-        out_shape=jax.ShapeDtypeStruct((1, query_heads, HEAD_SIZE), jnp.bfloat16),
-        in_specs=[whole] * (3 + len(parts)),
-        out_specs=whole,
+        functools.partial(attend_kernel, query_heads, kv_heads, len(parts), part),
+        out_shape=(
+            jax.ShapeDtypeStruct((1, query_heads, HEAD_SIZE), jnp.bfloat16),
+            jax.ShapeDtypeStruct((part[1], w_out.shape[1]), w_out.dtype),
+        ),
+        in_specs=[pl.BlockSpec(memory_space=pltpu.HBM)] + [whole] * (3 + len(parts)),
+        out_specs=(whole, whole),
+        scratch_shapes=[pltpu.SemaphoreType.DMA((PIECES,))],
         compiler_params=pltpu.CompilerParams(vmem_limit_bytes=12 * MIB),
         cost_estimate=pl.CostEstimate(
             flops=4 * query_heads * cache_len * HEAD_SIZE,
@@ -286,17 +300,13 @@
             transcendentals=query_heads * cache_len,
         ),
         name="attend",
-    )(turn, k_cache, value_cache, *parts)
+    )(in_hbm(w_out), turn, k_cache, value_cache, *parts)
 
 
 def output_kernel(bits, pieces, *refs):
     parts = refs[:pieces]
-    ready = refs[pieces:-8]
-    w_hbm, mine_ref, theirs_ref, rest, flat, left, sums, sems = refs[-8:]
-    skip = w_hbm.shape[0] - rest.shape[0]
-    copies = copies_in(w_hbm, rest, sems, skip, rest.shape[0], 0)
-    for copy in copies:
-        copy.start()
+    ready = refs[pieces:-5]
+    mine_ref, theirs_ref, flat, left, sums = refs[-5:]
     slots = left.shape[0]
     heads = flat.shape[0] // slots
     at = 0
@@ -310,10 +320,7 @@
         ].astype(jnp.bfloat16)
     total = None
     at = 0
-    for ref in (*ready, rest):
-        if ref is rest:
-            for copy in copies:
-                copy.wait()
+    for ref in ready:
         size = ref.shape[0]
         for start, rows in spread(size, 0, 2 * CHUNK):
             term = jnp.dot(
@@ -333,31 +340,28 @@
             ref[t : t + 1, :] = sums[pl.ds(slot, 1), :]
 
 
-def output(parts, ready, w_out, slots):
+def output(parts, ready, slots):
     bits = slots.bit_length() - 1
-    depth, width = w_out.shape
+    depth, width = sum(x.shape[0] for x in ready), ready[0].shape[1]
     heads = depth // HEAD_SIZE
-    rest = depth - sum(x.shape[0] for x in ready)
     whole = pl.BlockSpec(memory_space=pltpu.VMEM)
     piece = jax.ShapeDtypeStruct((slots // 2, width), jnp.float32)
     return pl.pallas_call(
         functools.partial(output_kernel, bits, len(parts)),
         out_shape=(piece, piece),
-        in_specs=[whole] * (len(parts) + len(ready)) + [pl.BlockSpec(memory_space=pltpu.HBM)],
+        in_specs=[whole] * (len(parts) + len(ready)),
         out_specs=(whole, whole),
         scratch_shapes=[
-            pltpu.VMEM((rest, width), jnp.bfloat16),
             pltpu.VMEM((slots * heads, HEAD_SIZE), jnp.float32),
             pltpu.VMEM((slots, depth), jnp.bfloat16),
             pltpu.VMEM((slots, width), jnp.float32),
-            pltpu.SemaphoreType.DMA((PIECES,)),
         ],
         compiler_params=pltpu.CompilerParams(vmem_limit_bytes=24 * MIB),
         cost_estimate=pl.CostEstimate(
             flops=2 * slots * depth * width, bytes_accessed=2 * depth * width, transcendentals=0
         ),
         name="output",
-    )(*parts, *ready, in_hbm(w_out))
+    )(*parts, *ready)
 
 
 def swap(block, axis, devices, mask):
@@ -378,18 +382,20 @@
     other = swap(activations, "gy", 2, 1)
     depth = w_query.shape[0]
     (first,) = stage((w_query,), ((0, min(FIRST, depth)),))
-    pieces = project(activations, other, w_query, first, key_weight, value_weight, slots)
-
     rows_out = w_out.shape[0]
+    fewest, few, most = rows_out // 16, rows_out // 8, rows_out // 4
+    *pieces, ready_zero = project(
+        activations, other, w_query, first, key_weight, value_weight, w_out, fewest, slots
+    )
+
     *pieces, w_out = lax.optimization_barrier((*pieces, w_out))
-    few, most = rows_out // 8, rows_out // 4
     arrived = fan(pieces, devices)
     half = HEAD_SIZE // 2
     frequency = jnp.power(
         jnp.float32(500000.0), -2.0 * jnp.arange(half, dtype=jnp.float32) / HEAD_SIZE
     )
     frequency = jnp.concatenate([frequency, frequency])[None, :]
-    turn, ready_one = stage((w_out,), ((0, few),), lengths, frequency)
+    turn, ready_one = stage((w_out,), ((fewest, few),), lengths, frequency)
     total = pieces[0] + (arrived[2] + (arrived[1] + arrived[0]))
     mask = FAN
     while total.shape[0] > 2:
@@ -397,13 +403,16 @@
         total = total[:rest] + swap(total[rest:], "gx", devices, mask)
         mask *= 2
     total, w_out, ready_one = lax.optimization_barrier((total, w_out, ready_one))
-    (ready_two,) = stage((w_out,), ((few, most),))
+    (ready_two,) = stage((w_out,), ((fewest + few, most),))
     parts = [total[:1], swap(total[1:], "gx", devices, mask)]
     parts[1], ready_two = lax.optimization_barrier((parts[1], ready_two))
-    heads = attend(parts, turn, k_cache, value_cache, query_heads)
+    at = fewest + few + most
+    heads, ready_more = attend(
+        parts, turn, k_cache, value_cache, query_heads, w_out, (at, fewest)
+    )
 
     heads, w_out = lax.optimization_barrier((heads, w_out))
-    (ready_three,) = stage((w_out,), ((few + most, most),))
+    (ready_three,) = stage((w_out,), ((at + fewest, most),))
     parts = [heads, swap(heads, "gx", devices, mask)]
     parts[1], ready_three = lax.optimization_barrier((parts[1], ready_three))
     while mask > FAN:
@@ -411,11 +420,11 @@
         parts.append(swap(jnp.concatenate(parts, axis=0), "gx", devices, mask))
     held = jnp.concatenate(parts, axis=0)
     held, w_out = lax.optimization_barrier((held, w_out))
-    (ready_four,) = stage((w_out,), ((few + 2 * most, most),))
+    (ready_four,) = stage((w_out,), ((at + fewest + most, most),))
     parts += fan([held] * FAN, devices)
     parts[-1], ready_four = lax.optimization_barrier((parts[-1], ready_four))
-    ready = (ready_one, ready_two, ready_three, ready_four)
-    mine, theirs = output(parts, ready, w_out, slots)
+    ready = (ready_zero, ready_one, ready_two, ready_more, ready_three, ready_four)
+    mine, theirs = output(parts, ready, slots)
     return (mine + swap(theirs, "gy", 2, 1)).astype(jnp.bfloat16)
 
 

time: 38.6 us -> 38 us (0.984)
  Pallas kernels: 20.1 us -> 19.5 us
    pallas_call x1, Pallas kernels: 3.55 us -> 2.33 us  [output(): pl.pallas_call(functools.partial(output_kernel, bits, len(parts)), out_sh...]
where the time goes in v11:
time: 38 us; the launch traced here: 37.8 us
  Pallas kernels  19.5 us (51%)
  starting transfers between devices  13.4 us (35%)
  waiting for transfers between devices  2.81 us (7%)
  between operations  0.85 us (2%)
  other arithmetic  0.72 us (2%)
  local copies, waits for them, and re-layouts  0.46 us (1%)
    ppermute x10, starting transfers between devices, swap(): return lax.ppermute(block, axis, [(i, i ^ mask) for i in range(devices)])  13.4 us
    pallas_call x5, Pallas kernels, stage(): pl.pallas_call(kernel, out_shape=out_shape, in_specs=in_specs, out_specs=...  9.87 us
    pallas_call x1, Pallas kernels, project(): pl.pallas_call(functools.partial(project_kernel, bits), out_shape=(piece,...  6.04 us
    ppermute x10, waiting for transfers between devices, swap(): return lax.ppermute(block, axis, [(i, i ^ mask) for i in range(devices)])  2.81 us
    pallas_call x1, Pallas kernels, output(): pl.pallas_call(functools.partial(output_kernel, bits, len(parts)), out_sh...  2.33 us
    pallas_call x1, Pallas kernels, attend(): pl.pallas_call(functools.partial(attend_kernel, query_heads, kv_heads, le...  1.28 us
  transfers between devices with their start and end apart: 10, of which 3 were waited for; matrix products, arithmetic and copies ran while one was open for 0% of the time, Pallas kernels for 26%

profile of v11, /device:TPU:0, one launch (start us, length us, event | category | flops | bytes accessed | tf_op | source)
XLA Modules:
  0.0 37.8 jit_solution(12438996455756115750)
XLA Ops:
  0.0 0.5 %collective-permute-start = (bf16[4,2048]{1,0:T(4,128)(2,1)}, bf16[4,2048]{1,0:T(4,128)(2,1)S(1)}, u32[]{:S(2)}, u32[]{:S(2)}) collective-permute-start(bf16[4,2048]{1,0:T(4,128)(2,1)} %rows_ref.1), channel_id=1, source_target_pairs={{0,1},{1,0},{2,3},{3,2},{4,5},{5,4},{6,7},{7,6},{8,9},{9,8},{10,11... | collective-permute-start | bytes 49160 | tf_op jit(solution)/shard_map/ppermute | solution.py:368
  0.5 1.7 %stage.5.first = bf16[256,4096]{1,0:T(8,128)(2,1)S(1)} custom-call(bf16[2048,4096]{1,0:T(8,128)(2,1)} %wq_hbm.1), custom_call_target="tpu_custom_call" | custom-call | bytes 2097152 | tf_op jit(solution)/shard_map/stage/pallas_call | solution.py:99
  2.2 0.1 copy-done
  2.3 0.3 copy-done.1
  2.6 6.0 %project.1 = (f32[2,40,128]{2,1,0:T(8,128)S(1)}, f32[2,40,128]{2,1,0:T(8,128)S(1)}, f32[2,40,128]{2,1,0:T(8,128)S(1)}, f32[2,40,128]{2,1,0:T(8,128)S(1)}, bf16[256,2048]{1,0:T(8,128)(2,1)S(1)}) custom-call(bf16[4,2048]{1,0:T(4,128)(2,1)S(1)} %copy-done.4, bf16[4,2048]{1,0:T(4,128)(2,1)S(1)} %collective-permute-done.other_ref, bf16[2048,4096]{1,0:T(8,128)(2,1)} %wq_hbm.1, ...), custom_call_target="tpu_custom_call" | custom-call | flops 150994944 | bytes 18874368 | tf_op jit(solution)/shard_map/project/pallas_call | solution.py:193
  8.7 3.6 %collective-permute-start.1 = (f32[2,40,128]{2,1,0:T(8,128)S(1)}, f32[2,40,128]{2,1,0:T(8,128)S(1)}, u32[]{:S(2)}, u32[]{:S(2)}) collective-permute-start(f32[2,40,128]{2,1,0:T(8,128)S(1)} %get-tuple-element.39), channel_id=1, source_target_pairs={{0,6},{2,4},{4,2},{6,0},{8,14},{10,12},{12,10},{14,8},{1,7},{3,5},... | collective-permute-start | bytes 122888 | tf_op jit(solution)/shard_map/ppermute | solution.py:368
  12.3 0.5 %collective-permute-start.2 = (f32[2,40,128]{2,1,0:T(8,128)S(1)}, f32[2,40,128]{2,1,0:T(8,128)S(1)}, u32[]{:S(2)}, u32[]{:S(2)}) collective-permute-start(f32[2,40,128]{2,1,0:T(8,128)S(1)} %get-tuple-element.40), channel_id=1, source_target_pairs={{0,2},{2,0},{4,6},{6,4},{8,10},{10,8},{12,14},{14,12},{1,3},{3,1},... | collective-permute-start | bytes 122888 | tf_op jit(solution)/shard_map/ppermute | solution.py:368
  12.8 0.1 collective-permute-start.3
  12.9 0.1 maximum_bitcast_fusion.frequency_ref
  13.6 1.6 %stage.6 = (f32[8,128]{1,0:T(8,128)S(1)}, bf16[512,2048]{1,0:T(8,128)(2,1)S(1)}) custom-call(s32[1]{0:T(128)S(6)} %copy.9.length_ref, f32[1,128]{1,0:T(1,128)S(1)} %maximum_bitcast_fusion.frequency_ref, bf16[4096,2048]{1,0:T(8,128)(2,1)} %refs_0_.5), custom_call_target="tpu_custom_call" | custom-call | bytes 2097152 | tf_op jit(solution)/shard_map/stage/pallas_call | solution.py:99
  15.2 1.1 %collective-permute-done.2 = f32[2,40,128]{2,1,0:T(8,128)S(1)} collective-permute-done((f32[2,40,128]{2,1,0:T(8,128)S(1)}, f32[2,40,128]{2,1,0:T(8,128)S(1)}, u32[]{:S(2)}, u32[]{:S(2)}) %collective-permute-start.2) | collective-permute-done | bytes 40992 | tf_op jit(solution)/shard_map/ppermute | solution.py:368
  16.3 0.5 %collective-permute-done.3 = f32[2,40,128]{2,1,0:T(8,128)S(1)} collective-permute-done((f32[2,40,128]{2,1,0:T(8,128)S(1)}, f32[2,40,128]{2,1,0:T(8,128)S(1)}, u32[]{:S(2)}, u32[]{:S(2)}) %collective-permute-start.3) | collective-permute-done | bytes 40992 | tf_op jit(solution)/shard_map/ppermute | solution.py:368
  16.8 2.7 %collective-permute-start.4 = (f32[1,40,128]{2,1,0:T(8,128)S(1)}, f32[1,40,128]{2,1,0:T(8,128)S(1)}, u32[]{:S(2)}, u32[]{:S(2)}) collective-permute-start(f32[1,40,128]{2,1,0:T(8,128)S(1)} %get-tuple-element.63), channel_id=1, source_target_pairs={{0,8},{2,10},{4,12},{6,14},{8,0},{10,2},{12,4},{14,6},{1,9},{3,11}... | collective-permute-start | bytes 61448 | tf_op jit(solution)/shard_map/ppermute | solution.py:368
  19.5 2.2 %stage.7.refs_7_ = bf16[1024,2048]{1,0:T(8,128)(2,1)S(1)} custom-call(bf16[4096,2048]{1,0:T(8,128)(2,1)} %refs_0_.5), custom_call_target="tpu_custom_call" | custom-call | bytes 4194304 | tf_op jit(solution)/shard_map/stage/pallas_call | solution.py:99
  21.7 1.3 %attend.1 = (bf16[1,32,128]{2,1,0:T(8,128)(2,1)S(1)}, bf16[256,2048]{1,0:T(8,128)(2,1)S(1)}) custom-call(bf16[4096,2048]{1,0:T(8,128)(2,1)} %refs_0_.5, f32[8,128]{1,0:T(8,128)S(1)} %get-tuple-element.45.turn_ref, bf16[1,2,2048,128]{3,2,1,0:T(8,128)(2,1)S(1)} %copy-done.2, bf16[1,2,2048,128]{3,2,1,0:T(8,128)(2,1)S(1)} %copy-done.3, ...), custom_call_target="tpu_custom_call" | custom-call | flops 33554432 | bytes 2097152 | tf_op jit(solution)/shard_map/attend/pallas_call | solution.py:287
  23.0 2.5 %collective-permute-start.5 = (bf16[1,32,128]{2,1,0:T(8,128)(2,1)S(1)}, bf16[1,32,128]{2,1,0:T(8,128)(2,1)S(1)}, u32[]{:S(2)}, u32[]{:S(2)}) collective-permute-start(bf16[1,32,128]{2,1,0:T(8,128)(2,1)S(1)} %get-tuple-element.49.refs_0_), channel_id=1, source_target_pairs={{0,8},{2,10},{4,12},{6,14},{8,0},{10,2},{12,4},{14,6},{1,9},{3,11}... | collective-permute-start | bytes 24584 | tf_op jit(solution)/shard_map/ppermute | solution.py:368
  25.5 2.2 %stage.8.refs_9_ = bf16[1024,2048]{1,0:T(8,128)(2,1)S(1)} custom-call(bf16[4096,2048]{1,0:T(8,128)(2,1)} %refs_0_.5), custom_call_target="tpu_custom_call" | custom-call | bytes 4194304 | tf_op jit(solution)/shard_map/stage/pallas_call | solution.py:99
  27.8 1.4 %collective-permute-start.8 = (bf16[2,32,128]{2,1,0:T(8,128)(2,1)S(1)}, bf16[2,32,128]{2,1,0:T(8,128)(2,1)S(1)}, u32[]{:S(2)}, u32[]{:S(2)}) collective-permute-start(bf16[2,32,128]{2,1,0:T(8,128)(2,1)S(1)} %pad_maximum_fusion), channel_id=1, source_target_pairs={{0,6},{2,4},{4,2},{6,0},{8,14},{10,12},{12,10},{14,8},{1,7},{3,5},... | collective-permute-start | bytes 49160 | tf_op jit(solution)/shard_map/ppermute | solution.py:368
  29.2 0.5 %collective-permute-start.7 = (bf16[2,32,128]{2,1,0:T(8,128)(2,1)S(1)}, bf16[2,32,128]{2,1,0:T(8,128)(2,1)S(1)}, u32[]{:S(2)}, u32[]{:S(2)}) collective-permute-start(bf16[2,32,128]{2,1,0:T(8,128)(2,1)S(1)} %pad_maximum_fusion), channel_id=1, source_target_pairs={{0,2},{2,0},{4,6},{6,4},{8,10},{10,8},{12,14},{14,12},{1,3},{3,1},... | collective-permute-start | bytes 49160 | tf_op jit(solution)/shard_map/ppermute | solution.py:368
  29.8 1.6 %collective-permute-start.6 = (bf16[2,32,128]{2,1,0:T(8,128)(2,1)S(1)}, bf16[2,32,128]{2,1,0:T(8,128)(2,1)S(1)}, u32[]{:S(2)}, u32[]{:S(2)}) collective-permute-start(bf16[2,32,128]{2,1,0:T(8,128)(2,1)S(1)} %pad_maximum_fusion), channel_id=1, source_target_pairs={{0,4},{2,6},{4,0},{6,2},{8,12},{10,14},{12,8},{14,10},{1,5},{3,7},... | collective-permute-start | bytes 49160 | tf_op jit(solution)/shard_map/ppermute | solution.py:368
  31.3 2.2 %stage.9.refs_10_ = bf16[1024,2048]{1,0:T(8,128)(2,1)S(1)} custom-call(bf16[4096,2048]{1,0:T(8,128)(2,1)} %refs_0_.5), custom_call_target="tpu_custom_call" | custom-call | bytes 4194304 | tf_op jit(solution)/shard_map/stage/pallas_call | solution.py:99
  33.6 2.3 %output.1 = (f32[4,2048]{1,0:T(4,128)S(1)}, f32[4,2048]{1,0:T(4,128)S(1)}) custom-call(bf16[1,32,128]{2,1,0:T(8,128)(2,1)S(1)} %get-tuple-element.49.refs_0_, bf16[1,32,128]{2,1,0:T(8,128)(2,1)S(1)} %collective-permute-done.5.refs_1_, bf16[2,32,128]{2,1,0:T(8,128)(2,1)S(1)} %collective-permute-done.6.refs_2_, ...), custom_call_target="tpu_custom_call" | custom-call | flops 134217728 | bytes 16777216 | tf_op jit(solution)/shard_map/output/pallas_call | solution.py:349
  36.0 1.2 %collective-permute-done.9 = f32[4,2048]{1,0:T(4,128)S(1)} collective-permute-done((f32[4,2048]{1,0:T(4,128)S(1)}, f32[4,2048]{1,0:T(4,128)S(1)}, u32[]{:S(2)}, u32[]{:S(2)}) %collective-permute-start.9) | collective-permute-done | bytes 32800 | tf_op jit(solution)/shard_map/ppermute | solution.py:368
  37.2 0.6 %add_convert_fusion = bf16[4,2048]{1,0:T(4,128)(2,1)} fusion(f32[4,2048]{1,0:T(4,128)S(1)} %get-tuple-element.61, f32[4,2048]{1,0:T(4,128)S(1)} %collective-permute-done.9), kind=kLoop, calls=%fused_computation.1 | loop fusion | flops 16384 | bytes 81920 | tf_op jit(solution)/shard_map/convert_element_type | solution.py:428
  (20 shorter events, 0.1 us)
Async XLA Ops:
  0.0 2.2 %collective-permute-start = (bf16[4,2048]{1,0:T(4,128)(2,1)}, bf16[4,2048]{1,0:T(4,128)(2,1)S(1)}, u32[]{:S(2)}, u32[]{:S(2)}) collective-permute-start(bf16[4,2048]{1,0:T(4,128)(2,1)} %rows_ref.1), channel_id=1, source_target_pairs={{0,1},{1,0},{2,3},{3,2},{4,5},{5,4},{6,7},{7,6},{8,9},{9,8},{10,11... | collective-permute-start | bytes 49160 | tf_op jit(solution)/shard_map/ppermute | solution.py:368
  0.5 1.9 %copy-start = (bf16[2048,256]{1,0:T(8,128)(2,1)S(1)}, bf16[2048,256]{1,0:T(8,128)(2,1)}, u32[]{:S(2)}) copy-start(bf16[2048,256]{1,0:T(8,128)(2,1)} %wk.1) | copy-start | bytes 3145732
  0.5 2.2 %copy-start.1 = (bf16[2048,256]{1,0:T(8,128)(2,1)S(1)}, bf16[2048,256]{1,0:T(8,128)(2,1)}, u32[]{:S(2)}) copy-start(bf16[2048,256]{1,0:T(8,128)(2,1)} %wv.1) | copy-start | bytes 3145732
  0.5 2.2 %copy-start.4 = (bf16[4,2048]{1,0:T(4,128)(2,1)S(1)}, bf16[4,2048]{1,0:T(4,128)(2,1)}, u32[]{:S(2)}) copy-start(bf16[4,2048]{1,0:T(4,128)(2,1)} %rows_ref.1) | copy-start | bytes 49156
  8.7 6.5 %collective-permute-start.1 = (f32[2,40,128]{2,1,0:T(8,128)S(1)}, f32[2,40,128]{2,1,0:T(8,128)S(1)}, u32[]{:S(2)}, u32[]{:S(2)}) collective-permute-start(f32[2,40,128]{2,1,0:T(8,128)S(1)} %get-tuple-element.39), channel_id=1, source_target_pairs={{0,6},{2,4},{4,2},{6,0},{8,14},{10,12},{12,10},{14,8},{1,7},{3,5},... | collective-permute-start | bytes 122888 | tf_op jit(solution)/shard_map/ppermute | solution.py:368
  12.3 4.0 %collective-permute-start.2 = (f32[2,40,128]{2,1,0:T(8,128)S(1)}, f32[2,40,128]{2,1,0:T(8,128)S(1)}, u32[]{:S(2)}, u32[]{:S(2)}) collective-permute-start(f32[2,40,128]{2,1,0:T(8,128)S(1)} %get-tuple-element.40), channel_id=1, source_target_pairs={{0,2},{2,0},{4,6},{6,4},{8,10},{10,8},{12,14},{14,12},{1,3},{3,1},... | collective-permute-start | bytes 122888 | tf_op jit(solution)/shard_map/ppermute | solution.py:368
  12.8 4.0 %collective-permute-start.3 = (f32[2,40,128]{2,1,0:T(8,128)S(1)}, f32[2,40,128]{2,1,0:T(8,128)S(1)}, u32[]{:S(2)}, u32[]{:S(2)}) collective-permute-start(f32[2,40,128]{2,1,0:T(8,128)S(1)} %get-tuple-element.41), channel_id=1, source_target_pairs={{0,4},{2,6},{4,0},{6,2},{8,12},{10,14},{12,8},{14,10},{1,5},{3,7},... | collective-permute-start | bytes 122888 | tf_op jit(solution)/shard_map/ppermute | solution.py:368
  16.8 4.9 %copy-start.2 = (bf16[1,2,2048,128]{3,2,1,0:T(8,128)(2,1)S(1)}, bf16[1,2,2048,128]{3,2,1,0:T(8,128)(2,1)}, u32[]{:S(2)}) copy-start(bf16[1,2,2048,128]{3,2,1,0:T(8,128)(2,1)} %k_ref.1) | copy-start | bytes 3145732
  16.8 4.9 %copy-start.3 = (bf16[1,2,2048,128]{3,2,1,0:T(8,128)(2,1)S(1)}, bf16[1,2,2048,128]{3,2,1,0:T(8,128)(2,1)}, u32[]{:S(2)}) copy-start(bf16[1,2,2048,128]{3,2,1,0:T(8,128)(2,1)} %v_ref.1) | copy-start | bytes 3145732
  16.8 4.9 %collective-permute-start.4 = (f32[1,40,128]{2,1,0:T(8,128)S(1)}, f32[1,40,128]{2,1,0:T(8,128)S(1)}, u32[]{:S(2)}, u32[]{:S(2)}) collective-permute-start(f32[1,40,128]{2,1,0:T(8,128)S(1)} %get-tuple-element.63), channel_id=1, source_target_pairs={{0,8},{2,10},{4,12},{6,14},{8,0},{10,2},{12,4},{14,6},{1,9},{3,11}... | collective-permute-start | bytes 61448 | tf_op jit(solution)/shard_map/ppermute | solution.py:368
  23.0 4.7 %collective-permute-start.5 = (bf16[1,32,128]{2,1,0:T(8,128)(2,1)S(1)}, bf16[1,32,128]{2,1,0:T(8,128)(2,1)S(1)}, u32[]{:S(2)}, u32[]{:S(2)}) collective-permute-start(bf16[1,32,128]{2,1,0:T(8,128)(2,1)S(1)} %get-tuple-element.49.refs_0_), channel_id=1, source_target_pairs={{0,8},{2,10},{4,12},{6,14},{8,0},{10,2},{12,4},{14,6},{1,9},{3,11}... | collective-permute-start | bytes 24584 | tf_op jit(solution)/shard_map/ppermute | solution.py:368
  27.8 5.8 %collective-permute-start.8 = (bf16[2,32,128]{2,1,0:T(8,128)(2,1)S(1)}, bf16[2,32,128]{2,1,0:T(8,128)(2,1)S(1)}, u32[]{:S(2)}, u32[]{:S(2)}) collective-permute-start(bf16[2,32,128]{2,1,0:T(8,128)(2,1)S(1)} %pad_maximum_fusion), channel_id=1, source_target_pairs={{0,6},{2,4},{4,2},{6,0},{8,14},{10,12},{12,10},{14,8},{1,7},{3,5},... | collective-permute-start | bytes 49160 | tf_op jit(solution)/shard_map/ppermute | solution.py:368
  29.2 4.3 %collective-permute-start.7 = (bf16[2,32,128]{2,1,0:T(8,128)(2,1)S(1)}, bf16[2,32,128]{2,1,0:T(8,128)(2,1)S(1)}, u32[]{:S(2)}, u32[]{:S(2)}) collective-permute-start(bf16[2,32,128]{2,1,0:T(8,128)(2,1)S(1)} %pad_maximum_fusion), channel_id=1, source_target_pairs={{0,2},{2,0},{4,6},{6,4},{8,10},{10,8},{12,14},{14,12},{1,3},{3,1},... | collective-permute-start | bytes 49160 | tf_op jit(solution)/shard_map/ppermute | solution.py:368
  29.8 3.8 %collective-permute-start.6 = (bf16[2,32,128]{2,1,0:T(8,128)(2,1)S(1)}, bf16[2,32,128]{2,1,0:T(8,128)(2,1)S(1)}, u32[]{:S(2)}, u32[]{:S(2)}) collective-permute-start(bf16[2,32,128]{2,1,0:T(8,128)(2,1)S(1)} %pad_maximum_fusion), channel_id=1, source_target_pairs={{0,4},{2,6},{4,0},{6,2},{8,12},{10,14},{12,8},{14,10},{1,5},{3,7},... | collective-permute-start | bytes 49160 | tf_op jit(solution)/shard_map/ppermute | solution.py:368
  35.9 1.3 %collective-permute-start.9 = (f32[4,2048]{1,0:T(4,128)S(1)}, f32[4,2048]{1,0:T(4,128)S(1)}, u32[]{:S(2)}, u32[]{:S(2)}) collective-permute-start(f32[4,2048]{1,0:T(4,128)S(1)} %get-tuple-element.62), channel_id=1, source_target_pairs={{0,1},{1,0},{2,3},{3,2},{4,5},{5,4},{6,7},{7,6},{8,9},{9,8},{10,11... | collective-permute-start | bytes 98312 | tf_op jit(solution)/shard_map/ppermute | solution.py:368

commit v12 on v10

--- a/solution.py
+++ b/solution.py
@@ -268,15 +268,17 @@
             block = block + own_weight[i * group : (i + 1) * group] * fresh_values[
                 head : head + 1
             ].astype(jnp.float32)
-            heads_ref[0, pl.ds(head * group, group), :] = block.astype(jnp.bfloat16)
-
-
-def attend(parts, turn, k_cache, value_cache, query_heads):
+            block = block.astype(jnp.bfloat16)
+            for i in range(heads_ref.shape[0]):
+                heads_ref[i, pl.ds(head * group, group), :] = block
+
+
+def attend(parts, turn, k_cache, value_cache, query_heads, copies):
     kv_heads, cache_len = k_cache.shape[1:3]
     whole = pl.BlockSpec(memory_space=pltpu.VMEM)
     return pl.pallas_call(
         functools.partial(attend_kernel, query_heads, kv_heads, len(parts)),
-        out_shape=jax.ShapeDtypeStruct((1, query_heads, HEAD_SIZE), jnp.bfloat16),
+        out_shape=jax.ShapeDtypeStruct((copies, query_heads, HEAD_SIZE), jnp.bfloat16),
         in_specs=[whole] * (3 + len(parts)),
         out_specs=whole,
         compiler_params=pltpu.CompilerParams(vmem_limit_bytes=12 * MIB),
@@ -289,31 +291,20 @@
     )(turn, k_cache, value_cache, *parts)
 
 
-def output_kernel(bits, pieces, *refs):
-    parts = refs[:pieces]
-    ready = refs[pieces:-8]
-    w_hbm, mine_ref, theirs_ref, rest, flat, left, sums, sems = refs[-8:]
-    skip = w_hbm.shape[0] - rest.shape[0]
-    copies = copies_in(w_hbm, rest, sems, skip, rest.shape[0], 0)
-    for copy in copies:
-        copy.start()
-    slots = left.shape[0]
-    heads = flat.shape[0] // slots
-    at = 0
-    for ref in parts:
-        for i in range(ref.shape[0]):
-            flat[at : at + heads, :] = ref[i].astype(jnp.float32)
-            at += heads
+def output_kernel(arrived_ref, *refs):
+    ready = refs[:-5]
+    mine_ref, theirs_ref, flat, left, sums = refs[-5:]
+    slots, heads = arrived_ref.shape[:2]
+    for i in range(slots):
+        row = slots - 1 - i
+        flat[row * heads : (row + 1) * heads, :] = arrived_ref[i].astype(jnp.float32)
     for head in range(heads):
         left[:, head * HEAD_SIZE : (head + 1) * HEAD_SIZE] = flat[
             pl.ds(head, slots, stride=heads), :
         ].astype(jnp.bfloat16)
     total = None
     at = 0
-    for ref in (*ready, rest):
-        if ref is rest:
-            for copy in copies:
-                copy.wait()
+    for ref in ready:
         size = ref.shape[0]
         for start, rows in spread(size, 0, 2 * CHUNK):
             term = jnp.dot(
@@ -325,39 +316,33 @@
         at += size
     sums[...] = total
     half = slots // 2
-    turn = bit_reverse(lax.axis_index("gx"), bits)
     gy = lax.axis_index("gy")
-    for ref, side in ((mine_ref, gy), (theirs_ref, 1 - gy)):
-        for t in range(half):
-            slot = bit_reverse(t, bits) ^ turn ^ side
-            ref[t : t + 1, :] = sums[pl.ds(slot, 1), :]
-
-
-def output(parts, ready, w_out, slots):
-    bits = slots.bit_length() - 1
-    depth, width = w_out.shape
-    heads = depth // HEAD_SIZE
-    rest = depth - sum(x.shape[0] for x in ready)
+    lower, upper = sums[:half], sums[half:]
+    mine_ref[...] = jnp.where(gy == 0, lower, upper)
+    theirs_ref[...] = jnp.where(gy == 0, upper, lower)
+
+
+def output(arrived, ready):
+    slots, heads = arrived.shape[:2]
+    depth, width = sum(x.shape[0] for x in ready), ready[0].shape[1]
     whole = pl.BlockSpec(memory_space=pltpu.VMEM)
     piece = jax.ShapeDtypeStruct((slots // 2, width), jnp.float32)
     return pl.pallas_call(
-        functools.partial(output_kernel, bits, len(parts)),
+        output_kernel,
         out_shape=(piece, piece),
-        in_specs=[whole] * (len(parts) + len(ready)) + [pl.BlockSpec(memory_space=pltpu.HBM)],
+        in_specs=[whole] * (1 + len(ready)),
         out_specs=(whole, whole),
         scratch_shapes=[
-            pltpu.VMEM((rest, width), jnp.bfloat16),
             pltpu.VMEM((slots * heads, HEAD_SIZE), jnp.float32),
             pltpu.VMEM((slots, depth), jnp.bfloat16),
             pltpu.VMEM((slots, width), jnp.float32),
-            pltpu.SemaphoreType.DMA((PIECES,)),
         ],
         compiler_params=pltpu.CompilerParams(vmem_limit_bytes=24 * MIB),
         cost_estimate=pl.CostEstimate(
             flops=2 * slots * depth * width, bytes_accessed=2 * depth * width, transcendentals=0
         ),
         name="output",
-    )(*parts, *ready, in_hbm(w_out))
+    )(arrived, *ready)
 
 
 def swap(block, axis, devices, mask):
@@ -400,22 +385,16 @@
     (ready_two,) = stage((w_out,), ((few, most),))
     parts = [total[:1], swap(total[1:], "gx", devices, mask)]
     parts[1], ready_two = lax.optimization_barrier((parts[1], ready_two))
-    heads = attend(parts, turn, k_cache, value_cache, query_heads)
+    heads = attend(parts, turn, k_cache, value_cache, query_heads, devices)
 
     heads, w_out = lax.optimization_barrier((heads, w_out))
-    (ready_three,) = stage((w_out,), ((few + most, most),))
-    parts = [heads, swap(heads, "gx", devices, mask)]
-    parts[1], ready_three = lax.optimization_barrier((parts[1], ready_three))
-    while mask > FAN:
-        mask //= 2
-        parts.append(swap(jnp.concatenate(parts, axis=0), "gx", devices, mask))
-    held = jnp.concatenate(parts, axis=0)
-    held, w_out = lax.optimization_barrier((held, w_out))
-    (ready_four,) = stage((w_out,), ((few + 2 * most, most),))
-    parts += fan([held] * FAN, devices)
-    parts[-1], ready_four = lax.optimization_barrier((parts[-1], ready_four))
+    ready_three, = stage((w_out,), ((few + most, most),))
+    ready_four, = stage((w_out,), ((few + 2 * most, rows_out - few - 2 * most),))
+    arrived = lax.all_to_all(
+        heads, "gx", 0, 0, axis_index_groups=[list(range(devices))[::-1]], tiled=True
+    )
     ready = (ready_one, ready_two, ready_three, ready_four)
-    mine, theirs = output(parts, ready, w_out, slots)
+    mine, theirs = output(arrived, ready)
     return (mine + swap(theirs, "gy", 2, 1)).astype(jnp.bfloat16)
 
 

time: 38.6 us -> 52.6 us (1.36)
  local copies, waits for them, and re-layouts: 0.46 us -> 14.4 us
    unnamed x10 -> x22, local copies, waits for them, and re-layouts: 0.46 us -> 14.4 us
    ppermute x10 -> x6, starting transfers between devices: 13.4 us -> 7.35 us  [swap(): return lax.ppermute(block, axis, [(i, i ^ mask) for i in range(devices)])]
    all_to_all x0 -> x1, starting transfers between devices: none -> 6.03 us  [body(): lax.all_to_all(heads, 'gx', 0, 0, axis_index_groups=[list(range(devices))...]
    pallas_call x1, Pallas kernels: 3.55 us -> 2.29 us  [output(): pl.pallas_call(output_kernel, out_shape=(piece, piece), in_specs=[whole]...]
    pallas_call x5, Pallas kernels: 9.86 us -> 10.5 us  [stage(): pl.pallas_call(kernel, out_shape=out_shape, in_specs=in_specs, out_specs=...]
    pallas_call x1, Pallas kernels: 0.97 us -> 1.62 us  [attend(): pl.pallas_call(functools.partial(attend_kernel, query_heads, kv_heads, le...]
    ppermute x10 -> x6, waiting for transfers between devices: 2.81 us -> 2.8 us  [swap(): return lax.ppermute(block, axis, [(i, i ^ mask) for i in range(devices)])]
  transfers between devices with their start and end apart: 10 -> 7, of which waited for: 3 -> 3; matrix products, arithmetic and copies ran while one was open for 0% -> 0% of each run, Pallas kernels for 26% -> 20%
where the time goes in v12:
time: 52.6 us; the launch traced here: 52.3 us
  Pallas kernels  20.2 us (38%)
  local copies, waits for them, and re-layouts  14.4 us (27%)
  starting transfers between devices  13.4 us (25%)
  waiting for transfers between devices  2.8 us (5%)
  between operations  0.81 us (2%)
  other arithmetic  0.71 us (1%)
    unnamed x22, local copies, waits for them, and re-layouts  14.4 us
    pallas_call x5, Pallas kernels, stage(): pl.pallas_call(kernel, out_shape=out_shape, in_specs=in_specs, out_specs=...  10.5 us
    ppermute x6, starting transfers between devices, swap(): return lax.ppermute(block, axis, [(i, i ^ mask) for i in range(devices)])  7.35 us
    all_to_all x1, starting transfers between devices, body(): lax.all_to_all(heads, 'gx', 0, 0, axis_index_groups=[list(range(devices))...  6.03 us
    pallas_call x1, Pallas kernels, project(): pl.pallas_call(functools.partial(project_kernel, bits), out_shape=(piece,...  5.73 us
    ppermute x6, waiting for transfers between devices, swap(): return lax.ppermute(block, axis, [(i, i ^ mask) for i in range(devices)])  2.8 us
    pallas_call x1, Pallas kernels, output(): pl.pallas_call(output_kernel, out_shape=(piece, piece), in_specs=[whole]...  2.29 us
    pallas_call x1, Pallas kernels, attend(): pl.pallas_call(functools.partial(attend_kernel, query_heads, kv_heads, le...  1.62 us
  transfers between devices with their start and end apart: 7, of which 3 were waited for; matrix products, arithmetic and copies ran while one was open for 0% of the time, Pallas kernels for 20%

profile of v12, /device:TPU:0, one launch (start us, length us, event | category | flops | bytes accessed | tf_op | source)
XLA Modules:
  0.0 52.3 jit_solution(16519440316429123997)
XLA Ops:
  0.0 0.5 collective-permute-start
  0.5 1.7 %stage.5.first = bf16[256,4096]{1,0:T(8,128)(2,1)S(1)} custom-call(bf16[2048,4096]{1,0:T(8,128)(2,1)} %wq_hbm.1), custom_call_target="tpu_custom_call" | custom-call | bytes 2097152 | tf_op jit(solution)/shard_map/stage/pallas_call | solution.py:99
  2.3 0.3 copy-done.7
  2.6 5.7 %project.1 = (f32[2,40,128]{2,1,0:T(8,128)S(1)}, f32[2,40,128]{2,1,0:T(8,128)S(1)}, f32[2,40,128]{2,1,0:T(8,128)S(1)}, f32[2,40,128]{2,1,0:T(8,128)S(1)}) custom-call(bf16[4,2048]{1,0:T(4,128)(2,1)S(1)} %copy-done.10, bf16[4,2048]{1,0:T(4,128)(2,1)S(1)} %collective-permute-done.other_ref, bf16[2048,4096]{1,0:T(8,128)(2,1)} %wq_hbm.1, ...), custom_call_target="tpu_custom_call" | custom-call | flops 150994944 | bytes 18874368 | tf_op jit(solution)/shard_map/project/pallas_call | solution.py:190
  8.4 3.6 %collective-permute-start.1 = (f32[2,40,128]{2,1,0:T(8,128)S(1)}, f32[2,40,128]{2,1,0:T(8,128)S(1)}, u32[]{:S(2)}, u32[]{:S(2)}) collective-permute-start(f32[2,40,128]{2,1,0:T(8,128)S(1)} %get-tuple-element.32), channel_id=1, source_target_pairs={{0,6},{2,4},{4,2},{6,0},{8,14},{10,12},{12,10},{14,8},{1,7},{3,5},... | collective-permute-start | bytes 122888 | tf_op jit(solution)/shard_map/ppermute | solution.py:349
  12.0 0.5 %collective-permute-start.2 = (f32[2,40,128]{2,1,0:T(8,128)S(1)}, f32[2,40,128]{2,1,0:T(8,128)S(1)}, u32[]{:S(2)}, u32[]{:S(2)}) collective-permute-start(f32[2,40,128]{2,1,0:T(8,128)S(1)} %get-tuple-element.33), channel_id=1, source_target_pairs={{0,2},{2,0},{4,6},{6,4},{8,10},{10,8},{12,14},{14,12},{1,3},{3,1},... | collective-permute-start | bytes 122888 | tf_op jit(solution)/shard_map/ppermute | solution.py:349
  13.3 1.6 %stage.6 = (f32[8,128]{1,0:T(8,128)S(1)}, bf16[512,2048]{1,0:T(8,128)(2,1)S(1)}) custom-call(s32[1]{0:T(128)S(6)} %copy.9.length_ref, f32[1,128]{1,0:T(1,128)S(1)} %maximum_bitcast_fusion.frequency_ref, bf16[4096,2048]{1,0:T(8,128)(2,1)} %refs_0_.5), custom_call_target="tpu_custom_call" | custom-call | bytes 2097152 | tf_op jit(solution)/shard_map/stage/pallas_call | solution.py:99
  14.9 1.1 %collective-permute-done.2 = f32[2,40,128]{2,1,0:T(8,128)S(1)} collective-permute-done((f32[2,40,128]{2,1,0:T(8,128)S(1)}, f32[2,40,128]{2,1,0:T(8,128)S(1)}, u32[]{:S(2)}, u32[]{:S(2)}) %collective-permute-start.2) | collective-permute-done | bytes 40992 | tf_op jit(solution)/shard_map/ppermute | solution.py:349
  16.0 0.5 %collective-permute-done.3 = f32[2,40,128]{2,1,0:T(8,128)S(1)} collective-permute-done((f32[2,40,128]{2,1,0:T(8,128)S(1)}, f32[2,40,128]{2,1,0:T(8,128)S(1)}, u32[]{:S(2)}, u32[]{:S(2)}) %collective-permute-start.3) | collective-permute-done | bytes 40992 | tf_op jit(solution)/shard_map/ppermute | solution.py:349
  16.5 2.7 %collective-permute-start.4 = (f32[1,40,128]{2,1,0:T(8,128)S(1)}, f32[1,40,128]{2,1,0:T(8,128)S(1)}, u32[]{:S(2)}, u32[]{:S(2)}) collective-permute-start(f32[1,40,128]{2,1,0:T(8,128)S(1)} %get-tuple-element.45), channel_id=1, source_target_pairs={{0,8},{2,10},{4,12},{6,14},{8,0},{10,2},{12,4},{14,6},{1,9},{3,11}... | collective-permute-start | bytes 61448 | tf_op jit(solution)/shard_map/ppermute | solution.py:349
  19.2 2.2 %stage.7.refs_1_ = bf16[1024,2048]{1,0:T(8,128)(2,1)S(1)} custom-call(bf16[4096,2048]{1,0:T(8,128)(2,1)} %refs_0_.5), custom_call_target="tpu_custom_call" | custom-call | bytes 4194304 | tf_op jit(solution)/shard_map/stage/pallas_call | solution.py:99
  21.4 2.0 %copy-done.2 = bf16[1024,2048]{1,0:T(8,128)(2,1)} copy-done((bf16[1024,2048]{1,0:T(8,128)(2,1)}, bf16[1024,2048]{1,0:T(8,128)(2,1)S(1)}, u32[]{:S(2)}) %copy-start.2) | copy-done | bytes 4194328
  23.5 1.6 %attend.1 = bf16[8,32,128]{2,1,0:T(8,128)(2,1)} custom-call(f32[8,128]{1,0:T(8,128)S(1)} %get-tuple-element.30.turn_ref, bf16[1,2,2048,128]{3,2,1,0:T(8,128)(2,1)S(1)} %copy-done.8, bf16[1,2,2048,128]{3,2,1,0:T(8,128)(2,1)S(1)} %copy-done.9, f32[1,40,128]{2,1,0:T(8,128)S(1)} %get-tuple-element.46.refs_0_, f32[1,40,128]{2,1,0:T(8,128)S(1)} %collective-permute-done.4.refs_1_), custom_call_target="tpu_custom_call" | custom-call | flops 33554432 | bytes 2097152 | tf_op jit(solution)/shard_map/attend/pallas_call | solution.py:279
  25.1 6.0 %all-to-all-start = ((bf16[8,32,128]{2,1,0:T(8,128)(2,1)}), bf16[8,32,128]{2,1,0:T(8,128)(2,1)S(1)}, u32[]{:S(2)}, u32[]{:S(2)}) async-start(bf16[8,32,128]{2,1,0:T(8,128)(2,1)} %attend.1), calls=%async_computation | async-start | bytes 131072 | tf_op jit(solution)/shard_map/all_to_all | solution.py:393
  31.1 2.2 %stage.8.refs_2_ = bf16[1024,2048]{1,0:T(8,128)(2,1)S(1)} custom-call(bf16[4096,2048]{1,0:T(8,128)(2,1)} %refs_0_.5), custom_call_target="tpu_custom_call" | custom-call | bytes 4194304 | tf_op jit(solution)/shard_map/stage/pallas_call | solution.py:99
  33.3 2.1 %copy-done.4 = bf16[1024,2048]{1,0:T(8,128)(2,1)} copy-done((bf16[1024,2048]{1,0:T(8,128)(2,1)}, bf16[1024,2048]{1,0:T(8,128)(2,1)S(1)}, u32[]{:S(2)}) %copy-start.4) | copy-done | bytes 4194328
  35.4 2.9 %stage.9.refs_3_ = bf16[1536,2048]{1,0:T(8,128)(2,1)S(1)} custom-call(bf16[4096,2048]{1,0:T(8,128)(2,1)} %refs_0_.5), custom_call_target="tpu_custom_call" | custom-call | bytes 6291456 | tf_op jit(solution)/shard_map/stage/pallas_call | solution.py:99
  38.3 2.6 %copy-done = bf16[1536,2048]{1,0:T(8,128)(2,1)} copy-done((bf16[1536,2048]{1,0:T(8,128)(2,1)}, bf16[1536,2048]{1,0:T(8,128)(2,1)S(1)}, u32[]{:S(2)}) %copy-start) | copy-done | bytes 6291480
  40.9 2.8 %copy-done.1 = bf16[1536,2048]{1,0:T(8,128)(2,1)S(1)} copy-done((bf16[1536,2048]{1,0:T(8,128)(2,1)S(1)}, bf16[1536,2048]{1,0:T(8,128)(2,1)}, u32[]{:S(2)}) %copy-start.1) | copy-done | bytes 6291480
  43.7 2.2 %copy-done.3 = bf16[1024,2048]{1,0:T(8,128)(2,1)S(1)} copy-done((bf16[1024,2048]{1,0:T(8,128)(2,1)S(1)}, bf16[1024,2048]{1,0:T(8,128)(2,1)}, u32[]{:S(2)}) %copy-start.3) | copy-done | bytes 4194328
  45.9 2.2 %copy-done.5 = bf16[1024,2048]{1,0:T(8,128)(2,1)S(1)} copy-done((bf16[1024,2048]{1,0:T(8,128)(2,1)S(1)}, bf16[1024,2048]{1,0:T(8,128)(2,1)}, u32[]{:S(2)}) %copy-start.5) | copy-done | bytes 4194328
  48.1 2.3 %output.1 = (f32[4,2048]{1,0:T(4,128)S(1)}, f32[4,2048]{1,0:T(4,128)S(1)}) custom-call(bf16[8,32,128]{2,1,0:T(8,128)(2,1)S(1)} %all-to-all-done.arrived_ref, bf16[512,2048]{1,0:T(8,128)(2,1)S(1)} %get-tuple-element.40.refs_0_, bf16[1024,2048]{1,0:T(8,128)(2,1)S(1)} %copy-done.3, bf16[1024,2048]{1,0:T(8,128)(2,1)S(1)} %copy-done.5, ...), custom_call_target="tpu_custom_call" | custom-call | flops 134217728 | bytes 16777216 | tf_op jit(solution)/shard_map/output/pallas_call | solution.py:330
  50.4 1.2 %collective-permute-done.5 = f32[4,2048]{1,0:T(4,128)S(1)} collective-permute-done((f32[4,2048]{1,0:T(4,128)S(1)}, f32[4,2048]{1,0:T(4,128)S(1)}, u32[]{:S(2)}, u32[]{:S(2)}) %collective-permute-start.5) | collective-permute-done | bytes 32800 | tf_op jit(solution)/shard_map/ppermute | solution.py:349
  51.6 0.6 %add_convert_fusion = bf16[4,2048]{1,0:T(4,128)(2,1)} fusion(f32[4,2048]{1,0:T(4,128)S(1)} %get-tuple-element.43, f32[4,2048]{1,0:T(4,128)S(1)} %collective-permute-done.5), kind=kLoop, calls=%fused_computation.1 | loop fusion | flops 16384 | bytes 81920 | tf_op jit(solution)/shard_map/convert_element_type | solution.py:398
  (25 shorter events, 0.4 us)
Async XLA Ops:
  0.0 2.2 %collective-permute-start = (bf16[4,2048]{1,0:T(4,128)(2,1)}, bf16[4,2048]{1,0:T(4,128)(2,1)S(1)}, u32[]{:S(2)}, u32[]{:S(2)}) collective-permute-start(bf16[4,2048]{1,0:T(4,128)(2,1)} %rows_ref.1), channel_id=1, source_target_pairs={{0,1},{1,0},{2,3},{3,2},{4,5},{5,4},{6,7},{7,6},{8,9},{9,8},{10,11... | collective-permute-start | bytes 49160 | tf_op jit(solution)/shard_map/ppermute | solution.py:349
  0.5 1.9 %copy-start.6 = (bf16[2048,256]{1,0:T(8,128)(2,1)S(1)}, bf16[2048,256]{1,0:T(8,128)(2,1)}, u32[]{:S(2)}) copy-start(bf16[2048,256]{1,0:T(8,128)(2,1)} %wk.1) | copy-start | bytes 3145732
  0.5 2.2 %copy-start.7 = (bf16[2048,256]{1,0:T(8,128)(2,1)S(1)}, bf16[2048,256]{1,0:T(8,128)(2,1)}, u32[]{:S(2)}) copy-start(bf16[2048,256]{1,0:T(8,128)(2,1)} %wv.1) | copy-start | bytes 3145732
  0.5 2.2 %copy-start.10 = (bf16[4,2048]{1,0:T(4,128)(2,1)S(1)}, bf16[4,2048]{1,0:T(4,128)(2,1)}, u32[]{:S(2)}) copy-start(bf16[4,2048]{1,0:T(4,128)(2,1)} %rows_ref.1) | copy-start | bytes 49156
  8.4 6.5 %collective-permute-start.1 = (f32[2,40,128]{2,1,0:T(8,128)S(1)}, f32[2,40,128]{2,1,0:T(8,128)S(1)}, u32[]{:S(2)}, u32[]{:S(2)}) collective-permute-start(f32[2,40,128]{2,1,0:T(8,128)S(1)} %get-tuple-element.32), channel_id=1, source_target_pairs={{0,6},{2,4},{4,2},{6,0},{8,14},{10,12},{12,10},{14,8},{1,7},{3,5},... | collective-permute-start | bytes 122888 | tf_op jit(solution)/shard_map/ppermute | solution.py:349
  12.0 4.0 %collective-permute-start.2 = (f32[2,40,128]{2,1,0:T(8,128)S(1)}, f32[2,40,128]{2,1,0:T(8,128)S(1)}, u32[]{:S(2)}, u32[]{:S(2)}) collective-permute-start(f32[2,40,128]{2,1,0:T(8,128)S(1)} %get-tuple-element.33), channel_id=1, source_target_pairs={{0,2},{2,0},{4,6},{6,4},{8,10},{10,8},{12,14},{14,12},{1,3},{3,1},... | collective-permute-start | bytes 122888 | tf_op jit(solution)/shard_map/ppermute | solution.py:349
  12.5 4.0 %collective-permute-start.3 = (f32[2,40,128]{2,1,0:T(8,128)S(1)}, f32[2,40,128]{2,1,0:T(8,128)S(1)}, u32[]{:S(2)}, u32[]{:S(2)}) collective-permute-start(f32[2,40,128]{2,1,0:T(8,128)S(1)} %get-tuple-element.34), channel_id=1, source_target_pairs={{0,4},{2,6},{4,0},{6,2},{8,12},{10,14},{12,8},{14,10},{1,5},{3,7},... | collective-permute-start | bytes 122888 | tf_op jit(solution)/shard_map/ppermute | solution.py:349
  16.5 6.9 %copy-start.8 = (bf16[1,2,2048,128]{3,2,1,0:T(8,128)(2,1)S(1)}, bf16[1,2,2048,128]{3,2,1,0:T(8,128)(2,1)}, u32[]{:S(2)}) copy-start(bf16[1,2,2048,128]{3,2,1,0:T(8,128)(2,1)} %k_ref.1) | copy-start | bytes 3145732
  16.5 6.9 %copy-start.9 = (bf16[1,2,2048,128]{3,2,1,0:T(8,128)(2,1)S(1)}, bf16[1,2,2048,128]{3,2,1,0:T(8,128)(2,1)}, u32[]{:S(2)}) copy-start(bf16[1,2,2048,128]{3,2,1,0:T(8,128)(2,1)} %v_ref.1) | copy-start | bytes 3145732
  16.5 6.9 %collective-permute-start.4 = (f32[1,40,128]{2,1,0:T(8,128)S(1)}, f32[1,40,128]{2,1,0:T(8,128)S(1)}, u32[]{:S(2)}, u32[]{:S(2)}) collective-permute-start(f32[1,40,128]{2,1,0:T(8,128)S(1)} %get-tuple-element.45), channel_id=1, source_target_pairs={{0,8},{2,10},{4,12},{6,14},{8,0},{10,2},{12,4},{14,6},{1,9},{3,11}... | collective-permute-start | bytes 61448 | tf_op jit(solution)/shard_map/ppermute | solution.py:349
  21.4 2.1 %copy-start.2 = (bf16[1024,2048]{1,0:T(8,128)(2,1)}, bf16[1024,2048]{1,0:T(8,128)(2,1)S(1)}, u32[]{:S(2)}) copy-start(bf16[1024,2048]{1,0:T(8,128)(2,1)S(1)} %stage.7.refs_1_) | copy-start | bytes 12582916
  25.1 15.8 %all-to-all-start = ((bf16[8,32,128]{2,1,0:T(8,128)(2,1)}), bf16[8,32,128]{2,1,0:T(8,128)(2,1)S(1)}, u32[]{:S(2)}, u32[]{:S(2)}) async-start(bf16[8,32,128]{2,1,0:T(8,128)(2,1)} %attend.1), calls=%async_computation | async-start | bytes 131072 | tf_op jit(solution)/shard_map/all_to_all | solution.py:393
  33.3 2.1 %copy-start.4 = (bf16[1024,2048]{1,0:T(8,128)(2,1)}, bf16[1024,2048]{1,0:T(8,128)(2,1)S(1)}, u32[]{:S(2)}) copy-start(bf16[1024,2048]{1,0:T(8,128)(2,1)S(1)} %stage.8.refs_2_) | copy-start | bytes 12582916
  38.3 2.7 %copy-start = (bf16[1536,2048]{1,0:T(8,128)(2,1)}, bf16[1536,2048]{1,0:T(8,128)(2,1)S(1)}, u32[]{:S(2)}) copy-start(bf16[1536,2048]{1,0:T(8,128)(2,1)S(1)} %stage.9.refs_3_) | copy-start | bytes 18874372
  40.9 2.8 %copy-start.1 = (bf16[1536,2048]{1,0:T(8,128)(2,1)S(1)}, bf16[1536,2048]{1,0:T(8,128)(2,1)}, u32[]{:S(2)}) copy-start(bf16[1536,2048]{1,0:T(8,128)(2,1)} %copy-done) | copy-start | bytes 18874372
  43.7 2.2 %copy-start.3 = (bf16[1024,2048]{1,0:T(8,128)(2,1)S(1)}, bf16[1024,2048]{1,0:T(8,128)(2,1)}, u32[]{:S(2)}) copy-start(bf16[1024,2048]{1,0:T(8,128)(2,1)} %copy-done.2) | copy-start | bytes 12582916
  45.9 2.2 %copy-start.5 = (bf16[1024,2048]{1,0:T(8,128)(2,1)S(1)}, bf16[1024,2048]{1,0:T(8,128)(2,1)}, u32[]{:S(2)}) copy-start(bf16[1024,2048]{1,0:T(8,128)(2,1)} %copy-done.4) | copy-start | bytes 12582916
  50.4 1.2 %collective-permute-start.5 = (f32[4,2048]{1,0:T(4,128)S(1)}, f32[4,2048]{1,0:T(4,128)S(1)}, u32[]{:S(2)}, u32[]{:S(2)}) collective-permute-start(f32[4,2048]{1,0:T(4,128)S(1)} %get-tuple-element.44), channel_id=1, source_target_pairs={{0,1},{1,0},{2,3},{3,2},{4,5},{5,4},{6,7},{7,6},{8,9},{9,8},{10,11... | collective-permute-start | bytes 98312 | tf_op jit(solution)/shard_map/ppermute | solution.py:349

commit v13 on v8

--- a/solution.py
+++ b/solution.py
@@ -89,6 +89,7 @@
             pl.BlockSpec(memory_space=pltpu.HBM),
         ],
         out_specs=vmem,
+        compiler_params=pltpu.CompilerParams(vmem_limit_bytes=2 * MIB),
         cost_estimate=pl.CostEstimate(flops=0, bytes_accessed=2 * beside.size, transcendentals=256),
         name="turning",
     )(lengths, frequency, in_hbm(beside))
@@ -200,19 +201,38 @@
     group = query_heads // kv_heads
     factor = 1.0 / math.sqrt(HEAD_SIZE)
     length = turn_ref[2:3, 0:1].astype(jnp.int32)
-    for head in range(kv_heads):
-        queries = turned[head * group : (head + 1) * group]
-        fresh_key = turned[query_heads + head : query_heads + head + 1].astype(jnp.float32)
-        own = jnp.sum(queries.astype(jnp.float32) * fresh_key, axis=1, keepdims=True) * factor
+    side = 2 if kv_heads % 2 == 0 else 1
+    for first in range(0, kv_heads, side):
+        members = range(first, first + side)
+        queries = [turned[head * group : (head + 1) * group] for head in members]
+        empty = jnp.zeros((group, HEAD_SIZE), jnp.bfloat16)
+        spread_out = jnp.concatenate(
+            [
+                jnp.concatenate([q if i == j else empty for j in range(side)], axis=1)
+                for i, q in enumerate(queries)
+            ],
+            axis=0,
+        )
+        keys = jnp.concatenate([k_ref[0, head] for head in members], axis=1)
+        values = jnp.concatenate([v_ref[0, head] for head in members], axis=1)
         scores = (
             lax.dot_general(
-                queries,
-                k_ref[0, head],
-                (((1,), (1,)), ((), ())),
-                preferred_element_type=jnp.float32,
+                spread_out, keys, (((1,), (1,)), ((), ())), preferred_element_type=jnp.float32
             )
             * factor
         )
+        own = jnp.concatenate(
+            [
+                jnp.sum(
+                    q.astype(jnp.float32)
+                    * turned[query_heads + head : query_heads + head + 1].astype(jnp.float32),
+                    axis=1,
+                    keepdims=True,
+                )
+                for q, head in zip(queries, members)
+            ],
+            axis=0,
+        ) * factor
         slot = lax.broadcasted_iota(jnp.int32, scores.shape, 1)
         scores = jnp.where(slot < length, scores, -jnp.inf)
         top = jnp.maximum(jnp.max(scores, axis=1, keepdims=True), own)
@@ -220,12 +240,14 @@
         own_exp = jnp.exp(own - top)
         share = 1.0 / (jnp.sum(exponent, axis=1, keepdims=True) + own_exp)
         weights = (exponent * share).astype(jnp.bfloat16)
-        own_weight = (own_exp * share).astype(jnp.bfloat16)
-        mixed = jnp.dot(weights, v_ref[0, head], preferred_element_type=jnp.float32)
-        mixed = mixed + own_weight.astype(jnp.float32) * fresh_values[head : head + 1].astype(
-            jnp.float32
-        )
-        heads_ref[0, pl.ds(head * group, group), :] = mixed.astype(jnp.bfloat16)
+        own_weight = (own_exp * share).astype(jnp.bfloat16).astype(jnp.float32)
+        mixed = jnp.dot(weights, values, preferred_element_type=jnp.float32)
+        for i, head in enumerate(members):
+            block = mixed[i * group : (i + 1) * group, i * HEAD_SIZE : (i + 1) * HEAD_SIZE]
+            block = block + own_weight[i * group : (i + 1) * group] * fresh_values[
+                head : head + 1
+            ].astype(jnp.float32)
+            heads_ref[0, pl.ds(head * group, group), :] = block.astype(jnp.bfloat16)
 
 
 def attend(parts, turn, k_cache, value_cache, query_heads, beside):
@@ -247,7 +269,7 @@
 
 
 def output_kernel(bits, pieces, *refs):
-    parts = refs[:pieces]
+    parts = refs[:pieces][::-1]
     w_ref, mine_ref, theirs_ref, flat, left, sums = refs[pieces:]
     slots = left.shape[0]
     heads = flat.shape[0] // slots
@@ -293,7 +315,7 @@
             pltpu.VMEM((slots, depth), jnp.bfloat16),
             pltpu.VMEM((slots, width), jnp.float32),
         ],
-        compiler_params=pltpu.CompilerParams(vmem_limit_bytes=24 * MIB),
+        compiler_params=pltpu.CompilerParams(vmem_limit_bytes=12 * MIB),
         cost_estimate=pl.CostEstimate(
             flops=2 * slots * depth * width, bytes_accessed=2 * depth * width, transcendentals=0
         ),
@@ -334,6 +356,7 @@
         rest = total.shape[0] // 2
         total = total[:rest] + swap(total[rest:], "gx", devices, mask)
         mask *= 2
+    total, turn = lax.optimization_barrier((total, turn))
     parts = [total[:1], swap(total[1:], "gx", devices, mask)]
     heads = attend(parts, turn, k_cache, value_cache, query_heads, w_out)
 
@@ -343,7 +366,7 @@
         parts.append(swap(jnp.concatenate(parts, axis=0), "gx", devices, mask))
     held = jnp.concatenate(parts, axis=0)
     parts += fan([held] * FAN, devices)
-    mine, theirs = output(parts, w_out, slots)
+    mine, theirs = output(parts[::-1], w_out, slots)
     return (mine + swap(theirs, "gy", 2, 1)).astype(jnp.bfloat16)
 
 

time: 45.2 us -> 36.8 us (0.81)
  local copies, waits for them, and re-layouts: 6.48 us -> 0.05 us
  Pallas kernels: 12.3 us -> 10.8 us
  starting transfers between devices: 13.7 us -> 14.5 us
  waiting for transfers between devices: 10.5 us -> 9.76 us
  other arithmetic: 1.3 us -> 0.72 us
    unnamed x14 -> x18, local copies, waits for them, and re-layouts: 6.48 us -> 0.04 us
    pallas_call x1, Pallas kernels: 1.31 us -> 0.04 us  [turning(): pl.pallas_call(turning_kernel, out_shape=jax.ShapeDtypeStruct((8, HEAD_SI...]
    ppermute x10, starting transfers between devices: 13.7 us -> 14.5 us  [swap(): return lax.ppermute(block, axis, [(i, i ^ mask) for i in range(devices)])]
    ppermute x10, waiting for transfers between devices: 10.5 us -> 9.76 us  [swap(): return lax.ppermute(block, axis, [(i, i ^ mask) for i in range(devices)])]
    broadcast_in_dim x1, other arithmetic: 0.66 us -> 0.07 us  [body(): frequency = jnp.concatenate([frequency, frequency])[None, :]]
  transfers between devices with their start and end apart: 10 -> 10, of which waited for: 8 -> 9; matrix products, arithmetic and copies ran while one was open for 1% -> 0% of each run, Pallas kernels for 7% -> 5%
where the time goes in v13:
time: 36.8 us; the launch traced here: 36.6 us
  starting transfers between devices  14.5 us (39%)
  Pallas kernels  10.8 us (29%)
  waiting for transfers between devices  9.76 us (27%)
  between operations  0.79 us (2%)
  other arithmetic  0.72 us (2%)
    ppermute x10, starting transfers between devices, swap(): return lax.ppermute(block, axis, [(i, i ^ mask) for i in range(devices)])  14.5 us
    ppermute x10, waiting for transfers between devices, swap(): return lax.ppermute(block, axis, [(i, i ^ mask) for i in range(devices)])  9.76 us
    pallas_call x1, Pallas kernels, project(): pl.pallas_call(functools.partial(project_kernel, bits), out_shape=(piece,...  5.86 us
    pallas_call x1, Pallas kernels, output(): pl.pallas_call(functools.partial(output_kernel, bits, len(parts)), out_sh...  2.31 us
    pallas_call x1, Pallas kernels, stage_rows(): pl.pallas_call(functools.partial(stage_kernel, rows), out_shape=jax.Shape...  1.66 us
    pallas_call x1, Pallas kernels, attend(): pl.pallas_call(functools.partial(attend_kernel, query_heads, kv_heads, le...  0.97 us
  transfers between devices with their start and end apart: 10, of which 9 were waited for; matrix products, arithmetic and copies ran while one was open for 0% of the time, Pallas kernels for 5%

profile of v13, /device:TPU:0, one launch (start us, length us, event | category | flops | bytes accessed | tf_op | source)
XLA Modules:
  0.0 36.6 jit_solution(14338648732455012090)
XLA Ops:
  0.0 0.5 %collective-permute-start = (bf16[4,2048]{1,0:T(4,128)(2,1)}, bf16[4,2048]{1,0:T(4,128)(2,1)S(1)}, u32[]{:S(2)}, u32[]{:S(2)}) collective-permute-start(bf16[4,2048]{1,0:T(4,128)(2,1)} %rows_ref.1), channel_id=1, source_target_pairs={{0,1},{1,0},{2,3},{3,2},{4,5},{5,4},{6,7},{7,6},{8,9},{9,8},{10,11... | collective-permute-start | bytes 49160 | tf_op jit(solution)/shard_map/ppermute | solution.py:327
  0.5 1.7 %stage.1.first = bf16[256,4096]{1,0:T(8,128)(2,1)S(1)} custom-call(bf16[2048,4096]{1,0:T(8,128)(2,1)} %wq_hbm.1), custom_call_target="tpu_custom_call" | custom-call | bytes 2097152 | tf_op jit(solution)/shard_map/stage/pallas_call | solution.py:57
  2.3 5.9 %project.1 = (f32[2,40,128]{2,1,0:T(8,128)S(1)}, f32[2,40,128]{2,1,0:T(8,128)S(1)}, f32[2,40,128]{2,1,0:T(8,128)S(1)}, f32[2,40,128]{2,1,0:T(8,128)S(1)}) custom-call(bf16[4,2048]{1,0:T(4,128)(2,1)S(1)} %copy-done.4, bf16[4,2048]{1,0:T(4,128)(2,1)S(1)} %collective-permute-done.other_ref, bf16[2048,4096]{1,0:T(8,128)(2,1)} %wq_hbm.1, ...), custom_call_target="tpu_custom_call" | custom-call | flops 150994944 | bytes 18874368 | tf_op jit(solution)/shard_map/project/pallas_call | solution.py:167
  8.1 4.0 %collective-permute-start.1 = (f32[2,40,128]{2,1,0:T(8,128)S(1)}, f32[2,40,128]{2,1,0:T(8,128)S(1)}, u32[]{:S(2)}, u32[]{:S(2)}) collective-permute-start(f32[2,40,128]{2,1,0:T(8,128)S(1)} %get-tuple-element.14), channel_id=1, source_target_pairs={{0,6},{2,4},{4,2},{6,0},{8,14},{10,12},{12,10},{14,8},{1,7},{3,5},... | collective-permute-start | bytes 122888 | tf_op jit(solution)/shard_map/ppermute | solution.py:327
  12.1 0.5 %collective-permute-start.2 = (f32[2,40,128]{2,1,0:T(8,128)S(1)}, f32[2,40,128]{2,1,0:T(8,128)S(1)}, u32[]{:S(2)}, u32[]{:S(2)}) collective-permute-start(f32[2,40,128]{2,1,0:T(8,128)S(1)} %get-tuple-element.15), channel_id=1, source_target_pairs={{0,2},{2,0},{4,6},{6,4},{8,10},{10,8},{12,14},{14,12},{1,3},{3,1},... | collective-permute-start | bytes 122888 | tf_op jit(solution)/shard_map/ppermute | solution.py:327
  12.7 0.1 collective-permute-start.3
  12.8 0.1 maximum_bitcast_fusion.frequency_ref
  13.6 0.5 %collective-permute-done.1 = f32[2,40,128]{2,1,0:T(8,128)S(1)} collective-permute-done((f32[2,40,128]{2,1,0:T(8,128)S(1)}, f32[2,40,128]{2,1,0:T(8,128)S(1)}, u32[]{:S(2)}, u32[]{:S(2)}) %collective-permute-start.1) | collective-permute-done | bytes 40992 | tf_op jit(solution)/shard_map/ppermute | solution.py:327
  14.1 2.0 %collective-permute-done.2 = f32[2,40,128]{2,1,0:T(8,128)S(1)} collective-permute-done((f32[2,40,128]{2,1,0:T(8,128)S(1)}, f32[2,40,128]{2,1,0:T(8,128)S(1)}, u32[]{:S(2)}, u32[]{:S(2)}) %collective-permute-start.2) | collective-permute-done | bytes 40992 | tf_op jit(solution)/shard_map/ppermute | solution.py:327
  16.1 0.5 %collective-permute-done.3 = f32[2,40,128]{2,1,0:T(8,128)S(1)} collective-permute-done((f32[2,40,128]{2,1,0:T(8,128)S(1)}, f32[2,40,128]{2,1,0:T(8,128)S(1)}, u32[]{:S(2)}, u32[]{:S(2)}) %collective-permute-start.3) | collective-permute-done | bytes 40992 | tf_op jit(solution)/shard_map/ppermute | solution.py:327
  16.7 2.9 %collective-permute-start.4 = (f32[1,40,128]{2,1,0:T(8,128)S(1)}, f32[1,40,128]{2,1,0:T(8,128)S(1)}, u32[]{:S(2)}, u32[]{:S(2)}) collective-permute-start(f32[1,40,128]{2,1,0:T(8,128)S(1)} %get-tuple-element.21), channel_id=1, source_target_pairs={{0,8},{2,10},{4,12},{6,14},{8,0},{10,2},{12,4},{14,6},{1,9},{3,11}... | collective-permute-start | bytes 61448 | tf_op jit(solution)/shard_map/ppermute | solution.py:327
  19.6 1.9 %collective-permute-done.4.refs_1_ = f32[1,40,128]{2,1,0:T(8,128)S(1)} collective-permute-done((f32[1,40,128]{2,1,0:T(8,128)S(1)}, f32[1,40,128]{2,1,0:T(8,128)S(1)}, u32[]{:S(2)}, u32[]{:S(2)}) %collective-permute-start.4) | collective-permute-done | bytes 20512 | tf_op jit(solution)/shard_map/ppermute | solution.py:327
  21.5 1.0 %attend.1.refs_4_ = bf16[1,32,128]{2,1,0:T(8,128)(2,1)S(1)} custom-call(bf16[4096,2048]{1,0:T(8,128)(2,1)} %refs_5_.1, f32[8,128]{1,0:T(8,128)S(1)} %turning.1.turn_ref, bf16[1,2,2048,128]{3,2,1,0:T(8,128)(2,1)S(1)} %copy-done.2, bf16[1,2,2048,128]{3,2,1,0:T(8,128)(2,1)S(1)} %copy-done.3, f32[1,40,128]{2,1,0:T(8,128)S(1)} %get-tuple-element.22.refs_0_, ...), custom_call_target="tpu_custom_call" | custom-call | flops 33554432 | bytes 2097152 | tf_op jit(solution)/shard_map/attend/pallas_call | solution.py:256
  22.4 2.9 %collective-permute-start.5 = (bf16[1,32,128]{2,1,0:T(8,128)(2,1)S(1)}, bf16[1,32,128]{2,1,0:T(8,128)(2,1)S(1)}, u32[]{:S(2)}, u32[]{:S(2)}) collective-permute-start(bf16[1,32,128]{2,1,0:T(8,128)(2,1)S(1)} %attend.1.refs_4_), channel_id=1, source_target_pairs={{0,8},{2,10},{4,12},{6,14},{8,0},{10,2},{12,4},{14,6},{1,9},{3,11}... | collective-permute-start | bytes 24584 | tf_op jit(solution)/shard_map/ppermute | solution.py:327
  25.3 1.8 %collective-permute-done.5.refs_3_ = bf16[1,32,128]{2,1,0:T(8,128)(2,1)S(1)} collective-permute-done((bf16[1,32,128]{2,1,0:T(8,128)(2,1)S(1)}, bf16[1,32,128]{2,1,0:T(8,128)(2,1)S(1)}, u32[]{:S(2)}, u32[]{:S(2)}) %collective-permute-start.5) | collective-permute-done | bytes 8224 | tf_op jit(solution)/shard_map/ppermute | solution.py:327
  27.1 1.3 %collective-permute-start.6 = (bf16[2,32,128]{2,1,0:T(8,128)(2,1)S(1)}, bf16[2,32,128]{2,1,0:T(8,128)(2,1)S(1)}, u32[]{:S(2)}, u32[]{:S(2)}) collective-permute-start(bf16[2,32,128]{2,1,0:T(8,128)(2,1)S(1)} %pad_maximum_fusion), channel_id=1, source_target_pairs={{0,6},{2,4},{4,2},{6,0},{8,14},{10,12},{12,10},{14,8},{1,7},{3,5},... | collective-permute-start | bytes 49160 | tf_op jit(solution)/shard_map/ppermute | solution.py:327
  28.4 0.2 collective-permute-start.7
  28.6 2.0 %collective-permute-start.8 = (bf16[2,32,128]{2,1,0:T(8,128)(2,1)S(1)}, bf16[2,32,128]{2,1,0:T(8,128)(2,1)S(1)}, u32[]{:S(2)}, u32[]{:S(2)}) collective-permute-start(bf16[2,32,128]{2,1,0:T(8,128)(2,1)S(1)} %pad_maximum_fusion), channel_id=1, source_target_pairs={{0,4},{2,6},{4,0},{6,2},{8,12},{10,14},{12,8},{14,10},{1,5},{3,7},... | collective-permute-start | bytes 49160 | tf_op jit(solution)/shard_map/ppermute | solution.py:327
  30.6 1.1 %collective-permute-done.6.refs_0_ = bf16[2,32,128]{2,1,0:T(8,128)(2,1)S(1)} collective-permute-done((bf16[2,32,128]{2,1,0:T(8,128)(2,1)S(1)}, bf16[2,32,128]{2,1,0:T(8,128)(2,1)S(1)}, u32[]{:S(2)}, u32[]{:S(2)}) %collective-permute-start.6) | collective-permute-done | bytes 16416 | tf_op jit(solution)/shard_map/ppermute | solution.py:327
  31.8 0.4 %collective-permute-done.7.refs_1_ = bf16[2,32,128]{2,1,0:T(8,128)(2,1)S(1)} collective-permute-done((bf16[2,32,128]{2,1,0:T(8,128)(2,1)S(1)}, bf16[2,32,128]{2,1,0:T(8,128)(2,1)S(1)}, u32[]{:S(2)}, u32[]{:S(2)}) %collective-permute-start.7) | collective-permute-done | bytes 16416 | tf_op jit(solution)/shard_map/ppermute | solution.py:327
  32.2 0.2 collective-permute-done.8.refs_2_
  32.4 2.3 %output.1 = (f32[4,2048]{1,0:T(4,128)S(1)}, f32[4,2048]{1,0:T(4,128)S(1)}) custom-call(bf16[2,32,128]{2,1,0:T(8,128)(2,1)S(1)} %collective-permute-done.6.refs_0_, bf16[2,32,128]{2,1,0:T(8,128)(2,1)S(1)} %collective-permute-done.7.refs_1_, bf16[2,32,128]{2,1,0:T(8,128)(2,1)S(1)} %collective-permute-done.8.refs_2_, ...), custom_call_target="tpu_custom_call" | custom-call | flops 134217728 | bytes 16777216 | tf_op jit(solution)/shard_map/output/pallas_call | solution.py:308
  34.8 1.2 %collective-permute-done.9 = f32[4,2048]{1,0:T(4,128)S(1)} collective-permute-done((f32[4,2048]{1,0:T(4,128)S(1)}, f32[4,2048]{1,0:T(4,128)S(1)}, u32[]{:S(2)}, u32[]{:S(2)}) %collective-permute-start.9) | collective-permute-done | bytes 32800 | tf_op jit(solution)/shard_map/ppermute | solution.py:327
  36.0 0.6 %add_convert_fusion = bf16[4,2048]{1,0:T(4,128)(2,1)} fusion(f32[4,2048]{1,0:T(4,128)S(1)} %get-tuple-element.19, f32[4,2048]{1,0:T(4,128)S(1)} %collective-permute-done.9), kind=kLoop, calls=%fused_computation.1 | loop fusion | flops 16384 | bytes 81920 | tf_op jit(solution)/shard_map/convert_element_type | solution.py:370
  (26 shorter events, 0.2 us)
Async XLA Ops:
  0.0 2.2 %copy-start.4 = (bf16[4,2048]{1,0:T(4,128)(2,1)S(1)}, bf16[4,2048]{1,0:T(4,128)(2,1)}, u32[]{:S(2)}) copy-start(bf16[4,2048]{1,0:T(4,128)(2,1)} %rows_ref.1) | copy-start | bytes 49156
  0.0 2.2 %copy-start = (bf16[2048,256]{1,0:T(8,128)(2,1)S(1)}, bf16[2048,256]{1,0:T(8,128)(2,1)}, u32[]{:S(2)}) copy-start(bf16[2048,256]{1,0:T(8,128)(2,1)} %wk.1) | copy-start | bytes 3145732
  0.0 2.3 %copy-start.1 = (bf16[2048,256]{1,0:T(8,128)(2,1)S(1)}, bf16[2048,256]{1,0:T(8,128)(2,1)}, u32[]{:S(2)}) copy-start(bf16[2048,256]{1,0:T(8,128)(2,1)} %wv.1) | copy-start | bytes 3145732
  0.0 2.2 %collective-permute-start = (bf16[4,2048]{1,0:T(4,128)(2,1)}, bf16[4,2048]{1,0:T(4,128)(2,1)S(1)}, u32[]{:S(2)}, u32[]{:S(2)}) collective-permute-start(bf16[4,2048]{1,0:T(4,128)(2,1)} %rows_ref.1), channel_id=1, source_target_pairs={{0,1},{1,0},{2,3},{3,2},{4,5},{5,4},{6,7},{7,6},{8,9},{9,8},{10,11... | collective-permute-start | bytes 49160 | tf_op jit(solution)/shard_map/ppermute | solution.py:327
  2.2 19.2 %copy-start.2 = (bf16[1,2,2048,128]{3,2,1,0:T(8,128)(2,1)S(1)}, bf16[1,2,2048,128]{3,2,1,0:T(8,128)(2,1)}, u32[]{:S(2)}) copy-start(bf16[1,2,2048,128]{3,2,1,0:T(8,128)(2,1)} %k_ref.1) | copy-start | bytes 3145732
  2.2 19.2 %copy-start.3 = (bf16[1,2,2048,128]{3,2,1,0:T(8,128)(2,1)S(1)}, bf16[1,2,2048,128]{3,2,1,0:T(8,128)(2,1)}, u32[]{:S(2)}) copy-start(bf16[1,2,2048,128]{3,2,1,0:T(8,128)(2,1)} %v_ref.1) | copy-start | bytes 3145732
  8.1 6.0 %collective-permute-start.1 = (f32[2,40,128]{2,1,0:T(8,128)S(1)}, f32[2,40,128]{2,1,0:T(8,128)S(1)}, u32[]{:S(2)}, u32[]{:S(2)}) collective-permute-start(f32[2,40,128]{2,1,0:T(8,128)S(1)} %get-tuple-element.14), channel_id=1, source_target_pairs={{0,6},{2,4},{4,2},{6,0},{8,14},{10,12},{12,10},{14,8},{1,7},{3,5},... | collective-permute-start | bytes 122888 | tf_op jit(solution)/shard_map/ppermute | solution.py:327
  12.1 4.0 %collective-permute-start.2 = (f32[2,40,128]{2,1,0:T(8,128)S(1)}, f32[2,40,128]{2,1,0:T(8,128)S(1)}, u32[]{:S(2)}, u32[]{:S(2)}) collective-permute-start(f32[2,40,128]{2,1,0:T(8,128)S(1)} %get-tuple-element.15), channel_id=1, source_target_pairs={{0,2},{2,0},{4,6},{6,4},{8,10},{10,8},{12,14},{14,12},{1,3},{3,1},... | collective-permute-start | bytes 122888 | tf_op jit(solution)/shard_map/ppermute | solution.py:327
  12.7 4.0 %collective-permute-start.3 = (f32[2,40,128]{2,1,0:T(8,128)S(1)}, f32[2,40,128]{2,1,0:T(8,128)S(1)}, u32[]{:S(2)}, u32[]{:S(2)}) collective-permute-start(f32[2,40,128]{2,1,0:T(8,128)S(1)} %get-tuple-element.16), channel_id=1, source_target_pairs={{0,4},{2,6},{4,0},{6,2},{8,12},{10,14},{12,8},{14,10},{1,5},{3,7},... | collective-permute-start | bytes 122888 | tf_op jit(solution)/shard_map/ppermute | solution.py:327
  13.5 18.9 %slice-start = ((s8[16777216]{0:T(1024)(128)(4,1)}), s8[4194304]{0:T(1024)(128)(4,1)S(1)}, s32[]{:S(2)}) async-start(s8[16777216]{0:T(1024)(128)(4,1)} %bitcast.2), calls=%async_computation | async-start | bytes 8388608
  13.5 18.9 %slice-start.1 = ((s8[16777216]{0:T(1024)(128)(4,1)}), s8[4194304]{0:T(1024)(128)(4,1)S(1)}, s32[]{:S(2)}) async-start(s8[16777216]{0:T(1024)(128)(4,1)} %bitcast.2), calls=%async_computation.1 | async-start | bytes 8388608
  16.7 4.7 %collective-permute-start.4 = (f32[1,40,128]{2,1,0:T(8,128)S(1)}, f32[1,40,128]{2,1,0:T(8,128)S(1)}, u32[]{:S(2)}, u32[]{:S(2)}) collective-permute-start(f32[1,40,128]{2,1,0:T(8,128)S(1)} %get-tuple-element.21), channel_id=1, source_target_pairs={{0,8},{2,10},{4,12},{6,14},{8,0},{10,2},{12,4},{14,6},{1,9},{3,11}... | collective-permute-start | bytes 61448 | tf_op jit(solution)/shard_map/ppermute | solution.py:327
  21.5 10.9 %slice-start.2 = ((s8[16777216]{0:T(1024)(128)(4,1)}), s8[4194304]{0:T(1024)(128)(4,1)S(1)}, s32[]{:S(2)}) async-start(s8[16777216]{0:T(1024)(128)(4,1)} %bitcast.2), calls=%async_computation.2 | async-start | bytes 8388608
  21.5 10.9 %slice-start.3 = ((s8[16777216]{0:T(1024)(128)(4,1)}), s8[4194304]{0:T(1024)(128)(4,1)S(1)}, s32[]{:S(2)}) async-start(s8[16777216]{0:T(1024)(128)(4,1)} %bitcast.2), calls=%async_computation.3 | async-start | bytes 8388608
  22.4 4.7 %collective-permute-start.5 = (bf16[1,32,128]{2,1,0:T(8,128)(2,1)S(1)}, bf16[1,32,128]{2,1,0:T(8,128)(2,1)S(1)}, u32[]{:S(2)}, u32[]{:S(2)}) collective-permute-start(bf16[1,32,128]{2,1,0:T(8,128)(2,1)S(1)} %attend.1.refs_4_), channel_id=1, source_target_pairs={{0,8},{2,10},{4,12},{6,14},{8,0},{10,2},{12,4},{14,6},{1,9},{3,11}... | collective-permute-start | bytes 24584 | tf_op jit(solution)/shard_map/ppermute | solution.py:327
  27.1 4.6 %collective-permute-start.6 = (bf16[2,32,128]{2,1,0:T(8,128)(2,1)S(1)}, bf16[2,32,128]{2,1,0:T(8,128)(2,1)S(1)}, u32[]{:S(2)}, u32[]{:S(2)}) collective-permute-start(bf16[2,32,128]{2,1,0:T(8,128)(2,1)S(1)} %pad_maximum_fusion), channel_id=1, source_target_pairs={{0,6},{2,4},{4,2},{6,0},{8,14},{10,12},{12,10},{14,8},{1,7},{3,5},... | collective-permute-start | bytes 49160 | tf_op jit(solution)/shard_map/ppermute | solution.py:327
  28.4 3.7 %collective-permute-start.7 = (bf16[2,32,128]{2,1,0:T(8,128)(2,1)S(1)}, bf16[2,32,128]{2,1,0:T(8,128)(2,1)S(1)}, u32[]{:S(2)}, u32[]{:S(2)}) collective-permute-start(bf16[2,32,128]{2,1,0:T(8,128)(2,1)S(1)} %pad_maximum_fusion), channel_id=1, source_target_pairs={{0,2},{2,0},{4,6},{6,4},{8,10},{10,8},{12,14},{14,12},{1,3},{3,1},... | collective-permute-start | bytes 49160 | tf_op jit(solution)/shard_map/ppermute | solution.py:327
  28.6 3.7 %collective-permute-start.8 = (bf16[2,32,128]{2,1,0:T(8,128)(2,1)S(1)}, bf16[2,32,128]{2,1,0:T(8,128)(2,1)S(1)}, u32[]{:S(2)}, u32[]{:S(2)}) collective-permute-start(bf16[2,32,128]{2,1,0:T(8,128)(2,1)S(1)} %pad_maximum_fusion), channel_id=1, source_target_pairs={{0,4},{2,6},{4,0},{6,2},{8,12},{10,14},{12,8},{14,10},{1,5},{3,7},... | collective-permute-start | bytes 49160 | tf_op jit(solution)/shard_map/ppermute | solution.py:327
  34.7 1.3 %collective-permute-start.9 = (f32[4,2048]{1,0:T(4,128)S(1)}, f32[4,2048]{1,0:T(4,128)S(1)}, u32[]{:S(2)}, u32[]{:S(2)}) collective-permute-start(f32[4,2048]{1,0:T(4,128)S(1)} %get-tuple-element.20), channel_id=1, source_target_pairs={{0,1},{1,0},{2,3},{3,2},{4,5},{5,4},{6,7},{7,6},{8,9},{9,8},{10,11... | collective-permute-start | bytes 98312 | tf_op jit(solution)/shard_map/ppermute | solution.py:327

commit v14 on v13

--- a/solution.py
+++ b/solution.py
@@ -15,7 +15,49 @@
 FIRST = 256
 PIECES = 4
 FAN = 4
+BLOCK = 8
+TO_OWNERS = (
+    "--016-54",
+    "-210--75",
+    "203-54--",
+    "3---764-",
+    "13-2-7-6",
+)
+TO_ALL = (
+    "-0----45",
+    "--0-54--",
+    "32107654",
+    "1-3267--",
+    "23-1--76",
+)
 MIB = 2**20
+LAST = 2
+
+
+def pairs_of(order, devices):
+    return [
+        (block + g, block + int(to))
+        for block in range(0, devices, BLOCK)
+        for g, to in enumerate(order)
+        if to != "-"
+    ]
+
+
+def sent_pieces(order):
+    return [0 if to == "-" else bit_reverse(g ^ int(to), 2) for g, to in enumerate(order)]
+
+
+def arriving_pieces(order):
+    pieces = [FAN] * BLOCK
+    for g, to in enumerate(order):
+        if to != "-":
+            pieces[int(to)] = bit_reverse(g ^ int(to), 2)
+    return pieces
+
+
+def look_up(table, device):
+    packed = sum(entry << (4 * g) for g, entry in enumerate(table))
+    return (jnp.int32(packed) >> (4 * (device % BLOCK))) & 7
 
 
 def bit_reverse(value, bits):
@@ -106,7 +148,8 @@
 def project_kernel(
     bits, rows_ref, other_ref, wq_hbm, first, wk, wv, *refs
 ):
-    pieces, (wq, rows, sems) = refs[:FAN], refs[FAN:]
+    count = len(TO_OWNERS)
+    keep_ref, send_refs, (wq, rows, out, sems) = refs[0], refs[1 : 1 + count], refs[1 + count :]
     skip = first.shape[0]
     ranges = spread(wq_hbm.shape[0], skip, CHUNK)
     copies = [
@@ -141,17 +184,18 @@
             preferred_element_type=jnp.float32,
         )
 
-    total = pieces[0].shape[1]
+    total = out.shape[2]
     blocks = []
     for part in (sums, *fresh):
         blocks += [part[:, i : i + LANES] for i in range(0, part.shape[1], LANES)]
     blocks.append(jnp.broadcast_to(squares, (slots, LANES)))
     blocks += [jnp.zeros((slots, LANES), jnp.float32)] * (total - len(blocks))
-    size = slots // FAN
-    for at, ref in enumerate(pieces):
-        flat = ref.reshape(size * total, LANES)
-        for i, block in enumerate(blocks):
-            flat[pl.ds(i, size, stride=total), :] = block[at * size : (at + 1) * size]
+    flat = out.reshape(slots * total, LANES)
+    for i, block in enumerate(blocks):
+        flat[pl.ds(i, slots, stride=total), :] = block
+    keep_ref[...] = out[0]
+    for order, ref in zip(TO_OWNERS, send_refs):
+        ref[...] = out[look_up(sent_pieces(order), lax.axis_index("gx"))]
 
 
 def project(rows, other, w_query, first, key_weight, value_weight, slots):
@@ -166,12 +210,13 @@
     whole = pl.BlockSpec(memory_space=pltpu.VMEM)
     return pl.pallas_call(
         functools.partial(project_kernel, bits),
-        out_shape=(piece,) * FAN,
+        out_shape=(piece,) * (1 + len(TO_OWNERS)),
         in_specs=[whole, whole, hbm, whole, whole, whole],
-        out_specs=(whole,) * FAN,
+        out_specs=(whole,) * (1 + len(TO_OWNERS)),
         scratch_shapes=[
             pltpu.VMEM((max(depth - skip, 16), query_width), jnp.bfloat16),
             pltpu.VMEM((slots, depth), jnp.float32),
+            pltpu.VMEM((FAN, slots // FAN, total, LANES), jnp.float32),
             pltpu.SemaphoreType.DMA((max(1, len(spread(depth, skip, CHUNK))), PIECES)),
         ],
         compiler_params=pltpu.CompilerParams(vmem_limit_bytes=46 * MIB),
@@ -268,16 +313,18 @@
     )(in_hbm(beside), turn, k_cache, value_cache, *parts)
 
 
-def output_kernel(bits, pieces, *refs):
-    parts = refs[:pieces][::-1]
-    w_ref, mine_ref, theirs_ref, flat, left, sums = refs[pieces:]
+def output_kernel(bits, held_ref, *refs):
+    count = len(TO_ALL)
+    arrived, (w_ref, mine_ref, theirs_ref, flat, left, sums) = refs[:count], refs[count:]
     slots = left.shape[0]
-    heads = flat.shape[0] // slots
-    at = 0
-    for ref in parts:
-        for i in range(ref.shape[0]):
-            flat[at : at + heads, :] = ref[i].astype(jnp.float32)
-            at += heads
+    size, heads = held_ref.shape[:2]
+    rows = size * heads
+    flat[:rows, :] = held_ref[...].reshape(rows, HEAD_SIZE).astype(jnp.float32)
+    for order, ref in zip(TO_ALL[-LAST:] + TO_ALL[:-LAST], arrived):
+        piece = look_up(arriving_pieces(order), lax.axis_index("gx"))
+        flat[pl.ds(pl.multiple_of(piece * rows, rows), rows), :] = (
+            ref[...].reshape(rows, HEAD_SIZE).astype(jnp.float32)
+        )
     for head in range(heads):
         left[:, head * HEAD_SIZE : (head + 1) * HEAD_SIZE] = flat[
             pl.ds(head, slots, stride=heads), :
@@ -299,19 +346,19 @@
             ref[t : t + 1, :] = sums[pl.ds(slot, 1), :]
 
 
-def output(parts, w_out, slots):
+def output(held, arrived, w_out, slots):
     bits = slots.bit_length() - 1
     depth, width = w_out.shape
     heads = depth // HEAD_SIZE
     whole = pl.BlockSpec(memory_space=pltpu.VMEM)
     piece = jax.ShapeDtypeStruct((slots // 2, width), jnp.float32)
     return pl.pallas_call(
-        functools.partial(output_kernel, bits, len(parts)),
+        functools.partial(output_kernel, bits),
         out_shape=(piece, piece),
-        in_specs=[whole] * (len(parts) + 1),
+        in_specs=[whole] * (2 + len(arrived)),
         out_specs=(whole, whole),
         scratch_shapes=[
-            pltpu.VMEM((slots * heads, HEAD_SIZE), jnp.float32),
+            pltpu.VMEM((slots // FAN * (FAN + 1) * heads, HEAD_SIZE), jnp.float32),
             pltpu.VMEM((slots, depth), jnp.bfloat16),
             pltpu.VMEM((slots, width), jnp.float32),
         ],
@@ -320,19 +367,11 @@
             flops=2 * slots * depth * width, bytes_accessed=2 * depth * width, transcendentals=0
         ),
         name="output",
-    )(*parts, w_out)
+    )(held, *arrived, w_out)
 
 
 def swap(block, axis, devices, mask):
     return lax.ppermute(block, axis, [(i, i ^ mask) for i in range(devices)])
-
-
-def fan(pieces, devices):
-    masks = [bit_reverse(q, 2) for q in range(FAN)]
-    arrived = [None] * FAN
-    for q in sorted(range(1, FAN), key=lambda q: (masks[q] + 1) % FAN):
-        arrived[q] = swap(pieces[q], "gx", devices, masks[q])
-    return arrived[1:]
 
 
 def body(devices, activations, w_query, key_weight, value_weight, w_out, k_cache, value_cache, lengths):
@@ -341,16 +380,18 @@
     other = swap(activations, "gy", 2, 1)
     depth = w_query.shape[0]
     first = stage_rows(w_query, min(FIRST, depth))
-    pieces = project(activations, other, w_query, first, key_weight, value_weight, slots)
-
-    arrived = fan(pieces, devices)
+    keep, *sends = project(activations, other, w_query, first, key_weight, value_weight, slots)
+
+    arrived = [
+        lax.ppermute(send, "gx", pairs_of(order, devices)) for order, send in zip(TO_OWNERS, sends)
+    ]
     half = HEAD_SIZE // 2
     frequency = jnp.power(
         jnp.float32(500000.0), -2.0 * jnp.arange(half, dtype=jnp.float32) / HEAD_SIZE
     )
     frequency = jnp.concatenate([frequency, frequency])[None, :]
     turn = turning(lengths, frequency, w_out)
-    total = pieces[0] + (arrived[2] + (arrived[1] + arrived[0]))
+    total = keep + functools.reduce(lambda later, earlier: earlier + later, arrived[::-1])
     mask = FAN
     while total.shape[0] > 2:
         rest = total.shape[0] // 2
@@ -365,8 +406,9 @@
         mask //= 2
         parts.append(swap(jnp.concatenate(parts, axis=0), "gx", devices, mask))
     held = jnp.concatenate(parts, axis=0)
-    parts += fan([held] * FAN, devices)
-    mine, theirs = output(parts[::-1], w_out, slots)
+    arrived = [lax.ppermute(held, "gx", pairs_of(order, devices)) for order in TO_ALL]
+    arrived = arrived[-LAST:] + arrived[:-LAST]
+    mine, theirs = output(held, arrived, w_out, slots)
     return (mine + swap(theirs, "gy", 2, 1)).astype(jnp.bfloat16)
 
 

time: 36.8 us -> 49.1 us (1.33)
  the two profiles are of different devices: /device:TPU:0 before, /device:TPU:15 now
where the time goes in v14:
time: 49.1 us; the launch traced here: 48.8 us
  starting transfers between devices  30.3 us (62%)
  Pallas kernels  10.7 us (22%)
  waiting for transfers between devices  5.99 us (12%)
  between operations  0.91 us (2%)
  other arithmetic  0.73 us (1%)
    ppermute x4, starting transfers between devices, swap(): return lax.ppermute(block, axis, [(i, i ^ mask) for i in range(devices)])  13.3 us
    ppermute x5, starting transfers between devices, body(): lax.ppermute(send, 'gx', pairs_of(order, devices))  9.31 us
    ppermute x5, starting transfers between devices, body(): lax.ppermute(held, 'gx', pairs_of(order, devices))  7.69 us
    pallas_call x1, Pallas kernels, project(): pl.pallas_call(functools.partial(project_kernel, bits), out_shape=(piece,...  5.86 us
    ppermute x4, waiting for transfers between devices, swap(): return lax.ppermute(block, axis, [(i, i ^ mask) for i in range(devices)])  3.08 us
    ppermute x5, waiting for transfers between devices, body(): lax.ppermute(held, 'gx', pairs_of(order, devices))  2.34 us
    pallas_call x1, Pallas kernels, output(): pl.pallas_call(functools.partial(output_kernel, bits), out_shape=(piece,...  2.3 us
    pallas_call x1, Pallas kernels, stage_rows(): pl.pallas_call(functools.partial(stage_kernel, rows), out_shape=jax.Shape...  1.55 us
  transfers between devices with their start and end apart: 14, of which 5 were waited for; matrix products, arithmetic and copies ran while one was open for 0% of the time, Pallas kernels for 3%

profile of v14, /device:TPU:15, one launch (start us, length us, event | category | flops | bytes accessed | tf_op | source)
XLA Modules:
  0.0 48.8 jit_solution(1584825408715535682)
XLA Ops:
  0.0 0.7 %collective-permute-start = (bf16[4,2048]{1,0:T(4,128)(2,1)}, bf16[4,2048]{1,0:T(4,128)(2,1)S(1)}, u32[]{:S(2)}, u32[]{:S(2)}) collective-permute-start(bf16[4,2048]{1,0:T(4,128)(2,1)} %rows_ref.1), channel_id=1, source_target_pairs={{0,1},{1,0},{2,3},{3,2},{4,5},{5,4},{6,7},{7,6},{8,9},{9,8},{10,11... | collective-permute-start | bytes 49160 | tf_op jit(solution)/shard_map/ppermute | solution.py:374
  0.8 1.6 %stage.1.first = bf16[256,4096]{1,0:T(8,128)(2,1)S(1)} custom-call(bf16[2048,4096]{1,0:T(8,128)(2,1)} %wq_hbm.1), custom_call_target="tpu_custom_call" | custom-call | bytes 2097152 | tf_op jit(solution)/shard_map/stage/pallas_call | solution.py:99
  2.4 5.9 %project.1 = (f32[2,40,128]{2,1,0:T(8,128)S(1)}, f32[2,40,128]{2,1,0:T(8,128)S(1)}, f32[2,40,128]{2,1,0:T(8,128)S(1)}, f32[2,40,128]{2,1,0:T(8,128)S(1)}, f32[2,...) custom-call(bf16[4,2048]{1,0:T(4,128)(2,1)S(1)} %copy-done.4, bf16[4,2048]{1,0:T(4,128)(2,1)S(1)} %collective-permute-done.other_ref, ...), custom_call_target="tpu_custom_call" | custom-call | flops 150994944 | bytes 18874368 | tf_op jit(solution)/shard_map/project/pallas_call | solution.py:211
  8.3 2.1 %collective-permute-start.1 = (f32[2,40,128]{2,1,0:T(8,128)S(1)}, f32[2,40,128]{2,1,0:T(8,128)S(1)}, u32[]{:S(2)}, u32[]{:S(2)}) collective-permute-start(f32[2,40,128]{2,1,0:T(8,128)S(1)} %get-tuple-element.16), channel_id=1, source_target_pairs={{4,0},{6,2},{8,12},{12,10},{14,8},{5,1},{7,3},{9,13},{13,11},{15,9... | collective-permute-start | bytes 122888 | tf_op jit(solution)/shard_map/ppermute | solution.py:386
  10.3 1.3 %collective-permute-start.2 = (f32[2,40,128]{2,1,0:T(8,128)S(1)}, f32[2,40,128]{2,1,0:T(8,128)S(1)}, u32[]{:S(2)}, u32[]{:S(2)}) collective-permute-start(f32[2,40,128]{2,1,0:T(8,128)S(1)} %get-tuple-element.17), channel_id=1, source_target_pairs={{2,4},{4,2},{6,0},{12,14},{14,10},{3,5},{5,3},{7,1},{13,15},{15,11... | collective-permute-start | bytes 122888 | tf_op jit(solution)/shard_map/ppermute | solution.py:386
  11.6 1.3 %collective-permute-start.3 = (f32[2,40,128]{2,1,0:T(8,128)S(1)}, f32[2,40,128]{2,1,0:T(8,128)S(1)}, u32[]{:S(2)}, u32[]{:S(2)}) collective-permute-start(f32[2,40,128]{2,1,0:T(8,128)S(1)} %get-tuple-element.18), channel_id=1, source_target_pairs={{0,4},{2,0},{4,6},{8,10},{10,8},{1,5},{3,1},{5,7},{9,11},{11,9},{1... | collective-permute-start | bytes 122888 | tf_op jit(solution)/shard_map/ppermute | solution.py:386
  12.9 1.3 %collective-permute-start.4 = (f32[2,40,128]{2,1,0:T(8,128)S(1)}, f32[2,40,128]{2,1,0:T(8,128)S(1)}, u32[]{:S(2)}, u32[]{:S(2)}) collective-permute-start(f32[2,40,128]{2,1,0:T(8,128)S(1)} %get-tuple-element.19), channel_id=1, source_target_pairs={{0,6},{8,14},{10,12},{12,8},{1,7},{9,15},{11,13},{13,9},{16,22},{2... | collective-permute-start | bytes 122888 | tf_op jit(solution)/shard_map/ppermute | solution.py:386
  14.2 3.4 %collective-permute-start.5 = (f32[2,40,128]{2,1,0:T(8,128)S(1)}, f32[2,40,128]{2,1,0:T(8,128)S(1)}, u32[]{:S(2)}, u32[]{:S(2)}) collective-permute-start(f32[2,40,128]{2,1,0:T(8,128)S(1)} %get-tuple-element.20), channel_id=1, source_target_pairs={{0,2},{2,6},{6,4},{10,14},{14,12},{1,3},{3,7},{7,5},{11,15},{15,13... | collective-permute-start | bytes 122888 | tf_op jit(solution)/shard_map/ppermute | solution.py:386
  18.4 0.6 %collective-permute-done.4 = f32[2,40,128]{2,1,0:T(8,128)S(1)} collective-permute-done((f32[2,40,128]{2,1,0:T(8,128)S(1)}, f32[2,40,128]{2,1,0:T(8,128)S(1)}, u32[]{:S(2)}, u32[]{:S(2)}) %collective-permute-start.4) | collective-permute-done | bytes 40992 | tf_op jit(solution)/shard_map/ppermute | solution.py:386
  19.0 3.7 %collective-permute-start.6 = (f32[1,40,128]{2,1,0:T(8,128)S(1)}, f32[1,40,128]{2,1,0:T(8,128)S(1)}, u32[]{:S(2)}, u32[]{:S(2)}) collective-permute-start(f32[1,40,128]{2,1,0:T(8,128)S(1)} %get-tuple-element.25), channel_id=1, source_target_pairs={{0,8},{2,10},{4,12},{6,14},{8,0},{10,2},{12,4},{14,6},{1,9},{3,11}... | collective-permute-start | bytes 61448 | tf_op jit(solution)/shard_map/ppermute | solution.py:374
  22.7 1.2 %collective-permute-done.6.refs_1_ = f32[1,40,128]{2,1,0:T(8,128)S(1)} collective-permute-done((f32[1,40,128]{2,1,0:T(8,128)S(1)}, f32[1,40,128]{2,1,0:T(8,128)S(1)}, u32[]{:S(2)}, u32[]{:S(2)}) %collective-permute-start.6) | collective-permute-done | bytes 20512 | tf_op jit(solution)/shard_map/ppermute | solution.py:374
  23.9 1.0 %attend.1 = bf16[1,32,128]{2,1,0:T(8,128)(2,1)S(1)} custom-call(bf16[4096,2048]{1,0:T(8,128)(2,1)} %refs_5_.1, f32[8,128]{1,0:T(8,128)S(1)} %turning.1.turn_ref, bf16[1,2,2048,128]{3,2,1,0:T(8,128)(2,1)S(1)} %copy-done.2, bf16[1,2,2048,128]{3,2,1,0:T(8,128)(2,1)S(1)} %copy-done.3, f32[1,40,128]{2,1,0:T(8,128)S(1)} %get-tuple-element.26.refs_0_, ...), custom_call_target="tpu_custom_call" | custom-call | flops 33554432 | bytes 2097152 | tf_op jit(solution)/shard_map/attend/pallas_call | solution.py:301
  24.9 2.4 %collective-permute-start.7 = (bf16[1,32,128]{2,1,0:T(8,128)(2,1)S(1)}, bf16[1,32,128]{2,1,0:T(8,128)(2,1)S(1)}, u32[]{:S(2)}, u32[]{:S(2)}) collective-permute-start(bf16[1,32,128]{2,1,0:T(8,128)(2,1)S(1)} %attend.1), channel_id=1, source_target_pairs={{0,8},{2,10},{4,12},{6,14},{8,0},{10,2},{12,4},{14,6},{1,9},{3,11}... | collective-permute-start | bytes 24584 | tf_op jit(solution)/shard_map/ppermute | solution.py:374
  27.3 1.0 %collective-permute-done.7 = bf16[1,32,128]{2,1,0:T(8,128)(2,1)S(1)} collective-permute-done((bf16[1,32,128]{2,1,0:T(8,128)(2,1)S(1)}, bf16[1,32,128]{2,1,0:T(8,128)(2,1)S(1)}, u32[]{:S(2)}, u32[]{:S(2)}) %collective-permute-start.7) | collective-permute-done | bytes 8224 | tf_op jit(solution)/shard_map/ppermute | solution.py:374
  28.3 0.7 %collective-permute-start.10 = (bf16[2,32,128]{2,1,0:T(8,128)(2,1)S(1)}, bf16[2,32,128]{2,1,0:T(8,128)(2,1)S(1)}, u32[]{:S(2)}, u32[]{:S(2)}) collective-permute-start(bf16[2,32,128]{2,1,0:T(8,128)(2,1)S(1)} %pad_maximum_fusion.held_ref), channel_id=1, source_target_pairs={{2,0},{12,8},{14,10},{3,1},{13,9},{15,11},{18,16},{28,24},{30,26},... | collective-permute-start | bytes 49160 | tf_op jit(solution)/shard_map/ppermute | solution.py:409
  29.0 0.7 %collective-permute-start.11 = (bf16[2,32,128]{2,1,0:T(8,128)(2,1)S(1)}, bf16[2,32,128]{2,1,0:T(8,128)(2,1)S(1)}, u32[]{:S(2)}, u32[]{:S(2)}) collective-permute-start(bf16[2,32,128]{2,1,0:T(8,128)(2,1)S(1)} %pad_maximum_fusion.held_ref), channel_id=1, source_target_pairs={{4,0},{8,10},{10,8},{5,1},{9,11},{11,9},{20,16},{24,26},{26,24},{2... | collective-permute-start | bytes 49160 | tf_op jit(solution)/shard_map/ppermute | solution.py:409
  29.7 0.9 %collective-permute-start.12 = (bf16[2,32,128]{2,1,0:T(8,128)(2,1)S(1)}, bf16[2,32,128]{2,1,0:T(8,128)(2,1)S(1)}, u32[]{:S(2)}, u32[]{:S(2)}) collective-permute-start(bf16[2,32,128]{2,1,0:T(8,128)(2,1)S(1)} %pad_maximum_fusion.held_ref), channel_id=1, source_target_pairs={{0,6},{2,4},{4,2},{6,0},{8,14},{10,12},{12,10},{14,8},{1,7},{3,5},... | collective-permute-start | bytes 49160 | tf_op jit(solution)/shard_map/ppermute | solution.py:409
  30.6 3.3 %collective-permute-start.8 = (bf16[2,32,128]{2,1,0:T(8,128)(2,1)S(1)}, bf16[2,32,128]{2,1,0:T(8,128)(2,1)S(1)}, u32[]{:S(2)}, u32[]{:S(2)}) collective-permute-start(bf16[2,32,128]{2,1,0:T(8,128)(2,1)S(1)} %pad_maximum_fusion.held_ref), channel_id=1, source_target_pairs={{0,2},{4,6},{6,4},{8,12},{10,14},{1,3},{5,7},{7,5},{9,13},{11,15},... | collective-permute-start | bytes 49160 | tf_op jit(solution)/shard_map/ppermute | solution.py:409
  33.9 2.1 %collective-permute-start.9 = (bf16[2,32,128]{2,1,0:T(8,128)(2,1)S(1)}, bf16[2,32,128]{2,1,0:T(8,128)(2,1)S(1)}, u32[]{:S(2)}, u32[]{:S(2)}) collective-permute-start(bf16[2,32,128]{2,1,0:T(8,128)(2,1)S(1)} %pad_maximum_fusion.held_ref), channel_id=1, source_target_pairs={{0,4},{2,6},{6,2},{12,14},{14,12},{1,5},{3,7},{7,3},{13,15},{15,13... | collective-permute-start | bytes 49160 | tf_op jit(solution)/shard_map/ppermute | solution.py:409
  36.1 2.3 %collective-permute-done.9.refs_1_ = bf16[2,32,128]{2,1,0:T(8,128)(2,1)S(1)} collective-permute-done((bf16[2,32,128]{2,1,0:T(8,128)(2,1)S(1)}, bf16[2,32,128]{2,1,0:T(8,128)(2,1)S(1)}, u32[]{:S(2)}, u32[]{:S(2)}) %collective-permute-start.9) | collective-permute-done | bytes 16416 | tf_op jit(solution)/shard_map/ppermute | solution.py:409
  38.4 2.3 %output.1 = (f32[4,2048]{1,0:T(4,128)S(1)}, f32[4,2048]{1,0:T(4,128)S(1)}) custom-call(bf16[2,32,128]{2,1,0:T(8,128)(2,1)S(1)} %pad_maximum_fusion.held_ref, bf16[2,32,128]{2,1,0:T(8,128)(2,1)S(1)} %collective-permute-done.8.refs_0_, bf16[2,32,128]{2,1,0:T(8,128)(2,1)S(1)} %collective-permute-done.9.refs_1_, ...), custom_call_target="tpu_custom_call" | custom-call | flops 134217728 | bytes 16777216 | tf_op jit(solution)/shard_map/output/pallas_call | solution.py:355
  40.8 6.5 %collective-permute-start.13 = (f32[4,2048]{1,0:T(4,128)S(1)}, f32[4,2048]{1,0:T(4,128)S(1)}, u32[]{:S(2)}, u32[]{:S(2)}) collective-permute-start(f32[4,2048]{1,0:T(4,128)S(1)} %get-tuple-element.24), channel_id=1, source_target_pairs={{0,1},{1,0},{2,3},{3,2},{4,5},{5,4},{6,7},{7,6},{8,9},{9,8},{10,11... | collective-permute-start | bytes 98312 | tf_op jit(solution)/shard_map/ppermute | solution.py:374
  47.3 0.9 %collective-permute-done.13 = f32[4,2048]{1,0:T(4,128)S(1)} collective-permute-done((f32[4,2048]{1,0:T(4,128)S(1)}, f32[4,2048]{1,0:T(4,128)S(1)}, u32[]{:S(2)}, u32[]{:S(2)}) %collective-permute-start.13) | collective-permute-done | bytes 32800 | tf_op jit(solution)/shard_map/ppermute | solution.py:374
  48.1 0.6 %add_convert_fusion = bf16[4,2048]{1,0:T(4,128)(2,1)} fusion(f32[4,2048]{1,0:T(4,128)S(1)} %get-tuple-element.23, f32[4,2048]{1,0:T(4,128)S(1)} %collective-permute-done.13), kind=kLoop, calls=%fused_computation.1 | loop fusion | flops 16384 | bytes 81920 | tf_op jit(solution)/shard_map/convert_element_type | solution.py:412
  (34 shorter events, 0.2 us)
Async XLA Ops:
  0.0 2.4 %copy-start.4 = (bf16[4,2048]{1,0:T(4,128)(2,1)S(1)}, bf16[4,2048]{1,0:T(4,128)(2,1)}, u32[]{:S(2)}) copy-start(bf16[4,2048]{1,0:T(4,128)(2,1)} %rows_ref.1) | copy-start | bytes 49156
  0.0 2.4 %copy-start = (bf16[2048,256]{1,0:T(8,128)(2,1)S(1)}, bf16[2048,256]{1,0:T(8,128)(2,1)}, u32[]{:S(2)}) copy-start(bf16[2048,256]{1,0:T(8,128)(2,1)} %wk.1) | copy-start | bytes 3145732
  0.0 2.4 %copy-start.1 = (bf16[2048,256]{1,0:T(8,128)(2,1)S(1)}, bf16[2048,256]{1,0:T(8,128)(2,1)}, u32[]{:S(2)}) copy-start(bf16[2048,256]{1,0:T(8,128)(2,1)} %wv.1) | copy-start | bytes 3145732
  0.0 2.3 %collective-permute-start = (bf16[4,2048]{1,0:T(4,128)(2,1)}, bf16[4,2048]{1,0:T(4,128)(2,1)S(1)}, u32[]{:S(2)}, u32[]{:S(2)}) collective-permute-start(bf16[4,2048]{1,0:T(4,128)(2,1)} %rows_ref.1), channel_id=1, source_target_pairs={{0,1},{1,0},{2,3},{3,2},{4,5},{5,4},{6,7},{7,6},{8,9},{9,8},{10,11... | collective-permute-start | bytes 49160 | tf_op jit(solution)/shard_map/ppermute | solution.py:374
  2.3 21.6 %copy-start.2 = (bf16[1,2,2048,128]{3,2,1,0:T(8,128)(2,1)S(1)}, bf16[1,2,2048,128]{3,2,1,0:T(8,128)(2,1)}, u32[]{:S(2)}) copy-start(bf16[1,2,2048,128]{3,2,1,0:T(8,128)(2,1)} %k_ref.1) | copy-start | bytes 3145732
  2.3 21.6 %copy-start.3 = (bf16[1,2,2048,128]{3,2,1,0:T(8,128)(2,1)S(1)}, bf16[1,2,2048,128]{3,2,1,0:T(8,128)(2,1)}, u32[]{:S(2)}) copy-start(bf16[1,2,2048,128]{3,2,1,0:T(8,128)(2,1)} %v_ref.1) | copy-start | bytes 3145732
  8.3 10.2 %collective-permute-start.1 = (f32[2,40,128]{2,1,0:T(8,128)S(1)}, f32[2,40,128]{2,1,0:T(8,128)S(1)}, u32[]{:S(2)}, u32[]{:S(2)}) collective-permute-start(f32[2,40,128]{2,1,0:T(8,128)S(1)} %get-tuple-element.16), channel_id=1, source_target_pairs={{4,0},{6,2},{8,12},{12,10},{14,8},{5,1},{7,3},{9,13},{13,11},{15,9... | collective-permute-start | bytes 122888 | tf_op jit(solution)/shard_map/ppermute | solution.py:386
  10.3 8.1 %collective-permute-start.2 = (f32[2,40,128]{2,1,0:T(8,128)S(1)}, f32[2,40,128]{2,1,0:T(8,128)S(1)}, u32[]{:S(2)}, u32[]{:S(2)}) collective-permute-start(f32[2,40,128]{2,1,0:T(8,128)S(1)} %get-tuple-element.17), channel_id=1, source_target_pairs={{2,4},{4,2},{6,0},{12,14},{14,10},{3,5},{5,3},{7,1},{13,15},{15,11... | collective-permute-start | bytes 122888 | tf_op jit(solution)/shard_map/ppermute | solution.py:386
  11.6 6.8 %collective-permute-start.3 = (f32[2,40,128]{2,1,0:T(8,128)S(1)}, f32[2,40,128]{2,1,0:T(8,128)S(1)}, u32[]{:S(2)}, u32[]{:S(2)}) collective-permute-start(f32[2,40,128]{2,1,0:T(8,128)S(1)} %get-tuple-element.18), channel_id=1, source_target_pairs={{0,4},{2,0},{4,6},{8,10},{10,8},{1,5},{3,1},{5,7},{9,11},{11,9},{1... | collective-permute-start | bytes 122888 | tf_op jit(solution)/shard_map/ppermute | solution.py:386
  12.9 6.1 %collective-permute-start.4 = (f32[2,40,128]{2,1,0:T(8,128)S(1)}, f32[2,40,128]{2,1,0:T(8,128)S(1)}, u32[]{:S(2)}, u32[]{:S(2)}) collective-permute-start(f32[2,40,128]{2,1,0:T(8,128)S(1)} %get-tuple-element.19), channel_id=1, source_target_pairs={{0,6},{8,14},{10,12},{12,8},{1,7},{9,15},{11,13},{13,9},{16,22},{2... | collective-permute-start | bytes 122888 | tf_op jit(solution)/shard_map/ppermute | solution.py:386
  14.2 4.8 %collective-permute-start.5 = (f32[2,40,128]{2,1,0:T(8,128)S(1)}, f32[2,40,128]{2,1,0:T(8,128)S(1)}, u32[]{:S(2)}, u32[]{:S(2)}) collective-permute-start(f32[2,40,128]{2,1,0:T(8,128)S(1)} %get-tuple-element.20), channel_id=1, source_target_pairs={{0,2},{2,6},{6,4},{10,14},{14,12},{1,3},{3,7},{7,5},{11,15},{15,13... | collective-permute-start | bytes 122888 | tf_op jit(solution)/shard_map/ppermute | solution.py:386
  18.3 20.1 %slice-start = ((s8[16777216]{0:T(1024)(128)(4,1)}), s8[4194304]{0:T(1024)(128)(4,1)S(1)}, s32[]{:S(2)}) async-start(s8[16777216]{0:T(1024)(128)(4,1)} %bitcast.2), calls=%async_computation | async-start | bytes 8388608
  18.3 20.1 %slice-start.1 = ((s8[16777216]{0:T(1024)(128)(4,1)}), s8[4194304]{0:T(1024)(128)(4,1)S(1)}, s32[]{:S(2)}) async-start(s8[16777216]{0:T(1024)(128)(4,1)} %bitcast.2), calls=%async_computation.1 | async-start | bytes 8388608
  19.0 4.8 %collective-permute-start.6 = (f32[1,40,128]{2,1,0:T(8,128)S(1)}, f32[1,40,128]{2,1,0:T(8,128)S(1)}, u32[]{:S(2)}, u32[]{:S(2)}) collective-permute-start(f32[1,40,128]{2,1,0:T(8,128)S(1)} %get-tuple-element.25), channel_id=1, source_target_pairs={{0,8},{2,10},{4,12},{6,14},{8,0},{10,2},{12,4},{14,6},{1,9},{3,11}... | collective-permute-start | bytes 61448 | tf_op jit(solution)/shard_map/ppermute | solution.py:374
  23.9 14.5 %slice-start.2 = ((s8[16777216]{0:T(1024)(128)(4,1)}), s8[4194304]{0:T(1024)(128)(4,1)S(1)}, s32[]{:S(2)}) async-start(s8[16777216]{0:T(1024)(128)(4,1)} %bitcast.2), calls=%async_computation.2 | async-start | bytes 8388608
  23.9 14.5 %slice-start.3 = ((s8[16777216]{0:T(1024)(128)(4,1)}), s8[4194304]{0:T(1024)(128)(4,1)S(1)}, s32[]{:S(2)}) async-start(s8[16777216]{0:T(1024)(128)(4,1)} %bitcast.2), calls=%async_computation.3 | async-start | bytes 8388608
  24.9 3.5 %collective-permute-start.7 = (bf16[1,32,128]{2,1,0:T(8,128)(2,1)S(1)}, bf16[1,32,128]{2,1,0:T(8,128)(2,1)S(1)}, u32[]{:S(2)}, u32[]{:S(2)}) collective-permute-start(bf16[1,32,128]{2,1,0:T(8,128)(2,1)S(1)} %attend.1), channel_id=1, source_target_pairs={{0,8},{2,10},{4,12},{6,14},{8,0},{10,2},{12,4},{14,6},{1,9},{3,11}... | collective-permute-start | bytes 24584 | tf_op jit(solution)/shard_map/ppermute | solution.py:374
  28.3 7.7 %collective-permute-start.10 = (bf16[2,32,128]{2,1,0:T(8,128)(2,1)S(1)}, bf16[2,32,128]{2,1,0:T(8,128)(2,1)S(1)}, u32[]{:S(2)}, u32[]{:S(2)}) collective-permute-start(bf16[2,32,128]{2,1,0:T(8,128)(2,1)S(1)} %pad_maximum_fusion.held_ref), channel_id=1, source_target_pairs={{2,0},{12,8},{14,10},{3,1},{13,9},{15,11},{18,16},{28,24},{30,26},... | collective-permute-start | bytes 49160 | tf_op jit(solution)/shard_map/ppermute | solution.py:409
  29.0 7.1 %collective-permute-start.11 = (bf16[2,32,128]{2,1,0:T(8,128)(2,1)S(1)}, bf16[2,32,128]{2,1,0:T(8,128)(2,1)S(1)}, u32[]{:S(2)}, u32[]{:S(2)}) collective-permute-start(bf16[2,32,128]{2,1,0:T(8,128)(2,1)S(1)} %pad_maximum_fusion.held_ref), channel_id=1, source_target_pairs={{4,0},{8,10},{10,8},{5,1},{9,11},{11,9},{20,16},{24,26},{26,24},{2... | collective-permute-start | bytes 49160 | tf_op jit(solution)/shard_map/ppermute | solution.py:409
  29.7 6.4 %collective-permute-start.12 = (bf16[2,32,128]{2,1,0:T(8,128)(2,1)S(1)}, bf16[2,32,128]{2,1,0:T(8,128)(2,1)S(1)}, u32[]{:S(2)}, u32[]{:S(2)}) collective-permute-start(bf16[2,32,128]{2,1,0:T(8,128)(2,1)S(1)} %pad_maximum_fusion.held_ref), channel_id=1, source_target_pairs={{0,6},{2,4},{4,2},{6,0},{8,14},{10,12},{12,10},{14,8},{1,7},{3,5},... | collective-permute-start | bytes 49160 | tf_op jit(solution)/shard_map/ppermute | solution.py:409
  30.6 5.5 %collective-permute-start.8 = (bf16[2,32,128]{2,1,0:T(8,128)(2,1)S(1)}, bf16[2,32,128]{2,1,0:T(8,128)(2,1)S(1)}, u32[]{:S(2)}, u32[]{:S(2)}) collective-permute-start(bf16[2,32,128]{2,1,0:T(8,128)(2,1)S(1)} %pad_maximum_fusion.held_ref), channel_id=1, source_target_pairs={{0,2},{4,6},{6,4},{8,12},{10,14},{1,3},{5,7},{7,5},{9,13},{11,15},... | collective-permute-start | bytes 49160 | tf_op jit(solution)/shard_map/ppermute | solution.py:409
  33.9 4.5 %collective-permute-start.9 = (bf16[2,32,128]{2,1,0:T(8,128)(2,1)S(1)}, bf16[2,32,128]{2,1,0:T(8,128)(2,1)S(1)}, u32[]{:S(2)}, u32[]{:S(2)}) collective-permute-start(bf16[2,32,128]{2,1,0:T(8,128)(2,1)S(1)} %pad_maximum_fusion.held_ref), channel_id=1, source_target_pairs={{0,4},{2,6},{6,2},{12,14},{14,12},{1,5},{3,7},{7,3},{13,15},{15,13... | collective-permute-start | bytes 49160 | tf_op jit(solution)/shard_map/ppermute | solution.py:409
  40.8 7.4 %collective-permute-start.13 = (f32[4,2048]{1,0:T(4,128)S(1)}, f32[4,2048]{1,0:T(4,128)S(1)}, u32[]{:S(2)}, u32[]{:S(2)}) collective-permute-start(f32[4,2048]{1,0:T(4,128)S(1)} %get-tuple-element.24), channel_id=1, source_target_pairs={{0,1},{1,0},{2,3},{3,2},{4,5},{5,4},{6,7},{7,6},{8,9},{9,8},{10,11... | collective-permute-start | bytes 98312 | tf_op jit(solution)/shard_map/ppermute | solution.py:374

commit v15 on v14

--- a/solution.py
+++ b/solution.py
@@ -15,23 +15,22 @@
 FIRST = 256
 PIECES = 4
 FAN = 4
+MIB = 2**20
+
 BLOCK = 8
 TO_OWNERS = (
-    "--016-54",
-    "-210--75",
-    "203-54--",
-    "3---764-",
-    "13-2-7-6",
+    "32014756",
+    "01325674",
+    "13207465",
+    "20136547",
 )
 TO_ALL = (
-    "-0----45",
-    "--0-54--",
-    "32107654",
-    "1-3267--",
-    "23-1--76",
+    "31206754",
+    "20135467",
+    "13027645",
+    "02314576",
 )
-MIB = 2**20
-LAST = 2
+LAST = 3
 
 
 def pairs_of(order, devices):
@@ -39,19 +38,17 @@
         (block + g, block + int(to))
         for block in range(0, devices, BLOCK)
         for g, to in enumerate(order)
-        if to != "-"
     ]
 
 
 def sent_pieces(order):
-    return [0 if to == "-" else bit_reverse(g ^ int(to), 2) for g, to in enumerate(order)]
+    return [bit_reverse(g ^ int(to), 2) or FAN for g, to in enumerate(order)]
 
 
 def arriving_pieces(order):
     pieces = [FAN] * BLOCK
     for g, to in enumerate(order):
-        if to != "-":
-            pieces[int(to)] = bit_reverse(g ^ int(to), 2)
+        pieces[int(to)] = bit_reverse(g ^ int(to), 2) or FAN
     return pieces
 
 
@@ -190,7 +187,8 @@
         blocks += [part[:, i : i + LANES] for i in range(0, part.shape[1], LANES)]
     blocks.append(jnp.broadcast_to(squares, (slots, LANES)))
     blocks += [jnp.zeros((slots, LANES), jnp.float32)] * (total - len(blocks))
-    flat = out.reshape(slots * total, LANES)
+    out[FAN] = jnp.zeros(out.shape[1:], jnp.float32)
+    flat = out.reshape((FAN + 1) * slots // FAN * total, LANES)
     for i, block in enumerate(blocks):
         flat[pl.ds(i, slots, stride=total), :] = block
     keep_ref[...] = out[0]
@@ -216,7 +214,7 @@
         scratch_shapes=[
             pltpu.VMEM((max(depth - skip, 16), query_width), jnp.bfloat16),
             pltpu.VMEM((slots, depth), jnp.float32),
-            pltpu.VMEM((FAN, slots // FAN, total, LANES), jnp.float32),
+            pltpu.VMEM((FAN + 1, slots // FAN, total, LANES), jnp.float32),
             pltpu.SemaphoreType.DMA((max(1, len(spread(depth, skip, CHUNK))), PIECES)),
         ],
         compiler_params=pltpu.CompilerParams(vmem_limit_bytes=46 * MIB),

time: 49.1 us -> 49 us (level)
  the two profiles are of different devices: /device:TPU:15 before, /device:TPU:13 now
where the time goes in v15:
time: 49 us; the launch traced here: 48.7 us
  starting transfers between devices  30.5 us (62%)
  Pallas kernels  10.7 us (22%)
  waiting for transfers between devices  5.86 us (12%)
  between operations  0.89 us (2%)
  other arithmetic  0.72 us (1%)
    ppermute x4, starting transfers between devices, swap(): return lax.ppermute(block, axis, [(i, i ^ mask) for i in range(devices)])  11.7 us
    ppermute x4, starting transfers between devices, body(): lax.ppermute(send, 'gx', pairs_of(order, devices))  10.5 us
    ppermute x4, starting transfers between devices, body(): lax.ppermute(held, 'gx', pairs_of(order, devices))  8.35 us
    pallas_call x1, Pallas kernels, project(): pl.pallas_call(functools.partial(project_kernel, bits), out_shape=(piece,...  5.86 us
    ppermute x4, waiting for transfers between devices, swap(): return lax.ppermute(block, axis, [(i, i ^ mask) for i in range(devices)])  3.38 us
    pallas_call x1, Pallas kernels, output(): pl.pallas_call(functools.partial(output_kernel, bits), out_shape=(piece,...  2.3 us
    ppermute x4, waiting for transfers between devices, body(): lax.ppermute(held, 'gx', pairs_of(order, devices))  2.22 us
    pallas_call x1, Pallas kernels, stage_rows(): pl.pallas_call(functools.partial(stage_kernel, rows), out_shape=jax.Shape...  1.55 us
  transfers between devices with their start and end apart: 12, of which 5 were waited for; matrix products, arithmetic and copies ran while one was open for 0% of the time, Pallas kernels for 3%

profile of v15, /device:TPU:13, one launch (start us, length us, event | category | flops | bytes accessed | tf_op | source)
XLA Modules:
  0.0 48.7 jit_solution(5900996125748227227)
XLA Ops:
  0.0 0.7 %collective-permute-start = (bf16[4,2048]{1,0:T(4,128)(2,1)}, bf16[4,2048]{1,0:T(4,128)(2,1)S(1)}, u32[]{:S(2)}, u32[]{:S(2)}) collective-permute-start(bf16[4,2048]{1,0:T(4,128)(2,1)} %rows_ref.1), channel_id=1, source_target_pairs={{0,1},{1,0},{2,3},{3,2},{4,5},{5,4},{6,7},{7,6},{8,9},{9,8},{10,11... | collective-permute-start | bytes 49160 | tf_op jit(solution)/shard_map/ppermute | solution.py:372
  0.8 1.6 %stage.1.first = bf16[256,4096]{1,0:T(8,128)(2,1)S(1)} custom-call(bf16[2048,4096]{1,0:T(8,128)(2,1)} %wq_hbm.1), custom_call_target="tpu_custom_call" | custom-call | bytes 2097152 | tf_op jit(solution)/shard_map/stage/pallas_call | solution.py:96
  2.4 5.9 %project.1 = (f32[2,40,128]{2,1,0:T(8,128)S(1)}, f32[2,40,128]{2,1,0:T(8,128)S(1)}, f32[2,40,128]{2,1,0:T(8,128)S(1)}, f32[2,40,128]{2,1,0:T(8,128)S(1)}, f32[2,40,128]{2,1,0:T(8,128)S(1)}) custom-call(bf16[4,2048]{1,0:T(4,128)(2,1)S(1)} %copy-done.4, bf16[4,2048]{1,0:T(4,128)(2,1)S(1)} %collective-permute-done.other_ref, bf16[2048,4096]{1,0:T(8,128)(2,1)} %wq_hbm.1, ...), custom_call_target="tpu_custom_call" | custom-call | flops 150994944 | bytes 18874368 | tf_op jit(solution)/shard_map/project/pallas_call | solution.py:209
  8.2 2.1 %collective-permute-start.1 = (f32[2,40,128]{2,1,0:T(8,128)S(1)}, f32[2,40,128]{2,1,0:T(8,128)S(1)}, u32[]{:S(2)}, u32[]{:S(2)}) collective-permute-start(f32[2,40,128]{2,1,0:T(8,128)S(1)} %get-tuple-element.15), channel_id=1, source_target_pairs={{0,6},{2,4},{4,0},{6,2},{8,8},{10,14},{12,10},{14,12},{1,7},{3,5},... | collective-permute-start | bytes 122888 | tf_op jit(solution)/shard_map/ppermute | solution.py:384
  10.3 3.1 %collective-permute-start.2 = (f32[2,40,128]{2,1,0:T(8,128)S(1)}, f32[2,40,128]{2,1,0:T(8,128)S(1)}, u32[]{:S(2)}, u32[]{:S(2)}) collective-permute-start(f32[2,40,128]{2,1,0:T(8,128)S(1)} %get-tuple-element.16), channel_id=1, source_target_pairs={{0,0},{2,2},{4,6},{6,4},{8,10},{10,12},{12,14},{14,8},{1,1},{3,3},... | collective-permute-start | bytes 122888 | tf_op jit(solution)/shard_map/ppermute | solution.py:384
  13.5 0.7 %collective-permute-start.3 = (f32[2,40,128]{2,1,0:T(8,128)S(1)}, f32[2,40,128]{2,1,0:T(8,128)S(1)}, u32[]{:S(2)}, u32[]{:S(2)}) collective-permute-start(f32[2,40,128]{2,1,0:T(8,128)S(1)} %get-tuple-element.17), channel_id=1, source_target_pairs={{0,2},{2,6},{4,4},{6,0},{8,14},{10,8},{12,12},{14,10},{1,3},{3,7},... | collective-permute-start | bytes 122888 | tf_op jit(solution)/shard_map/ppermute | solution.py:384
  14.1 4.6 %collective-permute-start.4 = (f32[2,40,128]{2,1,0:T(8,128)S(1)}, f32[2,40,128]{2,1,0:T(8,128)S(1)}, u32[]{:S(2)}, u32[]{:S(2)}) collective-permute-start(f32[2,40,128]{2,1,0:T(8,128)S(1)} %get-tuple-element.18), channel_id=1, source_target_pairs={{0,4},{2,0},{4,2},{6,6},{8,12},{10,10},{12,8},{14,14},{1,5},{3,1},... | collective-permute-start | bytes 122888 | tf_op jit(solution)/shard_map/ppermute | solution.py:384
  18.7 0.1 maximum_bitcast_fusion.frequency_ref
  19.5 0.0 slice-start
  19.6 0.3 collective-permute-done.4
  19.8 2.5 %collective-permute-start.5 = (f32[1,40,128]{2,1,0:T(8,128)S(1)}, f32[1,40,128]{2,1,0:T(8,128)S(1)}, u32[]{:S(2)}, u32[]{:S(2)}) collective-permute-start(f32[1,40,128]{2,1,0:T(8,128)S(1)} %get-tuple-element.23), channel_id=1, source_target_pairs={{0,8},{2,10},{4,12},{6,14},{8,0},{10,2},{12,4},{14,6},{1,9},{3,11}... | collective-permute-start | bytes 61448 | tf_op jit(solution)/shard_map/ppermute | solution.py:372
  22.4 1.3 %collective-permute-done.5.refs_1_ = f32[1,40,128]{2,1,0:T(8,128)S(1)} collective-permute-done((f32[1,40,128]{2,1,0:T(8,128)S(1)}, f32[1,40,128]{2,1,0:T(8,128)S(1)}, u32[]{:S(2)}, u32[]{:S(2)}) %collective-permute-start.5) | collective-permute-done | bytes 20512 | tf_op jit(solution)/shard_map/ppermute | solution.py:372
  23.7 1.0 %attend.1 = bf16[1,32,128]{2,1,0:T(8,128)(2,1)S(1)} custom-call(bf16[4096,2048]{1,0:T(8,128)(2,1)} %refs_4_.1, f32[8,128]{1,0:T(8,128)S(1)} %turning.1.turn_ref, bf16[1,2,2048,128]{3,2,1,0:T(8,128)(2,1)S(1)} %copy-done.2, bf16[1,2,2048,128]{3,2,1,0:T(8,128)(2,1)S(1)} %copy-done.3, f32[1,40,128]{2,1,0:T(8,128)S(1)} %get-tuple-element.24.refs_0_, ...), custom_call_target="tpu_custom_call" | custom-call | flops 33554432 | bytes 2097152 | tf_op jit(solution)/shard_map/attend/pallas_call | solution.py:299
  24.7 2.3 %collective-permute-start.6 = (bf16[1,32,128]{2,1,0:T(8,128)(2,1)S(1)}, bf16[1,32,128]{2,1,0:T(8,128)(2,1)S(1)}, u32[]{:S(2)}, u32[]{:S(2)}) collective-permute-start(bf16[1,32,128]{2,1,0:T(8,128)(2,1)S(1)} %attend.1), channel_id=1, source_target_pairs={{0,8},{2,10},{4,12},{6,14},{8,0},{10,2},{12,4},{14,6},{1,9},{3,11}... | collective-permute-start | bytes 24584 | tf_op jit(solution)/shard_map/ppermute | solution.py:372
  27.0 1.2 %collective-permute-done.6 = bf16[1,32,128]{2,1,0:T(8,128)(2,1)S(1)} collective-permute-done((bf16[1,32,128]{2,1,0:T(8,128)(2,1)S(1)}, bf16[1,32,128]{2,1,0:T(8,128)(2,1)S(1)}, u32[]{:S(2)}, u32[]{:S(2)}) %collective-permute-start.6) | collective-permute-done | bytes 8224 | tf_op jit(solution)/shard_map/ppermute | solution.py:372
  28.2 0.7 %collective-permute-start.10 = (bf16[2,32,128]{2,1,0:T(8,128)(2,1)S(1)}, bf16[2,32,128]{2,1,0:T(8,128)(2,1)S(1)}, u32[]{:S(2)}, u32[]{:S(2)}) collective-permute-start(bf16[2,32,128]{2,1,0:T(8,128)(2,1)S(1)} %pad_maximum_fusion.held_ref), channel_id=1, source_target_pairs={{0,6},{2,2},{4,4},{6,0},{8,12},{10,14},{12,10},{14,8},{1,7},{3,3},... | collective-permute-start | bytes 49160 | tf_op jit(solution)/shard_map/ppermute | solution.py:407
  28.8 4.3 %collective-permute-start.7 = (bf16[2,32,128]{2,1,0:T(8,128)(2,1)S(1)}, bf16[2,32,128]{2,1,0:T(8,128)(2,1)S(1)}, u32[]{:S(2)}, u32[]{:S(2)}) collective-permute-start(bf16[2,32,128]{2,1,0:T(8,128)(2,1)S(1)} %pad_maximum_fusion.held_ref), channel_id=1, source_target_pairs={{0,4},{2,0},{4,2},{6,6},{8,10},{10,8},{12,12},{14,14},{1,5},{3,1},... | collective-permute-start | bytes 49160 | tf_op jit(solution)/shard_map/ppermute | solution.py:407
  33.1 0.3 collective-permute-start.8
  33.4 3.1 %collective-permute-start.9 = (bf16[2,32,128]{2,1,0:T(8,128)(2,1)S(1)}, bf16[2,32,128]{2,1,0:T(8,128)(2,1)S(1)}, u32[]{:S(2)}, u32[]{:S(2)}) collective-permute-start(bf16[2,32,128]{2,1,0:T(8,128)(2,1)S(1)} %pad_maximum_fusion.held_ref), channel_id=1, source_target_pairs={{0,0},{2,4},{4,6},{6,2},{8,8},{10,10},{12,14},{14,12},{1,1},{3,5},... | collective-permute-start | bytes 49160 | tf_op jit(solution)/shard_map/ppermute | solution.py:407
  36.6 2.2 %collective-permute-done.9.refs_2_ = bf16[2,32,128]{2,1,0:T(8,128)(2,1)S(1)} collective-permute-done((bf16[2,32,128]{2,1,0:T(8,128)(2,1)S(1)}, bf16[2,32,128]{2,1,0:T(8,128)(2,1)S(1)}, u32[]{:S(2)}, u32[]{:S(2)}) %collective-permute-start.9) | collective-permute-done | bytes 16416 | tf_op jit(solution)/shard_map/ppermute | solution.py:407
  38.8 2.3 %output.1 = (f32[4,2048]{1,0:T(4,128)S(1)}, f32[4,2048]{1,0:T(4,128)S(1)}) custom-call(bf16[2,32,128]{2,1,0:T(8,128)(2,1)S(1)} %pad_maximum_fusion.held_ref, bf16[2,32,128]{2,1,0:T(8,128)(2,1)S(1)} %collective-permute-done.7.refs_0_, bf16[2,32,128]{2,1,0:T(8,128)(2,1)S(1)} %collective-permute-done.8.refs_1_, ...), custom_call_target="tpu_custom_call" | custom-call | flops 134217728 | bytes 16777216 | tf_op jit(solution)/shard_map/output/pallas_call | solution.py:353
  41.1 6.1 %collective-permute-start.11 = (f32[4,2048]{1,0:T(4,128)S(1)}, f32[4,2048]{1,0:T(4,128)S(1)}, u32[]{:S(2)}, u32[]{:S(2)}) collective-permute-start(f32[4,2048]{1,0:T(4,128)S(1)} %get-tuple-element.22), channel_id=1, source_target_pairs={{0,1},{1,0},{2,3},{3,2},{4,5},{5,4},{6,7},{7,6},{8,9},{9,8},{10,11... | collective-permute-start | bytes 98312 | tf_op jit(solution)/shard_map/ppermute | solution.py:372
  47.2 0.9 %collective-permute-done.11 = f32[4,2048]{1,0:T(4,128)S(1)} collective-permute-done((f32[4,2048]{1,0:T(4,128)S(1)}, f32[4,2048]{1,0:T(4,128)S(1)}, u32[]{:S(2)}, u32[]{:S(2)}) %collective-permute-start.11) | collective-permute-done | bytes 32800 | tf_op jit(solution)/shard_map/ppermute | solution.py:372
  48.1 0.6 %add_convert_fusion = bf16[4,2048]{1,0:T(4,128)(2,1)} fusion(f32[4,2048]{1,0:T(4,128)S(1)} %get-tuple-element.21, f32[4,2048]{1,0:T(4,128)S(1)} %collective-permute-done.11), kind=kLoop, calls=%fused_computation.1 | loop fusion | flops 16384 | bytes 81920 | tf_op jit(solution)/shard_map/convert_element_type | solution.py:410
  (30 shorter events, 0.1 us)
Async XLA Ops:
  0.0 2.4 %copy-start.4 = (bf16[4,2048]{1,0:T(4,128)(2,1)S(1)}, bf16[4,2048]{1,0:T(4,128)(2,1)}, u32[]{:S(2)}) copy-start(bf16[4,2048]{1,0:T(4,128)(2,1)} %rows_ref.1) | copy-start | bytes 49156
  0.0 2.4 %copy-start = (bf16[2048,256]{1,0:T(8,128)(2,1)S(1)}, bf16[2048,256]{1,0:T(8,128)(2,1)}, u32[]{:S(2)}) copy-start(bf16[2048,256]{1,0:T(8,128)(2,1)} %wk.1) | copy-start | bytes 3145732
  0.0 2.4 %copy-start.1 = (bf16[2048,256]{1,0:T(8,128)(2,1)S(1)}, bf16[2048,256]{1,0:T(8,128)(2,1)}, u32[]{:S(2)}) copy-start(bf16[2048,256]{1,0:T(8,128)(2,1)} %wv.1) | copy-start | bytes 3145732
  0.0 2.3 %collective-permute-start = (bf16[4,2048]{1,0:T(4,128)(2,1)}, bf16[4,2048]{1,0:T(4,128)(2,1)S(1)}, u32[]{:S(2)}, u32[]{:S(2)}) collective-permute-start(bf16[4,2048]{1,0:T(4,128)(2,1)} %rows_ref.1), channel_id=1, source_target_pairs={{0,1},{1,0},{2,3},{3,2},{4,5},{5,4},{6,7},{7,6},{8,9},{9,8},{10,11... | collective-permute-start | bytes 49160 | tf_op jit(solution)/shard_map/ppermute | solution.py:372
  2.3 21.4 %copy-start.2 = (bf16[1,2,2048,128]{3,2,1,0:T(8,128)(2,1)S(1)}, bf16[1,2,2048,128]{3,2,1,0:T(8,128)(2,1)}, u32[]{:S(2)}) copy-start(bf16[1,2,2048,128]{3,2,1,0:T(8,128)(2,1)} %k_ref.1) | copy-start | bytes 3145732
  2.3 21.4 %copy-start.3 = (bf16[1,2,2048,128]{3,2,1,0:T(8,128)(2,1)S(1)}, bf16[1,2,2048,128]{3,2,1,0:T(8,128)(2,1)}, u32[]{:S(2)}) copy-start(bf16[1,2,2048,128]{3,2,1,0:T(8,128)(2,1)} %v_ref.1) | copy-start | bytes 3145732
  8.2 11.3 %collective-permute-start.1 = (f32[2,40,128]{2,1,0:T(8,128)S(1)}, f32[2,40,128]{2,1,0:T(8,128)S(1)}, u32[]{:S(2)}, u32[]{:S(2)}) collective-permute-start(f32[2,40,128]{2,1,0:T(8,128)S(1)} %get-tuple-element.15), channel_id=1, source_target_pairs={{0,6},{2,4},{4,0},{6,2},{8,8},{10,14},{12,10},{14,12},{1,7},{3,5},... | collective-permute-start | bytes 122888 | tf_op jit(solution)/shard_map/ppermute | solution.py:384
  10.3 9.2 %collective-permute-start.2 = (f32[2,40,128]{2,1,0:T(8,128)S(1)}, f32[2,40,128]{2,1,0:T(8,128)S(1)}, u32[]{:S(2)}, u32[]{:S(2)}) collective-permute-start(f32[2,40,128]{2,1,0:T(8,128)S(1)} %get-tuple-element.16), channel_id=1, source_target_pairs={{0,0},{2,2},{4,6},{6,4},{8,10},{10,12},{12,14},{14,8},{1,1},{3,3},... | collective-permute-start | bytes 122888 | tf_op jit(solution)/shard_map/ppermute | solution.py:384
  13.5 6.1 %collective-permute-start.3 = (f32[2,40,128]{2,1,0:T(8,128)S(1)}, f32[2,40,128]{2,1,0:T(8,128)S(1)}, u32[]{:S(2)}, u32[]{:S(2)}) collective-permute-start(f32[2,40,128]{2,1,0:T(8,128)S(1)} %get-tuple-element.17), channel_id=1, source_target_pairs={{0,2},{2,6},{4,4},{6,0},{8,14},{10,8},{12,12},{14,10},{1,3},{3,7},... | collective-permute-start | bytes 122888 | tf_op jit(solution)/shard_map/ppermute | solution.py:384
  14.1 5.7 %collective-permute-start.4 = (f32[2,40,128]{2,1,0:T(8,128)S(1)}, f32[2,40,128]{2,1,0:T(8,128)S(1)}, u32[]{:S(2)}, u32[]{:S(2)}) collective-permute-start(f32[2,40,128]{2,1,0:T(8,128)S(1)} %get-tuple-element.18), channel_id=1, source_target_pairs={{0,4},{2,0},{4,2},{6,6},{8,12},{10,10},{12,8},{14,14},{1,5},{3,1},... | collective-permute-start | bytes 122888 | tf_op jit(solution)/shard_map/ppermute | solution.py:384
  19.5 19.3 %slice-start = ((s8[16777216]{0:T(1024)(128)(4,1)}), s8[4194304]{0:T(1024)(128)(4,1)S(1)}, s32[]{:S(2)}) async-start(s8[16777216]{0:T(1024)(128)(4,1)} %bitcast.2), calls=%async_computation | async-start | bytes 8388608
  19.5 19.3 %slice-start.1 = ((s8[16777216]{0:T(1024)(128)(4,1)}), s8[4194304]{0:T(1024)(128)(4,1)S(1)}, s32[]{:S(2)}) async-start(s8[16777216]{0:T(1024)(128)(4,1)} %bitcast.2), calls=%async_computation.1 | async-start | bytes 8388608
  19.8 3.9 %collective-permute-start.5 = (f32[1,40,128]{2,1,0:T(8,128)S(1)}, f32[1,40,128]{2,1,0:T(8,128)S(1)}, u32[]{:S(2)}, u32[]{:S(2)}) collective-permute-start(f32[1,40,128]{2,1,0:T(8,128)S(1)} %get-tuple-element.23), channel_id=1, source_target_pairs={{0,8},{2,10},{4,12},{6,14},{8,0},{10,2},{12,4},{14,6},{1,9},{3,11}... | collective-permute-start | bytes 61448 | tf_op jit(solution)/shard_map/ppermute | solution.py:372
  23.7 15.1 %slice-start.2 = ((s8[16777216]{0:T(1024)(128)(4,1)}), s8[4194304]{0:T(1024)(128)(4,1)S(1)}, s32[]{:S(2)}) async-start(s8[16777216]{0:T(1024)(128)(4,1)} %bitcast.2), calls=%async_computation.2 | async-start | bytes 8388608
  23.7 15.1 %slice-start.3 = ((s8[16777216]{0:T(1024)(128)(4,1)}), s8[4194304]{0:T(1024)(128)(4,1)S(1)}, s32[]{:S(2)}) async-start(s8[16777216]{0:T(1024)(128)(4,1)} %bitcast.2), calls=%async_computation.3 | async-start | bytes 8388608
  24.7 3.5 %collective-permute-start.6 = (bf16[1,32,128]{2,1,0:T(8,128)(2,1)S(1)}, bf16[1,32,128]{2,1,0:T(8,128)(2,1)S(1)}, u32[]{:S(2)}, u32[]{:S(2)}) collective-permute-start(bf16[1,32,128]{2,1,0:T(8,128)(2,1)S(1)} %attend.1), channel_id=1, source_target_pairs={{0,8},{2,10},{4,12},{6,14},{8,0},{10,2},{12,4},{14,6},{1,9},{3,11}... | collective-permute-start | bytes 24584 | tf_op jit(solution)/shard_map/ppermute | solution.py:372
  28.2 8.4 %collective-permute-start.10 = (bf16[2,32,128]{2,1,0:T(8,128)(2,1)S(1)}, bf16[2,32,128]{2,1,0:T(8,128)(2,1)S(1)}, u32[]{:S(2)}, u32[]{:S(2)}) collective-permute-start(bf16[2,32,128]{2,1,0:T(8,128)(2,1)S(1)} %pad_maximum_fusion.held_ref), channel_id=1, source_target_pairs={{0,6},{2,2},{4,4},{6,0},{8,12},{10,14},{12,10},{14,8},{1,7},{3,3},... | collective-permute-start | bytes 49160 | tf_op jit(solution)/shard_map/ppermute | solution.py:407
  28.8 7.7 %collective-permute-start.7 = (bf16[2,32,128]{2,1,0:T(8,128)(2,1)S(1)}, bf16[2,32,128]{2,1,0:T(8,128)(2,1)S(1)}, u32[]{:S(2)}, u32[]{:S(2)}) collective-permute-start(bf16[2,32,128]{2,1,0:T(8,128)(2,1)S(1)} %pad_maximum_fusion.held_ref), channel_id=1, source_target_pairs={{0,4},{2,0},{4,2},{6,6},{8,10},{10,8},{12,12},{14,14},{1,5},{3,1},... | collective-permute-start | bytes 49160 | tf_op jit(solution)/shard_map/ppermute | solution.py:407
  33.1 3.4 %collective-permute-start.8 = (bf16[2,32,128]{2,1,0:T(8,128)(2,1)S(1)}, bf16[2,32,128]{2,1,0:T(8,128)(2,1)S(1)}, u32[]{:S(2)}, u32[]{:S(2)}) collective-permute-start(bf16[2,32,128]{2,1,0:T(8,128)(2,1)S(1)} %pad_maximum_fusion.held_ref), channel_id=1, source_target_pairs={{0,2},{2,6},{4,0},{6,4},{8,14},{10,12},{12,8},{14,10},{1,3},{3,7},... | collective-permute-start | bytes 49160 | tf_op jit(solution)/shard_map/ppermute | solution.py:407
  33.4 5.4 %collective-permute-start.9 = (bf16[2,32,128]{2,1,0:T(8,128)(2,1)S(1)}, bf16[2,32,128]{2,1,0:T(8,128)(2,1)S(1)}, u32[]{:S(2)}, u32[]{:S(2)}) collective-permute-start(bf16[2,32,128]{2,1,0:T(8,128)(2,1)S(1)} %pad_maximum_fusion.held_ref), channel_id=1, source_target_pairs={{0,0},{2,4},{4,6},{6,2},{8,8},{10,10},{12,14},{14,12},{1,1},{3,5},... | collective-permute-start | bytes 49160 | tf_op jit(solution)/shard_map/ppermute | solution.py:407
  41.1 7.0 %collective-permute-start.11 = (f32[4,2048]{1,0:T(4,128)S(1)}, f32[4,2048]{1,0:T(4,128)S(1)}, u32[]{:S(2)}, u32[]{:S(2)}) collective-permute-start(f32[4,2048]{1,0:T(4,128)S(1)} %get-tuple-element.22), channel_id=1, source_target_pairs={{0,1},{1,0},{2,3},{3,2},{4,5},{5,4},{6,7},{7,6},{8,9},{9,8},{10,11... | collective-permute-start | bytes 98312 | tf_op jit(solution)/shard_map/ppermute | solution.py:372

commit v16 on v13

--- a/solution.py
+++ b/solution.py
@@ -68,7 +68,7 @@
     )(in_hbm(array))
 
 
-def turning_kernel(length_ref, frequency_ref, beside_ref, turn_ref):
+def turning_kernel(length_ref, frequency_ref, beside_ref, after_ref, turn_ref):
     position = length_ref[0].astype(jnp.float32)
     angle = position * frequency_ref[...]
     lane = lax.broadcasted_iota(jnp.int32, angle.shape, 1)
@@ -78,7 +78,7 @@
     turn_ref[2:3, :] = jnp.full(angle.shape, position)
 
 
-def turning(lengths, frequency, beside):
+def turning(lengths, frequency, beside, after):
     vmem = pl.BlockSpec(memory_space=pltpu.VMEM)
     return pl.pallas_call(
         turning_kernel,
@@ -87,12 +87,13 @@
             pl.BlockSpec(memory_space=pltpu.SMEM),
             vmem,
             pl.BlockSpec(memory_space=pltpu.HBM),
+            vmem,
         ],
         out_specs=vmem,
         compiler_params=pltpu.CompilerParams(vmem_limit_bytes=2 * MIB),
         cost_estimate=pl.CostEstimate(flops=0, bytes_accessed=2 * beside.size, transcendentals=256),
         name="turning",
-    )(lengths, frequency, in_hbm(beside))
+    )(lengths, frequency, in_hbm(beside), after)
 
 
 def spread(depth, skip, chunk):
@@ -268,16 +269,16 @@
     )(in_hbm(beside), turn, k_cache, value_cache, *parts)
 
 
-def output_kernel(bits, pieces, *refs):
-    parts = refs[:pieces][::-1]
+def output_kernel(bits, places, turned, *refs):
+    pieces = len(places)
+    parts = refs[:pieces]
     w_ref, mine_ref, theirs_ref, flat, left, sums = refs[pieces:]
     slots = left.shape[0]
     heads = flat.shape[0] // slots
-    at = 0
-    for ref in parts:
-        for i in range(ref.shape[0]):
-            flat[at : at + heads, :] = ref[i].astype(jnp.float32)
-            at += heads
+    for slot, ref in zip(places, parts):
+        for i, row in enumerate(range(ref.shape[0])[::turned]):
+            at = (slot + i) * heads
+            flat[at : at + heads, :] = ref[row].astype(jnp.float32)
     for head in range(heads):
         left[:, head * HEAD_SIZE : (head + 1) * HEAD_SIZE] = flat[
             pl.ds(head, slots, stride=heads), :
@@ -299,14 +300,17 @@
             ref[t : t + 1, :] = sums[pl.ds(slot, 1), :]
 
 
-def output(parts, w_out, slots):
+def output(parts, order, w_out, slots, turned=1):
     bits = slots.bit_length() - 1
     depth, width = w_out.shape
     heads = depth // HEAD_SIZE
+    starts = [sum(x.shape[0] for x in parts[:i]) for i in range(len(parts))]
+    places = tuple(starts[i] for i in order)
+    parts = [parts[i] for i in order]
     whole = pl.BlockSpec(memory_space=pltpu.VMEM)
     piece = jax.ShapeDtypeStruct((slots // 2, width), jnp.float32)
     return pl.pallas_call(
-        functools.partial(output_kernel, bits, len(parts)),
+        functools.partial(output_kernel, bits, places, turned),
         out_shape=(piece, piece),
         in_specs=[whole] * (len(parts) + 1),
         out_specs=(whole, whole),
@@ -327,11 +331,16 @@
     return lax.ppermute(block, axis, [(i, i ^ mask) for i in range(devices)])
 
 
-def fan(pieces, devices):
+def cross(block, devices, mask):
+    pairs = [(i, i ^ (2 * mask + 1)) for i in range(2 * devices)]
+    return lax.ppermute(block, ("gx", "gy"), pairs)
+
+
+def fan(pieces, trade):
     masks = [bit_reverse(q, 2) for q in range(FAN)]
     arrived = [None] * FAN
     for q in sorted(range(1, FAN), key=lambda q: (masks[q] + 1) % FAN):
-        arrived[q] = swap(pieces[q], "gx", devices, masks[q])
+        arrived[q] = trade(pieces[q], masks[q])
     return arrived[1:]
 
 
@@ -342,31 +351,49 @@
     depth = w_query.shape[0]
     first = stage_rows(w_query, min(FIRST, depth))
     pieces = project(activations, other, w_query, first, key_weight, value_weight, slots)
-
-    arrived = fan(pieces, devices)
     half = HEAD_SIZE // 2
     frequency = jnp.power(
         jnp.float32(500000.0), -2.0 * jnp.arange(half, dtype=jnp.float32) / HEAD_SIZE
     )
     frequency = jnp.concatenate([frequency, frequency])[None, :]
-    turn = turning(lengths, frequency, w_out)
-    total = pieces[0] + (arrived[2] + (arrived[1] + arrived[0]))
-    mask = FAN
-    while total.shape[0] > 2:
-        rest = total.shape[0] // 2
-        total = total[:rest] + swap(total[rest:], "gx", devices, mask)
-        mask *= 2
-    total, turn = lax.optimization_barrier((total, turn))
-    parts = [total[:1], swap(total[1:], "gx", devices, mask)]
-    heads = attend(parts, turn, k_cache, value_cache, query_heads, w_out)
-
-    parts = [heads, swap(heads, "gx", devices, mask)]
-    while mask > FAN:
-        mask //= 2
-        parts.append(swap(jnp.concatenate(parts, axis=0), "gx", devices, mask))
-    held = jnp.concatenate(parts, axis=0)
-    parts += fan([held] * FAN, devices)
-    mine, theirs = output(parts[::-1], w_out, slots)
+
+    if devices == 2 * FAN:
+        far = FAN
+        arrived = fan(pieces, lambda block, mask: cross(block, devices, mask))
+        early = swap(pieces[0][1:], "gx", devices, far)
+        turn = turning(lengths, frequency, w_out, pieces[0])
+        total = arrived[2] + (arrived[1] + arrived[0])
+        total, turn = lax.optimization_barrier((total, turn))
+        crossed = cross(total[1:], devices, far)
+        beside = swap(total[:1], "gy", 2, 1)
+        parts = [pieces[0][:1], early, crossed, beside]
+        heads = attend(parts, turn, k_cache, value_cache, query_heads, w_out)
+        crossed = cross(heads, devices, far)
+        beside = swap(heads, "gy", 2, 1)
+        held = jnp.concatenate([crossed, beside], axis=0)
+        arrived = fan([held] * FAN, lambda block, mask: cross(block, devices, mask))
+        parts = [heads, swap(crossed, "gy", 2, 1)] + arrived
+        order, turned = (2, 4, 3, 1, 0), -1
+    else:
+        arrived = fan(pieces, lambda block, mask: swap(block, "gx", devices, mask))
+        turn = turning(lengths, frequency, w_out, pieces[0])
+        total = pieces[0] + (arrived[2] + (arrived[1] + arrived[0]))
+        mask = FAN
+        while total.shape[0] > 2:
+            rest = total.shape[0] // 2
+            total = total[:rest] + swap(total[rest:], "gx", devices, mask)
+            mask *= 2
+        parts = [total[:1], swap(total[1:], "gx", devices, mask)]
+        heads = attend(parts, turn, k_cache, value_cache, query_heads, w_out)
+
+        parts = [heads, swap(heads, "gx", devices, mask)]
+        while mask > FAN:
+            mask //= 2
+            parts.append(swap(jnp.concatenate(parts, axis=0), "gx", devices, mask))
+        held = jnp.concatenate(parts, axis=0)
+        parts += fan([held] * FAN, lambda block, mask: swap(block, "gx", devices, mask))
+        order, turned = range(len(parts))[::-1], 1
+    mine, theirs = output(parts, order, w_out, slots, turned)
     return (mine + swap(theirs, "gy", 2, 1)).astype(jnp.bfloat16)
 
 

time: 36.8 us -> 35.7 us (0.970)
  waiting for transfers between devices: 9.76 us -> 6.64 us
  starting transfers between devices: 14.5 us -> 16.6 us
    ppermute x0 -> x8, starting transfers between devices: none -> 12.6 us  [cross(): return lax.ppermute(block, ('gx', 'gy'), pairs)]
    ppermute x10 -> x6, starting transfers between devices: 14.5 us -> 3.95 us  [swap(): return lax.ppermute(block, axis, [(i, i ^ mask) for i in range(devices)])]
    ppermute x10 -> x6, waiting for transfers between devices: 9.76 us -> 2.05 us  [swap(): return lax.ppermute(block, axis, [(i, i ^ mask) for i in range(devices)])]
    ppermute x0 -> x8, waiting for transfers between devices: none -> 4.59 us  [cross(): return lax.ppermute(block, ('gx', 'gy'), pairs)]
  transfers between devices with their start and end apart: 10 -> 14, of which waited for: 9 -> 8; matrix products, arithmetic and copies ran while one was open for 0% -> 0% of each run, Pallas kernels for 5% -> 5%
where the time goes in v16:
time: 35.7 us; the launch traced here: 35.6 us
  starting transfers between devices  16.6 us (46%)
  Pallas kernels  10.8 us (30%)
  waiting for transfers between devices  6.64 us (19%)
  between operations  0.8 us (2%)
  other arithmetic  0.71 us (2%)
    ppermute x8, starting transfers between devices, cross(): return lax.ppermute(block, ('gx', 'gy'), pairs)  12.6 us
    pallas_call x1, Pallas kernels, project(): pl.pallas_call(functools.partial(project_kernel, bits), out_shape=(piece,...  5.86 us
    ppermute x8, waiting for transfers between devices, cross(): return lax.ppermute(block, ('gx', 'gy'), pairs)  4.59 us
    ppermute x6, starting transfers between devices, swap(): return lax.ppermute(block, axis, [(i, i ^ mask) for i in range(devices)])  3.95 us
    pallas_call x1, Pallas kernels, output(): pl.pallas_call(functools.partial(output_kernel, bits, places, turned), ou...  2.31 us
    ppermute x6, waiting for transfers between devices, swap(): return lax.ppermute(block, axis, [(i, i ^ mask) for i in range(devices)])  2.05 us
    pallas_call x1, Pallas kernels, stage_rows(): pl.pallas_call(functools.partial(stage_kernel, rows), out_shape=jax.Shape...  1.59 us
    pallas_call x1, Pallas kernels, attend(): pl.pallas_call(functools.partial(attend_kernel, query_heads, kv_heads, le...  0.98 us
  transfers between devices with their start and end apart: 14, of which 8 were waited for; matrix products, arithmetic and copies ran while one was open for 0% of the time, Pallas kernels for 5%

profile of v16, /device:TPU:0, one launch (start us, length us, event | category | flops | bytes accessed | tf_op | source)
XLA Modules:
  0.0 35.6 jit_solution(11711316794370004758)
XLA Ops:
  0.0 0.5 %collective-permute-start = (bf16[4,2048]{1,0:T(4,128)(2,1)}, bf16[4,2048]{1,0:T(4,128)(2,1)S(1)}, u32[]{:S(2)}, u32[]{:S(2)}) collective-permute-start(bf16[4,2048]{1,0:T(4,128)(2,1)} %rows_ref.1), channel_id=1, source_target_pairs={{0,1},{1,0},{2,3},{3,2},{4,5},{5,4},{6,7},{7,6},{8,9},{9,8},{10,11... | collective-permute-start | bytes 49160 | tf_op jit(solution)/shard_map/ppermute | solution.py:331
  0.6 1.6 %stage.1.first = bf16[256,4096]{1,0:T(8,128)(2,1)S(1)} custom-call(bf16[2048,4096]{1,0:T(8,128)(2,1)} %wq_hbm.1), custom_call_target="tpu_custom_call" | custom-call | bytes 2097152 | tf_op jit(solution)/shard_map/stage/pallas_call | solution.py:57
  2.9 5.9 %project.1 = (f32[2,40,128]{2,1,0:T(8,128)S(1)}, f32[2,40,128]{2,1,0:T(8,128)S(1)}, f32[2,40,128]{2,1,0:T(8,128)S(1)}, f32[2,40,128]{2,1,0:T(8,128)S(1)}) custom-call(bf16[4,2048]{1,0:T(4,128)(2,1)S(1)} %copy-done.4, bf16[4,2048]{1,0:T(4,128)(2,1)S(1)} %collective-permute-done.other_ref, bf16[2048,4096]{1,0:T(8,128)(2,1)} %wq_hbm.1, ...), custom_call_target="tpu_custom_call" | custom-call | flops 150994944 | bytes 18874368 | tf_op jit(solution)/shard_map/project/pallas_call | solution.py:168
  8.8 3.6 %collective-permute-start.1 = (f32[2,40,128]{2,1,0:T(8,128)S(1)}, f32[2,40,128]{2,1,0:T(8,128)S(1)}, u32[]{:S(2)}, u32[]{:S(2)}) collective-permute-start(f32[2,40,128]{2,1,0:T(8,128)S(1)} %get-tuple-element.13), channel_id=1, source_target_pairs={{0,7},{1,6},{2,5},{3,4},{4,3},{5,2},{6,1},{7,0},{8,15},{9,14},{10,... | collective-permute-start | bytes 122888 | tf_op jit(solution)/shard_map/ppermute | solution.py:336
  12.4 0.3 collective-permute-start.2
  12.8 3.0 %collective-permute-start.4 = (f32[1,40,128]{2,1,0:T(8,128)S(1)}, f32[1,40,128]{2,1,0:T(8,128)S(1)}, u32[]{:S(2)}, u32[]{:S(2)}) collective-permute-start(f32[1,40,128]{2,1,0:T(8,128)S(1)} %get-tuple-element.23), channel_id=1, source_target_pairs={{0,8},{2,10},{4,12},{6,14},{8,0},{10,2},{12,4},{14,6},{1,9},{3,11}... | collective-permute-start | bytes 61448 | tf_op jit(solution)/shard_map/ppermute | solution.py:331
  15.9 0.1 collective-permute-done.2
  16.0 0.2 collective-permute-done.3
  16.2 2.7 %collective-permute-start.5 = (f32[1,40,128]{2,1,0:T(8,128)S(1)}, f32[1,40,128]{2,1,0:T(8,128)S(1)}, u32[]{:S(2)}, u32[]{:S(2)}) collective-permute-start(f32[1,40,128]{2,1,0:T(8,128)S(1)} %get-tuple-element.22), channel_id=1, source_target_pairs={{0,9},{1,8},{2,11},{3,10},{4,13},{5,12},{6,15},{7,14},{8,1},{9,0},... | collective-permute-start | bytes 61448 | tf_op jit(solution)/shard_map/ppermute | solution.py:336
  19.0 1.4 %collective-permute-done.5.refs_2_ = f32[1,40,128]{2,1,0:T(8,128)S(1)} collective-permute-done((f32[1,40,128]{2,1,0:T(8,128)S(1)}, f32[1,40,128]{2,1,0:T(8,128)S(1)}, u32[]{:S(2)}, u32[]{:S(2)}) %collective-permute-start.5) | collective-permute-done | bytes 20512 | tf_op jit(solution)/shard_map/ppermute | solution.py:336
  20.4 1.0 %attend.1.refs_4_ = bf16[1,32,128]{2,1,0:T(8,128)(2,1)S(1)} custom-call(bf16[4096,2048]{1,0:T(8,128)(2,1)} %refs_5_.1, f32[8,128]{1,0:T(8,128)S(1)} %turning.1.turn_ref, bf16[1,2,2048,128]{3,2,1,0:T(8,128)(2,1)S(1)} %copy-done.2, bf16[1,2,2048,128]{3,2,1,0:T(8,128)(2,1)S(1)} %copy-done.3, f32[1,40,128]{2,1,0:T(8,128)S(1)} %get-tuple-element.24.refs_0_, ...), custom_call_target="tpu_custom_call" | custom-call | flops 33554432 | bytes 2097152 | tf_op jit(solution)/shard_map/attend/pallas_call | solution.py:257
  21.4 2.7 %collective-permute-start.7 = (bf16[1,32,128]{2,1,0:T(8,128)(2,1)S(1)}, bf16[1,32,128]{2,1,0:T(8,128)(2,1)S(1)}, u32[]{:S(2)}, u32[]{:S(2)}) collective-permute-start(bf16[1,32,128]{2,1,0:T(8,128)(2,1)S(1)} %attend.1.refs_4_), channel_id=1, source_target_pairs={{0,9},{1,8},{2,11},{3,10},{4,13},{5,12},{6,15},{7,14},{8,1},{9,0},... | collective-permute-start | bytes 24584 | tf_op jit(solution)/shard_map/ppermute | solution.py:336
  24.1 1.3 %collective-permute-done.7 = bf16[1,32,128]{2,1,0:T(8,128)(2,1)S(1)} collective-permute-done((bf16[1,32,128]{2,1,0:T(8,128)(2,1)S(1)}, bf16[1,32,128]{2,1,0:T(8,128)(2,1)S(1)}, u32[]{:S(2)}, u32[]{:S(2)}) %collective-permute-start.7) | collective-permute-done | bytes 8224 | tf_op jit(solution)/shard_map/ppermute | solution.py:336
  25.5 2.1 %collective-permute-start.10 = (bf16[2,32,128]{2,1,0:T(8,128)(2,1)S(1)}, bf16[2,32,128]{2,1,0:T(8,128)(2,1)S(1)}, u32[]{:S(2)}, u32[]{:S(2)}) collective-permute-start(bf16[2,32,128]{2,1,0:T(8,128)(2,1)S(1)} %constant_dynamic-update-slice_fusion), channel_id=1, source_target_pairs={{0,7},{1,6},{2,5},{3,4},{4,3},{5,2},{6,1},{7,0},{8,15},{9,14},{10,... | collective-permute-start | bytes 49160 | tf_op jit(solution)/shard_map/ppermute | solution.py:336
  27.6 0.6 %collective-permute-start.11 = (bf16[2,32,128]{2,1,0:T(8,128)(2,1)S(1)}, bf16[2,32,128]{2,1,0:T(8,128)(2,1)S(1)}, u32[]{:S(2)}, u32[]{:S(2)}) collective-permute-start(bf16[2,32,128]{2,1,0:T(8,128)(2,1)S(1)} %constant_dynamic-update-slice_fusion), channel_id=1, source_target_pairs={{0,3},{1,2},{2,1},{3,0},{4,7},{5,6},{6,5},{7,4},{8,11},{9,10},{10,... | collective-permute-start | bytes 49160 | tf_op jit(solution)/shard_map/ppermute | solution.py:336
  28.2 0.5 %collective-permute-start.9 = (bf16[2,32,128]{2,1,0:T(8,128)(2,1)S(1)}, bf16[2,32,128]{2,1,0:T(8,128)(2,1)S(1)}, u32[]{:S(2)}, u32[]{:S(2)}) collective-permute-start(bf16[2,32,128]{2,1,0:T(8,128)(2,1)S(1)} %constant_dynamic-update-slice_fusion), channel_id=1, source_target_pairs={{0,5},{1,4},{2,7},{3,6},{4,1},{5,0},{6,3},{7,2},{8,13},{9,12},{10,... | collective-permute-start | bytes 49160 | tf_op jit(solution)/shard_map/ppermute | solution.py:336
  28.7 0.2 collective-permute-start.12
  28.9 1.0 %collective-permute-done.12.refs_3_ = bf16[1,32,128]{2,1,0:T(8,128)(2,1)S(1)} collective-permute-done((bf16[1,32,128]{2,1,0:T(8,128)(2,1)S(1)}, bf16[1,32,128]{2,1,0:T(8,128)(2,1)S(1)}, u32[]{:S(2)}, u32[]{:S(2)}) %collective-permute-start.12) | collective-permute-done | bytes 8224 | tf_op jit(solution)/shard_map/ppermute | solution.py:331
  29.8 0.9 %collective-permute-done.11.refs_2_ = bf16[2,32,128]{2,1,0:T(8,128)(2,1)S(1)} collective-permute-done((bf16[2,32,128]{2,1,0:T(8,128)(2,1)S(1)}, bf16[2,32,128]{2,1,0:T(8,128)(2,1)S(1)}, u32[]{:S(2)}, u32[]{:S(2)}) %collective-permute-start.11) | collective-permute-done | bytes 16416 | tf_op jit(solution)/shard_map/ppermute | solution.py:336
  30.8 0.6 %collective-permute-done.9.refs_0_ = bf16[2,32,128]{2,1,0:T(8,128)(2,1)S(1)} collective-permute-done((bf16[2,32,128]{2,1,0:T(8,128)(2,1)S(1)}, bf16[2,32,128]{2,1,0:T(8,128)(2,1)S(1)}, u32[]{:S(2)}, u32[]{:S(2)}) %collective-permute-start.9) | collective-permute-done | bytes 16416 | tf_op jit(solution)/shard_map/ppermute | solution.py:336
  31.4 2.3 %output.1 = (f32[4,2048]{1,0:T(4,128)S(1)}, f32[4,2048]{1,0:T(4,128)S(1)}) custom-call(bf16[2,32,128]{2,1,0:T(8,128)(2,1)S(1)} %collective-permute-done.9.refs_0_, bf16[2,32,128]{2,1,0:T(8,128)(2,1)S(1)} %collective-permute-done.10.refs_1_, bf16[2,32,128]{2,1,0:T(8,128)(2,1)S(1)} %collective-permute-done.11.refs_2_, ...), custom_call_target="tpu_custom_call" | custom-call | flops 134217728 | bytes 16777216 | tf_op jit(solution)/shard_map/output/pallas_call | solution.py:312
  33.7 0.2 collective-permute-start.13
  33.9 1.1 %collective-permute-done.13 = f32[4,2048]{1,0:T(4,128)S(1)} collective-permute-done((f32[4,2048]{1,0:T(4,128)S(1)}, f32[4,2048]{1,0:T(4,128)S(1)}, u32[]{:S(2)}, u32[]{:S(2)}) %collective-permute-start.13) | collective-permute-done | bytes 32800 | tf_op jit(solution)/shard_map/ppermute | solution.py:331
  35.0 0.6 %add_convert_fusion = bf16[4,2048]{1,0:T(4,128)(2,1)} fusion(f32[4,2048]{1,0:T(4,128)S(1)} %get-tuple-element.19, f32[4,2048]{1,0:T(4,128)S(1)} %collective-permute-done.13), kind=kLoop, calls=%fused_computation.1 | loop fusion | flops 16384 | bytes 81920 | tf_op jit(solution)/shard_map/convert_element_type | solution.py:397
  (36 shorter events, 0.4 us)
Async XLA Ops:
  0.0 2.9 %copy-start.4 = (bf16[4,2048]{1,0:T(4,128)(2,1)S(1)}, bf16[4,2048]{1,0:T(4,128)(2,1)}, u32[]{:S(2)}) copy-start(bf16[4,2048]{1,0:T(4,128)(2,1)} %rows_ref.1) | copy-start | bytes 49156
  0.0 2.9 %copy-start = (bf16[2048,256]{1,0:T(8,128)(2,1)S(1)}, bf16[2048,256]{1,0:T(8,128)(2,1)}, u32[]{:S(2)}) copy-start(bf16[2048,256]{1,0:T(8,128)(2,1)} %wk.1) | copy-start | bytes 3145732
  0.0 2.9 %copy-start.1 = (bf16[2048,256]{1,0:T(8,128)(2,1)S(1)}, bf16[2048,256]{1,0:T(8,128)(2,1)}, u32[]{:S(2)}) copy-start(bf16[2048,256]{1,0:T(8,128)(2,1)} %wv.1) | copy-start | bytes 3145732
  0.0 2.9 %collective-permute-start = (bf16[4,2048]{1,0:T(4,128)(2,1)}, bf16[4,2048]{1,0:T(4,128)(2,1)S(1)}, u32[]{:S(2)}, u32[]{:S(2)}) collective-permute-start(bf16[4,2048]{1,0:T(4,128)(2,1)} %rows_ref.1), channel_id=1, source_target_pairs={{0,1},{1,0},{2,3},{3,2},{4,5},{5,4},{6,7},{7,6},{8,9},{9,8},{10,11... | collective-permute-start | bytes 49160 | tf_op jit(solution)/shard_map/ppermute | solution.py:331
  2.9 17.6 %copy-start.2 = (bf16[1,2,2048,128]{3,2,1,0:T(8,128)(2,1)S(1)}, bf16[1,2,2048,128]{3,2,1,0:T(8,128)(2,1)}, u32[]{:S(2)}) copy-start(bf16[1,2,2048,128]{3,2,1,0:T(8,128)(2,1)} %k_ref.1) | copy-start | bytes 3145732
  2.9 17.5 %copy-start.3 = (bf16[1,2,2048,128]{3,2,1,0:T(8,128)(2,1)S(1)}, bf16[1,2,2048,128]{3,2,1,0:T(8,128)(2,1)}, u32[]{:S(2)}) copy-start(bf16[1,2,2048,128]{3,2,1,0:T(8,128)(2,1)} %v_ref.1) | copy-start | bytes 3145732
  8.8 7.1 %collective-permute-start.1 = (f32[2,40,128]{2,1,0:T(8,128)S(1)}, f32[2,40,128]{2,1,0:T(8,128)S(1)}, u32[]{:S(2)}, u32[]{:S(2)}) collective-permute-start(f32[2,40,128]{2,1,0:T(8,128)S(1)} %get-tuple-element.13), channel_id=1, source_target_pairs={{0,7},{1,6},{2,5},{3,4},{4,3},{5,2},{6,1},{7,0},{8,15},{9,14},{10,... | collective-permute-start | bytes 122888 | tf_op jit(solution)/shard_map/ppermute | solution.py:336
  12.4 3.5 %collective-permute-start.2 = (f32[2,40,128]{2,1,0:T(8,128)S(1)}, f32[2,40,128]{2,1,0:T(8,128)S(1)}, u32[]{:S(2)}, u32[]{:S(2)}) collective-permute-start(f32[2,40,128]{2,1,0:T(8,128)S(1)} %get-tuple-element.14), channel_id=1, source_target_pairs={{0,3},{1,2},{2,1},{3,0},{4,7},{5,6},{6,5},{7,4},{8,11},{9,10},{10,... | collective-permute-start | bytes 122888 | tf_op jit(solution)/shard_map/ppermute | solution.py:336
  12.7 3.4 %collective-permute-start.3 = (f32[2,40,128]{2,1,0:T(8,128)S(1)}, f32[2,40,128]{2,1,0:T(8,128)S(1)}, u32[]{:S(2)}, u32[]{:S(2)}) collective-permute-start(f32[2,40,128]{2,1,0:T(8,128)S(1)} %get-tuple-element.15), channel_id=1, source_target_pairs={{0,5},{1,4},{2,7},{3,6},{4,1},{5,0},{6,3},{7,2},{8,13},{9,12},{10,... | collective-permute-start | bytes 122888 | tf_op jit(solution)/shard_map/ppermute | solution.py:336
  12.8 18.5 %slice-start = ((s8[16777216]{0:T(1024)(128)(4,1)}), s8[4194304]{0:T(1024)(128)(4,1)S(1)}, s32[]{:S(2)}) async-start(s8[16777216]{0:T(1024)(128)(4,1)} %bitcast.2), calls=%async_computation | async-start | bytes 8388608
  12.8 18.5 %slice-start.1 = ((s8[16777216]{0:T(1024)(128)(4,1)}), s8[4194304]{0:T(1024)(128)(4,1)S(1)}, s32[]{:S(2)}) async-start(s8[16777216]{0:T(1024)(128)(4,1)} %bitcast.2), calls=%async_computation.1 | async-start | bytes 8388608
  12.8 6.1 %collective-permute-start.4 = (f32[1,40,128]{2,1,0:T(8,128)S(1)}, f32[1,40,128]{2,1,0:T(8,128)S(1)}, u32[]{:S(2)}, u32[]{:S(2)}) collective-permute-start(f32[1,40,128]{2,1,0:T(8,128)S(1)} %get-tuple-element.23), channel_id=1, source_target_pairs={{0,8},{2,10},{4,12},{6,14},{8,0},{10,2},{12,4},{14,6},{1,9},{3,11}... | collective-permute-start | bytes 61448 | tf_op jit(solution)/shard_map/ppermute | solution.py:331
  16.2 4.2 %collective-permute-start.5 = (f32[1,40,128]{2,1,0:T(8,128)S(1)}, f32[1,40,128]{2,1,0:T(8,128)S(1)}, u32[]{:S(2)}, u32[]{:S(2)}) collective-permute-start(f32[1,40,128]{2,1,0:T(8,128)S(1)} %get-tuple-element.22), channel_id=1, source_target_pairs={{0,9},{1,8},{2,11},{3,10},{4,13},{5,12},{6,15},{7,14},{8,1},{9,0},... | collective-permute-start | bytes 61448 | tf_op jit(solution)/shard_map/ppermute | solution.py:336
  18.9 1.5 %collective-permute-start.6 = (f32[1,40,128]{2,1,0:T(8,128)S(1)}, f32[1,40,128]{2,1,0:T(8,128)S(1)}, u32[]{:S(2)}, u32[]{:S(2)}) collective-permute-start(f32[1,40,128]{2,1,0:T(8,128)S(1)} %get-tuple-element.21), channel_id=1, source_target_pairs={{0,1},{1,0},{2,3},{3,2},{4,5},{5,4},{6,7},{7,6},{8,9},{9,8},{10,11... | collective-permute-start | bytes 61448 | tf_op jit(solution)/shard_map/ppermute | solution.py:331
  20.4 10.9 %slice-start.2 = ((s8[16777216]{0:T(1024)(128)(4,1)}), s8[4194304]{0:T(1024)(128)(4,1)S(1)}, s32[]{:S(2)}) async-start(s8[16777216]{0:T(1024)(128)(4,1)} %bitcast.2), calls=%async_computation.2 | async-start | bytes 8388608
  20.4 10.9 %slice-start.3 = ((s8[16777216]{0:T(1024)(128)(4,1)}), s8[4194304]{0:T(1024)(128)(4,1)S(1)}, s32[]{:S(2)}) async-start(s8[16777216]{0:T(1024)(128)(4,1)} %bitcast.2), calls=%async_computation.3 | async-start | bytes 8388608
  21.4 4.1 %collective-permute-start.7 = (bf16[1,32,128]{2,1,0:T(8,128)(2,1)S(1)}, bf16[1,32,128]{2,1,0:T(8,128)(2,1)S(1)}, u32[]{:S(2)}, u32[]{:S(2)}) collective-permute-start(bf16[1,32,128]{2,1,0:T(8,128)(2,1)S(1)} %attend.1.refs_4_), channel_id=1, source_target_pairs={{0,9},{1,8},{2,11},{3,10},{4,13},{5,12},{6,15},{7,14},{8,1},{9,0},... | collective-permute-start | bytes 24584 | tf_op jit(solution)/shard_map/ppermute | solution.py:336
  24.1 1.4 %collective-permute-start.8 = (bf16[1,32,128]{2,1,0:T(8,128)(2,1)S(1)}, bf16[1,32,128]{2,1,0:T(8,128)(2,1)S(1)}, u32[]{:S(2)}, u32[]{:S(2)}) collective-permute-start(bf16[1,32,128]{2,1,0:T(8,128)(2,1)S(1)} %attend.1.refs_4_), channel_id=1, source_target_pairs={{0,1},{1,0},{2,3},{3,2},{4,5},{5,4},{6,7},{7,6},{8,9},{9,8},{10,11... | collective-permute-start | bytes 24584 | tf_op jit(solution)/shard_map/ppermute | solution.py:331
  25.5 4.3 %collective-permute-start.10 = (bf16[2,32,128]{2,1,0:T(8,128)(2,1)S(1)}, bf16[2,32,128]{2,1,0:T(8,128)(2,1)S(1)}, u32[]{:S(2)}, u32[]{:S(2)}) collective-permute-start(bf16[2,32,128]{2,1,0:T(8,128)(2,1)S(1)} %constant_dynamic-update-slice_fusion), channel_id=1, source_target_pairs={{0,7},{1,6},{2,5},{3,4},{4,3},{5,2},{6,1},{7,0},{8,15},{9,14},{10,... | collective-permute-start | bytes 49160 | tf_op jit(solution)/shard_map/ppermute | solution.py:336
  27.6 3.2 %collective-permute-start.11 = (bf16[2,32,128]{2,1,0:T(8,128)(2,1)S(1)}, bf16[2,32,128]{2,1,0:T(8,128)(2,1)S(1)}, u32[]{:S(2)}, u32[]{:S(2)}) collective-permute-start(bf16[2,32,128]{2,1,0:T(8,128)(2,1)S(1)} %constant_dynamic-update-slice_fusion), channel_id=1, source_target_pairs={{0,3},{1,2},{2,1},{3,0},{4,7},{5,6},{6,5},{7,4},{8,11},{9,10},{10,... | collective-permute-start | bytes 49160 | tf_op jit(solution)/shard_map/ppermute | solution.py:336
  28.2 3.2 %collective-permute-start.9 = (bf16[2,32,128]{2,1,0:T(8,128)(2,1)S(1)}, bf16[2,32,128]{2,1,0:T(8,128)(2,1)S(1)}, u32[]{:S(2)}, u32[]{:S(2)}) collective-permute-start(bf16[2,32,128]{2,1,0:T(8,128)(2,1)S(1)} %constant_dynamic-update-slice_fusion), channel_id=1, source_target_pairs={{0,5},{1,4},{2,7},{3,6},{4,1},{5,0},{6,3},{7,2},{8,13},{9,12},{10,... | collective-permute-start | bytes 49160 | tf_op jit(solution)/shard_map/ppermute | solution.py:336
  28.7 1.2 %collective-permute-start.12 = (bf16[1,32,128]{2,1,0:T(8,128)(2,1)S(1)}, bf16[1,32,128]{2,1,0:T(8,128)(2,1)S(1)}, u32[]{:S(2)}, u32[]{:S(2)}) collective-permute-start(bf16[1,32,128]{2,1,0:T(8,128)(2,1)S(1)} %collective-permute-done.7), channel_id=1, source_target_pairs={{0,1},{1,0},{2,3},{3,2},{4,5},{5,4},{6,7},{7,6},{8,9},{9,8},{10,11... | collective-permute-start | bytes 24584 | tf_op jit(solution)/shard_map/ppermute | solution.py:331
  33.7 1.3 %collective-permute-start.13 = (f32[4,2048]{1,0:T(4,128)S(1)}, f32[4,2048]{1,0:T(4,128)S(1)}, u32[]{:S(2)}, u32[]{:S(2)}) collective-permute-start(f32[4,2048]{1,0:T(4,128)S(1)} %get-tuple-element.20), channel_id=1, source_target_pairs={{0,1},{1,0},{2,3},{3,2},{4,5},{5,4},{6,7},{7,6},{8,9},{9,8},{10,11... | collective-permute-start | bytes 98312 | tf_op jit(solution)/shard_map/ppermute | solution.py:331

commit v17 on v16

--- a/solution.py
+++ b/solution.py
@@ -360,13 +360,13 @@
     if devices == 2 * FAN:
         far = FAN
         arrived = fan(pieces, lambda block, mask: cross(block, devices, mask))
-        early = swap(pieces[0][1:], "gx", devices, far)
-        turn = turning(lengths, frequency, w_out, pieces[0])
-        total = arrived[2] + (arrived[1] + arrived[0])
+        beside = swap(pieces[0], "gy", 2, 1)
+        turn = turning(lengths, frequency, w_out, pieces[3])
+        total = arrived[2] + (arrived[1] + (arrived[0] + beside))
         total, turn = lax.optimization_barrier((total, turn))
         crossed = cross(total[1:], devices, far)
         beside = swap(total[:1], "gy", 2, 1)
-        parts = [pieces[0][:1], early, crossed, beside]
+        parts = [crossed, beside]
         heads = attend(parts, turn, k_cache, value_cache, query_heads, w_out)
         crossed = cross(heads, devices, far)
         beside = swap(heads, "gy", 2, 1)
@@ -376,7 +376,7 @@
         order, turned = (2, 4, 3, 1, 0), -1
     else:
         arrived = fan(pieces, lambda block, mask: swap(block, "gx", devices, mask))
-        turn = turning(lengths, frequency, w_out, pieces[0])
+        turn = turning(lengths, frequency, w_out, pieces[3])
         total = pieces[0] + (arrived[2] + (arrived[1] + arrived[0]))
         mask = FAN
         while total.shape[0] > 2:

time: 35.7 us -> 34.9 us (0.978)
  starting transfers between devices: 16.6 us -> 13.6 us
  waiting for transfers between devices: 6.64 us -> 8.72 us
    ppermute x8, waiting for transfers between devices: 4.59 us -> 6.86 us  [cross(): return lax.ppermute(block, ('gx', 'gy'), pairs)]
    ppermute x6, starting transfers between devices: 3.95 us -> 1.99 us  [swap(): return lax.ppermute(block, axis, [(i, i ^ mask) for i in range(devices)])]
    ppermute x8, starting transfers between devices: 12.6 us -> 11.6 us  [cross(): return lax.ppermute(block, ('gx', 'gy'), pairs)]
where the time goes in v17:
time: 34.9 us; the launch traced here: 34.8 us
  starting transfers between devices  13.6 us (39%)
  Pallas kernels  10.8 us (31%)
  waiting for transfers between devices  8.72 us (25%)
  between operations  0.79 us (2%)
  other arithmetic  0.71 us (2%)
    ppermute x8, starting transfers between devices, cross(): return lax.ppermute(block, ('gx', 'gy'), pairs)  11.6 us
    ppermute x8, waiting for transfers between devices, cross(): return lax.ppermute(block, ('gx', 'gy'), pairs)  6.86 us
    pallas_call x1, Pallas kernels, project(): pl.pallas_call(functools.partial(project_kernel, bits), out_shape=(piece,...  5.86 us
    pallas_call x1, Pallas kernels, output(): pl.pallas_call(functools.partial(output_kernel, bits, places, turned), ou...  2.32 us
    ppermute x6, starting transfers between devices, swap(): return lax.ppermute(block, axis, [(i, i ^ mask) for i in range(devices)])  1.99 us
    ppermute x6, waiting for transfers between devices, swap(): return lax.ppermute(block, axis, [(i, i ^ mask) for i in range(devices)])  1.86 us
    pallas_call x1, Pallas kernels, stage_rows(): pl.pallas_call(functools.partial(stage_kernel, rows), out_shape=jax.Shape...  1.66 us
    pallas_call x1, Pallas kernels, attend(): pl.pallas_call(functools.partial(attend_kernel, query_heads, kv_heads, le...  0.97 us
  transfers between devices with their start and end apart: 14, of which 8 were waited for; matrix products, arithmetic and copies ran while one was open for 0% of the time, Pallas kernels for 5%

profile of v17, /device:TPU:0, one launch (start us, length us, event | category | flops | bytes accessed | tf_op | source)
XLA Modules:
  0.0 34.8 jit_solution(16139832191788481199)
XLA Ops:
  0.0 0.5 %collective-permute-start = (bf16[4,2048]{1,0:T(4,128)(2,1)}, bf16[4,2048]{1,0:T(4,128)(2,1)S(1)}, u32[]{:S(2)}, u32[]{:S(2)}) collective-permute-start(bf16[4,2048]{1,0:T(4,128)(2,1)} %rows_ref.1), channel_id=1, source_target_pairs={{0,1},{1,0},{2,3},{3,2},{4,5},{5,4},{6,7},{7,6},{8,9},{9,8},{10,11... | collective-permute-start | bytes 49160 | tf_op jit(solution)/shard_map/ppermute | solution.py:331
  0.5 1.7 %stage.1.first = bf16[256,4096]{1,0:T(8,128)(2,1)S(1)} custom-call(bf16[2048,4096]{1,0:T(8,128)(2,1)} %wq_hbm.1), custom_call_target="tpu_custom_call" | custom-call | bytes 2097152 | tf_op jit(solution)/shard_map/stage/pallas_call | solution.py:57
  2.3 5.9 %project.1 = (f32[2,40,128]{2,1,0:T(8,128)S(1)}, f32[2,40,128]{2,1,0:T(8,128)S(1)}, f32[2,40,128]{2,1,0:T(8,128)S(1)}, f32[2,40,128]{2,1,0:T(8,128)S(1)}) custom-call(bf16[4,2048]{1,0:T(4,128)(2,1)S(1)} %copy-done.4, bf16[4,2048]{1,0:T(4,128)(2,1)S(1)} %collective-permute-done.other_ref, bf16[2048,4096]{1,0:T(8,128)(2,1)} %wq_hbm.1, ...), custom_call_target="tpu_custom_call" | custom-call | flops 150994944 | bytes 18874368 | tf_op jit(solution)/shard_map/project/pallas_call | solution.py:168
  8.1 3.6 %collective-permute-start.1 = (f32[2,40,128]{2,1,0:T(8,128)S(1)}, f32[2,40,128]{2,1,0:T(8,128)S(1)}, u32[]{:S(2)}, u32[]{:S(2)}) collective-permute-start(f32[2,40,128]{2,1,0:T(8,128)S(1)} %get-tuple-element.13.after_ref), channel_id=1, source_target_pairs={{0,7},{1,6},{2,5},{3,4},{4,3},{5,2},{6,1},{7,0},{8,15},{9,14},{10,... | collective-permute-start | bytes 122888 | tf_op jit(solution)/shard_map/ppermute | solution.py:336
  11.7 0.7 %collective-permute-start.2 = (f32[2,40,128]{2,1,0:T(8,128)S(1)}, f32[2,40,128]{2,1,0:T(8,128)S(1)}, u32[]{:S(2)}, u32[]{:S(2)}) collective-permute-start(f32[2,40,128]{2,1,0:T(8,128)S(1)} %get-tuple-element.14), channel_id=1, source_target_pairs={{0,3},{1,2},{2,1},{3,0},{4,7},{5,6},{6,5},{7,4},{8,11},{9,10},{10,... | collective-permute-start | bytes 122888 | tf_op jit(solution)/shard_map/ppermute | solution.py:336
  13.3 0.4 %collective-permute-done.1 = f32[2,40,128]{2,1,0:T(8,128)S(1)} collective-permute-done((f32[2,40,128]{2,1,0:T(8,128)S(1)}, f32[2,40,128]{2,1,0:T(8,128)S(1)}, u32[]{:S(2)}, u32[]{:S(2)}) %collective-permute-start.1) | collective-permute-done | bytes 40992 | tf_op jit(solution)/shard_map/ppermute | solution.py:336
  13.7 1.5 %collective-permute-done.2 = f32[2,40,128]{2,1,0:T(8,128)S(1)} collective-permute-done((f32[2,40,128]{2,1,0:T(8,128)S(1)}, f32[2,40,128]{2,1,0:T(8,128)S(1)}, u32[]{:S(2)}, u32[]{:S(2)}) %collective-permute-start.2) | collective-permute-done | bytes 40992 | tf_op jit(solution)/shard_map/ppermute | solution.py:336
  15.1 1.0 %collective-permute-done.3 = f32[2,40,128]{2,1,0:T(8,128)S(1)} collective-permute-done((f32[2,40,128]{2,1,0:T(8,128)S(1)}, f32[2,40,128]{2,1,0:T(8,128)S(1)}, u32[]{:S(2)}, u32[]{:S(2)}) %collective-permute-start.3) | collective-permute-done | bytes 40992 | tf_op jit(solution)/shard_map/ppermute | solution.py:336
  16.1 2.4 %collective-permute-start.5 = (f32[1,40,128]{2,1,0:T(8,128)S(1)}, f32[1,40,128]{2,1,0:T(8,128)S(1)}, u32[]{:S(2)}, u32[]{:S(2)}) collective-permute-start(f32[1,40,128]{2,1,0:T(8,128)S(1)} %get-tuple-element.22), channel_id=1, source_target_pairs={{0,9},{1,8},{2,11},{3,10},{4,13},{5,12},{6,15},{7,14},{8,1},{9,0},... | collective-permute-start | bytes 61448 | tf_op jit(solution)/shard_map/ppermute | solution.py:336
  18.5 0.4 %collective-permute-start.6 = (f32[1,40,128]{2,1,0:T(8,128)S(1)}, f32[1,40,128]{2,1,0:T(8,128)S(1)}, u32[]{:S(2)}, u32[]{:S(2)}) collective-permute-start(f32[1,40,128]{2,1,0:T(8,128)S(1)} %get-tuple-element.21), channel_id=1, source_target_pairs={{0,1},{1,0},{2,3},{3,2},{4,5},{5,4},{6,7},{7,6},{8,9},{9,8},{10,11... | collective-permute-start | bytes 61448 | tf_op jit(solution)/shard_map/ppermute | solution.py:331
  18.9 1.8 %collective-permute-done.5.refs_0_ = f32[1,40,128]{2,1,0:T(8,128)S(1)} collective-permute-done((f32[1,40,128]{2,1,0:T(8,128)S(1)}, f32[1,40,128]{2,1,0:T(8,128)S(1)}, u32[]{:S(2)}, u32[]{:S(2)}) %collective-permute-start.5) | collective-permute-done | bytes 20512 | tf_op jit(solution)/shard_map/ppermute | solution.py:336
  20.8 1.0 %attend.1.refs_4_ = bf16[1,32,128]{2,1,0:T(8,128)(2,1)S(1)} custom-call(bf16[4096,2048]{1,0:T(8,128)(2,1)} %refs_5_.1, f32[8,128]{1,0:T(8,128)S(1)} %turning.1.turn_ref, bf16[1,2,2048,128]{3,2,1,0:T(8,128)(2,1)S(1)} %copy-done.2, bf16[1,2,2048,128]{3,2,1,0:T(8,128)(2,1)S(1)} %copy-done.3, f32[1,40,128]{2,1,0:T(8,128)S(1)} %collective-permute-done.5.refs_0_, ...), custom_call_target="tpu_custom_call" | custom-call | flops 33554432 | bytes 2097152 | tf_op jit(solution)/shard_map/attend/pallas_call | solution.py:257
  21.7 1.9 %collective-permute-start.7 = (bf16[1,32,128]{2,1,0:T(8,128)(2,1)S(1)}, bf16[1,32,128]{2,1,0:T(8,128)(2,1)S(1)}, u32[]{:S(2)}, u32[]{:S(2)}) collective-permute-start(bf16[1,32,128]{2,1,0:T(8,128)(2,1)S(1)} %attend.1.refs_4_), channel_id=1, source_target_pairs={{0,9},{1,8},{2,11},{3,10},{4,13},{5,12},{6,15},{7,14},{8,1},{9,0},... | collective-permute-start | bytes 24584 | tf_op jit(solution)/shard_map/ppermute | solution.py:336
  23.7 0.4 %collective-permute-start.8 = (bf16[1,32,128]{2,1,0:T(8,128)(2,1)S(1)}, bf16[1,32,128]{2,1,0:T(8,128)(2,1)S(1)}, u32[]{:S(2)}, u32[]{:S(2)}) collective-permute-start(bf16[1,32,128]{2,1,0:T(8,128)(2,1)S(1)} %attend.1.refs_4_), channel_id=1, source_target_pairs={{0,1},{1,0},{2,3},{3,2},{4,5},{5,4},{6,7},{7,6},{8,9},{9,8},{10,11... | collective-permute-start | bytes 24584 | tf_op jit(solution)/shard_map/ppermute | solution.py:331
  24.1 1.8 %collective-permute-done.7 = bf16[1,32,128]{2,1,0:T(8,128)(2,1)S(1)} collective-permute-done((bf16[1,32,128]{2,1,0:T(8,128)(2,1)S(1)}, bf16[1,32,128]{2,1,0:T(8,128)(2,1)S(1)}, u32[]{:S(2)}, u32[]{:S(2)}) %collective-permute-start.7) | collective-permute-done | bytes 8224 | tf_op jit(solution)/shard_map/ppermute | solution.py:336
  25.9 0.7 %collective-permute-start.10 = (bf16[2,32,128]{2,1,0:T(8,128)(2,1)S(1)}, bf16[2,32,128]{2,1,0:T(8,128)(2,1)S(1)}, u32[]{:S(2)}, u32[]{:S(2)}) collective-permute-start(bf16[2,32,128]{2,1,0:T(8,128)(2,1)S(1)} %constant_dynamic-update-slice_fusion), channel_id=1, source_target_pairs={{0,7},{1,6},{2,5},{3,4},{4,3},{5,2},{6,1},{7,0},{8,15},{9,14},{10,... | collective-permute-start | bytes 49160 | tf_op jit(solution)/shard_map/ppermute | solution.py:336
  26.5 0.8 %collective-permute-start.11 = (bf16[2,32,128]{2,1,0:T(8,128)(2,1)S(1)}, bf16[2,32,128]{2,1,0:T(8,128)(2,1)S(1)}, u32[]{:S(2)}, u32[]{:S(2)}) collective-permute-start(bf16[2,32,128]{2,1,0:T(8,128)(2,1)S(1)} %constant_dynamic-update-slice_fusion), channel_id=1, source_target_pairs={{0,3},{1,2},{2,1},{3,0},{4,7},{5,6},{6,5},{7,4},{8,11},{9,10},{10,... | collective-permute-start | bytes 49160 | tf_op jit(solution)/shard_map/ppermute | solution.py:336
  27.4 1.5 %collective-permute-start.9 = (bf16[2,32,128]{2,1,0:T(8,128)(2,1)S(1)}, bf16[2,32,128]{2,1,0:T(8,128)(2,1)S(1)}, u32[]{:S(2)}, u32[]{:S(2)}) collective-permute-start(bf16[2,32,128]{2,1,0:T(8,128)(2,1)S(1)} %constant_dynamic-update-slice_fusion), channel_id=1, source_target_pairs={{0,5},{1,4},{2,7},{3,6},{4,1},{5,0},{6,3},{7,2},{8,13},{9,12},{10,... | collective-permute-start | bytes 49160 | tf_op jit(solution)/shard_map/ppermute | solution.py:336
  28.9 0.4 %collective-permute-start.12 = (bf16[1,32,128]{2,1,0:T(8,128)(2,1)S(1)}, bf16[1,32,128]{2,1,0:T(8,128)(2,1)S(1)}, u32[]{:S(2)}, u32[]{:S(2)}) collective-permute-start(bf16[1,32,128]{2,1,0:T(8,128)(2,1)S(1)} %collective-permute-done.7), channel_id=1, source_target_pairs={{0,1},{1,0},{2,3},{3,2},{4,5},{5,4},{6,7},{7,6},{8,9},{9,8},{10,11... | collective-permute-start | bytes 24584 | tf_op jit(solution)/shard_map/ppermute | solution.py:331
  29.3 0.8 %collective-permute-done.12.refs_3_ = bf16[1,32,128]{2,1,0:T(8,128)(2,1)S(1)} collective-permute-done((bf16[1,32,128]{2,1,0:T(8,128)(2,1)S(1)}, bf16[1,32,128]{2,1,0:T(8,128)(2,1)S(1)}, u32[]{:S(2)}, u32[]{:S(2)}) %collective-permute-start.12) | collective-permute-done | bytes 8224 | tf_op jit(solution)/shard_map/ppermute | solution.py:331
  30.1 0.4 %collective-permute-done.9.refs_0_ = bf16[2,32,128]{2,1,0:T(8,128)(2,1)S(1)} collective-permute-done((bf16[2,32,128]{2,1,0:T(8,128)(2,1)S(1)}, bf16[2,32,128]{2,1,0:T(8,128)(2,1)S(1)}, u32[]{:S(2)}, u32[]{:S(2)}) %collective-permute-start.9) | collective-permute-done | bytes 16416 | tf_op jit(solution)/shard_map/ppermute | solution.py:336
  30.6 2.3 %output.1 = (f32[4,2048]{1,0:T(4,128)S(1)}, f32[4,2048]{1,0:T(4,128)S(1)}) custom-call(bf16[2,32,128]{2,1,0:T(8,128)(2,1)S(1)} %collective-permute-done.9.refs_0_, bf16[2,32,128]{2,1,0:T(8,128)(2,1)S(1)} %collective-permute-done.10.refs_1_, bf16[2,32,128]{2,1,0:T(8,128)(2,1)S(1)} %collective-permute-done.11.refs_2_, ...), custom_call_target="tpu_custom_call" | custom-call | flops 134217728 | bytes 16777216 | tf_op jit(solution)/shard_map/output/pallas_call | solution.py:312
  33.1 1.0 %collective-permute-done.13 = f32[4,2048]{1,0:T(4,128)S(1)} collective-permute-done((f32[4,2048]{1,0:T(4,128)S(1)}, f32[4,2048]{1,0:T(4,128)S(1)}, u32[]{:S(2)}, u32[]{:S(2)}) %collective-permute-start.13) | collective-permute-done | bytes 32800 | tf_op jit(solution)/shard_map/ppermute | solution.py:331
  34.2 0.6 %add_convert_fusion = bf16[4,2048]{1,0:T(4,128)(2,1)} fusion(f32[4,2048]{1,0:T(4,128)S(1)} %get-tuple-element.19, f32[4,2048]{1,0:T(4,128)S(1)} %collective-permute-done.13), kind=kLoop, calls=%fused_computation.1 | loop fusion | flops 16384 | bytes 81920 | tf_op jit(solution)/shard_map/convert_element_type | solution.py:397
  (35 shorter events, 0.6 us)
Async XLA Ops:
  0.0 2.2 %copy-start.4 = (bf16[4,2048]{1,0:T(4,128)(2,1)S(1)}, bf16[4,2048]{1,0:T(4,128)(2,1)}, u32[]{:S(2)}) copy-start(bf16[4,2048]{1,0:T(4,128)(2,1)} %rows_ref.1) | copy-start | bytes 49156
  0.0 2.2 %copy-start = (bf16[2048,256]{1,0:T(8,128)(2,1)S(1)}, bf16[2048,256]{1,0:T(8,128)(2,1)}, u32[]{:S(2)}) copy-start(bf16[2048,256]{1,0:T(8,128)(2,1)} %wk.1) | copy-start | bytes 3145732
  0.0 2.3 %copy-start.1 = (bf16[2048,256]{1,0:T(8,128)(2,1)S(1)}, bf16[2048,256]{1,0:T(8,128)(2,1)}, u32[]{:S(2)}) copy-start(bf16[2048,256]{1,0:T(8,128)(2,1)} %wv.1) | copy-start | bytes 3145732
  0.0 2.2 %collective-permute-start = (bf16[4,2048]{1,0:T(4,128)(2,1)}, bf16[4,2048]{1,0:T(4,128)(2,1)S(1)}, u32[]{:S(2)}, u32[]{:S(2)}) collective-permute-start(bf16[4,2048]{1,0:T(4,128)(2,1)} %rows_ref.1), channel_id=1, source_target_pairs={{0,1},{1,0},{2,3},{3,2},{4,5},{5,4},{6,7},{7,6},{8,9},{9,8},{10,11... | collective-permute-start | bytes 49160 | tf_op jit(solution)/shard_map/ppermute | solution.py:331
  2.2 18.6 %copy-start.2 = (bf16[1,2,2048,128]{3,2,1,0:T(8,128)(2,1)S(1)}, bf16[1,2,2048,128]{3,2,1,0:T(8,128)(2,1)}, u32[]{:S(2)}) copy-start(bf16[1,2,2048,128]{3,2,1,0:T(8,128)(2,1)} %k_ref.1) | copy-start | bytes 3145732
  2.2 18.6 %copy-start.3 = (bf16[1,2,2048,128]{3,2,1,0:T(8,128)(2,1)S(1)}, bf16[1,2,2048,128]{3,2,1,0:T(8,128)(2,1)}, u32[]{:S(2)}) copy-start(bf16[1,2,2048,128]{3,2,1,0:T(8,128)(2,1)} %v_ref.1) | copy-start | bytes 3145732
  8.1 5.5 %collective-permute-start.1 = (f32[2,40,128]{2,1,0:T(8,128)S(1)}, f32[2,40,128]{2,1,0:T(8,128)S(1)}, u32[]{:S(2)}, u32[]{:S(2)}) collective-permute-start(f32[2,40,128]{2,1,0:T(8,128)S(1)} %get-tuple-element.13.after_ref), channel_id=1, source_target_pairs={{0,7},{1,6},{2,5},{3,4},{4,3},{5,2},{6,1},{7,0},{8,15},{9,14},{10,... | collective-permute-start | bytes 122888 | tf_op jit(solution)/shard_map/ppermute | solution.py:336
  11.7 3.4 %collective-permute-start.2 = (f32[2,40,128]{2,1,0:T(8,128)S(1)}, f32[2,40,128]{2,1,0:T(8,128)S(1)}, u32[]{:S(2)}, u32[]{:S(2)}) collective-permute-start(f32[2,40,128]{2,1,0:T(8,128)S(1)} %get-tuple-element.14), channel_id=1, source_target_pairs={{0,3},{1,2},{2,1},{3,0},{4,7},{5,6},{6,5},{7,4},{8,11},{9,10},{10,... | collective-permute-start | bytes 122888 | tf_op jit(solution)/shard_map/ppermute | solution.py:336
  12.4 3.7 %collective-permute-start.3 = (f32[2,40,128]{2,1,0:T(8,128)S(1)}, f32[2,40,128]{2,1,0:T(8,128)S(1)}, u32[]{:S(2)}, u32[]{:S(2)}) collective-permute-start(f32[2,40,128]{2,1,0:T(8,128)S(1)} %get-tuple-element.15), channel_id=1, source_target_pairs={{0,5},{1,4},{2,7},{3,6},{4,1},{5,0},{6,3},{7,2},{8,13},{9,12},{10,... | collective-permute-start | bytes 122888 | tf_op jit(solution)/shard_map/ppermute | solution.py:336
  12.5 3.6 %collective-permute-start.4 = (f32[2,40,128]{2,1,0:T(8,128)S(1)}, f32[2,40,128]{2,1,0:T(8,128)S(1)}, u32[]{:S(2)}, u32[]{:S(2)}) collective-permute-start(f32[2,40,128]{2,1,0:T(8,128)S(1)} %get-tuple-element.16), channel_id=1, source_target_pairs={{0,1},{1,0},{2,3},{3,2},{4,5},{5,4},{6,7},{7,6},{8,9},{9,8},{10,11... | collective-permute-start | bytes 122888 | tf_op jit(solution)/shard_map/ppermute | solution.py:331
  13.2 17.3 %slice-start = ((s8[16777216]{0:T(1024)(128)(4,1)}), s8[4194304]{0:T(1024)(128)(4,1)S(1)}, s32[]{:S(2)}) async-start(s8[16777216]{0:T(1024)(128)(4,1)} %bitcast.2), calls=%async_computation | async-start | bytes 8388608
  13.2 17.3 %slice-start.1 = ((s8[16777216]{0:T(1024)(128)(4,1)}), s8[4194304]{0:T(1024)(128)(4,1)S(1)}, s32[]{:S(2)}) async-start(s8[16777216]{0:T(1024)(128)(4,1)} %bitcast.2), calls=%async_computation.1 | async-start | bytes 8388608
  16.1 4.6 %collective-permute-start.5 = (f32[1,40,128]{2,1,0:T(8,128)S(1)}, f32[1,40,128]{2,1,0:T(8,128)S(1)}, u32[]{:S(2)}, u32[]{:S(2)}) collective-permute-start(f32[1,40,128]{2,1,0:T(8,128)S(1)} %get-tuple-element.22), channel_id=1, source_target_pairs={{0,9},{1,8},{2,11},{3,10},{4,13},{5,12},{6,15},{7,14},{8,1},{9,0},... | collective-permute-start | bytes 61448 | tf_op jit(solution)/shard_map/ppermute | solution.py:336
  18.5 12.0 %slice-start.2 = ((s8[16777216]{0:T(1024)(128)(4,1)}), s8[4194304]{0:T(1024)(128)(4,1)S(1)}, s32[]{:S(2)}) async-start(s8[16777216]{0:T(1024)(128)(4,1)} %bitcast.2), calls=%async_computation.2 | async-start | bytes 8388608
  18.5 12.0 %slice-start.3 = ((s8[16777216]{0:T(1024)(128)(4,1)}), s8[4194304]{0:T(1024)(128)(4,1)S(1)}, s32[]{:S(2)}) async-start(s8[16777216]{0:T(1024)(128)(4,1)} %bitcast.2), calls=%async_computation.3 | async-start | bytes 8388608
  18.5 2.2 %collective-permute-start.6 = (f32[1,40,128]{2,1,0:T(8,128)S(1)}, f32[1,40,128]{2,1,0:T(8,128)S(1)}, u32[]{:S(2)}, u32[]{:S(2)}) collective-permute-start(f32[1,40,128]{2,1,0:T(8,128)S(1)} %get-tuple-element.21), channel_id=1, source_target_pairs={{0,1},{1,0},{2,3},{3,2},{4,5},{5,4},{6,7},{7,6},{8,9},{9,8},{10,11... | collective-permute-start | bytes 61448 | tf_op jit(solution)/shard_map/ppermute | solution.py:331
  21.7 4.1 %collective-permute-start.7 = (bf16[1,32,128]{2,1,0:T(8,128)(2,1)S(1)}, bf16[1,32,128]{2,1,0:T(8,128)(2,1)S(1)}, u32[]{:S(2)}, u32[]{:S(2)}) collective-permute-start(bf16[1,32,128]{2,1,0:T(8,128)(2,1)S(1)} %attend.1.refs_4_), channel_id=1, source_target_pairs={{0,9},{1,8},{2,11},{3,10},{4,13},{5,12},{6,15},{7,14},{8,1},{9,0},... | collective-permute-start | bytes 24584 | tf_op jit(solution)/shard_map/ppermute | solution.py:336
  23.7 2.2 %collective-permute-start.8 = (bf16[1,32,128]{2,1,0:T(8,128)(2,1)S(1)}, bf16[1,32,128]{2,1,0:T(8,128)(2,1)S(1)}, u32[]{:S(2)}, u32[]{:S(2)}) collective-permute-start(bf16[1,32,128]{2,1,0:T(8,128)(2,1)S(1)} %attend.1.refs_4_), channel_id=1, source_target_pairs={{0,1},{1,0},{2,3},{3,2},{4,5},{5,4},{6,7},{7,6},{8,9},{9,8},{10,11... | collective-permute-start | bytes 24584 | tf_op jit(solution)/shard_map/ppermute | solution.py:331
  25.9 4.3 %collective-permute-start.10 = (bf16[2,32,128]{2,1,0:T(8,128)(2,1)S(1)}, bf16[2,32,128]{2,1,0:T(8,128)(2,1)S(1)}, u32[]{:S(2)}, u32[]{:S(2)}) collective-permute-start(bf16[2,32,128]{2,1,0:T(8,128)(2,1)S(1)} %constant_dynamic-update-slice_fusion), channel_id=1, source_target_pairs={{0,7},{1,6},{2,5},{3,4},{4,3},{5,2},{6,1},{7,0},{8,15},{9,14},{10,... | collective-permute-start | bytes 49160 | tf_op jit(solution)/shard_map/ppermute | solution.py:336
  26.5 3.6 %collective-permute-start.11 = (bf16[2,32,128]{2,1,0:T(8,128)(2,1)S(1)}, bf16[2,32,128]{2,1,0:T(8,128)(2,1)S(1)}, u32[]{:S(2)}, u32[]{:S(2)}) collective-permute-start(bf16[2,32,128]{2,1,0:T(8,128)(2,1)S(1)} %constant_dynamic-update-slice_fusion), channel_id=1, source_target_pairs={{0,3},{1,2},{2,1},{3,0},{4,7},{5,6},{6,5},{7,4},{8,11},{9,10},{10,... | collective-permute-start | bytes 49160 | tf_op jit(solution)/shard_map/ppermute | solution.py:336
  27.4 3.2 %collective-permute-start.9 = (bf16[2,32,128]{2,1,0:T(8,128)(2,1)S(1)}, bf16[2,32,128]{2,1,0:T(8,128)(2,1)S(1)}, u32[]{:S(2)}, u32[]{:S(2)}) collective-permute-start(bf16[2,32,128]{2,1,0:T(8,128)(2,1)S(1)} %constant_dynamic-update-slice_fusion), channel_id=1, source_target_pairs={{0,5},{1,4},{2,7},{3,6},{4,1},{5,0},{6,3},{7,2},{8,13},{9,12},{10,... | collective-permute-start | bytes 49160 | tf_op jit(solution)/shard_map/ppermute | solution.py:336
  28.9 1.3 %collective-permute-start.12 = (bf16[1,32,128]{2,1,0:T(8,128)(2,1)S(1)}, bf16[1,32,128]{2,1,0:T(8,128)(2,1)S(1)}, u32[]{:S(2)}, u32[]{:S(2)}) collective-permute-start(bf16[1,32,128]{2,1,0:T(8,128)(2,1)S(1)} %collective-permute-done.7), channel_id=1, source_target_pairs={{0,1},{1,0},{2,3},{3,2},{4,5},{5,4},{6,7},{7,6},{8,9},{9,8},{10,11... | collective-permute-start | bytes 24584 | tf_op jit(solution)/shard_map/ppermute | solution.py:331
  32.9 1.3 %collective-permute-start.13 = (f32[4,2048]{1,0:T(4,128)S(1)}, f32[4,2048]{1,0:T(4,128)S(1)}, u32[]{:S(2)}, u32[]{:S(2)}) collective-permute-start(f32[4,2048]{1,0:T(4,128)S(1)} %get-tuple-element.20), channel_id=1, source_target_pairs={{0,1},{1,0},{2,3},{3,2},{4,5},{5,4},{6,7},{7,6},{8,9},{9,8},{10,11... | collective-permute-start | bytes 98312 | tf_op jit(solution)/shard_map/ppermute | solution.py:331

commit v18 on v17

--- a/solution.py
+++ b/solution.py
@@ -68,28 +68,32 @@
     )(in_hbm(array))
 
 
-def turning_kernel(length_ref, frequency_ref, beside_ref, after_ref, turn_ref):
+def turning_kernel(length_ref, frequency_ref, beside_ref, after_ref, turn_ref, mask_ref):
     position = length_ref[0].astype(jnp.float32)
     angle = position * frequency_ref[...]
     lane = lax.broadcasted_iota(jnp.int32, angle.shape, 1)
     sine = jnp.sin(angle)
     turn_ref[0:1, :] = jnp.cos(angle)
     turn_ref[1:2, :] = jnp.where(lane < HEAD_SIZE // 2, -sine, sine)
-    turn_ref[2:3, :] = jnp.full(angle.shape, position)
-
-
-def turning(lengths, frequency, beside, after):
+    slot = lax.broadcasted_iota(jnp.int32, mask_ref.shape, 1)
+    mask_ref[...] = jnp.where(slot < length_ref[0], 0.0, -jnp.inf)
+
+
+def turning(lengths, frequency, beside, after, cache_len):
     vmem = pl.BlockSpec(memory_space=pltpu.VMEM)
     return pl.pallas_call(
         turning_kernel,
-        out_shape=jax.ShapeDtypeStruct((8, HEAD_SIZE), jnp.float32),
+        out_shape=(
+            jax.ShapeDtypeStruct((8, HEAD_SIZE), jnp.float32),
+            jax.ShapeDtypeStruct((1, cache_len), jnp.float32),
+        ),
         in_specs=[
             pl.BlockSpec(memory_space=pltpu.SMEM),
             vmem,
             pl.BlockSpec(memory_space=pltpu.HBM),
             vmem,
         ],
-        out_specs=vmem,
+        out_specs=(vmem, vmem),
         compiler_params=pltpu.CompilerParams(vmem_limit_bytes=2 * MIB),
         cost_estimate=pl.CostEstimate(flops=0, bytes_accessed=2 * beside.size, transcendentals=256),
         name="turning",
@@ -131,7 +135,24 @@
     squares = jnp.sum(wide * wide, axis=1, keepdims=True)
     narrow = wide.astype(jnp.bfloat16)
 
-    fresh = [jnp.dot(narrow, w[...], preferred_element_type=jnp.float32) for w in (wk, wv)]
+    total = pieces[0].shape[1]
+    each = slots // FAN
+    flats = [ref.reshape(each * total, LANES) for ref in pieces]
+
+    def put(first_block, part):
+        for i in range(0, part.shape[1], LANES):
+            for at, flat in enumerate(flats):
+                flat[pl.ds(first_block + i // LANES, each, stride=total), :] = part[
+                    at * each : (at + 1) * each, i : i + LANES
+                ]
+
+    at = wq.shape[1] // LANES
+    for w in (wk, wv):
+        put(at, jnp.dot(narrow, w[...], preferred_element_type=jnp.float32))
+        at += w.shape[1] // LANES
+    put(at, jnp.broadcast_to(squares, (slots, LANES)))
+    put(at + 1, jnp.zeros((slots, (total - at - 1) * LANES), jnp.float32))
+
     sums = jnp.dot(narrow[:, :skip], first[...], preferred_element_type=jnp.float32)
     for (start, size), group in zip(ranges, copies):
         for copy in group:
@@ -142,17 +163,7 @@
             preferred_element_type=jnp.float32,
         )
 
-    total = pieces[0].shape[1]
-    blocks = []
-    for part in (sums, *fresh):
-        blocks += [part[:, i : i + LANES] for i in range(0, part.shape[1], LANES)]
-    blocks.append(jnp.broadcast_to(squares, (slots, LANES)))
-    blocks += [jnp.zeros((slots, LANES), jnp.float32)] * (total - len(blocks))
-    size = slots // FAN
-    for at, ref in enumerate(pieces):
-        flat = ref.reshape(size * total, LANES)
-        for i, block in enumerate(blocks):
-            flat[pl.ds(i, size, stride=total), :] = block[at * size : (at + 1) * size]
+    put(0, sums)
 
 
 def project(rows, other, w_query, first, key_weight, value_weight, slots):
@@ -186,7 +197,7 @@
 
 
 def attend_kernel(
-    query_heads, kv_heads, pieces, beside_ref, turn_ref, k_ref, v_ref, *refs
+    query_heads, kv_heads, pieces, beside_ref, turn_ref, live_ref, k_ref, v_ref, *refs
 ):
     heads_ref = refs[pieces]
     total = refs[0][0]
@@ -201,7 +212,6 @@
     fresh_values = (total[query_heads + kv_heads : at] * scale).astype(jnp.bfloat16)
     group = query_heads // kv_heads
     factor = 1.0 / math.sqrt(HEAD_SIZE)
-    length = turn_ref[2:3, 0:1].astype(jnp.int32)
     side = 2 if kv_heads % 2 == 0 else 1
     for first in range(0, kv_heads, side):
         members = range(first, first + side)
@@ -221,6 +231,7 @@
                 spread_out, keys, (((1,), (1,)), ((), ())), preferred_element_type=jnp.float32
             )
             * factor
+            + live_ref[...]
         )
         own = jnp.concatenate(
             [
@@ -234,30 +245,28 @@
             ],
             axis=0,
         ) * factor
-        slot = lax.broadcasted_iota(jnp.int32, scores.shape, 1)
-        scores = jnp.where(slot < length, scores, -jnp.inf)
         top = jnp.maximum(jnp.max(scores, axis=1, keepdims=True), own)
         exponent = jnp.exp(scores - top)
         own_exp = jnp.exp(own - top)
+        mixed = jnp.dot(
+            exponent.astype(jnp.bfloat16), values, preferred_element_type=jnp.float32
+        )
         share = 1.0 / (jnp.sum(exponent, axis=1, keepdims=True) + own_exp)
-        weights = (exponent * share).astype(jnp.bfloat16)
-        own_weight = (own_exp * share).astype(jnp.bfloat16).astype(jnp.float32)
-        mixed = jnp.dot(weights, values, preferred_element_type=jnp.float32)
         for i, head in enumerate(members):
-            block = mixed[i * group : (i + 1) * group, i * HEAD_SIZE : (i + 1) * HEAD_SIZE]
-            block = block + own_weight[i * group : (i + 1) * group] * fresh_values[
-                head : head + 1
-            ].astype(jnp.float32)
+            part = slice(i * group, (i + 1) * group)
+            block = mixed[part, i * HEAD_SIZE : (i + 1) * HEAD_SIZE]
+            block = block + own_exp[part] * fresh_values[head : head + 1].astype(jnp.float32)
+            block = block * share[part]
             heads_ref[0, pl.ds(head * group, group), :] = block.astype(jnp.bfloat16)
 
 
-def attend(parts, turn, k_cache, value_cache, query_heads, beside):
+def attend(parts, turn, live, k_cache, value_cache, query_heads, beside):
     kv_heads, cache_len = k_cache.shape[1:3]
     whole = pl.BlockSpec(memory_space=pltpu.VMEM)
     return pl.pallas_call(
         functools.partial(attend_kernel, query_heads, kv_heads, len(parts)),
         out_shape=jax.ShapeDtypeStruct((1, query_heads, HEAD_SIZE), jnp.bfloat16),
-        in_specs=[pl.BlockSpec(memory_space=pltpu.HBM)] + [whole] * (3 + len(parts)),
+        in_specs=[pl.BlockSpec(memory_space=pltpu.HBM)] + [whole] * (4 + len(parts)),
         out_specs=whole,
         compiler_params=pltpu.CompilerParams(vmem_limit_bytes=12 * MIB),
         cost_estimate=pl.CostEstimate(
@@ -266,7 +275,7 @@
             transcendentals=query_heads * cache_len,
         ),
         name="attend",
-    )(in_hbm(beside), turn, k_cache, value_cache, *parts)
+    )(in_hbm(beside), turn, live, k_cache, value_cache, *parts)
 
 
 def output_kernel(bits, places, turned, *refs):
@@ -361,13 +370,15 @@
         far = FAN
         arrived = fan(pieces, lambda block, mask: cross(block, devices, mask))
         beside = swap(pieces[0], "gy", 2, 1)
-        turn = turning(lengths, frequency, w_out, pieces[3])
-        total = arrived[2] + (arrived[1] + (arrived[0] + beside))
+        turn, live = turning(lengths, frequency, w_out, pieces[3], k_cache.shape[2])
+        leaving = [x[1:] for x in (*arrived, beside)]
+        staying = [x[:1] for x in (*arrived, beside)]
+        total = leaving[2] + (leaving[1] + (leaving[0] + leaving[3]))
         total, turn = lax.optimization_barrier((total, turn))
-        crossed = cross(total[1:], devices, far)
-        beside = swap(total[:1], "gy", 2, 1)
+        crossed = cross(total, devices, far)
+        beside = swap(staying[2] + (staying[1] + (staying[0] + staying[3])), "gy", 2, 1)
         parts = [crossed, beside]
-        heads = attend(parts, turn, k_cache, value_cache, query_heads, w_out)
+        heads = attend(parts, turn, live, k_cache, value_cache, query_heads, w_out)
         crossed = cross(heads, devices, far)
         beside = swap(heads, "gy", 2, 1)
         held = jnp.concatenate([crossed, beside], axis=0)
@@ -376,7 +387,7 @@
         order, turned = (2, 4, 3, 1, 0), -1
     else:
         arrived = fan(pieces, lambda block, mask: swap(block, "gx", devices, mask))
-        turn = turning(lengths, frequency, w_out, pieces[3])
+        turn, live = turning(lengths, frequency, w_out, pieces[3], k_cache.shape[2])
         total = pieces[0] + (arrived[2] + (arrived[1] + arrived[0]))
         mask = FAN
         while total.shape[0] > 2:
@@ -384,7 +395,7 @@
             total = total[:rest] + swap(total[rest:], "gx", devices, mask)
             mask *= 2
         parts = [total[:1], swap(total[1:], "gx", devices, mask)]
-        heads = attend(parts, turn, k_cache, value_cache, query_heads, w_out)
+        heads = attend(parts, turn, live, k_cache, value_cache, query_heads, w_out)
 
         parts = [heads, swap(heads, "gx", devices, mask)]
         while mask > FAN:

time: 34.9 us -> 34.8 us (level)
  starting transfers between devices: 13.6 us -> 14 us
  waiting for transfers between devices: 8.72 us -> 8.35 us
    ppermute x8, starting transfers between devices: 11.6 us -> 12.4 us  [cross(): return lax.ppermute(block, ('gx', 'gy'), pairs)]
    ppermute x8, waiting for transfers between devices: 6.86 us -> 6.16 us  [cross(): return lax.ppermute(block, ('gx', 'gy'), pairs)]
    ppermute x6, starting transfers between devices: 1.99 us -> 1.58 us  [swap(): return lax.ppermute(block, axis, [(i, i ^ mask) for i in range(devices)])]
where the time goes in v18:
time: 34.8 us; the launch traced here: 34.7 us
  starting transfers between devices  14 us (40%)
  Pallas kernels  10.7 us (31%)
  waiting for transfers between devices  8.35 us (24%)
  between operations  0.82 us (2%)
  other arithmetic  0.71 us (2%)
    ppermute x8, starting transfers between devices, cross(): return lax.ppermute(block, ('gx', 'gy'), pairs)  12.4 us
    ppermute x8, waiting for transfers between devices, cross(): return lax.ppermute(block, ('gx', 'gy'), pairs)  6.16 us
    pallas_call x1, Pallas kernels, project(): pl.pallas_call(functools.partial(project_kernel, bits), out_shape=(piece,...  5.86 us
    pallas_call x1, Pallas kernels, output(): pl.pallas_call(functools.partial(output_kernel, bits, places, turned), ou...  2.31 us
    ppermute x6, waiting for transfers between devices, swap(): return lax.ppermute(block, axis, [(i, i ^ mask) for i in range(devices)])  2.19 us
    pallas_call x1, Pallas kernels, stage_rows(): pl.pallas_call(functools.partial(stage_kernel, rows), out_shape=jax.Shape...  1.66 us
    ppermute x6, starting transfers between devices, swap(): return lax.ppermute(block, axis, [(i, i ^ mask) for i in range(devices)])  1.58 us
    pallas_call x1, Pallas kernels, attend(): pl.pallas_call(functools.partial(attend_kernel, query_heads, kv_heads, le...  0.82 us
  transfers between devices with their start and end apart: 14, of which 8 were waited for; matrix products, arithmetic and copies ran while one was open for 0% of the time, Pallas kernels for 5%

profile of v18, /device:TPU:0, one launch (start us, length us, event | category | flops | bytes accessed | tf_op | source)
XLA Modules:
  0.0 34.7 jit_solution(14320673226950434030)
XLA Ops:
  0.0 0.5 %collective-permute-start = (bf16[4,2048]{1,0:T(4,128)(2,1)}, bf16[4,2048]{1,0:T(4,128)(2,1)S(1)}, u32[]{:S(2)}, u32[]{:S(2)}) collective-permute-start(bf16[4,2048]{1,0:T(4,128)(2,1)} %rows_ref.1), channel_id=1, source_target_pairs={{0,1},{1,0},{2,3},{3,2},{4,5},{5,4},{6,7},{7,6},{8,9},{9,8},{10,11... | collective-permute-start | bytes 49160 | tf_op jit(solution)/shard_map/ppermute | solution.py:340
  0.5 1.7 %stage.1.first = bf16[256,4096]{1,0:T(8,128)(2,1)S(1)} custom-call(bf16[2048,4096]{1,0:T(8,128)(2,1)} %wq_hbm.1), custom_call_target="tpu_custom_call" | custom-call | bytes 2097152 | tf_op jit(solution)/shard_map/stage/pallas_call | solution.py:57
  2.3 5.9 %project.1 = (f32[2,40,128]{2,1,0:T(8,128)S(1)}, f32[2,40,128]{2,1,0:T(8,128)S(1)}, f32[2,40,128]{2,1,0:T(8,128)S(1)}, f32[2,40,128]{2,1,0:T(8,128)S(1)}) custom-call(bf16[4,2048]{1,0:T(4,128)(2,1)S(1)} %copy-done.4, bf16[4,2048]{1,0:T(4,128)(2,1)S(1)} %collective-permute-done.other_ref, bf16[2048,4096]{1,0:T(8,128)(2,1)} %wq_hbm.1, ...), custom_call_target="tpu_custom_call" | custom-call | flops 150994944 | bytes 18874368 | tf_op jit(solution)/shard_map/project/pallas_call | solution.py:179
  8.1 3.6 %collective-permute-start.1 = (f32[2,40,128]{2,1,0:T(8,128)S(1)}, f32[2,40,128]{2,1,0:T(8,128)S(1)}, u32[]{:S(2)}, u32[]{:S(2)}) collective-permute-start(f32[2,40,128]{2,1,0:T(8,128)S(1)} %get-tuple-element.15.after_ref), channel_id=1, source_target_pairs={{0,7},{1,6},{2,5},{3,4},{4,3},{5,2},{6,1},{7,0},{8,15},{9,14},{10,... | collective-permute-start | bytes 122888 | tf_op jit(solution)/shard_map/ppermute | solution.py:345
  11.7 0.7 %collective-permute-start.2 = (f32[2,40,128]{2,1,0:T(8,128)S(1)}, f32[2,40,128]{2,1,0:T(8,128)S(1)}, u32[]{:S(2)}, u32[]{:S(2)}) collective-permute-start(f32[2,40,128]{2,1,0:T(8,128)S(1)} %get-tuple-element.16), channel_id=1, source_target_pairs={{0,3},{1,2},{2,1},{3,0},{4,7},{5,6},{6,5},{7,4},{8,11},{9,10},{10,... | collective-permute-start | bytes 122888 | tf_op jit(solution)/shard_map/ppermute | solution.py:345
  13.3 0.4 %collective-permute-done.1 = f32[2,40,128]{2,1,0:T(8,128)S(1)} collective-permute-done((f32[2,40,128]{2,1,0:T(8,128)S(1)}, f32[2,40,128]{2,1,0:T(8,128)S(1)}, u32[]{:S(2)}, u32[]{:S(2)}) %collective-permute-start.1) | collective-permute-done | bytes 40992 | tf_op jit(solution)/shard_map/ppermute | solution.py:345
  13.7 1.5 %collective-permute-done.2 = f32[2,40,128]{2,1,0:T(8,128)S(1)} collective-permute-done((f32[2,40,128]{2,1,0:T(8,128)S(1)}, f32[2,40,128]{2,1,0:T(8,128)S(1)}, u32[]{:S(2)}, u32[]{:S(2)}) %collective-permute-start.2) | collective-permute-done | bytes 40992 | tf_op jit(solution)/shard_map/ppermute | solution.py:345
  15.1 0.9 %collective-permute-done.3 = f32[2,40,128]{2,1,0:T(8,128)S(1)} collective-permute-done((f32[2,40,128]{2,1,0:T(8,128)S(1)}, f32[2,40,128]{2,1,0:T(8,128)S(1)}, u32[]{:S(2)}, u32[]{:S(2)}) %collective-permute-start.3) | collective-permute-done | bytes 40992 | tf_op jit(solution)/shard_map/ppermute | solution.py:345
  16.1 2.4 %collective-permute-start.5 = (f32[1,40,128]{2,1,0:T(8,128)S(1)}, f32[1,40,128]{2,1,0:T(8,128)S(1)}, u32[]{:S(2)}, u32[]{:S(2)}) collective-permute-start(f32[1,40,128]{2,1,0:T(8,128)S(1)} %get-tuple-element.22), channel_id=1, source_target_pairs={{0,9},{1,8},{2,11},{3,10},{4,13},{5,12},{6,15},{7,14},{8,1},{9,0},... | collective-permute-start | bytes 61448 | tf_op jit(solution)/shard_map/ppermute | solution.py:345
  18.5 0.4 %collective-permute-start.6 = (f32[1,40,128]{2,1,0:T(8,128)S(1)}, f32[1,40,128]{2,1,0:T(8,128)S(1)}, u32[]{:S(2)}, u32[]{:S(2)}) collective-permute-start(f32[1,40,128]{2,1,0:T(8,128)S(1)} %get-tuple-element.25), channel_id=1, source_target_pairs={{0,1},{1,0},{2,3},{3,2},{4,5},{5,4},{6,7},{7,6},{8,9},{9,8},{10,11... | collective-permute-start | bytes 61448 | tf_op jit(solution)/shard_map/ppermute | solution.py:340
  18.9 1.4 %collective-permute-done.5.refs_0_ = f32[1,40,128]{2,1,0:T(8,128)S(1)} collective-permute-done((f32[1,40,128]{2,1,0:T(8,128)S(1)}, f32[1,40,128]{2,1,0:T(8,128)S(1)}, u32[]{:S(2)}, u32[]{:S(2)}) %collective-permute-start.5) | collective-permute-done | bytes 20512 | tf_op jit(solution)/shard_map/ppermute | solution.py:345
  20.3 0.8 %attend.1.refs_4_ = bf16[1,32,128]{2,1,0:T(8,128)(2,1)S(1)} custom-call(bf16[4096,2048]{1,0:T(8,128)(2,1)} %refs_5_.1, f32[8,128]{1,0:T(8,128)S(1)} %get-tuple-element.20.turn_ref, f32[1,2048]{1,0:T(1,128)S(1)} %get-tuple-element.21.live_ref, bf16[1,2,2048,128]{3,2,1,0:T(8,128)(2,1)S(1)} %copy-done.2, bf16[1,2,2048,128]{3,2,1,0:T(8,128)(2,1)S(1)} %copy-done.3, ...), custom_call_target="tpu_custom_call" | custom-call | flops 33554432 | bytes 2097152 | tf_op jit(solution)/shard_map/attend/pallas_call | solution.py:266
  21.2 2.4 %collective-permute-start.7 = (bf16[1,32,128]{2,1,0:T(8,128)(2,1)S(1)}, bf16[1,32,128]{2,1,0:T(8,128)(2,1)S(1)}, u32[]{:S(2)}, u32[]{:S(2)}) collective-permute-start(bf16[1,32,128]{2,1,0:T(8,128)(2,1)S(1)} %attend.1.refs_4_), channel_id=1, source_target_pairs={{0,9},{1,8},{2,11},{3,10},{4,13},{5,12},{6,15},{7,14},{8,1},{9,0},... | collective-permute-start | bytes 24584 | tf_op jit(solution)/shard_map/ppermute | solution.py:345
  23.5 0.4 %collective-permute-start.8 = (bf16[1,32,128]{2,1,0:T(8,128)(2,1)S(1)}, bf16[1,32,128]{2,1,0:T(8,128)(2,1)S(1)}, u32[]{:S(2)}, u32[]{:S(2)}) collective-permute-start(bf16[1,32,128]{2,1,0:T(8,128)(2,1)S(1)} %attend.1.refs_4_), channel_id=1, source_target_pairs={{0,1},{1,0},{2,3},{3,2},{4,5},{5,4},{6,7},{7,6},{8,9},{9,8},{10,11... | collective-permute-start | bytes 24584 | tf_op jit(solution)/shard_map/ppermute | solution.py:340
  23.9 1.3 %collective-permute-done.7 = bf16[1,32,128]{2,1,0:T(8,128)(2,1)S(1)} collective-permute-done((bf16[1,32,128]{2,1,0:T(8,128)(2,1)S(1)}, bf16[1,32,128]{2,1,0:T(8,128)(2,1)S(1)}, u32[]{:S(2)}, u32[]{:S(2)}) %collective-permute-start.7) | collective-permute-done | bytes 8224 | tf_op jit(solution)/shard_map/ppermute | solution.py:345
  25.2 1.2 %collective-permute-start.10 = (bf16[2,32,128]{2,1,0:T(8,128)(2,1)S(1)}, bf16[2,32,128]{2,1,0:T(8,128)(2,1)S(1)}, u32[]{:S(2)}, u32[]{:S(2)}) collective-permute-start(bf16[2,32,128]{2,1,0:T(8,128)(2,1)S(1)} %constant_dynamic-update-slice_fusion), channel_id=1, source_target_pairs={{0,7},{1,6},{2,5},{3,4},{4,3},{5,2},{6,1},{7,0},{8,15},{9,14},{10,... | collective-permute-start | bytes 49160 | tf_op jit(solution)/shard_map/ppermute | solution.py:345
  26.4 0.9 %collective-permute-start.11 = (bf16[2,32,128]{2,1,0:T(8,128)(2,1)S(1)}, bf16[2,32,128]{2,1,0:T(8,128)(2,1)S(1)}, u32[]{:S(2)}, u32[]{:S(2)}) collective-permute-start(bf16[2,32,128]{2,1,0:T(8,128)(2,1)S(1)} %constant_dynamic-update-slice_fusion), channel_id=1, source_target_pairs={{0,3},{1,2},{2,1},{3,0},{4,7},{5,6},{6,5},{7,4},{8,11},{9,10},{10,... | collective-permute-start | bytes 49160 | tf_op jit(solution)/shard_map/ppermute | solution.py:345
  27.2 1.3 %collective-permute-start.9 = (bf16[2,32,128]{2,1,0:T(8,128)(2,1)S(1)}, bf16[2,32,128]{2,1,0:T(8,128)(2,1)S(1)}, u32[]{:S(2)}, u32[]{:S(2)}) collective-permute-start(bf16[2,32,128]{2,1,0:T(8,128)(2,1)S(1)} %constant_dynamic-update-slice_fusion), channel_id=1, source_target_pairs={{0,5},{1,4},{2,7},{3,6},{4,1},{5,0},{6,3},{7,2},{8,13},{9,12},{10,... | collective-permute-start | bytes 49160 | tf_op jit(solution)/shard_map/ppermute | solution.py:345
  28.6 1.1 %collective-permute-done.12.refs_3_ = bf16[1,32,128]{2,1,0:T(8,128)(2,1)S(1)} collective-permute-done((bf16[1,32,128]{2,1,0:T(8,128)(2,1)S(1)}, bf16[1,32,128]{2,1,0:T(8,128)(2,1)S(1)}, u32[]{:S(2)}, u32[]{:S(2)}) %collective-permute-start.12) | collective-permute-done | bytes 8224 | tf_op jit(solution)/shard_map/ppermute | solution.py:340
  29.7 0.7 %collective-permute-done.9.refs_0_ = bf16[2,32,128]{2,1,0:T(8,128)(2,1)S(1)} collective-permute-done((bf16[2,32,128]{2,1,0:T(8,128)(2,1)S(1)}, bf16[2,32,128]{2,1,0:T(8,128)(2,1)S(1)}, u32[]{:S(2)}, u32[]{:S(2)}) %collective-permute-start.9) | collective-permute-done | bytes 16416 | tf_op jit(solution)/shard_map/ppermute | solution.py:345
  30.4 2.3 %output.1 = (f32[4,2048]{1,0:T(4,128)S(1)}, f32[4,2048]{1,0:T(4,128)S(1)}) custom-call(bf16[2,32,128]{2,1,0:T(8,128)(2,1)S(1)} %collective-permute-done.9.refs_0_, bf16[2,32,128]{2,1,0:T(8,128)(2,1)S(1)} %collective-permute-done.10.refs_1_, bf16[2,32,128]{2,1,0:T(8,128)(2,1)S(1)} %collective-permute-done.11.refs_2_, ...), custom_call_target="tpu_custom_call" | custom-call | flops 134217728 | bytes 16777216 | tf_op jit(solution)/shard_map/output/pallas_call | solution.py:321
  32.8 0.2 collective-permute-start.13
  33.0 1.0 %collective-permute-done.13 = f32[4,2048]{1,0:T(4,128)S(1)} collective-permute-done((f32[4,2048]{1,0:T(4,128)S(1)}, f32[4,2048]{1,0:T(4,128)S(1)}, u32[]{:S(2)}, u32[]{:S(2)}) %collective-permute-start.13) | collective-permute-done | bytes 32800 | tf_op jit(solution)/shard_map/ppermute | solution.py:340
  34.0 0.6 %add_convert_fusion = bf16[4,2048]{1,0:T(4,128)(2,1)} fusion(f32[4,2048]{1,0:T(4,128)S(1)} %get-tuple-element.23, f32[4,2048]{1,0:T(4,128)S(1)} %collective-permute-done.13), kind=kLoop, calls=%fused_computation | loop fusion | flops 16384 | bytes 81920 | tf_op jit(solution)/shard_map/convert_element_type | solution.py:408
  (34 shorter events, 0.4 us)
Async XLA Ops:
  0.0 2.2 %copy-start.4 = (bf16[4,2048]{1,0:T(4,128)(2,1)S(1)}, bf16[4,2048]{1,0:T(4,128)(2,1)}, u32[]{:S(2)}) copy-start(bf16[4,2048]{1,0:T(4,128)(2,1)} %rows_ref.1) | copy-start | bytes 49156
  0.0 2.2 %copy-start = (bf16[2048,256]{1,0:T(8,128)(2,1)S(1)}, bf16[2048,256]{1,0:T(8,128)(2,1)}, u32[]{:S(2)}) copy-start(bf16[2048,256]{1,0:T(8,128)(2,1)} %wk.1) | copy-start | bytes 3145732
  0.0 2.3 %copy-start.1 = (bf16[2048,256]{1,0:T(8,128)(2,1)S(1)}, bf16[2048,256]{1,0:T(8,128)(2,1)}, u32[]{:S(2)}) copy-start(bf16[2048,256]{1,0:T(8,128)(2,1)} %wv.1) | copy-start | bytes 3145732
  0.0 2.2 %collective-permute-start = (bf16[4,2048]{1,0:T(4,128)(2,1)}, bf16[4,2048]{1,0:T(4,128)(2,1)S(1)}, u32[]{:S(2)}, u32[]{:S(2)}) collective-permute-start(bf16[4,2048]{1,0:T(4,128)(2,1)} %rows_ref.1), channel_id=1, source_target_pairs={{0,1},{1,0},{2,3},{3,2},{4,5},{5,4},{6,7},{7,6},{8,9},{9,8},{10,11... | collective-permute-start | bytes 49160 | tf_op jit(solution)/shard_map/ppermute | solution.py:340
  2.2 18.1 %copy-start.2 = (bf16[1,2,2048,128]{3,2,1,0:T(8,128)(2,1)S(1)}, bf16[1,2,2048,128]{3,2,1,0:T(8,128)(2,1)}, u32[]{:S(2)}) copy-start(bf16[1,2,2048,128]{3,2,1,0:T(8,128)(2,1)} %k_ref.1) | copy-start | bytes 3145732
  2.2 18.1 %copy-start.3 = (bf16[1,2,2048,128]{3,2,1,0:T(8,128)(2,1)S(1)}, bf16[1,2,2048,128]{3,2,1,0:T(8,128)(2,1)}, u32[]{:S(2)}) copy-start(bf16[1,2,2048,128]{3,2,1,0:T(8,128)(2,1)} %v_ref.1) | copy-start | bytes 3145732
  8.1 5.5 %collective-permute-start.1 = (f32[2,40,128]{2,1,0:T(8,128)S(1)}, f32[2,40,128]{2,1,0:T(8,128)S(1)}, u32[]{:S(2)}, u32[]{:S(2)}) collective-permute-start(f32[2,40,128]{2,1,0:T(8,128)S(1)} %get-tuple-element.15.after_ref), channel_id=1, source_target_pairs={{0,7},{1,6},{2,5},{3,4},{4,3},{5,2},{6,1},{7,0},{8,15},{9,14},{10,... | collective-permute-start | bytes 122888 | tf_op jit(solution)/shard_map/ppermute | solution.py:345
  11.7 3.4 %collective-permute-start.2 = (f32[2,40,128]{2,1,0:T(8,128)S(1)}, f32[2,40,128]{2,1,0:T(8,128)S(1)}, u32[]{:S(2)}, u32[]{:S(2)}) collective-permute-start(f32[2,40,128]{2,1,0:T(8,128)S(1)} %get-tuple-element.16), channel_id=1, source_target_pairs={{0,3},{1,2},{2,1},{3,0},{4,7},{5,6},{6,5},{7,4},{8,11},{9,10},{10,... | collective-permute-start | bytes 122888 | tf_op jit(solution)/shard_map/ppermute | solution.py:345
  12.4 3.7 %collective-permute-start.3 = (f32[2,40,128]{2,1,0:T(8,128)S(1)}, f32[2,40,128]{2,1,0:T(8,128)S(1)}, u32[]{:S(2)}, u32[]{:S(2)}) collective-permute-start(f32[2,40,128]{2,1,0:T(8,128)S(1)} %get-tuple-element.17), channel_id=1, source_target_pairs={{0,5},{1,4},{2,7},{3,6},{4,1},{5,0},{6,3},{7,2},{8,13},{9,12},{10,... | collective-permute-start | bytes 122888 | tf_op jit(solution)/shard_map/ppermute | solution.py:345
  12.5 3.6 %collective-permute-start.4 = (f32[2,40,128]{2,1,0:T(8,128)S(1)}, f32[2,40,128]{2,1,0:T(8,128)S(1)}, u32[]{:S(2)}, u32[]{:S(2)}) collective-permute-start(f32[2,40,128]{2,1,0:T(8,128)S(1)} %get-tuple-element.18), channel_id=1, source_target_pairs={{0,1},{1,0},{2,3},{3,2},{4,5},{5,4},{6,7},{7,6},{8,9},{9,8},{10,11... | collective-permute-start | bytes 122888 | tf_op jit(solution)/shard_map/ppermute | solution.py:340
  13.2 17.2 %slice-start = ((s8[16777216]{0:T(1024)(128)(4,1)}), s8[4194304]{0:T(1024)(128)(4,1)S(1)}, s32[]{:S(2)}) async-start(s8[16777216]{0:T(1024)(128)(4,1)} %bitcast.2), calls=%async_computation | async-start | bytes 8388608
  13.2 17.2 %slice-start.1 = ((s8[16777216]{0:T(1024)(128)(4,1)}), s8[4194304]{0:T(1024)(128)(4,1)S(1)}, s32[]{:S(2)}) async-start(s8[16777216]{0:T(1024)(128)(4,1)} %bitcast.2), calls=%async_computation.1 | async-start | bytes 8388608
  16.1 4.2 %collective-permute-start.5 = (f32[1,40,128]{2,1,0:T(8,128)S(1)}, f32[1,40,128]{2,1,0:T(8,128)S(1)}, u32[]{:S(2)}, u32[]{:S(2)}) collective-permute-start(f32[1,40,128]{2,1,0:T(8,128)S(1)} %get-tuple-element.22), channel_id=1, source_target_pairs={{0,9},{1,8},{2,11},{3,10},{4,13},{5,12},{6,15},{7,14},{8,1},{9,0},... | collective-permute-start | bytes 61448 | tf_op jit(solution)/shard_map/ppermute | solution.py:345
  18.5 1.8 %collective-permute-start.6 = (f32[1,40,128]{2,1,0:T(8,128)S(1)}, f32[1,40,128]{2,1,0:T(8,128)S(1)}, u32[]{:S(2)}, u32[]{:S(2)}) collective-permute-start(f32[1,40,128]{2,1,0:T(8,128)S(1)} %get-tuple-element.25), channel_id=1, source_target_pairs={{0,1},{1,0},{2,3},{3,2},{4,5},{5,4},{6,7},{7,6},{8,9},{9,8},{10,11... | collective-permute-start | bytes 61448 | tf_op jit(solution)/shard_map/ppermute | solution.py:340
  20.3 10.1 %slice-start.2 = ((s8[16777216]{0:T(1024)(128)(4,1)}), s8[4194304]{0:T(1024)(128)(4,1)S(1)}, s32[]{:S(2)}) async-start(s8[16777216]{0:T(1024)(128)(4,1)} %bitcast.2), calls=%async_computation.2 | async-start | bytes 8388608
  20.3 10.1 %slice-start.3 = ((s8[16777216]{0:T(1024)(128)(4,1)}), s8[4194304]{0:T(1024)(128)(4,1)S(1)}, s32[]{:S(2)}) async-start(s8[16777216]{0:T(1024)(128)(4,1)} %bitcast.2), calls=%async_computation.3 | async-start | bytes 8388608
  21.2 4.0 %collective-permute-start.7 = (bf16[1,32,128]{2,1,0:T(8,128)(2,1)S(1)}, bf16[1,32,128]{2,1,0:T(8,128)(2,1)S(1)}, u32[]{:S(2)}, u32[]{:S(2)}) collective-permute-start(bf16[1,32,128]{2,1,0:T(8,128)(2,1)S(1)} %attend.1.refs_4_), channel_id=1, source_target_pairs={{0,9},{1,8},{2,11},{3,10},{4,13},{5,12},{6,15},{7,14},{8,1},{9,0},... | collective-permute-start | bytes 24584 | tf_op jit(solution)/shard_map/ppermute | solution.py:345
  23.5 1.7 %collective-permute-start.8 = (bf16[1,32,128]{2,1,0:T(8,128)(2,1)S(1)}, bf16[1,32,128]{2,1,0:T(8,128)(2,1)S(1)}, u32[]{:S(2)}, u32[]{:S(2)}) collective-permute-start(bf16[1,32,128]{2,1,0:T(8,128)(2,1)S(1)} %attend.1.refs_4_), channel_id=1, source_target_pairs={{0,1},{1,0},{2,3},{3,2},{4,5},{5,4},{6,7},{7,6},{8,9},{9,8},{10,11... | collective-permute-start | bytes 24584 | tf_op jit(solution)/shard_map/ppermute | solution.py:340
  25.2 4.5 %collective-permute-start.10 = (bf16[2,32,128]{2,1,0:T(8,128)(2,1)S(1)}, bf16[2,32,128]{2,1,0:T(8,128)(2,1)S(1)}, u32[]{:S(2)}, u32[]{:S(2)}) collective-permute-start(bf16[2,32,128]{2,1,0:T(8,128)(2,1)S(1)} %constant_dynamic-update-slice_fusion), channel_id=1, source_target_pairs={{0,7},{1,6},{2,5},{3,4},{4,3},{5,2},{6,1},{7,0},{8,15},{9,14},{10,... | collective-permute-start | bytes 49160 | tf_op jit(solution)/shard_map/ppermute | solution.py:345
  26.4 3.4 %collective-permute-start.11 = (bf16[2,32,128]{2,1,0:T(8,128)(2,1)S(1)}, bf16[2,32,128]{2,1,0:T(8,128)(2,1)S(1)}, u32[]{:S(2)}, u32[]{:S(2)}) collective-permute-start(bf16[2,32,128]{2,1,0:T(8,128)(2,1)S(1)} %constant_dynamic-update-slice_fusion), channel_id=1, source_target_pairs={{0,3},{1,2},{2,1},{3,0},{4,7},{5,6},{6,5},{7,4},{8,11},{9,10},{10,... | collective-permute-start | bytes 49160 | tf_op jit(solution)/shard_map/ppermute | solution.py:345
  27.2 3.2 %collective-permute-start.9 = (bf16[2,32,128]{2,1,0:T(8,128)(2,1)S(1)}, bf16[2,32,128]{2,1,0:T(8,128)(2,1)S(1)}, u32[]{:S(2)}, u32[]{:S(2)}) collective-permute-start(bf16[2,32,128]{2,1,0:T(8,128)(2,1)S(1)} %constant_dynamic-update-slice_fusion), channel_id=1, source_target_pairs={{0,5},{1,4},{2,7},{3,6},{4,1},{5,0},{6,3},{7,2},{8,13},{9,12},{10,... | collective-permute-start | bytes 49160 | tf_op jit(solution)/shard_map/ppermute | solution.py:345
  28.6 1.2 %collective-permute-start.12 = (bf16[1,32,128]{2,1,0:T(8,128)(2,1)S(1)}, bf16[1,32,128]{2,1,0:T(8,128)(2,1)S(1)}, u32[]{:S(2)}, u32[]{:S(2)}) collective-permute-start(bf16[1,32,128]{2,1,0:T(8,128)(2,1)S(1)} %collective-permute-done.7), channel_id=1, source_target_pairs={{0,1},{1,0},{2,3},{3,2},{4,5},{5,4},{6,7},{7,6},{8,9},{9,8},{10,11... | collective-permute-start | bytes 24584 | tf_op jit(solution)/shard_map/ppermute | solution.py:340
  32.8 1.3 %collective-permute-start.13 = (f32[4,2048]{1,0:T(4,128)S(1)}, f32[4,2048]{1,0:T(4,128)S(1)}, u32[]{:S(2)}, u32[]{:S(2)}) collective-permute-start(f32[4,2048]{1,0:T(4,128)S(1)} %get-tuple-element.24), channel_id=1, source_target_pairs={{0,1},{1,0},{2,3},{3,2},{4,5},{5,4},{6,7},{7,6},{8,9},{9,8},{10,11... | collective-permute-start | bytes 98312 | tf_op jit(solution)/shard_map/ppermute | solution.py:340

commit v19 on v18

--- a/solution.py
+++ b/solution.py
@@ -12,7 +12,7 @@
 LANES = 128
 HEAD_SIZE = 128
 CHUNK = 256
-FIRST = 256
+FIRST = 384
 PIECES = 4
 FAN = 4
 MIB = 2**20

time: 34.8 us -> 34.8 us (level)
  transfers between devices with their start and end apart: 14 -> 14, of which waited for: 8 -> 8; matrix products, arithmetic and copies ran while one was open for 0% -> 0% of each run, Pallas kernels for 5% -> 6%
where the time goes in v19:
time: 34.8 us; the launch traced here: 34.6 us
  starting transfers between devices  14 us (40%)
  Pallas kernels  10.7 us (31%)
  waiting for transfers between devices  8.34 us (24%)
  between operations  0.82 us (2%)
  other arithmetic  0.71 us (2%)
    ppermute x8, starting transfers between devices, cross(): return lax.ppermute(block, ('gx', 'gy'), pairs)  12.4 us
    ppermute x8, waiting for transfers between devices, cross(): return lax.ppermute(block, ('gx', 'gy'), pairs)  6.15 us
    pallas_call x1, Pallas kernels, project(): pl.pallas_call(functools.partial(project_kernel, bits), out_shape=(piece,...  5.53 us
    pallas_call x1, Pallas kernels, output(): pl.pallas_call(functools.partial(output_kernel, bits, places, turned), ou...  2.31 us
    ppermute x6, waiting for transfers between devices, swap(): return lax.ppermute(block, axis, [(i, i ^ mask) for i in range(devices)])  2.18 us
    pallas_call x1, Pallas kernels, stage_rows(): pl.pallas_call(functools.partial(stage_kernel, rows), out_shape=jax.Shape...  1.99 us
    ppermute x6, starting transfers between devices, swap(): return lax.ppermute(block, axis, [(i, i ^ mask) for i in range(devices)])  1.59 us
    pallas_call x1, Pallas kernels, attend(): pl.pallas_call(functools.partial(attend_kernel, query_heads, kv_heads, le...  0.82 us
  transfers between devices with their start and end apart: 14, of which 8 were waited for; matrix products, arithmetic and copies ran while one was open for 0% of the time, Pallas kernels for 6%

profile of v19, /device:TPU:0, one launch (start us, length us, event | category | flops | bytes accessed | tf_op | source)
XLA Modules:
  0.0 34.6 jit_solution(17371220142613338867)
XLA Ops:
  0.0 0.5 %collective-permute-start = (bf16[4,2048]{1,0:T(4,128)(2,1)}, bf16[4,2048]{1,0:T(4,128)(2,1)S(1)}, u32[]{:S(2)}, u32[]{:S(2)}) collective-permute-start(bf16[4,2048]{1,0:T(4,128)(2,1)} %rows_ref.1), channel_id=1, source_target_pairs={{0,1},{1,0},{2,3},{3,2},{4,5},{5,4},{6,7},{7,6},{8,9},{9,8},{10,11... | collective-permute-start | bytes 49160 | tf_op jit(solution)/shard_map/ppermute | solution.py:340
  0.5 2.0 %stage.1.first = bf16[384,4096]{1,0:T(8,128)(2,1)S(1)} custom-call(bf16[2048,4096]{1,0:T(8,128)(2,1)} %wq_hbm.1), custom_call_target="tpu_custom_call" | custom-call | bytes 3145728 | tf_op jit(solution)/shard_map/stage/pallas_call | solution.py:57
  2.6 5.5 %project.1 = (f32[2,40,128]{2,1,0:T(8,128)S(1)}, f32[2,40,128]{2,1,0:T(8,128)S(1)}, f32[2,40,128]{2,1,0:T(8,128)S(1)}, f32[2,40,128]{2,1,0:T(8,128)S(1)}) custom-call(bf16[4,2048]{1,0:T(4,128)(2,1)S(1)} %copy-done.4, bf16[4,2048]{1,0:T(4,128)(2,1)S(1)} %collective-permute-done.other_ref, bf16[2048,4096]{1,0:T(8,128)(2,1)} %wq_hbm.1, ...), custom_call_target="tpu_custom_call" | custom-call | flops 150994944 | bytes 18874368 | tf_op jit(solution)/shard_map/project/pallas_call | solution.py:179
  8.1 3.6 %collective-permute-start.1 = (f32[2,40,128]{2,1,0:T(8,128)S(1)}, f32[2,40,128]{2,1,0:T(8,128)S(1)}, u32[]{:S(2)}, u32[]{:S(2)}) collective-permute-start(f32[2,40,128]{2,1,0:T(8,128)S(1)} %get-tuple-element.15.after_ref), channel_id=1, source_target_pairs={{0,7},{1,6},{2,5},{3,4},{4,3},{5,2},{6,1},{7,0},{8,15},{9,14},{10,... | collective-permute-start | bytes 122888 | tf_op jit(solution)/shard_map/ppermute | solution.py:345
  11.7 0.7 %collective-permute-start.2 = (f32[2,40,128]{2,1,0:T(8,128)S(1)}, f32[2,40,128]{2,1,0:T(8,128)S(1)}, u32[]{:S(2)}, u32[]{:S(2)}) collective-permute-start(f32[2,40,128]{2,1,0:T(8,128)S(1)} %get-tuple-element.16), channel_id=1, source_target_pairs={{0,3},{1,2},{2,1},{3,0},{4,7},{5,6},{6,5},{7,4},{8,11},{9,10},{10,... | collective-permute-start | bytes 122888 | tf_op jit(solution)/shard_map/ppermute | solution.py:345
  13.3 0.4 %collective-permute-done.1 = f32[2,40,128]{2,1,0:T(8,128)S(1)} collective-permute-done((f32[2,40,128]{2,1,0:T(8,128)S(1)}, f32[2,40,128]{2,1,0:T(8,128)S(1)}, u32[]{:S(2)}, u32[]{:S(2)}) %collective-permute-start.1) | collective-permute-done | bytes 40992 | tf_op jit(solution)/shard_map/ppermute | solution.py:345
  13.7 1.5 %collective-permute-done.2 = f32[2,40,128]{2,1,0:T(8,128)S(1)} collective-permute-done((f32[2,40,128]{2,1,0:T(8,128)S(1)}, f32[2,40,128]{2,1,0:T(8,128)S(1)}, u32[]{:S(2)}, u32[]{:S(2)}) %collective-permute-start.2) | collective-permute-done | bytes 40992 | tf_op jit(solution)/shard_map/ppermute | solution.py:345
  15.1 0.9 %collective-permute-done.3 = f32[2,40,128]{2,1,0:T(8,128)S(1)} collective-permute-done((f32[2,40,128]{2,1,0:T(8,128)S(1)}, f32[2,40,128]{2,1,0:T(8,128)S(1)}, u32[]{:S(2)}, u32[]{:S(2)}) %collective-permute-start.3) | collective-permute-done | bytes 40992 | tf_op jit(solution)/shard_map/ppermute | solution.py:345
  16.1 2.4 %collective-permute-start.5 = (f32[1,40,128]{2,1,0:T(8,128)S(1)}, f32[1,40,128]{2,1,0:T(8,128)S(1)}, u32[]{:S(2)}, u32[]{:S(2)}) collective-permute-start(f32[1,40,128]{2,1,0:T(8,128)S(1)} %get-tuple-element.22), channel_id=1, source_target_pairs={{0,9},{1,8},{2,11},{3,10},{4,13},{5,12},{6,15},{7,14},{8,1},{9,0},... | collective-permute-start | bytes 61448 | tf_op jit(solution)/shard_map/ppermute | solution.py:345
  18.5 0.4 %collective-permute-start.6 = (f32[1,40,128]{2,1,0:T(8,128)S(1)}, f32[1,40,128]{2,1,0:T(8,128)S(1)}, u32[]{:S(2)}, u32[]{:S(2)}) collective-permute-start(f32[1,40,128]{2,1,0:T(8,128)S(1)} %get-tuple-element.25), channel_id=1, source_target_pairs={{0,1},{1,0},{2,3},{3,2},{4,5},{5,4},{6,7},{7,6},{8,9},{9,8},{10,11... | collective-permute-start | bytes 61448 | tf_op jit(solution)/shard_map/ppermute | solution.py:340
  18.9 1.4 %collective-permute-done.5.refs_0_ = f32[1,40,128]{2,1,0:T(8,128)S(1)} collective-permute-done((f32[1,40,128]{2,1,0:T(8,128)S(1)}, f32[1,40,128]{2,1,0:T(8,128)S(1)}, u32[]{:S(2)}, u32[]{:S(2)}) %collective-permute-start.5) | collective-permute-done | bytes 20512 | tf_op jit(solution)/shard_map/ppermute | solution.py:345
  20.3 0.8 %attend.1.refs_4_ = bf16[1,32,128]{2,1,0:T(8,128)(2,1)S(1)} custom-call(bf16[4096,2048]{1,0:T(8,128)(2,1)} %refs_5_.1, f32[8,128]{1,0:T(8,128)S(1)} %get-tuple-element.20.turn_ref, f32[1,2048]{1,0:T(1,128)S(1)} %get-tuple-element.21.live_ref, bf16[1,2,2048,128]{3,2,1,0:T(8,128)(2,1)S(1)} %copy-done, bf16[1,2,2048,128]{3,2,1,0:T(8,128)(2,1)S(1)} %copy-done.1, ...), custom_call_target="tpu_custom_call" | custom-call | flops 33554432 | bytes 2097152 | tf_op jit(solution)/shard_map/attend/pallas_call | solution.py:266
  21.1 2.4 %collective-permute-start.7 = (bf16[1,32,128]{2,1,0:T(8,128)(2,1)S(1)}, bf16[1,32,128]{2,1,0:T(8,128)(2,1)S(1)}, u32[]{:S(2)}, u32[]{:S(2)}) collective-permute-start(bf16[1,32,128]{2,1,0:T(8,128)(2,1)S(1)} %attend.1.refs_4_), channel_id=1, source_target_pairs={{0,9},{1,8},{2,11},{3,10},{4,13},{5,12},{6,15},{7,14},{8,1},{9,0},... | collective-permute-start | bytes 24584 | tf_op jit(solution)/shard_map/ppermute | solution.py:345
  23.5 0.4 %collective-permute-start.8 = (bf16[1,32,128]{2,1,0:T(8,128)(2,1)S(1)}, bf16[1,32,128]{2,1,0:T(8,128)(2,1)S(1)}, u32[]{:S(2)}, u32[]{:S(2)}) collective-permute-start(bf16[1,32,128]{2,1,0:T(8,128)(2,1)S(1)} %attend.1.refs_4_), channel_id=1, source_target_pairs={{0,1},{1,0},{2,3},{3,2},{4,5},{5,4},{6,7},{7,6},{8,9},{9,8},{10,11... | collective-permute-start | bytes 24584 | tf_op jit(solution)/shard_map/ppermute | solution.py:340
  23.9 1.3 %collective-permute-done.7 = bf16[1,32,128]{2,1,0:T(8,128)(2,1)S(1)} collective-permute-done((bf16[1,32,128]{2,1,0:T(8,128)(2,1)S(1)}, bf16[1,32,128]{2,1,0:T(8,128)(2,1)S(1)}, u32[]{:S(2)}, u32[]{:S(2)}) %collective-permute-start.7) | collective-permute-done | bytes 8224 | tf_op jit(solution)/shard_map/ppermute | solution.py:345
  25.2 1.2 %collective-permute-start.10 = (bf16[2,32,128]{2,1,0:T(8,128)(2,1)S(1)}, bf16[2,32,128]{2,1,0:T(8,128)(2,1)S(1)}, u32[]{:S(2)}, u32[]{:S(2)}) collective-permute-start(bf16[2,32,128]{2,1,0:T(8,128)(2,1)S(1)} %constant_dynamic-update-slice_fusion), channel_id=1, source_target_pairs={{0,7},{1,6},{2,5},{3,4},{4,3},{5,2},{6,1},{7,0},{8,15},{9,14},{10,... | collective-permute-start | bytes 49160 | tf_op jit(solution)/shard_map/ppermute | solution.py:345
  26.4 0.9 %collective-permute-start.11 = (bf16[2,32,128]{2,1,0:T(8,128)(2,1)S(1)}, bf16[2,32,128]{2,1,0:T(8,128)(2,1)S(1)}, u32[]{:S(2)}, u32[]{:S(2)}) collective-permute-start(bf16[2,32,128]{2,1,0:T(8,128)(2,1)S(1)} %constant_dynamic-update-slice_fusion), channel_id=1, source_target_pairs={{0,3},{1,2},{2,1},{3,0},{4,7},{5,6},{6,5},{7,4},{8,11},{9,10},{10,... | collective-permute-start | bytes 49160 | tf_op jit(solution)/shard_map/ppermute | solution.py:345
  27.2 1.3 %collective-permute-start.9 = (bf16[2,32,128]{2,1,0:T(8,128)(2,1)S(1)}, bf16[2,32,128]{2,1,0:T(8,128)(2,1)S(1)}, u32[]{:S(2)}, u32[]{:S(2)}) collective-permute-start(bf16[2,32,128]{2,1,0:T(8,128)(2,1)S(1)} %constant_dynamic-update-slice_fusion), channel_id=1, source_target_pairs={{0,5},{1,4},{2,7},{3,6},{4,1},{5,0},{6,3},{7,2},{8,13},{9,12},{10,... | collective-permute-start | bytes 49160 | tf_op jit(solution)/shard_map/ppermute | solution.py:345
  28.6 1.1 %collective-permute-done.12.refs_3_ = bf16[1,32,128]{2,1,0:T(8,128)(2,1)S(1)} collective-permute-done((bf16[1,32,128]{2,1,0:T(8,128)(2,1)S(1)}, bf16[1,32,128]{2,1,0:T(8,128)(2,1)S(1)}, u32[]{:S(2)}, u32[]{:S(2)}) %collective-permute-start.12) | collective-permute-done | bytes 8224 | tf_op jit(solution)/shard_map/ppermute | solution.py:340
  29.7 0.7 %collective-permute-done.9.refs_0_ = bf16[2,32,128]{2,1,0:T(8,128)(2,1)S(1)} collective-permute-done((bf16[2,32,128]{2,1,0:T(8,128)(2,1)S(1)}, bf16[2,32,128]{2,1,0:T(8,128)(2,1)S(1)}, u32[]{:S(2)}, u32[]{:S(2)}) %collective-permute-start.9) | collective-permute-done | bytes 16416 | tf_op jit(solution)/shard_map/ppermute | solution.py:345
  30.4 2.3 %output.1 = (f32[4,2048]{1,0:T(4,128)S(1)}, f32[4,2048]{1,0:T(4,128)S(1)}) custom-call(bf16[2,32,128]{2,1,0:T(8,128)(2,1)S(1)} %collective-permute-done.9.refs_0_, bf16[2,32,128]{2,1,0:T(8,128)(2,1)S(1)} %collective-permute-done.10.refs_1_, bf16[2,32,128]{2,1,0:T(8,128)(2,1)S(1)} %collective-permute-done.11.refs_2_, ...), custom_call_target="tpu_custom_call" | custom-call | flops 134217728 | bytes 16777216 | tf_op jit(solution)/shard_map/output/pallas_call | solution.py:321
  32.7 0.2 collective-permute-start.13
  33.0 1.0 %collective-permute-done.13 = f32[4,2048]{1,0:T(4,128)S(1)} collective-permute-done((f32[4,2048]{1,0:T(4,128)S(1)}, f32[4,2048]{1,0:T(4,128)S(1)}, u32[]{:S(2)}, u32[]{:S(2)}) %collective-permute-start.13) | collective-permute-done | bytes 32800 | tf_op jit(solution)/shard_map/ppermute | solution.py:340
  34.0 0.6 %add_convert_fusion = bf16[4,2048]{1,0:T(4,128)(2,1)} fusion(f32[4,2048]{1,0:T(4,128)S(1)} %get-tuple-element.23, f32[4,2048]{1,0:T(4,128)S(1)} %collective-permute-done.13), kind=kLoop, calls=%fused_computation | loop fusion | flops 16384 | bytes 81920 | tf_op jit(solution)/shard_map/convert_element_type | solution.py:408
  (34 shorter events, 0.4 us)
Async XLA Ops:
  0.0 2.6 %copy-start.4 = (bf16[4,2048]{1,0:T(4,128)(2,1)S(1)}, bf16[4,2048]{1,0:T(4,128)(2,1)}, u32[]{:S(2)}) copy-start(bf16[4,2048]{1,0:T(4,128)(2,1)} %rows_ref.1) | copy-start | bytes 49156
  0.0 2.6 %copy-start.2 = (bf16[2048,256]{1,0:T(8,128)(2,1)S(1)}, bf16[2048,256]{1,0:T(8,128)(2,1)}, u32[]{:S(2)}) copy-start(bf16[2048,256]{1,0:T(8,128)(2,1)} %wk.1) | copy-start | bytes 3145732
  0.0 2.6 %copy-start.3 = (bf16[2048,256]{1,0:T(8,128)(2,1)S(1)}, bf16[2048,256]{1,0:T(8,128)(2,1)}, u32[]{:S(2)}) copy-start(bf16[2048,256]{1,0:T(8,128)(2,1)} %wv.1) | copy-start | bytes 3145732
  0.0 2.6 %collective-permute-start = (bf16[4,2048]{1,0:T(4,128)(2,1)}, bf16[4,2048]{1,0:T(4,128)(2,1)S(1)}, u32[]{:S(2)}, u32[]{:S(2)}) collective-permute-start(bf16[4,2048]{1,0:T(4,128)(2,1)} %rows_ref.1), channel_id=1, source_target_pairs={{0,1},{1,0},{2,3},{3,2},{4,5},{5,4},{6,7},{7,6},{8,9},{9,8},{10,11... | collective-permute-start | bytes 49160 | tf_op jit(solution)/shard_map/ppermute | solution.py:340
  2.5 17.7 %copy-start = (bf16[1,2,2048,128]{3,2,1,0:T(8,128)(2,1)S(1)}, bf16[1,2,2048,128]{3,2,1,0:T(8,128)(2,1)}, u32[]{:S(2)}) copy-start(bf16[1,2,2048,128]{3,2,1,0:T(8,128)(2,1)} %k_ref.1) | copy-start | bytes 3145732
  2.5 17.7 %copy-start.1 = (bf16[1,2,2048,128]{3,2,1,0:T(8,128)(2,1)S(1)}, bf16[1,2,2048,128]{3,2,1,0:T(8,128)(2,1)}, u32[]{:S(2)}) copy-start(bf16[1,2,2048,128]{3,2,1,0:T(8,128)(2,1)} %v_ref.1) | copy-start | bytes 3145732
  8.1 5.5 %collective-permute-start.1 = (f32[2,40,128]{2,1,0:T(8,128)S(1)}, f32[2,40,128]{2,1,0:T(8,128)S(1)}, u32[]{:S(2)}, u32[]{:S(2)}) collective-permute-start(f32[2,40,128]{2,1,0:T(8,128)S(1)} %get-tuple-element.15.after_ref), channel_id=1, source_target_pairs={{0,7},{1,6},{2,5},{3,4},{4,3},{5,2},{6,1},{7,0},{8,15},{9,14},{10,... | collective-permute-start | bytes 122888 | tf_op jit(solution)/shard_map/ppermute | solution.py:345
  11.7 3.4 %collective-permute-start.2 = (f32[2,40,128]{2,1,0:T(8,128)S(1)}, f32[2,40,128]{2,1,0:T(8,128)S(1)}, u32[]{:S(2)}, u32[]{:S(2)}) collective-permute-start(f32[2,40,128]{2,1,0:T(8,128)S(1)} %get-tuple-element.16), channel_id=1, source_target_pairs={{0,3},{1,2},{2,1},{3,0},{4,7},{5,6},{6,5},{7,4},{8,11},{9,10},{10,... | collective-permute-start | bytes 122888 | tf_op jit(solution)/shard_map/ppermute | solution.py:345
  12.4 3.7 %collective-permute-start.3 = (f32[2,40,128]{2,1,0:T(8,128)S(1)}, f32[2,40,128]{2,1,0:T(8,128)S(1)}, u32[]{:S(2)}, u32[]{:S(2)}) collective-permute-start(f32[2,40,128]{2,1,0:T(8,128)S(1)} %get-tuple-element.17), channel_id=1, source_target_pairs={{0,5},{1,4},{2,7},{3,6},{4,1},{5,0},{6,3},{7,2},{8,13},{9,12},{10,... | collective-permute-start | bytes 122888 | tf_op jit(solution)/shard_map/ppermute | solution.py:345
  12.5 3.6 %collective-permute-start.4 = (f32[2,40,128]{2,1,0:T(8,128)S(1)}, f32[2,40,128]{2,1,0:T(8,128)S(1)}, u32[]{:S(2)}, u32[]{:S(2)}) collective-permute-start(f32[2,40,128]{2,1,0:T(8,128)S(1)} %get-tuple-element.18), channel_id=1, source_target_pairs={{0,1},{1,0},{2,3},{3,2},{4,5},{5,4},{6,7},{7,6},{8,9},{9,8},{10,11... | collective-permute-start | bytes 122888 | tf_op jit(solution)/shard_map/ppermute | solution.py:340
  13.2 17.2 %slice-start = ((s8[16777216]{0:T(1024)(128)(4,1)}), s8[4194304]{0:T(1024)(128)(4,1)S(1)}, s32[]{:S(2)}) async-start(s8[16777216]{0:T(1024)(128)(4,1)} %bitcast.2), calls=%async_computation | async-start | bytes 8388608
  13.2 17.2 %slice-start.1 = ((s8[16777216]{0:T(1024)(128)(4,1)}), s8[4194304]{0:T(1024)(128)(4,1)S(1)}, s32[]{:S(2)}) async-start(s8[16777216]{0:T(1024)(128)(4,1)} %bitcast.2), calls=%async_computation.1 | async-start | bytes 8388608
  16.1 4.2 %collective-permute-start.5 = (f32[1,40,128]{2,1,0:T(8,128)S(1)}, f32[1,40,128]{2,1,0:T(8,128)S(1)}, u32[]{:S(2)}, u32[]{:S(2)}) collective-permute-start(f32[1,40,128]{2,1,0:T(8,128)S(1)} %get-tuple-element.22), channel_id=1, source_target_pairs={{0,9},{1,8},{2,11},{3,10},{4,13},{5,12},{6,15},{7,14},{8,1},{9,0},... | collective-permute-start | bytes 61448 | tf_op jit(solution)/shard_map/ppermute | solution.py:345
  18.5 1.8 %collective-permute-start.6 = (f32[1,40,128]{2,1,0:T(8,128)S(1)}, f32[1,40,128]{2,1,0:T(8,128)S(1)}, u32[]{:S(2)}, u32[]{:S(2)}) collective-permute-start(f32[1,40,128]{2,1,0:T(8,128)S(1)} %get-tuple-element.25), channel_id=1, source_target_pairs={{0,1},{1,0},{2,3},{3,2},{4,5},{5,4},{6,7},{7,6},{8,9},{9,8},{10,11... | collective-permute-start | bytes 61448 | tf_op jit(solution)/shard_map/ppermute | solution.py:340
  20.3 10.1 %slice-start.2 = ((s8[16777216]{0:T(1024)(128)(4,1)}), s8[4194304]{0:T(1024)(128)(4,1)S(1)}, s32[]{:S(2)}) async-start(s8[16777216]{0:T(1024)(128)(4,1)} %bitcast.2), calls=%async_computation.2 | async-start | bytes 8388608
  20.3 10.1 %slice-start.3 = ((s8[16777216]{0:T(1024)(128)(4,1)}), s8[4194304]{0:T(1024)(128)(4,1)S(1)}, s32[]{:S(2)}) async-start(s8[16777216]{0:T(1024)(128)(4,1)} %bitcast.2), calls=%async_computation.3 | async-start | bytes 8388608
  21.1 4.0 %collective-permute-start.7 = (bf16[1,32,128]{2,1,0:T(8,128)(2,1)S(1)}, bf16[1,32,128]{2,1,0:T(8,128)(2,1)S(1)}, u32[]{:S(2)}, u32[]{:S(2)}) collective-permute-start(bf16[1,32,128]{2,1,0:T(8,128)(2,1)S(1)} %attend.1.refs_4_), channel_id=1, source_target_pairs={{0,9},{1,8},{2,11},{3,10},{4,13},{5,12},{6,15},{7,14},{8,1},{9,0},... | collective-permute-start | bytes 24584 | tf_op jit(solution)/shard_map/ppermute | solution.py:345
  23.5 1.7 %collective-permute-start.8 = (bf16[1,32,128]{2,1,0:T(8,128)(2,1)S(1)}, bf16[1,32,128]{2,1,0:T(8,128)(2,1)S(1)}, u32[]{:S(2)}, u32[]{:S(2)}) collective-permute-start(bf16[1,32,128]{2,1,0:T(8,128)(2,1)S(1)} %attend.1.refs_4_), channel_id=1, source_target_pairs={{0,1},{1,0},{2,3},{3,2},{4,5},{5,4},{6,7},{7,6},{8,9},{9,8},{10,11... | collective-permute-start | bytes 24584 | tf_op jit(solution)/shard_map/ppermute | solution.py:340
  25.2 4.5 %collective-permute-start.10 = (bf16[2,32,128]{2,1,0:T(8,128)(2,1)S(1)}, bf16[2,32,128]{2,1,0:T(8,128)(2,1)S(1)}, u32[]{:S(2)}, u32[]{:S(2)}) collective-permute-start(bf16[2,32,128]{2,1,0:T(8,128)(2,1)S(1)} %constant_dynamic-update-slice_fusion), channel_id=1, source_target_pairs={{0,7},{1,6},{2,5},{3,4},{4,3},{5,2},{6,1},{7,0},{8,15},{9,14},{10,... | collective-permute-start | bytes 49160 | tf_op jit(solution)/shard_map/ppermute | solution.py:345
  26.4 3.4 %collective-permute-start.11 = (bf16[2,32,128]{2,1,0:T(8,128)(2,1)S(1)}, bf16[2,32,128]{2,1,0:T(8,128)(2,1)S(1)}, u32[]{:S(2)}, u32[]{:S(2)}) collective-permute-start(bf16[2,32,128]{2,1,0:T(8,128)(2,1)S(1)} %constant_dynamic-update-slice_fusion), channel_id=1, source_target_pairs={{0,3},{1,2},{2,1},{3,0},{4,7},{5,6},{6,5},{7,4},{8,11},{9,10},{10,... | collective-permute-start | bytes 49160 | tf_op jit(solution)/shard_map/ppermute | solution.py:345
  27.2 3.2 %collective-permute-start.9 = (bf16[2,32,128]{2,1,0:T(8,128)(2,1)S(1)}, bf16[2,32,128]{2,1,0:T(8,128)(2,1)S(1)}, u32[]{:S(2)}, u32[]{:S(2)}) collective-permute-start(bf16[2,32,128]{2,1,0:T(8,128)(2,1)S(1)} %constant_dynamic-update-slice_fusion), channel_id=1, source_target_pairs={{0,5},{1,4},{2,7},{3,6},{4,1},{5,0},{6,3},{7,2},{8,13},{9,12},{10,... | collective-permute-start | bytes 49160 | tf_op jit(solution)/shard_map/ppermute | solution.py:345
  28.5 1.2 %collective-permute-start.12 = (bf16[1,32,128]{2,1,0:T(8,128)(2,1)S(1)}, bf16[1,32,128]{2,1,0:T(8,128)(2,1)S(1)}, u32[]{:S(2)}, u32[]{:S(2)}) collective-permute-start(bf16[1,32,128]{2,1,0:T(8,128)(2,1)S(1)} %collective-permute-done.7), channel_id=1, source_target_pairs={{0,1},{1,0},{2,3},{3,2},{4,5},{5,4},{6,7},{7,6},{8,9},{9,8},{10,11... | collective-permute-start | bytes 24584 | tf_op jit(solution)/shard_map/ppermute | solution.py:340
  32.7 1.3 %collective-permute-start.13 = (f32[4,2048]{1,0:T(4,128)S(1)}, f32[4,2048]{1,0:T(4,128)S(1)}, u32[]{:S(2)}, u32[]{:S(2)}) collective-permute-start(f32[4,2048]{1,0:T(4,128)S(1)} %get-tuple-element.24), channel_id=1, source_target_pairs={{0,1},{1,0},{2,3},{3,2},{4,5},{5,4},{6,7},{7,6},{8,9},{9,8},{10,11... | collective-permute-start | bytes 98312 | tf_op jit(solution)/shard_map/ppermute | solution.py:340

commit v20 on v19

--- a/solution.py
+++ b/solution.py
@@ -111,7 +111,7 @@
 def project_kernel(
     bits, rows_ref, other_ref, wq_hbm, first, wk, wv, *refs
 ):
-    pieces, (wq, rows, sems) = refs[:FAN], refs[FAN:]
+    pieces, (wq, rows, out, sems) = refs[:FAN], refs[FAN:]
     skip = first.shape[0]
     ranges = spread(wq_hbm.shape[0], skip, CHUNK)
     copies = [
@@ -136,15 +136,11 @@
     narrow = wide.astype(jnp.bfloat16)
 
     total = pieces[0].shape[1]
-    each = slots // FAN
-    flats = [ref.reshape(each * total, LANES) for ref in pieces]
+    flat = out.reshape(slots * total, LANES)
 
     def put(first_block, part):
         for i in range(0, part.shape[1], LANES):
-            for at, flat in enumerate(flats):
-                flat[pl.ds(first_block + i // LANES, each, stride=total), :] = part[
-                    at * each : (at + 1) * each, i : i + LANES
-                ]
+            flat[pl.ds(first_block + i // LANES, slots, stride=total), :] = part[:, i : i + LANES]
 
     at = wq.shape[1] // LANES
     for w in (wk, wv):
@@ -164,6 +160,8 @@
         )
 
     put(0, sums)
+    for at, ref in enumerate(pieces):
+        ref[...] = out[at]
 
 
 def project(rows, other, w_query, first, key_weight, value_weight, slots):
@@ -184,6 +182,7 @@
         scratch_shapes=[
             pltpu.VMEM((max(depth - skip, 16), query_width), jnp.bfloat16),
             pltpu.VMEM((slots, depth), jnp.float32),
+            pltpu.VMEM((FAN, slots // FAN, total, LANES), jnp.float32),
             pltpu.SemaphoreType.DMA((max(1, len(spread(depth, skip, CHUNK))), PIECES)),
         ],
         compiler_params=pltpu.CompilerParams(vmem_limit_bytes=46 * MIB),
@@ -281,23 +280,25 @@
 def output_kernel(bits, places, turned, *refs):
     pieces = len(places)
     parts = refs[:pieces]
-    w_ref, mine_ref, theirs_ref, flat, left, sums = refs[pieces:]
-    slots = left.shape[0]
+    w_ref, mine_ref, theirs_ref, flat, sums = refs[pieces:]
+    slots = sums.shape[0]
     heads = flat.shape[0] // slots
     for slot, ref in zip(places, parts):
         for i, row in enumerate(range(ref.shape[0])[::turned]):
             at = (slot + i) * heads
             flat[at : at + heads, :] = ref[row].astype(jnp.float32)
-    for head in range(heads):
-        left[:, head * HEAD_SIZE : (head + 1) * HEAD_SIZE] = flat[
-            pl.ds(head, slots, stride=heads), :
-        ].astype(jnp.bfloat16)
     total = None
     depth = w_ref.shape[0]
     chunk = min(2 * CHUNK, depth)
     for at in range(0, depth, chunk):
-        part = slice(at, at + chunk)
-        term = jnp.dot(left[:, part], w_ref[part, :], preferred_element_type=jnp.float32)
+        left = jnp.concatenate(
+            [
+                flat[pl.ds(head, slots, stride=heads), :]
+                for head in range(at // HEAD_SIZE, (at + chunk) // HEAD_SIZE)
+            ],
+            axis=1,
+        ).astype(jnp.bfloat16)
+        term = jnp.dot(left, w_ref[at : at + chunk, :], preferred_element_type=jnp.float32)
         total = term if total is None else total + term
     sums[...] = total
     half = slots // 2
@@ -325,7 +326,6 @@
         out_specs=(whole, whole),
         scratch_shapes=[
             pltpu.VMEM((slots * heads, HEAD_SIZE), jnp.float32),
-            pltpu.VMEM((slots, depth), jnp.bfloat16),
             pltpu.VMEM((slots, width), jnp.float32),
         ],
         compiler_params=pltpu.CompilerParams(vmem_limit_bytes=12 * MIB),

time: 34.8 us -> 34.8 us (level)
  no operation moved by 1% of the time
where the time goes in v20:
time: 34.8 us; the launch traced here: 34.6 us
  starting transfers between devices  14 us (40%)
  Pallas kernels  10.7 us (31%)
  waiting for transfers between devices  8.33 us (24%)
  between operations  0.82 us (2%)
  other arithmetic  0.71 us (2%)
    ppermute x8, starting transfers between devices, cross(): return lax.ppermute(block, ('gx', 'gy'), pairs)  12.4 us
    ppermute x8, waiting for transfers between devices, cross(): return lax.ppermute(block, ('gx', 'gy'), pairs)  6.16 us
    pallas_call x1, Pallas kernels, project(): pl.pallas_call(functools.partial(project_kernel, bits), out_shape=(piece,...  5.52 us
    pallas_call x1, Pallas kernels, output(): pl.pallas_call(functools.partial(output_kernel, bits, places, turned), ou...  2.3 us
    ppermute x6, waiting for transfers between devices, swap(): return lax.ppermute(block, axis, [(i, i ^ mask) for i in range(devices)])  2.17 us
    pallas_call x1, Pallas kernels, stage_rows(): pl.pallas_call(functools.partial(stage_kernel, rows), out_shape=jax.Shape...  1.99 us
    ppermute x6, starting transfers between devices, swap(): return lax.ppermute(block, axis, [(i, i ^ mask) for i in range(devices)])  1.6 us
    pallas_call x1, Pallas kernels, attend(): pl.pallas_call(functools.partial(attend_kernel, query_heads, kv_heads, le...  0.83 us
  transfers between devices with their start and end apart: 14, of which 8 were waited for; matrix products, arithmetic and copies ran while one was open for 0% of the time, Pallas kernels for 6%

profile of v20, /device:TPU:0, one launch (start us, length us, event | category | flops | bytes accessed | tf_op | source)
XLA Modules:
  0.0 34.6 jit_solution(18190608950179916753)
XLA Ops:
  0.0 0.5 %collective-permute-start = (bf16[4,2048]{1,0:T(4,128)(2,1)}, bf16[4,2048]{1,0:T(4,128)(2,1)S(1)}, u32[]{:S(2)}, u32[]{:S(2)}) collective-permute-start(bf16[4,2048]{1,0:T(4,128)(2,1)} %rows_ref.1), channel_id=1, source_target_pairs={{0,1},{1,0},{2,3},{3,2},{4,5},{5,4},{6,7},{7,6},{8,9},{9,8},{10,11... | collective-permute-start | bytes 49160 | tf_op jit(solution)/shard_map/ppermute | solution.py:340
  0.5 2.0 %stage.1.first = bf16[384,4096]{1,0:T(8,128)(2,1)S(1)} custom-call(bf16[2048,4096]{1,0:T(8,128)(2,1)} %wq_hbm.1), custom_call_target="tpu_custom_call" | custom-call | bytes 3145728 | tf_op jit(solution)/shard_map/stage/pallas_call | solution.py:57
  2.6 5.5 %project.1 = (f32[2,40,128]{2,1,0:T(8,128)S(1)}, f32[2,40,128]{2,1,0:T(8,128)S(1)}, f32[2,40,128]{2,1,0:T(8,128)S(1)}, f32[2,40,128]{2,1,0:T(8,128)S(1)}) custom-call(bf16[4,2048]{1,0:T(4,128)(2,1)S(1)} %copy-done.4, bf16[4,2048]{1,0:T(4,128)(2,1)S(1)} %collective-permute-done.other_ref, bf16[2048,4096]{1,0:T(8,128)(2,1)} %wq_hbm.1, ...), custom_call_target="tpu_custom_call" | custom-call | flops 150994944 | bytes 18874368 | tf_op jit(solution)/shard_map/project/pallas_call | solution.py:177
  8.1 3.6 %collective-permute-start.1 = (f32[2,40,128]{2,1,0:T(8,128)S(1)}, f32[2,40,128]{2,1,0:T(8,128)S(1)}, u32[]{:S(2)}, u32[]{:S(2)}) collective-permute-start(f32[2,40,128]{2,1,0:T(8,128)S(1)} %get-tuple-element.15.after_ref), channel_id=1, source_target_pairs={{0,7},{1,6},{2,5},{3,4},{4,3},{5,2},{6,1},{7,0},{8,15},{9,14},{10,... | collective-permute-start | bytes 122888 | tf_op jit(solution)/shard_map/ppermute | solution.py:345
  11.7 0.7 %collective-permute-start.2 = (f32[2,40,128]{2,1,0:T(8,128)S(1)}, f32[2,40,128]{2,1,0:T(8,128)S(1)}, u32[]{:S(2)}, u32[]{:S(2)}) collective-permute-start(f32[2,40,128]{2,1,0:T(8,128)S(1)} %get-tuple-element.16), channel_id=1, source_target_pairs={{0,3},{1,2},{2,1},{3,0},{4,7},{5,6},{6,5},{7,4},{8,11},{9,10},{10,... | collective-permute-start | bytes 122888 | tf_op jit(solution)/shard_map/ppermute | solution.py:345
  13.3 0.4 %collective-permute-done.1 = f32[2,40,128]{2,1,0:T(8,128)S(1)} collective-permute-done((f32[2,40,128]{2,1,0:T(8,128)S(1)}, f32[2,40,128]{2,1,0:T(8,128)S(1)}, u32[]{:S(2)}, u32[]{:S(2)}) %collective-permute-start.1) | collective-permute-done | bytes 40992 | tf_op jit(solution)/shard_map/ppermute | solution.py:345
  13.7 1.5 %collective-permute-done.2 = f32[2,40,128]{2,1,0:T(8,128)S(1)} collective-permute-done((f32[2,40,128]{2,1,0:T(8,128)S(1)}, f32[2,40,128]{2,1,0:T(8,128)S(1)}, u32[]{:S(2)}, u32[]{:S(2)}) %collective-permute-start.2) | collective-permute-done | bytes 40992 | tf_op jit(solution)/shard_map/ppermute | solution.py:345
  15.1 1.0 %collective-permute-done.3 = f32[2,40,128]{2,1,0:T(8,128)S(1)} collective-permute-done((f32[2,40,128]{2,1,0:T(8,128)S(1)}, f32[2,40,128]{2,1,0:T(8,128)S(1)}, u32[]{:S(2)}, u32[]{:S(2)}) %collective-permute-start.3) | collective-permute-done | bytes 40992 | tf_op jit(solution)/shard_map/ppermute | solution.py:345
  16.1 2.4 %collective-permute-start.5 = (f32[1,40,128]{2,1,0:T(8,128)S(1)}, f32[1,40,128]{2,1,0:T(8,128)S(1)}, u32[]{:S(2)}, u32[]{:S(2)}) collective-permute-start(f32[1,40,128]{2,1,0:T(8,128)S(1)} %get-tuple-element.22), channel_id=1, source_target_pairs={{0,9},{1,8},{2,11},{3,10},{4,13},{5,12},{6,15},{7,14},{8,1},{9,0},... | collective-permute-start | bytes 61448 | tf_op jit(solution)/shard_map/ppermute | solution.py:345
  18.5 0.4 %collective-permute-start.6 = (f32[1,40,128]{2,1,0:T(8,128)S(1)}, f32[1,40,128]{2,1,0:T(8,128)S(1)}, u32[]{:S(2)}, u32[]{:S(2)}) collective-permute-start(f32[1,40,128]{2,1,0:T(8,128)S(1)} %get-tuple-element.25), channel_id=1, source_target_pairs={{0,1},{1,0},{2,3},{3,2},{4,5},{5,4},{6,7},{7,6},{8,9},{9,8},{10,11... | collective-permute-start | bytes 61448 | tf_op jit(solution)/shard_map/ppermute | solution.py:340
  18.9 1.4 %collective-permute-done.5.refs_0_ = f32[1,40,128]{2,1,0:T(8,128)S(1)} collective-permute-done((f32[1,40,128]{2,1,0:T(8,128)S(1)}, f32[1,40,128]{2,1,0:T(8,128)S(1)}, u32[]{:S(2)}, u32[]{:S(2)}) %collective-permute-start.5) | collective-permute-done | bytes 20512 | tf_op jit(solution)/shard_map/ppermute | solution.py:345
  20.3 0.8 %attend.1.refs_4_ = bf16[1,32,128]{2,1,0:T(8,128)(2,1)S(1)} custom-call(bf16[4096,2048]{1,0:T(8,128)(2,1)} %refs_5_.1, f32[8,128]{1,0:T(8,128)S(1)} %get-tuple-element.20.turn_ref, f32[1,2048]{1,0:T(1,128)S(1)} %get-tuple-element.21.live_ref, bf16[1,2,2048,128]{3,2,1,0:T(8,128)(2,1)S(1)} %copy-done, bf16[1,2,2048,128]{3,2,1,0:T(8,128)(2,1)S(1)} %copy-done.1, ...), custom_call_target="tpu_custom_call" | custom-call | flops 33554432 | bytes 2097152 | tf_op jit(solution)/shard_map/attend/pallas_call | solution.py:265
  21.2 2.4 %collective-permute-start.7 = (bf16[1,32,128]{2,1,0:T(8,128)(2,1)S(1)}, bf16[1,32,128]{2,1,0:T(8,128)(2,1)S(1)}, u32[]{:S(2)}, u32[]{:S(2)}) collective-permute-start(bf16[1,32,128]{2,1,0:T(8,128)(2,1)S(1)} %attend.1.refs_4_), channel_id=1, source_target_pairs={{0,9},{1,8},{2,11},{3,10},{4,13},{5,12},{6,15},{7,14},{8,1},{9,0},... | collective-permute-start | bytes 24584 | tf_op jit(solution)/shard_map/ppermute | solution.py:345
  23.5 0.4 %collective-permute-start.8 = (bf16[1,32,128]{2,1,0:T(8,128)(2,1)S(1)}, bf16[1,32,128]{2,1,0:T(8,128)(2,1)S(1)}, u32[]{:S(2)}, u32[]{:S(2)}) collective-permute-start(bf16[1,32,128]{2,1,0:T(8,128)(2,1)S(1)} %attend.1.refs_4_), channel_id=1, source_target_pairs={{0,1},{1,0},{2,3},{3,2},{4,5},{5,4},{6,7},{7,6},{8,9},{9,8},{10,11... | collective-permute-start | bytes 24584 | tf_op jit(solution)/shard_map/ppermute | solution.py:340
  23.9 1.3 %collective-permute-done.7 = bf16[1,32,128]{2,1,0:T(8,128)(2,1)S(1)} collective-permute-done((bf16[1,32,128]{2,1,0:T(8,128)(2,1)S(1)}, bf16[1,32,128]{2,1,0:T(8,128)(2,1)S(1)}, u32[]{:S(2)}, u32[]{:S(2)}) %collective-permute-start.7) | collective-permute-done | bytes 8224 | tf_op jit(solution)/shard_map/ppermute | solution.py:345
  25.2 1.2 %collective-permute-start.10 = (bf16[2,32,128]{2,1,0:T(8,128)(2,1)S(1)}, bf16[2,32,128]{2,1,0:T(8,128)(2,1)S(1)}, u32[]{:S(2)}, u32[]{:S(2)}) collective-permute-start(bf16[2,32,128]{2,1,0:T(8,128)(2,1)S(1)} %constant_dynamic-update-slice_fusion), channel_id=1, source_target_pairs={{0,7},{1,6},{2,5},{3,4},{4,3},{5,2},{6,1},{7,0},{8,15},{9,14},{10,... | collective-permute-start | bytes 49160 | tf_op jit(solution)/shard_map/ppermute | solution.py:345
  26.4 0.8 %collective-permute-start.11 = (bf16[2,32,128]{2,1,0:T(8,128)(2,1)S(1)}, bf16[2,32,128]{2,1,0:T(8,128)(2,1)S(1)}, u32[]{:S(2)}, u32[]{:S(2)}) collective-permute-start(bf16[2,32,128]{2,1,0:T(8,128)(2,1)S(1)} %constant_dynamic-update-slice_fusion), channel_id=1, source_target_pairs={{0,3},{1,2},{2,1},{3,0},{4,7},{5,6},{6,5},{7,4},{8,11},{9,10},{10,... | collective-permute-start | bytes 49160 | tf_op jit(solution)/shard_map/ppermute | solution.py:345
  27.2 1.3 %collective-permute-start.9 = (bf16[2,32,128]{2,1,0:T(8,128)(2,1)S(1)}, bf16[2,32,128]{2,1,0:T(8,128)(2,1)S(1)}, u32[]{:S(2)}, u32[]{:S(2)}) collective-permute-start(bf16[2,32,128]{2,1,0:T(8,128)(2,1)S(1)} %constant_dynamic-update-slice_fusion), channel_id=1, source_target_pairs={{0,5},{1,4},{2,7},{3,6},{4,1},{5,0},{6,3},{7,2},{8,13},{9,12},{10,... | collective-permute-start | bytes 49160 | tf_op jit(solution)/shard_map/ppermute | solution.py:345
  28.6 1.1 %collective-permute-done.12.refs_3_ = bf16[1,32,128]{2,1,0:T(8,128)(2,1)S(1)} collective-permute-done((bf16[1,32,128]{2,1,0:T(8,128)(2,1)S(1)}, bf16[1,32,128]{2,1,0:T(8,128)(2,1)S(1)}, u32[]{:S(2)}, u32[]{:S(2)}) %collective-permute-start.12) | collective-permute-done | bytes 8224 | tf_op jit(solution)/shard_map/ppermute | solution.py:340
  29.8 0.7 %collective-permute-done.9.refs_0_ = bf16[2,32,128]{2,1,0:T(8,128)(2,1)S(1)} collective-permute-done((bf16[2,32,128]{2,1,0:T(8,128)(2,1)S(1)}, bf16[2,32,128]{2,1,0:T(8,128)(2,1)S(1)}, u32[]{:S(2)}, u32[]{:S(2)}) %collective-permute-start.9) | collective-permute-done | bytes 16416 | tf_op jit(solution)/shard_map/ppermute | solution.py:345
  30.4 2.3 %output.1 = (f32[4,2048]{1,0:T(4,128)S(1)}, f32[4,2048]{1,0:T(4,128)S(1)}) custom-call(bf16[2,32,128]{2,1,0:T(8,128)(2,1)S(1)} %collective-permute-done.9.refs_0_, bf16[2,32,128]{2,1,0:T(8,128)(2,1)S(1)} %collective-permute-done.10.refs_1_, bf16[2,32,128]{2,1,0:T(8,128)(2,1)S(1)} %collective-permute-done.11.refs_2_, ...), custom_call_target="tpu_custom_call" | custom-call | flops 134217728 | bytes 16777216 | tf_op jit(solution)/shard_map/output/pallas_call | solution.py:322
  32.7 0.2 collective-permute-start.13
  33.0 1.0 %collective-permute-done.13 = f32[4,2048]{1,0:T(4,128)S(1)} collective-permute-done((f32[4,2048]{1,0:T(4,128)S(1)}, f32[4,2048]{1,0:T(4,128)S(1)}, u32[]{:S(2)}, u32[]{:S(2)}) %collective-permute-start.13) | collective-permute-done | bytes 32800 | tf_op jit(solution)/shard_map/ppermute | solution.py:340
  34.0 0.6 %add_convert_fusion = bf16[4,2048]{1,0:T(4,128)(2,1)} fusion(f32[4,2048]{1,0:T(4,128)S(1)} %get-tuple-element.23, f32[4,2048]{1,0:T(4,128)S(1)} %collective-permute-done.13), kind=kLoop, calls=%fused_computation | loop fusion | flops 16384 | bytes 81920 | tf_op jit(solution)/shard_map/convert_element_type | solution.py:408
  (34 shorter events, 0.4 us)
Async XLA Ops:
  0.0 2.6 %copy-start.4 = (bf16[4,2048]{1,0:T(4,128)(2,1)S(1)}, bf16[4,2048]{1,0:T(4,128)(2,1)}, u32[]{:S(2)}) copy-start(bf16[4,2048]{1,0:T(4,128)(2,1)} %rows_ref.1) | copy-start | bytes 49156
  0.0 2.6 %copy-start.2 = (bf16[2048,256]{1,0:T(8,128)(2,1)S(1)}, bf16[2048,256]{1,0:T(8,128)(2,1)}, u32[]{:S(2)}) copy-start(bf16[2048,256]{1,0:T(8,128)(2,1)} %wk.1) | copy-start | bytes 3145732
  0.0 2.6 %copy-start.3 = (bf16[2048,256]{1,0:T(8,128)(2,1)S(1)}, bf16[2048,256]{1,0:T(8,128)(2,1)}, u32[]{:S(2)}) copy-start(bf16[2048,256]{1,0:T(8,128)(2,1)} %wv.1) | copy-start | bytes 3145732
  0.0 2.6 %collective-permute-start = (bf16[4,2048]{1,0:T(4,128)(2,1)}, bf16[4,2048]{1,0:T(4,128)(2,1)S(1)}, u32[]{:S(2)}, u32[]{:S(2)}) collective-permute-start(bf16[4,2048]{1,0:T(4,128)(2,1)} %rows_ref.1), channel_id=1, source_target_pairs={{0,1},{1,0},{2,3},{3,2},{4,5},{5,4},{6,7},{7,6},{8,9},{9,8},{10,11... | collective-permute-start | bytes 49160 | tf_op jit(solution)/shard_map/ppermute | solution.py:340
  2.5 17.8 %copy-start = (bf16[1,2,2048,128]{3,2,1,0:T(8,128)(2,1)S(1)}, bf16[1,2,2048,128]{3,2,1,0:T(8,128)(2,1)}, u32[]{:S(2)}) copy-start(bf16[1,2,2048,128]{3,2,1,0:T(8,128)(2,1)} %k_ref.1) | copy-start | bytes 3145732
  2.5 17.8 %copy-start.1 = (bf16[1,2,2048,128]{3,2,1,0:T(8,128)(2,1)S(1)}, bf16[1,2,2048,128]{3,2,1,0:T(8,128)(2,1)}, u32[]{:S(2)}) copy-start(bf16[1,2,2048,128]{3,2,1,0:T(8,128)(2,1)} %v_ref.1) | copy-start | bytes 3145732
  8.1 5.5 %collective-permute-start.1 = (f32[2,40,128]{2,1,0:T(8,128)S(1)}, f32[2,40,128]{2,1,0:T(8,128)S(1)}, u32[]{:S(2)}, u32[]{:S(2)}) collective-permute-start(f32[2,40,128]{2,1,0:T(8,128)S(1)} %get-tuple-element.15.after_ref), channel_id=1, source_target_pairs={{0,7},{1,6},{2,5},{3,4},{4,3},{5,2},{6,1},{7,0},{8,15},{9,14},{10,... | collective-permute-start | bytes 122888 | tf_op jit(solution)/shard_map/ppermute | solution.py:345
  11.7 3.4 %collective-permute-start.2 = (f32[2,40,128]{2,1,0:T(8,128)S(1)}, f32[2,40,128]{2,1,0:T(8,128)S(1)}, u32[]{:S(2)}, u32[]{:S(2)}) collective-permute-start(f32[2,40,128]{2,1,0:T(8,128)S(1)} %get-tuple-element.16), channel_id=1, source_target_pairs={{0,3},{1,2},{2,1},{3,0},{4,7},{5,6},{6,5},{7,4},{8,11},{9,10},{10,... | collective-permute-start | bytes 122888 | tf_op jit(solution)/shard_map/ppermute | solution.py:345
  12.4 3.7 %collective-permute-start.3 = (f32[2,40,128]{2,1,0:T(8,128)S(1)}, f32[2,40,128]{2,1,0:T(8,128)S(1)}, u32[]{:S(2)}, u32[]{:S(2)}) collective-permute-start(f32[2,40,128]{2,1,0:T(8,128)S(1)} %get-tuple-element.17), channel_id=1, source_target_pairs={{0,5},{1,4},{2,7},{3,6},{4,1},{5,0},{6,3},{7,2},{8,13},{9,12},{10,... | collective-permute-start | bytes 122888 | tf_op jit(solution)/shard_map/ppermute | solution.py:345
  12.5 3.6 %collective-permute-start.4 = (f32[2,40,128]{2,1,0:T(8,128)S(1)}, f32[2,40,128]{2,1,0:T(8,128)S(1)}, u32[]{:S(2)}, u32[]{:S(2)}) collective-permute-start(f32[2,40,128]{2,1,0:T(8,128)S(1)} %get-tuple-element.18), channel_id=1, source_target_pairs={{0,1},{1,0},{2,3},{3,2},{4,5},{5,4},{6,7},{7,6},{8,9},{9,8},{10,11... | collective-permute-start | bytes 122888 | tf_op jit(solution)/shard_map/ppermute | solution.py:340
  13.2 17.2 %slice-start = ((s8[16777216]{0:T(1024)(128)(4,1)}), s8[4194304]{0:T(1024)(128)(4,1)S(1)}, s32[]{:S(2)}) async-start(s8[16777216]{0:T(1024)(128)(4,1)} %bitcast.2), calls=%async_computation | async-start | bytes 8388608
  13.2 17.2 %slice-start.1 = ((s8[16777216]{0:T(1024)(128)(4,1)}), s8[4194304]{0:T(1024)(128)(4,1)S(1)}, s32[]{:S(2)}) async-start(s8[16777216]{0:T(1024)(128)(4,1)} %bitcast.2), calls=%async_computation.1 | async-start | bytes 8388608
  16.1 4.2 %collective-permute-start.5 = (f32[1,40,128]{2,1,0:T(8,128)S(1)}, f32[1,40,128]{2,1,0:T(8,128)S(1)}, u32[]{:S(2)}, u32[]{:S(2)}) collective-permute-start(f32[1,40,128]{2,1,0:T(8,128)S(1)} %get-tuple-element.22), channel_id=1, source_target_pairs={{0,9},{1,8},{2,11},{3,10},{4,13},{5,12},{6,15},{7,14},{8,1},{9,0},... | collective-permute-start | bytes 61448 | tf_op jit(solution)/shard_map/ppermute | solution.py:345
  18.5 1.8 %collective-permute-start.6 = (f32[1,40,128]{2,1,0:T(8,128)S(1)}, f32[1,40,128]{2,1,0:T(8,128)S(1)}, u32[]{:S(2)}, u32[]{:S(2)}) collective-permute-start(f32[1,40,128]{2,1,0:T(8,128)S(1)} %get-tuple-element.25), channel_id=1, source_target_pairs={{0,1},{1,0},{2,3},{3,2},{4,5},{5,4},{6,7},{7,6},{8,9},{9,8},{10,11... | collective-permute-start | bytes 61448 | tf_op jit(solution)/shard_map/ppermute | solution.py:340
  20.3 10.1 %slice-start.2 = ((s8[16777216]{0:T(1024)(128)(4,1)}), s8[4194304]{0:T(1024)(128)(4,1)S(1)}, s32[]{:S(2)}) async-start(s8[16777216]{0:T(1024)(128)(4,1)} %bitcast.2), calls=%async_computation.2 | async-start | bytes 8388608
  20.3 10.1 %slice-start.3 = ((s8[16777216]{0:T(1024)(128)(4,1)}), s8[4194304]{0:T(1024)(128)(4,1)S(1)}, s32[]{:S(2)}) async-start(s8[16777216]{0:T(1024)(128)(4,1)} %bitcast.2), calls=%async_computation.3 | async-start | bytes 8388608
  21.2 4.0 %collective-permute-start.7 = (bf16[1,32,128]{2,1,0:T(8,128)(2,1)S(1)}, bf16[1,32,128]{2,1,0:T(8,128)(2,1)S(1)}, u32[]{:S(2)}, u32[]{:S(2)}) collective-permute-start(bf16[1,32,128]{2,1,0:T(8,128)(2,1)S(1)} %attend.1.refs_4_), channel_id=1, source_target_pairs={{0,9},{1,8},{2,11},{3,10},{4,13},{5,12},{6,15},{7,14},{8,1},{9,0},... | collective-permute-start | bytes 24584 | tf_op jit(solution)/shard_map/ppermute | solution.py:345
  23.5 1.7 %collective-permute-start.8 = (bf16[1,32,128]{2,1,0:T(8,128)(2,1)S(1)}, bf16[1,32,128]{2,1,0:T(8,128)(2,1)S(1)}, u32[]{:S(2)}, u32[]{:S(2)}) collective-permute-start(bf16[1,32,128]{2,1,0:T(8,128)(2,1)S(1)} %attend.1.refs_4_), channel_id=1, source_target_pairs={{0,1},{1,0},{2,3},{3,2},{4,5},{5,4},{6,7},{7,6},{8,9},{9,8},{10,11... | collective-permute-start | bytes 24584 | tf_op jit(solution)/shard_map/ppermute | solution.py:340
  25.2 4.5 %collective-permute-start.10 = (bf16[2,32,128]{2,1,0:T(8,128)(2,1)S(1)}, bf16[2,32,128]{2,1,0:T(8,128)(2,1)S(1)}, u32[]{:S(2)}, u32[]{:S(2)}) collective-permute-start(bf16[2,32,128]{2,1,0:T(8,128)(2,1)S(1)} %constant_dynamic-update-slice_fusion), channel_id=1, source_target_pairs={{0,7},{1,6},{2,5},{3,4},{4,3},{5,2},{6,1},{7,0},{8,15},{9,14},{10,... | collective-permute-start | bytes 49160 | tf_op jit(solution)/shard_map/ppermute | solution.py:345
  26.4 3.4 %collective-permute-start.11 = (bf16[2,32,128]{2,1,0:T(8,128)(2,1)S(1)}, bf16[2,32,128]{2,1,0:T(8,128)(2,1)S(1)}, u32[]{:S(2)}, u32[]{:S(2)}) collective-permute-start(bf16[2,32,128]{2,1,0:T(8,128)(2,1)S(1)} %constant_dynamic-update-slice_fusion), channel_id=1, source_target_pairs={{0,3},{1,2},{2,1},{3,0},{4,7},{5,6},{6,5},{7,4},{8,11},{9,10},{10,... | collective-permute-start | bytes 49160 | tf_op jit(solution)/shard_map/ppermute | solution.py:345
  27.2 3.2 %collective-permute-start.9 = (bf16[2,32,128]{2,1,0:T(8,128)(2,1)S(1)}, bf16[2,32,128]{2,1,0:T(8,128)(2,1)S(1)}, u32[]{:S(2)}, u32[]{:S(2)}) collective-permute-start(bf16[2,32,128]{2,1,0:T(8,128)(2,1)S(1)} %constant_dynamic-update-slice_fusion), channel_id=1, source_target_pairs={{0,5},{1,4},{2,7},{3,6},{4,1},{5,0},{6,3},{7,2},{8,13},{9,12},{10,... | collective-permute-start | bytes 49160 | tf_op jit(solution)/shard_map/ppermute | solution.py:345
  28.6 1.2 %collective-permute-start.12 = (bf16[1,32,128]{2,1,0:T(8,128)(2,1)S(1)}, bf16[1,32,128]{2,1,0:T(8,128)(2,1)S(1)}, u32[]{:S(2)}, u32[]{:S(2)}) collective-permute-start(bf16[1,32,128]{2,1,0:T(8,128)(2,1)S(1)} %collective-permute-done.7), channel_id=1, source_target_pairs={{0,1},{1,0},{2,3},{3,2},{4,5},{5,4},{6,7},{7,6},{8,9},{9,8},{10,11... | collective-permute-start | bytes 24584 | tf_op jit(solution)/shard_map/ppermute | solution.py:340
  32.7 1.3 %collective-permute-start.13 = (f32[4,2048]{1,0:T(4,128)S(1)}, f32[4,2048]{1,0:T(4,128)S(1)}, u32[]{:S(2)}, u32[]{:S(2)}) collective-permute-start(f32[4,2048]{1,0:T(4,128)S(1)} %get-tuple-element.24), channel_id=1, source_target_pairs={{0,1},{1,0},{2,3},{3,2},{4,5},{5,4},{6,7},{7,6},{8,9},{9,8},{10,11... | collective-permute-start | bytes 98312 | tf_op jit(solution)/shard_map/ppermute | solution.py:340

commit v21 on v19

--- a/solution.py
+++ b/solution.py
@@ -66,6 +66,34 @@
         ),
         name="stage",
     )(in_hbm(array))
+
+
+def caches_kernel(k_hbm, v_hbm, after_ref, k_ref, v_ref, sems):
+    copies = [
+        pltpu.make_async_copy(src, dst, sems.at[i])
+        for i, (src, dst) in enumerate(((k_hbm, k_ref), (v_hbm, v_ref)))
+    ]
+    for copy in copies:
+        copy.start()
+    for copy in copies:
+        copy.wait()
+
+
+def stage_caches(k_cache, value_cache, after):
+    vmem = pl.BlockSpec(memory_space=pltpu.VMEM)
+    hbm = pl.BlockSpec(memory_space=pltpu.HBM)
+    return pl.pallas_call(
+        caches_kernel,
+        out_shape=tuple(jax.ShapeDtypeStruct(a.shape, a.dtype) for a in (k_cache, value_cache)),
+        in_specs=[hbm, hbm, vmem],
+        out_specs=(vmem, vmem),
+        scratch_shapes=[pltpu.SemaphoreType.DMA((2,))],
+        compiler_params=pltpu.CompilerParams(vmem_limit_bytes=4 * MIB),
+        cost_estimate=pl.CostEstimate(
+            flops=0, bytes_accessed=4 * k_cache.size, transcendentals=0
+        ),
+        name="caches",
+    )(in_hbm(k_cache), in_hbm(value_cache), after)
 
 
 def turning_kernel(length_ref, frequency_ref, beside_ref, after_ref, turn_ref, mask_ref):
@@ -94,7 +122,7 @@
             vmem,
         ],
         out_specs=(vmem, vmem),
-        compiler_params=pltpu.CompilerParams(vmem_limit_bytes=2 * MIB),
+        compiler_params=pltpu.CompilerParams(vmem_limit_bytes=4 * MIB),
         cost_estimate=pl.CostEstimate(flops=0, bytes_accessed=2 * beside.size, transcendentals=256),
         name="turning",
     )(lengths, frequency, in_hbm(beside), after)
@@ -370,7 +398,8 @@
         far = FAN
         arrived = fan(pieces, lambda block, mask: cross(block, devices, mask))
         beside = swap(pieces[0], "gy", 2, 1)
-        turn, live = turning(lengths, frequency, w_out, pieces[3], k_cache.shape[2])
+        k_cache, value_cache = stage_caches(k_cache, value_cache, pieces[3])
+        turn, live = turning(lengths, frequency, w_out, k_cache, k_cache.shape[2])
         leaving = [x[1:] for x in (*arrived, beside)]
         staying = [x[:1] for x in (*arrived, beside)]
         total = leaving[2] + (leaving[1] + (leaving[0] + leaving[3]))
@@ -387,7 +416,8 @@
         order, turned = (2, 4, 3, 1, 0), -1
     else:
         arrived = fan(pieces, lambda block, mask: swap(block, "gx", devices, mask))
-        turn, live = turning(lengths, frequency, w_out, pieces[3], k_cache.shape[2])
+        k_cache, value_cache = stage_caches(k_cache, value_cache, pieces[3])
+        turn, live = turning(lengths, frequency, w_out, k_cache, k_cache.shape[2])
         total = pieces[0] + (arrived[2] + (arrived[1] + arrived[0]))
         mask = FAN
         while total.shape[0] > 2:

time: 34.8 us -> 34.8 us (level)
  Pallas kernels: 10.7 us -> 12.2 us
  waiting for transfers between devices: 8.34 us -> 6.91 us
    pallas_call x0 -> x1, Pallas kernels: none -> 1.56 us  [stage_caches(): pl.pallas_call(caches_kernel, out_shape=tuple((jax.ShapeDtypeStruct(a.sha...]
    ppermute x8, waiting for transfers between devices: 6.15 us -> 4.65 us  [cross(): return lax.ppermute(block, ('gx', 'gy'), pairs)]
  transfers between devices with their start and end apart: 14 -> 14, of which waited for: 8 -> 8; matrix products, arithmetic and copies ran while one was open for 0% -> 0% of each run, Pallas kernels for 6% -> 10%
where the time goes in v21:
time: 34.8 us; the launch traced here: 34.7 us
  starting transfers between devices  14 us (40%)
  Pallas kernels  12.2 us (35%)
  waiting for transfers between devices  6.91 us (20%)
  between operations  0.8 us (2%)
  other arithmetic  0.71 us (2%)
    ppermute x8, starting transfers between devices, cross(): return lax.ppermute(block, ('gx', 'gy'), pairs)  12.5 us
    pallas_call x1, Pallas kernels, project(): pl.pallas_call(functools.partial(project_kernel, bits), out_shape=(piece,...  5.43 us
    ppermute x8, waiting for transfers between devices, cross(): return lax.ppermute(block, ('gx', 'gy'), pairs)  4.65 us
    pallas_call x1, Pallas kernels, output(): pl.pallas_call(functools.partial(output_kernel, bits, places, turned), ou...  2.31 us
    ppermute x6, waiting for transfers between devices, swap(): return lax.ppermute(block, axis, [(i, i ^ mask) for i in range(devices)])  2.26 us
    pallas_call x1, Pallas kernels, stage_rows(): pl.pallas_call(functools.partial(stage_kernel, rows), out_shape=jax.Shape...  1.99 us
    pallas_call x1, Pallas kernels, stage_caches(): pl.pallas_call(caches_kernel, out_shape=tuple((jax.ShapeDtypeStruct(a.sha...  1.56 us
    ppermute x6, starting transfers between devices, swap(): return lax.ppermute(block, axis, [(i, i ^ mask) for i in range(devices)])  1.53 us
  transfers between devices with their start and end apart: 14, of which 8 were waited for; matrix products, arithmetic and copies ran while one was open for 0% of the time, Pallas kernels for 10%

profile of v21, /device:TPU:0, one launch (start us, length us, event | category | flops | bytes accessed | tf_op | source)
XLA Modules:
  0.0 34.7 jit_solution(11462559259680289572)
XLA Ops:
  0.0 0.5 %collective-permute-start = (bf16[4,2048]{1,0:T(4,128)(2,1)}, bf16[4,2048]{1,0:T(4,128)(2,1)S(1)}, u32[]{:S(2)}, u32[]{:S(2)}) collective-permute-start(bf16[4,2048]{1,0:T(4,128)(2,1)} %rows_ref.1), channel_id=1, source_target_pairs={{0,1},{1,0},{2,3},{3,2},{4,5},{5,4},{6,7},{7,6},{8,9},{9,8},{10,11... | collective-permute-start | bytes 49160 | tf_op jit(solution)/shard_map/ppermute | solution.py:368
  0.5 2.0 %stage.1.first = bf16[384,4096]{1,0:T(8,128)(2,1)S(1)} custom-call(bf16[2048,4096]{1,0:T(8,128)(2,1)} %wq_hbm.1), custom_call_target="tpu_custom_call" | custom-call | bytes 3145728 | tf_op jit(solution)/shard_map/stage/pallas_call | solution.py:57
  2.6 5.4 %project.1 = (f32[2,40,128]{2,1,0:T(8,128)S(1)}, f32[2,40,128]{2,1,0:T(8,128)S(1)}, f32[2,40,128]{2,1,0:T(8,128)S(1)}, f32[2,40,128]{2,1,0:T(8,128)S(1)}) custom-call(bf16[4,2048]{1,0:T(4,128)(2,1)S(1)} %copy-done.2, bf16[4,2048]{1,0:T(4,128)(2,1)S(1)} %collective-permute-done.other_ref, bf16[2048,4096]{1,0:T(8,128)(2,1)} %wq_hbm.1, ...), custom_call_target="tpu_custom_call" | custom-call | flops 150994944 | bytes 18874368 | tf_op jit(solution)/shard_map/project/pallas_call | solution.py:207
  8.0 3.6 %collective-permute-start.1 = (f32[2,40,128]{2,1,0:T(8,128)S(1)}, f32[2,40,128]{2,1,0:T(8,128)S(1)}, u32[]{:S(2)}, u32[]{:S(2)}) collective-permute-start(f32[2,40,128]{2,1,0:T(8,128)S(1)} %get-tuple-element.17.after_ref), channel_id=1, source_target_pairs={{0,7},{1,6},{2,5},{3,4},{4,3},{5,2},{6,1},{7,0},{8,15},{9,14},{10,... | collective-permute-start | bytes 122888 | tf_op jit(solution)/shard_map/ppermute | solution.py:373
  11.6 0.6 %collective-permute-start.2 = (f32[2,40,128]{2,1,0:T(8,128)S(1)}, f32[2,40,128]{2,1,0:T(8,128)S(1)}, u32[]{:S(2)}, u32[]{:S(2)}) collective-permute-start(f32[2,40,128]{2,1,0:T(8,128)S(1)} %get-tuple-element.18), channel_id=1, source_target_pairs={{0,3},{1,2},{2,1},{3,0},{4,7},{5,6},{6,5},{7,4},{8,11},{9,10},{10,... | collective-permute-start | bytes 122888 | tf_op jit(solution)/shard_map/ppermute | solution.py:373
  13.1 1.6 %caches.1 = (bf16[1,2,2048,128]{3,2,1,0:T(8,128)(2,1)S(1)}, bf16[1,2,2048,128]{3,2,1,0:T(8,128)(2,1)S(1)}) custom-call(bf16[1,2,2048,128]{3,2,1,0:T(8,128)(2,1)} %k_hbm.1, bf16[1,2,2048,128]{3,2,1,0:T(8,128)(2,1)} %v_hbm.1, f32[2,40,128]{2,1,0:T(8,128)S(1)} %get-tuple-element.17.after_ref), custom_call_target="tpu_custom_call" | custom-call | bytes 2097152 | tf_op jit(solution)/shard_map/caches/pallas_call | solution.py:85
  14.7 0.3 collective-permute-done.2
  15.0 0.9 %collective-permute-done.3 = f32[2,40,128]{2,1,0:T(8,128)S(1)} collective-permute-done((f32[2,40,128]{2,1,0:T(8,128)S(1)}, f32[2,40,128]{2,1,0:T(8,128)S(1)}, u32[]{:S(2)}, u32[]{:S(2)}) %collective-permute-start.3) | collective-permute-done | bytes 40992 | tf_op jit(solution)/shard_map/ppermute | solution.py:373
  15.9 2.4 %collective-permute-start.5 = (f32[1,40,128]{2,1,0:T(8,128)S(1)}, f32[1,40,128]{2,1,0:T(8,128)S(1)}, u32[]{:S(2)}, u32[]{:S(2)}) collective-permute-start(f32[1,40,128]{2,1,0:T(8,128)S(1)} %get-tuple-element.26), channel_id=1, source_target_pairs={{0,9},{1,8},{2,11},{3,10},{4,13},{5,12},{6,15},{7,14},{8,1},{9,0},... | collective-permute-start | bytes 61448 | tf_op jit(solution)/shard_map/ppermute | solution.py:373
  18.3 0.4 %collective-permute-start.6 = (f32[1,40,128]{2,1,0:T(8,128)S(1)}, f32[1,40,128]{2,1,0:T(8,128)S(1)}, u32[]{:S(2)}, u32[]{:S(2)}) collective-permute-start(f32[1,40,128]{2,1,0:T(8,128)S(1)} %get-tuple-element.29), channel_id=1, source_target_pairs={{0,1},{1,0},{2,3},{3,2},{4,5},{5,4},{6,7},{7,6},{8,9},{9,8},{10,11... | collective-permute-start | bytes 61448 | tf_op jit(solution)/shard_map/ppermute | solution.py:368
  18.7 1.4 %collective-permute-done.5.refs_0_ = f32[1,40,128]{2,1,0:T(8,128)S(1)} collective-permute-done((f32[1,40,128]{2,1,0:T(8,128)S(1)}, f32[1,40,128]{2,1,0:T(8,128)S(1)}, u32[]{:S(2)}, u32[]{:S(2)}) %collective-permute-start.5) | collective-permute-done | bytes 20512 | tf_op jit(solution)/shard_map/ppermute | solution.py:373
  20.1 0.8 %attend.1.refs_4_ = bf16[1,32,128]{2,1,0:T(8,128)(2,1)S(1)} custom-call(bf16[4096,2048]{1,0:T(8,128)(2,1)} %refs_5_.1, f32[8,128]{1,0:T(8,128)S(1)} %get-tuple-element.23.turn_ref, f32[1,2048]{1,0:T(1,128)S(1)} %get-tuple-element.24.live_ref, bf16[1,2,2048,128]{3,2,1,0:T(8,128)(2,1)S(1)} %get-tuple-element.21.after_ref.k_ref, ...), custom_call_target="tpu_custom_call" | custom-call | flops 33554432 | bytes 2097152 | tf_op jit(solution)/shard_map/attend/pallas_call | solution.py:294
  20.9 2.4 %collective-permute-start.7 = (bf16[1,32,128]{2,1,0:T(8,128)(2,1)S(1)}, bf16[1,32,128]{2,1,0:T(8,128)(2,1)S(1)}, u32[]{:S(2)}, u32[]{:S(2)}) collective-permute-start(bf16[1,32,128]{2,1,0:T(8,128)(2,1)S(1)} %attend.1.refs_4_), channel_id=1, source_target_pairs={{0,9},{1,8},{2,11},{3,10},{4,13},{5,12},{6,15},{7,14},{8,1},{9,0},... | collective-permute-start | bytes 24584 | tf_op jit(solution)/shard_map/ppermute | solution.py:373
  23.3 0.4 %collective-permute-start.8 = (bf16[1,32,128]{2,1,0:T(8,128)(2,1)S(1)}, bf16[1,32,128]{2,1,0:T(8,128)(2,1)S(1)}, u32[]{:S(2)}, u32[]{:S(2)}) collective-permute-start(bf16[1,32,128]{2,1,0:T(8,128)(2,1)S(1)} %attend.1.refs_4_), channel_id=1, source_target_pairs={{0,1},{1,0},{2,3},{3,2},{4,5},{5,4},{6,7},{7,6},{8,9},{9,8},{10,11... | collective-permute-start | bytes 24584 | tf_op jit(solution)/shard_map/ppermute | solution.py:368
  23.7 1.3 %collective-permute-done.7 = bf16[1,32,128]{2,1,0:T(8,128)(2,1)S(1)} collective-permute-done((bf16[1,32,128]{2,1,0:T(8,128)(2,1)S(1)}, bf16[1,32,128]{2,1,0:T(8,128)(2,1)S(1)}, u32[]{:S(2)}, u32[]{:S(2)}) %collective-permute-start.7) | collective-permute-done | bytes 8224 | tf_op jit(solution)/shard_map/ppermute | solution.py:373
  25.0 1.7 %collective-permute-start.10 = (bf16[2,32,128]{2,1,0:T(8,128)(2,1)S(1)}, bf16[2,32,128]{2,1,0:T(8,128)(2,1)S(1)}, u32[]{:S(2)}, u32[]{:S(2)}) collective-permute-start(bf16[2,32,128]{2,1,0:T(8,128)(2,1)S(1)} %constant_dynamic-update-slice_fusion), channel_id=1, source_target_pairs={{0,7},{1,6},{2,5},{3,4},{4,3},{5,2},{6,1},{7,0},{8,15},{9,14},{10,... | collective-permute-start | bytes 49160 | tf_op jit(solution)/shard_map/ppermute | solution.py:373
  26.7 0.6 %collective-permute-start.11 = (bf16[2,32,128]{2,1,0:T(8,128)(2,1)S(1)}, bf16[2,32,128]{2,1,0:T(8,128)(2,1)S(1)}, u32[]{:S(2)}, u32[]{:S(2)}) collective-permute-start(bf16[2,32,128]{2,1,0:T(8,128)(2,1)S(1)} %constant_dynamic-update-slice_fusion), channel_id=1, source_target_pairs={{0,3},{1,2},{2,1},{3,0},{4,7},{5,6},{6,5},{7,4},{8,11},{9,10},{10,... | collective-permute-start | bytes 49160 | tf_op jit(solution)/shard_map/ppermute | solution.py:373
  27.2 1.2 %collective-permute-start.9 = (bf16[2,32,128]{2,1,0:T(8,128)(2,1)S(1)}, bf16[2,32,128]{2,1,0:T(8,128)(2,1)S(1)}, u32[]{:S(2)}, u32[]{:S(2)}) collective-permute-start(bf16[2,32,128]{2,1,0:T(8,128)(2,1)S(1)} %constant_dynamic-update-slice_fusion), channel_id=1, source_target_pairs={{0,5},{1,4},{2,7},{3,6},{4,1},{5,0},{6,3},{7,2},{8,13},{9,12},{10,... | collective-permute-start | bytes 49160 | tf_op jit(solution)/shard_map/ppermute | solution.py:373
  28.4 1.2 %collective-permute-done.12.refs_3_ = bf16[1,32,128]{2,1,0:T(8,128)(2,1)S(1)} collective-permute-done((bf16[1,32,128]{2,1,0:T(8,128)(2,1)S(1)}, bf16[1,32,128]{2,1,0:T(8,128)(2,1)S(1)}, u32[]{:S(2)}, u32[]{:S(2)}) %collective-permute-start.12) | collective-permute-done | bytes 8224 | tf_op jit(solution)/shard_map/ppermute | solution.py:368
  29.6 0.4 %collective-permute-done.11.refs_2_ = bf16[2,32,128]{2,1,0:T(8,128)(2,1)S(1)} collective-permute-done((bf16[2,32,128]{2,1,0:T(8,128)(2,1)S(1)}, bf16[2,32,128]{2,1,0:T(8,128)(2,1)S(1)}, u32[]{:S(2)}, u32[]{:S(2)}) %collective-permute-start.11) | collective-permute-done | bytes 16416 | tf_op jit(solution)/shard_map/ppermute | solution.py:373
  30.0 0.4 %collective-permute-done.9.refs_0_ = bf16[2,32,128]{2,1,0:T(8,128)(2,1)S(1)} collective-permute-done((bf16[2,32,128]{2,1,0:T(8,128)(2,1)S(1)}, bf16[2,32,128]{2,1,0:T(8,128)(2,1)S(1)}, u32[]{:S(2)}, u32[]{:S(2)}) %collective-permute-start.9) | collective-permute-done | bytes 16416 | tf_op jit(solution)/shard_map/ppermute | solution.py:373
  30.4 2.3 %output.1 = (f32[4,2048]{1,0:T(4,128)S(1)}, f32[4,2048]{1,0:T(4,128)S(1)}) custom-call(bf16[2,32,128]{2,1,0:T(8,128)(2,1)S(1)} %collective-permute-done.9.refs_0_, bf16[2,32,128]{2,1,0:T(8,128)(2,1)S(1)} %collective-permute-done.10.refs_1_, bf16[2,32,128]{2,1,0:T(8,128)(2,1)S(1)} %collective-permute-done.11.refs_2_, ...), custom_call_target="tpu_custom_call" | custom-call | flops 134217728 | bytes 16777216 | tf_op jit(solution)/shard_map/output/pallas_call | solution.py:349
  33.0 1.1 %collective-permute-done.13 = f32[4,2048]{1,0:T(4,128)S(1)} collective-permute-done((f32[4,2048]{1,0:T(4,128)S(1)}, f32[4,2048]{1,0:T(4,128)S(1)}, u32[]{:S(2)}, u32[]{:S(2)}) %collective-permute-start.13) | collective-permute-done | bytes 32800 | tf_op jit(solution)/shard_map/ppermute | solution.py:368
  34.0 0.6 %add_convert_fusion = bf16[4,2048]{1,0:T(4,128)(2,1)} fusion(f32[4,2048]{1,0:T(4,128)S(1)} %get-tuple-element.27, f32[4,2048]{1,0:T(4,128)S(1)} %collective-permute-done.13), kind=kLoop, calls=%fused_computation | loop fusion | flops 16384 | bytes 81920 | tf_op jit(solution)/shard_map/convert_element_type | solution.py:438
  (31 shorter events, 0.5 us)
Async XLA Ops:
  0.0 2.5 %copy-start.2 = (bf16[4,2048]{1,0:T(4,128)(2,1)S(1)}, bf16[4,2048]{1,0:T(4,128)(2,1)}, u32[]{:S(2)}) copy-start(bf16[4,2048]{1,0:T(4,128)(2,1)} %rows_ref.1) | copy-start | bytes 49156
  0.0 2.6 %copy-start = (bf16[2048,256]{1,0:T(8,128)(2,1)S(1)}, bf16[2048,256]{1,0:T(8,128)(2,1)}, u32[]{:S(2)}) copy-start(bf16[2048,256]{1,0:T(8,128)(2,1)} %wk.1) | copy-start | bytes 3145732
  0.0 2.6 %copy-start.1 = (bf16[2048,256]{1,0:T(8,128)(2,1)S(1)}, bf16[2048,256]{1,0:T(8,128)(2,1)}, u32[]{:S(2)}) copy-start(bf16[2048,256]{1,0:T(8,128)(2,1)} %wv.1) | copy-start | bytes 3145732
  0.0 2.5 %collective-permute-start = (bf16[4,2048]{1,0:T(4,128)(2,1)}, bf16[4,2048]{1,0:T(4,128)(2,1)S(1)}, u32[]{:S(2)}, u32[]{:S(2)}) collective-permute-start(bf16[4,2048]{1,0:T(4,128)(2,1)} %rows_ref.1), channel_id=1, source_target_pairs={{0,1},{1,0},{2,3},{3,2},{4,5},{5,4},{6,7},{7,6},{8,9},{9,8},{10,11... | collective-permute-start | bytes 49160 | tf_op jit(solution)/shard_map/ppermute | solution.py:368
  8.0 6.7 %collective-permute-start.1 = (f32[2,40,128]{2,1,0:T(8,128)S(1)}, f32[2,40,128]{2,1,0:T(8,128)S(1)}, u32[]{:S(2)}, u32[]{:S(2)}) collective-permute-start(f32[2,40,128]{2,1,0:T(8,128)S(1)} %get-tuple-element.17.after_ref), channel_id=1, source_target_pairs={{0,7},{1,6},{2,5},{3,4},{4,3},{5,2},{6,1},{7,0},{8,15},{9,14},{10,... | collective-permute-start | bytes 122888 | tf_op jit(solution)/shard_map/ppermute | solution.py:373
  11.6 3.4 %collective-permute-start.2 = (f32[2,40,128]{2,1,0:T(8,128)S(1)}, f32[2,40,128]{2,1,0:T(8,128)S(1)}, u32[]{:S(2)}, u32[]{:S(2)}) collective-permute-start(f32[2,40,128]{2,1,0:T(8,128)S(1)} %get-tuple-element.18), channel_id=1, source_target_pairs={{0,3},{1,2},{2,1},{3,0},{4,7},{5,6},{6,5},{7,4},{8,11},{9,10},{10,... | collective-permute-start | bytes 122888 | tf_op jit(solution)/shard_map/ppermute | solution.py:373
  12.2 3.7 %collective-permute-start.3 = (f32[2,40,128]{2,1,0:T(8,128)S(1)}, f32[2,40,128]{2,1,0:T(8,128)S(1)}, u32[]{:S(2)}, u32[]{:S(2)}) collective-permute-start(f32[2,40,128]{2,1,0:T(8,128)S(1)} %get-tuple-element.19), channel_id=1, source_target_pairs={{0,5},{1,4},{2,7},{3,6},{4,1},{5,0},{6,3},{7,2},{8,13},{9,12},{10,... | collective-permute-start | bytes 122888 | tf_op jit(solution)/shard_map/ppermute | solution.py:373
  12.3 3.6 %collective-permute-start.4 = (f32[2,40,128]{2,1,0:T(8,128)S(1)}, f32[2,40,128]{2,1,0:T(8,128)S(1)}, u32[]{:S(2)}, u32[]{:S(2)}) collective-permute-start(f32[2,40,128]{2,1,0:T(8,128)S(1)} %get-tuple-element.20), channel_id=1, source_target_pairs={{0,1},{1,0},{2,3},{3,2},{4,5},{5,4},{6,7},{7,6},{8,9},{9,8},{10,11... | collective-permute-start | bytes 122888 | tf_op jit(solution)/shard_map/ppermute | solution.py:368
  14.6 15.8 %slice-start = ((s8[16777216]{0:T(1024)(128)(4,1)}), s8[4194304]{0:T(1024)(128)(4,1)S(1)}, s32[]{:S(2)}) async-start(s8[16777216]{0:T(1024)(128)(4,1)} %bitcast.2), calls=%async_computation | async-start | bytes 8388608
  14.7 15.8 %slice-start.1 = ((s8[16777216]{0:T(1024)(128)(4,1)}), s8[4194304]{0:T(1024)(128)(4,1)S(1)}, s32[]{:S(2)}) async-start(s8[16777216]{0:T(1024)(128)(4,1)} %bitcast.2), calls=%async_computation.1 | async-start | bytes 8388608
  15.9 4.2 %collective-permute-start.5 = (f32[1,40,128]{2,1,0:T(8,128)S(1)}, f32[1,40,128]{2,1,0:T(8,128)S(1)}, u32[]{:S(2)}, u32[]{:S(2)}) collective-permute-start(f32[1,40,128]{2,1,0:T(8,128)S(1)} %get-tuple-element.26), channel_id=1, source_target_pairs={{0,9},{1,8},{2,11},{3,10},{4,13},{5,12},{6,15},{7,14},{8,1},{9,0},... | collective-permute-start | bytes 61448 | tf_op jit(solution)/shard_map/ppermute | solution.py:373
  18.3 1.8 %collective-permute-start.6 = (f32[1,40,128]{2,1,0:T(8,128)S(1)}, f32[1,40,128]{2,1,0:T(8,128)S(1)}, u32[]{:S(2)}, u32[]{:S(2)}) collective-permute-start(f32[1,40,128]{2,1,0:T(8,128)S(1)} %get-tuple-element.29), channel_id=1, source_target_pairs={{0,1},{1,0},{2,3},{3,2},{4,5},{5,4},{6,7},{7,6},{8,9},{9,8},{10,11... | collective-permute-start | bytes 61448 | tf_op jit(solution)/shard_map/ppermute | solution.py:368
  20.1 10.4 %slice-start.2 = ((s8[16777216]{0:T(1024)(128)(4,1)}), s8[4194304]{0:T(1024)(128)(4,1)S(1)}, s32[]{:S(2)}) async-start(s8[16777216]{0:T(1024)(128)(4,1)} %bitcast.2), calls=%async_computation.2 | async-start | bytes 8388608
  20.1 10.4 %slice-start.3 = ((s8[16777216]{0:T(1024)(128)(4,1)}), s8[4194304]{0:T(1024)(128)(4,1)S(1)}, s32[]{:S(2)}) async-start(s8[16777216]{0:T(1024)(128)(4,1)} %bitcast.2), calls=%async_computation.3 | async-start | bytes 8388608
  20.9 4.0 %collective-permute-start.7 = (bf16[1,32,128]{2,1,0:T(8,128)(2,1)S(1)}, bf16[1,32,128]{2,1,0:T(8,128)(2,1)S(1)}, u32[]{:S(2)}, u32[]{:S(2)}) collective-permute-start(bf16[1,32,128]{2,1,0:T(8,128)(2,1)S(1)} %attend.1.refs_4_), channel_id=1, source_target_pairs={{0,9},{1,8},{2,11},{3,10},{4,13},{5,12},{6,15},{7,14},{8,1},{9,0},... | collective-permute-start | bytes 24584 | tf_op jit(solution)/shard_map/ppermute | solution.py:373
  23.3 1.7 %collective-permute-start.8 = (bf16[1,32,128]{2,1,0:T(8,128)(2,1)S(1)}, bf16[1,32,128]{2,1,0:T(8,128)(2,1)S(1)}, u32[]{:S(2)}, u32[]{:S(2)}) collective-permute-start(bf16[1,32,128]{2,1,0:T(8,128)(2,1)S(1)} %attend.1.refs_4_), channel_id=1, source_target_pairs={{0,1},{1,0},{2,3},{3,2},{4,5},{5,4},{6,7},{7,6},{8,9},{9,8},{10,11... | collective-permute-start | bytes 24584 | tf_op jit(solution)/shard_map/ppermute | solution.py:368
  25.0 4.6 %collective-permute-start.10 = (bf16[2,32,128]{2,1,0:T(8,128)(2,1)S(1)}, bf16[2,32,128]{2,1,0:T(8,128)(2,1)S(1)}, u32[]{:S(2)}, u32[]{:S(2)}) collective-permute-start(bf16[2,32,128]{2,1,0:T(8,128)(2,1)S(1)} %constant_dynamic-update-slice_fusion), channel_id=1, source_target_pairs={{0,7},{1,6},{2,5},{3,4},{4,3},{5,2},{6,1},{7,0},{8,15},{9,14},{10,... | collective-permute-start | bytes 49160 | tf_op jit(solution)/shard_map/ppermute | solution.py:373
  26.7 3.3 %collective-permute-start.11 = (bf16[2,32,128]{2,1,0:T(8,128)(2,1)S(1)}, bf16[2,32,128]{2,1,0:T(8,128)(2,1)S(1)}, u32[]{:S(2)}, u32[]{:S(2)}) collective-permute-start(bf16[2,32,128]{2,1,0:T(8,128)(2,1)S(1)} %constant_dynamic-update-slice_fusion), channel_id=1, source_target_pairs={{0,3},{1,2},{2,1},{3,0},{4,7},{5,6},{6,5},{7,4},{8,11},{9,10},{10,... | collective-permute-start | bytes 49160 | tf_op jit(solution)/shard_map/ppermute | solution.py:373
  27.2 3.2 %collective-permute-start.9 = (bf16[2,32,128]{2,1,0:T(8,128)(2,1)S(1)}, bf16[2,32,128]{2,1,0:T(8,128)(2,1)S(1)}, u32[]{:S(2)}, u32[]{:S(2)}) collective-permute-start(bf16[2,32,128]{2,1,0:T(8,128)(2,1)S(1)} %constant_dynamic-update-slice_fusion), channel_id=1, source_target_pairs={{0,5},{1,4},{2,7},{3,6},{4,1},{5,0},{6,3},{7,2},{8,13},{9,12},{10,... | collective-permute-start | bytes 49160 | tf_op jit(solution)/shard_map/ppermute | solution.py:373
  28.4 1.2 %collective-permute-start.12 = (bf16[1,32,128]{2,1,0:T(8,128)(2,1)S(1)}, bf16[1,32,128]{2,1,0:T(8,128)(2,1)S(1)}, u32[]{:S(2)}, u32[]{:S(2)}) collective-permute-start(bf16[1,32,128]{2,1,0:T(8,128)(2,1)S(1)} %collective-permute-done.7), channel_id=1, source_target_pairs={{0,1},{1,0},{2,3},{3,2},{4,5},{5,4},{6,7},{7,6},{8,9},{9,8},{10,11... | collective-permute-start | bytes 24584 | tf_op jit(solution)/shard_map/ppermute | solution.py:368
  32.8 1.3 %collective-permute-start.13 = (f32[4,2048]{1,0:T(4,128)S(1)}, f32[4,2048]{1,0:T(4,128)S(1)}, u32[]{:S(2)}, u32[]{:S(2)}) collective-permute-start(f32[4,2048]{1,0:T(4,128)S(1)} %get-tuple-element.28), channel_id=1, source_target_pairs={{0,1},{1,0},{2,3},{3,2},{4,5},{5,4},{6,7},{7,6},{8,9},{9,8},{10,11... | collective-permute-start | bytes 98312 | tf_op jit(solution)/shard_map/ppermute | solution.py:368

commit v22 on v19

--- a/solution.py
+++ b/solution.py
@@ -281,13 +281,14 @@
 def output_kernel(bits, places, turned, *refs):
     pieces = len(places)
     parts = refs[:pieces]
-    w_ref, mine_ref, theirs_ref, flat, left, sums = refs[pieces:]
+    w_ref, mine_ref, theirs_ref, flat, left = refs[pieces:]
     slots = left.shape[0]
     heads = flat.shape[0] // slots
+    here = lax.axis_index("gx")
     for slot, ref in zip(places, parts):
         for i, row in enumerate(range(ref.shape[0])[::turned]):
-            at = (slot + i) * heads
-            flat[at : at + heads, :] = ref[row].astype(jnp.float32)
+            at = pl.multiple_of((here ^ bit_reverse(slot + i, bits)) * heads, heads)
+            flat[pl.ds(at, heads), :] = ref[row].astype(jnp.float32)
     for head in range(heads):
         left[:, head * HEAD_SIZE : (head + 1) * HEAD_SIZE] = flat[
             pl.ds(head, slots, stride=heads), :
@@ -299,14 +300,11 @@
         part = slice(at, at + chunk)
         term = jnp.dot(left[:, part], w_ref[part, :], preferred_element_type=jnp.float32)
         total = term if total is None else total + term
-    sums[...] = total
     half = slots // 2
-    turn = bit_reverse(lax.axis_index("gx"), bits)
     gy = lax.axis_index("gy")
-    for ref, side in ((mine_ref, gy), (theirs_ref, 1 - gy)):
-        for t in range(half):
-            slot = bit_reverse(t, bits) ^ turn ^ side
-            ref[t : t + 1, :] = sums[pl.ds(slot, 1), :]
+    lower, upper = total[:half], total[half:]
+    mine_ref[...] = jnp.where(gy == 0, lower, upper)
+    theirs_ref[...] = jnp.where(gy == 0, upper, lower)
 
 
 def output(parts, order, w_out, slots, turned=1):
@@ -326,7 +324,6 @@
         scratch_shapes=[
             pltpu.VMEM((slots * heads, HEAD_SIZE), jnp.float32),
             pltpu.VMEM((slots, depth), jnp.bfloat16),
-            pltpu.VMEM((slots, width), jnp.float32),
         ],
         compiler_params=pltpu.CompilerParams(vmem_limit_bytes=12 * MIB),
         cost_estimate=pl.CostEstimate(

time: 34.8 us -> 34.7 us (level)
  no operation moved by 1% of the time
where the time goes in v22:
time: 34.7 us; the launch traced here: 34.5 us
  starting transfers between devices  14 us (40%)
  Pallas kernels  10.7 us (31%)
  waiting for transfers between devices  8.34 us (24%)
  between operations  0.81 us (2%)
  other arithmetic  0.71 us (2%)
    ppermute x8, starting transfers between devices, cross(): return lax.ppermute(block, ('gx', 'gy'), pairs)  12.4 us
    ppermute x8, waiting for transfers between devices, cross(): return lax.ppermute(block, ('gx', 'gy'), pairs)  6.15 us
    pallas_call x1, Pallas kernels, project(): pl.pallas_call(functools.partial(project_kernel, bits), out_shape=(piece,...  5.53 us
    pallas_call x1, Pallas kernels, output(): pl.pallas_call(functools.partial(output_kernel, bits, places, turned), ou...  2.28 us
    ppermute x6, waiting for transfers between devices, swap(): return lax.ppermute(block, axis, [(i, i ^ mask) for i in range(devices)])  2.18 us
    pallas_call x1, Pallas kernels, stage_rows(): pl.pallas_call(functools.partial(stage_kernel, rows), out_shape=jax.Shape...  1.99 us
    ppermute x6, starting transfers between devices, swap(): return lax.ppermute(block, axis, [(i, i ^ mask) for i in range(devices)])  1.54 us
    pallas_call x1, Pallas kernels, attend(): pl.pallas_call(functools.partial(attend_kernel, query_heads, kv_heads, le...  0.82 us
  transfers between devices with their start and end apart: 14, of which 8 were waited for; matrix products, arithmetic and copies ran while one was open for 0% of the time, Pallas kernels for 6%

profile of v22, /device:TPU:0, one launch (start us, length us, event | category | flops | bytes accessed | tf_op | source)
XLA Modules:
  0.0 34.5 jit_solution(6456743059254743799)
XLA Ops:
  0.0 0.5 %collective-permute-start = (bf16[4,2048]{1,0:T(4,128)(2,1)}, bf16[4,2048]{1,0:T(4,128)(2,1)S(1)}, u32[]{:S(2)}, u32[]{:S(2)}) collective-permute-start(bf16[4,2048]{1,0:T(4,128)(2,1)} %rows_ref.1), channel_id=1, source_target_pairs={{0,1},{1,0},{2,3},{3,2},{4,5},{5,4},{6,7},{7,6},{8,9},{9,8},{10,11... | collective-permute-start | bytes 49160 | tf_op jit(solution)/shard_map/ppermute | solution.py:337
  0.5 2.0 %stage.1.first = bf16[384,4096]{1,0:T(8,128)(2,1)S(1)} custom-call(bf16[2048,4096]{1,0:T(8,128)(2,1)} %wq_hbm.1), custom_call_target="tpu_custom_call" | custom-call | bytes 3145728 | tf_op jit(solution)/shard_map/stage/pallas_call | solution.py:57
  2.6 5.5 %project.1 = (f32[2,40,128]{2,1,0:T(8,128)S(1)}, f32[2,40,128]{2,1,0:T(8,128)S(1)}, f32[2,40,128]{2,1,0:T(8,128)S(1)}, f32[2,40,128]{2,1,0:T(8,128)S(1)}) custom-call(bf16[4,2048]{1,0:T(4,128)(2,1)S(1)} %copy-done.4, bf16[4,2048]{1,0:T(4,128)(2,1)S(1)} %collective-permute-done.other_ref, bf16[2048,4096]{1,0:T(8,128)(2,1)} %wq_hbm.1, ...), custom_call_target="tpu_custom_call" | custom-call | flops 150994944 | bytes 18874368 | tf_op jit(solution)/shard_map/project/pallas_call | solution.py:179
  8.1 3.6 %collective-permute-start.1 = (f32[2,40,128]{2,1,0:T(8,128)S(1)}, f32[2,40,128]{2,1,0:T(8,128)S(1)}, u32[]{:S(2)}, u32[]{:S(2)}) collective-permute-start(f32[2,40,128]{2,1,0:T(8,128)S(1)} %get-tuple-element.15.after_ref), channel_id=1, source_target_pairs={{0,7},{1,6},{2,5},{3,4},{4,3},{5,2},{6,1},{7,0},{8,15},{9,14},{10,... | collective-permute-start | bytes 122888 | tf_op jit(solution)/shard_map/ppermute | solution.py:342
  11.7 0.7 %collective-permute-start.2 = (f32[2,40,128]{2,1,0:T(8,128)S(1)}, f32[2,40,128]{2,1,0:T(8,128)S(1)}, u32[]{:S(2)}, u32[]{:S(2)}) collective-permute-start(f32[2,40,128]{2,1,0:T(8,128)S(1)} %get-tuple-element.16), channel_id=1, source_target_pairs={{0,3},{1,2},{2,1},{3,0},{4,7},{5,6},{6,5},{7,4},{8,11},{9,10},{10,... | collective-permute-start | bytes 122888 | tf_op jit(solution)/shard_map/ppermute | solution.py:342
  13.3 0.4 %collective-permute-done.1 = f32[2,40,128]{2,1,0:T(8,128)S(1)} collective-permute-done((f32[2,40,128]{2,1,0:T(8,128)S(1)}, f32[2,40,128]{2,1,0:T(8,128)S(1)}, u32[]{:S(2)}, u32[]{:S(2)}) %collective-permute-start.1) | collective-permute-done | bytes 40992 | tf_op jit(solution)/shard_map/ppermute | solution.py:342
  13.7 1.5 %collective-permute-done.2 = f32[2,40,128]{2,1,0:T(8,128)S(1)} collective-permute-done((f32[2,40,128]{2,1,0:T(8,128)S(1)}, f32[2,40,128]{2,1,0:T(8,128)S(1)}, u32[]{:S(2)}, u32[]{:S(2)}) %collective-permute-start.2) | collective-permute-done | bytes 40992 | tf_op jit(solution)/shard_map/ppermute | solution.py:342
  15.1 0.9 %collective-permute-done.3 = f32[2,40,128]{2,1,0:T(8,128)S(1)} collective-permute-done((f32[2,40,128]{2,1,0:T(8,128)S(1)}, f32[2,40,128]{2,1,0:T(8,128)S(1)}, u32[]{:S(2)}, u32[]{:S(2)}) %collective-permute-start.3) | collective-permute-done | bytes 40992 | tf_op jit(solution)/shard_map/ppermute | solution.py:342
  16.1 2.4 %collective-permute-start.5 = (f32[1,40,128]{2,1,0:T(8,128)S(1)}, f32[1,40,128]{2,1,0:T(8,128)S(1)}, u32[]{:S(2)}, u32[]{:S(2)}) collective-permute-start(f32[1,40,128]{2,1,0:T(8,128)S(1)} %get-tuple-element.22), channel_id=1, source_target_pairs={{0,9},{1,8},{2,11},{3,10},{4,13},{5,12},{6,15},{7,14},{8,1},{9,0},... | collective-permute-start | bytes 61448 | tf_op jit(solution)/shard_map/ppermute | solution.py:342
  18.5 0.4 %collective-permute-start.6 = (f32[1,40,128]{2,1,0:T(8,128)S(1)}, f32[1,40,128]{2,1,0:T(8,128)S(1)}, u32[]{:S(2)}, u32[]{:S(2)}) collective-permute-start(f32[1,40,128]{2,1,0:T(8,128)S(1)} %get-tuple-element.25), channel_id=1, source_target_pairs={{0,1},{1,0},{2,3},{3,2},{4,5},{5,4},{6,7},{7,6},{8,9},{9,8},{10,11... | collective-permute-start | bytes 61448 | tf_op jit(solution)/shard_map/ppermute | solution.py:337
  18.9 1.4 %collective-permute-done.5.refs_0_ = f32[1,40,128]{2,1,0:T(8,128)S(1)} collective-permute-done((f32[1,40,128]{2,1,0:T(8,128)S(1)}, f32[1,40,128]{2,1,0:T(8,128)S(1)}, u32[]{:S(2)}, u32[]{:S(2)}) %collective-permute-start.5) | collective-permute-done | bytes 20512 | tf_op jit(solution)/shard_map/ppermute | solution.py:342
  20.3 0.8 %attend.1.refs_4_ = bf16[1,32,128]{2,1,0:T(8,128)(2,1)S(1)} custom-call(bf16[4096,2048]{1,0:T(8,128)(2,1)} %refs_5_.1, f32[8,128]{1,0:T(8,128)S(1)} %get-tuple-element.20.turn_ref, f32[1,2048]{1,0:T(1,128)S(1)} %get-tuple-element.21.live_ref, bf16[1,2,2048,128]{3,2,1,0:T(8,128)(2,1)S(1)} %copy-done, bf16[1,2,2048,128]{3,2,1,0:T(8,128)(2,1)S(1)} %copy-done.1, ...), custom_call_target="tpu_custom_call" | custom-call | flops 33554432 | bytes 2097152 | tf_op jit(solution)/shard_map/attend/pallas_call | solution.py:266
  21.1 2.4 %collective-permute-start.7 = (bf16[1,32,128]{2,1,0:T(8,128)(2,1)S(1)}, bf16[1,32,128]{2,1,0:T(8,128)(2,1)S(1)}, u32[]{:S(2)}, u32[]{:S(2)}) collective-permute-start(bf16[1,32,128]{2,1,0:T(8,128)(2,1)S(1)} %attend.1.refs_4_), channel_id=1, source_target_pairs={{0,9},{1,8},{2,11},{3,10},{4,13},{5,12},{6,15},{7,14},{8,1},{9,0},... | collective-permute-start | bytes 24584 | tf_op jit(solution)/shard_map/ppermute | solution.py:342
  23.5 0.4 %collective-permute-start.8 = (bf16[1,32,128]{2,1,0:T(8,128)(2,1)S(1)}, bf16[1,32,128]{2,1,0:T(8,128)(2,1)S(1)}, u32[]{:S(2)}, u32[]{:S(2)}) collective-permute-start(bf16[1,32,128]{2,1,0:T(8,128)(2,1)S(1)} %attend.1.refs_4_), channel_id=1, source_target_pairs={{0,1},{1,0},{2,3},{3,2},{4,5},{5,4},{6,7},{7,6},{8,9},{9,8},{10,11... | collective-permute-start | bytes 24584 | tf_op jit(solution)/shard_map/ppermute | solution.py:337
  23.9 1.3 %collective-permute-done.7 = bf16[1,32,128]{2,1,0:T(8,128)(2,1)S(1)} collective-permute-done((bf16[1,32,128]{2,1,0:T(8,128)(2,1)S(1)}, bf16[1,32,128]{2,1,0:T(8,128)(2,1)S(1)}, u32[]{:S(2)}, u32[]{:S(2)}) %collective-permute-start.7) | collective-permute-done | bytes 8224 | tf_op jit(solution)/shard_map/ppermute | solution.py:342
  25.2 1.2 %collective-permute-start.10 = (bf16[2,32,128]{2,1,0:T(8,128)(2,1)S(1)}, bf16[2,32,128]{2,1,0:T(8,128)(2,1)S(1)}, u32[]{:S(2)}, u32[]{:S(2)}) collective-permute-start(bf16[2,32,128]{2,1,0:T(8,128)(2,1)S(1)} %constant_dynamic-update-slice_fusion), channel_id=1, source_target_pairs={{0,7},{1,6},{2,5},{3,4},{4,3},{5,2},{6,1},{7,0},{8,15},{9,14},{10,... | collective-permute-start | bytes 49160 | tf_op jit(solution)/shard_map/ppermute | solution.py:342
  26.4 0.9 %collective-permute-start.11 = (bf16[2,32,128]{2,1,0:T(8,128)(2,1)S(1)}, bf16[2,32,128]{2,1,0:T(8,128)(2,1)S(1)}, u32[]{:S(2)}, u32[]{:S(2)}) collective-permute-start(bf16[2,32,128]{2,1,0:T(8,128)(2,1)S(1)} %constant_dynamic-update-slice_fusion), channel_id=1, source_target_pairs={{0,3},{1,2},{2,1},{3,0},{4,7},{5,6},{6,5},{7,4},{8,11},{9,10},{10,... | collective-permute-start | bytes 49160 | tf_op jit(solution)/shard_map/ppermute | solution.py:342
  27.2 1.3 %collective-permute-start.9 = (bf16[2,32,128]{2,1,0:T(8,128)(2,1)S(1)}, bf16[2,32,128]{2,1,0:T(8,128)(2,1)S(1)}, u32[]{:S(2)}, u32[]{:S(2)}) collective-permute-start(bf16[2,32,128]{2,1,0:T(8,128)(2,1)S(1)} %constant_dynamic-update-slice_fusion), channel_id=1, source_target_pairs={{0,5},{1,4},{2,7},{3,6},{4,1},{5,0},{6,3},{7,2},{8,13},{9,12},{10,... | collective-permute-start | bytes 49160 | tf_op jit(solution)/shard_map/ppermute | solution.py:342
  28.6 1.1 %collective-permute-done.12.refs_3_ = bf16[1,32,128]{2,1,0:T(8,128)(2,1)S(1)} collective-permute-done((bf16[1,32,128]{2,1,0:T(8,128)(2,1)S(1)}, bf16[1,32,128]{2,1,0:T(8,128)(2,1)S(1)}, u32[]{:S(2)}, u32[]{:S(2)}) %collective-permute-start.12) | collective-permute-done | bytes 8224 | tf_op jit(solution)/shard_map/ppermute | solution.py:337
  29.7 0.7 %collective-permute-done.9.refs_0_ = bf16[2,32,128]{2,1,0:T(8,128)(2,1)S(1)} collective-permute-done((bf16[2,32,128]{2,1,0:T(8,128)(2,1)S(1)}, bf16[2,32,128]{2,1,0:T(8,128)(2,1)S(1)}, u32[]{:S(2)}, u32[]{:S(2)}) %collective-permute-start.9) | collective-permute-done | bytes 16416 | tf_op jit(solution)/shard_map/ppermute | solution.py:342
  30.4 2.3 %output.1 = (f32[4,2048]{1,0:T(4,128)S(1)}, f32[4,2048]{1,0:T(4,128)S(1)}) custom-call(bf16[2,32,128]{2,1,0:T(8,128)(2,1)S(1)} %collective-permute-done.9.refs_0_, bf16[2,32,128]{2,1,0:T(8,128)(2,1)S(1)} %collective-permute-done.10.refs_1_, bf16[2,32,128]{2,1,0:T(8,128)(2,1)S(1)} %collective-permute-done.11.refs_2_, ...), custom_call_target="tpu_custom_call" | custom-call | flops 134217728 | bytes 16777216 | tf_op jit(solution)/shard_map/output/pallas_call | solution.py:319
  32.7 0.2 collective-permute-start.13
  32.9 1.0 %collective-permute-done.13 = f32[4,2048]{1,0:T(4,128)S(1)} collective-permute-done((f32[4,2048]{1,0:T(4,128)S(1)}, f32[4,2048]{1,0:T(4,128)S(1)}, u32[]{:S(2)}, u32[]{:S(2)}) %collective-permute-start.13) | collective-permute-done | bytes 32800 | tf_op jit(solution)/shard_map/ppermute | solution.py:337
  33.9 0.6 %add_convert_fusion = bf16[4,2048]{1,0:T(4,128)(2,1)} fusion(f32[4,2048]{1,0:T(4,128)S(1)} %get-tuple-element.23, f32[4,2048]{1,0:T(4,128)S(1)} %collective-permute-done.13), kind=kLoop, calls=%fused_computation | loop fusion | flops 16384 | bytes 81920 | tf_op jit(solution)/shard_map/convert_element_type | solution.py:405
  (34 shorter events, 0.4 us)
Async XLA Ops:
  0.0 2.6 %copy-start.4 = (bf16[4,2048]{1,0:T(4,128)(2,1)S(1)}, bf16[4,2048]{1,0:T(4,128)(2,1)}, u32[]{:S(2)}) copy-start(bf16[4,2048]{1,0:T(4,128)(2,1)} %rows_ref.1) | copy-start | bytes 49156
  0.0 2.6 %copy-start.2 = (bf16[2048,256]{1,0:T(8,128)(2,1)S(1)}, bf16[2048,256]{1,0:T(8,128)(2,1)}, u32[]{:S(2)}) copy-start(bf16[2048,256]{1,0:T(8,128)(2,1)} %wk.1) | copy-start | bytes 3145732
  0.0 2.6 %copy-start.3 = (bf16[2048,256]{1,0:T(8,128)(2,1)S(1)}, bf16[2048,256]{1,0:T(8,128)(2,1)}, u32[]{:S(2)}) copy-start(bf16[2048,256]{1,0:T(8,128)(2,1)} %wv.1) | copy-start | bytes 3145732
  0.0 2.6 %collective-permute-start = (bf16[4,2048]{1,0:T(4,128)(2,1)}, bf16[4,2048]{1,0:T(4,128)(2,1)S(1)}, u32[]{:S(2)}, u32[]{:S(2)}) collective-permute-start(bf16[4,2048]{1,0:T(4,128)(2,1)} %rows_ref.1), channel_id=1, source_target_pairs={{0,1},{1,0},{2,3},{3,2},{4,5},{5,4},{6,7},{7,6},{8,9},{9,8},{10,11... | collective-permute-start | bytes 49160 | tf_op jit(solution)/shard_map/ppermute | solution.py:337
  2.5 17.7 %copy-start = (bf16[1,2,2048,128]{3,2,1,0:T(8,128)(2,1)S(1)}, bf16[1,2,2048,128]{3,2,1,0:T(8,128)(2,1)}, u32[]{:S(2)}) copy-start(bf16[1,2,2048,128]{3,2,1,0:T(8,128)(2,1)} %k_ref.1) | copy-start | bytes 3145732
  2.5 17.7 %copy-start.1 = (bf16[1,2,2048,128]{3,2,1,0:T(8,128)(2,1)S(1)}, bf16[1,2,2048,128]{3,2,1,0:T(8,128)(2,1)}, u32[]{:S(2)}) copy-start(bf16[1,2,2048,128]{3,2,1,0:T(8,128)(2,1)} %v_ref.1) | copy-start | bytes 3145732
  8.1 5.5 %collective-permute-start.1 = (f32[2,40,128]{2,1,0:T(8,128)S(1)}, f32[2,40,128]{2,1,0:T(8,128)S(1)}, u32[]{:S(2)}, u32[]{:S(2)}) collective-permute-start(f32[2,40,128]{2,1,0:T(8,128)S(1)} %get-tuple-element.15.after_ref), channel_id=1, source_target_pairs={{0,7},{1,6},{2,5},{3,4},{4,3},{5,2},{6,1},{7,0},{8,15},{9,14},{10,... | collective-permute-start | bytes 122888 | tf_op jit(solution)/shard_map/ppermute | solution.py:342
  11.7 3.4 %collective-permute-start.2 = (f32[2,40,128]{2,1,0:T(8,128)S(1)}, f32[2,40,128]{2,1,0:T(8,128)S(1)}, u32[]{:S(2)}, u32[]{:S(2)}) collective-permute-start(f32[2,40,128]{2,1,0:T(8,128)S(1)} %get-tuple-element.16), channel_id=1, source_target_pairs={{0,3},{1,2},{2,1},{3,0},{4,7},{5,6},{6,5},{7,4},{8,11},{9,10},{10,... | collective-permute-start | bytes 122888 | tf_op jit(solution)/shard_map/ppermute | solution.py:342
  12.4 3.7 %collective-permute-start.3 = (f32[2,40,128]{2,1,0:T(8,128)S(1)}, f32[2,40,128]{2,1,0:T(8,128)S(1)}, u32[]{:S(2)}, u32[]{:S(2)}) collective-permute-start(f32[2,40,128]{2,1,0:T(8,128)S(1)} %get-tuple-element.17), channel_id=1, source_target_pairs={{0,5},{1,4},{2,7},{3,6},{4,1},{5,0},{6,3},{7,2},{8,13},{9,12},{10,... | collective-permute-start | bytes 122888 | tf_op jit(solution)/shard_map/ppermute | solution.py:342
  12.5 3.6 %collective-permute-start.4 = (f32[2,40,128]{2,1,0:T(8,128)S(1)}, f32[2,40,128]{2,1,0:T(8,128)S(1)}, u32[]{:S(2)}, u32[]{:S(2)}) collective-permute-start(f32[2,40,128]{2,1,0:T(8,128)S(1)} %get-tuple-element.18), channel_id=1, source_target_pairs={{0,1},{1,0},{2,3},{3,2},{4,5},{5,4},{6,7},{7,6},{8,9},{9,8},{10,11... | collective-permute-start | bytes 122888 | tf_op jit(solution)/shard_map/ppermute | solution.py:337
  13.2 17.2 %slice-start = ((s8[16777216]{0:T(1024)(128)(4,1)}), s8[4194304]{0:T(1024)(128)(4,1)S(1)}, s32[]{:S(2)}) async-start(s8[16777216]{0:T(1024)(128)(4,1)} %bitcast.2), calls=%async_computation | async-start | bytes 8388608
  13.2 17.2 %slice-start.1 = ((s8[16777216]{0:T(1024)(128)(4,1)}), s8[4194304]{0:T(1024)(128)(4,1)S(1)}, s32[]{:S(2)}) async-start(s8[16777216]{0:T(1024)(128)(4,1)} %bitcast.2), calls=%async_computation.1 | async-start | bytes 8388608
  16.1 4.2 %collective-permute-start.5 = (f32[1,40,128]{2,1,0:T(8,128)S(1)}, f32[1,40,128]{2,1,0:T(8,128)S(1)}, u32[]{:S(2)}, u32[]{:S(2)}) collective-permute-start(f32[1,40,128]{2,1,0:T(8,128)S(1)} %get-tuple-element.22), channel_id=1, source_target_pairs={{0,9},{1,8},{2,11},{3,10},{4,13},{5,12},{6,15},{7,14},{8,1},{9,0},... | collective-permute-start | bytes 61448 | tf_op jit(solution)/shard_map/ppermute | solution.py:342
  18.5 1.8 %collective-permute-start.6 = (f32[1,40,128]{2,1,0:T(8,128)S(1)}, f32[1,40,128]{2,1,0:T(8,128)S(1)}, u32[]{:S(2)}, u32[]{:S(2)}) collective-permute-start(f32[1,40,128]{2,1,0:T(8,128)S(1)} %get-tuple-element.25), channel_id=1, source_target_pairs={{0,1},{1,0},{2,3},{3,2},{4,5},{5,4},{6,7},{7,6},{8,9},{9,8},{10,11... | collective-permute-start | bytes 61448 | tf_op jit(solution)/shard_map/ppermute | solution.py:337
  20.3 10.1 %slice-start.2 = ((s8[16777216]{0:T(1024)(128)(4,1)}), s8[4194304]{0:T(1024)(128)(4,1)S(1)}, s32[]{:S(2)}) async-start(s8[16777216]{0:T(1024)(128)(4,1)} %bitcast.2), calls=%async_computation.2 | async-start | bytes 8388608
  20.3 10.1 %slice-start.3 = ((s8[16777216]{0:T(1024)(128)(4,1)}), s8[4194304]{0:T(1024)(128)(4,1)S(1)}, s32[]{:S(2)}) async-start(s8[16777216]{0:T(1024)(128)(4,1)} %bitcast.2), calls=%async_computation.3 | async-start | bytes 8388608
  21.1 4.0 %collective-permute-start.7 = (bf16[1,32,128]{2,1,0:T(8,128)(2,1)S(1)}, bf16[1,32,128]{2,1,0:T(8,128)(2,1)S(1)}, u32[]{:S(2)}, u32[]{:S(2)}) collective-permute-start(bf16[1,32,128]{2,1,0:T(8,128)(2,1)S(1)} %attend.1.refs_4_), channel_id=1, source_target_pairs={{0,9},{1,8},{2,11},{3,10},{4,13},{5,12},{6,15},{7,14},{8,1},{9,0},... | collective-permute-start | bytes 24584 | tf_op jit(solution)/shard_map/ppermute | solution.py:342
  23.5 1.7 %collective-permute-start.8 = (bf16[1,32,128]{2,1,0:T(8,128)(2,1)S(1)}, bf16[1,32,128]{2,1,0:T(8,128)(2,1)S(1)}, u32[]{:S(2)}, u32[]{:S(2)}) collective-permute-start(bf16[1,32,128]{2,1,0:T(8,128)(2,1)S(1)} %attend.1.refs_4_), channel_id=1, source_target_pairs={{0,1},{1,0},{2,3},{3,2},{4,5},{5,4},{6,7},{7,6},{8,9},{9,8},{10,11... | collective-permute-start | bytes 24584 | tf_op jit(solution)/shard_map/ppermute | solution.py:337
  25.2 4.5 %collective-permute-start.10 = (bf16[2,32,128]{2,1,0:T(8,128)(2,1)S(1)}, bf16[2,32,128]{2,1,0:T(8,128)(2,1)S(1)}, u32[]{:S(2)}, u32[]{:S(2)}) collective-permute-start(bf16[2,32,128]{2,1,0:T(8,128)(2,1)S(1)} %constant_dynamic-update-slice_fusion), channel_id=1, source_target_pairs={{0,7},{1,6},{2,5},{3,4},{4,3},{5,2},{6,1},{7,0},{8,15},{9,14},{10,... | collective-permute-start | bytes 49160 | tf_op jit(solution)/shard_map/ppermute | solution.py:342
  26.4 3.4 %collective-permute-start.11 = (bf16[2,32,128]{2,1,0:T(8,128)(2,1)S(1)}, bf16[2,32,128]{2,1,0:T(8,128)(2,1)S(1)}, u32[]{:S(2)}, u32[]{:S(2)}) collective-permute-start(bf16[2,32,128]{2,1,0:T(8,128)(2,1)S(1)} %constant_dynamic-update-slice_fusion), channel_id=1, source_target_pairs={{0,3},{1,2},{2,1},{3,0},{4,7},{5,6},{6,5},{7,4},{8,11},{9,10},{10,... | collective-permute-start | bytes 49160 | tf_op jit(solution)/shard_map/ppermute | solution.py:342
  27.2 3.2 %collective-permute-start.9 = (bf16[2,32,128]{2,1,0:T(8,128)(2,1)S(1)}, bf16[2,32,128]{2,1,0:T(8,128)(2,1)S(1)}, u32[]{:S(2)}, u32[]{:S(2)}) collective-permute-start(bf16[2,32,128]{2,1,0:T(8,128)(2,1)S(1)} %constant_dynamic-update-slice_fusion), channel_id=1, source_target_pairs={{0,5},{1,4},{2,7},{3,6},{4,1},{5,0},{6,3},{7,2},{8,13},{9,12},{10,... | collective-permute-start | bytes 49160 | tf_op jit(solution)/shard_map/ppermute | solution.py:342
  28.5 1.2 %collective-permute-start.12 = (bf16[1,32,128]{2,1,0:T(8,128)(2,1)S(1)}, bf16[1,32,128]{2,1,0:T(8,128)(2,1)S(1)}, u32[]{:S(2)}, u32[]{:S(2)}) collective-permute-start(bf16[1,32,128]{2,1,0:T(8,128)(2,1)S(1)} %collective-permute-done.7), channel_id=1, source_target_pairs={{0,1},{1,0},{2,3},{3,2},{4,5},{5,4},{6,7},{7,6},{8,9},{9,8},{10,11... | collective-permute-start | bytes 24584 | tf_op jit(solution)/shard_map/ppermute | solution.py:337
  32.7 1.2 %collective-permute-start.13 = (f32[4,2048]{1,0:T(4,128)S(1)}, f32[4,2048]{1,0:T(4,128)S(1)}, u32[]{:S(2)}, u32[]{:S(2)}) collective-permute-start(f32[4,2048]{1,0:T(4,128)S(1)} %get-tuple-element.24), channel_id=1, source_target_pairs={{0,1},{1,0},{2,3},{3,2},{4,5},{5,4},{6,7},{7,6},{8,9},{9,8},{10,11... | collective-permute-start | bytes 98312 | tf_op jit(solution)/shard_map/ppermute | solution.py:337

commit v23 on v22

--- a/solution.py
+++ b/solution.py
@@ -13,7 +13,7 @@
 HEAD_SIZE = 128
 CHUNK = 256
 FIRST = 384
-PIECES = 4
+PIECES = 1
 FAN = 4
 MIB = 2**20
 

time: 34.7 us -> 34.6 us (level)
  no operation moved by 1% of the time
where the time goes in v23:
time: 34.6 us; the launch traced here: 34.4 us
  starting transfers between devices  13.9 us (40%)
  Pallas kernels  10.6 us (31%)
  waiting for transfers between devices  8.33 us (24%)
  between operations  0.81 us (2%)
  other arithmetic  0.71 us (2%)
    ppermute x8, starting transfers between devices, cross(): return lax.ppermute(block, ('gx', 'gy'), pairs)  12.4 us
    ppermute x8, waiting for transfers between devices, cross(): return lax.ppermute(block, ('gx', 'gy'), pairs)  6.15 us
    pallas_call x1, Pallas kernels, project(): pl.pallas_call(functools.partial(project_kernel, bits), out_shape=(piece,...  5.41 us
    pallas_call x1, Pallas kernels, output(): pl.pallas_call(functools.partial(output_kernel, bits, places, turned), ou...  2.28 us
    ppermute x6, waiting for transfers between devices, swap(): return lax.ppermute(block, axis, [(i, i ^ mask) for i in range(devices)])  2.19 us
    pallas_call x1, Pallas kernels, stage_rows(): pl.pallas_call(functools.partial(stage_kernel, rows), out_shape=jax.Shape...  2.01 us
    ppermute x6, starting transfers between devices, swap(): return lax.ppermute(block, axis, [(i, i ^ mask) for i in range(devices)])  1.53 us
    pallas_call x1, Pallas kernels, attend(): pl.pallas_call(functools.partial(attend_kernel, query_heads, kv_heads, le...  0.82 us
  transfers between devices with their start and end apart: 14, of which 8 were waited for; matrix products, arithmetic and copies ran while one was open for 0% of the time, Pallas kernels for 6%

profile of v23, /device:TPU:0, one launch (start us, length us, event | category | flops | bytes accessed | tf_op | source)
XLA Modules:
  0.0 34.4 jit_solution(7071508706702544212)
XLA Ops:
  0.0 0.5 %collective-permute-start = (bf16[4,2048]{1,0:T(4,128)(2,1)}, bf16[4,2048]{1,0:T(4,128)(2,1)S(1)}, u32[]{:S(2)}, u32[]{:S(2)}) collective-permute-start(bf16[4,2048]{1,0:T(4,128)(2,1)} %rows_ref.1), channel_id=1, source_target_pairs={{0,1},{1,0},{2,3},{3,2},{4,5},{5,4},{6,7},{7,6},{8,9},{9,8},{10,11... | collective-permute-start | bytes 49160 | tf_op jit(solution)/shard_map/ppermute | solution.py:337
  0.5 2.0 %stage.1.first = bf16[384,4096]{1,0:T(8,128)(2,1)S(1)} custom-call(bf16[2048,4096]{1,0:T(8,128)(2,1)} %wq_hbm.1), custom_call_target="tpu_custom_call" | custom-call | bytes 3145728 | tf_op jit(solution)/shard_map/stage/pallas_call | solution.py:57
  2.6 5.4 %project.1 = (f32[2,40,128]{2,1,0:T(8,128)S(1)}, f32[2,40,128]{2,1,0:T(8,128)S(1)}, f32[2,40,128]{2,1,0:T(8,128)S(1)}, f32[2,40,128]{2,1,0:T(8,128)S(1)}) custom-call(bf16[4,2048]{1,0:T(4,128)(2,1)S(1)} %copy-done.4, bf16[4,2048]{1,0:T(4,128)(2,1)S(1)} %collective-permute-done.other_ref, bf16[2048,4096]{1,0:T(8,128)(2,1)} %wq_hbm.1, ...), custom_call_target="tpu_custom_call" | custom-call | flops 150994944 | bytes 18874368 | tf_op jit(solution)/shard_map/project/pallas_call | solution.py:179
  8.0 3.6 %collective-permute-start.1 = (f32[2,40,128]{2,1,0:T(8,128)S(1)}, f32[2,40,128]{2,1,0:T(8,128)S(1)}, u32[]{:S(2)}, u32[]{:S(2)}) collective-permute-start(f32[2,40,128]{2,1,0:T(8,128)S(1)} %get-tuple-element.15.after_ref), channel_id=1, source_target_pairs={{0,7},{1,6},{2,5},{3,4},{4,3},{5,2},{6,1},{7,0},{8,15},{9,14},{10,... | collective-permute-start | bytes 122888 | tf_op jit(solution)/shard_map/ppermute | solution.py:342
  11.6 0.7 %collective-permute-start.2 = (f32[2,40,128]{2,1,0:T(8,128)S(1)}, f32[2,40,128]{2,1,0:T(8,128)S(1)}, u32[]{:S(2)}, u32[]{:S(2)}) collective-permute-start(f32[2,40,128]{2,1,0:T(8,128)S(1)} %get-tuple-element.16), channel_id=1, source_target_pairs={{0,3},{1,2},{2,1},{3,0},{4,7},{5,6},{6,5},{7,4},{8,11},{9,10},{10,... | collective-permute-start | bytes 122888 | tf_op jit(solution)/shard_map/ppermute | solution.py:342
  13.2 0.4 %collective-permute-done.1 = f32[2,40,128]{2,1,0:T(8,128)S(1)} collective-permute-done((f32[2,40,128]{2,1,0:T(8,128)S(1)}, f32[2,40,128]{2,1,0:T(8,128)S(1)}, u32[]{:S(2)}, u32[]{:S(2)}) %collective-permute-start.1) | collective-permute-done | bytes 40992 | tf_op jit(solution)/shard_map/ppermute | solution.py:342
  13.6 1.5 %collective-permute-done.2 = f32[2,40,128]{2,1,0:T(8,128)S(1)} collective-permute-done((f32[2,40,128]{2,1,0:T(8,128)S(1)}, f32[2,40,128]{2,1,0:T(8,128)S(1)}, u32[]{:S(2)}, u32[]{:S(2)}) %collective-permute-start.2) | collective-permute-done | bytes 40992 | tf_op jit(solution)/shard_map/ppermute | solution.py:342
  15.0 0.9 %collective-permute-done.3 = f32[2,40,128]{2,1,0:T(8,128)S(1)} collective-permute-done((f32[2,40,128]{2,1,0:T(8,128)S(1)}, f32[2,40,128]{2,1,0:T(8,128)S(1)}, u32[]{:S(2)}, u32[]{:S(2)}) %collective-permute-start.3) | collective-permute-done | bytes 40992 | tf_op jit(solution)/shard_map/ppermute | solution.py:342
  16.0 2.4 %collective-permute-start.5 = (f32[1,40,128]{2,1,0:T(8,128)S(1)}, f32[1,40,128]{2,1,0:T(8,128)S(1)}, u32[]{:S(2)}, u32[]{:S(2)}) collective-permute-start(f32[1,40,128]{2,1,0:T(8,128)S(1)} %get-tuple-element.22), channel_id=1, source_target_pairs={{0,9},{1,8},{2,11},{3,10},{4,13},{5,12},{6,15},{7,14},{8,1},{9,0},... | collective-permute-start | bytes 61448 | tf_op jit(solution)/shard_map/ppermute | solution.py:342
  18.3 0.4 %collective-permute-start.6 = (f32[1,40,128]{2,1,0:T(8,128)S(1)}, f32[1,40,128]{2,1,0:T(8,128)S(1)}, u32[]{:S(2)}, u32[]{:S(2)}) collective-permute-start(f32[1,40,128]{2,1,0:T(8,128)S(1)} %get-tuple-element.25), channel_id=1, source_target_pairs={{0,1},{1,0},{2,3},{3,2},{4,5},{5,4},{6,7},{7,6},{8,9},{9,8},{10,11... | collective-permute-start | bytes 61448 | tf_op jit(solution)/shard_map/ppermute | solution.py:337
  18.7 1.4 %collective-permute-done.5.refs_0_ = f32[1,40,128]{2,1,0:T(8,128)S(1)} collective-permute-done((f32[1,40,128]{2,1,0:T(8,128)S(1)}, f32[1,40,128]{2,1,0:T(8,128)S(1)}, u32[]{:S(2)}, u32[]{:S(2)}) %collective-permute-start.5) | collective-permute-done | bytes 20512 | tf_op jit(solution)/shard_map/ppermute | solution.py:342
  20.2 0.8 %attend.1.refs_4_ = bf16[1,32,128]{2,1,0:T(8,128)(2,1)S(1)} custom-call(bf16[4096,2048]{1,0:T(8,128)(2,1)} %refs_5_.1, f32[8,128]{1,0:T(8,128)S(1)} %get-tuple-element.20.turn_ref, f32[1,2048]{1,0:T(1,128)S(1)} %get-tuple-element.21.live_ref, bf16[1,2,2048,128]{3,2,1,0:T(8,128)(2,1)S(1)} %copy-done, bf16[1,2,2048,128]{3,2,1,0:T(8,128)(2,1)S(1)} %copy-done.1, ...), custom_call_target="tpu_custom_call" | custom-call | flops 33554432 | bytes 2097152 | tf_op jit(solution)/shard_map/attend/pallas_call | solution.py:266
  21.0 2.4 %collective-permute-start.7 = (bf16[1,32,128]{2,1,0:T(8,128)(2,1)S(1)}, bf16[1,32,128]{2,1,0:T(8,128)(2,1)S(1)}, u32[]{:S(2)}, u32[]{:S(2)}) collective-permute-start(bf16[1,32,128]{2,1,0:T(8,128)(2,1)S(1)} %attend.1.refs_4_), channel_id=1, source_target_pairs={{0,9},{1,8},{2,11},{3,10},{4,13},{5,12},{6,15},{7,14},{8,1},{9,0},... | collective-permute-start | bytes 24584 | tf_op jit(solution)/shard_map/ppermute | solution.py:342
  23.4 0.4 %collective-permute-start.8 = (bf16[1,32,128]{2,1,0:T(8,128)(2,1)S(1)}, bf16[1,32,128]{2,1,0:T(8,128)(2,1)S(1)}, u32[]{:S(2)}, u32[]{:S(2)}) collective-permute-start(bf16[1,32,128]{2,1,0:T(8,128)(2,1)S(1)} %attend.1.refs_4_), channel_id=1, source_target_pairs={{0,1},{1,0},{2,3},{3,2},{4,5},{5,4},{6,7},{7,6},{8,9},{9,8},{10,11... | collective-permute-start | bytes 24584 | tf_op jit(solution)/shard_map/ppermute | solution.py:337
  23.8 1.3 %collective-permute-done.7 = bf16[1,32,128]{2,1,0:T(8,128)(2,1)S(1)} collective-permute-done((bf16[1,32,128]{2,1,0:T(8,128)(2,1)S(1)}, bf16[1,32,128]{2,1,0:T(8,128)(2,1)S(1)}, u32[]{:S(2)}, u32[]{:S(2)}) %collective-permute-start.7) | collective-permute-done | bytes 8224 | tf_op jit(solution)/shard_map/ppermute | solution.py:342
  25.1 1.2 %collective-permute-start.10 = (bf16[2,32,128]{2,1,0:T(8,128)(2,1)S(1)}, bf16[2,32,128]{2,1,0:T(8,128)(2,1)S(1)}, u32[]{:S(2)}, u32[]{:S(2)}) collective-permute-start(bf16[2,32,128]{2,1,0:T(8,128)(2,1)S(1)} %constant_dynamic-update-slice_fusion), channel_id=1, source_target_pairs={{0,7},{1,6},{2,5},{3,4},{4,3},{5,2},{6,1},{7,0},{8,15},{9,14},{10,... | collective-permute-start | bytes 49160 | tf_op jit(solution)/shard_map/ppermute | solution.py:342
  26.3 0.9 %collective-permute-start.11 = (bf16[2,32,128]{2,1,0:T(8,128)(2,1)S(1)}, bf16[2,32,128]{2,1,0:T(8,128)(2,1)S(1)}, u32[]{:S(2)}, u32[]{:S(2)}) collective-permute-start(bf16[2,32,128]{2,1,0:T(8,128)(2,1)S(1)} %constant_dynamic-update-slice_fusion), channel_id=1, source_target_pairs={{0,3},{1,2},{2,1},{3,0},{4,7},{5,6},{6,5},{7,4},{8,11},{9,10},{10,... | collective-permute-start | bytes 49160 | tf_op jit(solution)/shard_map/ppermute | solution.py:342
  27.1 1.3 %collective-permute-start.9 = (bf16[2,32,128]{2,1,0:T(8,128)(2,1)S(1)}, bf16[2,32,128]{2,1,0:T(8,128)(2,1)S(1)}, u32[]{:S(2)}, u32[]{:S(2)}) collective-permute-start(bf16[2,32,128]{2,1,0:T(8,128)(2,1)S(1)} %constant_dynamic-update-slice_fusion), channel_id=1, source_target_pairs={{0,5},{1,4},{2,7},{3,6},{4,1},{5,0},{6,3},{7,2},{8,13},{9,12},{10,... | collective-permute-start | bytes 49160 | tf_op jit(solution)/shard_map/ppermute | solution.py:342
  28.5 1.1 %collective-permute-done.12.refs_3_ = bf16[1,32,128]{2,1,0:T(8,128)(2,1)S(1)} collective-permute-done((bf16[1,32,128]{2,1,0:T(8,128)(2,1)S(1)}, bf16[1,32,128]{2,1,0:T(8,128)(2,1)S(1)}, u32[]{:S(2)}, u32[]{:S(2)}) %collective-permute-start.12) | collective-permute-done | bytes 8224 | tf_op jit(solution)/shard_map/ppermute | solution.py:337
  29.6 0.7 %collective-permute-done.9.refs_0_ = bf16[2,32,128]{2,1,0:T(8,128)(2,1)S(1)} collective-permute-done((bf16[2,32,128]{2,1,0:T(8,128)(2,1)S(1)}, bf16[2,32,128]{2,1,0:T(8,128)(2,1)S(1)}, u32[]{:S(2)}, u32[]{:S(2)}) %collective-permute-start.9) | collective-permute-done | bytes 16416 | tf_op jit(solution)/shard_map/ppermute | solution.py:342
  30.3 2.3 %output.1 = (f32[4,2048]{1,0:T(4,128)S(1)}, f32[4,2048]{1,0:T(4,128)S(1)}) custom-call(bf16[2,32,128]{2,1,0:T(8,128)(2,1)S(1)} %collective-permute-done.9.refs_0_, bf16[2,32,128]{2,1,0:T(8,128)(2,1)S(1)} %collective-permute-done.10.refs_1_, bf16[2,32,128]{2,1,0:T(8,128)(2,1)S(1)} %collective-permute-done.11.refs_2_, ...), custom_call_target="tpu_custom_call" | custom-call | flops 134217728 | bytes 16777216 | tf_op jit(solution)/shard_map/output/pallas_call | solution.py:319
  32.6 0.2 collective-permute-start.13
  32.8 1.0 %collective-permute-done.13 = f32[4,2048]{1,0:T(4,128)S(1)} collective-permute-done((f32[4,2048]{1,0:T(4,128)S(1)}, f32[4,2048]{1,0:T(4,128)S(1)}, u32[]{:S(2)}, u32[]{:S(2)}) %collective-permute-start.13) | collective-permute-done | bytes 32800 | tf_op jit(solution)/shard_map/ppermute | solution.py:337
  33.8 0.6 %add_convert_fusion = bf16[4,2048]{1,0:T(4,128)(2,1)} fusion(f32[4,2048]{1,0:T(4,128)S(1)} %get-tuple-element.23, f32[4,2048]{1,0:T(4,128)S(1)} %collective-permute-done.13), kind=kLoop, calls=%fused_computation | loop fusion | flops 16384 | bytes 81920 | tf_op jit(solution)/shard_map/convert_element_type | solution.py:405
  (34 shorter events, 0.4 us)
Async XLA Ops:
  0.0 2.6 %copy-start.4 = (bf16[4,2048]{1,0:T(4,128)(2,1)S(1)}, bf16[4,2048]{1,0:T(4,128)(2,1)}, u32[]{:S(2)}) copy-start(bf16[4,2048]{1,0:T(4,128)(2,1)} %rows_ref.1) | copy-start | bytes 49156
  0.0 2.6 %copy-start.2 = (bf16[2048,256]{1,0:T(8,128)(2,1)S(1)}, bf16[2048,256]{1,0:T(8,128)(2,1)}, u32[]{:S(2)}) copy-start(bf16[2048,256]{1,0:T(8,128)(2,1)} %wk.1) | copy-start | bytes 3145732
  0.0 2.6 %copy-start.3 = (bf16[2048,256]{1,0:T(8,128)(2,1)S(1)}, bf16[2048,256]{1,0:T(8,128)(2,1)}, u32[]{:S(2)}) copy-start(bf16[2048,256]{1,0:T(8,128)(2,1)} %wv.1) | copy-start | bytes 3145732
  0.0 2.6 %collective-permute-start = (bf16[4,2048]{1,0:T(4,128)(2,1)}, bf16[4,2048]{1,0:T(4,128)(2,1)S(1)}, u32[]{:S(2)}, u32[]{:S(2)}) collective-permute-start(bf16[4,2048]{1,0:T(4,128)(2,1)} %rows_ref.1), channel_id=1, source_target_pairs={{0,1},{1,0},{2,3},{3,2},{4,5},{5,4},{6,7},{7,6},{8,9},{9,8},{10,11... | collective-permute-start | bytes 49160 | tf_op jit(solution)/shard_map/ppermute | solution.py:337
  2.6 17.6 %copy-start = (bf16[1,2,2048,128]{3,2,1,0:T(8,128)(2,1)S(1)}, bf16[1,2,2048,128]{3,2,1,0:T(8,128)(2,1)}, u32[]{:S(2)}) copy-start(bf16[1,2,2048,128]{3,2,1,0:T(8,128)(2,1)} %k_ref.1) | copy-start | bytes 3145732
  2.6 17.6 %copy-start.1 = (bf16[1,2,2048,128]{3,2,1,0:T(8,128)(2,1)S(1)}, bf16[1,2,2048,128]{3,2,1,0:T(8,128)(2,1)}, u32[]{:S(2)}) copy-start(bf16[1,2,2048,128]{3,2,1,0:T(8,128)(2,1)} %v_ref.1) | copy-start | bytes 3145732
  8.0 5.5 %collective-permute-start.1 = (f32[2,40,128]{2,1,0:T(8,128)S(1)}, f32[2,40,128]{2,1,0:T(8,128)S(1)}, u32[]{:S(2)}, u32[]{:S(2)}) collective-permute-start(f32[2,40,128]{2,1,0:T(8,128)S(1)} %get-tuple-element.15.after_ref), channel_id=1, source_target_pairs={{0,7},{1,6},{2,5},{3,4},{4,3},{5,2},{6,1},{7,0},{8,15},{9,14},{10,... | collective-permute-start | bytes 122888 | tf_op jit(solution)/shard_map/ppermute | solution.py:342
  11.6 3.4 %collective-permute-start.2 = (f32[2,40,128]{2,1,0:T(8,128)S(1)}, f32[2,40,128]{2,1,0:T(8,128)S(1)}, u32[]{:S(2)}, u32[]{:S(2)}) collective-permute-start(f32[2,40,128]{2,1,0:T(8,128)S(1)} %get-tuple-element.16), channel_id=1, source_target_pairs={{0,3},{1,2},{2,1},{3,0},{4,7},{5,6},{6,5},{7,4},{8,11},{9,10},{10,... | collective-permute-start | bytes 122888 | tf_op jit(solution)/shard_map/ppermute | solution.py:342
  12.3 3.7 %collective-permute-start.3 = (f32[2,40,128]{2,1,0:T(8,128)S(1)}, f32[2,40,128]{2,1,0:T(8,128)S(1)}, u32[]{:S(2)}, u32[]{:S(2)}) collective-permute-start(f32[2,40,128]{2,1,0:T(8,128)S(1)} %get-tuple-element.17), channel_id=1, source_target_pairs={{0,5},{1,4},{2,7},{3,6},{4,1},{5,0},{6,3},{7,2},{8,13},{9,12},{10,... | collective-permute-start | bytes 122888 | tf_op jit(solution)/shard_map/ppermute | solution.py:342
  12.4 3.6 %collective-permute-start.4 = (f32[2,40,128]{2,1,0:T(8,128)S(1)}, f32[2,40,128]{2,1,0:T(8,128)S(1)}, u32[]{:S(2)}, u32[]{:S(2)}) collective-permute-start(f32[2,40,128]{2,1,0:T(8,128)S(1)} %get-tuple-element.18), channel_id=1, source_target_pairs={{0,1},{1,0},{2,3},{3,2},{4,5},{5,4},{6,7},{7,6},{8,9},{9,8},{10,11... | collective-permute-start | bytes 122888 | tf_op jit(solution)/shard_map/ppermute | solution.py:337
  13.1 17.2 %slice-start = ((s8[16777216]{0:T(1024)(128)(4,1)}), s8[4194304]{0:T(1024)(128)(4,1)S(1)}, s32[]{:S(2)}) async-start(s8[16777216]{0:T(1024)(128)(4,1)} %bitcast.2), calls=%async_computation | async-start | bytes 8388608
  13.1 17.2 %slice-start.1 = ((s8[16777216]{0:T(1024)(128)(4,1)}), s8[4194304]{0:T(1024)(128)(4,1)S(1)}, s32[]{:S(2)}) async-start(s8[16777216]{0:T(1024)(128)(4,1)} %bitcast.2), calls=%async_computation.1 | async-start | bytes 8388608
  16.0 4.2 %collective-permute-start.5 = (f32[1,40,128]{2,1,0:T(8,128)S(1)}, f32[1,40,128]{2,1,0:T(8,128)S(1)}, u32[]{:S(2)}, u32[]{:S(2)}) collective-permute-start(f32[1,40,128]{2,1,0:T(8,128)S(1)} %get-tuple-element.22), channel_id=1, source_target_pairs={{0,9},{1,8},{2,11},{3,10},{4,13},{5,12},{6,15},{7,14},{8,1},{9,0},... | collective-permute-start | bytes 61448 | tf_op jit(solution)/shard_map/ppermute | solution.py:342
  18.3 1.8 %collective-permute-start.6 = (f32[1,40,128]{2,1,0:T(8,128)S(1)}, f32[1,40,128]{2,1,0:T(8,128)S(1)}, u32[]{:S(2)}, u32[]{:S(2)}) collective-permute-start(f32[1,40,128]{2,1,0:T(8,128)S(1)} %get-tuple-element.25), channel_id=1, source_target_pairs={{0,1},{1,0},{2,3},{3,2},{4,5},{5,4},{6,7},{7,6},{8,9},{9,8},{10,11... | collective-permute-start | bytes 61448 | tf_op jit(solution)/shard_map/ppermute | solution.py:337
  20.2 10.1 %slice-start.2 = ((s8[16777216]{0:T(1024)(128)(4,1)}), s8[4194304]{0:T(1024)(128)(4,1)S(1)}, s32[]{:S(2)}) async-start(s8[16777216]{0:T(1024)(128)(4,1)} %bitcast.2), calls=%async_computation.2 | async-start | bytes 8388608
  20.2 10.1 %slice-start.3 = ((s8[16777216]{0:T(1024)(128)(4,1)}), s8[4194304]{0:T(1024)(128)(4,1)S(1)}, s32[]{:S(2)}) async-start(s8[16777216]{0:T(1024)(128)(4,1)} %bitcast.2), calls=%async_computation.3 | async-start | bytes 8388608
  21.0 4.0 %collective-permute-start.7 = (bf16[1,32,128]{2,1,0:T(8,128)(2,1)S(1)}, bf16[1,32,128]{2,1,0:T(8,128)(2,1)S(1)}, u32[]{:S(2)}, u32[]{:S(2)}) collective-permute-start(bf16[1,32,128]{2,1,0:T(8,128)(2,1)S(1)} %attend.1.refs_4_), channel_id=1, source_target_pairs={{0,9},{1,8},{2,11},{3,10},{4,13},{5,12},{6,15},{7,14},{8,1},{9,0},... | collective-permute-start | bytes 24584 | tf_op jit(solution)/shard_map/ppermute | solution.py:342
  23.4 1.7 %collective-permute-start.8 = (bf16[1,32,128]{2,1,0:T(8,128)(2,1)S(1)}, bf16[1,32,128]{2,1,0:T(8,128)(2,1)S(1)}, u32[]{:S(2)}, u32[]{:S(2)}) collective-permute-start(bf16[1,32,128]{2,1,0:T(8,128)(2,1)S(1)} %attend.1.refs_4_), channel_id=1, source_target_pairs={{0,1},{1,0},{2,3},{3,2},{4,5},{5,4},{6,7},{7,6},{8,9},{9,8},{10,11... | collective-permute-start | bytes 24584 | tf_op jit(solution)/shard_map/ppermute | solution.py:337
  25.1 4.5 %collective-permute-start.10 = (bf16[2,32,128]{2,1,0:T(8,128)(2,1)S(1)}, bf16[2,32,128]{2,1,0:T(8,128)(2,1)S(1)}, u32[]{:S(2)}, u32[]{:S(2)}) collective-permute-start(bf16[2,32,128]{2,1,0:T(8,128)(2,1)S(1)} %constant_dynamic-update-slice_fusion), channel_id=1, source_target_pairs={{0,7},{1,6},{2,5},{3,4},{4,3},{5,2},{6,1},{7,0},{8,15},{9,14},{10,... | collective-permute-start | bytes 49160 | tf_op jit(solution)/shard_map/ppermute | solution.py:342
  26.3 3.4 %collective-permute-start.11 = (bf16[2,32,128]{2,1,0:T(8,128)(2,1)S(1)}, bf16[2,32,128]{2,1,0:T(8,128)(2,1)S(1)}, u32[]{:S(2)}, u32[]{:S(2)}) collective-permute-start(bf16[2,32,128]{2,1,0:T(8,128)(2,1)S(1)} %constant_dynamic-update-slice_fusion), channel_id=1, source_target_pairs={{0,3},{1,2},{2,1},{3,0},{4,7},{5,6},{6,5},{7,4},{8,11},{9,10},{10,... | collective-permute-start | bytes 49160 | tf_op jit(solution)/shard_map/ppermute | solution.py:342
  27.1 3.2 %collective-permute-start.9 = (bf16[2,32,128]{2,1,0:T(8,128)(2,1)S(1)}, bf16[2,32,128]{2,1,0:T(8,128)(2,1)S(1)}, u32[]{:S(2)}, u32[]{:S(2)}) collective-permute-start(bf16[2,32,128]{2,1,0:T(8,128)(2,1)S(1)} %constant_dynamic-update-slice_fusion), channel_id=1, source_target_pairs={{0,5},{1,4},{2,7},{3,6},{4,1},{5,0},{6,3},{7,2},{8,13},{9,12},{10,... | collective-permute-start | bytes 49160 | tf_op jit(solution)/shard_map/ppermute | solution.py:342
  28.4 1.2 %collective-permute-start.12 = (bf16[1,32,128]{2,1,0:T(8,128)(2,1)S(1)}, bf16[1,32,128]{2,1,0:T(8,128)(2,1)S(1)}, u32[]{:S(2)}, u32[]{:S(2)}) collective-permute-start(bf16[1,32,128]{2,1,0:T(8,128)(2,1)S(1)} %collective-permute-done.7), channel_id=1, source_target_pairs={{0,1},{1,0},{2,3},{3,2},{4,5},{5,4},{6,7},{7,6},{8,9},{9,8},{10,11... | collective-permute-start | bytes 24584 | tf_op jit(solution)/shard_map/ppermute | solution.py:337
  32.6 1.2 %collective-permute-start.13 = (f32[4,2048]{1,0:T(4,128)S(1)}, f32[4,2048]{1,0:T(4,128)S(1)}, u32[]{:S(2)}, u32[]{:S(2)}) collective-permute-start(f32[4,2048]{1,0:T(4,128)S(1)} %get-tuple-element.24), channel_id=1, source_target_pairs={{0,1},{1,0},{2,3},{3,2},{4,5},{5,4},{6,7},{7,6},{8,9},{9,8},{10,11... | collective-permute-start | bytes 98312 | tf_op jit(solution)/shard_map/ppermute | solution.py:337

commit v24 on v23

--- a/solution.py
+++ b/solution.py
@@ -293,13 +293,7 @@
         left[:, head * HEAD_SIZE : (head + 1) * HEAD_SIZE] = flat[
             pl.ds(head, slots, stride=heads), :
         ].astype(jnp.bfloat16)
-    total = None
-    depth = w_ref.shape[0]
-    chunk = min(2 * CHUNK, depth)
-    for at in range(0, depth, chunk):
-        part = slice(at, at + chunk)
-        term = jnp.dot(left[:, part], w_ref[part, :], preferred_element_type=jnp.float32)
-        total = term if total is None else total + term
+    total = jnp.dot(left[...], w_ref[...], preferred_element_type=jnp.float32)
     half = slots // 2
     gy = lax.axis_index("gy")
     lower, upper = total[:half], total[half:]

time: 34.6 us -> 34.6 us (level)
  no operation moved by 1% of the time
where the time goes in v24:
time: 34.6 us; the launch traced here: 34.4 us
  starting transfers between devices  13.9 us (40%)
  Pallas kernels  10.6 us (31%)
  waiting for transfers between devices  8.33 us (24%)
  between operations  0.81 us (2%)
  other arithmetic  0.71 us (2%)
    ppermute x8, starting transfers between devices, cross(): return lax.ppermute(block, ('gx', 'gy'), pairs)  12.4 us
    ppermute x8, waiting for transfers between devices, cross(): return lax.ppermute(block, ('gx', 'gy'), pairs)  6.15 us
    pallas_call x1, Pallas kernels, project(): pl.pallas_call(functools.partial(project_kernel, bits), out_shape=(piece,...  5.41 us
    pallas_call x1, Pallas kernels, output(): pl.pallas_call(functools.partial(output_kernel, bits, places, turned), ou...  2.28 us
    ppermute x6, waiting for transfers between devices, swap(): return lax.ppermute(block, axis, [(i, i ^ mask) for i in range(devices)])  2.19 us
    pallas_call x1, Pallas kernels, stage_rows(): pl.pallas_call(functools.partial(stage_kernel, rows), out_shape=jax.Shape...  2.01 us
    ppermute x6, starting transfers between devices, swap(): return lax.ppermute(block, axis, [(i, i ^ mask) for i in range(devices)])  1.53 us
    pallas_call x1, Pallas kernels, attend(): pl.pallas_call(functools.partial(attend_kernel, query_heads, kv_heads, le...  0.82 us
  transfers between devices with their start and end apart: 14, of which 8 were waited for; matrix products, arithmetic and copies ran while one was open for 0% of the time, Pallas kernels for 6%

profile of v24, /device:TPU:0, one launch (start us, length us, event | category | flops | bytes accessed | tf_op | source)
XLA Modules:
  0.0 34.4 jit_solution(13087963750496173107)
XLA Ops:
  0.0 0.5 %collective-permute-start = (bf16[4,2048]{1,0:T(4,128)(2,1)}, bf16[4,2048]{1,0:T(4,128)(2,1)S(1)}, u32[]{:S(2)}, u32[]{:S(2)}) collective-permute-start(bf16[4,2048]{1,0:T(4,128)(2,1)} %rows_ref.1), channel_id=1, source_target_pairs={{0,1},{1,0},{2,3},{3,2},{4,5},{5,4},{6,7},{7,6},{8,9},{9,8},{10,11... | collective-permute-start | bytes 49160 | tf_op jit(solution)/shard_map/ppermute | solution.py:331
  0.5 2.0 %stage.1.first = bf16[384,4096]{1,0:T(8,128)(2,1)S(1)} custom-call(bf16[2048,4096]{1,0:T(8,128)(2,1)} %wq_hbm.1), custom_call_target="tpu_custom_call" | custom-call | bytes 3145728 | tf_op jit(solution)/shard_map/stage/pallas_call | solution.py:57
  2.6 5.4 %project.1 = (f32[2,40,128]{2,1,0:T(8,128)S(1)}, f32[2,40,128]{2,1,0:T(8,128)S(1)}, f32[2,40,128]{2,1,0:T(8,128)S(1)}, f32[2,40,128]{2,1,0:T(8,128)S(1)}) custom-call(bf16[4,2048]{1,0:T(4,128)(2,1)S(1)} %copy-done.4, bf16[4,2048]{1,0:T(4,128)(2,1)S(1)} %collective-permute-done.other_ref, bf16[2048,4096]{1,0:T(8,128)(2,1)} %wq_hbm.1, ...), custom_call_target="tpu_custom_call" | custom-call | flops 150994944 | bytes 18874368 | tf_op jit(solution)/shard_map/project/pallas_call | solution.py:179
  8.0 3.6 %collective-permute-start.1 = (f32[2,40,128]{2,1,0:T(8,128)S(1)}, f32[2,40,128]{2,1,0:T(8,128)S(1)}, u32[]{:S(2)}, u32[]{:S(2)}) collective-permute-start(f32[2,40,128]{2,1,0:T(8,128)S(1)} %get-tuple-element.15.after_ref), channel_id=1, source_target_pairs={{0,7},{1,6},{2,5},{3,4},{4,3},{5,2},{6,1},{7,0},{8,15},{9,14},{10,... | collective-permute-start | bytes 122888 | tf_op jit(solution)/shard_map/ppermute | solution.py:336
  11.6 0.7 %collective-permute-start.2 = (f32[2,40,128]{2,1,0:T(8,128)S(1)}, f32[2,40,128]{2,1,0:T(8,128)S(1)}, u32[]{:S(2)}, u32[]{:S(2)}) collective-permute-start(f32[2,40,128]{2,1,0:T(8,128)S(1)} %get-tuple-element.16), channel_id=1, source_target_pairs={{0,3},{1,2},{2,1},{3,0},{4,7},{5,6},{6,5},{7,4},{8,11},{9,10},{10,... | collective-permute-start | bytes 122888 | tf_op jit(solution)/shard_map/ppermute | solution.py:336
  13.2 0.4 %collective-permute-done.1 = f32[2,40,128]{2,1,0:T(8,128)S(1)} collective-permute-done((f32[2,40,128]{2,1,0:T(8,128)S(1)}, f32[2,40,128]{2,1,0:T(8,128)S(1)}, u32[]{:S(2)}, u32[]{:S(2)}) %collective-permute-start.1) | collective-permute-done | bytes 40992 | tf_op jit(solution)/shard_map/ppermute | solution.py:336
  13.6 1.5 %collective-permute-done.2 = f32[2,40,128]{2,1,0:T(8,128)S(1)} collective-permute-done((f32[2,40,128]{2,1,0:T(8,128)S(1)}, f32[2,40,128]{2,1,0:T(8,128)S(1)}, u32[]{:S(2)}, u32[]{:S(2)}) %collective-permute-start.2) | collective-permute-done | bytes 40992 | tf_op jit(solution)/shard_map/ppermute | solution.py:336
  15.0 0.9 %collective-permute-done.3 = f32[2,40,128]{2,1,0:T(8,128)S(1)} collective-permute-done((f32[2,40,128]{2,1,0:T(8,128)S(1)}, f32[2,40,128]{2,1,0:T(8,128)S(1)}, u32[]{:S(2)}, u32[]{:S(2)}) %collective-permute-start.3) | collective-permute-done | bytes 40992 | tf_op jit(solution)/shard_map/ppermute | solution.py:336
  16.0 2.4 %collective-permute-start.5 = (f32[1,40,128]{2,1,0:T(8,128)S(1)}, f32[1,40,128]{2,1,0:T(8,128)S(1)}, u32[]{:S(2)}, u32[]{:S(2)}) collective-permute-start(f32[1,40,128]{2,1,0:T(8,128)S(1)} %get-tuple-element.22), channel_id=1, source_target_pairs={{0,9},{1,8},{2,11},{3,10},{4,13},{5,12},{6,15},{7,14},{8,1},{9,0},... | collective-permute-start | bytes 61448 | tf_op jit(solution)/shard_map/ppermute | solution.py:336
  18.3 0.4 %collective-permute-start.6 = (f32[1,40,128]{2,1,0:T(8,128)S(1)}, f32[1,40,128]{2,1,0:T(8,128)S(1)}, u32[]{:S(2)}, u32[]{:S(2)}) collective-permute-start(f32[1,40,128]{2,1,0:T(8,128)S(1)} %get-tuple-element.25), channel_id=1, source_target_pairs={{0,1},{1,0},{2,3},{3,2},{4,5},{5,4},{6,7},{7,6},{8,9},{9,8},{10,11... | collective-permute-start | bytes 61448 | tf_op jit(solution)/shard_map/ppermute | solution.py:331
  18.7 1.4 %collective-permute-done.5.refs_0_ = f32[1,40,128]{2,1,0:T(8,128)S(1)} collective-permute-done((f32[1,40,128]{2,1,0:T(8,128)S(1)}, f32[1,40,128]{2,1,0:T(8,128)S(1)}, u32[]{:S(2)}, u32[]{:S(2)}) %collective-permute-start.5) | collective-permute-done | bytes 20512 | tf_op jit(solution)/shard_map/ppermute | solution.py:336
  20.2 0.8 %attend.1.refs_4_ = bf16[1,32,128]{2,1,0:T(8,128)(2,1)S(1)} custom-call(bf16[4096,2048]{1,0:T(8,128)(2,1)} %refs_5_.1, f32[8,128]{1,0:T(8,128)S(1)} %get-tuple-element.20.turn_ref, f32[1,2048]{1,0:T(1,128)S(1)} %get-tuple-element.21.live_ref, bf16[1,2,2048,128]{3,2,1,0:T(8,128)(2,1)S(1)} %copy-done, bf16[1,2,2048,128]{3,2,1,0:T(8,128)(2,1)S(1)} %copy-done.1, ...), custom_call_target="tpu_custom_call" | custom-call | flops 33554432 | bytes 2097152 | tf_op jit(solution)/shard_map/attend/pallas_call | solution.py:266
  21.0 2.4 %collective-permute-start.7 = (bf16[1,32,128]{2,1,0:T(8,128)(2,1)S(1)}, bf16[1,32,128]{2,1,0:T(8,128)(2,1)S(1)}, u32[]{:S(2)}, u32[]{:S(2)}) collective-permute-start(bf16[1,32,128]{2,1,0:T(8,128)(2,1)S(1)} %attend.1.refs_4_), channel_id=1, source_target_pairs={{0,9},{1,8},{2,11},{3,10},{4,13},{5,12},{6,15},{7,14},{8,1},{9,0},... | collective-permute-start | bytes 24584 | tf_op jit(solution)/shard_map/ppermute | solution.py:336
  23.4 0.4 %collective-permute-start.8 = (bf16[1,32,128]{2,1,0:T(8,128)(2,1)S(1)}, bf16[1,32,128]{2,1,0:T(8,128)(2,1)S(1)}, u32[]{:S(2)}, u32[]{:S(2)}) collective-permute-start(bf16[1,32,128]{2,1,0:T(8,128)(2,1)S(1)} %attend.1.refs_4_), channel_id=1, source_target_pairs={{0,1},{1,0},{2,3},{3,2},{4,5},{5,4},{6,7},{7,6},{8,9},{9,8},{10,11... | collective-permute-start | bytes 24584 | tf_op jit(solution)/shard_map/ppermute | solution.py:331
  23.8 1.3 %collective-permute-done.7 = bf16[1,32,128]{2,1,0:T(8,128)(2,1)S(1)} collective-permute-done((bf16[1,32,128]{2,1,0:T(8,128)(2,1)S(1)}, bf16[1,32,128]{2,1,0:T(8,128)(2,1)S(1)}, u32[]{:S(2)}, u32[]{:S(2)}) %collective-permute-start.7) | collective-permute-done | bytes 8224 | tf_op jit(solution)/shard_map/ppermute | solution.py:336
  25.1 1.2 %collective-permute-start.10 = (bf16[2,32,128]{2,1,0:T(8,128)(2,1)S(1)}, bf16[2,32,128]{2,1,0:T(8,128)(2,1)S(1)}, u32[]{:S(2)}, u32[]{:S(2)}) collective-permute-start(bf16[2,32,128]{2,1,0:T(8,128)(2,1)S(1)} %constant_dynamic-update-slice_fusion), channel_id=1, source_target_pairs={{0,7},{1,6},{2,5},{3,4},{4,3},{5,2},{6,1},{7,0},{8,15},{9,14},{10,... | collective-permute-start | bytes 49160 | tf_op jit(solution)/shard_map/ppermute | solution.py:336
  26.3 0.9 %collective-permute-start.11 = (bf16[2,32,128]{2,1,0:T(8,128)(2,1)S(1)}, bf16[2,32,128]{2,1,0:T(8,128)(2,1)S(1)}, u32[]{:S(2)}, u32[]{:S(2)}) collective-permute-start(bf16[2,32,128]{2,1,0:T(8,128)(2,1)S(1)} %constant_dynamic-update-slice_fusion), channel_id=1, source_target_pairs={{0,3},{1,2},{2,1},{3,0},{4,7},{5,6},{6,5},{7,4},{8,11},{9,10},{10,... | collective-permute-start | bytes 49160 | tf_op jit(solution)/shard_map/ppermute | solution.py:336
  27.1 1.3 %collective-permute-start.9 = (bf16[2,32,128]{2,1,0:T(8,128)(2,1)S(1)}, bf16[2,32,128]{2,1,0:T(8,128)(2,1)S(1)}, u32[]{:S(2)}, u32[]{:S(2)}) collective-permute-start(bf16[2,32,128]{2,1,0:T(8,128)(2,1)S(1)} %constant_dynamic-update-slice_fusion), channel_id=1, source_target_pairs={{0,5},{1,4},{2,7},{3,6},{4,1},{5,0},{6,3},{7,2},{8,13},{9,12},{10,... | collective-permute-start | bytes 49160 | tf_op jit(solution)/shard_map/ppermute | solution.py:336
  28.5 1.1 %collective-permute-done.12.refs_3_ = bf16[1,32,128]{2,1,0:T(8,128)(2,1)S(1)} collective-permute-done((bf16[1,32,128]{2,1,0:T(8,128)(2,1)S(1)}, bf16[1,32,128]{2,1,0:T(8,128)(2,1)S(1)}, u32[]{:S(2)}, u32[]{:S(2)}) %collective-permute-start.12) | collective-permute-done | bytes 8224 | tf_op jit(solution)/shard_map/ppermute | solution.py:331
  29.6 0.7 %collective-permute-done.9.refs_0_ = bf16[2,32,128]{2,1,0:T(8,128)(2,1)S(1)} collective-permute-done((bf16[2,32,128]{2,1,0:T(8,128)(2,1)S(1)}, bf16[2,32,128]{2,1,0:T(8,128)(2,1)S(1)}, u32[]{:S(2)}, u32[]{:S(2)}) %collective-permute-start.9) | collective-permute-done | bytes 16416 | tf_op jit(solution)/shard_map/ppermute | solution.py:336
  30.3 2.3 %output.1 = (f32[4,2048]{1,0:T(4,128)S(1)}, f32[4,2048]{1,0:T(4,128)S(1)}) custom-call(bf16[2,32,128]{2,1,0:T(8,128)(2,1)S(1)} %collective-permute-done.9.refs_0_, bf16[2,32,128]{2,1,0:T(8,128)(2,1)S(1)} %collective-permute-done.10.refs_1_, bf16[2,32,128]{2,1,0:T(8,128)(2,1)S(1)} %collective-permute-done.11.refs_2_, ...), custom_call_target="tpu_custom_call" | custom-call | flops 134217728 | bytes 16777216 | tf_op jit(solution)/shard_map/output/pallas_call | solution.py:313
  32.6 0.2 collective-permute-start.13
  32.8 1.0 %collective-permute-done.13 = f32[4,2048]{1,0:T(4,128)S(1)} collective-permute-done((f32[4,2048]{1,0:T(4,128)S(1)}, f32[4,2048]{1,0:T(4,128)S(1)}, u32[]{:S(2)}, u32[]{:S(2)}) %collective-permute-start.13) | collective-permute-done | bytes 32800 | tf_op jit(solution)/shard_map/ppermute | solution.py:331
  33.8 0.6 %add_convert_fusion = bf16[4,2048]{1,0:T(4,128)(2,1)} fusion(f32[4,2048]{1,0:T(4,128)S(1)} %get-tuple-element.23, f32[4,2048]{1,0:T(4,128)S(1)} %collective-permute-done.13), kind=kLoop, calls=%fused_computation | loop fusion | flops 16384 | bytes 81920 | tf_op jit(solution)/shard_map/convert_element_type | solution.py:399
  (34 shorter events, 0.4 us)
Async XLA Ops:
  0.0 2.6 %copy-start.4 = (bf16[4,2048]{1,0:T(4,128)(2,1)S(1)}, bf16[4,2048]{1,0:T(4,128)(2,1)}, u32[]{:S(2)}) copy-start(bf16[4,2048]{1,0:T(4,128)(2,1)} %rows_ref.1) | copy-start | bytes 49156
  0.0 2.6 %copy-start.2 = (bf16[2048,256]{1,0:T(8,128)(2,1)S(1)}, bf16[2048,256]{1,0:T(8,128)(2,1)}, u32[]{:S(2)}) copy-start(bf16[2048,256]{1,0:T(8,128)(2,1)} %wk.1) | copy-start | bytes 3145732
  0.0 2.6 %copy-start.3 = (bf16[2048,256]{1,0:T(8,128)(2,1)S(1)}, bf16[2048,256]{1,0:T(8,128)(2,1)}, u32[]{:S(2)}) copy-start(bf16[2048,256]{1,0:T(8,128)(2,1)} %wv.1) | copy-start | bytes 3145732
  0.0 2.6 %collective-permute-start = (bf16[4,2048]{1,0:T(4,128)(2,1)}, bf16[4,2048]{1,0:T(4,128)(2,1)S(1)}, u32[]{:S(2)}, u32[]{:S(2)}) collective-permute-start(bf16[4,2048]{1,0:T(4,128)(2,1)} %rows_ref.1), channel_id=1, source_target_pairs={{0,1},{1,0},{2,3},{3,2},{4,5},{5,4},{6,7},{7,6},{8,9},{9,8},{10,11... | collective-permute-start | bytes 49160 | tf_op jit(solution)/shard_map/ppermute | solution.py:331
  2.6 17.6 %copy-start = (bf16[1,2,2048,128]{3,2,1,0:T(8,128)(2,1)S(1)}, bf16[1,2,2048,128]{3,2,1,0:T(8,128)(2,1)}, u32[]{:S(2)}) copy-start(bf16[1,2,2048,128]{3,2,1,0:T(8,128)(2,1)} %k_ref.1) | copy-start | bytes 3145732
  2.6 17.6 %copy-start.1 = (bf16[1,2,2048,128]{3,2,1,0:T(8,128)(2,1)S(1)}, bf16[1,2,2048,128]{3,2,1,0:T(8,128)(2,1)}, u32[]{:S(2)}) copy-start(bf16[1,2,2048,128]{3,2,1,0:T(8,128)(2,1)} %v_ref.1) | copy-start | bytes 3145732
  8.0 5.5 %collective-permute-start.1 = (f32[2,40,128]{2,1,0:T(8,128)S(1)}, f32[2,40,128]{2,1,0:T(8,128)S(1)}, u32[]{:S(2)}, u32[]{:S(2)}) collective-permute-start(f32[2,40,128]{2,1,0:T(8,128)S(1)} %get-tuple-element.15.after_ref), channel_id=1, source_target_pairs={{0,7},{1,6},{2,5},{3,4},{4,3},{5,2},{6,1},{7,0},{8,15},{9,14},{10,... | collective-permute-start | bytes 122888 | tf_op jit(solution)/shard_map/ppermute | solution.py:336
  11.6 3.4 %collective-permute-start.2 = (f32[2,40,128]{2,1,0:T(8,128)S(1)}, f32[2,40,128]{2,1,0:T(8,128)S(1)}, u32[]{:S(2)}, u32[]{:S(2)}) collective-permute-start(f32[2,40,128]{2,1,0:T(8,128)S(1)} %get-tuple-element.16), channel_id=1, source_target_pairs={{0,3},{1,2},{2,1},{3,0},{4,7},{5,6},{6,5},{7,4},{8,11},{9,10},{10,... | collective-permute-start | bytes 122888 | tf_op jit(solution)/shard_map/ppermute | solution.py:336
  12.3 3.7 %collective-permute-start.3 = (f32[2,40,128]{2,1,0:T(8,128)S(1)}, f32[2,40,128]{2,1,0:T(8,128)S(1)}, u32[]{:S(2)}, u32[]{:S(2)}) collective-permute-start(f32[2,40,128]{2,1,0:T(8,128)S(1)} %get-tuple-element.17), channel_id=1, source_target_pairs={{0,5},{1,4},{2,7},{3,6},{4,1},{5,0},{6,3},{7,2},{8,13},{9,12},{10,... | collective-permute-start | bytes 122888 | tf_op jit(solution)/shard_map/ppermute | solution.py:336
  12.4 3.6 %collective-permute-start.4 = (f32[2,40,128]{2,1,0:T(8,128)S(1)}, f32[2,40,128]{2,1,0:T(8,128)S(1)}, u32[]{:S(2)}, u32[]{:S(2)}) collective-permute-start(f32[2,40,128]{2,1,0:T(8,128)S(1)} %get-tuple-element.18), channel_id=1, source_target_pairs={{0,1},{1,0},{2,3},{3,2},{4,5},{5,4},{6,7},{7,6},{8,9},{9,8},{10,11... | collective-permute-start | bytes 122888 | tf_op jit(solution)/shard_map/ppermute | solution.py:331
  13.1 17.2 %slice-start = ((s8[16777216]{0:T(1024)(128)(4,1)}), s8[4194304]{0:T(1024)(128)(4,1)S(1)}, s32[]{:S(2)}) async-start(s8[16777216]{0:T(1024)(128)(4,1)} %bitcast.2), calls=%async_computation | async-start | bytes 8388608
  13.1 17.2 %slice-start.1 = ((s8[16777216]{0:T(1024)(128)(4,1)}), s8[4194304]{0:T(1024)(128)(4,1)S(1)}, s32[]{:S(2)}) async-start(s8[16777216]{0:T(1024)(128)(4,1)} %bitcast.2), calls=%async_computation.1 | async-start | bytes 8388608
  16.0 4.2 %collective-permute-start.5 = (f32[1,40,128]{2,1,0:T(8,128)S(1)}, f32[1,40,128]{2,1,0:T(8,128)S(1)}, u32[]{:S(2)}, u32[]{:S(2)}) collective-permute-start(f32[1,40,128]{2,1,0:T(8,128)S(1)} %get-tuple-element.22), channel_id=1, source_target_pairs={{0,9},{1,8},{2,11},{3,10},{4,13},{5,12},{6,15},{7,14},{8,1},{9,0},... | collective-permute-start | bytes 61448 | tf_op jit(solution)/shard_map/ppermute | solution.py:336
  18.3 1.8 %collective-permute-start.6 = (f32[1,40,128]{2,1,0:T(8,128)S(1)}, f32[1,40,128]{2,1,0:T(8,128)S(1)}, u32[]{:S(2)}, u32[]{:S(2)}) collective-permute-start(f32[1,40,128]{2,1,0:T(8,128)S(1)} %get-tuple-element.25), channel_id=1, source_target_pairs={{0,1},{1,0},{2,3},{3,2},{4,5},{5,4},{6,7},{7,6},{8,9},{9,8},{10,11... | collective-permute-start | bytes 61448 | tf_op jit(solution)/shard_map/ppermute | solution.py:331
  20.2 10.1 %slice-start.2 = ((s8[16777216]{0:T(1024)(128)(4,1)}), s8[4194304]{0:T(1024)(128)(4,1)S(1)}, s32[]{:S(2)}) async-start(s8[16777216]{0:T(1024)(128)(4,1)} %bitcast.2), calls=%async_computation.2 | async-start | bytes 8388608
  20.2 10.1 %slice-start.3 = ((s8[16777216]{0:T(1024)(128)(4,1)}), s8[4194304]{0:T(1024)(128)(4,1)S(1)}, s32[]{:S(2)}) async-start(s8[16777216]{0:T(1024)(128)(4,1)} %bitcast.2), calls=%async_computation.3 | async-start | bytes 8388608
  21.0 4.0 %collective-permute-start.7 = (bf16[1,32,128]{2,1,0:T(8,128)(2,1)S(1)}, bf16[1,32,128]{2,1,0:T(8,128)(2,1)S(1)}, u32[]{:S(2)}, u32[]{:S(2)}) collective-permute-start(bf16[1,32,128]{2,1,0:T(8,128)(2,1)S(1)} %attend.1.refs_4_), channel_id=1, source_target_pairs={{0,9},{1,8},{2,11},{3,10},{4,13},{5,12},{6,15},{7,14},{8,1},{9,0},... | collective-permute-start | bytes 24584 | tf_op jit(solution)/shard_map/ppermute | solution.py:336
  23.4 1.7 %collective-permute-start.8 = (bf16[1,32,128]{2,1,0:T(8,128)(2,1)S(1)}, bf16[1,32,128]{2,1,0:T(8,128)(2,1)S(1)}, u32[]{:S(2)}, u32[]{:S(2)}) collective-permute-start(bf16[1,32,128]{2,1,0:T(8,128)(2,1)S(1)} %attend.1.refs_4_), channel_id=1, source_target_pairs={{0,1},{1,0},{2,3},{3,2},{4,5},{5,4},{6,7},{7,6},{8,9},{9,8},{10,11... | collective-permute-start | bytes 24584 | tf_op jit(solution)/shard_map/ppermute | solution.py:331
  25.1 4.5 %collective-permute-start.10 = (bf16[2,32,128]{2,1,0:T(8,128)(2,1)S(1)}, bf16[2,32,128]{2,1,0:T(8,128)(2,1)S(1)}, u32[]{:S(2)}, u32[]{:S(2)}) collective-permute-start(bf16[2,32,128]{2,1,0:T(8,128)(2,1)S(1)} %constant_dynamic-update-slice_fusion), channel_id=1, source_target_pairs={{0,7},{1,6},{2,5},{3,4},{4,3},{5,2},{6,1},{7,0},{8,15},{9,14},{10,... | collective-permute-start | bytes 49160 | tf_op jit(solution)/shard_map/ppermute | solution.py:336
  26.3 3.4 %collective-permute-start.11 = (bf16[2,32,128]{2,1,0:T(8,128)(2,1)S(1)}, bf16[2,32,128]{2,1,0:T(8,128)(2,1)S(1)}, u32[]{:S(2)}, u32[]{:S(2)}) collective-permute-start(bf16[2,32,128]{2,1,0:T(8,128)(2,1)S(1)} %constant_dynamic-update-slice_fusion), channel_id=1, source_target_pairs={{0,3},{1,2},{2,1},{3,0},{4,7},{5,6},{6,5},{7,4},{8,11},{9,10},{10,... | collective-permute-start | bytes 49160 | tf_op jit(solution)/shard_map/ppermute | solution.py:336
  27.1 3.2 %collective-permute-start.9 = (bf16[2,32,128]{2,1,0:T(8,128)(2,1)S(1)}, bf16[2,32,128]{2,1,0:T(8,128)(2,1)S(1)}, u32[]{:S(2)}, u32[]{:S(2)}) collective-permute-start(bf16[2,32,128]{2,1,0:T(8,128)(2,1)S(1)} %constant_dynamic-update-slice_fusion), channel_id=1, source_target_pairs={{0,5},{1,4},{2,7},{3,6},{4,1},{5,0},{6,3},{7,2},{8,13},{9,12},{10,... | collective-permute-start | bytes 49160 | tf_op jit(solution)/shard_map/ppermute | solution.py:336
  28.4 1.2 %collective-permute-start.12 = (bf16[1,32,128]{2,1,0:T(8,128)(2,1)S(1)}, bf16[1,32,128]{2,1,0:T(8,128)(2,1)S(1)}, u32[]{:S(2)}, u32[]{:S(2)}) collective-permute-start(bf16[1,32,128]{2,1,0:T(8,128)(2,1)S(1)} %collective-permute-done.7), channel_id=1, source_target_pairs={{0,1},{1,0},{2,3},{3,2},{4,5},{5,4},{6,7},{7,6},{8,9},{9,8},{10,11... | collective-permute-start | bytes 24584 | tf_op jit(solution)/shard_map/ppermute | solution.py:331
  32.6 1.2 %collective-permute-start.13 = (f32[4,2048]{1,0:T(4,128)S(1)}, f32[4,2048]{1,0:T(4,128)S(1)}, u32[]{:S(2)}, u32[]{:S(2)}) collective-permute-start(f32[4,2048]{1,0:T(4,128)S(1)} %get-tuple-element.24), channel_id=1, source_target_pairs={{0,1},{1,0},{2,3},{3,2},{4,5},{5,4},{6,7},{7,6},{8,9},{9,8},{10,11... | collective-permute-start | bytes 98312 | tf_op jit(solution)/shard_map/ppermute | solution.py:331

commit v25 on v24

--- a/solution.py
+++ b/solution.py
@@ -11,7 +11,7 @@
 MODEL_WIDTH = 16384
 LANES = 128
 HEAD_SIZE = 128
-CHUNK = 256
+CHUNK = 512
 FIRST = 384
 PIECES = 1
 FAN = 4

time: 34.6 us -> 34.8 us (level)
  no operation moved by 1% of the time
where the time goes in v25:
time: 34.8 us; the launch traced here: 34.7 us
  starting transfers between devices  13.9 us (40%)
  Pallas kernels  10.8 us (31%)
  waiting for transfers between devices  8.32 us (24%)
  between operations  0.81 us (2%)
  other arithmetic  0.71 us (2%)
    ppermute x8, starting transfers between devices, cross(): return lax.ppermute(block, ('gx', 'gy'), pairs)  12.4 us
    ppermute x8, waiting for transfers between devices, cross(): return lax.ppermute(block, ('gx', 'gy'), pairs)  6.14 us
    pallas_call x1, Pallas kernels, project(): pl.pallas_call(functools.partial(project_kernel, bits), out_shape=(piece,...  5.65 us
    pallas_call x1, Pallas kernels, output(): pl.pallas_call(functools.partial(output_kernel, bits, places, turned), ou...  2.28 us
    ppermute x6, waiting for transfers between devices, swap(): return lax.ppermute(block, axis, [(i, i ^ mask) for i in range(devices)])  2.18 us
    pallas_call x1, Pallas kernels, stage_rows(): pl.pallas_call(functools.partial(stage_kernel, rows), out_shape=jax.Shape...  2.01 us
    ppermute x6, starting transfers between devices, swap(): return lax.ppermute(block, axis, [(i, i ^ mask) for i in range(devices)])  1.54 us
    pallas_call x1, Pallas kernels, attend(): pl.pallas_call(functools.partial(attend_kernel, query_heads, kv_heads, le...  0.82 us
  transfers between devices with their start and end apart: 14, of which 8 were waited for; matrix products, arithmetic and copies ran while one was open for 0% of the time, Pallas kernels for 6%

profile of v25, /device:TPU:0, one launch (start us, length us, event | category | flops | bytes accessed | tf_op | source)
XLA Modules:
  0.0 34.7 jit_solution(4062315642113353017)
XLA Ops:
  0.0 0.5 %collective-permute-start = (bf16[4,2048]{1,0:T(4,128)(2,1)}, bf16[4,2048]{1,0:T(4,128)(2,1)S(1)}, u32[]{:S(2)}, u32[]{:S(2)}) collective-permute-start(bf16[4,2048]{1,0:T(4,128)(2,1)} %rows_ref.1), channel_id=1, source_target_pairs={{0,1},{1,0},{2,3},{3,2},{4,5},{5,4},{6,7},{7,6},{8,9},{9,8},{10,11... | collective-permute-start | bytes 49160 | tf_op jit(solution)/shard_map/ppermute | solution.py:331
  0.5 2.0 %stage.1.first = bf16[384,4096]{1,0:T(8,128)(2,1)S(1)} custom-call(bf16[2048,4096]{1,0:T(8,128)(2,1)} %wq_hbm.1), custom_call_target="tpu_custom_call" | custom-call | bytes 3145728 | tf_op jit(solution)/shard_map/stage/pallas_call | solution.py:57
  2.6 5.7 %project.1 = (f32[2,40,128]{2,1,0:T(8,128)S(1)}, f32[2,40,128]{2,1,0:T(8,128)S(1)}, f32[2,40,128]{2,1,0:T(8,128)S(1)}, f32[2,40,128]{2,1,0:T(8,128)S(1)}) custom-call(bf16[4,2048]{1,0:T(4,128)(2,1)S(1)} %copy-done.4, bf16[4,2048]{1,0:T(4,128)(2,1)S(1)} %collective-permute-done.other_ref, bf16[2048,4096]{1,0:T(8,128)(2,1)} %wq_hbm.1, ...), custom_call_target="tpu_custom_call" | custom-call | flops 150994944 | bytes 18874368 | tf_op jit(solution)/shard_map/project/pallas_call | solution.py:179
  8.3 3.6 %collective-permute-start.1 = (f32[2,40,128]{2,1,0:T(8,128)S(1)}, f32[2,40,128]{2,1,0:T(8,128)S(1)}, u32[]{:S(2)}, u32[]{:S(2)}) collective-permute-start(f32[2,40,128]{2,1,0:T(8,128)S(1)} %get-tuple-element.15.after_ref), channel_id=1, source_target_pairs={{0,7},{1,6},{2,5},{3,4},{4,3},{5,2},{6,1},{7,0},{8,15},{9,14},{10,... | collective-permute-start | bytes 122888 | tf_op jit(solution)/shard_map/ppermute | solution.py:336
  11.8 0.6 %collective-permute-start.2 = (f32[2,40,128]{2,1,0:T(8,128)S(1)}, f32[2,40,128]{2,1,0:T(8,128)S(1)}, u32[]{:S(2)}, u32[]{:S(2)}) collective-permute-start(f32[2,40,128]{2,1,0:T(8,128)S(1)} %get-tuple-element.16), channel_id=1, source_target_pairs={{0,3},{1,2},{2,1},{3,0},{4,7},{5,6},{6,5},{7,4},{8,11},{9,10},{10,... | collective-permute-start | bytes 122888 | tf_op jit(solution)/shard_map/ppermute | solution.py:336
  13.4 0.4 %collective-permute-done.1 = f32[2,40,128]{2,1,0:T(8,128)S(1)} collective-permute-done((f32[2,40,128]{2,1,0:T(8,128)S(1)}, f32[2,40,128]{2,1,0:T(8,128)S(1)}, u32[]{:S(2)}, u32[]{:S(2)}) %collective-permute-start.1) | collective-permute-done | bytes 40992 | tf_op jit(solution)/shard_map/ppermute | solution.py:336
  13.8 1.5 %collective-permute-done.2 = f32[2,40,128]{2,1,0:T(8,128)S(1)} collective-permute-done((f32[2,40,128]{2,1,0:T(8,128)S(1)}, f32[2,40,128]{2,1,0:T(8,128)S(1)}, u32[]{:S(2)}, u32[]{:S(2)}) %collective-permute-start.2) | collective-permute-done | bytes 40992 | tf_op jit(solution)/shard_map/ppermute | solution.py:336
  15.3 0.9 %collective-permute-done.3 = f32[2,40,128]{2,1,0:T(8,128)S(1)} collective-permute-done((f32[2,40,128]{2,1,0:T(8,128)S(1)}, f32[2,40,128]{2,1,0:T(8,128)S(1)}, u32[]{:S(2)}, u32[]{:S(2)}) %collective-permute-start.3) | collective-permute-done | bytes 40992 | tf_op jit(solution)/shard_map/ppermute | solution.py:336
  16.2 2.4 %collective-permute-start.5 = (f32[1,40,128]{2,1,0:T(8,128)S(1)}, f32[1,40,128]{2,1,0:T(8,128)S(1)}, u32[]{:S(2)}, u32[]{:S(2)}) collective-permute-start(f32[1,40,128]{2,1,0:T(8,128)S(1)} %get-tuple-element.22), channel_id=1, source_target_pairs={{0,9},{1,8},{2,11},{3,10},{4,13},{5,12},{6,15},{7,14},{8,1},{9,0},... | collective-permute-start | bytes 61448 | tf_op jit(solution)/shard_map/ppermute | solution.py:336
  18.6 0.4 %collective-permute-start.6 = (f32[1,40,128]{2,1,0:T(8,128)S(1)}, f32[1,40,128]{2,1,0:T(8,128)S(1)}, u32[]{:S(2)}, u32[]{:S(2)}) collective-permute-start(f32[1,40,128]{2,1,0:T(8,128)S(1)} %get-tuple-element.25), channel_id=1, source_target_pairs={{0,1},{1,0},{2,3},{3,2},{4,5},{5,4},{6,7},{7,6},{8,9},{9,8},{10,11... | collective-permute-start | bytes 61448 | tf_op jit(solution)/shard_map/ppermute | solution.py:331
  19.0 1.4 %collective-permute-done.5.refs_0_ = f32[1,40,128]{2,1,0:T(8,128)S(1)} collective-permute-done((f32[1,40,128]{2,1,0:T(8,128)S(1)}, f32[1,40,128]{2,1,0:T(8,128)S(1)}, u32[]{:S(2)}, u32[]{:S(2)}) %collective-permute-start.5) | collective-permute-done | bytes 20512 | tf_op jit(solution)/shard_map/ppermute | solution.py:336
  20.4 0.8 %attend.1.refs_4_ = bf16[1,32,128]{2,1,0:T(8,128)(2,1)S(1)} custom-call(bf16[4096,2048]{1,0:T(8,128)(2,1)} %refs_5_.1, f32[8,128]{1,0:T(8,128)S(1)} %get-tuple-element.20.turn_ref, f32[1,2048]{1,0:T(1,128)S(1)} %get-tuple-element.21.live_ref, bf16[1,2,2048,128]{3,2,1,0:T(8,128)(2,1)S(1)} %copy-done, bf16[1,2,2048,128]{3,2,1,0:T(8,128)(2,1)S(1)} %copy-done.1, ...), custom_call_target="tpu_custom_call" | custom-call | flops 33554432 | bytes 2097152 | tf_op jit(solution)/shard_map/attend/pallas_call | solution.py:266
  21.3 2.4 %collective-permute-start.7 = (bf16[1,32,128]{2,1,0:T(8,128)(2,1)S(1)}, bf16[1,32,128]{2,1,0:T(8,128)(2,1)S(1)}, u32[]{:S(2)}, u32[]{:S(2)}) collective-permute-start(bf16[1,32,128]{2,1,0:T(8,128)(2,1)S(1)} %attend.1.refs_4_), channel_id=1, source_target_pairs={{0,9},{1,8},{2,11},{3,10},{4,13},{5,12},{6,15},{7,14},{8,1},{9,0},... | collective-permute-start | bytes 24584 | tf_op jit(solution)/shard_map/ppermute | solution.py:336
  23.6 0.4 %collective-permute-start.8 = (bf16[1,32,128]{2,1,0:T(8,128)(2,1)S(1)}, bf16[1,32,128]{2,1,0:T(8,128)(2,1)S(1)}, u32[]{:S(2)}, u32[]{:S(2)}) collective-permute-start(bf16[1,32,128]{2,1,0:T(8,128)(2,1)S(1)} %attend.1.refs_4_), channel_id=1, source_target_pairs={{0,1},{1,0},{2,3},{3,2},{4,5},{5,4},{6,7},{7,6},{8,9},{9,8},{10,11... | collective-permute-start | bytes 24584 | tf_op jit(solution)/shard_map/ppermute | solution.py:331
  24.0 1.3 %collective-permute-done.7 = bf16[1,32,128]{2,1,0:T(8,128)(2,1)S(1)} collective-permute-done((bf16[1,32,128]{2,1,0:T(8,128)(2,1)S(1)}, bf16[1,32,128]{2,1,0:T(8,128)(2,1)S(1)}, u32[]{:S(2)}, u32[]{:S(2)}) %collective-permute-start.7) | collective-permute-done | bytes 8224 | tf_op jit(solution)/shard_map/ppermute | solution.py:336
  25.3 1.2 %collective-permute-start.10 = (bf16[2,32,128]{2,1,0:T(8,128)(2,1)S(1)}, bf16[2,32,128]{2,1,0:T(8,128)(2,1)S(1)}, u32[]{:S(2)}, u32[]{:S(2)}) collective-permute-start(bf16[2,32,128]{2,1,0:T(8,128)(2,1)S(1)} %constant_dynamic-update-slice_fusion), channel_id=1, source_target_pairs={{0,7},{1,6},{2,5},{3,4},{4,3},{5,2},{6,1},{7,0},{8,15},{9,14},{10,... | collective-permute-start | bytes 49160 | tf_op jit(solution)/shard_map/ppermute | solution.py:336
  26.5 0.9 %collective-permute-start.11 = (bf16[2,32,128]{2,1,0:T(8,128)(2,1)S(1)}, bf16[2,32,128]{2,1,0:T(8,128)(2,1)S(1)}, u32[]{:S(2)}, u32[]{:S(2)}) collective-permute-start(bf16[2,32,128]{2,1,0:T(8,128)(2,1)S(1)} %constant_dynamic-update-slice_fusion), channel_id=1, source_target_pairs={{0,3},{1,2},{2,1},{3,0},{4,7},{5,6},{6,5},{7,4},{8,11},{9,10},{10,... | collective-permute-start | bytes 49160 | tf_op jit(solution)/shard_map/ppermute | solution.py:336
  27.3 1.3 %collective-permute-start.9 = (bf16[2,32,128]{2,1,0:T(8,128)(2,1)S(1)}, bf16[2,32,128]{2,1,0:T(8,128)(2,1)S(1)}, u32[]{:S(2)}, u32[]{:S(2)}) collective-permute-start(bf16[2,32,128]{2,1,0:T(8,128)(2,1)S(1)} %constant_dynamic-update-slice_fusion), channel_id=1, source_target_pairs={{0,5},{1,4},{2,7},{3,6},{4,1},{5,0},{6,3},{7,2},{8,13},{9,12},{10,... | collective-permute-start | bytes 49160 | tf_op jit(solution)/shard_map/ppermute | solution.py:336
  28.7 1.1 %collective-permute-done.12.refs_3_ = bf16[1,32,128]{2,1,0:T(8,128)(2,1)S(1)} collective-permute-done((bf16[1,32,128]{2,1,0:T(8,128)(2,1)S(1)}, bf16[1,32,128]{2,1,0:T(8,128)(2,1)S(1)}, u32[]{:S(2)}, u32[]{:S(2)}) %collective-permute-start.12) | collective-permute-done | bytes 8224 | tf_op jit(solution)/shard_map/ppermute | solution.py:331
  29.8 0.7 %collective-permute-done.9.refs_0_ = bf16[2,32,128]{2,1,0:T(8,128)(2,1)S(1)} collective-permute-done((bf16[2,32,128]{2,1,0:T(8,128)(2,1)S(1)}, bf16[2,32,128]{2,1,0:T(8,128)(2,1)S(1)}, u32[]{:S(2)}, u32[]{:S(2)}) %collective-permute-start.9) | collective-permute-done | bytes 16416 | tf_op jit(solution)/shard_map/ppermute | solution.py:336
  30.5 2.3 %output.1 = (f32[4,2048]{1,0:T(4,128)S(1)}, f32[4,2048]{1,0:T(4,128)S(1)}) custom-call(bf16[2,32,128]{2,1,0:T(8,128)(2,1)S(1)} %collective-permute-done.9.refs_0_, bf16[2,32,128]{2,1,0:T(8,128)(2,1)S(1)} %collective-permute-done.10.refs_1_, bf16[2,32,128]{2,1,0:T(8,128)(2,1)S(1)} %collective-permute-done.11.refs_2_, ...), custom_call_target="tpu_custom_call" | custom-call | flops 134217728 | bytes 16777216 | tf_op jit(solution)/shard_map/output/pallas_call | solution.py:313
  32.8 0.2 collective-permute-start.13
  33.0 1.0 %collective-permute-done.13 = f32[4,2048]{1,0:T(4,128)S(1)} collective-permute-done((f32[4,2048]{1,0:T(4,128)S(1)}, f32[4,2048]{1,0:T(4,128)S(1)}, u32[]{:S(2)}, u32[]{:S(2)}) %collective-permute-start.13) | collective-permute-done | bytes 32800 | tf_op jit(solution)/shard_map/ppermute | solution.py:331
  34.0 0.6 %add_convert_fusion = bf16[4,2048]{1,0:T(4,128)(2,1)} fusion(f32[4,2048]{1,0:T(4,128)S(1)} %get-tuple-element.23, f32[4,2048]{1,0:T(4,128)S(1)} %collective-permute-done.13), kind=kLoop, calls=%fused_computation | loop fusion | flops 16384 | bytes 81920 | tf_op jit(solution)/shard_map/convert_element_type | solution.py:399
  (34 shorter events, 0.4 us)
Async XLA Ops:
  0.0 2.6 %copy-start.4 = (bf16[4,2048]{1,0:T(4,128)(2,1)S(1)}, bf16[4,2048]{1,0:T(4,128)(2,1)}, u32[]{:S(2)}) copy-start(bf16[4,2048]{1,0:T(4,128)(2,1)} %rows_ref.1) | copy-start | bytes 49156
  0.0 2.6 %copy-start.2 = (bf16[2048,256]{1,0:T(8,128)(2,1)S(1)}, bf16[2048,256]{1,0:T(8,128)(2,1)}, u32[]{:S(2)}) copy-start(bf16[2048,256]{1,0:T(8,128)(2,1)} %wk.1) | copy-start | bytes 3145732
  0.0 2.6 %copy-start.3 = (bf16[2048,256]{1,0:T(8,128)(2,1)S(1)}, bf16[2048,256]{1,0:T(8,128)(2,1)}, u32[]{:S(2)}) copy-start(bf16[2048,256]{1,0:T(8,128)(2,1)} %wv.1) | copy-start | bytes 3145732
  0.0 2.6 %collective-permute-start = (bf16[4,2048]{1,0:T(4,128)(2,1)}, bf16[4,2048]{1,0:T(4,128)(2,1)S(1)}, u32[]{:S(2)}, u32[]{:S(2)}) collective-permute-start(bf16[4,2048]{1,0:T(4,128)(2,1)} %rows_ref.1), channel_id=1, source_target_pairs={{0,1},{1,0},{2,3},{3,2},{4,5},{5,4},{6,7},{7,6},{8,9},{9,8},{10,11... | collective-permute-start | bytes 49160 | tf_op jit(solution)/shard_map/ppermute | solution.py:331
  2.6 17.8 %copy-start = (bf16[1,2,2048,128]{3,2,1,0:T(8,128)(2,1)S(1)}, bf16[1,2,2048,128]{3,2,1,0:T(8,128)(2,1)}, u32[]{:S(2)}) copy-start(bf16[1,2,2048,128]{3,2,1,0:T(8,128)(2,1)} %k_ref.1) | copy-start | bytes 3145732
  2.6 17.8 %copy-start.1 = (bf16[1,2,2048,128]{3,2,1,0:T(8,128)(2,1)S(1)}, bf16[1,2,2048,128]{3,2,1,0:T(8,128)(2,1)}, u32[]{:S(2)}) copy-start(bf16[1,2,2048,128]{3,2,1,0:T(8,128)(2,1)} %v_ref.1) | copy-start | bytes 3145732
  8.3 5.5 %collective-permute-start.1 = (f32[2,40,128]{2,1,0:T(8,128)S(1)}, f32[2,40,128]{2,1,0:T(8,128)S(1)}, u32[]{:S(2)}, u32[]{:S(2)}) collective-permute-start(f32[2,40,128]{2,1,0:T(8,128)S(1)} %get-tuple-element.15.after_ref), channel_id=1, source_target_pairs={{0,7},{1,6},{2,5},{3,4},{4,3},{5,2},{6,1},{7,0},{8,15},{9,14},{10,... | collective-permute-start | bytes 122888 | tf_op jit(solution)/shard_map/ppermute | solution.py:336
  11.8 3.4 %collective-permute-start.2 = (f32[2,40,128]{2,1,0:T(8,128)S(1)}, f32[2,40,128]{2,1,0:T(8,128)S(1)}, u32[]{:S(2)}, u32[]{:S(2)}) collective-permute-start(f32[2,40,128]{2,1,0:T(8,128)S(1)} %get-tuple-element.16), channel_id=1, source_target_pairs={{0,3},{1,2},{2,1},{3,0},{4,7},{5,6},{6,5},{7,4},{8,11},{9,10},{10,... | collective-permute-start | bytes 122888 | tf_op jit(solution)/shard_map/ppermute | solution.py:336
  12.5 3.7 %collective-permute-start.3 = (f32[2,40,128]{2,1,0:T(8,128)S(1)}, f32[2,40,128]{2,1,0:T(8,128)S(1)}, u32[]{:S(2)}, u32[]{:S(2)}) collective-permute-start(f32[2,40,128]{2,1,0:T(8,128)S(1)} %get-tuple-element.17), channel_id=1, source_target_pairs={{0,5},{1,4},{2,7},{3,6},{4,1},{5,0},{6,3},{7,2},{8,13},{9,12},{10,... | collective-permute-start | bytes 122888 | tf_op jit(solution)/shard_map/ppermute | solution.py:336
  12.6 3.6 %collective-permute-start.4 = (f32[2,40,128]{2,1,0:T(8,128)S(1)}, f32[2,40,128]{2,1,0:T(8,128)S(1)}, u32[]{:S(2)}, u32[]{:S(2)}) collective-permute-start(f32[2,40,128]{2,1,0:T(8,128)S(1)} %get-tuple-element.18), channel_id=1, source_target_pairs={{0,1},{1,0},{2,3},{3,2},{4,5},{5,4},{6,7},{7,6},{8,9},{9,8},{10,11... | collective-permute-start | bytes 122888 | tf_op jit(solution)/shard_map/ppermute | solution.py:331
  13.3 17.2 %slice-start = ((s8[16777216]{0:T(1024)(128)(4,1)}), s8[4194304]{0:T(1024)(128)(4,1)S(1)}, s32[]{:S(2)}) async-start(s8[16777216]{0:T(1024)(128)(4,1)} %bitcast.2), calls=%async_computation | async-start | bytes 8388608
  13.3 17.2 %slice-start.1 = ((s8[16777216]{0:T(1024)(128)(4,1)}), s8[4194304]{0:T(1024)(128)(4,1)S(1)}, s32[]{:S(2)}) async-start(s8[16777216]{0:T(1024)(128)(4,1)} %bitcast.2), calls=%async_computation.1 | async-start | bytes 8388608
  16.2 4.2 %collective-permute-start.5 = (f32[1,40,128]{2,1,0:T(8,128)S(1)}, f32[1,40,128]{2,1,0:T(8,128)S(1)}, u32[]{:S(2)}, u32[]{:S(2)}) collective-permute-start(f32[1,40,128]{2,1,0:T(8,128)S(1)} %get-tuple-element.22), channel_id=1, source_target_pairs={{0,9},{1,8},{2,11},{3,10},{4,13},{5,12},{6,15},{7,14},{8,1},{9,0},... | collective-permute-start | bytes 61448 | tf_op jit(solution)/shard_map/ppermute | solution.py:336
  18.6 1.8 %collective-permute-start.6 = (f32[1,40,128]{2,1,0:T(8,128)S(1)}, f32[1,40,128]{2,1,0:T(8,128)S(1)}, u32[]{:S(2)}, u32[]{:S(2)}) collective-permute-start(f32[1,40,128]{2,1,0:T(8,128)S(1)} %get-tuple-element.25), channel_id=1, source_target_pairs={{0,1},{1,0},{2,3},{3,2},{4,5},{5,4},{6,7},{7,6},{8,9},{9,8},{10,11... | collective-permute-start | bytes 61448 | tf_op jit(solution)/shard_map/ppermute | solution.py:331
  20.4 10.1 %slice-start.2 = ((s8[16777216]{0:T(1024)(128)(4,1)}), s8[4194304]{0:T(1024)(128)(4,1)S(1)}, s32[]{:S(2)}) async-start(s8[16777216]{0:T(1024)(128)(4,1)} %bitcast.2), calls=%async_computation.2 | async-start | bytes 8388608
  20.4 10.1 %slice-start.3 = ((s8[16777216]{0:T(1024)(128)(4,1)}), s8[4194304]{0:T(1024)(128)(4,1)S(1)}, s32[]{:S(2)}) async-start(s8[16777216]{0:T(1024)(128)(4,1)} %bitcast.2), calls=%async_computation.3 | async-start | bytes 8388608
  21.3 4.0 %collective-permute-start.7 = (bf16[1,32,128]{2,1,0:T(8,128)(2,1)S(1)}, bf16[1,32,128]{2,1,0:T(8,128)(2,1)S(1)}, u32[]{:S(2)}, u32[]{:S(2)}) collective-permute-start(bf16[1,32,128]{2,1,0:T(8,128)(2,1)S(1)} %attend.1.refs_4_), channel_id=1, source_target_pairs={{0,9},{1,8},{2,11},{3,10},{4,13},{5,12},{6,15},{7,14},{8,1},{9,0},... | collective-permute-start | bytes 24584 | tf_op jit(solution)/shard_map/ppermute | solution.py:336
  23.6 1.7 %collective-permute-start.8 = (bf16[1,32,128]{2,1,0:T(8,128)(2,1)S(1)}, bf16[1,32,128]{2,1,0:T(8,128)(2,1)S(1)}, u32[]{:S(2)}, u32[]{:S(2)}) collective-permute-start(bf16[1,32,128]{2,1,0:T(8,128)(2,1)S(1)} %attend.1.refs_4_), channel_id=1, source_target_pairs={{0,1},{1,0},{2,3},{3,2},{4,5},{5,4},{6,7},{7,6},{8,9},{9,8},{10,11... | collective-permute-start | bytes 24584 | tf_op jit(solution)/shard_map/ppermute | solution.py:331
  25.3 4.5 %collective-permute-start.10 = (bf16[2,32,128]{2,1,0:T(8,128)(2,1)S(1)}, bf16[2,32,128]{2,1,0:T(8,128)(2,1)S(1)}, u32[]{:S(2)}, u32[]{:S(2)}) collective-permute-start(bf16[2,32,128]{2,1,0:T(8,128)(2,1)S(1)} %constant_dynamic-update-slice_fusion), channel_id=1, source_target_pairs={{0,7},{1,6},{2,5},{3,4},{4,3},{5,2},{6,1},{7,0},{8,15},{9,14},{10,... | collective-permute-start | bytes 49160 | tf_op jit(solution)/shard_map/ppermute | solution.py:336
  26.5 3.4 %collective-permute-start.11 = (bf16[2,32,128]{2,1,0:T(8,128)(2,1)S(1)}, bf16[2,32,128]{2,1,0:T(8,128)(2,1)S(1)}, u32[]{:S(2)}, u32[]{:S(2)}) collective-permute-start(bf16[2,32,128]{2,1,0:T(8,128)(2,1)S(1)} %constant_dynamic-update-slice_fusion), channel_id=1, source_target_pairs={{0,3},{1,2},{2,1},{3,0},{4,7},{5,6},{6,5},{7,4},{8,11},{9,10},{10,... | collective-permute-start | bytes 49160 | tf_op jit(solution)/shard_map/ppermute | solution.py:336
  27.3 3.2 %collective-permute-start.9 = (bf16[2,32,128]{2,1,0:T(8,128)(2,1)S(1)}, bf16[2,32,128]{2,1,0:T(8,128)(2,1)S(1)}, u32[]{:S(2)}, u32[]{:S(2)}) collective-permute-start(bf16[2,32,128]{2,1,0:T(8,128)(2,1)S(1)} %constant_dynamic-update-slice_fusion), channel_id=1, source_target_pairs={{0,5},{1,4},{2,7},{3,6},{4,1},{5,0},{6,3},{7,2},{8,13},{9,12},{10,... | collective-permute-start | bytes 49160 | tf_op jit(solution)/shard_map/ppermute | solution.py:336
  28.7 1.2 %collective-permute-start.12 = (bf16[1,32,128]{2,1,0:T(8,128)(2,1)S(1)}, bf16[1,32,128]{2,1,0:T(8,128)(2,1)S(1)}, u32[]{:S(2)}, u32[]{:S(2)}) collective-permute-start(bf16[1,32,128]{2,1,0:T(8,128)(2,1)S(1)} %collective-permute-done.7), channel_id=1, source_target_pairs={{0,1},{1,0},{2,3},{3,2},{4,5},{5,4},{6,7},{7,6},{8,9},{9,8},{10,11... | collective-permute-start | bytes 24584 | tf_op jit(solution)/shard_map/ppermute | solution.py:331
  32.8 1.2 %collective-permute-start.13 = (f32[4,2048]{1,0:T(4,128)S(1)}, f32[4,2048]{1,0:T(4,128)S(1)}, u32[]{:S(2)}, u32[]{:S(2)}) collective-permute-start(f32[4,2048]{1,0:T(4,128)S(1)} %get-tuple-element.24), channel_id=1, source_target_pairs={{0,1},{1,0},{2,3},{3,2},{4,5},{5,4},{6,7},{7,6},{8,9},{9,8},{10,11... | collective-permute-start | bytes 98312 | tf_op jit(solution)/shard_map/ppermute | solution.py:331

commit v26 on v24

--- a/solution.py
+++ b/solution.py
@@ -339,7 +339,7 @@
 def fan(pieces, trade):
     masks = [bit_reverse(q, 2) for q in range(FAN)]
     arrived = [None] * FAN
-    for q in sorted(range(1, FAN), key=lambda q: (masks[q] + 1) % FAN):
+    for q in sorted(range(1, FAN), key=lambda q: -masks[q]):
         arrived[q] = trade(pieces[q], masks[q])
     return arrived[1:]
 
@@ -364,10 +364,10 @@
         turn, live = turning(lengths, frequency, w_out, pieces[3], k_cache.shape[2])
         leaving = [x[1:] for x in (*arrived, beside)]
         staying = [x[:1] for x in (*arrived, beside)]
-        total = leaving[2] + (leaving[1] + (leaving[0] + leaving[3]))
+        total = leaving[2] + (leaving[0] + (leaving[1] + leaving[3]))
         total, turn = lax.optimization_barrier((total, turn))
         crossed = cross(total, devices, far)
-        beside = swap(staying[2] + (staying[1] + (staying[0] + staying[3])), "gy", 2, 1)
+        beside = swap(staying[2] + (staying[0] + (staying[1] + staying[3])), "gy", 2, 1)
         parts = [crossed, beside]
         heads = attend(parts, turn, live, k_cache, value_cache, query_heads, w_out)
         crossed = cross(heads, devices, far)
@@ -375,7 +375,7 @@
         held = jnp.concatenate([crossed, beside], axis=0)
         arrived = fan([held] * FAN, lambda block, mask: cross(block, devices, mask))
         parts = [heads, swap(crossed, "gy", 2, 1)] + arrived
-        order, turned = (2, 4, 3, 1, 0), -1
+        order, turned = (3, 4, 2, 1, 0), -1
     else:
         arrived = fan(pieces, lambda block, mask: swap(block, "gx", devices, mask))
         turn, live = turning(lengths, frequency, w_out, pieces[3], k_cache.shape[2])

time: 34.6 us -> 34.3 us (level)
    ppermute x6, starting transfers between devices: 1.53 us -> 1.89 us  [swap(): return lax.ppermute(block, axis, [(i, i ^ mask) for i in range(devices)])]
  transfers between devices with their start and end apart: 14 -> 14, of which waited for: 8 -> 9; matrix products, arithmetic and copies ran while one was open for 0% -> 0% of each run, Pallas kernels for 6% -> 6%
where the time goes in v26:
time: 34.3 us; the launch traced here: 34.1 us
  starting transfers between devices  14 us (41%)
  Pallas kernels  10.6 us (31%)
  waiting for transfers between devices  8.01 us (23%)
  between operations  0.81 us (2%)
  other arithmetic  0.71 us (2%)
    ppermute x8, starting transfers between devices, cross(): return lax.ppermute(block, ('gx', 'gy'), pairs)  12.1 us
    ppermute x8, waiting for transfers between devices, cross(): return lax.ppermute(block, ('gx', 'gy'), pairs)  6.11 us
    pallas_call x1, Pallas kernels, project(): pl.pallas_call(functools.partial(project_kernel, bits), out_shape=(piece,...  5.41 us
    pallas_call x1, Pallas kernels, output(): pl.pallas_call(functools.partial(output_kernel, bits, places, turned), ou...  2.28 us
    pallas_call x1, Pallas kernels, stage_rows(): pl.pallas_call(functools.partial(stage_kernel, rows), out_shape=jax.Shape...  2.01 us
    ppermute x6, waiting for transfers between devices, swap(): return lax.ppermute(block, axis, [(i, i ^ mask) for i in range(devices)])  1.9 us
    ppermute x6, starting transfers between devices, swap(): return lax.ppermute(block, axis, [(i, i ^ mask) for i in range(devices)])  1.89 us
    pallas_call x1, Pallas kernels, attend(): pl.pallas_call(functools.partial(attend_kernel, query_heads, kv_heads, le...  0.82 us
  transfers between devices with their start and end apart: 14, of which 9 were waited for; matrix products, arithmetic and copies ran while one was open for 0% of the time, Pallas kernels for 6%

profile of v26, /device:TPU:0, one launch (start us, length us, event | category | flops | bytes accessed | tf_op | source)
XLA Modules:
  0.0 34.1 jit_solution(11771344063439928306)
XLA Ops:
  0.0 0.5 %collective-permute-start = (bf16[4,2048]{1,0:T(4,128)(2,1)}, bf16[4,2048]{1,0:T(4,128)(2,1)S(1)}, u32[]{:S(2)}, u32[]{:S(2)}) collective-permute-start(bf16[4,2048]{1,0:T(4,128)(2,1)} %rows_ref.1), channel_id=1, source_target_pairs={{0,1},{1,0},{2,3},{3,2},{4,5},{5,4},{6,7},{7,6},{8,9},{9,8},{10,11... | collective-permute-start | bytes 49160 | tf_op jit(solution)/shard_map/ppermute | solution.py:331
  0.5 2.0 %stage.1.first = bf16[384,4096]{1,0:T(8,128)(2,1)S(1)} custom-call(bf16[2048,4096]{1,0:T(8,128)(2,1)} %wq_hbm.1), custom_call_target="tpu_custom_call" | custom-call | bytes 3145728 | tf_op jit(solution)/shard_map/stage/pallas_call | solution.py:57
  2.6 5.4 %project.1 = (f32[2,40,128]{2,1,0:T(8,128)S(1)}, f32[2,40,128]{2,1,0:T(8,128)S(1)}, f32[2,40,128]{2,1,0:T(8,128)S(1)}, f32[2,40,128]{2,1,0:T(8,128)S(1)}) custom-call(bf16[4,2048]{1,0:T(4,128)(2,1)S(1)} %copy-done.4, bf16[4,2048]{1,0:T(4,128)(2,1)S(1)} %collective-permute-done.other_ref, bf16[2048,4096]{1,0:T(8,128)(2,1)} %wq_hbm.1, ...), custom_call_target="tpu_custom_call" | custom-call | flops 150994944 | bytes 18874368 | tf_op jit(solution)/shard_map/project/pallas_call | solution.py:179
  8.0 3.6 %collective-permute-start.1 = (f32[2,40,128]{2,1,0:T(8,128)S(1)}, f32[2,40,128]{2,1,0:T(8,128)S(1)}, u32[]{:S(2)}, u32[]{:S(2)}) collective-permute-start(f32[2,40,128]{2,1,0:T(8,128)S(1)} %get-tuple-element.15.after_ref), channel_id=1, source_target_pairs={{0,7},{1,6},{2,5},{3,4},{4,3},{5,2},{6,1},{7,0},{8,15},{9,14},{10,... | collective-permute-start | bytes 122888 | tf_op jit(solution)/shard_map/ppermute | solution.py:336
  11.6 0.6 %collective-permute-start.2 = (f32[2,40,128]{2,1,0:T(8,128)S(1)}, f32[2,40,128]{2,1,0:T(8,128)S(1)}, u32[]{:S(2)}, u32[]{:S(2)}) collective-permute-start(f32[2,40,128]{2,1,0:T(8,128)S(1)} %get-tuple-element.16), channel_id=1, source_target_pairs={{0,5},{1,4},{2,7},{3,6},{4,1},{5,0},{6,3},{7,2},{8,13},{9,12},{10,... | collective-permute-start | bytes 122888 | tf_op jit(solution)/shard_map/ppermute | solution.py:336
  12.2 0.2 collective-permute-start.3
  13.2 0.4 %collective-permute-done.1 = f32[2,40,128]{2,1,0:T(8,128)S(1)} collective-permute-done((f32[2,40,128]{2,1,0:T(8,128)S(1)}, f32[2,40,128]{2,1,0:T(8,128)S(1)}, u32[]{:S(2)}, u32[]{:S(2)}) %collective-permute-start.1) | collective-permute-done | bytes 40992 | tf_op jit(solution)/shard_map/ppermute | solution.py:336
  13.6 1.5 %collective-permute-done.2 = f32[2,40,128]{2,1,0:T(8,128)S(1)} collective-permute-done((f32[2,40,128]{2,1,0:T(8,128)S(1)}, f32[2,40,128]{2,1,0:T(8,128)S(1)}, u32[]{:S(2)}, u32[]{:S(2)}) %collective-permute-start.2) | collective-permute-done | bytes 40992 | tf_op jit(solution)/shard_map/ppermute | solution.py:336
  15.0 0.8 %collective-permute-done.3 = f32[2,40,128]{2,1,0:T(8,128)S(1)} collective-permute-done((f32[2,40,128]{2,1,0:T(8,128)S(1)}, f32[2,40,128]{2,1,0:T(8,128)S(1)}, u32[]{:S(2)}, u32[]{:S(2)}) %collective-permute-start.3) | collective-permute-done | bytes 40992 | tf_op jit(solution)/shard_map/ppermute | solution.py:336
  15.9 2.4 %collective-permute-start.5 = (f32[1,40,128]{2,1,0:T(8,128)S(1)}, f32[1,40,128]{2,1,0:T(8,128)S(1)}, u32[]{:S(2)}, u32[]{:S(2)}) collective-permute-start(f32[1,40,128]{2,1,0:T(8,128)S(1)} %get-tuple-element.22), channel_id=1, source_target_pairs={{0,9},{1,8},{2,11},{3,10},{4,13},{5,12},{6,15},{7,14},{8,1},{9,0},... | collective-permute-start | bytes 61448 | tf_op jit(solution)/shard_map/ppermute | solution.py:336
  18.3 0.4 %collective-permute-start.6 = (f32[1,40,128]{2,1,0:T(8,128)S(1)}, f32[1,40,128]{2,1,0:T(8,128)S(1)}, u32[]{:S(2)}, u32[]{:S(2)}) collective-permute-start(f32[1,40,128]{2,1,0:T(8,128)S(1)} %get-tuple-element.25), channel_id=1, source_target_pairs={{0,1},{1,0},{2,3},{3,2},{4,5},{5,4},{6,7},{7,6},{8,9},{9,8},{10,11... | collective-permute-start | bytes 61448 | tf_op jit(solution)/shard_map/ppermute | solution.py:331
  18.7 1.4 %collective-permute-done.5.refs_0_ = f32[1,40,128]{2,1,0:T(8,128)S(1)} collective-permute-done((f32[1,40,128]{2,1,0:T(8,128)S(1)}, f32[1,40,128]{2,1,0:T(8,128)S(1)}, u32[]{:S(2)}, u32[]{:S(2)}) %collective-permute-start.5) | collective-permute-done | bytes 20512 | tf_op jit(solution)/shard_map/ppermute | solution.py:336
  20.1 0.8 %attend.1.refs_4_ = bf16[1,32,128]{2,1,0:T(8,128)(2,1)S(1)} custom-call(bf16[4096,2048]{1,0:T(8,128)(2,1)} %refs_5_.1, f32[8,128]{1,0:T(8,128)S(1)} %get-tuple-element.20.turn_ref, f32[1,2048]{1,0:T(1,128)S(1)} %get-tuple-element.21.live_ref, bf16[1,2,2048,128]{3,2,1,0:T(8,128)(2,1)S(1)} %copy-done, bf16[1,2,2048,128]{3,2,1,0:T(8,128)(2,1)S(1)} %copy-done.1, ...), custom_call_target="tpu_custom_call" | custom-call | flops 33554432 | bytes 2097152 | tf_op jit(solution)/shard_map/attend/pallas_call | solution.py:266
  20.9 2.4 %collective-permute-start.7 = (bf16[1,32,128]{2,1,0:T(8,128)(2,1)S(1)}, bf16[1,32,128]{2,1,0:T(8,128)(2,1)S(1)}, u32[]{:S(2)}, u32[]{:S(2)}) collective-permute-start(bf16[1,32,128]{2,1,0:T(8,128)(2,1)S(1)} %attend.1.refs_4_), channel_id=1, source_target_pairs={{0,9},{1,8},{2,11},{3,10},{4,13},{5,12},{6,15},{7,14},{8,1},{9,0},... | collective-permute-start | bytes 24584 | tf_op jit(solution)/shard_map/ppermute | solution.py:336
  23.3 0.4 %collective-permute-start.8 = (bf16[1,32,128]{2,1,0:T(8,128)(2,1)S(1)}, bf16[1,32,128]{2,1,0:T(8,128)(2,1)S(1)}, u32[]{:S(2)}, u32[]{:S(2)}) collective-permute-start(bf16[1,32,128]{2,1,0:T(8,128)(2,1)S(1)} %attend.1.refs_4_), channel_id=1, source_target_pairs={{0,1},{1,0},{2,3},{3,2},{4,5},{5,4},{6,7},{7,6},{8,9},{9,8},{10,11... | collective-permute-start | bytes 24584 | tf_op jit(solution)/shard_map/ppermute | solution.py:331
  23.7 1.3 %collective-permute-done.7 = bf16[1,32,128]{2,1,0:T(8,128)(2,1)S(1)} collective-permute-done((bf16[1,32,128]{2,1,0:T(8,128)(2,1)S(1)}, bf16[1,32,128]{2,1,0:T(8,128)(2,1)S(1)}, u32[]{:S(2)}, u32[]{:S(2)}) %collective-permute-start.7) | collective-permute-done | bytes 8224 | tf_op jit(solution)/shard_map/ppermute | solution.py:336
  25.0 1.8 %collective-permute-start.10 = (bf16[2,32,128]{2,1,0:T(8,128)(2,1)S(1)}, bf16[2,32,128]{2,1,0:T(8,128)(2,1)S(1)}, u32[]{:S(2)}, u32[]{:S(2)}) collective-permute-start(bf16[2,32,128]{2,1,0:T(8,128)(2,1)S(1)} %constant_dynamic-update-slice_fusion), channel_id=1, source_target_pairs={{0,7},{1,6},{2,5},{3,4},{4,3},{5,2},{6,1},{7,0},{8,15},{9,14},{10,... | collective-permute-start | bytes 49160 | tf_op jit(solution)/shard_map/ppermute | solution.py:336
  26.8 1.1 %collective-permute-start.9 = (bf16[2,32,128]{2,1,0:T(8,128)(2,1)S(1)}, bf16[2,32,128]{2,1,0:T(8,128)(2,1)S(1)}, u32[]{:S(2)}, u32[]{:S(2)}) collective-permute-start(bf16[2,32,128]{2,1,0:T(8,128)(2,1)S(1)} %constant_dynamic-update-slice_fusion), channel_id=1, source_target_pairs={{0,3},{1,2},{2,1},{3,0},{4,7},{5,6},{6,5},{7,4},{8,11},{9,10},{10,... | collective-permute-start | bytes 49160 | tf_op jit(solution)/shard_map/ppermute | solution.py:336
  28.0 0.4 %collective-permute-start.12 = (bf16[1,32,128]{2,1,0:T(8,128)(2,1)S(1)}, bf16[1,32,128]{2,1,0:T(8,128)(2,1)S(1)}, u32[]{:S(2)}, u32[]{:S(2)}) collective-permute-start(bf16[1,32,128]{2,1,0:T(8,128)(2,1)S(1)} %collective-permute-done.7), channel_id=1, source_target_pairs={{0,1},{1,0},{2,3},{3,2},{4,5},{5,4},{6,7},{7,6},{8,9},{9,8},{10,11... | collective-permute-start | bytes 24584 | tf_op jit(solution)/shard_map/ppermute | solution.py:331
  28.4 0.8 %collective-permute-done.12.refs_3_ = bf16[1,32,128]{2,1,0:T(8,128)(2,1)S(1)} collective-permute-done((bf16[1,32,128]{2,1,0:T(8,128)(2,1)S(1)}, bf16[1,32,128]{2,1,0:T(8,128)(2,1)S(1)}, u32[]{:S(2)}, u32[]{:S(2)}) %collective-permute-start.12) | collective-permute-done | bytes 8224 | tf_op jit(solution)/shard_map/ppermute | solution.py:331
  29.2 0.7 %collective-permute-done.11.refs_2_ = bf16[2,32,128]{2,1,0:T(8,128)(2,1)S(1)} collective-permute-done((bf16[2,32,128]{2,1,0:T(8,128)(2,1)S(1)}, bf16[2,32,128]{2,1,0:T(8,128)(2,1)S(1)}, u32[]{:S(2)}, u32[]{:S(2)}) %collective-permute-start.11) | collective-permute-done | bytes 16416 | tf_op jit(solution)/shard_map/ppermute | solution.py:336
  30.0 2.3 %output.1 = (f32[4,2048]{1,0:T(4,128)S(1)}, f32[4,2048]{1,0:T(4,128)S(1)}) custom-call(bf16[2,32,128]{2,1,0:T(8,128)(2,1)S(1)} %collective-permute-done.9.refs_0_, bf16[2,32,128]{2,1,0:T(8,128)(2,1)S(1)} %collective-permute-done.10.refs_1_, bf16[2,32,128]{2,1,0:T(8,128)(2,1)S(1)} %collective-permute-done.11.refs_2_, ...), custom_call_target="tpu_custom_call" | custom-call | flops 134217728 | bytes 16777216 | tf_op jit(solution)/shard_map/output/pallas_call | solution.py:313
  32.5 1.1 %collective-permute-done.13 = f32[4,2048]{1,0:T(4,128)S(1)} collective-permute-done((f32[4,2048]{1,0:T(4,128)S(1)}, f32[4,2048]{1,0:T(4,128)S(1)}, u32[]{:S(2)}, u32[]{:S(2)}) %collective-permute-start.13) | collective-permute-done | bytes 32800 | tf_op jit(solution)/shard_map/ppermute | solution.py:331
  33.5 0.6 %add_convert_fusion = bf16[4,2048]{1,0:T(4,128)(2,1)} fusion(f32[4,2048]{1,0:T(4,128)S(1)} %get-tuple-element.23, f32[4,2048]{1,0:T(4,128)S(1)} %collective-permute-done.13), kind=kLoop, calls=%fused_computation | loop fusion | flops 16384 | bytes 81920 | tf_op jit(solution)/shard_map/convert_element_type | solution.py:399
  (34 shorter events, 0.5 us)
Async XLA Ops:
  0.0 2.6 %copy-start.4 = (bf16[4,2048]{1,0:T(4,128)(2,1)S(1)}, bf16[4,2048]{1,0:T(4,128)(2,1)}, u32[]{:S(2)}) copy-start(bf16[4,2048]{1,0:T(4,128)(2,1)} %rows_ref.1) | copy-start | bytes 49156
  0.0 2.6 %copy-start.2 = (bf16[2048,256]{1,0:T(8,128)(2,1)S(1)}, bf16[2048,256]{1,0:T(8,128)(2,1)}, u32[]{:S(2)}) copy-start(bf16[2048,256]{1,0:T(8,128)(2,1)} %wk.1) | copy-start | bytes 3145732
  0.0 2.6 %copy-start.3 = (bf16[2048,256]{1,0:T(8,128)(2,1)S(1)}, bf16[2048,256]{1,0:T(8,128)(2,1)}, u32[]{:S(2)}) copy-start(bf16[2048,256]{1,0:T(8,128)(2,1)} %wv.1) | copy-start | bytes 3145732
  0.0 2.6 %collective-permute-start = (bf16[4,2048]{1,0:T(4,128)(2,1)}, bf16[4,2048]{1,0:T(4,128)(2,1)S(1)}, u32[]{:S(2)}, u32[]{:S(2)}) collective-permute-start(bf16[4,2048]{1,0:T(4,128)(2,1)} %rows_ref.1), channel_id=1, source_target_pairs={{0,1},{1,0},{2,3},{3,2},{4,5},{5,4},{6,7},{7,6},{8,9},{9,8},{10,11... | collective-permute-start | bytes 49160 | tf_op jit(solution)/shard_map/ppermute | solution.py:331
  2.6 17.5 %copy-start = (bf16[1,2,2048,128]{3,2,1,0:T(8,128)(2,1)S(1)}, bf16[1,2,2048,128]{3,2,1,0:T(8,128)(2,1)}, u32[]{:S(2)}) copy-start(bf16[1,2,2048,128]{3,2,1,0:T(8,128)(2,1)} %k_ref.1) | copy-start | bytes 3145732
  2.6 17.5 %copy-start.1 = (bf16[1,2,2048,128]{3,2,1,0:T(8,128)(2,1)S(1)}, bf16[1,2,2048,128]{3,2,1,0:T(8,128)(2,1)}, u32[]{:S(2)}) copy-start(bf16[1,2,2048,128]{3,2,1,0:T(8,128)(2,1)} %v_ref.1) | copy-start | bytes 3145732
  8.0 5.5 %collective-permute-start.1 = (f32[2,40,128]{2,1,0:T(8,128)S(1)}, f32[2,40,128]{2,1,0:T(8,128)S(1)}, u32[]{:S(2)}, u32[]{:S(2)}) collective-permute-start(f32[2,40,128]{2,1,0:T(8,128)S(1)} %get-tuple-element.15.after_ref), channel_id=1, source_target_pairs={{0,7},{1,6},{2,5},{3,4},{4,3},{5,2},{6,1},{7,0},{8,15},{9,14},{10,... | collective-permute-start | bytes 122888 | tf_op jit(solution)/shard_map/ppermute | solution.py:336
  11.6 3.4 %collective-permute-start.2 = (f32[2,40,128]{2,1,0:T(8,128)S(1)}, f32[2,40,128]{2,1,0:T(8,128)S(1)}, u32[]{:S(2)}, u32[]{:S(2)}) collective-permute-start(f32[2,40,128]{2,1,0:T(8,128)S(1)} %get-tuple-element.16), channel_id=1, source_target_pairs={{0,5},{1,4},{2,7},{3,6},{4,1},{5,0},{6,3},{7,2},{8,13},{9,12},{10,... | collective-permute-start | bytes 122888 | tf_op jit(solution)/shard_map/ppermute | solution.py:336
  12.2 3.7 %collective-permute-start.3 = (f32[2,40,128]{2,1,0:T(8,128)S(1)}, f32[2,40,128]{2,1,0:T(8,128)S(1)}, u32[]{:S(2)}, u32[]{:S(2)}) collective-permute-start(f32[2,40,128]{2,1,0:T(8,128)S(1)} %get-tuple-element.17), channel_id=1, source_target_pairs={{0,3},{1,2},{2,1},{3,0},{4,7},{5,6},{6,5},{7,4},{8,11},{9,10},{10,... | collective-permute-start | bytes 122888 | tf_op jit(solution)/shard_map/ppermute | solution.py:336
  12.4 3.5 %collective-permute-start.4 = (f32[2,40,128]{2,1,0:T(8,128)S(1)}, f32[2,40,128]{2,1,0:T(8,128)S(1)}, u32[]{:S(2)}, u32[]{:S(2)}) collective-permute-start(f32[2,40,128]{2,1,0:T(8,128)S(1)} %get-tuple-element.18), channel_id=1, source_target_pairs={{0,1},{1,0},{2,3},{3,2},{4,5},{5,4},{6,7},{7,6},{8,9},{9,8},{10,11... | collective-permute-start | bytes 122888 | tf_op jit(solution)/shard_map/ppermute | solution.py:331
  13.1 16.9 %slice-start = ((s8[16777216]{0:T(1024)(128)(4,1)}), s8[4194304]{0:T(1024)(128)(4,1)S(1)}, s32[]{:S(2)}) async-start(s8[16777216]{0:T(1024)(128)(4,1)} %bitcast.2), calls=%async_computation | async-start | bytes 8388608
  13.1 16.9 %slice-start.1 = ((s8[16777216]{0:T(1024)(128)(4,1)}), s8[4194304]{0:T(1024)(128)(4,1)S(1)}, s32[]{:S(2)}) async-start(s8[16777216]{0:T(1024)(128)(4,1)} %bitcast.2), calls=%async_computation.1 | async-start | bytes 8388608
  15.9 4.2 %collective-permute-start.5 = (f32[1,40,128]{2,1,0:T(8,128)S(1)}, f32[1,40,128]{2,1,0:T(8,128)S(1)}, u32[]{:S(2)}, u32[]{:S(2)}) collective-permute-start(f32[1,40,128]{2,1,0:T(8,128)S(1)} %get-tuple-element.22), channel_id=1, source_target_pairs={{0,9},{1,8},{2,11},{3,10},{4,13},{5,12},{6,15},{7,14},{8,1},{9,0},... | collective-permute-start | bytes 61448 | tf_op jit(solution)/shard_map/ppermute | solution.py:336
  18.3 1.8 %collective-permute-start.6 = (f32[1,40,128]{2,1,0:T(8,128)S(1)}, f32[1,40,128]{2,1,0:T(8,128)S(1)}, u32[]{:S(2)}, u32[]{:S(2)}) collective-permute-start(f32[1,40,128]{2,1,0:T(8,128)S(1)} %get-tuple-element.25), channel_id=1, source_target_pairs={{0,1},{1,0},{2,3},{3,2},{4,5},{5,4},{6,7},{7,6},{8,9},{9,8},{10,11... | collective-permute-start | bytes 61448 | tf_op jit(solution)/shard_map/ppermute | solution.py:331
  20.1 9.9 %slice-start.2 = ((s8[16777216]{0:T(1024)(128)(4,1)}), s8[4194304]{0:T(1024)(128)(4,1)S(1)}, s32[]{:S(2)}) async-start(s8[16777216]{0:T(1024)(128)(4,1)} %bitcast.2), calls=%async_computation.2 | async-start | bytes 8388608
  20.1 9.9 %slice-start.3 = ((s8[16777216]{0:T(1024)(128)(4,1)}), s8[4194304]{0:T(1024)(128)(4,1)S(1)}, s32[]{:S(2)}) async-start(s8[16777216]{0:T(1024)(128)(4,1)} %bitcast.2), calls=%async_computation.3 | async-start | bytes 8388608
  20.9 4.0 %collective-permute-start.7 = (bf16[1,32,128]{2,1,0:T(8,128)(2,1)S(1)}, bf16[1,32,128]{2,1,0:T(8,128)(2,1)S(1)}, u32[]{:S(2)}, u32[]{:S(2)}) collective-permute-start(bf16[1,32,128]{2,1,0:T(8,128)(2,1)S(1)} %attend.1.refs_4_), channel_id=1, source_target_pairs={{0,9},{1,8},{2,11},{3,10},{4,13},{5,12},{6,15},{7,14},{8,1},{9,0},... | collective-permute-start | bytes 24584 | tf_op jit(solution)/shard_map/ppermute | solution.py:336
  23.3 1.6 %collective-permute-start.8 = (bf16[1,32,128]{2,1,0:T(8,128)(2,1)S(1)}, bf16[1,32,128]{2,1,0:T(8,128)(2,1)S(1)}, u32[]{:S(2)}, u32[]{:S(2)}) collective-permute-start(bf16[1,32,128]{2,1,0:T(8,128)(2,1)S(1)} %attend.1.refs_4_), channel_id=1, source_target_pairs={{0,1},{1,0},{2,3},{3,2},{4,5},{5,4},{6,7},{7,6},{8,9},{9,8},{10,11... | collective-permute-start | bytes 24584 | tf_op jit(solution)/shard_map/ppermute | solution.py:331
  25.0 4.3 %collective-permute-start.10 = (bf16[2,32,128]{2,1,0:T(8,128)(2,1)S(1)}, bf16[2,32,128]{2,1,0:T(8,128)(2,1)S(1)}, u32[]{:S(2)}, u32[]{:S(2)}) collective-permute-start(bf16[2,32,128]{2,1,0:T(8,128)(2,1)S(1)} %constant_dynamic-update-slice_fusion), channel_id=1, source_target_pairs={{0,7},{1,6},{2,5},{3,4},{4,3},{5,2},{6,1},{7,0},{8,15},{9,14},{10,... | collective-permute-start | bytes 49160 | tf_op jit(solution)/shard_map/ppermute | solution.py:336
  26.8 3.2 %collective-permute-start.11 = (bf16[2,32,128]{2,1,0:T(8,128)(2,1)S(1)}, bf16[2,32,128]{2,1,0:T(8,128)(2,1)S(1)}, u32[]{:S(2)}, u32[]{:S(2)}) collective-permute-start(bf16[2,32,128]{2,1,0:T(8,128)(2,1)S(1)} %constant_dynamic-update-slice_fusion), channel_id=1, source_target_pairs={{0,5},{1,4},{2,7},{3,6},{4,1},{5,0},{6,3},{7,2},{8,13},{9,12},{10,... | collective-permute-start | bytes 49160 | tf_op jit(solution)/shard_map/ppermute | solution.py:336
  26.8 3.2 %collective-permute-start.9 = (bf16[2,32,128]{2,1,0:T(8,128)(2,1)S(1)}, bf16[2,32,128]{2,1,0:T(8,128)(2,1)S(1)}, u32[]{:S(2)}, u32[]{:S(2)}) collective-permute-start(bf16[2,32,128]{2,1,0:T(8,128)(2,1)S(1)} %constant_dynamic-update-slice_fusion), channel_id=1, source_target_pairs={{0,3},{1,2},{2,1},{3,0},{4,7},{5,6},{6,5},{7,4},{8,11},{9,10},{10,... | collective-permute-start | bytes 49160 | tf_op jit(solution)/shard_map/ppermute | solution.py:336
  28.0 1.3 %collective-permute-start.12 = (bf16[1,32,128]{2,1,0:T(8,128)(2,1)S(1)}, bf16[1,32,128]{2,1,0:T(8,128)(2,1)S(1)}, u32[]{:S(2)}, u32[]{:S(2)}) collective-permute-start(bf16[1,32,128]{2,1,0:T(8,128)(2,1)S(1)} %collective-permute-done.7), channel_id=1, source_target_pairs={{0,1},{1,0},{2,3},{3,2},{4,5},{5,4},{6,7},{7,6},{8,9},{9,8},{10,11... | collective-permute-start | bytes 24584 | tf_op jit(solution)/shard_map/ppermute | solution.py:331
  32.3 1.2 %collective-permute-start.13 = (f32[4,2048]{1,0:T(4,128)S(1)}, f32[4,2048]{1,0:T(4,128)S(1)}, u32[]{:S(2)}, u32[]{:S(2)}) collective-permute-start(f32[4,2048]{1,0:T(4,128)S(1)} %get-tuple-element.24), channel_id=1, source_target_pairs={{0,1},{1,0},{2,3},{3,2},{4,5},{5,4},{6,7},{7,6},{8,9},{9,8},{10,11... | collective-permute-start | bytes 98312 | tf_op jit(solution)/shard_map/ppermute | solution.py:331

commit v27 on v26

--- a/solution.py
+++ b/solution.py
@@ -68,7 +68,9 @@
     )(in_hbm(array))
 
 
-def turning_kernel(length_ref, frequency_ref, beside_ref, after_ref, turn_ref, mask_ref):
+def turning_kernel(
+    length_ref, frequency_ref, beside_ref, more_ref, after_ref, turn_ref, mask_ref
+):
     position = length_ref[0].astype(jnp.float32)
     angle = position * frequency_ref[...]
     lane = lax.broadcasted_iota(jnp.int32, angle.shape, 1)
@@ -79,7 +81,7 @@
     mask_ref[...] = jnp.where(slot < length_ref[0], 0.0, -jnp.inf)
 
 
-def turning(lengths, frequency, beside, after, cache_len):
+def turning(lengths, frequency, beside, more, after, cache_len):
     vmem = pl.BlockSpec(memory_space=pltpu.VMEM)
     return pl.pallas_call(
         turning_kernel,
@@ -91,13 +93,14 @@
             pl.BlockSpec(memory_space=pltpu.SMEM),
             vmem,
             pl.BlockSpec(memory_space=pltpu.HBM),
+            pl.BlockSpec(memory_space=pltpu.HBM),
             vmem,
         ],
         out_specs=(vmem, vmem),
         compiler_params=pltpu.CompilerParams(vmem_limit_bytes=2 * MIB),
         cost_estimate=pl.CostEstimate(flops=0, bytes_accessed=2 * beside.size, transcendentals=256),
         name="turning",
-    )(lengths, frequency, in_hbm(beside), after)
+    )(lengths, frequency, in_hbm(beside), in_hbm(more), after)
 
 
 def spread(depth, skip, chunk):
@@ -361,7 +364,7 @@
         far = FAN
         arrived = fan(pieces, lambda block, mask: cross(block, devices, mask))
         beside = swap(pieces[0], "gy", 2, 1)
-        turn, live = turning(lengths, frequency, w_out, pieces[3], k_cache.shape[2])
+        turn, live = turning(lengths, frequency, w_out, w_query, pieces[3], k_cache.shape[2])
         leaving = [x[1:] for x in (*arrived, beside)]
         staying = [x[:1] for x in (*arrived, beside)]
         total = leaving[2] + (leaving[0] + (leaving[1] + leaving[3]))
@@ -378,7 +381,7 @@
         order, turned = (3, 4, 2, 1, 0), -1
     else:
         arrived = fan(pieces, lambda block, mask: swap(block, "gx", devices, mask))
-        turn, live = turning(lengths, frequency, w_out, pieces[3], k_cache.shape[2])
+        turn, live = turning(lengths, frequency, w_out, w_query, pieces[3], k_cache.shape[2])
         total = pieces[0] + (arrived[2] + (arrived[1] + arrived[0]))
         mask = FAN
         while total.shape[0] > 2:

time: 34.3 us -> 34.1 us (level)
  no operation moved by 1% of the time
where the time goes in v27:
time: 34.1 us; the launch traced here: 34 us
  starting transfers between devices  13.9 us (41%)
  Pallas kernels  10.4 us (30%)
  waiting for transfers between devices  8.02 us (24%)
  between operations  0.81 us (2%)
  other arithmetic  0.71 us (2%)
    ppermute x8, starting transfers between devices, cross(): return lax.ppermute(block, ('gx', 'gy'), pairs)  12.1 us
    ppermute x8, waiting for transfers between devices, cross(): return lax.ppermute(block, ('gx', 'gy'), pairs)  6.1 us
    pallas_call x1, Pallas kernels, project(): pl.pallas_call(functools.partial(project_kernel, bits), out_shape=(piece,...  5.29 us
    pallas_call x1, Pallas kernels, output(): pl.pallas_call(functools.partial(output_kernel, bits, places, turned), ou...  2.28 us
    pallas_call x1, Pallas kernels, stage_rows(): pl.pallas_call(functools.partial(stage_kernel, rows), out_shape=jax.Shape...  2.01 us
    ppermute x6, waiting for transfers between devices, swap(): return lax.ppermute(block, axis, [(i, i ^ mask) for i in range(devices)])  1.92 us
    ppermute x6, starting transfers between devices, swap(): return lax.ppermute(block, axis, [(i, i ^ mask) for i in range(devices)])  1.84 us
    pallas_call x1, Pallas kernels, attend(): pl.pallas_call(functools.partial(attend_kernel, query_heads, kv_heads, le...  0.82 us
  transfers between devices with their start and end apart: 14, of which 9 were waited for; matrix products, arithmetic and copies ran while one was open for 0% of the time, Pallas kernels for 6%

profile of v27, /device:TPU:0, one launch (start us, length us, event | category | flops | bytes accessed | tf_op | source)
XLA Modules:
  0.0 34.0 jit_solution(12947020513142007465)
XLA Ops:
  0.0 0.5 %collective-permute-start = (bf16[4,2048]{1,0:T(4,128)(2,1)}, bf16[4,2048]{1,0:T(4,128)(2,1)S(1)}, u32[]{:S(2)}, u32[]{:S(2)}) collective-permute-start(bf16[4,2048]{1,0:T(4,128)(2,1)} %rows_ref.1), channel_id=1, source_target_pairs={{0,1},{1,0},{2,3},{3,2},{4,5},{5,4},{6,7},{7,6},{8,9},{9,8},{10,11... | collective-permute-start | bytes 49160 | tf_op jit(solution)/shard_map/ppermute | solution.py:334
  0.5 2.0 %stage.1.first = bf16[384,4096]{1,0:T(8,128)(2,1)S(1)} custom-call(bf16[2048,4096]{1,0:T(8,128)(2,1)} %more_ref.1), custom_call_target="tpu_custom_call" | custom-call | bytes 3145728 | tf_op jit(solution)/shard_map/stage/pallas_call | solution.py:57
  2.6 5.3 %project.1 = (f32[2,40,128]{2,1,0:T(8,128)S(1)}, f32[2,40,128]{2,1,0:T(8,128)S(1)}, f32[2,40,128]{2,1,0:T(8,128)S(1)}, f32[2,40,128]{2,1,0:T(8,128)S(1)}) custom-call(bf16[4,2048]{1,0:T(4,128)(2,1)S(1)} %copy-done.4, bf16[4,2048]{1,0:T(4,128)(2,1)S(1)} %collective-permute-done.other_ref, bf16[2048,4096]{1,0:T(8,128)(2,1)} %more_ref.1, ...), custom_call_target="tpu_custom_call" | custom-call | flops 150994944 | bytes 18874368 | tf_op jit(solution)/shard_map/project/pallas_call | solution.py:182
  7.9 3.6 %collective-permute-start.1 = (f32[2,40,128]{2,1,0:T(8,128)S(1)}, f32[2,40,128]{2,1,0:T(8,128)S(1)}, u32[]{:S(2)}, u32[]{:S(2)}) collective-permute-start(f32[2,40,128]{2,1,0:T(8,128)S(1)} %get-tuple-element.15.after_ref), channel_id=1, source_target_pairs={{0,7},{1,6},{2,5},{3,4},{4,3},{5,2},{6,1},{7,0},{8,15},{9,14},{10,... | collective-permute-start | bytes 122888 | tf_op jit(solution)/shard_map/ppermute | solution.py:339
  11.5 0.5 %collective-permute-start.2 = (f32[2,40,128]{2,1,0:T(8,128)S(1)}, f32[2,40,128]{2,1,0:T(8,128)S(1)}, u32[]{:S(2)}, u32[]{:S(2)}) collective-permute-start(f32[2,40,128]{2,1,0:T(8,128)S(1)} %get-tuple-element.16), channel_id=1, source_target_pairs={{0,5},{1,4},{2,7},{3,6},{4,1},{5,0},{6,3},{7,2},{8,13},{9,12},{10,... | collective-permute-start | bytes 122888 | tf_op jit(solution)/shard_map/ppermute | solution.py:339
  12.0 0.2 collective-permute-start.3
  13.1 0.4 %collective-permute-done.1 = f32[2,40,128]{2,1,0:T(8,128)S(1)} collective-permute-done((f32[2,40,128]{2,1,0:T(8,128)S(1)}, f32[2,40,128]{2,1,0:T(8,128)S(1)}, u32[]{:S(2)}, u32[]{:S(2)}) %collective-permute-start.1) | collective-permute-done | bytes 40992 | tf_op jit(solution)/shard_map/ppermute | solution.py:339
  13.4 1.5 %collective-permute-done.2 = f32[2,40,128]{2,1,0:T(8,128)S(1)} collective-permute-done((f32[2,40,128]{2,1,0:T(8,128)S(1)}, f32[2,40,128]{2,1,0:T(8,128)S(1)}, u32[]{:S(2)}, u32[]{:S(2)}) %collective-permute-start.2) | collective-permute-done | bytes 40992 | tf_op jit(solution)/shard_map/ppermute | solution.py:339
  14.9 0.7 %collective-permute-done.3 = f32[2,40,128]{2,1,0:T(8,128)S(1)} collective-permute-done((f32[2,40,128]{2,1,0:T(8,128)S(1)}, f32[2,40,128]{2,1,0:T(8,128)S(1)}, u32[]{:S(2)}, u32[]{:S(2)}) %collective-permute-start.3) | collective-permute-done | bytes 40992 | tf_op jit(solution)/shard_map/ppermute | solution.py:339
  15.7 2.4 %collective-permute-start.5 = (f32[1,40,128]{2,1,0:T(8,128)S(1)}, f32[1,40,128]{2,1,0:T(8,128)S(1)}, u32[]{:S(2)}, u32[]{:S(2)}) collective-permute-start(f32[1,40,128]{2,1,0:T(8,128)S(1)} %get-tuple-element.22), channel_id=1, source_target_pairs={{0,9},{1,8},{2,11},{3,10},{4,13},{5,12},{6,15},{7,14},{8,1},{9,0},... | collective-permute-start | bytes 61448 | tf_op jit(solution)/shard_map/ppermute | solution.py:339
  18.0 0.4 %collective-permute-start.6 = (f32[1,40,128]{2,1,0:T(8,128)S(1)}, f32[1,40,128]{2,1,0:T(8,128)S(1)}, u32[]{:S(2)}, u32[]{:S(2)}) collective-permute-start(f32[1,40,128]{2,1,0:T(8,128)S(1)} %get-tuple-element.25), channel_id=1, source_target_pairs={{0,1},{1,0},{2,3},{3,2},{4,5},{5,4},{6,7},{7,6},{8,9},{9,8},{10,11... | collective-permute-start | bytes 61448 | tf_op jit(solution)/shard_map/ppermute | solution.py:334
  18.4 1.4 %collective-permute-done.5.refs_0_ = f32[1,40,128]{2,1,0:T(8,128)S(1)} collective-permute-done((f32[1,40,128]{2,1,0:T(8,128)S(1)}, f32[1,40,128]{2,1,0:T(8,128)S(1)}, u32[]{:S(2)}, u32[]{:S(2)}) %collective-permute-start.5) | collective-permute-done | bytes 20512 | tf_op jit(solution)/shard_map/ppermute | solution.py:339
  19.8 0.8 %attend.1.refs_4_ = bf16[1,32,128]{2,1,0:T(8,128)(2,1)S(1)} custom-call(bf16[4096,2048]{1,0:T(8,128)(2,1)} %refs_5_.1, f32[8,128]{1,0:T(8,128)S(1)} %get-tuple-element.20.turn_ref, f32[1,2048]{1,0:T(1,128)S(1)} %get-tuple-element.21.live_ref, bf16[1,2,2048,128]{3,2,1,0:T(8,128)(2,1)S(1)} %copy-done, bf16[1,2,2048,128]{3,2,1,0:T(8,128)(2,1)S(1)} %copy-done.1, ...), custom_call_target="tpu_custom_call" | custom-call | flops 33554432 | bytes 2097152 | tf_op jit(solution)/shard_map/attend/pallas_call | solution.py:269
  20.7 2.4 %collective-permute-start.7 = (bf16[1,32,128]{2,1,0:T(8,128)(2,1)S(1)}, bf16[1,32,128]{2,1,0:T(8,128)(2,1)S(1)}, u32[]{:S(2)}, u32[]{:S(2)}) collective-permute-start(bf16[1,32,128]{2,1,0:T(8,128)(2,1)S(1)} %attend.1.refs_4_), channel_id=1, source_target_pairs={{0,9},{1,8},{2,11},{3,10},{4,13},{5,12},{6,15},{7,14},{8,1},{9,0},... | collective-permute-start | bytes 24584 | tf_op jit(solution)/shard_map/ppermute | solution.py:339
  23.1 0.4 %collective-permute-start.8 = (bf16[1,32,128]{2,1,0:T(8,128)(2,1)S(1)}, bf16[1,32,128]{2,1,0:T(8,128)(2,1)S(1)}, u32[]{:S(2)}, u32[]{:S(2)}) collective-permute-start(bf16[1,32,128]{2,1,0:T(8,128)(2,1)S(1)} %attend.1.refs_4_), channel_id=1, source_target_pairs={{0,1},{1,0},{2,3},{3,2},{4,5},{5,4},{6,7},{7,6},{8,9},{9,8},{10,11... | collective-permute-start | bytes 24584 | tf_op jit(solution)/shard_map/ppermute | solution.py:334
  23.5 1.3 %collective-permute-done.7 = bf16[1,32,128]{2,1,0:T(8,128)(2,1)S(1)} collective-permute-done((bf16[1,32,128]{2,1,0:T(8,128)(2,1)S(1)}, bf16[1,32,128]{2,1,0:T(8,128)(2,1)S(1)}, u32[]{:S(2)}, u32[]{:S(2)}) %collective-permute-start.7) | collective-permute-done | bytes 8224 | tf_op jit(solution)/shard_map/ppermute | solution.py:339
  24.7 1.8 %collective-permute-start.10 = (bf16[2,32,128]{2,1,0:T(8,128)(2,1)S(1)}, bf16[2,32,128]{2,1,0:T(8,128)(2,1)S(1)}, u32[]{:S(2)}, u32[]{:S(2)}) collective-permute-start(bf16[2,32,128]{2,1,0:T(8,128)(2,1)S(1)} %constant_dynamic-update-slice_fusion), channel_id=1, source_target_pairs={{0,7},{1,6},{2,5},{3,4},{4,3},{5,2},{6,1},{7,0},{8,15},{9,14},{10,... | collective-permute-start | bytes 49160 | tf_op jit(solution)/shard_map/ppermute | solution.py:339
  26.7 1.1 %collective-permute-start.9 = (bf16[2,32,128]{2,1,0:T(8,128)(2,1)S(1)}, bf16[2,32,128]{2,1,0:T(8,128)(2,1)S(1)}, u32[]{:S(2)}, u32[]{:S(2)}) collective-permute-start(bf16[2,32,128]{2,1,0:T(8,128)(2,1)S(1)} %constant_dynamic-update-slice_fusion), channel_id=1, source_target_pairs={{0,3},{1,2},{2,1},{3,0},{4,7},{5,6},{6,5},{7,4},{8,11},{9,10},{10,... | collective-permute-start | bytes 49160 | tf_op jit(solution)/shard_map/ppermute | solution.py:339
  27.8 0.4 %collective-permute-start.12 = (bf16[1,32,128]{2,1,0:T(8,128)(2,1)S(1)}, bf16[1,32,128]{2,1,0:T(8,128)(2,1)S(1)}, u32[]{:S(2)}, u32[]{:S(2)}) collective-permute-start(bf16[1,32,128]{2,1,0:T(8,128)(2,1)S(1)} %collective-permute-done.7), channel_id=1, source_target_pairs={{0,1},{1,0},{2,3},{3,2},{4,5},{5,4},{6,7},{7,6},{8,9},{9,8},{10,11... | collective-permute-start | bytes 24584 | tf_op jit(solution)/shard_map/ppermute | solution.py:334
  28.1 0.8 %collective-permute-done.12.refs_3_ = bf16[1,32,128]{2,1,0:T(8,128)(2,1)S(1)} collective-permute-done((bf16[1,32,128]{2,1,0:T(8,128)(2,1)S(1)}, bf16[1,32,128]{2,1,0:T(8,128)(2,1)S(1)}, u32[]{:S(2)}, u32[]{:S(2)}) %collective-permute-start.12) | collective-permute-done | bytes 8224 | tf_op jit(solution)/shard_map/ppermute | solution.py:334
  29.0 0.8 %collective-permute-done.11.refs_2_ = bf16[2,32,128]{2,1,0:T(8,128)(2,1)S(1)} collective-permute-done((bf16[2,32,128]{2,1,0:T(8,128)(2,1)S(1)}, bf16[2,32,128]{2,1,0:T(8,128)(2,1)S(1)}, u32[]{:S(2)}, u32[]{:S(2)}) %collective-permute-start.11) | collective-permute-done | bytes 16416 | tf_op jit(solution)/shard_map/ppermute | solution.py:339
  29.9 2.3 %output.1 = (f32[4,2048]{1,0:T(4,128)S(1)}, f32[4,2048]{1,0:T(4,128)S(1)}) custom-call(bf16[2,32,128]{2,1,0:T(8,128)(2,1)S(1)} %collective-permute-done.9.refs_0_, bf16[2,32,128]{2,1,0:T(8,128)(2,1)S(1)} %collective-permute-done.10.refs_1_, bf16[2,32,128]{2,1,0:T(8,128)(2,1)S(1)} %collective-permute-done.11.refs_2_, ...), custom_call_target="tpu_custom_call" | custom-call | flops 134217728 | bytes 16777216 | tf_op jit(solution)/shard_map/output/pallas_call | solution.py:316
  32.3 1.1 %collective-permute-done.13 = f32[4,2048]{1,0:T(4,128)S(1)} collective-permute-done((f32[4,2048]{1,0:T(4,128)S(1)}, f32[4,2048]{1,0:T(4,128)S(1)}, u32[]{:S(2)}, u32[]{:S(2)}) %collective-permute-start.13) | collective-permute-done | bytes 32800 | tf_op jit(solution)/shard_map/ppermute | solution.py:334
  33.4 0.6 %add_convert_fusion = bf16[4,2048]{1,0:T(4,128)(2,1)} fusion(f32[4,2048]{1,0:T(4,128)S(1)} %get-tuple-element.23, f32[4,2048]{1,0:T(4,128)S(1)} %collective-permute-done.13), kind=kLoop, calls=%fused_computation | loop fusion | flops 16384 | bytes 81920 | tf_op jit(solution)/shard_map/convert_element_type | solution.py:402
  (34 shorter events, 0.6 us)
Async XLA Ops:
  0.0 2.6 %copy-start.4 = (bf16[4,2048]{1,0:T(4,128)(2,1)S(1)}, bf16[4,2048]{1,0:T(4,128)(2,1)}, u32[]{:S(2)}) copy-start(bf16[4,2048]{1,0:T(4,128)(2,1)} %rows_ref.1) | copy-start | bytes 49156
  0.0 2.6 %copy-start.2 = (bf16[2048,256]{1,0:T(8,128)(2,1)S(1)}, bf16[2048,256]{1,0:T(8,128)(2,1)}, u32[]{:S(2)}) copy-start(bf16[2048,256]{1,0:T(8,128)(2,1)} %wk.1) | copy-start | bytes 3145732
  0.0 2.6 %copy-start.3 = (bf16[2048,256]{1,0:T(8,128)(2,1)S(1)}, bf16[2048,256]{1,0:T(8,128)(2,1)}, u32[]{:S(2)}) copy-start(bf16[2048,256]{1,0:T(8,128)(2,1)} %wv.1) | copy-start | bytes 3145732
  0.0 2.5 %collective-permute-start = (bf16[4,2048]{1,0:T(4,128)(2,1)}, bf16[4,2048]{1,0:T(4,128)(2,1)S(1)}, u32[]{:S(2)}, u32[]{:S(2)}) collective-permute-start(bf16[4,2048]{1,0:T(4,128)(2,1)} %rows_ref.1), channel_id=1, source_target_pairs={{0,1},{1,0},{2,3},{3,2},{4,5},{5,4},{6,7},{7,6},{8,9},{9,8},{10,11... | collective-permute-start | bytes 49160 | tf_op jit(solution)/shard_map/ppermute | solution.py:334
  7.9 5.5 %collective-permute-start.1 = (f32[2,40,128]{2,1,0:T(8,128)S(1)}, f32[2,40,128]{2,1,0:T(8,128)S(1)}, u32[]{:S(2)}, u32[]{:S(2)}) collective-permute-start(f32[2,40,128]{2,1,0:T(8,128)S(1)} %get-tuple-element.15.after_ref), channel_id=1, source_target_pairs={{0,7},{1,6},{2,5},{3,4},{4,3},{5,2},{6,1},{7,0},{8,15},{9,14},{10,... | collective-permute-start | bytes 122888 | tf_op jit(solution)/shard_map/ppermute | solution.py:339
  11.5 3.4 %collective-permute-start.2 = (f32[2,40,128]{2,1,0:T(8,128)S(1)}, f32[2,40,128]{2,1,0:T(8,128)S(1)}, u32[]{:S(2)}, u32[]{:S(2)}) collective-permute-start(f32[2,40,128]{2,1,0:T(8,128)S(1)} %get-tuple-element.16), channel_id=1, source_target_pairs={{0,5},{1,4},{2,7},{3,6},{4,1},{5,0},{6,3},{7,2},{8,13},{9,12},{10,... | collective-permute-start | bytes 122888 | tf_op jit(solution)/shard_map/ppermute | solution.py:339
  12.0 3.6 %collective-permute-start.3 = (f32[2,40,128]{2,1,0:T(8,128)S(1)}, f32[2,40,128]{2,1,0:T(8,128)S(1)}, u32[]{:S(2)}, u32[]{:S(2)}) collective-permute-start(f32[2,40,128]{2,1,0:T(8,128)S(1)} %get-tuple-element.17), channel_id=1, source_target_pairs={{0,3},{1,2},{2,1},{3,0},{4,7},{5,6},{6,5},{7,4},{8,11},{9,10},{10,... | collective-permute-start | bytes 122888 | tf_op jit(solution)/shard_map/ppermute | solution.py:339
  12.2 3.5 %collective-permute-start.4 = (f32[2,40,128]{2,1,0:T(8,128)S(1)}, f32[2,40,128]{2,1,0:T(8,128)S(1)}, u32[]{:S(2)}, u32[]{:S(2)}) collective-permute-start(f32[2,40,128]{2,1,0:T(8,128)S(1)} %get-tuple-element.18), channel_id=1, source_target_pairs={{0,1},{1,0},{2,3},{3,2},{4,5},{5,4},{6,7},{7,6},{8,9},{9,8},{10,11... | collective-permute-start | bytes 122888 | tf_op jit(solution)/shard_map/ppermute | solution.py:334
  13.0 6.9 %copy-start = (bf16[1,2,2048,128]{3,2,1,0:T(8,128)(2,1)S(1)}, bf16[1,2,2048,128]{3,2,1,0:T(8,128)(2,1)}, u32[]{:S(2)}) copy-start(bf16[1,2,2048,128]{3,2,1,0:T(8,128)(2,1)} %k_ref.1) | copy-start | bytes 3145732
  13.0 6.9 %copy-start.1 = (bf16[1,2,2048,128]{3,2,1,0:T(8,128)(2,1)S(1)}, bf16[1,2,2048,128]{3,2,1,0:T(8,128)(2,1)}, u32[]{:S(2)}) copy-start(bf16[1,2,2048,128]{3,2,1,0:T(8,128)(2,1)} %v_ref.1) | copy-start | bytes 3145732
  13.0 16.9 %slice-start = ((s8[16777216]{0:T(1024)(128)(4,1)}), s8[4194304]{0:T(1024)(128)(4,1)S(1)}, s32[]{:S(2)}) async-start(s8[16777216]{0:T(1024)(128)(4,1)} %bitcast.2), calls=%async_computation | async-start | bytes 8388608
  13.0 16.8 %slice-start.1 = ((s8[16777216]{0:T(1024)(128)(4,1)}), s8[4194304]{0:T(1024)(128)(4,1)S(1)}, s32[]{:S(2)}) async-start(s8[16777216]{0:T(1024)(128)(4,1)} %bitcast.2), calls=%async_computation.1 | async-start | bytes 8388608
  13.0 16.8 %slice-start.2 = ((s8[16777216]{0:T(1024)(128)(4,1)}), s8[4194304]{0:T(1024)(128)(4,1)S(1)}, s32[]{:S(2)}) async-start(s8[16777216]{0:T(1024)(128)(4,1)} %bitcast.2), calls=%async_computation.2 | async-start | bytes 8388608
  15.7 4.2 %collective-permute-start.5 = (f32[1,40,128]{2,1,0:T(8,128)S(1)}, f32[1,40,128]{2,1,0:T(8,128)S(1)}, u32[]{:S(2)}, u32[]{:S(2)}) collective-permute-start(f32[1,40,128]{2,1,0:T(8,128)S(1)} %get-tuple-element.22), channel_id=1, source_target_pairs={{0,9},{1,8},{2,11},{3,10},{4,13},{5,12},{6,15},{7,14},{8,1},{9,0},... | collective-permute-start | bytes 61448 | tf_op jit(solution)/shard_map/ppermute | solution.py:339
  18.0 1.8 %collective-permute-start.6 = (f32[1,40,128]{2,1,0:T(8,128)S(1)}, f32[1,40,128]{2,1,0:T(8,128)S(1)}, u32[]{:S(2)}, u32[]{:S(2)}) collective-permute-start(f32[1,40,128]{2,1,0:T(8,128)S(1)} %get-tuple-element.25), channel_id=1, source_target_pairs={{0,1},{1,0},{2,3},{3,2},{4,5},{5,4},{6,7},{7,6},{8,9},{9,8},{10,11... | collective-permute-start | bytes 61448 | tf_op jit(solution)/shard_map/ppermute | solution.py:334
  19.8 10.0 %slice-start.3 = ((s8[16777216]{0:T(1024)(128)(4,1)}), s8[4194304]{0:T(1024)(128)(4,1)S(1)}, s32[]{:S(2)}) async-start(s8[16777216]{0:T(1024)(128)(4,1)} %bitcast.2), calls=%async_computation.3 | async-start | bytes 8388608
  20.7 4.0 %collective-permute-start.7 = (bf16[1,32,128]{2,1,0:T(8,128)(2,1)S(1)}, bf16[1,32,128]{2,1,0:T(8,128)(2,1)S(1)}, u32[]{:S(2)}, u32[]{:S(2)}) collective-permute-start(bf16[1,32,128]{2,1,0:T(8,128)(2,1)S(1)} %attend.1.refs_4_), channel_id=1, source_target_pairs={{0,9},{1,8},{2,11},{3,10},{4,13},{5,12},{6,15},{7,14},{8,1},{9,0},... | collective-permute-start | bytes 24584 | tf_op jit(solution)/shard_map/ppermute | solution.py:339
  23.1 1.6 %collective-permute-start.8 = (bf16[1,32,128]{2,1,0:T(8,128)(2,1)S(1)}, bf16[1,32,128]{2,1,0:T(8,128)(2,1)S(1)}, u32[]{:S(2)}, u32[]{:S(2)}) collective-permute-start(bf16[1,32,128]{2,1,0:T(8,128)(2,1)S(1)} %attend.1.refs_4_), channel_id=1, source_target_pairs={{0,1},{1,0},{2,3},{3,2},{4,5},{5,4},{6,7},{7,6},{8,9},{9,8},{10,11... | collective-permute-start | bytes 24584 | tf_op jit(solution)/shard_map/ppermute | solution.py:334
  24.7 4.2 %collective-permute-start.10 = (bf16[2,32,128]{2,1,0:T(8,128)(2,1)S(1)}, bf16[2,32,128]{2,1,0:T(8,128)(2,1)S(1)}, u32[]{:S(2)}, u32[]{:S(2)}) collective-permute-start(bf16[2,32,128]{2,1,0:T(8,128)(2,1)S(1)} %constant_dynamic-update-slice_fusion), channel_id=1, source_target_pairs={{0,7},{1,6},{2,5},{3,4},{4,3},{5,2},{6,1},{7,0},{8,15},{9,14},{10,... | collective-permute-start | bytes 49160 | tf_op jit(solution)/shard_map/ppermute | solution.py:339
  26.6 3.2 %collective-permute-start.11 = (bf16[2,32,128]{2,1,0:T(8,128)(2,1)S(1)}, bf16[2,32,128]{2,1,0:T(8,128)(2,1)S(1)}, u32[]{:S(2)}, u32[]{:S(2)}) collective-permute-start(bf16[2,32,128]{2,1,0:T(8,128)(2,1)S(1)} %constant_dynamic-update-slice_fusion), channel_id=1, source_target_pairs={{0,5},{1,4},{2,7},{3,6},{4,1},{5,0},{6,3},{7,2},{8,13},{9,12},{10,... | collective-permute-start | bytes 49160 | tf_op jit(solution)/shard_map/ppermute | solution.py:339
  26.7 3.2 %collective-permute-start.9 = (bf16[2,32,128]{2,1,0:T(8,128)(2,1)S(1)}, bf16[2,32,128]{2,1,0:T(8,128)(2,1)S(1)}, u32[]{:S(2)}, u32[]{:S(2)}) collective-permute-start(bf16[2,32,128]{2,1,0:T(8,128)(2,1)S(1)} %constant_dynamic-update-slice_fusion), channel_id=1, source_target_pairs={{0,3},{1,2},{2,1},{3,0},{4,7},{5,6},{6,5},{7,4},{8,11},{9,10},{10,... | collective-permute-start | bytes 49160 | tf_op jit(solution)/shard_map/ppermute | solution.py:339
  27.8 1.2 %collective-permute-start.12 = (bf16[1,32,128]{2,1,0:T(8,128)(2,1)S(1)}, bf16[1,32,128]{2,1,0:T(8,128)(2,1)S(1)}, u32[]{:S(2)}, u32[]{:S(2)}) collective-permute-start(bf16[1,32,128]{2,1,0:T(8,128)(2,1)S(1)} %collective-permute-done.7), channel_id=1, source_target_pairs={{0,1},{1,0},{2,3},{3,2},{4,5},{5,4},{6,7},{7,6},{8,9},{9,8},{10,11... | collective-permute-start | bytes 24584 | tf_op jit(solution)/shard_map/ppermute | solution.py:334
  32.1 1.2 %collective-permute-start.13 = (f32[4,2048]{1,0:T(4,128)S(1)}, f32[4,2048]{1,0:T(4,128)S(1)}, u32[]{:S(2)}, u32[]{:S(2)}) collective-permute-start(f32[4,2048]{1,0:T(4,128)S(1)} %get-tuple-element.24), channel_id=1, source_target_pairs={{0,1},{1,0},{2,3},{3,2},{4,5},{5,4},{6,7},{7,6},{8,9},{9,8},{10,11... | collective-permute-start | bytes 98312 | tf_op jit(solution)/shard_map/ppermute | solution.py:334

commit v28 on v27

--- a/solution.py
+++ b/solution.py
@@ -12,7 +12,7 @@
 LANES = 128
 HEAD_SIZE = 128
 CHUNK = 256
-FIRST = 384
+FIRST = 512
 PIECES = 1
 FAN = 4
 MIB = 2**20

time: 34.1 us -> 34.1 us (level)
  transfers between devices with their start and end apart: 14 -> 14, of which waited for: 9 -> 9; matrix products, arithmetic and copies ran while one was open for 0% -> 0% of each run, Pallas kernels for 6% -> 7%
where the time goes in v28:
time: 34.1 us; the launch traced here: 33.9 us
  starting transfers between devices  14 us (41%)
  Pallas kernels  10.4 us (30%)
  waiting for transfers between devices  7.95 us (23%)
  between operations  0.81 us (2%)
  other arithmetic  0.71 us (2%)
    ppermute x8, starting transfers between devices, cross(): return lax.ppermute(block, ('gx', 'gy'), pairs)  12.1 us
    ppermute x8, waiting for transfers between devices, cross(): return lax.ppermute(block, ('gx', 'gy'), pairs)  6.05 us
    pallas_call x1, Pallas kernels, project(): pl.pallas_call(functools.partial(project_kernel, bits), out_shape=(piece,...  4.99 us
    pallas_call x1, Pallas kernels, stage_rows(): pl.pallas_call(functools.partial(stage_kernel, rows), out_shape=jax.Shape...  2.3 us
    pallas_call x1, Pallas kernels, output(): pl.pallas_call(functools.partial(output_kernel, bits, places, turned), ou...  2.28 us
    ppermute x6, starting transfers between devices, swap(): return lax.ppermute(block, axis, [(i, i ^ mask) for i in range(devices)])  1.91 us
    ppermute x6, waiting for transfers between devices, swap(): return lax.ppermute(block, axis, [(i, i ^ mask) for i in range(devices)])  1.9 us
    pallas_call x1, Pallas kernels, attend(): pl.pallas_call(functools.partial(attend_kernel, query_heads, kv_heads, le...  0.82 us
  transfers between devices with their start and end apart: 14, of which 9 were waited for; matrix products, arithmetic and copies ran while one was open for 0% of the time, Pallas kernels for 7%

profile of v28, /device:TPU:0, one launch (start us, length us, event | category | flops | bytes accessed | tf_op | source)
XLA Modules:
  0.0 33.9 jit_solution(18002819478672186749)
XLA Ops:
  0.0 0.5 %collective-permute-start = (bf16[4,2048]{1,0:T(4,128)(2,1)}, bf16[4,2048]{1,0:T(4,128)(2,1)S(1)}, u32[]{:S(2)}, u32[]{:S(2)}) collective-permute-start(bf16[4,2048]{1,0:T(4,128)(2,1)} %rows_ref.1), channel_id=1, source_target_pairs={{0,1},{1,0},{2,3},{3,2},{4,5},{5,4},{6,7},{7,6},{8,9},{9,8},{10,11... | collective-permute-start | bytes 49160 | tf_op jit(solution)/shard_map/ppermute | solution.py:334
  0.5 2.3 %stage.1.first = bf16[512,4096]{1,0:T(8,128)(2,1)S(1)} custom-call(bf16[2048,4096]{1,0:T(8,128)(2,1)} %more_ref.1), custom_call_target="tpu_custom_call" | custom-call | bytes 4194304 | tf_op jit(solution)/shard_map/stage/pallas_call | solution.py:57
  2.9 5.0 %project.1 = (f32[2,40,128]{2,1,0:T(8,128)S(1)}, f32[2,40,128]{2,1,0:T(8,128)S(1)}, f32[2,40,128]{2,1,0:T(8,128)S(1)}, f32[2,40,128]{2,1,0:T(8,128)S(1)}) custom-call(bf16[4,2048]{1,0:T(4,128)(2,1)S(1)} %copy-done.4, bf16[4,2048]{1,0:T(4,128)(2,1)S(1)} %collective-permute-done.other_ref, bf16[2048,4096]{1,0:T(8,128)(2,1)} %more_ref.1, ...), custom_call_target="tpu_custom_call" | custom-call | flops 150994944 | bytes 18874368 | tf_op jit(solution)/shard_map/project/pallas_call | solution.py:182
  7.9 3.6 %collective-permute-start.1 = (f32[2,40,128]{2,1,0:T(8,128)S(1)}, f32[2,40,128]{2,1,0:T(8,128)S(1)}, u32[]{:S(2)}, u32[]{:S(2)}) collective-permute-start(f32[2,40,128]{2,1,0:T(8,128)S(1)} %get-tuple-element.15.after_ref), channel_id=1, source_target_pairs={{0,7},{1,6},{2,5},{3,4},{4,3},{5,2},{6,1},{7,0},{8,15},{9,14},{10,... | collective-permute-start | bytes 122888 | tf_op jit(solution)/shard_map/ppermute | solution.py:339
  11.5 0.5 %collective-permute-start.2 = (f32[2,40,128]{2,1,0:T(8,128)S(1)}, f32[2,40,128]{2,1,0:T(8,128)S(1)}, u32[]{:S(2)}, u32[]{:S(2)}) collective-permute-start(f32[2,40,128]{2,1,0:T(8,128)S(1)} %get-tuple-element.16), channel_id=1, source_target_pairs={{0,5},{1,4},{2,7},{3,6},{4,1},{5,0},{6,3},{7,2},{8,13},{9,12},{10,... | collective-permute-start | bytes 122888 | tf_op jit(solution)/shard_map/ppermute | solution.py:339
  12.0 0.2 collective-permute-start.3
  13.1 0.4 %collective-permute-done.1 = f32[2,40,128]{2,1,0:T(8,128)S(1)} collective-permute-done((f32[2,40,128]{2,1,0:T(8,128)S(1)}, f32[2,40,128]{2,1,0:T(8,128)S(1)}, u32[]{:S(2)}, u32[]{:S(2)}) %collective-permute-start.1) | collective-permute-done | bytes 40992 | tf_op jit(solution)/shard_map/ppermute | solution.py:339
  13.4 1.5 %collective-permute-done.2 = f32[2,40,128]{2,1,0:T(8,128)S(1)} collective-permute-done((f32[2,40,128]{2,1,0:T(8,128)S(1)}, f32[2,40,128]{2,1,0:T(8,128)S(1)}, u32[]{:S(2)}, u32[]{:S(2)}) %collective-permute-start.2) | collective-permute-done | bytes 40992 | tf_op jit(solution)/shard_map/ppermute | solution.py:339
  14.9 0.8 %collective-permute-done.3 = f32[2,40,128]{2,1,0:T(8,128)S(1)} collective-permute-done((f32[2,40,128]{2,1,0:T(8,128)S(1)}, f32[2,40,128]{2,1,0:T(8,128)S(1)}, u32[]{:S(2)}, u32[]{:S(2)}) %collective-permute-start.3) | collective-permute-done | bytes 40992 | tf_op jit(solution)/shard_map/ppermute | solution.py:339
  15.7 2.4 %collective-permute-start.5 = (f32[1,40,128]{2,1,0:T(8,128)S(1)}, f32[1,40,128]{2,1,0:T(8,128)S(1)}, u32[]{:S(2)}, u32[]{:S(2)}) collective-permute-start(f32[1,40,128]{2,1,0:T(8,128)S(1)} %get-tuple-element.22), channel_id=1, source_target_pairs={{0,9},{1,8},{2,11},{3,10},{4,13},{5,12},{6,15},{7,14},{8,1},{9,0},... | collective-permute-start | bytes 61448 | tf_op jit(solution)/shard_map/ppermute | solution.py:339
  18.0 0.4 %collective-permute-start.6 = (f32[1,40,128]{2,1,0:T(8,128)S(1)}, f32[1,40,128]{2,1,0:T(8,128)S(1)}, u32[]{:S(2)}, u32[]{:S(2)}) collective-permute-start(f32[1,40,128]{2,1,0:T(8,128)S(1)} %get-tuple-element.25), channel_id=1, source_target_pairs={{0,1},{1,0},{2,3},{3,2},{4,5},{5,4},{6,7},{7,6},{8,9},{9,8},{10,11... | collective-permute-start | bytes 61448 | tf_op jit(solution)/shard_map/ppermute | solution.py:334
  18.4 1.4 %collective-permute-done.5.refs_0_ = f32[1,40,128]{2,1,0:T(8,128)S(1)} collective-permute-done((f32[1,40,128]{2,1,0:T(8,128)S(1)}, f32[1,40,128]{2,1,0:T(8,128)S(1)}, u32[]{:S(2)}, u32[]{:S(2)}) %collective-permute-start.5) | collective-permute-done | bytes 20512 | tf_op jit(solution)/shard_map/ppermute | solution.py:339
  19.9 0.8 %attend.1.refs_4_ = bf16[1,32,128]{2,1,0:T(8,128)(2,1)S(1)} custom-call(bf16[4096,2048]{1,0:T(8,128)(2,1)} %refs_5_.1, f32[8,128]{1,0:T(8,128)S(1)} %get-tuple-element.20.turn_ref, f32[1,2048]{1,0:T(1,128)S(1)} %get-tuple-element.21.live_ref, bf16[1,2,2048,128]{3,2,1,0:T(8,128)(2,1)S(1)} %copy-done.2, bf16[1,2,2048,128]{3,2,1,0:T(8,128)(2,1)S(1)} %copy-done.3, ...), custom_call_target="tpu_custom_call" | custom-call | flops 33554432 | bytes 2097152 | tf_op jit(solution)/shard_map/attend/pallas_call | solution.py:269
  20.7 2.4 %collective-permute-start.7 = (bf16[1,32,128]{2,1,0:T(8,128)(2,1)S(1)}, bf16[1,32,128]{2,1,0:T(8,128)(2,1)S(1)}, u32[]{:S(2)}, u32[]{:S(2)}) collective-permute-start(bf16[1,32,128]{2,1,0:T(8,128)(2,1)S(1)} %attend.1.refs_4_), channel_id=1, source_target_pairs={{0,9},{1,8},{2,11},{3,10},{4,13},{5,12},{6,15},{7,14},{8,1},{9,0},... | collective-permute-start | bytes 24584 | tf_op jit(solution)/shard_map/ppermute | solution.py:339
  23.1 0.4 %collective-permute-start.8 = (bf16[1,32,128]{2,1,0:T(8,128)(2,1)S(1)}, bf16[1,32,128]{2,1,0:T(8,128)(2,1)S(1)}, u32[]{:S(2)}, u32[]{:S(2)}) collective-permute-start(bf16[1,32,128]{2,1,0:T(8,128)(2,1)S(1)} %attend.1.refs_4_), channel_id=1, source_target_pairs={{0,1},{1,0},{2,3},{3,2},{4,5},{5,4},{6,7},{7,6},{8,9},{9,8},{10,11... | collective-permute-start | bytes 24584 | tf_op jit(solution)/shard_map/ppermute | solution.py:334
  23.5 1.3 %collective-permute-done.7 = bf16[1,32,128]{2,1,0:T(8,128)(2,1)S(1)} collective-permute-done((bf16[1,32,128]{2,1,0:T(8,128)(2,1)S(1)}, bf16[1,32,128]{2,1,0:T(8,128)(2,1)S(1)}, u32[]{:S(2)}, u32[]{:S(2)}) %collective-permute-start.7) | collective-permute-done | bytes 8224 | tf_op jit(solution)/shard_map/ppermute | solution.py:339
  24.8 1.8 %collective-permute-start.10 = (bf16[2,32,128]{2,1,0:T(8,128)(2,1)S(1)}, bf16[2,32,128]{2,1,0:T(8,128)(2,1)S(1)}, u32[]{:S(2)}, u32[]{:S(2)}) collective-permute-start(bf16[2,32,128]{2,1,0:T(8,128)(2,1)S(1)} %constant_dynamic-update-slice_fusion), channel_id=1, source_target_pairs={{0,7},{1,6},{2,5},{3,4},{4,3},{5,2},{6,1},{7,0},{8,15},{9,14},{10,... | collective-permute-start | bytes 49160 | tf_op jit(solution)/shard_map/ppermute | solution.py:339
  26.6 1.1 %collective-permute-start.9 = (bf16[2,32,128]{2,1,0:T(8,128)(2,1)S(1)}, bf16[2,32,128]{2,1,0:T(8,128)(2,1)S(1)}, u32[]{:S(2)}, u32[]{:S(2)}) collective-permute-start(bf16[2,32,128]{2,1,0:T(8,128)(2,1)S(1)} %constant_dynamic-update-slice_fusion), channel_id=1, source_target_pairs={{0,3},{1,2},{2,1},{3,0},{4,7},{5,6},{6,5},{7,4},{8,11},{9,10},{10,... | collective-permute-start | bytes 49160 | tf_op jit(solution)/shard_map/ppermute | solution.py:339
  27.8 0.4 %collective-permute-start.12 = (bf16[1,32,128]{2,1,0:T(8,128)(2,1)S(1)}, bf16[1,32,128]{2,1,0:T(8,128)(2,1)S(1)}, u32[]{:S(2)}, u32[]{:S(2)}) collective-permute-start(bf16[1,32,128]{2,1,0:T(8,128)(2,1)S(1)} %collective-permute-done.7), channel_id=1, source_target_pairs={{0,1},{1,0},{2,3},{3,2},{4,5},{5,4},{6,7},{7,6},{8,9},{9,8},{10,11... | collective-permute-start | bytes 24584 | tf_op jit(solution)/shard_map/ppermute | solution.py:334
  28.2 0.8 %collective-permute-done.12.refs_3_ = bf16[1,32,128]{2,1,0:T(8,128)(2,1)S(1)} collective-permute-done((bf16[1,32,128]{2,1,0:T(8,128)(2,1)S(1)}, bf16[1,32,128]{2,1,0:T(8,128)(2,1)S(1)}, u32[]{:S(2)}, u32[]{:S(2)}) %collective-permute-start.12) | collective-permute-done | bytes 8224 | tf_op jit(solution)/shard_map/ppermute | solution.py:334
  29.0 0.7 %collective-permute-done.11.refs_2_ = bf16[2,32,128]{2,1,0:T(8,128)(2,1)S(1)} collective-permute-done((bf16[2,32,128]{2,1,0:T(8,128)(2,1)S(1)}, bf16[2,32,128]{2,1,0:T(8,128)(2,1)S(1)}, u32[]{:S(2)}, u32[]{:S(2)}) %collective-permute-start.11) | collective-permute-done | bytes 16416 | tf_op jit(solution)/shard_map/ppermute | solution.py:339
  29.8 2.3 %output.1 = (f32[4,2048]{1,0:T(4,128)S(1)}, f32[4,2048]{1,0:T(4,128)S(1)}) custom-call(bf16[2,32,128]{2,1,0:T(8,128)(2,1)S(1)} %collective-permute-done.9.refs_0_, bf16[2,32,128]{2,1,0:T(8,128)(2,1)S(1)} %collective-permute-done.10.refs_1_, bf16[2,32,128]{2,1,0:T(8,128)(2,1)S(1)} %collective-permute-done.11.refs_2_, ...), custom_call_target="tpu_custom_call" | custom-call | flops 134217728 | bytes 16777216 | tf_op jit(solution)/shard_map/output/pallas_call | solution.py:316
  32.3 1.1 %collective-permute-done.13 = f32[4,2048]{1,0:T(4,128)S(1)} collective-permute-done((f32[4,2048]{1,0:T(4,128)S(1)}, f32[4,2048]{1,0:T(4,128)S(1)}, u32[]{:S(2)}, u32[]{:S(2)}) %collective-permute-start.13) | collective-permute-done | bytes 32800 | tf_op jit(solution)/shard_map/ppermute | solution.py:334
  33.3 0.6 %add_convert_fusion = bf16[4,2048]{1,0:T(4,128)(2,1)} fusion(f32[4,2048]{1,0:T(4,128)S(1)} %get-tuple-element.23, f32[4,2048]{1,0:T(4,128)S(1)} %collective-permute-done.13), kind=kLoop, calls=%fused_computation | loop fusion | flops 16384 | bytes 81920 | tf_op jit(solution)/shard_map/convert_element_type | solution.py:402
  (34 shorter events, 0.5 us)
Async XLA Ops:
  0.0 2.9 %copy-start.4 = (bf16[4,2048]{1,0:T(4,128)(2,1)S(1)}, bf16[4,2048]{1,0:T(4,128)(2,1)}, u32[]{:S(2)}) copy-start(bf16[4,2048]{1,0:T(4,128)(2,1)} %rows_ref.1) | copy-start | bytes 49156
  0.0 2.9 %copy-start = (bf16[2048,256]{1,0:T(8,128)(2,1)S(1)}, bf16[2048,256]{1,0:T(8,128)(2,1)}, u32[]{:S(2)}) copy-start(bf16[2048,256]{1,0:T(8,128)(2,1)} %wk.1) | copy-start | bytes 3145732
  0.0 2.9 %copy-start.1 = (bf16[2048,256]{1,0:T(8,128)(2,1)S(1)}, bf16[2048,256]{1,0:T(8,128)(2,1)}, u32[]{:S(2)}) copy-start(bf16[2048,256]{1,0:T(8,128)(2,1)} %wv.1) | copy-start | bytes 3145732
  0.0 2.8 %collective-permute-start = (bf16[4,2048]{1,0:T(4,128)(2,1)}, bf16[4,2048]{1,0:T(4,128)(2,1)S(1)}, u32[]{:S(2)}, u32[]{:S(2)}) collective-permute-start(bf16[4,2048]{1,0:T(4,128)(2,1)} %rows_ref.1), channel_id=1, source_target_pairs={{0,1},{1,0},{2,3},{3,2},{4,5},{5,4},{6,7},{7,6},{8,9},{9,8},{10,11... | collective-permute-start | bytes 49160 | tf_op jit(solution)/shard_map/ppermute | solution.py:334
  7.9 5.5 %collective-permute-start.1 = (f32[2,40,128]{2,1,0:T(8,128)S(1)}, f32[2,40,128]{2,1,0:T(8,128)S(1)}, u32[]{:S(2)}, u32[]{:S(2)}) collective-permute-start(f32[2,40,128]{2,1,0:T(8,128)S(1)} %get-tuple-element.15.after_ref), channel_id=1, source_target_pairs={{0,7},{1,6},{2,5},{3,4},{4,3},{5,2},{6,1},{7,0},{8,15},{9,14},{10,... | collective-permute-start | bytes 122888 | tf_op jit(solution)/shard_map/ppermute | solution.py:339
  11.5 3.4 %collective-permute-start.2 = (f32[2,40,128]{2,1,0:T(8,128)S(1)}, f32[2,40,128]{2,1,0:T(8,128)S(1)}, u32[]{:S(2)}, u32[]{:S(2)}) collective-permute-start(f32[2,40,128]{2,1,0:T(8,128)S(1)} %get-tuple-element.16), channel_id=1, source_target_pairs={{0,5},{1,4},{2,7},{3,6},{4,1},{5,0},{6,3},{7,2},{8,13},{9,12},{10,... | collective-permute-start | bytes 122888 | tf_op jit(solution)/shard_map/ppermute | solution.py:339
  12.0 3.7 %collective-permute-start.3 = (f32[2,40,128]{2,1,0:T(8,128)S(1)}, f32[2,40,128]{2,1,0:T(8,128)S(1)}, u32[]{:S(2)}, u32[]{:S(2)}) collective-permute-start(f32[2,40,128]{2,1,0:T(8,128)S(1)} %get-tuple-element.17), channel_id=1, source_target_pairs={{0,3},{1,2},{2,1},{3,0},{4,7},{5,6},{6,5},{7,4},{8,11},{9,10},{10,... | collective-permute-start | bytes 122888 | tf_op jit(solution)/shard_map/ppermute | solution.py:339
  12.2 3.5 %collective-permute-start.4 = (f32[2,40,128]{2,1,0:T(8,128)S(1)}, f32[2,40,128]{2,1,0:T(8,128)S(1)}, u32[]{:S(2)}, u32[]{:S(2)}) collective-permute-start(f32[2,40,128]{2,1,0:T(8,128)S(1)} %get-tuple-element.18), channel_id=1, source_target_pairs={{0,1},{1,0},{2,3},{3,2},{4,5},{5,4},{6,7},{7,6},{8,9},{9,8},{10,11... | collective-permute-start | bytes 122888 | tf_op jit(solution)/shard_map/ppermute | solution.py:334
  12.9 6.9 %copy-start.2 = (bf16[1,2,2048,128]{3,2,1,0:T(8,128)(2,1)S(1)}, bf16[1,2,2048,128]{3,2,1,0:T(8,128)(2,1)}, u32[]{:S(2)}) copy-start(bf16[1,2,2048,128]{3,2,1,0:T(8,128)(2,1)} %k_ref.1) | copy-start | bytes 3145732
  13.0 6.9 %copy-start.3 = (bf16[1,2,2048,128]{3,2,1,0:T(8,128)(2,1)S(1)}, bf16[1,2,2048,128]{3,2,1,0:T(8,128)(2,1)}, u32[]{:S(2)}) copy-start(bf16[1,2,2048,128]{3,2,1,0:T(8,128)(2,1)} %v_ref.1) | copy-start | bytes 3145732
  13.0 16.8 %slice-start = ((s8[16777216]{0:T(1024)(128)(4,1)}), s8[4194304]{0:T(1024)(128)(4,1)S(1)}, s32[]{:S(2)}) async-start(s8[16777216]{0:T(1024)(128)(4,1)} %bitcast.2), calls=%async_computation | async-start | bytes 8388608
  13.0 16.8 %slice-start.1 = ((s8[16777216]{0:T(1024)(128)(4,1)}), s8[4194304]{0:T(1024)(128)(4,1)S(1)}, s32[]{:S(2)}) async-start(s8[16777216]{0:T(1024)(128)(4,1)} %bitcast.2), calls=%async_computation.1 | async-start | bytes 8388608
  13.0 16.8 %slice-start.2 = ((s8[16777216]{0:T(1024)(128)(4,1)}), s8[4194304]{0:T(1024)(128)(4,1)S(1)}, s32[]{:S(2)}) async-start(s8[16777216]{0:T(1024)(128)(4,1)} %bitcast.2), calls=%async_computation.2 | async-start | bytes 8388608
  15.7 4.2 %collective-permute-start.5 = (f32[1,40,128]{2,1,0:T(8,128)S(1)}, f32[1,40,128]{2,1,0:T(8,128)S(1)}, u32[]{:S(2)}, u32[]{:S(2)}) collective-permute-start(f32[1,40,128]{2,1,0:T(8,128)S(1)} %get-tuple-element.22), channel_id=1, source_target_pairs={{0,9},{1,8},{2,11},{3,10},{4,13},{5,12},{6,15},{7,14},{8,1},{9,0},... | collective-permute-start | bytes 61448 | tf_op jit(solution)/shard_map/ppermute | solution.py:339
  18.0 1.8 %collective-permute-start.6 = (f32[1,40,128]{2,1,0:T(8,128)S(1)}, f32[1,40,128]{2,1,0:T(8,128)S(1)}, u32[]{:S(2)}, u32[]{:S(2)}) collective-permute-start(f32[1,40,128]{2,1,0:T(8,128)S(1)} %get-tuple-element.25), channel_id=1, source_target_pairs={{0,1},{1,0},{2,3},{3,2},{4,5},{5,4},{6,7},{7,6},{8,9},{9,8},{10,11... | collective-permute-start | bytes 61448 | tf_op jit(solution)/shard_map/ppermute | solution.py:334
  19.9 10.0 %slice-start.3 = ((s8[16777216]{0:T(1024)(128)(4,1)}), s8[4194304]{0:T(1024)(128)(4,1)S(1)}, s32[]{:S(2)}) async-start(s8[16777216]{0:T(1024)(128)(4,1)} %bitcast.2), calls=%async_computation.3 | async-start | bytes 8388608
  20.7 4.0 %collective-permute-start.7 = (bf16[1,32,128]{2,1,0:T(8,128)(2,1)S(1)}, bf16[1,32,128]{2,1,0:T(8,128)(2,1)S(1)}, u32[]{:S(2)}, u32[]{:S(2)}) collective-permute-start(bf16[1,32,128]{2,1,0:T(8,128)(2,1)S(1)} %attend.1.refs_4_), channel_id=1, source_target_pairs={{0,9},{1,8},{2,11},{3,10},{4,13},{5,12},{6,15},{7,14},{8,1},{9,0},... | collective-permute-start | bytes 24584 | tf_op jit(solution)/shard_map/ppermute | solution.py:339
  23.1 1.6 %collective-permute-start.8 = (bf16[1,32,128]{2,1,0:T(8,128)(2,1)S(1)}, bf16[1,32,128]{2,1,0:T(8,128)(2,1)S(1)}, u32[]{:S(2)}, u32[]{:S(2)}) collective-permute-start(bf16[1,32,128]{2,1,0:T(8,128)(2,1)S(1)} %attend.1.refs_4_), channel_id=1, source_target_pairs={{0,1},{1,0},{2,3},{3,2},{4,5},{5,4},{6,7},{7,6},{8,9},{9,8},{10,11... | collective-permute-start | bytes 24584 | tf_op jit(solution)/shard_map/ppermute | solution.py:334
  24.8 4.3 %collective-permute-start.10 = (bf16[2,32,128]{2,1,0:T(8,128)(2,1)S(1)}, bf16[2,32,128]{2,1,0:T(8,128)(2,1)S(1)}, u32[]{:S(2)}, u32[]{:S(2)}) collective-permute-start(bf16[2,32,128]{2,1,0:T(8,128)(2,1)S(1)} %constant_dynamic-update-slice_fusion), channel_id=1, source_target_pairs={{0,7},{1,6},{2,5},{3,4},{4,3},{5,2},{6,1},{7,0},{8,15},{9,14},{10,... | collective-permute-start | bytes 49160 | tf_op jit(solution)/shard_map/ppermute | solution.py:339
  26.6 3.2 %collective-permute-start.11 = (bf16[2,32,128]{2,1,0:T(8,128)(2,1)S(1)}, bf16[2,32,128]{2,1,0:T(8,128)(2,1)S(1)}, u32[]{:S(2)}, u32[]{:S(2)}) collective-permute-start(bf16[2,32,128]{2,1,0:T(8,128)(2,1)S(1)} %constant_dynamic-update-slice_fusion), channel_id=1, source_target_pairs={{0,5},{1,4},{2,7},{3,6},{4,1},{5,0},{6,3},{7,2},{8,13},{9,12},{10,... | collective-permute-start | bytes 49160 | tf_op jit(solution)/shard_map/ppermute | solution.py:339
  26.6 3.2 %collective-permute-start.9 = (bf16[2,32,128]{2,1,0:T(8,128)(2,1)S(1)}, bf16[2,32,128]{2,1,0:T(8,128)(2,1)S(1)}, u32[]{:S(2)}, u32[]{:S(2)}) collective-permute-start(bf16[2,32,128]{2,1,0:T(8,128)(2,1)S(1)} %constant_dynamic-update-slice_fusion), channel_id=1, source_target_pairs={{0,3},{1,2},{2,1},{3,0},{4,7},{5,6},{6,5},{7,4},{8,11},{9,10},{10,... | collective-permute-start | bytes 49160 | tf_op jit(solution)/shard_map/ppermute | solution.py:339
  27.8 1.3 %collective-permute-start.12 = (bf16[1,32,128]{2,1,0:T(8,128)(2,1)S(1)}, bf16[1,32,128]{2,1,0:T(8,128)(2,1)S(1)}, u32[]{:S(2)}, u32[]{:S(2)}) collective-permute-start(bf16[1,32,128]{2,1,0:T(8,128)(2,1)S(1)} %collective-permute-done.7), channel_id=1, source_target_pairs={{0,1},{1,0},{2,3},{3,2},{4,5},{5,4},{6,7},{7,6},{8,9},{9,8},{10,11... | collective-permute-start | bytes 24584 | tf_op jit(solution)/shard_map/ppermute | solution.py:334
  32.1 1.2 %collective-permute-start.13 = (f32[4,2048]{1,0:T(4,128)S(1)}, f32[4,2048]{1,0:T(4,128)S(1)}, u32[]{:S(2)}, u32[]{:S(2)}) collective-permute-start(f32[4,2048]{1,0:T(4,128)S(1)} %get-tuple-element.24), channel_id=1, source_target_pairs={{0,1},{1,0},{2,3},{3,2},{4,5},{5,4},{6,7},{7,6},{8,9},{9,8},{10,11... | collective-permute-start | bytes 98312 | tf_op jit(solution)/shard_map/ppermute | solution.py:334

commit v29 on v28

--- a/solution.py
+++ b/solution.py
@@ -378,7 +378,7 @@
         held = jnp.concatenate([crossed, beside], axis=0)
         arrived = fan([held] * FAN, lambda block, mask: cross(block, devices, mask))
         parts = [heads, swap(crossed, "gy", 2, 1)] + arrived
-        order, turned = (3, 4, 2, 1, 0), -1
+        order, turned = (2, 4, 3, 1, 0), -1
     else:
         arrived = fan(pieces, lambda block, mask: swap(block, "gx", devices, mask))
         turn, live = turning(lengths, frequency, w_out, w_query, pieces[3], k_cache.shape[2])

time: 34.1 us -> 35.2 us (1.032)
  waiting for transfers between devices: 7.95 us -> 8.88 us
    ppermute x8, waiting for transfers between devices: 6.05 us -> 7.18 us  [cross(): return lax.ppermute(block, ('gx', 'gy'), pairs)]
where the time goes in v29:
time: 35.2 us; the launch traced here: 35.1 us
  starting transfers between devices  14.2 us (40%)
  Pallas kernels  10.4 us (30%)
  waiting for transfers between devices  8.88 us (25%)
  between operations  0.81 us (2%)
  other arithmetic  0.71 us (2%)
    ppermute x8, starting transfers between devices, cross(): return lax.ppermute(block, ('gx', 'gy'), pairs)  12.1 us
    ppermute x8, waiting for transfers between devices, cross(): return lax.ppermute(block, ('gx', 'gy'), pairs)  7.18 us
    pallas_call x1, Pallas kernels, project(): pl.pallas_call(functools.partial(project_kernel, bits), out_shape=(piece,...  4.99 us
    pallas_call x1, Pallas kernels, stage_rows(): pl.pallas_call(functools.partial(stage_kernel, rows), out_shape=jax.Shape...  2.3 us
    pallas_call x1, Pallas kernels, output(): pl.pallas_call(functools.partial(output_kernel, bits, places, turned), ou...  2.28 us
    ppermute x6, starting transfers between devices, swap(): return lax.ppermute(block, axis, [(i, i ^ mask) for i in range(devices)])  2.11 us
    ppermute x6, waiting for transfers between devices, swap(): return lax.ppermute(block, axis, [(i, i ^ mask) for i in range(devices)])  1.7 us
    pallas_call x1, Pallas kernels, attend(): pl.pallas_call(functools.partial(attend_kernel, query_heads, kv_heads, le...  0.82 us
  transfers between devices with their start and end apart: 14, of which 9 were waited for; matrix products, arithmetic and copies ran while one was open for 0% of the time, Pallas kernels for 7%

profile of v29, /device:TPU:0, one launch (start us, length us, event | category | flops | bytes accessed | tf_op | source)
XLA Modules:
  0.0 35.1 jit_solution(13445445747828216263)
XLA Ops:
  0.0 0.5 %collective-permute-start = (bf16[4,2048]{1,0:T(4,128)(2,1)}, bf16[4,2048]{1,0:T(4,128)(2,1)S(1)}, u32[]{:S(2)}, u32[]{:S(2)}) collective-permute-start(bf16[4,2048]{1,0:T(4,128)(2,1)} %rows_ref.1), channel_id=1, source_target_pairs={{0,1},{1,0},{2,3},{3,2},{4,5},{5,4},{6,7},{7,6},{8,9},{9,8},{10,11... | collective-permute-start | bytes 49160 | tf_op jit(solution)/shard_map/ppermute | solution.py:334
  0.5 2.3 %stage.1.first = bf16[512,4096]{1,0:T(8,128)(2,1)S(1)} custom-call(bf16[2048,4096]{1,0:T(8,128)(2,1)} %more_ref.1), custom_call_target="tpu_custom_call" | custom-call | bytes 4194304 | tf_op jit(solution)/shard_map/stage/pallas_call | solution.py:57
  2.9 5.0 %project.1 = (f32[2,40,128]{2,1,0:T(8,128)S(1)}, f32[2,40,128]{2,1,0:T(8,128)S(1)}, f32[2,40,128]{2,1,0:T(8,128)S(1)}, f32[2,40,128]{2,1,0:T(8,128)S(1)}) custom-call(bf16[4,2048]{1,0:T(4,128)(2,1)S(1)} %copy-done.4, bf16[4,2048]{1,0:T(4,128)(2,1)S(1)} %collective-permute-done.other_ref, bf16[2048,4096]{1,0:T(8,128)(2,1)} %more_ref.1, ...), custom_call_target="tpu_custom_call" | custom-call | flops 150994944 | bytes 18874368 | tf_op jit(solution)/shard_map/project/pallas_call | solution.py:182
  7.9 3.6 %collective-permute-start.1 = (f32[2,40,128]{2,1,0:T(8,128)S(1)}, f32[2,40,128]{2,1,0:T(8,128)S(1)}, u32[]{:S(2)}, u32[]{:S(2)}) collective-permute-start(f32[2,40,128]{2,1,0:T(8,128)S(1)} %get-tuple-element.15.after_ref), channel_id=1, source_target_pairs={{0,7},{1,6},{2,5},{3,4},{4,3},{5,2},{6,1},{7,0},{8,15},{9,14},{10,... | collective-permute-start | bytes 122888 | tf_op jit(solution)/shard_map/ppermute | solution.py:339
  11.5 0.5 %collective-permute-start.2 = (f32[2,40,128]{2,1,0:T(8,128)S(1)}, f32[2,40,128]{2,1,0:T(8,128)S(1)}, u32[]{:S(2)}, u32[]{:S(2)}) collective-permute-start(f32[2,40,128]{2,1,0:T(8,128)S(1)} %get-tuple-element.16), channel_id=1, source_target_pairs={{0,5},{1,4},{2,7},{3,6},{4,1},{5,0},{6,3},{7,2},{8,13},{9,12},{10,... | collective-permute-start | bytes 122888 | tf_op jit(solution)/shard_map/ppermute | solution.py:339
  13.1 0.4 %collective-permute-done.1 = f32[2,40,128]{2,1,0:T(8,128)S(1)} collective-permute-done((f32[2,40,128]{2,1,0:T(8,128)S(1)}, f32[2,40,128]{2,1,0:T(8,128)S(1)}, u32[]{:S(2)}, u32[]{:S(2)}) %collective-permute-start.1) | collective-permute-done | bytes 40992 | tf_op jit(solution)/shard_map/ppermute | solution.py:339
  13.4 1.5 %collective-permute-done.2 = f32[2,40,128]{2,1,0:T(8,128)S(1)} collective-permute-done((f32[2,40,128]{2,1,0:T(8,128)S(1)}, f32[2,40,128]{2,1,0:T(8,128)S(1)}, u32[]{:S(2)}, u32[]{:S(2)}) %collective-permute-start.2) | collective-permute-done | bytes 40992 | tf_op jit(solution)/shard_map/ppermute | solution.py:339
  14.9 0.8 %collective-permute-done.3 = f32[2,40,128]{2,1,0:T(8,128)S(1)} collective-permute-done((f32[2,40,128]{2,1,0:T(8,128)S(1)}, f32[2,40,128]{2,1,0:T(8,128)S(1)}, u32[]{:S(2)}, u32[]{:S(2)}) %collective-permute-start.3) | collective-permute-done | bytes 40992 | tf_op jit(solution)/shard_map/ppermute | solution.py:339
  15.7 2.4 %collective-permute-start.5 = (f32[1,40,128]{2,1,0:T(8,128)S(1)}, f32[1,40,128]{2,1,0:T(8,128)S(1)}, u32[]{:S(2)}, u32[]{:S(2)}) collective-permute-start(f32[1,40,128]{2,1,0:T(8,128)S(1)} %get-tuple-element.22), channel_id=1, source_target_pairs={{0,9},{1,8},{2,11},{3,10},{4,13},{5,12},{6,15},{7,14},{8,1},{9,0},... | collective-permute-start | bytes 61448 | tf_op jit(solution)/shard_map/ppermute | solution.py:339
  18.0 0.4 %collective-permute-start.6 = (f32[1,40,128]{2,1,0:T(8,128)S(1)}, f32[1,40,128]{2,1,0:T(8,128)S(1)}, u32[]{:S(2)}, u32[]{:S(2)}) collective-permute-start(f32[1,40,128]{2,1,0:T(8,128)S(1)} %get-tuple-element.25), channel_id=1, source_target_pairs={{0,1},{1,0},{2,3},{3,2},{4,5},{5,4},{6,7},{7,6},{8,9},{9,8},{10,11... | collective-permute-start | bytes 61448 | tf_op jit(solution)/shard_map/ppermute | solution.py:334
  18.4 1.4 %collective-permute-done.5.refs_0_ = f32[1,40,128]{2,1,0:T(8,128)S(1)} collective-permute-done((f32[1,40,128]{2,1,0:T(8,128)S(1)}, f32[1,40,128]{2,1,0:T(8,128)S(1)}, u32[]{:S(2)}, u32[]{:S(2)}) %collective-permute-start.5) | collective-permute-done | bytes 20512 | tf_op jit(solution)/shard_map/ppermute | solution.py:339
  19.9 0.8 %attend.1.refs_4_ = bf16[1,32,128]{2,1,0:T(8,128)(2,1)S(1)} custom-call(bf16[4096,2048]{1,0:T(8,128)(2,1)} %refs_5_.1, f32[8,128]{1,0:T(8,128)S(1)} %get-tuple-element.20.turn_ref, f32[1,2048]{1,0:T(1,128)S(1)} %get-tuple-element.21.live_ref, bf16[1,2,2048,128]{3,2,1,0:T(8,128)(2,1)S(1)} %copy-done.2, bf16[1,2,2048,128]{3,2,1,0:T(8,128)(2,1)S(1)} %copy-done.3, ...), custom_call_target="tpu_custom_call" | custom-call | flops 33554432 | bytes 2097152 | tf_op jit(solution)/shard_map/attend/pallas_call | solution.py:269
  20.7 2.4 %collective-permute-start.7 = (bf16[1,32,128]{2,1,0:T(8,128)(2,1)S(1)}, bf16[1,32,128]{2,1,0:T(8,128)(2,1)S(1)}, u32[]{:S(2)}, u32[]{:S(2)}) collective-permute-start(bf16[1,32,128]{2,1,0:T(8,128)(2,1)S(1)} %attend.1.refs_4_), channel_id=1, source_target_pairs={{0,9},{1,8},{2,11},{3,10},{4,13},{5,12},{6,15},{7,14},{8,1},{9,0},... | collective-permute-start | bytes 24584 | tf_op jit(solution)/shard_map/ppermute | solution.py:339
  23.1 0.4 %collective-permute-start.8 = (bf16[1,32,128]{2,1,0:T(8,128)(2,1)S(1)}, bf16[1,32,128]{2,1,0:T(8,128)(2,1)S(1)}, u32[]{:S(2)}, u32[]{:S(2)}) collective-permute-start(bf16[1,32,128]{2,1,0:T(8,128)(2,1)S(1)} %attend.1.refs_4_), channel_id=1, source_target_pairs={{0,1},{1,0},{2,3},{3,2},{4,5},{5,4},{6,7},{7,6},{8,9},{9,8},{10,11... | collective-permute-start | bytes 24584 | tf_op jit(solution)/shard_map/ppermute | solution.py:334
  23.5 1.3 %collective-permute-done.7 = bf16[1,32,128]{2,1,0:T(8,128)(2,1)S(1)} collective-permute-done((bf16[1,32,128]{2,1,0:T(8,128)(2,1)S(1)}, bf16[1,32,128]{2,1,0:T(8,128)(2,1)S(1)}, u32[]{:S(2)}, u32[]{:S(2)}) %collective-permute-start.7) | collective-permute-done | bytes 8224 | tf_op jit(solution)/shard_map/ppermute | solution.py:339
  24.8 1.8 %collective-permute-start.10 = (bf16[2,32,128]{2,1,0:T(8,128)(2,1)S(1)}, bf16[2,32,128]{2,1,0:T(8,128)(2,1)S(1)}, u32[]{:S(2)}, u32[]{:S(2)}) collective-permute-start(bf16[2,32,128]{2,1,0:T(8,128)(2,1)S(1)} %constant_dynamic-update-slice_fusion), channel_id=1, source_target_pairs={{0,7},{1,6},{2,5},{3,4},{4,3},{5,2},{6,1},{7,0},{8,15},{9,14},{10,... | collective-permute-start | bytes 49160 | tf_op jit(solution)/shard_map/ppermute | solution.py:339
  26.6 1.2 %collective-permute-start.11 = (bf16[2,32,128]{2,1,0:T(8,128)(2,1)S(1)}, bf16[2,32,128]{2,1,0:T(8,128)(2,1)S(1)}, u32[]{:S(2)}, u32[]{:S(2)}) collective-permute-start(bf16[2,32,128]{2,1,0:T(8,128)(2,1)S(1)} %constant_dynamic-update-slice_fusion), channel_id=1, source_target_pairs={{0,3},{1,2},{2,1},{3,0},{4,7},{5,6},{6,5},{7,4},{8,11},{9,10},{10,... | collective-permute-start | bytes 49160 | tf_op jit(solution)/shard_map/ppermute | solution.py:339
  27.8 0.4 %collective-permute-start.12 = (bf16[1,32,128]{2,1,0:T(8,128)(2,1)S(1)}, bf16[1,32,128]{2,1,0:T(8,128)(2,1)S(1)}, u32[]{:S(2)}, u32[]{:S(2)}) collective-permute-start(bf16[1,32,128]{2,1,0:T(8,128)(2,1)S(1)} %collective-permute-done.7), channel_id=1, source_target_pairs={{0,1},{1,0},{2,3},{3,2},{4,5},{5,4},{6,7},{7,6},{8,9},{9,8},{10,11... | collective-permute-start | bytes 24584 | tf_op jit(solution)/shard_map/ppermute | solution.py:334
  28.2 0.8 %collective-permute-done.12.refs_3_ = bf16[1,32,128]{2,1,0:T(8,128)(2,1)S(1)} collective-permute-done((bf16[1,32,128]{2,1,0:T(8,128)(2,1)S(1)}, bf16[1,32,128]{2,1,0:T(8,128)(2,1)S(1)}, u32[]{:S(2)}, u32[]{:S(2)}) %collective-permute-start.12) | collective-permute-done | bytes 8224 | tf_op jit(solution)/shard_map/ppermute | solution.py:334
  29.0 0.7 %collective-permute-done.11.refs_2_ = bf16[2,32,128]{2,1,0:T(8,128)(2,1)S(1)} collective-permute-done((bf16[2,32,128]{2,1,0:T(8,128)(2,1)S(1)}, bf16[2,32,128]{2,1,0:T(8,128)(2,1)S(1)}, u32[]{:S(2)}, u32[]{:S(2)}) %collective-permute-start.11) | collective-permute-done | bytes 16416 | tf_op jit(solution)/shard_map/ppermute | solution.py:339
  29.7 1.2 %collective-permute-done.9.refs_0_ = bf16[2,32,128]{2,1,0:T(8,128)(2,1)S(1)} collective-permute-done((bf16[2,32,128]{2,1,0:T(8,128)(2,1)S(1)}, bf16[2,32,128]{2,1,0:T(8,128)(2,1)S(1)}, u32[]{:S(2)}, u32[]{:S(2)}) %collective-permute-start.9) | collective-permute-done | bytes 16416 | tf_op jit(solution)/shard_map/ppermute | solution.py:339
  31.0 2.3 %output.1 = (f32[4,2048]{1,0:T(4,128)S(1)}, f32[4,2048]{1,0:T(4,128)S(1)}) custom-call(bf16[2,32,128]{2,1,0:T(8,128)(2,1)S(1)} %collective-permute-done.9.refs_0_, bf16[2,32,128]{2,1,0:T(8,128)(2,1)S(1)} %collective-permute-done.10.refs_1_, bf16[2,32,128]{2,1,0:T(8,128)(2,1)S(1)} %collective-permute-done.11.refs_2_, ...), custom_call_target="tpu_custom_call" | custom-call | flops 134217728 | bytes 16777216 | tf_op jit(solution)/shard_map/output/pallas_call | solution.py:316
  33.6 0.9 %collective-permute-done.13 = f32[4,2048]{1,0:T(4,128)S(1)} collective-permute-done((f32[4,2048]{1,0:T(4,128)S(1)}, f32[4,2048]{1,0:T(4,128)S(1)}, u32[]{:S(2)}, u32[]{:S(2)}) %collective-permute-start.13) | collective-permute-done | bytes 32800 | tf_op jit(solution)/shard_map/ppermute | solution.py:334
  34.5 0.6 %add_convert_fusion = bf16[4,2048]{1,0:T(4,128)(2,1)} fusion(f32[4,2048]{1,0:T(4,128)S(1)} %get-tuple-element.23, f32[4,2048]{1,0:T(4,128)S(1)} %collective-permute-done.13), kind=kLoop, calls=%fused_computation | loop fusion | flops 16384 | bytes 81920 | tf_op jit(solution)/shard_map/convert_element_type | solution.py:402
  (34 shorter events, 0.8 us)
Async XLA Ops:
  0.0 2.9 %copy-start.4 = (bf16[4,2048]{1,0:T(4,128)(2,1)S(1)}, bf16[4,2048]{1,0:T(4,128)(2,1)}, u32[]{:S(2)}) copy-start(bf16[4,2048]{1,0:T(4,128)(2,1)} %rows_ref.1) | copy-start | bytes 49156
  0.0 2.9 %copy-start = (bf16[2048,256]{1,0:T(8,128)(2,1)S(1)}, bf16[2048,256]{1,0:T(8,128)(2,1)}, u32[]{:S(2)}) copy-start(bf16[2048,256]{1,0:T(8,128)(2,1)} %wk.1) | copy-start | bytes 3145732
  0.0 2.9 %copy-start.1 = (bf16[2048,256]{1,0:T(8,128)(2,1)S(1)}, bf16[2048,256]{1,0:T(8,128)(2,1)}, u32[]{:S(2)}) copy-start(bf16[2048,256]{1,0:T(8,128)(2,1)} %wv.1) | copy-start | bytes 3145732
  0.0 2.8 %collective-permute-start = (bf16[4,2048]{1,0:T(4,128)(2,1)}, bf16[4,2048]{1,0:T(4,128)(2,1)S(1)}, u32[]{:S(2)}, u32[]{:S(2)}) collective-permute-start(bf16[4,2048]{1,0:T(4,128)(2,1)} %rows_ref.1), channel_id=1, source_target_pairs={{0,1},{1,0},{2,3},{3,2},{4,5},{5,4},{6,7},{7,6},{8,9},{9,8},{10,11... | collective-permute-start | bytes 49160 | tf_op jit(solution)/shard_map/ppermute | solution.py:334
  7.9 5.5 %collective-permute-start.1 = (f32[2,40,128]{2,1,0:T(8,128)S(1)}, f32[2,40,128]{2,1,0:T(8,128)S(1)}, u32[]{:S(2)}, u32[]{:S(2)}) collective-permute-start(f32[2,40,128]{2,1,0:T(8,128)S(1)} %get-tuple-element.15.after_ref), channel_id=1, source_target_pairs={{0,7},{1,6},{2,5},{3,4},{4,3},{5,2},{6,1},{7,0},{8,15},{9,14},{10,... | collective-permute-start | bytes 122888 | tf_op jit(solution)/shard_map/ppermute | solution.py:339
  11.5 3.4 %collective-permute-start.2 = (f32[2,40,128]{2,1,0:T(8,128)S(1)}, f32[2,40,128]{2,1,0:T(8,128)S(1)}, u32[]{:S(2)}, u32[]{:S(2)}) collective-permute-start(f32[2,40,128]{2,1,0:T(8,128)S(1)} %get-tuple-element.16), channel_id=1, source_target_pairs={{0,5},{1,4},{2,7},{3,6},{4,1},{5,0},{6,3},{7,2},{8,13},{9,12},{10,... | collective-permute-start | bytes 122888 | tf_op jit(solution)/shard_map/ppermute | solution.py:339
  12.0 3.7 %collective-permute-start.3 = (f32[2,40,128]{2,1,0:T(8,128)S(1)}, f32[2,40,128]{2,1,0:T(8,128)S(1)}, u32[]{:S(2)}, u32[]{:S(2)}) collective-permute-start(f32[2,40,128]{2,1,0:T(8,128)S(1)} %get-tuple-element.17), channel_id=1, source_target_pairs={{0,3},{1,2},{2,1},{3,0},{4,7},{5,6},{6,5},{7,4},{8,11},{9,10},{10,... | collective-permute-start | bytes 122888 | tf_op jit(solution)/shard_map/ppermute | solution.py:339
  12.2 3.5 %collective-permute-start.4 = (f32[2,40,128]{2,1,0:T(8,128)S(1)}, f32[2,40,128]{2,1,0:T(8,128)S(1)}, u32[]{:S(2)}, u32[]{:S(2)}) collective-permute-start(f32[2,40,128]{2,1,0:T(8,128)S(1)} %get-tuple-element.18), channel_id=1, source_target_pairs={{0,1},{1,0},{2,3},{3,2},{4,5},{5,4},{6,7},{7,6},{8,9},{9,8},{10,11... | collective-permute-start | bytes 122888 | tf_op jit(solution)/shard_map/ppermute | solution.py:334
  12.9 6.9 %copy-start.2 = (bf16[1,2,2048,128]{3,2,1,0:T(8,128)(2,1)S(1)}, bf16[1,2,2048,128]{3,2,1,0:T(8,128)(2,1)}, u32[]{:S(2)}) copy-start(bf16[1,2,2048,128]{3,2,1,0:T(8,128)(2,1)} %k_ref.1) | copy-start | bytes 3145732
  13.0 6.9 %copy-start.3 = (bf16[1,2,2048,128]{3,2,1,0:T(8,128)(2,1)S(1)}, bf16[1,2,2048,128]{3,2,1,0:T(8,128)(2,1)}, u32[]{:S(2)}) copy-start(bf16[1,2,2048,128]{3,2,1,0:T(8,128)(2,1)} %v_ref.1) | copy-start | bytes 3145732
  13.0 18.0 %slice-start = ((s8[16777216]{0:T(1024)(128)(4,1)}), s8[4194304]{0:T(1024)(128)(4,1)S(1)}, s32[]{:S(2)}) async-start(s8[16777216]{0:T(1024)(128)(4,1)} %bitcast.2), calls=%async_computation | async-start | bytes 8388608
  13.0 18.0 %slice-start.1 = ((s8[16777216]{0:T(1024)(128)(4,1)}), s8[4194304]{0:T(1024)(128)(4,1)S(1)}, s32[]{:S(2)}) async-start(s8[16777216]{0:T(1024)(128)(4,1)} %bitcast.2), calls=%async_computation.1 | async-start | bytes 8388608
  13.0 17.9 %slice-start.2 = ((s8[16777216]{0:T(1024)(128)(4,1)}), s8[4194304]{0:T(1024)(128)(4,1)S(1)}, s32[]{:S(2)}) async-start(s8[16777216]{0:T(1024)(128)(4,1)} %bitcast.2), calls=%async_computation.2 | async-start | bytes 8388608
  15.7 4.2 %collective-permute-start.5 = (f32[1,40,128]{2,1,0:T(8,128)S(1)}, f32[1,40,128]{2,1,0:T(8,128)S(1)}, u32[]{:S(2)}, u32[]{:S(2)}) collective-permute-start(f32[1,40,128]{2,1,0:T(8,128)S(1)} %get-tuple-element.22), channel_id=1, source_target_pairs={{0,9},{1,8},{2,11},{3,10},{4,13},{5,12},{6,15},{7,14},{8,1},{9,0},... | collective-permute-start | bytes 61448 | tf_op jit(solution)/shard_map/ppermute | solution.py:339
  18.0 1.8 %collective-permute-start.6 = (f32[1,40,128]{2,1,0:T(8,128)S(1)}, f32[1,40,128]{2,1,0:T(8,128)S(1)}, u32[]{:S(2)}, u32[]{:S(2)}) collective-permute-start(f32[1,40,128]{2,1,0:T(8,128)S(1)} %get-tuple-element.25), channel_id=1, source_target_pairs={{0,1},{1,0},{2,3},{3,2},{4,5},{5,4},{6,7},{7,6},{8,9},{9,8},{10,11... | collective-permute-start | bytes 61448 | tf_op jit(solution)/shard_map/ppermute | solution.py:334
  19.9 11.1 %slice-start.3 = ((s8[16777216]{0:T(1024)(128)(4,1)}), s8[4194304]{0:T(1024)(128)(4,1)S(1)}, s32[]{:S(2)}) async-start(s8[16777216]{0:T(1024)(128)(4,1)} %bitcast.2), calls=%async_computation.3 | async-start | bytes 8388608
  20.7 4.0 %collective-permute-start.7 = (bf16[1,32,128]{2,1,0:T(8,128)(2,1)S(1)}, bf16[1,32,128]{2,1,0:T(8,128)(2,1)S(1)}, u32[]{:S(2)}, u32[]{:S(2)}) collective-permute-start(bf16[1,32,128]{2,1,0:T(8,128)(2,1)S(1)} %attend.1.refs_4_), channel_id=1, source_target_pairs={{0,9},{1,8},{2,11},{3,10},{4,13},{5,12},{6,15},{7,14},{8,1},{9,0},... | collective-permute-start | bytes 24584 | tf_op jit(solution)/shard_map/ppermute | solution.py:339
  23.1 1.6 %collective-permute-start.8 = (bf16[1,32,128]{2,1,0:T(8,128)(2,1)S(1)}, bf16[1,32,128]{2,1,0:T(8,128)(2,1)S(1)}, u32[]{:S(2)}, u32[]{:S(2)}) collective-permute-start(bf16[1,32,128]{2,1,0:T(8,128)(2,1)S(1)} %attend.1.refs_4_), channel_id=1, source_target_pairs={{0,1},{1,0},{2,3},{3,2},{4,5},{5,4},{6,7},{7,6},{8,9},{9,8},{10,11... | collective-permute-start | bytes 24584 | tf_op jit(solution)/shard_map/ppermute | solution.py:334
  24.8 4.3 %collective-permute-start.10 = (bf16[2,32,128]{2,1,0:T(8,128)(2,1)S(1)}, bf16[2,32,128]{2,1,0:T(8,128)(2,1)S(1)}, u32[]{:S(2)}, u32[]{:S(2)}) collective-permute-start(bf16[2,32,128]{2,1,0:T(8,128)(2,1)S(1)} %constant_dynamic-update-slice_fusion), channel_id=1, source_target_pairs={{0,7},{1,6},{2,5},{3,4},{4,3},{5,2},{6,1},{7,0},{8,15},{9,14},{10,... | collective-permute-start | bytes 49160 | tf_op jit(solution)/shard_map/ppermute | solution.py:339
  26.6 3.2 %collective-permute-start.11 = (bf16[2,32,128]{2,1,0:T(8,128)(2,1)S(1)}, bf16[2,32,128]{2,1,0:T(8,128)(2,1)S(1)}, u32[]{:S(2)}, u32[]{:S(2)}) collective-permute-start(bf16[2,32,128]{2,1,0:T(8,128)(2,1)S(1)} %constant_dynamic-update-slice_fusion), channel_id=1, source_target_pairs={{0,3},{1,2},{2,1},{3,0},{4,7},{5,6},{6,5},{7,4},{8,11},{9,10},{10,... | collective-permute-start | bytes 49160 | tf_op jit(solution)/shard_map/ppermute | solution.py:339
  27.8 3.2 %collective-permute-start.9 = (bf16[2,32,128]{2,1,0:T(8,128)(2,1)S(1)}, bf16[2,32,128]{2,1,0:T(8,128)(2,1)S(1)}, u32[]{:S(2)}, u32[]{:S(2)}) collective-permute-start(bf16[2,32,128]{2,1,0:T(8,128)(2,1)S(1)} %constant_dynamic-update-slice_fusion), channel_id=1, source_target_pairs={{0,5},{1,4},{2,7},{3,6},{4,1},{5,0},{6,3},{7,2},{8,13},{9,12},{10,... | collective-permute-start | bytes 49160 | tf_op jit(solution)/shard_map/ppermute | solution.py:339
  27.8 1.3 %collective-permute-start.12 = (bf16[1,32,128]{2,1,0:T(8,128)(2,1)S(1)}, bf16[1,32,128]{2,1,0:T(8,128)(2,1)S(1)}, u32[]{:S(2)}, u32[]{:S(2)}) collective-permute-start(bf16[1,32,128]{2,1,0:T(8,128)(2,1)S(1)} %collective-permute-done.7), channel_id=1, source_target_pairs={{0,1},{1,0},{2,3},{3,2},{4,5},{5,4},{6,7},{7,6},{8,9},{9,8},{10,11... | collective-permute-start | bytes 24584 | tf_op jit(solution)/shard_map/ppermute | solution.py:334
  33.2 1.2 %collective-permute-start.13 = (f32[4,2048]{1,0:T(4,128)S(1)}, f32[4,2048]{1,0:T(4,128)S(1)}, u32[]{:S(2)}, u32[]{:S(2)}) collective-permute-start(f32[4,2048]{1,0:T(4,128)S(1)} %get-tuple-element.24), channel_id=1, source_target_pairs={{0,1},{1,0},{2,3},{3,2},{4,5},{5,4},{6,7},{7,6},{8,9},{9,8},{10,11... | collective-permute-start | bytes 98312 | tf_op jit(solution)/shard_map/ppermute | solution.py:334
